TPU v7x, 32 devices: a whole 2x2x4 slice. The times are simulated.
32 devices in a mesh: dp: 4 (over z), pipe: 4 (over y, x), tensor: 2 (over core).
Axes of the slice: x: 2, y: 2, z: 4, core: 2. Of those that a mesh axis runs over, the one named last changes fastest.
Arguments:
- tokens: bfloat16 [4096, 8192], P('dp', ('pipe', 'tensor')), may hold values from -6 to 6
- key_value_weight: bfloat16 [8192, 2048], P(('pipe', 'tensor')), may hold values from -0.0625 to 0.0625
- adapter_down: bfloat16 [24, 8192, 128], P(None, ('pipe', 'tensor', 'dp')), may hold values from -0.0625 to 0.0625
- adapter_up: bfloat16 [24, 64, 2048], P(None, 'dp'), may hold values from -0.75 to 0.75
- tenant_of_block: int32 [32], replicated, may hold values from 0 to 23
- slot_of_tenant: int32 [24], replicated, may hold values from 0 to 23, each once
- cotangent: bfloat16 [4096, 2048], P(('dp', 'pipe', 'tensor')), may hold values from -1.5 to 1.5
Outputs:
- key_value: bfloat16 [4096, 2048], P(('dp', 'pipe', 'tensor'))
- input_grad: bfloat16 [4096, 8192], P('dp', ('pipe', 'tensor'))
- grad_a: float32 [24, 8192, 128], P(None, ('pipe', 'tensor', 'dp'))
- grad_b: float32 [24, 64, 2048], P(None, 'dp', ('pipe', 'tensor'))
Inputs may be any that keep to these rules, and one draw needn't show every extreme that they name: `slot_of_tenant`: each slot holds exactly one tenant.
All inputs are finite; a program needn't handle non-finite values.
Results may differ from a plain program's by a relative error of at most 0.017.
Values may be sent and summed in bfloat16 or wider, within the bound.
No kernel may reach another device: no remote copies, remote signals or barrier semaphores. Data moves between devices by JAX's collectives and lax.ppermute only.
A program may use at most 64 MiB of HBM per device.

v0:
```python
import jax
import jax.numpy as jnp
from jax import lax
from jax.sharding import PartitionSpec as P

KEY_WIDTH = 1024
ADAPTER_RANK = 64
BLOCK = 128


def body(
    tokens, key_value_weight, adapter_down, adapter_up, tenant_of_block, slot_of_tenant, cotangent
):
    data_count = lax.axis_size("dp")
    group_count = lax.axis_size(("pipe", "tensor"))
    my_group = lax.axis_index(("pipe", "tensor"))
    tok_dev, feature_count = tokens.shape
    blocks_dev = tok_dev // BLOCK
    row_count = tok_dev // group_count
    tenant_list = slot_of_tenant.shape[0]
    all_blocks = tenant_of_block.shape[0]
    tenant_ids = lax.broadcasted_iota(jnp.int32, (all_blocks, tenant_list), 1)
    slot_of_block = jnp.sum(
        jnp.where(tenant_of_block[:, None] == tenant_ids, slot_of_tenant[None, :], 0), axis=1
    )
    slot_match = slot_of_block[:, None] == tenant_ids
    down_rows = adapter_down.shape[1]
    a_send = jnp.dot(
        slot_match.astype(jnp.bfloat16),
        adapter_down.reshape(tenant_list, down_rows * 2 * ADAPTER_RANK),
        preferred_element_type=jnp.float32,
    )
    a_send = a_send.astype(jnp.bfloat16).reshape(all_blocks, down_rows, 2 * ADAPTER_RANK)
    own_block = my_group * row_count // BLOCK
    own_slots = lax.dynamic_index_in_dim(
        slot_of_block.reshape(data_count, blocks_dev), own_block, 1, False
    )
    owner_choice = (
        own_slots[:, None] == lax.broadcasted_iota(jnp.int32, (data_count, tenant_list), 1)
    ).astype(jnp.bfloat16)
    up_rows = adapter_up.shape[1]
    b_send = jnp.dot(
        owner_choice,
        adapter_up.reshape(tenant_list, up_rows * 2 * KEY_WIDTH),
        preferred_element_type=jnp.float32,
    )
    b_send = b_send.astype(jnp.bfloat16).reshape(data_count, up_rows, 2 * KEY_WIDTH)
    down_blocks, b_own = (
        lax.all_to_all(a_send, "dp", split_axis=0, concat_axis=1, tiled=True),
        lax.all_to_all(b_send, "dp", split_axis=0, concat_axis=1, tiled=True),
    )
    b_own = b_own[0]
    tok_blocks = tokens.reshape(blocks_dev, BLOCK, feature_count)
    low_part = jnp.einsum(
        "bif,bfr->bir", tok_blocks, down_blocks, preferred_element_type=jnp.float32
    ).reshape(tok_dev, 2 * ADAPTER_RANK)
    summed = lax.psum_scatter(
        jnp.concatenate(
            [jnp.dot(tokens, key_value_weight, preferred_element_type=jnp.float32), low_part],
            axis=1,
        ).astype(jnp.bfloat16),
        ("pipe", "tensor"),
        scatter_dimension=0,
        tiled=True,
    ).astype(jnp.float32)
    base_out = summed[:, : 2 * KEY_WIDTH]
    low_rows = summed[:, 2 * KEY_WIDTH :].astype(jnp.bfloat16)
    lowrank = jnp.concatenate(
        [
            jnp.dot(
                low_rows[:, :ADAPTER_RANK], b_own[:, :KEY_WIDTH], preferred_element_type=jnp.float32
            ),
            jnp.dot(
                low_rows[:, ADAPTER_RANK:], b_own[:, KEY_WIDTH:], preferred_element_type=jnp.float32
            ),
        ],
        axis=1,
    )
    key_value = (base_out + lowrank).astype(jnp.bfloat16)
    contract_last = (((1,), (1,)), ((), ()))
    grad_rows = jnp.concatenate(
        [
            lax.dot_general(
                cotangent[:, :KEY_WIDTH],
                b_own[:, :KEY_WIDTH],
                contract_last,
                preferred_element_type=jnp.float32,
            ),
            lax.dot_general(
                cotangent[:, KEY_WIDTH:],
                b_own[:, KEY_WIDTH:],
                contract_last,
                preferred_element_type=jnp.float32,
            ),
        ],
        axis=1,
    )
    grad_rows = grad_rows.astype(jnp.bfloat16)
    cot_all, grad_low, low_all = (
        lax.all_gather(cotangent, ("pipe", "tensor"), axis=0, tiled=True),
        lax.all_gather(grad_rows, ("pipe", "tensor"), axis=0, tiled=True),
        lax.all_gather(low_rows, ("pipe", "tensor"), axis=0, tiled=True),
    )
    grad_blocks = grad_low.reshape(blocks_dev, BLOCK, 2 * ADAPTER_RANK)
    input_grad = lax.dot_general(
        cot_all, key_value_weight, contract_last, preferred_element_type=jnp.float32
    )
    input_grad = input_grad + jnp.einsum(
        "bir,bfr->bif", grad_blocks, down_blocks, preferred_element_type=jnp.float32
    ).reshape(tok_dev, feature_count)
    input_grad = input_grad.astype(jnp.bfloat16)
    grad_a_part = jnp.einsum(
        "bif,bir->bfr", tok_blocks, grad_blocks, preferred_element_type=jnp.float32
    )
    col_count = 2 * KEY_WIDTH // group_count
    col_start = my_group * col_count
    half_index = col_start // KEY_WIDTH
    low_half = lax.dynamic_slice_in_dim(
        low_all, half_index * ADAPTER_RANK, ADAPTER_RANK, 1
    ).reshape(blocks_dev, BLOCK, ADAPTER_RANK)
    cot_cols = lax.dynamic_slice_in_dim(cot_all, col_start, col_count, 1).reshape(
        blocks_dev, BLOCK, col_count
    )
    grad_b_part = jnp.einsum("bir,bic->brc", low_half, cot_cols, preferred_element_type=jnp.float32)
    grad_a_recv, grad_b_recv = (
        lax.all_to_all(
            grad_a_part.astype(jnp.bfloat16), "dp", split_axis=1, concat_axis=0, tiled=True
        ).astype(grad_a_part.dtype),
        lax.all_to_all(
            grad_b_part.astype(jnp.bfloat16), "dp", split_axis=1, concat_axis=0, tiled=True
        ).astype(grad_b_part.dtype),
    )
    slot_weight = slot_match.astype(jnp.float32)
    grad_a = jnp.einsum(
        "bt,bx->tx",
        slot_weight,
        grad_a_recv.reshape(all_blocks, down_rows * 2 * ADAPTER_RANK),
        precision=lax.Precision.HIGHEST,
    )
    grad_a = grad_a.reshape(tenant_list, down_rows, 2 * ADAPTER_RANK)
    grad_b = jnp.einsum(
        "bt,bx->tx",
        slot_weight,
        grad_b_recv.reshape(all_blocks, grad_b_recv.shape[1] * col_count),
        precision=lax.Precision.HIGHEST,
    )
    grad_b = grad_b.reshape(tenant_list, grad_b_recv.shape[1], col_count)
    return (key_value, input_grad, grad_a, grad_b)


def solution(mesh):
    placed = (
        P("dp", ("pipe", "tensor")),
        P(("pipe", "tensor"), None),
        P(None, ("pipe", "tensor", "dp"), None),
        P(None, "dp", None),
        P(),
        P(),
        P(("dp", "pipe", "tensor"), None),
    )
    return jax.shard_map(
        body,
        mesh=mesh,
        in_specs=placed,
        out_specs=(
            P(("dp", "pipe", "tensor"), None),
            P("dp", ("pipe", "tensor")),
            P(None, ("pipe", "tensor", "dp"), None),
            P(None, "dp", ("pipe", "tensor")),
        ),
        check_vma=False,
    )
```

profile of v0, /device:TPU:0, one launch (start us, length us, event | category | flops | bytes accessed | tf_op | source)
XLA Modules:
  0.0 211.3 jit_solution(5688823630316936763)
XLA Ops:
  7.2 0.0 copy-start
  7.2 0.0 all-gather.2.cloned.1.call-start
  7.2 0.7 all-gather.2.cloned.1.call-update
  7.9 0.8 select_reduce_fusion
  8.7 2.7 %fusion.4 = bf16[4,8,256,128]{3,1,2,0:T(8,128)(2,1)S(1)} fusion(bf16[3,8,256,128]{3,2,1,0:T(8,128)(2,1)} %bitcast.104, s32[32]{0:T(128)S(1)} %select_reduce_fusion), kind=kOutput, calls=%fused_computation.12 | convolution fusion | flops 51380992 | bytes 3670144 | tf_op jit(solution)/shard_map/dot_general | solution.py:28
  11.4 1.8 copy.59
  13.2 6.3 %all-to-all-start = ((bf16[32,256,128]{2,1,0:T(8,128)(2,1)}), bf16[32,256,128]{2,1,0:T(8,128)(2,1)}, u32[]{:S(2)}, u32[]{:S(2)}) async-start(bf16[32,256,128]{2,1,0:T(8,128)(2,1)} %bitcast.99), calls=%async_computation | async-start | bytes 4194304 | tf_op jit(solution)/shard_map/all_to_all | solution.py:49
  19.5 0.0 reduce-scatter.2.cloned.1.call-start
  19.5 0.0 copy-done
  19.5 8.5 %convolution_convert_fusion.2 = bf16[1024,2048]{1,0:T(8,128)(2,1)} fusion(bf16[1024,1024]{1,0:T(8,128)(2,1)S(1)} %copy-done, bf16[1024,2048]{1,0:T(8,128)(2,1)} %param.8), kind=kOutput, calls=%fused_computation.5 | convolution fusion | flops 4297064448 | bytes 10485760 | tf_op jit(solution)/shard_map/dot_general | solution.py:59
  27.9 39.8 %all-to-all-done = bf16[32,256,128]{2,1,0:T(8,128)(2,1)} async-done(((bf16[32,256,128]{2,1,0:T(8,128)(2,1)}), bf16[32,256,128]{2,1,0:T(8,128)(2,1)}, u32[]{:S(2)}, u32[]{:S(2)}) %all-to-all-start) | async-done | bytes 2097184 | tf_op jit(solution)/shard_map/all_to_all | solution.py:49
  67.8 1.7 copy.40
  69.5 0.0 copy-start.1
  69.5 0.0 copy-start.2
  69.5 0.7 convolution_convert_fusion.3
  70.3 0.5 copy-done.1
  70.8 1.6 copy-done.2
  72.5 2.4 %pad_maximum_fusion = bf16[1024,2176]{1,0:T(8,128)(2,1)} fusion(bf16[1024,128]{1,0:T(8,128)(2,1)S(1)} %bitcast.105, bf16[1024,2048]{1,0:T(8,128)(2,1)S(1)} %copy-done.2), kind=kLoop, calls=%fused_computation.2 | loop fusion | flops 8912896 | bytes 8912896 | tf_op jit(solution)/shard_map/concatenate | solution.py:58
  74.9 0.0 reduce-scatter.2.cloned.1.call-update
  75.0 0.1 reshape.65
  75.0 3.4 %copy.60 = bf16[3,8,16,2048]{3,1,2,0:T(8,128)(2,1)} copy(bf16[3,8,16,2048]{3,2,1,0:T(8,128)(2,1)} %bitcast.103) | data formatting | bytes 3145728
  78.5 0.0 copy-start.4
  78.5 0.2 dynamic-slice_reduce_fusion
  78.7 2.2 %convolution_convert_fusion.1 = bf16[4,32768]{1,0:T(4,128)(2,1)S(1)} fusion(bf16[24,32768]{1,0:T(8,128)(2,1)} %bitcast.101, s32[4]{0:T(128)S(1)} %dynamic-slice_reduce_fusion), kind=kOutput, calls=%fused_computation.1 | convolution fusion | flops 6422624 | bytes 1835024 | tf_op jit(solution)/shard_map/dot_general | solution.py:42
  80.9 0.2 copy.94
  81.0 10.4 %all_to_all.57 = bf16[4,16,2048]{2,1,0:T(8,128)(2,1)S(1)} all-to-all(bf16[4,16,2048]{2,1,0:T(8,128)(2,1)S(1)} %bitcast.108), channel_id=1, replica_groups=mesh['dp'=4,'pipe'=4,'tensor'=2] {'dp'}, dimensions={0} | all-to-all | bytes 524288 | tf_op jit(solution)/shard_map/all_to_all | solution.py:50
  91.4 0.0 copy-done.4
  91.4 0.2 fusion.7
  91.7 0.2 fusion.8
  91.9 9.8 %all_gather.10 = bf16[1024,128]{0,1:T(8,128)(2,1)S(1)} all-gather(bf16[128,128]{0,1:T(8,128)(2,1)S(1)} %pad_maximum_fusion.1), channel_id=1, replica_groups=mesh['dp'=4,'pipe'=4,'tensor'=2] {'pipe','tensor'}, dimensions={0}, use_global_device_ids=true | all-gather | bytes 294912 | tf_op jit(solution)/shard_map/all_gather | solution.py:101
  101.7 2.0 convert_bitcast_fusion
  103.7 4.1 %copy.43 = bf16[8,1024,128]{2,0,1:T(8,128)(2,1)} copy(bf16[8,1024,128]{1,2,0:T(8,128)(2,1)} %convert_bitcast_fusion) | data formatting | bytes 4194304 | tf_op jit(solution)/shard_map/convert_element_type | solution.py:127
  107.8 4.7 %all-to-all-start.2 = ((bf16[8,1024,128]{2,0,1:T(8,128)(2,1)}), bf16[8,1024,128]{2,0,1:T(8,128)(2,1)}, u32[]{:S(2)}, u32[]{:S(2)}) async-start(bf16[8,1024,128]{2,0,1:T(8,128)(2,1)} %copy.43), calls=%async_computation.3 | async-start | bytes 4194304 | tf_op jit(solution)/shard_map/all_to_all | solution.py:126
  112.6 4.3 %fusion.13 = f32[8,128,1024]{2,1,0:T(8,128)} fusion(bf16[8,1024,128]{2,1,0:T(8,128)(2,1)} %bitcast.98, bf16[1024,128]{0,1:T(8,128)(2,1)S(1)} %all_gather.10), kind=kOutput, calls=%fused_computation.27 | convolution fusion | flops 268435456 | bytes 6553600 | tf_op jit(solution)/shard_map/bir,bfr->bif/dot_general | solution.py:108
  116.9 44.5 %all-to-all-done.2 = bf16[8,1024,128]{2,0,1:T(8,128)(2,1)} async-done(((bf16[8,1024,128]{2,0,1:T(8,128)(2,1)}), bf16[8,1024,128]{2,0,1:T(8,128)(2,1)}, u32[]{:S(2)}, u32[]{:S(2)}) %all-to-all-start.2) | async-done | bytes 2097184 | tf_op jit(solution)/shard_map/all_to_all | solution.py:126
  161.4 2.1 copy.93
  163.5 1.3 fusion.1
  164.8 2.2 %copy.51 = f32[24,256,128]{2,1,0:T(8,128)} copy(f32[24,256,128]{2,0,1:T(8,128)S(1)} %fusion.1) | data formatting | bytes 6291456
  167.0 0.0 all-gather.2.cloned.1.call-done
  167.0 1.1 constant_dynamic-slice_fusion.1
  168.1 10.5 %fusion = bf16[1024,1024]{1,0:T(8,128)(2,1)} fusion(f32[8,128,1024]{2,1,0:T(8,128)} %fusion.13, bf16[1024,2048]{1,0:T(8,128)(2,1)} %all-gather.2.cloned.1.call-done, bf16[1024,2048]{1,0:T(8,128)(2,1)} %param.8), kind=kOutput, calls=%fused_computation.4 | convolution fusion | flops 4297064448 | bytes 14680064 | tf_op jit(solution)/shard_map/dot_general | solution.py:105
  178.6 0.0 reduce-scatter.2.cloned.1.call-done
  178.6 0.0 copy-start.3
  178.6 0.8 slice.46
  179.5 9.5 %all_gather.11 = bf16[1024,128]{1,0:T(8,128)(2,1)S(1)} all-gather(bf16[128,128]{1,0:T(8,128)(2,1)S(1)} %slice.46), channel_id=1, replica_groups=mesh['dp'=4,'pipe'=4,'tensor'=2] {'pipe','tensor'}, dimensions={0}, use_global_device_ids=true | all-gather | bytes 294912 | tf_op jit(solution)/shard_map/all_gather | solution.py:102
  189.0 0.1 constant_dynamic-slice_fusion
  189.1 0.3 convolution_convert_fusion.4
  189.4 0.9 copy.48
  190.3 3.4 %all-to-all-start.3 = ((bf16[8,64,256]{2,0,1:T(8,128)(2,1)}), bf16[8,64,256]{2,0,1:T(8,128)(2,1)S(1)}, u32[]{:S(2)}, u32[]{:S(2)}) async-start(bf16[8,64,256]{2,0,1:T(8,128)(2,1)} %copy.48), calls=%async_computation.4 | async-start | bytes 524288 | tf_op jit(solution)/shard_map/all_to_all | solution.py:129
  193.7 0.0 copy-done.3
  193.7 0.2 fusion.24
  193.9 0.3 fusion.21
  194.2 0.9 fusion.9
  195.0 8.3 %all-to-all-done.3 = bf16[8,64,256]{2,0,1:T(8,128)(2,1)S(1)} async-done(((bf16[8,64,256]{2,0,1:T(8,128)(2,1)}), bf16[8,64,256]{2,0,1:T(8,128)(2,1)S(1)}, u32[]{:S(2)}, u32[]{:S(2)}) %all-to-all-start.3) | async-done | bytes 262176 | tf_op jit(solution)/shard_map/all_to_all | solution.py:129
  203.4 0.2 fusion.10
  203.6 0.9 copy.52
  (2 shorter events, 0.1 us)
Async XLA Ops:
  7.2 12.3 %copy-start = (bf16[1024,1024]{1,0:T(8,128)(2,1)S(1)}, bf16[1024,1024]{1,0:T(8,128)(2,1)}, u32[]{:S(2)}) copy-start(bf16[1024,1024]{1,0:T(8,128)(2,1)} %param.7) | copy-start | bytes 6291460
  7.2 159.9 %all-gather.2.cloned.1.call-start = ((), (), s32[]{:S(2)}) async-start(), calls=%async_computation.6 | async-start | bytes 4718592 | tf_op jit(solution)/shard_map/all_gather | solution.py:100
  13.2 54.6 %all-to-all-start = ((bf16[32,256,128]{2,1,0:T(8,128)(2,1)}), bf16[32,256,128]{2,1,0:T(8,128)(2,1)}, u32[]{:S(2)}, u32[]{:S(2)}) async-start(bf16[32,256,128]{2,1,0:T(8,128)(2,1)} %bitcast.99), calls=%async_computation | async-start | bytes 4194304 | tf_op jit(solution)/shard_map/all_to_all | solution.py:49
  19.5 159.2 %reduce-scatter.2.cloned.1.call-start = ((), (), s32[]{:S(2)}) async-start(), calls=%async_computation.5 | async-start | bytes 5013504 | tf_op jit(solution)/shard_map/reduce_scatter | solution.py:57
  69.5 1.3 copy-start.1
  69.5 2.9 %copy-start.2 = (bf16[1024,2048]{1,0:T(8,128)(2,1)S(1)}, bf16[1024,2048]{1,0:T(8,128)(2,1)}, u32[]{:S(2)}) copy-start(bf16[1024,2048]{1,0:T(8,128)(2,1)} %convolution_convert_fusion.2) | copy-start | bytes 12582916
  78.5 13.0 %copy-start.4 = (bf16[128,2048]{1,0:T(8,128)(2,1)S(1)}, bf16[128,2048]{1,0:T(8,128)(2,1)}, u32[]{:S(2)}) copy-start(bf16[128,2048]{1,0:T(8,128)(2,1)} %param.13) | copy-start | bytes 1572868
  107.8 53.6 %all-to-all-start.2 = ((bf16[8,1024,128]{2,0,1:T(8,128)(2,1)}), bf16[8,1024,128]{2,0,1:T(8,128)(2,1)}, u32[]{:S(2)}, u32[]{:S(2)}) async-start(bf16[8,1024,128]{2,0,1:T(8,128)(2,1)} %copy.43), calls=%async_computation.3 | async-start | bytes 4194304 | tf_op jit(solution)/shard_map/all_to_all | solution.py:126
  178.6 15.0 %copy-start.3 = (bf16[128,2176]{1,0:T(8,128)(2,1)S(1)}, bf16[128,2176]{1,0:T(8,128)(2,1)}, u32[]{:S(2)}) copy-start(bf16[128,2176]{1,0:T(8,128)(2,1)} %reduce-scatter.2.cloned.1.call-done) | copy-start | bytes 1671172
  190.3 13.0 %all-to-all-start.3 = ((bf16[8,64,256]{2,0,1:T(8,128)(2,1)}), bf16[8,64,256]{2,0,1:T(8,128)(2,1)S(1)}, u32[]{:S(2)}, u32[]{:S(2)}) async-start(bf16[8,64,256]{2,0,1:T(8,128)(2,1)} %copy.48), calls=%async_computation.4 | async-start | bytes 524288 | tf_op jit(solution)/shard_map/all_to_all | solution.py:129
Sparse Core Ops, SparseCore 0:
  9.9 39.4 all-gather.1
  75.1 51.8 reduce-scatter.1
where the time goes:
time: 212 us; the launch traced here: 211 us
  waiting for transfers between devices  93.3 us (44%)
  matrix products  33.6 us (16%)
  blocking collectives  29.7 us (14%)
  local copies, waits for them, and re-layouts  21.8 us (10%)
  starting transfers between devices  14.4 us (7%)
  between operations  14.2 us (7%)
  other arithmetic  4.1 us (2%)
    all_to_all x1, waiting for transfers between devices, body(): lax.all_to_all(grad_a_part.astype(jnp.bfloat16), 'dp', split_axis=1, conc...  44.5 us
    all_to_all x1, waiting for transfers between devices, body(): lax.all_to_all(a_send, 'dp', split_axis=0, concat_axis=1, tiled=True)  39.8 us
    unnamed x15, local copies, waits for them, and re-layouts  10.7 us
    dot_general x1, matrix products, body(): lax.dot_general(cot_all, key_value_weight, contract_last, preferred_eleme...  10.5 us
    all_to_all x1, blocking collectives, body(): lax.all_to_all(b_send, 'dp', split_axis=0, concat_axis=1, tiled=True)  10.4 us
    all_gather x1, blocking collectives, body(): lax.all_gather(grad_rows, ('pipe', 'tensor'), axis=0, tiled=True)  9.81 us
    all_gather x1, blocking collectives, body(): lax.all_gather(low_rows, ('pipe', 'tensor'), axis=0, tiled=True)  9.51 us
    dot_general x1, matrix products, body(): jnp.dot(tokens, key_value_weight, preferred_element_type=jnp.float32)  8.46 us
  transfers between devices with their start and end apart: 5, of which 3 were waited for; matrix products, arithmetic and copies ran while one was open for 26% of the time, Pallas kernels for 0%

commit v1 on v0

v1 whole, which is shorter than its diff:
```python
import functools

import jax
import jax.numpy as jnp
from jax import lax
from jax.experimental import pallas as pl
from jax.experimental.pallas import tpu as pltpu
from jax.sharding import PartitionSpec as P

KEY_WIDTH = 1024
ADAPTER_RANK = 64
BLOCK = 128
RANKS = 2 * ADAPTER_RANK
WIDTH = 2 * KEY_WIDTH
VMEM_LIMIT = 48 * 1024 * 1024
LAST_BOTH = (((1,), (1,)), ((), ()))


def params(**more):
    return pltpu.CompilerParams(vmem_limit_bytes=VMEM_LIMIT, **more)


def pick_kernel(tenant_ref, slot_ref, own_ref, down_ref, up_ref, a_ref, b_ref, a_sem, b_sem):
    block_count = a_ref.shape[0]
    data_count = b_ref.shape[0]
    blocks_dev = block_count // data_count

    def a_copy(block):
        slot = slot_ref[tenant_ref[block]]
        return pltpu.make_async_copy(down_ref.at[slot], a_ref.at[block], a_sem.at[block])

    def b_copy(data):
        slot = slot_ref[tenant_ref[data * blocks_dev + own_ref[0]]]
        return pltpu.make_async_copy(up_ref.at[slot], b_ref.at[data], b_sem.at[data])

    @pl.loop(0, data_count)
    def _(data):
        b_copy(data).start()

    @pl.loop(0, block_count)
    def _(block):
        a_copy(block).start()

    @pl.loop(0, data_count)
    def _(data):
        b_copy(data).wait()

    @pl.loop(0, block_count)
    def _(block):
        a_copy(block).wait()


def pick(tenant_of_block, slot_of_tenant, own_block, adapter_down, adapter_up, data_count):
    block_count = tenant_of_block.shape[0]
    smem = pl.BlockSpec(memory_space=pltpu.SMEM)
    hbm = pl.BlockSpec(memory_space=pl.ANY)
    return pl.pallas_call(
        pick_kernel,
        out_shape=(
            jax.ShapeDtypeStruct((block_count,) + adapter_down.shape[1:], adapter_down.dtype),
            jax.ShapeDtypeStruct((data_count,) + adapter_up.shape[1:], adapter_up.dtype),
        ),
        in_specs=[smem, smem, smem, hbm, hbm],
        out_specs=(hbm, hbm),
        scratch_shapes=[
            pltpu.SemaphoreType.DMA((block_count,)),
            pltpu.SemaphoreType.DMA((data_count,)),
        ],
        name="pick_rows",
    )(tenant_of_block, slot_of_tenant, own_block, adapter_down, adapter_up)


def base_kernel(x_ref, w_ref, out_ref):
    pipe_count, _, rows, depth = x_ref.shape
    x = x_ref[...].reshape(pipe_count * rows, depth)
    y = jnp.dot(x, w_ref[...], preferred_element_type=jnp.float32)
    out_ref[0] = y.astype(out_ref.dtype).reshape(out_ref.shape[1:])


def base_product(tokens, weight, pipe_count, tensor_count):
    tok_dev, depth = tokens.shape
    rows = tok_dev // (pipe_count * tensor_count)
    tile = 512
    return pl.pallas_call(
        base_kernel,
        grid=(WIDTH // tile, tensor_count),
        out_shape=jax.ShapeDtypeStruct((tensor_count, pipe_count, rows, WIDTH), jnp.bfloat16),
        in_specs=[
            pl.BlockSpec((pipe_count, 1, rows, depth), lambda n, t: (0, t, 0, 0)),
            pl.BlockSpec((depth, tile), lambda n, t: (0, n)),
        ],
        out_specs=pl.BlockSpec((1, pipe_count, rows, tile), lambda n, t: (t, 0, 0, n)),
        compiler_params=params(),
        cost_estimate=pl.CostEstimate(
            flops=2 * tok_dev * depth * WIDTH, bytes_accessed=16 * 2**20, transcendentals=0
        ),
        name="base_product",
    )(tokens.reshape(pipe_count, tensor_count, rows, depth), weight)


def low_kernel(x_ref, a_ref, out_ref):
    depth = x_ref.shape[1]
    a = a_ref[...].reshape(depth, RANKS)
    out_ref[...] = jnp.dot(x_ref[...], a, preferred_element_type=jnp.float32).astype(out_ref.dtype)


def low_product(tokens, down):
    tok_dev, depth = tokens.shape
    data_count, blocks_dev, down_rows, _ = down.shape
    return pl.pallas_call(
        low_kernel,
        grid=(blocks_dev,),
        out_shape=jax.ShapeDtypeStruct((tok_dev, RANKS), jnp.bfloat16),
        in_specs=[
            pl.BlockSpec((BLOCK, depth), lambda b: (b, 0)),
            pl.BlockSpec((data_count, 1, down_rows, RANKS), lambda b: (0, b, 0, 0)),
        ],
        out_specs=pl.BlockSpec((BLOCK, RANKS), lambda b: (b, 0)),
        compiler_params=params(),
        cost_estimate=pl.CostEstimate(
            flops=2 * tok_dev * depth * RANKS, bytes_accessed=5 * 2**20, transcendentals=0
        ),
        name="low_product",
    )(tokens, down)


def input_grad_kernel(cot_ref, w_ref, grad_ref, a_ref, out_ref):
    tensor_count, pipe_count, rows, width = cot_ref.shape
    cot = cot_ref[...].reshape(tensor_count * pipe_count * rows, width)
    base = lax.dot_general(cot, w_ref[...], LAST_BOTH, preferred_element_type=jnp.float32)
    for t in range(tensor_count):
        for p in range(pipe_count):
            piece = t * pipe_count + p
            first = (p * tensor_count + t) * rows
            a = a_ref[:, first // BLOCK].reshape(out_ref.shape[1], RANKS)
            low = lax.dot_general(
                grad_ref[first : first + rows], a, LAST_BOTH, preferred_element_type=jnp.float32
            )
            out_ref[first : first + rows] = (base[piece * rows : (piece + 1) * rows] + low).astype(
                out_ref.dtype
            )


def input_gradient(cot, weight, grad_low, down):
    data_count, blocks_dev, down_rows, _ = down.shape
    depth = weight.shape[0]
    tok_dev = grad_low.shape[0]
    group = next((n for n in range(1, data_count) if n * down_rows % 256 == 0), data_count)
    tile = group * down_rows
    return pl.pallas_call(
        input_grad_kernel,
        grid=(data_count // group,),
        out_shape=jax.ShapeDtypeStruct((tok_dev, depth), jnp.bfloat16),
        in_specs=[
            pl.BlockSpec(cot.shape, lambda d: (0, 0, 0, 0)),
            pl.BlockSpec((tile, WIDTH), lambda d: (d, 0)),
            pl.BlockSpec((tok_dev, RANKS), lambda d: (0, 0)),
            pl.BlockSpec((group, blocks_dev, down_rows, RANKS), lambda d: (d, 0, 0, 0)),
        ],
        out_specs=pl.BlockSpec((tok_dev, tile), lambda d: (0, d)),
        compiler_params=params(),
        cost_estimate=pl.CostEstimate(
            flops=2 * tok_dev * depth * (WIDTH + RANKS),
            bytes_accessed=12 * 2**20,
            transcendentals=0,
        ),
        name="input_gradient",
    )(cot, weight, grad_low, down)


def grad_a_kernel(tenant_ref, slot_ref, x_ref, grad_ref, out_ref):
    data_count, _, tok_dev = x_ref.shape
    blocks_dev = tok_dev // BLOCK
    out_ref[...] = jnp.zeros(out_ref.shape, out_ref.dtype)

    for data in range(data_count):
        for block in range(blocks_dev):
            slot = slot_ref[tenant_ref[data * blocks_dev + block]]
            x = x_ref[data, :, block * BLOCK : (block + 1) * BLOCK]
            grad = grad_ref[data, block * BLOCK : (block + 1) * BLOCK]
            out_ref[slot] += jnp.dot(x, grad, preferred_element_type=jnp.float32)


def grad_down(tenant_of_block, slot_of_tenant, x_features, grad_low):
    data_count, down_rows, tok_dev = x_features.shape
    slots = slot_of_tenant.shape[0]
    tile = 128 if down_rows % 128 == 0 else down_rows
    smem = pl.BlockSpec(memory_space=pltpu.SMEM)
    return pl.pallas_call(
        grad_a_kernel,
        grid=(down_rows // tile,),
        out_shape=jax.ShapeDtypeStruct((slots, down_rows, RANKS), jnp.float32),
        in_specs=[
            smem,
            smem,
            pl.BlockSpec((data_count, tile, tok_dev), lambda f: (0, f, 0)),
            pl.BlockSpec((data_count, tok_dev, RANKS), lambda f: (0, 0, 0)),
        ],
        out_specs=pl.BlockSpec((slots, tile, RANKS), lambda f: (0, f, 0)),
        compiler_params=params(),
        cost_estimate=pl.CostEstimate(
            flops=2 * data_count * tok_dev * down_rows * RANKS,
            bytes_accessed=6 * 2**20,
            transcendentals=0,
        ),
        name="grad_down",
    )(tenant_of_block, slot_of_tenant, x_features, grad_low)


def halves(product, left, right):
    return jnp.concatenate([product(*pair) for pair in zip(left, right)], axis=1)


def body(
    tokens, key_value_weight, adapter_down, adapter_up, tenant_of_block, slot_of_tenant, cotangent
):
    data_count = lax.axis_size("dp")
    pipe_count = lax.axis_size("pipe")
    tensor_count = lax.axis_size("tensor")
    group_count = pipe_count * tensor_count
    my_group = lax.axis_index(("pipe", "tensor"))
    tok_dev, feature_count = tokens.shape
    blocks_dev = tok_dev // BLOCK
    row_count = tok_dev // group_count
    slots = slot_of_tenant.shape[0]
    all_blocks = tenant_of_block.shape[0]
    down_rows = adapter_down.shape[1]
    up_rows = adapter_up.shape[1]

    cot_chips = lax.all_gather(cotangent, "pipe", axis=0, tiled=False)
    cot_all = lax.all_gather(cot_chips, "tensor", axis=0, tiled=False)

    own_block = (my_group * row_count // BLOCK).reshape(1)
    a_send, b_send = pick(
        tenant_of_block, slot_of_tenant, own_block, adapter_down, adapter_up, data_count
    )
    b_own = lax.all_to_all(b_send, "dp", split_axis=0, concat_axis=0, tiled=True)
    b_own = b_own.reshape(data_count * up_rows, WIDTH)
    a_recv = lax.all_to_all(
        a_send.reshape(data_count, blocks_dev, down_rows, RANKS),
        "dp",
        split_axis=0,
        concat_axis=0,
        tiled=True,
    )

    x_send = tokens.T.reshape(data_count, down_rows, tok_dev)
    x_recv = lax.all_to_all(x_send, "dp", split_axis=0, concat_axis=0, tiled=True)

    base = base_product(tokens, key_value_weight, pipe_count, tensor_count)
    base_chips = lax.psum_scatter(base, "tensor", scatter_dimension=0, tiled=True)
    base_rows = lax.psum_scatter(
        base_chips.reshape(pipe_count, row_count, WIDTH), "pipe", scatter_dimension=0, tiled=True
    ).reshape(row_count, WIDTH)

    low_part = low_product(tokens, a_recv)
    low_all = lax.psum(low_part, ("pipe", "tensor"))
    low_rows = lax.dynamic_slice_in_dim(low_all, my_group * row_count, row_count, 0)

    left = lambda m: (m[:, :ADAPTER_RANK], m[:, ADAPTER_RANK:])
    wide = lambda m: (m[:, :KEY_WIDTH], m[:, KEY_WIDTH:])
    lowrank = halves(
        lambda p, q: jnp.dot(p, q, preferred_element_type=jnp.float32), left(low_rows), wide(b_own)
    )
    key_value = (base_rows.astype(jnp.float32) + lowrank).astype(jnp.bfloat16)

    grad_rows = halves(
        lambda p, q: lax.dot_general(p, q, LAST_BOTH, preferred_element_type=jnp.float32),
        wide(cotangent),
        wide(b_own),
    ).astype(jnp.bfloat16)
    grad_all = lax.all_gather(grad_rows, ("dp", "pipe", "tensor"), axis=0, tiled=True)
    grad_all = grad_all.reshape(data_count, tok_dev, RANKS)
    grad_low = lax.dynamic_index_in_dim(grad_all, lax.axis_index("dp"), 0, False)

    input_grad = input_gradient(cot_all, key_value_weight, grad_low, a_recv)
    grad_a = grad_down(tenant_of_block, slot_of_tenant, x_recv, grad_all)

    col_count = WIDTH // group_count
    col_start = my_group * col_count
    half_index = col_start // KEY_WIDTH
    low_half = lax.dynamic_slice_in_dim(
        low_all, half_index * ADAPTER_RANK, ADAPTER_RANK, 1
    ).reshape(blocks_dev, BLOCK, ADAPTER_RANK)
    cot_cols = lax.dynamic_slice_in_dim(cot_all, col_start, col_count, 3)
    cot_cols = cot_cols.transpose(1, 0, 2, 3).reshape(blocks_dev, BLOCK, col_count)
    grad_b_part = jnp.einsum("bir,bic->brc", low_half, cot_cols, preferred_element_type=jnp.float32)
    grad_b_part = grad_b_part.astype(jnp.bfloat16).reshape(
        blocks_dev, data_count, up_rows, col_count
    )
    grad_b_recv = lax.all_to_all(
        grad_b_part.transpose(1, 0, 2, 3), "dp", split_axis=0, concat_axis=0, tiled=True
    ).astype(jnp.float32)
    tenant_ids = lax.broadcasted_iota(jnp.int32, (all_blocks, slots), 1)
    slot_of_block = jnp.sum(
        jnp.where(tenant_of_block[:, None] == tenant_ids, slot_of_tenant[None, :], 0), axis=1
    )
    slot_weight = (slot_of_block[:, None] == tenant_ids).astype(jnp.float32)
    grad_b = jnp.einsum(
        "bt,bx->tx",
        slot_weight,
        grad_b_recv.reshape(all_blocks, up_rows * col_count),
        precision=lax.Precision.HIGHEST,
    ).reshape(slots, up_rows, col_count)
    return (key_value, input_grad, grad_a, grad_b)


def solution(mesh):
    placed = (
        P("dp", ("pipe", "tensor")),
        P(("pipe", "tensor"), None),
        P(None, ("pipe", "tensor", "dp"), None),
        P(None, "dp", None),
        P(),
        P(),
        P(("dp", "pipe", "tensor"), None),
    )
    return jax.shard_map(
        body,
        mesh=mesh,
        in_specs=placed,
        out_specs=(
            P(("dp", "pipe", "tensor"), None),
            P("dp", ("pipe", "tensor")),
            P(None, ("pipe", "tensor", "dp"), None),
            P(None, "dp", ("pipe", "tensor")),
        ),
        check_vma=False,
    )
```

time: 212 us -> 256 us (1.21)
  Pallas kernels: 0 us -> 102 us
  matrix products: 33.6 us -> 3.21 us
  blocking collectives: 29.7 us -> 15.2 us
  local copies, waits for them, and re-layouts: 21.8 us -> 9.66 us
    pallas_call x0 -> x5, Pallas kernels: none -> 102 us  [the longest x1 73.6 us: pick(): pl.pallas_call(pick_kernel, out_shape=(jax.ShapeDtypeStruct((block_count,...]
    dot_general x13 -> x5, matrix products: 33.3 us -> 2.94 us  [the longest x2 2.33 us: body(): jnp.dot(p, q, preferred_element_type=jnp.float32)]
    all_gather x2 -> x0, blocking collectives: 19.3 us -> none  [the longest x1 9.81 us: body(): lax.all_gather(grad_rows, ('pipe', 'tensor'), axis=0, tiled=True)]
    unnamed x15 -> x13, local copies, waits for them, and re-layouts: 10.7 us -> 2.51 us
    convert_element_type x2 -> x0, local copies, waits for them, and re-layouts: 5 us -> none  [the longest x1 4.14 us: body(): grad_a_part.astype(jnp.bfloat16)]
    all_to_all x1, blocking collectives: 10.4 us -> 15.2 us  [body(): lax.all_to_all(b_send, 'dp', split_axis=0, concat_axis=0, tiled=True)]
    all_to_all x3 -> x0, local copies, waits for them, and re-layouts: 3.86 us -> none  [the longest x1 2.08 us: body(): lax.all_to_all(grad_a_part.astype(jnp.bfloat16), 'dp', split_axis=1, conc...]
    transpose x0 -> x3, local copies, waits for them, and re-layouts: none -> 3.69 us  [the longest x1 2.56 us: body(): x_send = tokens.T.reshape(data_count, down_rows, tok_dev)]
  transfers between devices with their start and end apart: 5 -> 9, of which waited for: 3 -> 3; matrix products, arithmetic and copies ran while one was open for 26% -> 5% of each run, Pallas kernels for 0% -> 40%
where the time goes in v1:
time: 256 us; the launch traced here: 255 us
  Pallas kernels  102 us (40%)
  waiting for transfers between devices  94.3 us (37%)
  between operations  15.4 us (6%)
  blocking collectives  15.2 us (6%)
  starting transfers between devices  12 us (5%)
  local copies, waits for them, and re-layouts  9.66 us (4%)
  matrix products  3.21 us (1%)
  other arithmetic  2.65 us (1%)
    pallas_call x1, Pallas kernels, pick(): pl.pallas_call(pick_kernel, out_shape=(jax.ShapeDtypeStruct((block_count,...  73.6 us
    all_to_all x1, waiting for transfers between devices, body(): lax.all_to_all(a_send.reshape(data_count, blocks_dev, down_rows, RANKS),...  47.3 us
    all_to_all x1, waiting for transfers between devices, body(): lax.all_to_all(x_send, 'dp', split_axis=0, concat_axis=0, tiled=True)  44.6 us
    all_to_all x1, blocking collectives, body(): lax.all_to_all(b_send, 'dp', split_axis=0, concat_axis=0, tiled=True)  15.2 us
    pallas_call x1, Pallas kernels, base_product(): pl.pallas_call(base_kernel, grid=(WIDTH // tile, tensor_count), out_shape...  10 us
    pallas_call x1, Pallas kernels, input_gradient(): pl.pallas_call(input_grad_kernel, grid=(data_count // group,), out_shape=...  9.69 us
    pallas_call x1, Pallas kernels, low_product(): pl.pallas_call(low_kernel, grid=(blocks_dev,), out_shape=jax.ShapeDtypeSt...  6.01 us
  transfers between devices with their start and end apart: 9, of which 3 were waited for; matrix products, arithmetic and copies ran while one was open for 5% of the time, Pallas kernels for 40%

profile of v1, /device:TPU:0, one launch (start us, length us, event | category | flops | bytes accessed | tf_op | source)
XLA Modules:
  0.0 254.7 jit_solution(3082455634359765312)
XLA Ops:
  8.0 0.0 all-gather.8.cloned.1.call-start
  8.0 0.7 all-gather.8.cloned.1.call-update
  8.7 0.0 reduce-scatter.5.cloned.1.call-start
  8.8 0.0 copy-start
  8.8 1.6 copy-done
  10.4 10.0 %base_product.1 = bf16[2,4,128,2048]{3,2,1,0:T(8,128)(2,1)} custom-call(bf16[4,2,128,1024]{3,2,1,0:T(8,128)(2,1)S(1)} %bitcast.45, bf16[1024,2048]{1,0:T(8,128)(2,1)} %w_ref.3), custom_call_target="tpu_custom_call" | custom-call | flops 4294967296 | bytes 16777216 | tf_op jit(solution)/shard_map/base_product/pallas_call | solution.py:84
  20.4 0.0 reduce-scatter.5.cloned.1.call-update
  20.4 73.6 %pick_rows.1 = (bf16[32,256,128]{2,1,0:T(8,128)(2,1)}, bf16[4,16,2048]{2,1,0:T(8,128)(2,1)}) custom-call(s32[32]{0:T(128)} %tenant_ref.3, s32[24]{0:T(128)} %slot_ref.3, s32[1]{0:T(128)} %bitcast.3.own_ref, bf16[24,256,128]{2,1,0:T(8,128)(2,1)} %down_ref.1, bf16[24,16,2048]{2,1,0:T(8,128)(2,1)} %up_ref.1), custom_call_target="tpu_custom_call" | custom-call | tf_op jit(solution)/shard_map/pick_rows/pallas_call | solution.py:57
  94.0 15.2 %all_to_all.20 = bf16[4,16,2048]{2,1,0:T(8,128)(2,1)S(1)} all-to-all(bf16[4,16,2048]{2,1,0:T(8,128)(2,1)} %get-tuple-element.7), channel_id=1, replica_groups=mesh['dp'=4,'pipe'=4,'tensor'=2] {'dp'}, dimensions={0} | all-to-all | bytes 524288 | tf_op jit(solution)/shard_map/all_to_all | solution.py:237
  109.2 0.0 copy-start.4
  109.2 0.0 copy-start.5
  109.2 0.0 copy-start.1
  109.2 4.8 %all-to-all-start = ((bf16[4,8,256,128]{3,2,1,0:T(8,128)(2,1)}), bf16[4,8,256,128]{3,2,1,0:T(8,128)(2,1)}, u32[]{:S(2)}, u32[]{:S(2)}) async-start(bf16[4,8,256,128]{3,2,1,0:T(8,128)(2,1)} %bitcast.52), calls=%async_computation.1 | async-start | bytes 4194304 | tf_op jit(solution)/shard_map/all_to_all | solution.py:239
  114.0 0.0 all-gather.6.cloned.1.call-start
  114.0 0.0 copy-done.5
  114.0 0.2 fusion
  114.3 0.0 copy-done.4
  114.3 0.2 fusion.1
  114.5 0.6 pad_maximum_fusion
  115.1 0.0 all-gather.6.cloned.1.call-update
  115.1 0.0 all-reduce.3.cloned.1.call-start
  115.2 47.3 %all-to-all-done.a_ref = bf16[4,8,256,128]{3,2,1,0:T(8,128)(2,1)} async-done(((bf16[4,8,256,128]{3,2,1,0:T(8,128)(2,1)}), bf16[4,8,256,128]{3,2,1,0:T(8,128)(2,1)}, u32[]{:S(2)}, u32[]{:S(2)}) %all-to-all-start) | async-done | bytes 2097184 | tf_op jit(solution)/shard_map/all_to_all | solution.py:239
  162.4 0.0 copy-done.1
  162.4 6.0 %low_product.1 = bf16[1024,128]{1,0:T(8,128)(2,1)} custom-call(bf16[1024,1024]{1,0:T(8,128)(2,1)S(1)} %copy-done.1, bf16[4,8,256,128]{3,2,1,0:T(8,128)(2,1)} %all-to-all-done.a_ref), custom_call_target="tpu_custom_call" | custom-call | flops 268435456 | bytes 5242880 | tf_op jit(solution)/shard_map/low_product/pallas_call | solution.py:110
  168.4 0.0 all-reduce.3.cloned.1.call-update
  168.5 0.0 all-gather.10.cloned.1.call-start
  168.5 0.0 all-gather.8.cloned.1.call-done
  168.5 0.5 all-gather.10.cloned.1.call-update
  169.0 2.6 %copy.31 = bf16[1024,1024]{1,0:T(8,128)(2,1)} copy(bf16[1024,1024]{0,1:T(8,128)(2,1)S(1)} %bitcast.46) | data formatting | bytes 4194304 | tf_op jit(solution)/shard_map/transpose | solution.py:247
  171.6 3.6 %all-to-all-start.2 = ((bf16[4,256,1024]{2,1,0:T(8,128)(2,1)}), bf16[4,256,1024]{2,1,0:T(8,128)(2,1)S(1)}, u32[]{:S(2)}, u32[]{:S(2)}) async-start(bf16[4,256,1024]{2,1,0:T(8,128)(2,1)} %bitcast.49), calls=%async_computation.3 | async-start | bytes 4194304 | tf_op jit(solution)/shard_map/all_to_all | solution.py:248
  175.2 0.0 copy-start.2
  175.2 0.0 copy-start.3
  175.2 0.0 reduce-scatter.7.cloned.1.call-start
  175.3 0.0 reduce-scatter.5.cloned.1.call-done
  175.3 0.5 reduce-scatter.7.cloned.1.call-update
  175.9 0.0 copy-done.2
  175.9 0.0 copy-done.3
  175.9 0.1 select_reduce_fusion
  176.0 0.7 all-gather.6.cloned.1.call-done
  176.7 1.6 copy.30
  178.3 44.6 %all-to-all-done.2.x_ref = bf16[4,256,1024]{2,1,0:T(8,128)(2,1)S(1)} async-done(((bf16[4,256,1024]{2,1,0:T(8,128)(2,1)}), bf16[4,256,1024]{2,1,0:T(8,128)(2,1)S(1)}, u32[]{:S(2)}, u32[]{:S(2)}) %all-to-all-start.2) | async-done | bytes 2097184 | tf_op jit(solution)/shard_map/all_to_all | solution.py:248
  222.9 2.9 %grad_down.1 = f32[24,256,128]{2,1,0:T(8,128)} custom-call(s32[32]{0:T(128)S(1)} %copy-done.2, s32[24]{0:T(128)S(1)} %copy-done.3, bf16[4,256,1024]{2,1,0:T(8,128)(2,1)S(1)} %all-to-all-done.2.x_ref, bf16[4,1024,128]{2,1,0:T(8,128)(2,1)S(1)} %bitcast.48), custom_call_target="tpu_custom_call" | custom-call | flops 268435456 | bytes 6291456 | tf_op jit(solution)/shard_map/grad_down/pallas_call | solution.py:189
  225.8 0.0 all-reduce.3.cloned.1.call-done
  225.8 1.1 constant_dynamic-slice_fusion
  226.9 1.1 fusion.12
  228.1 1.2 fusion.9
  229.3 0.0 all-gather.10.cloned.1.call-done
  229.3 1.1 dynamic-slice_bitcast_fusion
  230.4 0.3 convolution_convert_fusion
  230.7 0.7 copy.50
  231.5 3.4 %all-to-all-start.3 = ((bf16[4,8,16,256]{3,2,1,0:T(8,128)(2,1)}), bf16[4,8,16,256]{3,2,1,0:T(8,128)(2,1)S(1)}, u32[]{:S(2)}, u32[]{:S(2)}) async-start(bf16[4,8,16,256]{3,2,1,0:T(8,128)(2,1)} %bitcast.44), calls=%async_computation.4 | async-start | bytes 524288 | tf_op jit(solution)/shard_map/all_to_all | solution.py:291
  234.9 9.7 %input_gradient.1 = bf16[1024,1024]{1,0:T(8,128)(2,1)} custom-call(bf16[2,4,128,2048]{3,2,1,0:T(8,128)(2,1)} %bitcast.61, bf16[1024,2048]{1,0:T(8,128)(2,1)} %w_ref.3, bf16[1024,128]{1,0:T(8,128)(2,1)S(1)} %dynamic-slice_bitcast_fusion.1.grad_ref, bf16[4,8,256,128]{3,2,1,0:T(8,128)(2,1)} %all-to-all-done.a_ref), custom_call_target="tpu_custom_call" | custom-call | flops 4563402752 | bytes 12582912 | tf_op jit(solution)/shard_map/input_gradient/pallas_call | solution.py:150
  244.6 0.0 all-to-all-done.3
  244.6 0.2 fusion.3
  244.8 0.9 copy.37
  245.6 0.0 reduce-scatter.7.cloned.1.call-done
  245.6 1.9 fusion.2
  (2 shorter events, 0.1 us)
Async XLA Ops:
  8.0 160.5 %all-gather.8.cloned.1.call-start = ((), (), s32[]{:S(2)}) async-start(), calls=%async_computation.9 | async-start | bytes 2621440 | tf_op jit(solution)/shard_map/all_gather | solution.py:230
  8.7 166.6 %reduce-scatter.5.cloned.1.call-start = ((), (), s32[]{:S(2)}) async-start(), calls=%async_computation.6 | async-start | bytes 6291456 | tf_op jit(solution)/shard_map/reduce_scatter | solution.py:251
  8.8 1.6 copy-start
  109.2 5.0 %copy-start.4 = (bf16[4,16,2048]{2,1,0:T(8,128)(2,1)}, bf16[4,16,2048]{2,1,0:T(8,128)(2,1)S(1)}, u32[]{:S(2)}) copy-start(bf16[4,16,2048]{2,1,0:T(8,128)(2,1)S(1)} %all_to_all.20) | copy-start | bytes 786436
  109.2 4.8 %copy-start.5 = (bf16[128,2048]{1,0:T(8,128)(2,1)S(1)}, bf16[128,2048]{1,0:T(8,128)(2,1)}, u32[]{:S(2)}) copy-start(bf16[128,2048]{1,0:T(8,128)(2,1)} %param.13) | copy-start | bytes 1572868
  109.2 53.2 %copy-start.1 = (bf16[1024,1024]{1,0:T(8,128)(2,1)S(1)}, bf16[1024,1024]{1,0:T(8,128)(2,1)}, u32[]{:S(2)}) copy-start(bf16[1024,1024]{1,0:T(8,128)(2,1)} %x_ref.1) | copy-start | bytes 6291460
  109.2 53.2 %all-to-all-start = ((bf16[4,8,256,128]{3,2,1,0:T(8,128)(2,1)}), bf16[4,8,256,128]{3,2,1,0:T(8,128)(2,1)}, u32[]{:S(2)}, u32[]{:S(2)}) async-start(bf16[4,8,256,128]{3,2,1,0:T(8,128)(2,1)} %bitcast.52), calls=%async_computation.1 | async-start | bytes 4194304 | tf_op jit(solution)/shard_map/all_to_all | solution.py:239
  114.0 62.7 %all-gather.6.cloned.1.call-start = ((), (), s32[]{:S(2)}) async-start(), calls=%async_computation.8 | async-start | bytes 1081344 | tf_op jit(solution)/shard_map/all_gather | solution.py:272
  115.1 110.7 %all-reduce.3.cloned.1.call-start = ((), (), s32[]{:S(2)}) async-start(), calls=%async_computation.7 | async-start | bytes 524288 | tf_op jit(solution)/shard_map/psum | solution.py:257
  168.5 60.8 %all-gather.10.cloned.1.call-start = ((), (), s32[]{:S(2)}) async-start(), calls=%async_computation.10 | async-start | bytes 6291456 | tf_op jit(solution)/shard_map/all_gather | solution.py:231
  171.6 51.3 %all-to-all-start.2 = ((bf16[4,256,1024]{2,1,0:T(8,128)(2,1)}), bf16[4,256,1024]{2,1,0:T(8,128)(2,1)S(1)}, u32[]{:S(2)}, u32[]{:S(2)}) async-start(bf16[4,256,1024]{2,1,0:T(8,128)(2,1)} %bitcast.49), calls=%async_computation.3 | async-start | bytes 4194304 | tf_op jit(solution)/shard_map/all_to_all | solution.py:248
  175.2 0.7 copy-start.2
  175.2 0.7 copy-start.3
  175.2 70.4 %reduce-scatter.7.cloned.1.call-start = ((), (), s32[]{:S(2)}) async-start(), calls=%async_computation.11 | async-start | bytes 2621440
  231.5 13.1 %all-to-all-start.3 = ((bf16[4,8,16,256]{3,2,1,0:T(8,128)(2,1)}), bf16[4,8,16,256]{3,2,1,0:T(8,128)(2,1)S(1)}, u32[]{:S(2)}, u32[]{:S(2)}) async-start(bf16[4,8,16,256]{3,2,1,0:T(8,128)(2,1)} %bitcast.44), calls=%async_computation.4 | async-start | bytes 524288 | tf_op jit(solution)/shard_map/all_to_all | solution.py:291
Sparse Core Ops, SparseCore 0:
  10.8 38.0 all-gather.7
  51.3 12.0 reduce-scatter.4
  118.3 58.3 all-gather.5
  178.1 13.2 all-gather.9
  194.2 36.6 reduce-scatter.6
Sparse Core Ops, SparseCore 1:
  168.6 53.3 all-reduce.2

commit v2 on v0

v2 whole, which is shorter than its diff:
```python
import jax
import jax.numpy as jnp
from jax import lax
from jax.experimental import pallas as pl
from jax.experimental.pallas import tpu as pltpu
from jax.sharding import PartitionSpec as P

KEY_WIDTH = 1024
ADAPTER_RANK = 64
BLOCK = 128
RANKS = 2 * ADAPTER_RANK
WIDTH = 2 * KEY_WIDTH
VMEM_LIMIT = 48 * 1024 * 1024
LAST_BOTH = (((1,), (1,)), ((), ()))
FIRST_BOTH = (((0,), (0,)), ((), ()))
SMEM = pl.BlockSpec(memory_space=pltpu.SMEM)
VMEM = pl.BlockSpec(memory_space=pltpu.VMEM)
HBM = pl.BlockSpec(memory_space=pl.ANY)


def call(kernel, name, flops, mib, **more):
    return pl.pallas_call(
        kernel,
        compiler_params=pltpu.CompilerParams(vmem_limit_bytes=VMEM_LIMIT),
        cost_estimate=pl.CostEstimate(
            flops=int(flops), bytes_accessed=int(mib * 2**20), transcendentals=0
        ),
        name=name,
        **more,
    )


def shift(piece, axis, step):
    count = lax.axis_size(axis)
    return lax.ppermute(piece, axis, [(i, (i + step) % count) for i in range(count)])


def wrap(index, count):
    return lax.rem(index + 2 * count, count)


def pick(tenant_of_block, slot_of_tenant, place, own_block, adapter_down, adapter_up, data_count):
    block_count = tenant_of_block.shape[0]
    blocks_dev = block_count // data_count

    def kernel(tenant_ref, slot_ref, place_ref, own_ref, down_ref, up_ref, a_ref, *rest):
        b_refs, (a_sem, b_sem) = rest[:data_count], rest[data_count:]

        def a_copy(block):
            slot = slot_ref[tenant_ref[block]]
            return pltpu.make_async_copy(down_ref.at[slot], a_ref.at[block], a_sem.at[block])

        def b_copy(k):
            data = wrap(place_ref[0] + k, data_count)
            slot = slot_ref[tenant_ref[data * blocks_dev + own_ref[0]]]
            return pltpu.make_async_copy(up_ref.at[slot], b_refs[k], b_sem.at[k])

        for k in range(data_count):
            b_copy(k).start()

        @pl.loop(0, block_count)
        def _(block):
            a_copy(block).start()

        for k in range(data_count):
            b_copy(k).wait()

        @pl.loop(0, block_count)
        def _(block):
            a_copy(block).wait()

    up_shape = jax.ShapeDtypeStruct(adapter_up.shape[1:], adapter_up.dtype)
    down_shape = jax.ShapeDtypeStruct((block_count,) + adapter_down.shape[1:], adapter_down.dtype)
    out = call(
        kernel,
        "pick_rows",
        0,
        4,
        out_shape=(down_shape,) + (up_shape,) * data_count,
        in_specs=[SMEM, SMEM, SMEM, SMEM, HBM, HBM],
        out_specs=(VMEM,) * (1 + data_count),
        scratch_shapes=[
            pltpu.SemaphoreType.DMA((block_count,)),
            pltpu.SemaphoreType.DMA((data_count,)),
        ],
    )(tenant_of_block, slot_of_tenant, place, own_block, adapter_down, adapter_up)
    return out[0], out[1:]


def base_product(place, tokens, weight, first, count):
    pipe_count, tensor_count, rows, depth = tokens.shape
    tile = 1024

    def kernel(place_ref, x_ref, w_ref, out_ref):
        x = x_ref[...].reshape(pipe_count * rows, depth)
        y = jnp.dot(x, w_ref[...], preferred_element_type=jnp.float32).astype(out_ref.dtype)
        for chip in range(pipe_count):
            out_ref[0, wrap(chip - place_ref[1], pipe_count)] = y[chip * rows : (chip + 1) * rows]

    return call(
        kernel,
        "base_product",
        2 * pipe_count * count * rows * depth * WIDTH,
        8,
        grid_spec=pltpu.PrefetchScalarGridSpec(
            num_scalar_prefetch=1,
            grid=(WIDTH // tile, count),
            in_specs=[
                pl.BlockSpec(
                    (pipe_count, 1, rows, depth),
                    lambda n, s, at: (0, wrap(at[2] + s + first, tensor_count), 0, 0),
                ),
                pl.BlockSpec((depth, tile), lambda n, s, at: (0, n)),
            ],
            out_specs=pl.BlockSpec((1, pipe_count, rows, tile), lambda n, s, at: (s, 0, 0, n)),
        ),
        out_shape=jax.ShapeDtypeStruct((count, pipe_count, rows, WIDTH), jnp.bfloat16),
    )(place, tokens, weight)


def low_product(place, tokens, down, pipe_count, tensor_count):
    tok_dev, depth = tokens.shape
    rows = tok_dev // (pipe_count * tensor_count)

    def kernel(place_ref, x_ref, a_ref, out_ref):
        for block in range(tok_dev // BLOCK):
            a = a_ref[:, block].reshape(depth, RANKS)
            x = x_ref[block * BLOCK : (block + 1) * BLOCK]
            y = jnp.dot(x, a, preferred_element_type=jnp.float32).astype(out_ref.dtype)
            for part in range(BLOCK // rows):
                chip, core = divmod(block * (BLOCK // rows) + part, tensor_count)
                core = wrap(core - place_ref[2], tensor_count)
                out_ref[core, chip] = y[part * rows : (part + 1) * rows]

    return call(
        kernel,
        "low_product",
        2 * tok_dev * depth * RANKS,
        4.5,
        in_specs=[SMEM, VMEM, VMEM],
        out_specs=VMEM,
        out_shape=jax.ShapeDtypeStruct((tensor_count, pipe_count, rows, RANKS), jnp.bfloat16),
    )(place, tokens, down)


def input_gradient(place, cot_pieces, weight, grad_pieces, down):
    data_count, blocks_dev, down_rows, _ = down.shape
    tensor_count, pipe_count = len(cot_pieces), len(cot_pieces[0])
    rows = cot_pieces[0][0].shape[0]
    depth = weight.shape[0]
    tok_dev = blocks_dev * BLOCK
    planes = next((n for n in range(1, data_count) if n * down_rows % 256 == 0), data_count)
    tile = planes * down_rows
    order = [(s, k) for s in range(tensor_count) for k in range(pipe_count)]

    def kernel(place_ref, w_ref, a_ref, *rest):
        grad_refs, rest = rest[:tensor_count], rest[tensor_count:]
        cot_refs, (out_ref, cot, grad, sems) = rest[: len(order)], rest[len(order) :]

        def first_row(s, k):
            chip = wrap(place_ref[1] - k, pipe_count)
            core = wrap(place_ref[2] - s, tensor_count)
            return pl.multiple_of((chip * tensor_count + core) * rows, rows)

        @pl.when(pl.program_id(0) == 0)
        def _():
            copies = [
                pltpu.make_async_copy(ref, cot.at[pl.ds(first_row(*at), rows)], sems.at[i])
                for i, (at, ref) in enumerate(zip(order, cot_refs))
            ]
            for copy in copies:
                copy.start()
            for s, k in order:
                grad[pl.ds(first_row(s, k), rows)] = grad_refs[s][k, 0]
            for copy in copies:
                copy.wait()

        base = lax.dot_general(cot[...], w_ref[...], LAST_BOTH, preferred_element_type=jnp.float32)
        for block in range(blocks_dev):
            at = slice(block * BLOCK, (block + 1) * BLOCK)
            a = a_ref[:, block].reshape(tile, RANKS)
            low = lax.dot_general(grad[at], a, LAST_BOTH, preferred_element_type=jnp.float32)
            out_ref[at] = (base[at] + low).astype(out_ref.dtype)

    grad_shape = (pipe_count, 1, rows, RANKS)
    return call(
        kernel,
        "input_gradient",
        2 * tok_dev * depth * (WIDTH + RANKS),
        12,
        grid=(data_count // planes,),
        in_specs=[
            SMEM,
            pl.BlockSpec((tile, WIDTH), lambda n: (n, 0)),
            pl.BlockSpec((planes, blocks_dev, down_rows, RANKS), lambda n: (n, 0, 0, 0)),
        ]
        + [pl.BlockSpec(grad_shape, lambda n: (0, 0, 0, 0))] * tensor_count
        + [HBM] * len(order),
        out_specs=pl.BlockSpec((tok_dev, tile), lambda n: (0, n)),
        out_shape=jax.ShapeDtypeStruct((tok_dev, depth), jnp.bfloat16),
        scratch_shapes=[
            pltpu.VMEM((tok_dev, WIDTH), jnp.bfloat16),
            pltpu.VMEM((tok_dev, RANKS), jnp.bfloat16),
            pltpu.SemaphoreType.DMA((len(order),)),
        ],
    )(place, weight, down, *grad_pieces, *[cot_pieces[s][k] for s, k in order])


def grad_down(tenant_of_block, slot_of_tenant, place, x_features, grad_pieces):
    data_count, down_rows, tok_dev = x_features.shape
    tensor_count = len(grad_pieces)
    pipe_count, _, rows, _ = grad_pieces[0].shape
    blocks_dev = tok_dev // BLOCK
    slots = slot_of_tenant.shape[0]

    def kernel(tenant_ref, slot_ref, place_ref, x_ref, *rest):
        grad_refs, (out_ref, grad) = rest[:tensor_count], rest[tensor_count:]
        for s in range(tensor_count):
            core = wrap(place_ref[2] - s, tensor_count)
            for k in range(pipe_count):
                chip = wrap(place_ref[1] - k, pipe_count)
                first = pl.multiple_of((chip * tensor_count + core) * rows, rows)
                for m in range(data_count):
                    data = wrap(place_ref[0] - m, data_count)
                    grad[data, pl.ds(first, rows)] = grad_refs[s][k, m]
        out_ref[...] = jnp.zeros(out_ref.shape, out_ref.dtype)
        for data in range(data_count):
            for block in range(blocks_dev):
                slot = slot_ref[tenant_ref[data * blocks_dev + block]]
                at = slice(block * BLOCK, (block + 1) * BLOCK)
                out_ref[slot] += jnp.dot(
                    x_ref[data, :, at], grad[data, at], preferred_element_type=jnp.float32
                )

    return call(
        kernel,
        "grad_down",
        2 * data_count * tok_dev * down_rows * RANKS,
        6,
        in_specs=[SMEM, SMEM, SMEM, VMEM] + [VMEM] * tensor_count,
        out_specs=VMEM,
        out_shape=jax.ShapeDtypeStruct((slots, down_rows, RANKS), jnp.float32),
        scratch_shapes=[pltpu.VMEM((data_count, tok_dev, RANKS), jnp.bfloat16)],
    )(tenant_of_block, slot_of_tenant, place, x_features, *grad_pieces)


def grad_up_pieces(place, low_pieces, cot_cols, data_count, up_rows):
    tensor_count = len(low_pieces)
    pipe_count, rows, _ = low_pieces[0].shape
    cols = cot_cols.shape[-1]
    tok_dev = tensor_count * pipe_count * rows
    blocks_dev = tok_dev // BLOCK
    group_half = tensor_count * pipe_count // 2

    def kernel(place_ref, cot_ref, *rest):
        low_refs, (out_ref, low, cot) = rest[:tensor_count], rest[tensor_count:]
        for s in range(tensor_count):
            core = wrap(place_ref[2] - s, tensor_count)
            for k in range(pipe_count):
                first = pl.multiple_of((k * tensor_count + core) * rows, rows)
                low[pl.ds(first, rows)] = low_refs[s][k]
                chip = wrap(place_ref[1] - k, pipe_count)
                first = pl.multiple_of((chip * tensor_count + core) * rows, rows)
                cot[pl.ds(first, rows)] = cot_ref[s * pipe_count + k]
        is_key = place_ref[1] * tensor_count + place_ref[2] < group_half
        for block in range(blocks_dev):
            at = slice(block * BLOCK, (block + 1) * BLOCK)
            both = lax.dot_general(low[at], cot[at], FIRST_BOTH, preferred_element_type=jnp.float32)
            half = jnp.where(is_key, both[:ADAPTER_RANK], both[ADAPTER_RANK:])
            half = half.astype(out_ref.dtype)
            for data in range(data_count):
                k = wrap(data - place_ref[0], data_count)
                out_ref[k, block] = half[data * up_rows : (data + 1) * up_rows]

    return call(
        kernel,
        "grad_up_pieces",
        2 * tok_dev * cols * RANKS,
        2,
        in_specs=[SMEM, VMEM] + [VMEM] * tensor_count,
        out_specs=VMEM,
        out_shape=jax.ShapeDtypeStruct((data_count, blocks_dev, up_rows, cols), jnp.bfloat16),
        scratch_shapes=[
            pltpu.VMEM((tok_dev, RANKS), jnp.bfloat16),
            pltpu.VMEM((tok_dev, cols), jnp.bfloat16),
        ],
    )(place, cot_cols, *low_pieces)


def grad_up(tenant_of_block, slot_of_tenant, place, pieces):
    data_count = len(pieces)
    blocks_dev, up_rows, cols = pieces[0].shape
    slots = slot_of_tenant.shape[0]

    def kernel(tenant_ref, slot_ref, place_ref, *rest):
        piece_refs, out_ref = rest[:data_count], rest[data_count]
        out_ref[...] = jnp.zeros(out_ref.shape, out_ref.dtype)
        for k in range(data_count):
            data = wrap(place_ref[0] - k, data_count)
            for block in range(blocks_dev):
                slot = slot_ref[tenant_ref[data * blocks_dev + block]]
                out_ref[slot] += piece_refs[k][block].astype(out_ref.dtype)

    return call(
        kernel,
        "grad_up",
        0,
        1,
        in_specs=[SMEM, SMEM, SMEM] + [VMEM] * data_count,
        out_specs=VMEM,
        out_shape=jax.ShapeDtypeStruct((slots, up_rows, cols), jnp.float32),
    )(tenant_of_block, slot_of_tenant, place, *pieces)


def halves(product, left, right):
    return jnp.concatenate([product(*pair) for pair in zip(left, right)], axis=1)


def body(
    tokens, key_value_weight, adapter_down, adapter_up, tenant_of_block, slot_of_tenant, cotangent
):
    data_count = lax.axis_size("dp")
    pipe_count = lax.axis_size("pipe")
    tensor_count = lax.axis_size("tensor")
    group_count = pipe_count * tensor_count
    at_data, at_pipe, at_tensor = (lax.axis_index(a) for a in ("dp", "pipe", "tensor"))
    place = jnp.stack([at_data, at_pipe, at_tensor]).astype(jnp.int32)
    my_group = at_pipe * tensor_count + at_tensor
    tok_dev, feature_count = tokens.shape
    blocks_dev = tok_dev // BLOCK
    rows = tok_dev // group_count
    down_rows = adapter_down.shape[1]
    up_rows = adapter_up.shape[1]

    own_block = (my_group * rows // BLOCK).reshape(1)
    a_send, b_send = pick(
        tenant_of_block, slot_of_tenant, place, own_block, adapter_down, adapter_up, data_count
    )
    b_came = [b_send[0]] + [shift(b_send[k], "dp", k) for k in range(1, data_count)]
    a_recv = lax.all_to_all(
        a_send.reshape(data_count, blocks_dev, down_rows, RANKS), "dp", 0, 0, tiled=True
    )

    cot_chips = [cotangent] + [shift(cotangent, "pipe", k) for k in range(1, pipe_count)]
    cot_pieces = [cot_chips] + [
        [shift(piece, "tensor", s) for piece in cot_chips] for s in range(1, tensor_count)
    ]

    x_send = tokens.T.reshape(data_count, down_rows, tok_dev)
    x_send, a_recv = lax.optimization_barrier((x_send, a_recv))
    x_recv = lax.all_to_all(x_send, "dp", 0, 0, tiled=True)

    tokens_by_group = tokens.reshape(pipe_count, tensor_count, rows, feature_count)
    base_send = base_product(place, tokens_by_group, key_value_weight, 1, tensor_count - 1)
    base_came = [shift(base_send[s - 1], "tensor", s) for s in range(1, tensor_count)]
    base_keep = base_product(place, tokens_by_group, key_value_weight, 0, 1)[0]
    base_chip = [
        sum([base_keep[k].astype(jnp.float32)] + [b[k].astype(jnp.float32) for b in base_came])
        for k in range(pipe_count)
    ]
    base_chip_came = [
        shift(base_chip[k].astype(jnp.bfloat16), "pipe", k) for k in range(1, pipe_count)
    ]
    base_rows = sum([base_chip[0]] + [b.astype(jnp.float32) for b in base_chip_came])

    b_own = jnp.concatenate(
        [lax.select_n(wrap(at_data - i, data_count), *b_came) for i in range(data_count)]
        if data_count > 1
        else b_came
    )
    left = lambda m: (m[:, :ADAPTER_RANK], m[:, ADAPTER_RANK:])
    wide = lambda m: (m[:, :KEY_WIDTH], m[:, KEY_WIDTH:])
    grad_rows = halves(
        lambda p, q: lax.dot_general(p, q, LAST_BOTH, preferred_element_type=jnp.float32),
        wide(cotangent),
        wide(b_own),
    ).astype(jnp.bfloat16)
    grad_data = jnp.stack([grad_rows] + [shift(grad_rows, "dp", k) for k in range(1, data_count)])
    grad_chips = jnp.stack([grad_data] + [shift(grad_data, "pipe", k) for k in range(1, pipe_count)])
    grad_pieces = [grad_chips] + [shift(grad_chips, "tensor", s) for s in range(1, tensor_count)]

    low_part = low_product(place, tokens, a_recv, pipe_count, tensor_count)
    low_core = sum(
        [low_part[0].astype(jnp.float32)]
        + [shift(low_part[s], "tensor", s).astype(jnp.float32) for s in range(1, tensor_count)]
    ).astype(jnp.bfloat16)
    low_sum = sum(
        [low_core.astype(jnp.float32)]
        + [shift(low_core, "pipe", k).astype(jnp.float32) for k in range(1, pipe_count)]
    ).astype(jnp.bfloat16)
    low_pieces = [low_sum] + [shift(low_sum, "tensor", s) for s in range(1, tensor_count)]
    low_rows = lax.dynamic_index_in_dim(low_sum, at_pipe, 0, False)
    lowrank = halves(
        lambda p, q: jnp.dot(p, q, preferred_element_type=jnp.float32), left(low_rows), wide(b_own)
    )
    key_value = (base_rows + lowrank).astype(jnp.bfloat16)

    col_count = WIDTH // group_count
    cot_cols = jnp.stack(
        [
            lax.dynamic_slice_in_dim(piece, my_group * col_count, col_count, 1)
            for pieces in cot_pieces
            for piece in pieces
        ]
    )
    up_pieces = grad_up_pieces(place, low_pieces, cot_cols, data_count, up_rows)
    up_came = [up_pieces[0]] + [shift(up_pieces[k], "dp", k) for k in range(1, data_count)]
    grad_b = grad_up(tenant_of_block, slot_of_tenant, place, up_came)

    input_grad = input_gradient(place, cot_pieces, key_value_weight, grad_pieces, a_recv)
    grad_a = grad_down(tenant_of_block, slot_of_tenant, place, x_recv, grad_pieces)
    return (key_value, input_grad, grad_a, grad_b)


def solution(mesh):
    placed = (
        P("dp", ("pipe", "tensor")),
        P(("pipe", "tensor"), None),
        P(None, ("pipe", "tensor", "dp"), None),
        P(None, "dp", None),
        P(),
        P(),
        P(("dp", "pipe", "tensor"), None),
    )
    return jax.shard_map(
        body,
        mesh=mesh,
        in_specs=placed,
        out_specs=(
            P(("dp", "pipe", "tensor"), None),
            P("dp", ("pipe", "tensor")),
            P(None, ("pipe", "tensor", "dp"), None),
            P(None, "dp", ("pipe", "tensor")),
        ),
        check_vma=False,
    )
```

time: 212 us -> 184 us (0.87)
  Pallas kernels: 0 us -> 34.2 us
  matrix products: 33.6 us -> 2.77 us
  blocking collectives: 29.7 us -> 0 us
  starting transfers between devices: 14.4 us -> 41 us
  between operations: 14.2 us -> 0.99 us
  waiting for transfers between devices: 93.3 us -> 82.1 us
  local copies, waits for them, and re-layouts: 21.8 us -> 16.3 us
    all_to_all x3 -> x2, waiting for transfers between devices: 92.6 us -> 0.01 us  [the longest x1 0.01 us: body(): lax.all_to_all(a_send.reshape(data_count, blocks_dev, down_rows, RANKS),...]
    ppermute x0 -> x29, waiting for transfers between devices: none -> 82.1 us  [shift(): lax.ppermute(piece, axis, [(i, (i + step) % count) for i in range(count)])]
    pallas_call x0 -> x8, Pallas kernels: none -> 34.2 us  [the longest x2 10.5 us: base_product(): call(kernel, 'base_product', 2 * pipe_count * count * rows * depth * WIDT...]
    dot_general x14 -> x4, matrix products: 33.6 us -> 2.77 us  [the longest x2 2.32 us: body(): lax.dot_general(p, q, LAST_BOTH, preferred_element_type=jnp.float32)]
    ppermute x0 -> x29, starting transfers between devices: none -> 30.1 us  [shift(): lax.ppermute(piece, axis, [(i, (i + step) % count) for i in range(count)])]
    all_gather x2 -> x0, blocking collectives: 19.3 us -> none  [the longest x1 9.81 us: body(): lax.all_gather(grad_rows, ('pipe', 'tensor'), axis=0, tiled=True)]
    all_to_all x1 -> x0, blocking collectives: 10.4 us -> none  [body(): lax.all_to_all(b_send, 'dp', split_axis=0, concat_axis=1, tiled=True)]
    convert_element_type x2 -> x0, local copies, waits for them, and re-layouts: 5 us -> none  [the longest x1 4.14 us: body(): grad_a_part.astype(jnp.bfloat16)]
  transfers between devices with their start and end apart: 5 -> 31, of which waited for: 3 -> 13; matrix products, arithmetic and copies ran while one was open for 26% -> 9% of each run, Pallas kernels for 0% -> 14%
where the time goes in v2:
time: 184 us; the launch traced here: 183 us
  waiting for transfers between devices  82.1 us (45%)
  starting transfers between devices  41 us (22%)
  Pallas kernels  34.2 us (19%)
  local copies, waits for them, and re-layouts  16.3 us (9%)
  other arithmetic  5.85 us (3%)
  matrix products  2.77 us (2%)
    ppermute x29, waiting for transfers between devices, shift(): lax.ppermute(piece, axis, [(i, (i + step) % count) for i in range(count)])  82.1 us
    ppermute x29, starting transfers between devices, shift(): lax.ppermute(piece, axis, [(i, (i + step) % count) for i in range(count)])  30.1 us
    unnamed x41, local copies, waits for them, and re-layouts  12.6 us
    pallas_call x2, Pallas kernels, base_product(): call(kernel, 'base_product', 2 * pipe_count * count * rows * depth * WIDT...  10.5 us
    pallas_call x1, Pallas kernels, input_gradient(): call(kernel, 'input_gradient', 2 * tok_dev * depth * (WIDTH + RANKS), 12,...  9.96 us
    all_to_all x1, starting transfers between devices, body(): lax.all_to_all(a_send.reshape(data_count, blocks_dev, down_rows, RANKS),...  6.45 us
    pallas_call x1, Pallas kernels, pick(): call(kernel, 'pick_rows', 0, 4, out_shape=(down_shape,) + (up_shape,) * d...  4.53 us
    all_to_all x1, starting transfers between devices, body(): x_recv = lax.all_to_all(x_send, 'dp', 0, 0, tiled=True)  4.45 us
  transfers between devices with their start and end apart: 31, of which 13 were waited for; matrix products, arithmetic and copies ran while one was open for 9% of the time, Pallas kernels for 14%

profile of v2, /device:TPU:0, one launch (start us, length us, event | category | flops | bytes accessed | tf_op | source)
XLA Modules:
  0.0 183.1 jit_solution(12859158087659388301)
XLA Ops:
  0.7 1.4 copy-done.4
  2.1 1.4 copy-done.5
  3.5 0.7 copy-done.12
  4.2 0.7 copy-done.14
  4.9 4.5 %pick_rows.1 = (bf16[32,256,128]{2,1,0:T(8,128)(2,1)S(1)}, bf16[16,2048]{1,0:T(8,128)(2,1)S(1)}, bf16[16,2048]{1,0:T(8,128)(2,1)S(1)}, bf16[16,2048]{1,0:T(8,128)(2,1)S(1)}, bf16[16,2048]{1,0:T(8,128)(2,1)S(1)}) custom-call(s32[32]{0:T(128)S(1)} %copy-done.12, s32[24]{0:T(128)S(1)} %copy-done.14, s32[3]{0:T(128)S(1)} %pad_add_fusion.place_ref, ...), custom_call_target="tpu_custom_call" | custom-call | bytes 4194304 | tf_op jit(solution)/shard_map/pick_rows/pallas_call | solution.py:74
  9.4 1.3 copy-done.3
  10.7 6.4 %all-to-all-start = ((bf16[4,8,256,128]{3,2,1,0:T(8,128)(2,1)}), bf16[4,8,256,128]{3,2,1,0:T(8,128)(2,1)}, u32[]{:S(2)}, u32[]{:S(2)}) async-start(bf16[4,8,256,128]{3,2,1,0:T(8,128)(2,1)} %bitcast.99), calls=%async_computation | async-start | bytes 4194304 | tf_op jit(solution)/shard_map/all_to_all | solution.py:340
  17.2 2.9 %collective-permute-start.9 = (bf16[16,2048]{1,0:T(8,128)(2,1)S(1)}, bf16[16,2048]{1,0:T(8,128)(2,1)S(1)}, u32[]{:S(2)}, u32[]{:S(2)}) collective-permute-start(bf16[16,2048]{1,0:T(8,128)(2,1)S(1)} %get-tuple-element.15), channel_id=1, source_target_pairs={{0,16},{8,24},{16,0},{24,8},{1,17},{9,25},{17,1},{25,9},{2,18},{10... | collective-permute-start | bytes 196616 | tf_op jit(solution)/shard_map/ppermute | solution.py:35
  20.1 1.5 collective-permute-start.10
  21.6 0.6 collective-permute-start.8
  22.1 5.6 %base_product.3 = bf16[1,4,128,2048]{3,2,1,0:T(8,128)(2,1)} custom-call(s32[3]{0:T(128)S(1)} %pad_add_fusion.place_ref, bf16[4,2,128,1024]{3,2,1,0:T(8,128)(2,1)S(1)} %bitcast.96, bf16[1024,2048]{1,0:T(8,128)(2,1)} %w_ref.5), custom_call_target="tpu_custom_call" | custom-call | flops 2147483648 | bytes 8388608 | tf_op jit(solution)/shard_map/base_product/pallas_call | solution.py:100
  27.8 42.5 %collective-permute-done.9 = bf16[16,2048]{1,0:T(8,128)(2,1)S(1)} collective-permute-done((bf16[16,2048]{1,0:T(8,128)(2,1)S(1)}, bf16[16,2048]{1,0:T(8,128)(2,1)S(1)}, u32[]{:S(2)}, u32[]{:S(2)}) %collective-permute-start.9) | collective-permute-done | bytes 65568 | tf_op jit(solution)/shard_map/ppermute | solution.py:35
  70.4 1.2 convolution_convert_fusion
  71.5 1.2 convolution_convert_fusion.1
  73.0 1.5 collective-permute-start.13
  74.6 1.3 collective-permute-start.12
  75.8 0.6 collective-permute-start.11
  76.4 0.6 collective-permute-done.13
  77.0 2.7 %collective-permute-done.12 = bf16[128,128]{1,0:T(8,128)(2,1)S(1)} collective-permute-done((bf16[128,128]{1,0:T(8,128)(2,1)S(1)}, bf16[128,128]{1,0:T(8,128)(2,1)S(1)}, u32[]{:S(2)}, u32[]{:S(2)}) %collective-permute-start.12) | collective-permute-done | bytes 32800 | tf_op jit(solution)/shard_map/ppermute | solution.py:35
  79.7 1.8 collective-permute-done.11
  81.6 2.5 %collective-permute-start.16 = (bf16[4,128,128]{2,1,0:T(8,128)(2,1)S(1)}, bf16[4,128,128]{2,1,0:T(8,128)(2,1)S(1)}, u32[]{:S(2)}, u32[]{:S(2)}) collective-permute-start(bf16[4,128,128]{2,1,0:T(8,128)(2,1)S(1)} %pad_maximum_fusion.2), channel_id=1, source_target_pairs={{0,6},{2,0},{4,2},{6,4},{1,7},{3,1},{5,3},{7,5},{8,14},{10,8},{12,... | collective-permute-start | bytes 393224 | tf_op jit(solution)/shard_map/ppermute | solution.py:35
  84.1 0.5 collective-permute-start.15
  84.6 0.6 collective-permute-start.18
  85.2 0.9 collective-permute-start.19
  86.1 1.9 %collective-permute-done.16 = bf16[4,128,128]{2,1,0:T(8,128)(2,1)S(1)} collective-permute-done((bf16[4,128,128]{2,1,0:T(8,128)(2,1)S(1)}, bf16[4,128,128]{2,1,0:T(8,128)(2,1)S(1)}, u32[]{:S(2)}, u32[]{:S(2)}) %collective-permute-start.16) | collective-permute-done | bytes 131104 | tf_op jit(solution)/shard_map/ppermute | solution.py:35
  88.1 3.4 %collective-permute-start.20 = (bf16[128,2048]{1,0:T(8,128)(2,1)}, bf16[128,2048]{1,0:T(8,128)(2,1)}, u32[]{:S(2)}, u32[]{:S(2)}) collective-permute-start(bf16[128,2048]{1,0:T(8,128)(2,1)} %rest_2_.1), channel_id=1, source_target_pairs={{0,6},{2,0},{4,2},{6,4},{1,7},{3,1},{5,3},{7,5},{8,14},{10,8},{12,... | collective-permute-start | bytes 1572872 | tf_op jit(solution)/shard_map/ppermute | solution.py:35
  91.5 7.3 %collective-permute-done.15 = bf16[4,128,128]{2,1,0:T(8,128)(2,1)S(1)} collective-permute-done((bf16[4,128,128]{2,1,0:T(8,128)(2,1)S(1)}, bf16[4,128,128]{2,1,0:T(8,128)(2,1)S(1)}, u32[]{:S(2)}, u32[]{:S(2)}) %collective-permute-start.15) | collective-permute-done | bytes 131104 | tf_op jit(solution)/shard_map/ppermute | solution.py:35
  98.8 4.8 %base_product.2 = bf16[1,4,128,2048]{3,2,1,0:T(8,128)(2,1)S(1)} custom-call(s32[3]{0:T(128)S(1)} %pad_add_fusion.place_ref, bf16[4,2,128,1024]{3,2,1,0:T(8,128)(2,1)S(1)} %bitcast.97, bf16[1024,2048]{1,0:T(8,128)(2,1)} %w_ref.5), custom_call_target="tpu_custom_call" | custom-call | flops 2147483648 | bytes 8388608 | tf_op jit(solution)/shard_map/base_product/pallas_call | solution.py:100
  103.7 1.3 copy-done.1
  105.0 2.6 %copy.14 = bf16[1024,1024]{1,0:T(8,128)(2,1)} copy(bf16[1024,1024]{0,1:T(8,128)(2,1)S(1)} %bitcast.98) | data formatting | bytes 4194304 | tf_op jit(solution)/shard_map/transpose | solution.py:349
  107.5 0.8 bitcast_dynamic-update-slice_fusion.7
  108.4 3.3 %collective-permute-done.14 = bf16[4,128,128]{2,1,0:T(8,128)(2,1)} collective-permute-done((bf16[4,128,128]{2,1,0:T(8,128)(2,1)S(1)}, bf16[4,128,128]{2,1,0:T(8,128)(2,1)}, u32[]{:S(2)}, u32[]{:S(2)}) %collective-permute-start.14) | collective-permute-done | bytes 131104 | tf_op jit(solution)/shard_map/ppermute | solution.py:35
  111.8 0.6 collective-permute-start.22
  112.4 1.0 pad_maximum_fusion.rest_0_
  113.5 0.5 collective-permute-start.24
  114.0 0.8 bitcast_dynamic-update-slice_fusion.6
  114.8 0.8 bitcast_dynamic-update-slice_fusion.5
  115.7 0.8 bitcast_dynamic-update-slice_fusion.4
  116.6 0.8 copy-done.6
  117.4 0.8 copy-done.8
  118.3 0.8 copy-done.10
  119.1 4.5 %all-to-all-start.1 = ((bf16[4,256,1024]{2,1,0:T(8,128)(2,1)}), bf16[4,256,1024]{2,1,0:T(8,128)(2,1)}, u32[]{:S(2)}, u32[]{:S(2)}) async-start(bf16[4,256,1024]{2,1,0:T(8,128)(2,1)} %bitcast.100), calls=%async_computation.1 | async-start | bytes 4194304 | tf_op jit(solution)/shard_map/all_to_all | solution.py:351
  123.5 0.9 bitcast_dynamic-update-slice_fusion.cot_ref
  124.4 2.5 %low_product.1 = bf16[2,4,128,128]{3,2,1,0:T(8,128)(2,1)S(1)} custom-call(s32[3]{0:T(128)S(1)} %pad_add_fusion.place_ref, bf16[1024,1024]{1,0:T(8,128)(2,1)S(1)} %copy-done, bf16[4,8,256,128]{3,2,1,0:T(8,128)(2,1)} %all-to-all-done.a_ref), custom_call_target="tpu_custom_call" | custom-call | flops 268435456 | bytes 4718592 | tf_op jit(solution)/shard_map/low_product/pallas_call | solution.py:135
  126.9 0.5 collective-permute-start.4
  127.4 2.0 %fusion.3 = (bf16[128,2048]{1,0:T(8,128)(2,1)S(1)}, bf16[128,2048]{1,0:T(8,128)(2,1)S(1)}, bf16[128,2048]{1,0:T(8,128)(2,1)S(1)}) fusion(bf16[4,128,2048]{2,1,0:T(8,128)(2,1)} %collective-permute-done, bf16[1,4,128,2048]{3,2,1,0:T(8,128)(2,1)S(1)} %copy-done.2), kind=kLoop, calls=%fused_computation.9 | loop fusion | flops 3145728 | bytes 4718592 | tf_op jit(solution)/shard_map/convert_element_type | solution.py:362
  129.8 1.5 collective-permute-start.2
  131.4 1.7 collective-permute-start.7
  133.1 1.5 collective-permute-start.6
  134.6 10.0 %input_gradient.1 = bf16[1024,1024]{1,0:T(8,128)(2,1)} custom-call(s32[3]{0:T(128)S(1)} %pad_add_fusion.place_ref, bf16[1024,2048]{1,0:T(8,128)(2,1)} %w_ref.5, bf16[4,8,256,128]{3,2,1,0:T(8,128)(2,1)} %all-to-all-done.a_ref, bf16[4,4,128,128]{3,2,1,0:T(8,128)(2,1)S(1)} %pad_maximum_fusion.rest_0_, bf16[4,4,128,128]{3,2,1,0:T(8,128)(2,1)} %collective-permute-done.17.rest_1_, ...), custom_call_target="tpu_custom_call" | custom-call | flops 4563402752 | bytes 12582912 | tf_op jit(solution)/shard_map/input_gradient/pallas_call | solution.py:186
  144.5 2.5 %collective-permute-done.7 = bf16[4,128,128]{2,1,0:T(8,128)(2,1)S(1)} collective-permute-done((bf16[4,128,128]{2,1,0:T(8,128)(2,1)S(1)}, bf16[4,128,128]{2,1,0:T(8,128)(2,1)S(1)}, u32[]{:S(2)}, u32[]{:S(2)}) %collective-permute-start.7) | collective-permute-done | bytes 131104 | tf_op jit(solution)/shard_map/ppermute | solution.py:35
  147.0 1.3 collective-permute-start.1
  148.4 2.3 %collective-permute-done.5 = bf16[4,128,128]{2,1,0:T(8,128)(2,1)S(1)} collective-permute-done((bf16[4,128,128]{2,1,0:T(8,128)(2,1)S(1)}, bf16[4,128,128]{2,1,0:T(8,128)(2,1)S(1)}, u32[]{:S(2)}, u32[]{:S(2)}) %collective-permute-start.5) | collective-permute-done | bytes 131104 | tf_op jit(solution)/shard_map/ppermute | solution.py:35
  151.3 0.8 collective-permute-done.25.rest_1_
  152.2 0.9 grad_up_pieces.1
  153.1 1.9 %collective-permute-start.26 = (bf16[8,16,256]{2,1,0:T(8,128)(2,1)S(1)}, bf16[8,16,256]{2,1,0:T(8,128)(2,1)S(1)}, u32[]{:S(2)}, u32[]{:S(2)}) collective-permute-start(bf16[8,16,256]{2,1,0:T(8,128)(2,1)S(1)} %get-tuple-element.23), channel_id=1, source_target_pairs={{0,8},{8,16},{16,24},{24,0},{1,9},{9,17},{17,25},{25,1},{2,10},{10... | collective-permute-start | bytes 196616 | tf_op jit(solution)/shard_map/ppermute | solution.py:35
  155.0 2.4 %collective-permute-start.27 = (bf16[8,16,256]{2,1,0:T(8,128)(2,1)S(1)}, bf16[8,16,256]{2,1,0:T(8,128)(2,1)S(1)}, u32[]{:S(2)}, u32[]{:S(2)}) collective-permute-start(bf16[8,16,256]{2,1,0:T(8,128)(2,1)S(1)} %get-tuple-element.22), channel_id=1, source_target_pairs={{0,16},{8,24},{16,0},{24,8},{1,17},{9,25},{17,1},{25,9},{2,18},{10... | collective-permute-start | bytes 196616 | tf_op jit(solution)/shard_map/ppermute | solution.py:35
  157.3 1.5 collective-permute-start.28
  158.8 2.4 %collective-permute-done.1 = bf16[128,2048]{1,0:T(8,128)(2,1)S(1)} collective-permute-done((bf16[128,2048]{1,0:T(8,128)(2,1)S(1)}, bf16[128,2048]{1,0:T(8,128)(2,1)S(1)}, u32[]{:S(2)}, u32[]{:S(2)}) %collective-permute-start.1) | collective-permute-done | bytes 524320 | tf_op jit(solution)/shard_map/ppermute | solution.py:35
  161.2 2.3 %fusion = bf16[128,2048]{1,0:T(8,128)(2,1)} fusion(f32[128,1024]{1,0:T(8,128)S(1)} %fusion.11, f32[128,1024]{1,0:T(8,128)S(1)} %fusion.14, bf16[128,2048]{1,0:T(8,128)(2,1)S(1)} %collective-permute-done.3, bf16[128,2048]{1,0:T(8,128)(2,1)S(1)} %collective-permute-done.2, bf16[128,2048]{1,0:T(8,128)(2,1)S(1)} %collective-permute-done.1, ...), kind=kLoop, calls=%fused_computation.3 | loop fusion | flops 3145728 | bytes 4194304 | tf_op jit(solution)/shard_map/convert_element_type | solution.py:396
  163.5 0.7 collective-permute-done.26.rest_1_
  164.2 13.0 %collective-permute-done.27.rest_2_ = bf16[8,16,256]{2,1,0:T(8,128)(2,1)S(1)} collective-permute-done((bf16[8,16,256]{2,1,0:T(8,128)(2,1)S(1)}, bf16[8,16,256]{2,1,0:T(8,128)(2,1)S(1)}, u32[]{:S(2)}, u32[]{:S(2)}) %collective-permute-start.27) | collective-permute-done | bytes 65568 | tf_op jit(solution)/shard_map/ppermute | solution.py:35
  177.2 1.5 grad_up.1
  178.7 4.4 %grad_down.1 = f32[24,256,128]{2,1,0:T(8,128)} custom-call(s32[32]{0:T(128)S(1)} %copy-done.13, s32[24]{0:T(128)S(1)} %copy-done.15, s32[3]{0:T(128)S(1)} %pad_add_fusion.place_ref, bf16[4,256,1024]{2,1,0:T(8,128)(2,1)} %all-to-all-done.1.x_ref, bf16[4,4,128,128]{3,2,1,0:T(8,128)(2,1)S(1)} %pad_maximum_fusion.rest_0_, ...), custom_call_target="tpu_custom_call" | custom-call | flops 268435456 | bytes 6291456 | tf_op jit(solution)/shard_map/grad_down/pallas_call | solution.py:235
  (69 shorter events, 2.0 us)
Async XLA Ops:
  0.7 1.4 copy-start.4
  2.1 1.4 copy-start.5
  3.5 0.7 copy-start.12
  4.2 0.7 copy-start.14
  9.4 1.3 copy-start.3
  10.7 11.4 %copy-start = (bf16[1024,1024]{1,0:T(8,128)(2,1)S(1)}, bf16[1024,1024]{1,0:T(8,128)(2,1)}, u32[]{:S(2)}) copy-start(bf16[1024,1024]{1,0:T(8,128)(2,1)} %x_ref.1) | copy-start | bytes 6291460
  10.7 108.3 %all-to-all-start = ((bf16[4,8,256,128]{3,2,1,0:T(8,128)(2,1)}), bf16[4,8,256,128]{3,2,1,0:T(8,128)(2,1)}, u32[]{:S(2)}, u32[]{:S(2)}) async-start(bf16[4,8,256,128]{3,2,1,0:T(8,128)(2,1)} %bitcast.99), calls=%async_computation | async-start | bytes 4194304 | tf_op jit(solution)/shard_map/all_to_all | solution.py:340
  17.2 53.1 %collective-permute-start.9 = (bf16[16,2048]{1,0:T(8,128)(2,1)S(1)}, bf16[16,2048]{1,0:T(8,128)(2,1)S(1)}, u32[]{:S(2)}, u32[]{:S(2)}) collective-permute-start(bf16[16,2048]{1,0:T(8,128)(2,1)S(1)} %get-tuple-element.15), channel_id=1, source_target_pairs={{0,16},{8,24},{16,0},{24,8},{1,17},{9,25},{17,1},{25,9},{2,18},{10... | collective-permute-start | bytes 196616 | tf_op jit(solution)/shard_map/ppermute | solution.py:35
  20.1 50.2 %collective-permute-start.10 = (bf16[16,2048]{1,0:T(8,128)(2,1)S(1)}, bf16[16,2048]{1,0:T(8,128)(2,1)S(1)}, u32[]{:S(2)}, u32[]{:S(2)}) collective-permute-start(bf16[16,2048]{1,0:T(8,128)(2,1)S(1)} %get-tuple-element.16), channel_id=1, source_target_pairs={{0,24},{8,0},{16,8},{24,16},{1,25},{9,1},{17,9},{25,17},{2,26},{10... | collective-permute-start | bytes 196616 | tf_op jit(solution)/shard_map/ppermute | solution.py:35
  21.6 48.7 %collective-permute-start.8 = (bf16[16,2048]{1,0:T(8,128)(2,1)S(1)}, bf16[16,2048]{1,0:T(8,128)(2,1)S(1)}, u32[]{:S(2)}, u32[]{:S(2)}) collective-permute-start(bf16[16,2048]{1,0:T(8,128)(2,1)S(1)} %get-tuple-element.14), channel_id=1, source_target_pairs={{0,8},{8,16},{16,24},{24,0},{1,9},{9,17},{17,25},{25,1},{2,10},{10... | collective-permute-start | bytes 196616 | tf_op jit(solution)/shard_map/ppermute | solution.py:35
  27.8 99.6 %collective-permute-start = (bf16[4,128,2048]{2,1,0:T(8,128)(2,1)}, bf16[4,128,2048]{2,1,0:T(8,128)(2,1)}, u32[]{:S(2)}, u32[]{:S(2)}) collective-permute-start(bf16[4,128,2048]{2,1,0:T(8,128)(2,1)} %bitcast.5), channel_id=1, source_target_pairs={{0,1},{1,0},{2,3},{3,2},{4,5},{5,4},{6,7},{7,6},{8,9},{9,8},{10,11... | collective-permute-start | bytes 6291464 | tf_op jit(solution)/shard_map/ppermute | solution.py:35
  73.0 4.0 %collective-permute-start.13 = (bf16[128,128]{1,0:T(8,128)(2,1)S(1)}, bf16[128,128]{1,0:T(8,128)(2,1)S(1)}, u32[]{:S(2)}, u32[]{:S(2)}) collective-permute-start(bf16[128,128]{1,0:T(8,128)(2,1)S(1)} %pad_maximum_fusion.3), channel_id=1, source_target_pairs={{0,24},{8,0},{16,8},{24,16},{1,25},{9,1},{17,9},{25,17},{2,26},{10... | collective-permute-start | bytes 98312 | tf_op jit(solution)/shard_map/ppermute | solution.py:35
  74.6 5.2 %collective-permute-start.12 = (bf16[128,128]{1,0:T(8,128)(2,1)S(1)}, bf16[128,128]{1,0:T(8,128)(2,1)S(1)}, u32[]{:S(2)}, u32[]{:S(2)}) collective-permute-start(bf16[128,128]{1,0:T(8,128)(2,1)S(1)} %pad_maximum_fusion.3), channel_id=1, source_target_pairs={{0,16},{8,24},{16,0},{24,8},{1,17},{9,25},{17,1},{25,9},{2,18},{10... | collective-permute-start | bytes 98312 | tf_op jit(solution)/shard_map/ppermute | solution.py:35
  75.8 5.7 %collective-permute-start.11 = (bf16[128,128]{1,0:T(8,128)(2,1)S(1)}, bf16[128,128]{1,0:T(8,128)(2,1)S(1)}, u32[]{:S(2)}, u32[]{:S(2)}) collective-permute-start(bf16[128,128]{1,0:T(8,128)(2,1)S(1)} %pad_maximum_fusion.3), channel_id=1, source_target_pairs={{0,8},{8,16},{16,24},{24,0},{1,9},{9,17},{17,25},{25,1},{2,10},{10... | collective-permute-start | bytes 98312 | tf_op jit(solution)/shard_map/ppermute | solution.py:35
  81.6 6.5 %collective-permute-start.16 = (bf16[4,128,128]{2,1,0:T(8,128)(2,1)S(1)}, bf16[4,128,128]{2,1,0:T(8,128)(2,1)S(1)}, u32[]{:S(2)}, u32[]{:S(2)}) collective-permute-start(bf16[4,128,128]{2,1,0:T(8,128)(2,1)S(1)} %pad_maximum_fusion.2), channel_id=1, source_target_pairs={{0,6},{2,0},{4,2},{6,4},{1,7},{3,1},{5,3},{7,5},{8,14},{10,8},{12,... | collective-permute-start | bytes 393224 | tf_op jit(solution)/shard_map/ppermute | solution.py:35
  84.1 14.7 %collective-permute-start.15 = (bf16[4,128,128]{2,1,0:T(8,128)(2,1)S(1)}, bf16[4,128,128]{2,1,0:T(8,128)(2,1)S(1)}, u32[]{:S(2)}, u32[]{:S(2)}) collective-permute-start(bf16[4,128,128]{2,1,0:T(8,128)(2,1)S(1)} %pad_maximum_fusion.2), channel_id=1, source_target_pairs={{0,4},{2,6},{4,0},{6,2},{1,5},{3,7},{5,1},{7,3},{8,12},{10,14},{12... | collective-permute-start | bytes 393224 | tf_op jit(solution)/shard_map/ppermute | solution.py:35
  84.6 27.2 %collective-permute-start.18 = (bf16[128,2048]{1,0:T(8,128)(2,1)}, bf16[128,2048]{1,0:T(8,128)(2,1)}, u32[]{:S(2)}, u32[]{:S(2)}) collective-permute-start(bf16[128,2048]{1,0:T(8,128)(2,1)} %rest_2_.1), channel_id=1, source_target_pairs={{0,2},{2,4},{4,6},{6,0},{1,3},{3,5},{5,7},{7,1},{8,10},{10,12},{12... | collective-permute-start | bytes 1572872 | tf_op jit(solution)/shard_map/ppermute | solution.py:35
  85.2 28.2 %collective-permute-start.19 = (bf16[128,2048]{1,0:T(8,128)(2,1)}, bf16[128,2048]{1,0:T(8,128)(2,1)}, u32[]{:S(2)}, u32[]{:S(2)}) collective-permute-start(bf16[128,2048]{1,0:T(8,128)(2,1)} %rest_2_.1), channel_id=1, source_target_pairs={{0,4},{2,6},{4,0},{6,2},{1,5},{3,7},{5,1},{7,3},{8,12},{10,14},{12... | collective-permute-start | bytes 1572872 | tf_op jit(solution)/shard_map/ppermute | solution.py:35
  88.1 25.4 %collective-permute-start.20 = (bf16[128,2048]{1,0:T(8,128)(2,1)}, bf16[128,2048]{1,0:T(8,128)(2,1)}, u32[]{:S(2)}, u32[]{:S(2)}) collective-permute-start(bf16[128,2048]{1,0:T(8,128)(2,1)} %rest_2_.1), channel_id=1, source_target_pairs={{0,6},{2,0},{4,2},{6,4},{1,7},{3,1},{5,3},{7,5},{8,14},{10,8},{12,... | collective-permute-start | bytes 1572872 | tf_op jit(solution)/shard_map/ppermute | solution.py:35
  98.8 4.9 %copy-start.16 = (bf16[4,128,128]{2,1,0:T(8,128)(2,1)}, bf16[4,128,128]{2,1,0:T(8,128)(2,1)S(1)}, u32[]{:S(2)}) copy-start(bf16[4,128,128]{2,1,0:T(8,128)(2,1)S(1)} %collective-permute-done.15) | copy-start | bytes 393220
  98.8 12.9 %collective-permute-start.14 = (bf16[4,128,128]{2,1,0:T(8,128)(2,1)S(1)}, bf16[4,128,128]{2,1,0:T(8,128)(2,1)}, u32[]{:S(2)}, u32[]{:S(2)}) collective-permute-start(bf16[4,128,128]{2,1,0:T(8,128)(2,1)S(1)} %pad_maximum_fusion.2), channel_id=1, source_target_pairs={{0,2},{2,4},{4,6},{6,0},{1,3},{3,5},{5,7},{7,1},{8,10},{10,12},{12... | collective-permute-start | bytes 393224 | tf_op jit(solution)/shard_map/ppermute | solution.py:35
  103.7 1.3 copy-start.1
  111.7 4.8 %collective-permute-start.21 = (bf16[128,2048]{1,0:T(8,128)(2,1)}, bf16[128,2048]{1,0:T(8,128)(2,1)S(1)}, u32[]{:S(2)}, u32[]{:S(2)}) collective-permute-start(bf16[128,2048]{1,0:T(8,128)(2,1)} %rest_2_.1), channel_id=1, source_target_pairs={{0,1},{1,0},{2,3},{3,2},{4,5},{5,4},{6,7},{7,6},{8,9},{9,8},{10,11... | collective-permute-start | bytes 1572872 | tf_op jit(solution)/shard_map/ppermute | solution.py:35
  111.8 5.6 %collective-permute-start.22 = (bf16[128,2048]{1,0:T(8,128)(2,1)}, bf16[128,2048]{1,0:T(8,128)(2,1)S(1)}, u32[]{:S(2)}, u32[]{:S(2)}) collective-permute-start(bf16[128,2048]{1,0:T(8,128)(2,1)} %collective-permute-done.18.rest_3_), channel_id=1, source_target_pairs={{0,1},{1,0},{2,3},{3,2},{4,5},{5,4},{6,7},{7,6},{8,9},{9,8},{10,11... | collective-permute-start | bytes 1572872 | tf_op jit(solution)/shard_map/ppermute | solution.py:35
  113.4 4.8 %collective-permute-start.23 = (bf16[128,2048]{1,0:T(8,128)(2,1)}, bf16[128,2048]{1,0:T(8,128)(2,1)S(1)}, u32[]{:S(2)}, u32[]{:S(2)}) collective-permute-start(bf16[128,2048]{1,0:T(8,128)(2,1)} %collective-permute-done.19.rest_4_), channel_id=1, source_target_pairs={{0,1},{1,0},{2,3},{3,2},{4,5},{5,4},{6,7},{7,6},{8,9},{9,8},{10,11... | collective-permute-start | bytes 1572872 | tf_op jit(solution)/shard_map/ppermute | solution.py:35
  113.5 10.0 %collective-permute-start.24 = (bf16[128,2048]{1,0:T(8,128)(2,1)}, bf16[128,2048]{1,0:T(8,128)(2,1)}, u32[]{:S(2)}, u32[]{:S(2)}) collective-permute-start(bf16[128,2048]{1,0:T(8,128)(2,1)} %collective-permute-done.20.rest_5_), channel_id=1, source_target_pairs={{0,1},{1,0},{2,3},{3,2},{4,5},{5,4},{6,7},{7,6},{8,9},{9,8},{10,11... | collective-permute-start | bytes 1572872 | tf_op jit(solution)/shard_map/ppermute | solution.py:35
  116.5 18.0 %collective-permute-start.17 = (bf16[4,4,128,128]{3,2,1,0:T(8,128)(2,1)S(1)}, bf16[4,4,128,128]{3,2,1,0:T(8,128)(2,1)}, u32[]{:S(2)}, u32[]{:S(2)}) collective-permute-start(bf16[4,4,128,128]{3,2,1,0:T(8,128)(2,1)S(1)} %pad_maximum_fusion.rest_0_), channel_id=1, source_target_pairs={{0,1},{1,0},{2,3},{3,2},{4,5},{5,4},{6,7},{7,6},{8,9},{9,8},{10,11... | collective-permute-start | bytes 1572872 | tf_op jit(solution)/shard_map/ppermute | solution.py:35
  116.6 0.8 copy-start.6
  117.4 0.8 copy-start.8
  118.2 0.8 copy-start.10
  119.1 59.7 %all-to-all-start.1 = ((bf16[4,256,1024]{2,1,0:T(8,128)(2,1)}), bf16[4,256,1024]{2,1,0:T(8,128)(2,1)}, u32[]{:S(2)}, u32[]{:S(2)}) async-start(bf16[4,256,1024]{2,1,0:T(8,128)(2,1)} %bitcast.100), calls=%async_computation.1 | async-start | bytes 4194304 | tf_op jit(solution)/shard_map/all_to_all | solution.py:351
  124.4 3.0 %copy-start.2 = (bf16[1,4,128,2048]{3,2,1,0:T(8,128)(2,1)S(1)}, bf16[1,4,128,2048]{3,2,1,0:T(8,128)(2,1)}, u32[]{:S(2)}) copy-start(bf16[1,4,128,2048]{3,2,1,0:T(8,128)(2,1)} %copy-done.1) | copy-start | bytes 6291460
  126.9 7.7 %copy-start.7 = (bf16[128,2048]{1,0:T(8,128)(2,1)S(1)}, bf16[128,2048]{1,0:T(8,128)(2,1)}, u32[]{:S(2)}) copy-start(bf16[128,2048]{1,0:T(8,128)(2,1)} %copy-done.6) | copy-start | bytes 1572868
  126.9 7.6 %copy-start.9 = (bf16[128,2048]{1,0:T(8,128)(2,1)S(1)}, bf16[128,2048]{1,0:T(8,128)(2,1)}, u32[]{:S(2)}) copy-start(bf16[128,2048]{1,0:T(8,128)(2,1)} %copy-done.8) | copy-start | bytes 1572868
  126.9 7.6 %copy-start.11 = (bf16[128,2048]{1,0:T(8,128)(2,1)S(1)}, bf16[128,2048]{1,0:T(8,128)(2,1)}, u32[]{:S(2)}) copy-start(bf16[128,2048]{1,0:T(8,128)(2,1)} %copy-done.10) | copy-start | bytes 1572868
  126.9 4.4 %collective-permute-start.4 = (bf16[4,128,128]{2,1,0:T(8,128)(2,1)S(1)}, bf16[4,128,128]{2,1,0:T(8,128)(2,1)S(1)}, u32[]{:S(2)}, u32[]{:S(2)}) collective-permute-start(bf16[4,128,128]{2,1,0:T(8,128)(2,1)S(1)} %slice_bitcast_fusion.8), channel_id=1, source_target_pairs={{0,1},{1,0},{2,3},{3,2},{4,5},{5,4},{6,7},{7,6},{8,9},{9,8},{10,11... | collective-permute-start | bytes 393224 | tf_op jit(solution)/shard_map/ppermute | solution.py:35
  129.4 27.9 %collective-permute-start.3 = (bf16[128,2048]{1,0:T(8,128)(2,1)S(1)}, bf16[128,2048]{1,0:T(8,128)(2,1)S(1)}, u32[]{:S(2)}, u32[]{:S(2)}) collective-permute-start(bf16[128,2048]{1,0:T(8,128)(2,1)S(1)} %get-tuple-element.19), channel_id=1, source_target_pairs={{0,6},{2,0},{4,2},{6,4},{1,7},{3,1},{5,3},{7,5},{8,14},{10,8},{12,... | collective-permute-start | bytes 1572872 | tf_op jit(solution)/shard_map/ppermute | solution.py:35
  129.8 29.0 %collective-permute-start.2 = (bf16[128,2048]{1,0:T(8,128)(2,1)S(1)}, bf16[128,2048]{1,0:T(8,128)(2,1)S(1)}, u32[]{:S(2)}, u32[]{:S(2)}) collective-permute-start(bf16[128,2048]{1,0:T(8,128)(2,1)S(1)} %get-tuple-element.20), channel_id=1, source_target_pairs={{0,4},{2,6},{4,0},{6,2},{1,5},{3,7},{5,1},{7,3},{8,12},{10,14},{12... | collective-permute-start | bytes 1572872 | tf_op jit(solution)/shard_map/ppermute | solution.py:35
  131.4 15.7 %collective-permute-start.7 = (bf16[4,128,128]{2,1,0:T(8,128)(2,1)S(1)}, bf16[4,128,128]{2,1,0:T(8,128)(2,1)S(1)}, u32[]{:S(2)}, u32[]{:S(2)}) collective-permute-start(bf16[4,128,128]{2,1,0:T(8,128)(2,1)S(1)} %fusion.7), channel_id=1, source_target_pairs={{0,6},{2,0},{4,2},{6,4},{1,7},{3,1},{5,3},{7,5},{8,14},{10,8},{12,... | collective-permute-start | bytes 393224 | tf_op jit(solution)/shard_map/ppermute | solution.py:35
  133.1 15.3 %collective-permute-start.6 = (bf16[4,128,128]{2,1,0:T(8,128)(2,1)S(1)}, bf16[4,128,128]{2,1,0:T(8,128)(2,1)S(1)}, u32[]{:S(2)}, u32[]{:S(2)}) collective-permute-start(bf16[4,128,128]{2,1,0:T(8,128)(2,1)S(1)} %fusion.7), channel_id=1, source_target_pairs={{0,4},{2,6},{4,0},{6,2},{1,5},{3,7},{5,1},{7,3},{8,12},{10,14},{12... | collective-permute-start | bytes 393224 | tf_op jit(solution)/shard_map/ppermute | solution.py:35
  134.5 16.1 %collective-permute-start.5 = (bf16[4,128,128]{2,1,0:T(8,128)(2,1)S(1)}, bf16[4,128,128]{2,1,0:T(8,128)(2,1)S(1)}, u32[]{:S(2)}, u32[]{:S(2)}) collective-permute-start(bf16[4,128,128]{2,1,0:T(8,128)(2,1)S(1)} %fusion.7), channel_id=1, source_target_pairs={{0,2},{2,4},{4,6},{6,0},{1,3},{3,5},{5,7},{7,1},{8,10},{10,12},{12... | collective-permute-start | bytes 393224 | tf_op jit(solution)/shard_map/ppermute | solution.py:35
  147.0 14.2 %collective-permute-start.1 = (bf16[128,2048]{1,0:T(8,128)(2,1)S(1)}, bf16[128,2048]{1,0:T(8,128)(2,1)S(1)}, u32[]{:S(2)}, u32[]{:S(2)}) collective-permute-start(bf16[128,2048]{1,0:T(8,128)(2,1)S(1)} %get-tuple-element.18), channel_id=1, source_target_pairs={{0,2},{2,4},{4,6},{6,0},{1,3},{3,5},{5,7},{7,1},{8,10},{10,12},{12... | collective-permute-start | bytes 1572872 | tf_op jit(solution)/shard_map/ppermute | solution.py:35
  150.7 1.4 collective-permute-start.25
  153.1 11.1 %collective-permute-start.26 = (bf16[8,16,256]{2,1,0:T(8,128)(2,1)S(1)}, bf16[8,16,256]{2,1,0:T(8,128)(2,1)S(1)}, u32[]{:S(2)}, u32[]{:S(2)}) collective-permute-start(bf16[8,16,256]{2,1,0:T(8,128)(2,1)S(1)} %get-tuple-element.23), channel_id=1, source_target_pairs={{0,8},{8,16},{16,24},{24,0},{1,9},{9,17},{17,25},{25,1},{2,10},{10... | collective-permute-start | bytes 196616 | tf_op jit(solution)/shard_map/ppermute | solution.py:35
  155.0 22.3 %collective-permute-start.27 = (bf16[8,16,256]{2,1,0:T(8,128)(2,1)S(1)}, bf16[8,16,256]{2,1,0:T(8,128)(2,1)S(1)}, u32[]{:S(2)}, u32[]{:S(2)}) collective-permute-start(bf16[8,16,256]{2,1,0:T(8,128)(2,1)S(1)} %get-tuple-element.22), channel_id=1, source_target_pairs={{0,16},{8,24},{16,0},{24,8},{1,17},{9,25},{17,1},{25,9},{2,18},{10... | collective-permute-start | bytes 196616 | tf_op jit(solution)/shard_map/ppermute | solution.py:35
  157.3 19.9 %copy-start.13 = (s32[32]{0:T(128)S(1)}, s32[32]{0:T(128)}, u32[]{:S(2)}) copy-start(s32[32]{0:T(128)} %tenant_ref.5) | copy-start | bytes 388
  157.3 19.9 %copy-start.15 = (s32[24]{0:T(128)S(1)}, s32[24]{0:T(128)}, u32[]{:S(2)}) copy-start(s32[24]{0:T(128)} %slot_ref.5) | copy-start | bytes 292
  157.3 19.9 %collective-permute-start.28 = (bf16[8,16,256]{2,1,0:T(8,128)(2,1)S(1)}, bf16[8,16,256]{2,1,0:T(8,128)(2,1)S(1)}, u32[]{:S(2)}, u32[]{:S(2)}) collective-permute-start(bf16[8,16,256]{2,1,0:T(8,128)(2,1)S(1)} %get-tuple-element.21), channel_id=1, source_target_pairs={{0,24},{8,0},{16,8},{24,16},{1,25},{9,1},{17,9},{25,17},{2,26},{10... | collective-permute-start | bytes 196616 | tf_op jit(solution)/shard_map/ppermute | solution.py:35

commit v3 on v2

--- a/solution.py
+++ b/solution.py
@@ -15,16 +15,15 @@
 FIRST_BOTH = (((0,), (0,)), ((), ()))
 SMEM = pl.BlockSpec(memory_space=pltpu.SMEM)
 VMEM = pl.BlockSpec(memory_space=pltpu.VMEM)
-HBM = pl.BlockSpec(memory_space=pl.ANY)
-
-
-def call(kernel, name, flops, mib, **more):
+HBM = pl.BlockSpec(memory_space=pltpu.HBM)
+ANY = pl.BlockSpec(memory_space=pl.ANY)
+
+
+def call(kernel, name, **more):
     return pl.pallas_call(
         kernel,
         compiler_params=pltpu.CompilerParams(vmem_limit_bytes=VMEM_LIMIT),
-        cost_estimate=pl.CostEstimate(
-            flops=int(flops), bytes_accessed=int(mib * 2**20), transcendentals=0
-        ),
+        cost_estimate=pl.CostEstimate(flops=1024, bytes_accessed=1024, transcendentals=0),
         name=name,
         **more,
     )
@@ -39,52 +38,54 @@
     return lax.rem(index + 2 * count, count)
 
 
-def pick(tenant_of_block, slot_of_tenant, place, own_block, adapter_down, adapter_up, data_count):
-    block_count = tenant_of_block.shape[0]
-    blocks_dev = block_count // data_count
-
-    def kernel(tenant_ref, slot_ref, place_ref, own_ref, down_ref, up_ref, a_ref, *rest):
-        b_refs, (a_sem, b_sem) = rest[:data_count], rest[data_count:]
-
-        def a_copy(block):
-            slot = slot_ref[tenant_ref[block]]
-            return pltpu.make_async_copy(down_ref.at[slot], a_ref.at[block], a_sem.at[block])
-
-        def b_copy(k):
+def pick_up(tenant_of_block, slot_of_tenant, place, own_block, adapter_up, data_count):
+    blocks_dev = tenant_of_block.shape[0] // data_count
+
+    def kernel(tenant_ref, slot_ref, place_ref, own_ref, up_ref, *rest):
+        out_refs, sems = rest[:data_count], rest[data_count]
+        copies = []
+        for k in range(data_count):
             data = wrap(place_ref[0] + k, data_count)
             slot = slot_ref[tenant_ref[data * blocks_dev + own_ref[0]]]
-            return pltpu.make_async_copy(up_ref.at[slot], b_refs[k], b_sem.at[k])
-
-        for k in range(data_count):
-            b_copy(k).start()
-
-        @pl.loop(0, block_count)
-        def _(block):
-            a_copy(block).start()
-
-        for k in range(data_count):
-            b_copy(k).wait()
-
-        @pl.loop(0, block_count)
-        def _(block):
-            a_copy(block).wait()
-
-    up_shape = jax.ShapeDtypeStruct(adapter_up.shape[1:], adapter_up.dtype)
-    down_shape = jax.ShapeDtypeStruct((block_count,) + adapter_down.shape[1:], adapter_down.dtype)
-    out = call(
-        kernel,
-        "pick_rows",
-        0,
-        4,
-        out_shape=(down_shape,) + (up_shape,) * data_count,
-        in_specs=[SMEM, SMEM, SMEM, SMEM, HBM, HBM],
-        out_specs=(VMEM,) * (1 + data_count),
-        scratch_shapes=[
-            pltpu.SemaphoreType.DMA((block_count,)),
-            pltpu.SemaphoreType.DMA((data_count,)),
-        ],
-    )(tenant_of_block, slot_of_tenant, place, own_block, adapter_down, adapter_up)
-    return out[0], out[1:]
+            copies.append(pltpu.make_async_copy(up_ref.at[slot], out_refs[k], sems.at[k]))
+        for copy in copies:
+            copy.start()
+        for copy in copies:
+            copy.wait()
+
+    return call(
+        kernel,
+        "pick_up",
+        out_shape=(jax.ShapeDtypeStruct(adapter_up.shape[1:], adapter_up.dtype),) * data_count,
+        in_specs=[SMEM, SMEM, SMEM, SMEM, HBM],
+        out_specs=(VMEM,) * data_count,
+        scratch_shapes=[pltpu.SemaphoreType.DMA((data_count,))],
+    )(tenant_of_block, slot_of_tenant, place, own_block, adapter_up)
+
+
+def pick_down(tenant_of_block, slot_of_tenant, adapter_down):
+    block_count = tenant_of_block.shape[0]
+
+    def kernel(tenant_ref, slot_ref, down_ref, out_ref, sems):
+        copies = [
+            pltpu.make_async_copy(
+                down_ref.at[slot_ref[tenant_ref[block]]], out_ref.at[block], sems.at[block]
+            )
+            for block in range(block_count)
+        ]
+        for copy in copies:
+            copy.start()
+        for copy in copies:
+            copy.wait()
+
+    return call(
+        kernel,
+        "pick_down",
+        out_shape=jax.ShapeDtypeStruct((block_count,) + adapter_down.shape[1:], adapter_down.dtype),
+        in_specs=[SMEM, SMEM, HBM],
+        out_specs=VMEM,
+        scratch_shapes=[pltpu.SemaphoreType.DMA((block_count,))],
+    )(tenant_of_block, slot_of_tenant, adapter_down)
 
 
 def base_product(place, tokens, weight, first, count):
@@ -100,8 +101,6 @@
     return call(
         kernel,
         "base_product",
-        2 * pipe_count * count * rows * depth * WIDTH,
-        8,
         grid_spec=pltpu.PrefetchScalarGridSpec(
             num_scalar_prefetch=1,
             grid=(WIDTH // tile, count),
@@ -135,8 +134,6 @@
     return call(
         kernel,
         "low_product",
-        2 * tok_dev * depth * RANKS,
-        4.5,
         in_specs=[SMEM, VMEM, VMEM],
         out_specs=VMEM,
         out_shape=jax.ShapeDtypeStruct((tensor_count, pipe_count, rows, RANKS), jnp.bfloat16),
@@ -186,8 +183,6 @@
     return call(
         kernel,
         "input_gradient",
-        2 * tok_dev * depth * (WIDTH + RANKS),
-        12,
         grid=(data_count // planes,),
         in_specs=[
             SMEM,
@@ -195,7 +190,7 @@
             pl.BlockSpec((planes, blocks_dev, down_rows, RANKS), lambda n: (n, 0, 0, 0)),
         ]
         + [pl.BlockSpec(grad_shape, lambda n: (0, 0, 0, 0))] * tensor_count
-        + [HBM] * len(order),
+        + [ANY] * len(order),
         out_specs=pl.BlockSpec((tok_dev, tile), lambda n: (0, n)),
         out_shape=jax.ShapeDtypeStruct((tok_dev, depth), jnp.bfloat16),
         scratch_shapes=[
@@ -235,8 +230,6 @@
     return call(
         kernel,
         "grad_down",
-        2 * data_count * tok_dev * down_rows * RANKS,
-        6,
         in_specs=[SMEM, SMEM, SMEM, VMEM] + [VMEM] * tensor_count,
         out_specs=VMEM,
         out_shape=jax.ShapeDtypeStruct((slots, down_rows, RANKS), jnp.float32),
@@ -244,29 +237,47 @@
     )(tenant_of_block, slot_of_tenant, place, x_features, *grad_pieces)
 
 
-def grad_up_pieces(place, low_pieces, cot_cols, data_count, up_rows):
-    tensor_count = len(low_pieces)
-    pipe_count, rows, _ = low_pieces[0].shape
-    cols = cot_cols.shape[-1]
-    tok_dev = tensor_count * pipe_count * rows
+def grad_up_pieces(place, low_pieces, cot_pieces, data_count, up_rows):
+    tensor_count, pipe_count = len(cot_pieces), len(cot_pieces[0])
+    group_count = tensor_count * pipe_count
+    rows = cot_pieces[0][0].shape[0]
+    cols = WIDTH // group_count
+    tok_dev = group_count * rows
     blocks_dev = tok_dev // BLOCK
-    group_half = tensor_count * pipe_count // 2
-
-    def kernel(place_ref, cot_ref, *rest):
-        low_refs, (out_ref, low, cot) = rest[:tensor_count], rest[tensor_count:]
+    group_half = group_count // 2
+    order = [(s, k) for s in range(tensor_count) for k in range(pipe_count)]
+    pieces = [cot_pieces[s][k] for s, k in order]
+    in_kernel = cols % 128 == 0
+    if not in_kernel:
+        first_col = (place[1] * tensor_count + place[2]) * cols
+        pieces = [lax.dynamic_slice_in_dim(piece, first_col, cols, 1) for piece in pieces]
+
+    def kernel(place_ref, *rest):
+        low_refs, rest = rest[:tensor_count], rest[tensor_count:]
+        cot_refs, (out_ref, low, cot, sems) = rest[: len(order)], rest[len(order) :]
+        my_group = place_ref[1] * tensor_count + place_ref[2]
+        copies = []
+        for i, (s, k) in enumerate(order):
+            core = wrap(place_ref[2] - s, tensor_count)
+            chip = wrap(place_ref[1] - k, pipe_count)
+            first = pl.multiple_of((chip * tensor_count + core) * rows, rows)
+            piece = cot_refs[i]
+            if in_kernel:
+                piece = piece.at[:, pl.ds(pl.multiple_of(my_group * cols, cols), cols)]
+            copies.append(pltpu.make_async_copy(piece, cot.at[pl.ds(first, rows)], sems.at[i]))
+        for copy in copies:
+            copy.start()
         for s in range(tensor_count):
             core = wrap(place_ref[2] - s, tensor_count)
             for k in range(pipe_count):
                 first = pl.multiple_of((k * tensor_count + core) * rows, rows)
                 low[pl.ds(first, rows)] = low_refs[s][k]
-                chip = wrap(place_ref[1] - k, pipe_count)
-                first = pl.multiple_of((chip * tensor_count + core) * rows, rows)
-                cot[pl.ds(first, rows)] = cot_ref[s * pipe_count + k]
-        is_key = place_ref[1] * tensor_count + place_ref[2] < group_half
+        for copy in copies:
+            copy.wait()
         for block in range(blocks_dev):
             at = slice(block * BLOCK, (block + 1) * BLOCK)
             both = lax.dot_general(low[at], cot[at], FIRST_BOTH, preferred_element_type=jnp.float32)
-            half = jnp.where(is_key, both[:ADAPTER_RANK], both[ADAPTER_RANK:])
+            half = jnp.where(my_group < group_half, both[:ADAPTER_RANK], both[ADAPTER_RANK:])
             half = half.astype(out_ref.dtype)
             for data in range(data_count):
                 k = wrap(data - place_ref[0], data_count)
@@ -275,16 +286,15 @@
     return call(
         kernel,
         "grad_up_pieces",
-        2 * tok_dev * cols * RANKS,
-        2,
-        in_specs=[SMEM, VMEM] + [VMEM] * tensor_count,
+        in_specs=[SMEM] + [VMEM] * tensor_count + [ANY] * len(order),
         out_specs=VMEM,
         out_shape=jax.ShapeDtypeStruct((data_count, blocks_dev, up_rows, cols), jnp.bfloat16),
         scratch_shapes=[
             pltpu.VMEM((tok_dev, RANKS), jnp.bfloat16),
             pltpu.VMEM((tok_dev, cols), jnp.bfloat16),
+            pltpu.SemaphoreType.DMA((len(order),)),
         ],
-    )(place, cot_cols, *low_pieces)
+    )(place, *low_pieces, *pieces)
 
 
 def grad_up(tenant_of_block, slot_of_tenant, place, pieces):
@@ -304,16 +314,69 @@
     return call(
         kernel,
         "grad_up",
-        0,
-        1,
         in_specs=[SMEM, SMEM, SMEM] + [VMEM] * data_count,
         out_specs=VMEM,
         out_shape=jax.ShapeDtypeStruct((slots, up_rows, cols), jnp.float32),
     )(tenant_of_block, slot_of_tenant, place, *pieces)
 
 
-def halves(product, left, right):
-    return jnp.concatenate([product(*pair) for pair in zip(left, right)], axis=1)
+def own_rows(place, up, cotangent):
+    data_count = len(up)
+    rows = cotangent.shape[0]
+
+    def kernel(place_ref, cot_ref, *rest):
+        up_refs, (b_ref, grad_ref) = rest[:data_count], rest[data_count:]
+        pieces = []
+        for data in range(data_count):
+            came = wrap(place_ref[0] - data, data_count)
+            piece = up_refs[0][...]
+            for k in range(1, data_count):
+                piece = jnp.where(came == k, up_refs[k][...], piece)
+            pieces.append(piece)
+        b = jnp.concatenate(pieces, axis=0)
+        b_ref[...] = b
+        cot = cot_ref[...]
+        grad_ref[...] = jnp.concatenate(
+            [
+                lax.dot_general(cot[:, half], b[:, half], LAST_BOTH, preferred_element_type=jnp.float32)
+                for half in (slice(0, KEY_WIDTH), slice(KEY_WIDTH, WIDTH))
+            ],
+            axis=1,
+        ).astype(grad_ref.dtype)
+
+    return call(
+        kernel,
+        "own_rows",
+        in_specs=[SMEM, VMEM] + [VMEM] * data_count,
+        out_specs=(VMEM, VMEM),
+        out_shape=(
+            jax.ShapeDtypeStruct((ADAPTER_RANK, WIDTH), jnp.bfloat16),
+            jax.ShapeDtypeStruct((rows, RANKS), jnp.bfloat16),
+        ),
+    )(place, cotangent, *up)
+
+
+def keys_and_values(place, base_pieces, low_sum, b_own):
+    rows = base_pieces[0].shape[0]
+    count = len(base_pieces)
+
+    def kernel(place_ref, low_ref, b_ref, *rest):
+        base_refs, out_ref = rest[:count], rest[count]
+        low = low_ref[place_ref[1]]
+        for first, ranks in ((0, slice(0, ADAPTER_RANK)), (KEY_WIDTH, slice(ADAPTER_RANK, RANKS))):
+            at = slice(first, first + KEY_WIDTH)
+            y = jnp.dot(low[:, ranks], b_ref[:, at], preferred_element_type=jnp.float32)
+            for base_ref in base_refs:
+                y += base_ref[:, at].astype(jnp.float32)
+            out_ref[:, at] = y.astype(out_ref.dtype)
+
+    return call(
+        kernel,
+        "keys_and_values",
+        in_specs=[SMEM, VMEM, VMEM] + [VMEM] * count,
+        out_specs=VMEM,
+        out_shape=jax.ShapeDtypeStruct((rows, WIDTH), jnp.bfloat16),
+    )(place, low_sum, b_own, *base_pieces)
 
 
 def body(
@@ -333,24 +396,29 @@
     up_rows = adapter_up.shape[1]
 
     own_block = (my_group * rows // BLOCK).reshape(1)
-    a_send, b_send = pick(
-        tenant_of_block, slot_of_tenant, place, own_block, adapter_down, adapter_up, data_count
-    )
+    b_send = pick_up(tenant_of_block, slot_of_tenant, place, own_block, adapter_up, data_count)
     b_came = [b_send[0]] + [shift(b_send[k], "dp", k) for k in range(1, data_count)]
+    b_own, grad_rows = own_rows(place, b_came, cotangent)
+    grad_data = [grad_rows] + [shift(grad_rows, "dp", k) for k in range(1, data_count)]
+
+    a_send = pick_down(tenant_of_block, slot_of_tenant, adapter_down)
+    a_send, grad_data = lax.optimization_barrier((a_send, grad_data))
     a_recv = lax.all_to_all(
         a_send.reshape(data_count, blocks_dev, down_rows, RANKS), "dp", 0, 0, tiled=True
     )
 
-    cot_chips = [cotangent] + [shift(cotangent, "pipe", k) for k in range(1, pipe_count)]
+    grad_data = jnp.stack(grad_data)
+    grad_chips = jnp.stack([grad_data] + [shift(grad_data, "pipe", k) for k in range(1, pipe_count)])
+    grad_pieces = [grad_chips] + [shift(grad_chips, "tensor", s) for s in range(1, tensor_count)]
+
+    cot_send, grad_rows = lax.optimization_barrier((cotangent, grad_rows))
+    cot_chips = [cotangent] + [shift(cot_send, "pipe", k) for k in range(1, pipe_count)]
     cot_pieces = [cot_chips] + [
         [shift(piece, "tensor", s) for piece in cot_chips] for s in range(1, tensor_count)
     ]
 
-    x_send = tokens.T.reshape(data_count, down_rows, tok_dev)
-    x_send, a_recv = lax.optimization_barrier((x_send, a_recv))
-    x_recv = lax.all_to_all(x_send, "dp", 0, 0, tiled=True)
-
-    tokens_by_group = tokens.reshape(pipe_count, tensor_count, rows, feature_count)
+    base_tokens, a_send = lax.optimization_barrier((tokens, a_send))
+    tokens_by_group = base_tokens.reshape(pipe_count, tensor_count, rows, feature_count)
     base_send = base_product(place, tokens_by_group, key_value_weight, 1, tensor_count - 1)
     base_came = [shift(base_send[s - 1], "tensor", s) for s in range(1, tensor_count)]
     base_keep = base_product(place, tokens_by_group, key_value_weight, 0, 1)[0]
@@ -361,24 +429,11 @@
     base_chip_came = [
         shift(base_chip[k].astype(jnp.bfloat16), "pipe", k) for k in range(1, pipe_count)
     ]
-    base_rows = sum([base_chip[0]] + [b.astype(jnp.float32) for b in base_chip_came])
-
-    b_own = jnp.concatenate(
-        [lax.select_n(wrap(at_data - i, data_count), *b_came) for i in range(data_count)]
-        if data_count > 1
-        else b_came
+    x_send = tokens.T.reshape(data_count, down_rows, tok_dev)
+    a_recv, x_send, base_chip_came, cot_pieces, grad_pieces = lax.optimization_barrier(
+        (a_recv, x_send, base_chip_came, cot_pieces, grad_pieces)
     )
-    left = lambda m: (m[:, :ADAPTER_RANK], m[:, ADAPTER_RANK:])
-    wide = lambda m: (m[:, :KEY_WIDTH], m[:, KEY_WIDTH:])
-    grad_rows = halves(
-        lambda p, q: lax.dot_general(p, q, LAST_BOTH, preferred_element_type=jnp.float32),
-        wide(cotangent),
-        wide(b_own),
-    ).astype(jnp.bfloat16)
-    grad_data = jnp.stack([grad_rows] + [shift(grad_rows, "dp", k) for k in range(1, data_count)])
-    grad_chips = jnp.stack([grad_data] + [shift(grad_data, "pipe", k) for k in range(1, pipe_count)])
-    grad_pieces = [grad_chips] + [shift(grad_chips, "tensor", s) for s in range(1, tensor_count)]
-
+    x_recv = lax.all_to_all(x_send, "dp", 0, 0, tiled=True)
     low_part = low_product(place, tokens, a_recv, pipe_count, tensor_count)
     low_core = sum(
         [low_part[0].astype(jnp.float32)]
@@ -389,21 +444,9 @@
         + [shift(low_core, "pipe", k).astype(jnp.float32) for k in range(1, pipe_count)]
     ).astype(jnp.bfloat16)
     low_pieces = [low_sum] + [shift(low_sum, "tensor", s) for s in range(1, tensor_count)]
-    low_rows = lax.dynamic_index_in_dim(low_sum, at_pipe, 0, False)
-    lowrank = halves(
-        lambda p, q: jnp.dot(p, q, preferred_element_type=jnp.float32), left(low_rows), wide(b_own)
-    )
-    key_value = (base_rows + lowrank).astype(jnp.bfloat16)
-
-    col_count = WIDTH // group_count
-    cot_cols = jnp.stack(
-        [
-            lax.dynamic_slice_in_dim(piece, my_group * col_count, col_count, 1)
-            for pieces in cot_pieces
-            for piece in pieces
-        ]
-    )
-    up_pieces = grad_up_pieces(place, low_pieces, cot_cols, data_count, up_rows)
+    key_value = keys_and_values(place, base_chip[:1] + base_chip_came, low_sum, b_own)
+
+    up_pieces = grad_up_pieces(place, low_pieces, cot_pieces, data_count, up_rows)
     up_came = [up_pieces[0]] + [shift(up_pieces[k], "dp", k) for k in range(1, data_count)]
     grad_b = grad_up(tenant_of_block, slot_of_tenant, place, up_came)
 

time: 184 us -> 174 us (0.946)
  local copies, waits for them, and re-layouts: 16.3 us -> 10.1 us
  Pallas kernels: 34.2 us -> 38.6 us
  waiting for transfers between devices: 82.1 us -> 78.8 us
  matrix products: 2.77 us -> 0 us
  other arithmetic: 5.85 us -> 3.89 us
    unnamed x41 -> x38, local copies, waits for them, and re-layouts: 12.6 us -> 7.51 us
    pallas_call x8 -> x11, Pallas kernels: 34.2 us -> 38.6 us  [the longest x2 10.5 us: base_product(): call(kernel, 'base_product', grid_spec=pltpu.PrefetchScalarGridSpec(num_s...]
    convert_element_type x2 -> x0, other arithmetic: 4.31 us -> none  [the longest x1 2.31 us: body(): key_value = (base_rows + lowrank).astype(jnp.bfloat16)]
    add x0 -> x1, other arithmetic: none -> 3.6 us  [body(): sum([base_keep[k].astype(jnp.float32)] + [b[k].astype(jnp.float32) for b...]
    ppermute x29, waiting for transfers between devices: 82.1 us -> 78.8 us  [shift(): lax.ppermute(piece, axis, [(i, (i + step) % count) for i in range(count)])]
    dot_general x4 -> x0, matrix products: 2.77 us -> none  [the longest x2 2.32 us: body(): lax.dot_general(p, q, LAST_BOTH, preferred_element_type=jnp.float32)]
    ppermute x29, starting transfers between devices: 30.1 us -> 32.1 us  [shift(): lax.ppermute(piece, axis, [(i, (i + step) % count) for i in range(count)])]
    all_to_all x1, starting transfers between devices: 6.45 us -> 4.6 us  [body(): lax.all_to_all(a_send.reshape(data_count, blocks_dev, down_rows, RANKS),...]
  transfers between devices with their start and end apart: 31 -> 31, of which waited for: 13 -> 13; matrix products, arithmetic and copies ran while one was open for 9% -> 4% of each run, Pallas kernels for 14% -> 15%
where the time goes in v3:
time: 174 us; the launch traced here: 173 us
  waiting for transfers between devices  78.8 us (45%)
  starting transfers between devices  41.2 us (24%)
  Pallas kernels  38.6 us (22%)
  local copies, waits for them, and re-layouts  10.1 us (6%)
  other arithmetic  3.89 us (2%)
    ppermute x29, waiting for transfers between devices, shift(): lax.ppermute(piece, axis, [(i, (i + step) % count) for i in range(count)])  78.8 us
    ppermute x29, starting transfers between devices, shift(): lax.ppermute(piece, axis, [(i, (i + step) % count) for i in range(count)])  32.1 us
    pallas_call x2, Pallas kernels, base_product(): call(kernel, 'base_product', grid_spec=pltpu.PrefetchScalarGridSpec(num_s...  10.5 us
    pallas_call x1, Pallas kernels, input_gradient(): call(kernel, 'input_gradient', grid=(data_count // planes,), in_specs=[SM...  9.82 us
    unnamed x38, local copies, waits for them, and re-layouts  7.51 us
    all_to_all x1, starting transfers between devices, body(): lax.all_to_all(a_send.reshape(data_count, blocks_dev, down_rows, RANKS),...  4.6 us
    all_to_all x1, starting transfers between devices, body(): x_recv = lax.all_to_all(x_send, 'dp', 0, 0, tiled=True)  4.5 us
    pallas_call x1, Pallas kernels, grad_down(): call(kernel, 'grad_down', in_specs=[SMEM, SMEM, SMEM, VMEM] + [VMEM] * te...  4.31 us
  transfers between devices with their start and end apart: 31, of which 13 were waited for; matrix products, arithmetic and copies ran while one was open for 4% of the time, Pallas kernels for 15%

profile of v3, /device:TPU:0, one launch (start us, length us, event | category | flops | bytes accessed | tf_op | source)
XLA Modules:
  0.0 173.4 jit_solution(14886315775873504654)
XLA Ops:
  0.7 0.1 pad_add_fusion.place_ref
  0.8 1.4 copy-done.13
  2.2 0.7 copy-done.15
  2.8 0.7 copy-done.17
  3.5 0.9 pick_up.1
  4.4 3.1 %collective-permute-start = (bf16[16,2048]{1,0:T(8,128)(2,1)S(1)}, bf16[16,2048]{1,0:T(8,128)(2,1)S(1)}, u32[]{:S(2)}, u32[]{:S(2)}) collective-permute-start(bf16[16,2048]{1,0:T(8,128)(2,1)S(1)} %get-tuple-element.33), channel_id=1, source_target_pairs={{0,8},{8,16},{16,24},{24,0},{1,9},{9,17},{17,25},{25,1},{2,10},{10... | collective-permute-start | bytes 196616 | tf_op jit(solution)/shard_map/ppermute | solution.py:34
  7.5 2.6 %collective-permute-start.1 = (bf16[16,2048]{1,0:T(8,128)(2,1)S(1)}, bf16[16,2048]{1,0:T(8,128)(2,1)S(1)}, u32[]{:S(2)}, u32[]{:S(2)}) collective-permute-start(bf16[16,2048]{1,0:T(8,128)(2,1)S(1)} %get-tuple-element.34), channel_id=1, source_target_pairs={{0,16},{8,24},{16,0},{24,8},{1,17},{9,25},{17,1},{25,9},{2,18},{10... | collective-permute-start | bytes 196616 | tf_op jit(solution)/shard_map/ppermute | solution.py:34
  10.1 1.3 collective-permute-start.2
  11.4 0.6 collective-permute-done.rest_1_
  12.1 2.5 %collective-permute-done.1.rest_2_ = bf16[16,2048]{1,0:T(8,128)(2,1)S(1)} collective-permute-done((bf16[16,2048]{1,0:T(8,128)(2,1)S(1)}, bf16[16,2048]{1,0:T(8,128)(2,1)S(1)}, u32[]{:S(2)}, u32[]{:S(2)}) %collective-permute-start.1) | collective-permute-done | bytes 65568 | tf_op jit(solution)/shard_map/ppermute | solution.py:34
  14.6 0.2 collective-permute-done.2.rest_3_
  14.8 1.0 copy-done.2
  15.9 0.9 own_rows.1
  16.8 1.6 collective-permute-start.3
  18.4 2.0 %collective-permute-start.4 = (bf16[128,128]{1,0:T(8,128)(2,1)S(1)}, bf16[128,128]{1,0:T(8,128)(2,1)S(1)}, u32[]{:S(2)}, u32[]{:S(2)}) collective-permute-start(bf16[128,128]{1,0:T(8,128)(2,1)S(1)} %get-tuple-element.40), channel_id=1, source_target_pairs={{0,16},{8,24},{16,0},{24,8},{1,17},{9,25},{17,1},{25,9},{2,18},{10... | collective-permute-start | bytes 98312 | tf_op jit(solution)/shard_map/ppermute | solution.py:34
  20.4 0.4 collective-permute-start.5
  20.9 3.7 %pick_down.1 = bf16[32,256,128]{2,1,0:T(8,128)(2,1)S(1)} custom-call(s32[32]{0:T(128)S(1)} %copy-done.16, s32[24]{0:T(128)S(1)} %copy-done.18, bf16[24,256,128]{2,1,0:T(8,128)(2,1)S(1)} %copy-done.14), custom_call_target="tpu_custom_call" | custom-call | flops 1024 | bytes 1024 | tf_op jit(solution)/shard_map/pick_down/pallas_call | solution.py:81
  24.6 1.3 copy-done.1
  25.9 5.6 %base_product.3 = bf16[1,4,128,2048]{3,2,1,0:T(8,128)(2,1)} custom-call(s32[3]{0:T(128)S(1)} %pad_add_fusion.place_ref, bf16[4,2,128,1024]{3,2,1,0:T(8,128)(2,1)S(1)} %bitcast.73, bf16[1024,2048]{1,0:T(8,128)(2,1)} %w_ref.5), custom_call_target="tpu_custom_call" | custom-call | flops 1024 | bytes 1024 | tf_op jit(solution)/shard_map/base_product/pallas_call | solution.py:101
  31.6 4.6 %all-to-all-start = ((bf16[4,8,256,128]{3,2,1,0:T(8,128)(2,1)}), bf16[4,8,256,128]{3,2,1,0:T(8,128)(2,1)}, u32[]{:S(2)}, u32[]{:S(2)}) async-start(bf16[4,8,256,128]{3,2,1,0:T(8,128)(2,1)} %bitcast.76), calls=%async_computation | async-start | bytes 4194304 | tf_op jit(solution)/shard_map/all_to_all | solution.py:406
  36.2 1.5 collective-permute-start.10
  37.7 1.5 collective-permute-start.11
  39.2 1.4 collective-permute-start.12
  40.7 0.6 collective-permute-start.19
  41.3 24.3 %collective-permute-done.19 = bf16[4,128,128]{2,1,0:T(8,128)(2,1)S(1)} collective-permute-done((bf16[4,128,128]{2,1,0:T(8,128)(2,1)S(1)}, bf16[4,128,128]{2,1,0:T(8,128)(2,1)S(1)}, u32[]{:S(2)}, u32[]{:S(2)}) %collective-permute-start.19) | collective-permute-done | bytes 131104 | tf_op jit(solution)/shard_map/ppermute | solution.py:34
  65.6 0.5 collective-permute-start.18
  66.1 4.7 %collective-permute-done.18 = bf16[4,128,128]{2,1,0:T(8,128)(2,1)S(1)} collective-permute-done((bf16[4,128,128]{2,1,0:T(8,128)(2,1)S(1)}, bf16[4,128,128]{2,1,0:T(8,128)(2,1)S(1)}, u32[]{:S(2)}, u32[]{:S(2)}) %collective-permute-start.18) | collective-permute-done | bytes 131104 | tf_op jit(solution)/shard_map/ppermute | solution.py:34
  70.8 1.5 collective-permute-start.17
  72.3 4.8 %base_product.2 = bf16[1,4,128,2048]{3,2,1,0:T(8,128)(2,1)S(1)} custom-call(s32[3]{0:T(128)S(1)} %pad_add_fusion.place_ref, bf16[4,2,128,1024]{3,2,1,0:T(8,128)(2,1)S(1)} %bitcast.74, bf16[1024,2048]{1,0:T(8,128)(2,1)} %w_ref.5), custom_call_target="tpu_custom_call" | custom-call | flops 1024 | bytes 1024 | tf_op jit(solution)/shard_map/base_product/pallas_call | solution.py:101
  77.4 0.6 collective-permute-start.20
  77.9 0.1 collective-permute-start.14
  78.0 0.4 collective-permute-start.15
  78.4 0.1 collective-permute-start.16
  78.5 3.6 %convert_add_fusion = (f32[128,2048]{1,0:T(8,128)}, bf16[128,2048]{1,0:T(8,128)(2,1)}, bf16[128,2048]{1,0:T(8,128)(2,1)}, bf16[128,2048]{1,0:T(8,128)(2,1)}) fusion(bf16[4,128,2048]{2,1,0:T(8,128)(2,1)} %collective-permute-done.6, bf16[1,4,128,2048]{3,2,1,0:T(8,128)(2,1)S(1)} %base_product.2), kind=kLoop, calls=%fused_computation | loop fusion | flops 3932160 | bytes 6815744 | tf_op jit(solution)/shard_map/add | solution.py:426
  82.1 0.8 copy-done.7
  82.9 0.5 collective-permute-start.7
  83.4 0.8 copy-done.11
  84.2 1.5 collective-permute-start.8
  85.7 0.8 copy-done.9
  86.5 1.4 collective-permute-start.9
  88.0 2.5 %copy.11 = bf16[1024,1024]{1,0:T(8,128)(2,1)} copy(bf16[1024,1024]{0,1:T(8,128)(2,1)S(1)} %bitcast.75) | data formatting | bytes 4194304 | tf_op jit(solution)/shard_map/transpose | solution.py:432
  90.5 8.4 %collective-permute-done.7.rest_1_ = bf16[128,2048]{1,0:T(8,128)(2,1)} collective-permute-done((bf16[128,2048]{1,0:T(8,128)(2,1)}, bf16[128,2048]{1,0:T(8,128)(2,1)}, u32[]{:S(2)}, u32[]{:S(2)}) %collective-permute-start.7) | collective-permute-done | bytes 524320 | tf_op jit(solution)/shard_map/ppermute | solution.py:34
  98.9 10.7 %collective-permute-done.8.rest_2_ = bf16[128,2048]{1,0:T(8,128)(2,1)} collective-permute-done((bf16[128,2048]{1,0:T(8,128)(2,1)}, bf16[128,2048]{1,0:T(8,128)(2,1)}, u32[]{:S(2)}, u32[]{:S(2)}) %collective-permute-start.8) | collective-permute-done | bytes 524320 | tf_op jit(solution)/shard_map/ppermute | solution.py:34
  109.7 4.5 %all-to-all-start.1 = ((bf16[4,256,1024]{2,1,0:T(8,128)(2,1)}), bf16[4,256,1024]{2,1,0:T(8,128)(2,1)}, u32[]{:S(2)}, u32[]{:S(2)}) async-start(bf16[4,256,1024]{2,1,0:T(8,128)(2,1)} %bitcast.78), calls=%async_computation.1 | async-start | bytes 4194304 | tf_op jit(solution)/shard_map/all_to_all | solution.py:436
  114.2 2.4 %low_product.1 = bf16[2,4,128,128]{3,2,1,0:T(8,128)(2,1)S(1)} custom-call(s32[3]{0:T(128)S(1)} %pad_add_fusion.place_ref, bf16[1024,1024]{1,0:T(8,128)(2,1)S(1)} %copy-done, bf16[4,8,256,128]{3,2,1,0:T(8,128)(2,1)} %all-to-all-done.a_ref), custom_call_target="tpu_custom_call" | custom-call | flops 1024 | bytes 1024 | tf_op jit(solution)/shard_map/low_product/pallas_call | solution.py:134
  116.6 0.1 collective-permute-start.21
  116.7 1.3 collective-permute-done.21
  118.1 2.6 %collective-permute-start.24 = (bf16[4,128,128]{2,1,0:T(8,128)(2,1)S(1)}, bf16[4,128,128]{2,1,0:T(8,128)(2,1)S(1)}, u32[]{:S(2)}, u32[]{:S(2)}) collective-permute-start(bf16[4,128,128]{2,1,0:T(8,128)(2,1)S(1)} %fusion.3), channel_id=1, source_target_pairs={{0,6},{2,0},{4,2},{6,4},{1,7},{3,1},{5,3},{7,5},{8,14},{10,8},{12,... | collective-permute-start | bytes 393224 | tf_op jit(solution)/shard_map/ppermute | solution.py:34
  120.7 0.5 collective-permute-start.23
  121.2 0.1 collective-permute-start.22
  121.3 3.3 %collective-permute-done.24 = bf16[4,128,128]{2,1,0:T(8,128)(2,1)S(1)} collective-permute-done((bf16[4,128,128]{2,1,0:T(8,128)(2,1)S(1)}, bf16[4,128,128]{2,1,0:T(8,128)(2,1)S(1)}, u32[]{:S(2)}, u32[]{:S(2)}) %collective-permute-start.24) | collective-permute-done | bytes 131104 | tf_op jit(solution)/shard_map/ppermute | solution.py:34
  124.6 4.2 %collective-permute-done.23 = bf16[4,128,128]{2,1,0:T(8,128)(2,1)S(1)} collective-permute-done((bf16[4,128,128]{2,1,0:T(8,128)(2,1)S(1)}, bf16[4,128,128]{2,1,0:T(8,128)(2,1)S(1)}, u32[]{:S(2)}, u32[]{:S(2)}) %collective-permute-start.23) | collective-permute-done | bytes 131104 | tf_op jit(solution)/shard_map/ppermute | solution.py:34
  128.8 0.1 add_convert_fusion.low_ref.rest_0_
  128.9 1.3 collective-permute-done.25.rest_1_
  130.3 1.9 %grad_up_pieces.1 = bf16[4,8,16,256]{3,2,1,0:T(8,128)(2,1)S(1)} custom-call(s32[3]{0:T(128)S(1)} %pad_add_fusion.place_ref, bf16[4,128,128]{2,1,0:T(8,128)(2,1)S(1)} %add_convert_fusion.low_ref.rest_0_, bf16[4,128,128]{2,1,0:T(8,128)(2,1)S(1)} %collective-permute-done.25.rest_1_, bf16[128,2048]{1,0:T(8,128)(2,1)S(1)} %copy-done.3, ...), custom_call_target="tpu_custom_call" | custom-call | flops 1024 | bytes 1024 | tf_op jit(solution)/shard_map/grad_up_pieces/pallas_call | solution.py:286
  132.2 2.1 %collective-permute-start.26 = (bf16[8,16,256]{2,1,0:T(8,128)(2,1)S(1)}, bf16[8,16,256]{2,1,0:T(8,128)(2,1)S(1)}, u32[]{:S(2)}, u32[]{:S(2)}) collective-permute-start(bf16[8,16,256]{2,1,0:T(8,128)(2,1)S(1)} %get-tuple-element.66), channel_id=1, source_target_pairs={{0,8},{8,16},{16,24},{24,0},{1,9},{9,17},{17,25},{25,1},{2,10},{10... | collective-permute-start | bytes 196616 | tf_op jit(solution)/shard_map/ppermute | solution.py:34
  134.3 2.4 %collective-permute-start.27 = (bf16[8,16,256]{2,1,0:T(8,128)(2,1)S(1)}, bf16[8,16,256]{2,1,0:T(8,128)(2,1)S(1)}, u32[]{:S(2)}, u32[]{:S(2)}) collective-permute-start(bf16[8,16,256]{2,1,0:T(8,128)(2,1)S(1)} %get-tuple-element.65), channel_id=1, source_target_pairs={{0,16},{8,24},{16,0},{24,8},{1,17},{9,25},{17,1},{25,9},{2,18},{10... | collective-permute-start | bytes 196616 | tf_op jit(solution)/shard_map/ppermute | solution.py:34
  136.7 1.5 collective-permute-start.28
  138.1 9.8 %input_gradient.1 = bf16[1024,1024]{1,0:T(8,128)(2,1)} custom-call(s32[3]{0:T(128)S(1)} %pad_add_fusion.place_ref, bf16[1024,2048]{1,0:T(8,128)(2,1)} %w_ref.5, bf16[4,8,256,128]{3,2,1,0:T(8,128)(2,1)} %all-to-all-done.a_ref, bf16[4,4,128,128]{3,2,1,0:T(8,128)(2,1)S(1)} %pad_maximum_fusion.rest_0_, bf16[4,4,128,128]{3,2,1,0:T(8,128)(2,1)S(1)} %copy-done.12, ...), custom_call_target="tpu_custom_call" | custom-call | flops 1024 | bytes 1024 | tf_op jit(solution)/shard_map/input_gradient/pallas_call | solution.py:183
  148.0 2.6 %keys_and_values.1 = bf16[128,2048]{1,0:T(8,128)(2,1)} custom-call(s32[3]{0:T(128)S(1)} %pad_add_fusion.place_ref, bf16[4,128,128]{2,1,0:T(8,128)(2,1)S(1)} %add_convert_fusion.low_ref.rest_0_, bf16[64,2048]{1,0:T(8,128)(2,1)S(1)} %get-tuple-element.45.b_ref, f32[128,2048]{1,0:T(8,128)S(1)} %copy-done.4, bf16[128,2048]{1,0:T(8,128)(2,1)} %collective-permute-done.7.rest_1_, ...), custom_call_target="tpu_custom_call" | custom-call | flops 1024 | bytes 1024 | tf_op jit(solution)/shard_map/keys_and_values/pallas_call | solution.py:373
  150.6 4.3 %collective-permute-done.26.rest_1_ = bf16[8,16,256]{2,1,0:T(8,128)(2,1)S(1)} collective-permute-done((bf16[8,16,256]{2,1,0:T(8,128)(2,1)S(1)}, bf16[8,16,256]{2,1,0:T(8,128)(2,1)S(1)}, u32[]{:S(2)}, u32[]{:S(2)}) %collective-permute-start.26) | collective-permute-done | bytes 65568 | tf_op jit(solution)/shard_map/ppermute | solution.py:34
  154.9 12.8 %collective-permute-done.27.rest_2_ = bf16[8,16,256]{2,1,0:T(8,128)(2,1)S(1)} collective-permute-done((bf16[8,16,256]{2,1,0:T(8,128)(2,1)S(1)}, bf16[8,16,256]{2,1,0:T(8,128)(2,1)S(1)}, u32[]{:S(2)}, u32[]{:S(2)}) %collective-permute-start.27) | collective-permute-done | bytes 65568 | tf_op jit(solution)/shard_map/ppermute | solution.py:34
  167.7 1.5 grad_up.1
  169.1 4.3 %grad_down.1 = f32[24,256,128]{2,1,0:T(8,128)} custom-call(s32[32]{0:T(128)S(1)} %copy-done.16, s32[24]{0:T(128)S(1)} %copy-done.18, s32[3]{0:T(128)S(1)} %pad_add_fusion.place_ref, bf16[4,256,1024]{2,1,0:T(8,128)(2,1)} %all-to-all-done.1.x_ref, bf16[4,4,128,128]{3,2,1,0:T(8,128)(2,1)S(1)} %pad_maximum_fusion.rest_0_, bf16[4,4,128,128]{3,2,1,0:T(8,128)(2,1)S(1)} %copy-done.12), custom_call_target="tpu_custom_call" | custom-call | flops 1024 | bytes 1024 | tf_op jit(solution)/shard_map/grad_down/pallas_call | solution.py:230
  (56 shorter events, 0.4 us)
Async XLA Ops:
  0.6 20.2 %copy-start.16 = (s32[32]{0:T(128)S(1)}, s32[32]{0:T(128)}, u32[]{:S(2)}) copy-start(s32[32]{0:T(128)} %tenant_ref.7) | copy-start | bytes 388
  0.6 20.2 %copy-start.18 = (s32[24]{0:T(128)S(1)}, s32[24]{0:T(128)}, u32[]{:S(2)}) copy-start(s32[24]{0:T(128)} %slot_ref.7) | copy-start | bytes 292
  0.7 1.4 copy-start.13
  2.2 0.7 copy-start.15
  2.8 0.7 copy-start.17
  3.5 17.4 %copy-start.14 = (bf16[24,256,128]{2,1,0:T(8,128)(2,1)S(1)}, bf16[24,256,128]{2,1,0:T(8,128)(2,1)}, u32[]{:S(2)}) copy-start(bf16[24,256,128]{2,1,0:T(8,128)(2,1)} %down_ref.1) | copy-start | bytes 4718596
  4.4 7.6 %collective-permute-start = (bf16[16,2048]{1,0:T(8,128)(2,1)S(1)}, bf16[16,2048]{1,0:T(8,128)(2,1)S(1)}, u32[]{:S(2)}, u32[]{:S(2)}) collective-permute-start(bf16[16,2048]{1,0:T(8,128)(2,1)S(1)} %get-tuple-element.33), channel_id=1, source_target_pairs={{0,8},{8,16},{16,24},{24,0},{1,9},{9,17},{17,25},{25,1},{2,10},{10... | collective-permute-start | bytes 196616 | tf_op jit(solution)/shard_map/ppermute | solution.py:34
  7.5 7.1 %collective-permute-start.1 = (bf16[16,2048]{1,0:T(8,128)(2,1)S(1)}, bf16[16,2048]{1,0:T(8,128)(2,1)S(1)}, u32[]{:S(2)}, u32[]{:S(2)}) collective-permute-start(bf16[16,2048]{1,0:T(8,128)(2,1)S(1)} %get-tuple-element.34), channel_id=1, source_target_pairs={{0,16},{8,24},{16,0},{24,8},{1,17},{9,25},{17,1},{25,9},{2,18},{10... | collective-permute-start | bytes 196616 | tf_op jit(solution)/shard_map/ppermute | solution.py:34
  10.1 4.7 %collective-permute-start.2 = (bf16[16,2048]{1,0:T(8,128)(2,1)S(1)}, bf16[16,2048]{1,0:T(8,128)(2,1)S(1)}, u32[]{:S(2)}, u32[]{:S(2)}) collective-permute-start(bf16[16,2048]{1,0:T(8,128)(2,1)S(1)} %get-tuple-element.35), channel_id=1, source_target_pairs={{0,24},{8,0},{16,8},{24,16},{1,25},{9,1},{17,9},{25,17},{2,26},{10... | collective-permute-start | bytes 196616 | tf_op jit(solution)/shard_map/ppermute | solution.py:34
  14.8 1.0 copy-start.2
  15.9 10.0 %copy-start = (bf16[1024,1024]{1,0:T(8,128)(2,1)S(1)}, bf16[1024,1024]{1,0:T(8,128)(2,1)}, u32[]{:S(2)}) copy-start(bf16[1024,1024]{1,0:T(8,128)(2,1)} %x_ref.1) | copy-start | bytes 6291460
  16.8 9.1 %collective-permute-start.3 = (bf16[128,128]{1,0:T(8,128)(2,1)S(1)}, bf16[128,128]{1,0:T(8,128)(2,1)S(1)}, u32[]{:S(2)}, u32[]{:S(2)}) collective-permute-start(bf16[128,128]{1,0:T(8,128)(2,1)S(1)} %get-tuple-element.40), channel_id=1, source_target_pairs={{0,8},{8,16},{16,24},{24,0},{1,9},{9,17},{17,25},{25,1},{2,10},{10... | collective-permute-start | bytes 98312 | tf_op jit(solution)/shard_map/ppermute | solution.py:34
  18.4 7.5 %collective-permute-start.4 = (bf16[128,128]{1,0:T(8,128)(2,1)S(1)}, bf16[128,128]{1,0:T(8,128)(2,1)S(1)}, u32[]{:S(2)}, u32[]{:S(2)}) collective-permute-start(bf16[128,128]{1,0:T(8,128)(2,1)S(1)} %get-tuple-element.40), channel_id=1, source_target_pairs={{0,16},{8,24},{16,0},{24,8},{1,17},{9,25},{17,1},{25,9},{2,18},{10... | collective-permute-start | bytes 98312 | tf_op jit(solution)/shard_map/ppermute | solution.py:34
  20.4 5.5 %collective-permute-start.5 = (bf16[128,128]{1,0:T(8,128)(2,1)S(1)}, bf16[128,128]{1,0:T(8,128)(2,1)S(1)}, u32[]{:S(2)}, u32[]{:S(2)}) collective-permute-start(bf16[128,128]{1,0:T(8,128)(2,1)S(1)} %get-tuple-element.40), channel_id=1, source_target_pairs={{0,24},{8,0},{16,8},{24,16},{1,25},{9,1},{17,9},{25,17},{2,26},{10... | collective-permute-start | bytes 98312 | tf_op jit(solution)/shard_map/ppermute | solution.py:34
  24.6 1.3 copy-start.1
  31.5 46.9 %collective-permute-start.6 = (bf16[4,128,2048]{2,1,0:T(8,128)(2,1)}, bf16[4,128,2048]{2,1,0:T(8,128)(2,1)}, u32[]{:S(2)}, u32[]{:S(2)}) collective-permute-start(bf16[4,128,2048]{2,1,0:T(8,128)(2,1)} %bitcast.9), channel_id=1, source_target_pairs={{0,1},{1,0},{2,3},{3,2},{4,5},{5,4},{6,7},{7,6},{8,9},{9,8},{10,11... | collective-permute-start | bytes 6291464 | tf_op jit(solution)/shard_map/ppermute | solution.py:34
  31.5 4.6 %copy-start.3 = (bf16[128,2048]{1,0:T(8,128)(2,1)S(1)}, bf16[128,2048]{1,0:T(8,128)(2,1)}, u32[]{:S(2)}) copy-start(bf16[128,2048]{1,0:T(8,128)(2,1)} %rest_2_.1) | copy-start | bytes 1572868
  31.6 78.1 %all-to-all-start = ((bf16[4,8,256,128]{3,2,1,0:T(8,128)(2,1)}), bf16[4,8,256,128]{3,2,1,0:T(8,128)(2,1)}, u32[]{:S(2)}, u32[]{:S(2)}) async-start(bf16[4,8,256,128]{3,2,1,0:T(8,128)(2,1)} %bitcast.76), calls=%async_computation | async-start | bytes 4194304 | tf_op jit(solution)/shard_map/all_to_all | solution.py:406
  36.2 41.2 %collective-permute-start.10 = (bf16[128,2048]{1,0:T(8,128)(2,1)S(1)}, bf16[128,2048]{1,0:T(8,128)(2,1)S(1)}, u32[]{:S(2)}, u32[]{:S(2)}) collective-permute-start(bf16[128,2048]{1,0:T(8,128)(2,1)S(1)} %copy-done.3), channel_id=1, source_target_pairs={{0,2},{2,4},{4,6},{6,0},{1,3},{3,5},{5,7},{7,1},{8,10},{10,12},{12... | collective-permute-start | bytes 1572872 | tf_op jit(solution)/shard_map/ppermute | solution.py:34
  37.7 40.2 %collective-permute-start.11 = (bf16[128,2048]{1,0:T(8,128)(2,1)S(1)}, bf16[128,2048]{1,0:T(8,128)(2,1)}, u32[]{:S(2)}, u32[]{:S(2)}) collective-permute-start(bf16[128,2048]{1,0:T(8,128)(2,1)S(1)} %copy-done.3), channel_id=1, source_target_pairs={{0,4},{2,6},{4,0},{6,2},{1,5},{3,7},{5,1},{7,3},{8,12},{10,14},{12... | collective-permute-start | bytes 1572872 | tf_op jit(solution)/shard_map/ppermute | solution.py:34
  39.2 38.8 %collective-permute-start.12 = (bf16[128,2048]{1,0:T(8,128)(2,1)S(1)}, bf16[128,2048]{1,0:T(8,128)(2,1)}, u32[]{:S(2)}, u32[]{:S(2)}) collective-permute-start(bf16[128,2048]{1,0:T(8,128)(2,1)S(1)} %copy-done.3), channel_id=1, source_target_pairs={{0,6},{2,0},{4,2},{6,4},{1,7},{3,1},{5,3},{7,5},{8,14},{10,8},{12,... | collective-permute-start | bytes 1572872 | tf_op jit(solution)/shard_map/ppermute | solution.py:34
  40.7 24.9 %collective-permute-start.19 = (bf16[4,128,128]{2,1,0:T(8,128)(2,1)S(1)}, bf16[4,128,128]{2,1,0:T(8,128)(2,1)S(1)}, u32[]{:S(2)}, u32[]{:S(2)}) collective-permute-start(bf16[4,128,128]{2,1,0:T(8,128)(2,1)S(1)} %get-tuple-element.69), channel_id=1, source_target_pairs={{0,6},{2,0},{4,2},{6,4},{1,7},{3,1},{5,3},{7,5},{8,14},{10,8},{12,... | collective-permute-start | bytes 393224 | tf_op jit(solution)/shard_map/ppermute | solution.py:34
  65.6 5.2 %collective-permute-start.18 = (bf16[4,128,128]{2,1,0:T(8,128)(2,1)S(1)}, bf16[4,128,128]{2,1,0:T(8,128)(2,1)S(1)}, u32[]{:S(2)}, u32[]{:S(2)}) collective-permute-start(bf16[4,128,128]{2,1,0:T(8,128)(2,1)S(1)} %get-tuple-element.69), channel_id=1, source_target_pairs={{0,4},{2,6},{4,0},{6,2},{1,5},{3,7},{5,1},{7,3},{8,12},{10,14},{12... | collective-permute-start | bytes 393224 | tf_op jit(solution)/shard_map/ppermute | solution.py:34
  70.8 6.3 %collective-permute-start.17 = (bf16[4,128,128]{2,1,0:T(8,128)(2,1)S(1)}, bf16[4,128,128]{2,1,0:T(8,128)(2,1)S(1)}, u32[]{:S(2)}, u32[]{:S(2)}) collective-permute-start(bf16[4,128,128]{2,1,0:T(8,128)(2,1)S(1)} %get-tuple-element.69), channel_id=1, source_target_pairs={{0,2},{2,4},{4,6},{6,0},{1,3},{3,5},{5,7},{7,1},{8,10},{10,12},{12... | collective-permute-start | bytes 393224 | tf_op jit(solution)/shard_map/ppermute | solution.py:34
  77.2 4.9 %collective-permute-start.13 = (bf16[128,2048]{1,0:T(8,128)(2,1)S(1)}, bf16[128,2048]{1,0:T(8,128)(2,1)S(1)}, u32[]{:S(2)}, u32[]{:S(2)}) collective-permute-start(bf16[128,2048]{1,0:T(8,128)(2,1)S(1)} %copy-done.3), channel_id=1, source_target_pairs={{0,1},{1,0},{2,3},{3,2},{4,5},{5,4},{6,7},{7,6},{8,9},{9,8},{10,11... | collective-permute-start | bytes 1572872 | tf_op jit(solution)/shard_map/ppermute | solution.py:34
  77.3 4.8 %copy-start.5 = (bf16[128,2048]{1,0:T(8,128)(2,1)}, bf16[128,2048]{1,0:T(8,128)(2,1)S(1)}, u32[]{:S(2)}) copy-start(bf16[128,2048]{1,0:T(8,128)(2,1)S(1)} %collective-permute-done.10.rest_3_) | copy-start | bytes 1572868
  77.4 6.0 %collective-permute-start.20 = (bf16[4,4,128,128]{3,2,1,0:T(8,128)(2,1)S(1)}, bf16[4,4,128,128]{3,2,1,0:T(8,128)(2,1)S(1)}, u32[]{:S(2)}, u32[]{:S(2)}) collective-permute-start(bf16[4,4,128,128]{3,2,1,0:T(8,128)(2,1)S(1)} %pad_maximum_fusion.rest_0_), channel_id=1, source_target_pairs={{0,1},{1,0},{2,3},{3,2},{4,5},{5,4},{6,7},{7,6},{8,9},{9,8},{10,11... | collective-permute-start | bytes 1572872 | tf_op jit(solution)/shard_map/ppermute | solution.py:34
  77.9 7.8 %collective-permute-start.14 = (bf16[128,2048]{1,0:T(8,128)(2,1)S(1)}, bf16[128,2048]{1,0:T(8,128)(2,1)S(1)}, u32[]{:S(2)}, u32[]{:S(2)}) collective-permute-start(bf16[128,2048]{1,0:T(8,128)(2,1)S(1)} %collective-permute-done.10.rest_3_), channel_id=1, source_target_pairs={{0,1},{1,0},{2,3},{3,2},{4,5},{5,4},{6,7},{7,6},{8,9},{9,8},{10,11... | collective-permute-start | bytes 1572872 | tf_op jit(solution)/shard_map/ppermute | solution.py:34
  78.0 12.5 %collective-permute-start.15 = (bf16[128,2048]{1,0:T(8,128)(2,1)}, bf16[128,2048]{1,0:T(8,128)(2,1)}, u32[]{:S(2)}, u32[]{:S(2)}) collective-permute-start(bf16[128,2048]{1,0:T(8,128)(2,1)} %collective-permute-done.11.rest_4_), channel_id=1, source_target_pairs={{0,1},{1,0},{2,3},{3,2},{4,5},{5,4},{6,7},{7,6},{8,9},{9,8},{10,11... | collective-permute-start | bytes 1572872 | tf_op jit(solution)/shard_map/ppermute | solution.py:34
  78.4 12.1 %collective-permute-start.16 = (bf16[128,2048]{1,0:T(8,128)(2,1)}, bf16[128,2048]{1,0:T(8,128)(2,1)}, u32[]{:S(2)}, u32[]{:S(2)}) collective-permute-start(bf16[128,2048]{1,0:T(8,128)(2,1)} %collective-permute-done.12.rest_5_), channel_id=1, source_target_pairs={{0,1},{1,0},{2,3},{3,2},{4,5},{5,4},{6,7},{7,6},{8,9},{9,8},{10,11... | collective-permute-start | bytes 1572872 | tf_op jit(solution)/shard_map/ppermute | solution.py:34
  82.1 0.8 copy-start.7
  82.9 16.0 %collective-permute-start.7 = (bf16[128,2048]{1,0:T(8,128)(2,1)}, bf16[128,2048]{1,0:T(8,128)(2,1)}, u32[]{:S(2)}, u32[]{:S(2)}) collective-permute-start(bf16[128,2048]{1,0:T(8,128)(2,1)} %get-tuple-element.63), channel_id=1, source_target_pairs={{0,2},{2,4},{4,6},{6,0},{1,3},{3,5},{5,7},{7,1},{8,10},{10,12},{12... | collective-permute-start | bytes 1572872 | tf_op jit(solution)/shard_map/ppermute | solution.py:34
  83.4 0.8 copy-start.11
  84.2 25.4 %collective-permute-start.8 = (bf16[128,2048]{1,0:T(8,128)(2,1)}, bf16[128,2048]{1,0:T(8,128)(2,1)}, u32[]{:S(2)}, u32[]{:S(2)}) collective-permute-start(bf16[128,2048]{1,0:T(8,128)(2,1)} %get-tuple-element.62), channel_id=1, source_target_pairs={{0,4},{2,6},{4,0},{6,2},{1,5},{3,7},{5,1},{7,3},{8,12},{10,14},{12... | collective-permute-start | bytes 1572872 | tf_op jit(solution)/shard_map/ppermute | solution.py:34
  85.7 0.8 copy-start.9
  86.5 23.1 %collective-permute-start.9 = (bf16[128,2048]{1,0:T(8,128)(2,1)}, bf16[128,2048]{1,0:T(8,128)(2,1)}, u32[]{:S(2)}, u32[]{:S(2)}) collective-permute-start(bf16[128,2048]{1,0:T(8,128)(2,1)} %get-tuple-element.61), channel_id=1, source_target_pairs={{0,6},{2,0},{4,2},{6,4},{1,7},{3,1},{5,3},{7,5},{8,14},{10,8},{12,... | collective-permute-start | bytes 1572872 | tf_op jit(solution)/shard_map/ppermute | solution.py:34
  109.7 59.5 %all-to-all-start.1 = ((bf16[4,256,1024]{2,1,0:T(8,128)(2,1)}), bf16[4,256,1024]{2,1,0:T(8,128)(2,1)}, u32[]{:S(2)}, u32[]{:S(2)}) async-start(bf16[4,256,1024]{2,1,0:T(8,128)(2,1)} %bitcast.78), calls=%async_computation.1 | async-start | bytes 4194304 | tf_op jit(solution)/shard_map/all_to_all | solution.py:436
  114.2 16.1 %copy-start.6 = (bf16[128,2048]{1,0:T(8,128)(2,1)S(1)}, bf16[128,2048]{1,0:T(8,128)(2,1)}, u32[]{:S(2)}) copy-start(bf16[128,2048]{1,0:T(8,128)(2,1)} %copy-done.5) | copy-start | bytes 1572868
  114.2 16.1 %copy-start.8 = (bf16[128,2048]{1,0:T(8,128)(2,1)S(1)}, bf16[128,2048]{1,0:T(8,128)(2,1)}, u32[]{:S(2)}) copy-start(bf16[128,2048]{1,0:T(8,128)(2,1)} %copy-done.7) | copy-start | bytes 1572868
  114.2 16.1 %copy-start.10 = (bf16[128,2048]{1,0:T(8,128)(2,1)S(1)}, bf16[128,2048]{1,0:T(8,128)(2,1)}, u32[]{:S(2)}) copy-start(bf16[128,2048]{1,0:T(8,128)(2,1)} %copy-done.9) | copy-start | bytes 1572868
  116.6 1.4 collective-permute-start.21
  118.1 6.5 %collective-permute-start.24 = (bf16[4,128,128]{2,1,0:T(8,128)(2,1)S(1)}, bf16[4,128,128]{2,1,0:T(8,128)(2,1)S(1)}, u32[]{:S(2)}, u32[]{:S(2)}) collective-permute-start(bf16[4,128,128]{2,1,0:T(8,128)(2,1)S(1)} %fusion.3), channel_id=1, source_target_pairs={{0,6},{2,0},{4,2},{6,4},{1,7},{3,1},{5,3},{7,5},{8,14},{10,8},{12,... | collective-permute-start | bytes 393224 | tf_op jit(solution)/shard_map/ppermute | solution.py:34
  120.7 8.1 %collective-permute-start.23 = (bf16[4,128,128]{2,1,0:T(8,128)(2,1)S(1)}, bf16[4,128,128]{2,1,0:T(8,128)(2,1)S(1)}, u32[]{:S(2)}, u32[]{:S(2)}) collective-permute-start(bf16[4,128,128]{2,1,0:T(8,128)(2,1)S(1)} %fusion.3), channel_id=1, source_target_pairs={{0,4},{2,6},{4,0},{6,2},{1,5},{3,7},{5,1},{7,3},{8,12},{10,14},{12... | collective-permute-start | bytes 393224 | tf_op jit(solution)/shard_map/ppermute | solution.py:34
  121.2 7.6 %collective-permute-start.22 = (bf16[4,128,128]{2,1,0:T(8,128)(2,1)S(1)}, bf16[4,128,128]{2,1,0:T(8,128)(2,1)S(1)}, u32[]{:S(2)}, u32[]{:S(2)}) collective-permute-start(bf16[4,128,128]{2,1,0:T(8,128)(2,1)S(1)} %fusion.3), channel_id=1, source_target_pairs={{0,2},{2,4},{4,6},{6,0},{1,3},{3,5},{5,7},{7,1},{8,10},{10,12},{12... | collective-permute-start | bytes 393224 | tf_op jit(solution)/shard_map/ppermute | solution.py:34
  128.9 9.3 %copy-start.12 = (bf16[4,4,128,128]{3,2,1,0:T(8,128)(2,1)S(1)}, bf16[4,4,128,128]{3,2,1,0:T(8,128)(2,1)}, u32[]{:S(2)}) copy-start(bf16[4,4,128,128]{3,2,1,0:T(8,128)(2,1)} %copy-done.11) | copy-start | bytes 1572868
  128.9 1.4 collective-permute-start.25
  132.2 22.6 %collective-permute-start.26 = (bf16[8,16,256]{2,1,0:T(8,128)(2,1)S(1)}, bf16[8,16,256]{2,1,0:T(8,128)(2,1)S(1)}, u32[]{:S(2)}, u32[]{:S(2)}) collective-permute-start(bf16[8,16,256]{2,1,0:T(8,128)(2,1)S(1)} %get-tuple-element.66), channel_id=1, source_target_pairs={{0,8},{8,16},{16,24},{24,0},{1,9},{9,17},{17,25},{25,1},{2,10},{10... | collective-permute-start | bytes 196616 | tf_op jit(solution)/shard_map/ppermute | solution.py:34
  134.3 33.3 %collective-permute-start.27 = (bf16[8,16,256]{2,1,0:T(8,128)(2,1)S(1)}, bf16[8,16,256]{2,1,0:T(8,128)(2,1)S(1)}, u32[]{:S(2)}, u32[]{:S(2)}) collective-permute-start(bf16[8,16,256]{2,1,0:T(8,128)(2,1)S(1)} %get-tuple-element.65), channel_id=1, source_target_pairs={{0,16},{8,24},{16,0},{24,8},{1,17},{9,25},{17,1},{25,9},{2,18},{10... | collective-permute-start | bytes 196616 | tf_op jit(solution)/shard_map/ppermute | solution.py:34
  136.7 11.3 %copy-start.4 = (f32[128,2048]{1,0:T(8,128)S(1)}, f32[128,2048]{1,0:T(8,128)}, u32[]{:S(2)}) copy-start(f32[128,2048]{1,0:T(8,128)} %get-tuple-element.60.rest_0_) | copy-start | bytes 3145732
  136.7 31.0 %collective-permute-start.28 = (bf16[8,16,256]{2,1,0:T(8,128)(2,1)S(1)}, bf16[8,16,256]{2,1,0:T(8,128)(2,1)S(1)}, u32[]{:S(2)}, u32[]{:S(2)}) collective-permute-start(bf16[8,16,256]{2,1,0:T(8,128)(2,1)S(1)} %get-tuple-element.64), channel_id=1, source_target_pairs={{0,24},{8,0},{16,8},{24,16},{1,25},{9,1},{17,9},{25,17},{2,26},{10... | collective-permute-start | bytes 196616 | tf_op jit(solution)/shard_map/ppermute | solution.py:34

commit v4 on v3

v4 whole, which is shorter than its diff:
```python
import jax
import jax.numpy as jnp
from jax import lax
from jax.experimental import pallas as pl
from jax.experimental.pallas import tpu as pltpu
from jax.sharding import PartitionSpec as P

KEY_WIDTH = 1024
ADAPTER_RANK = 64
BLOCK = 128
RANKS = 2 * ADAPTER_RANK
WIDTH = 2 * KEY_WIDTH
VMEM_LIMIT = 48 * 1024 * 1024
LAST_BOTH = (((1,), (1,)), ((), ()))
FIRST_BOTH = (((0,), (0,)), ((), ()))
SMEM = pl.BlockSpec(memory_space=pltpu.SMEM)
VMEM = pl.BlockSpec(memory_space=pltpu.VMEM)
HBM = pl.BlockSpec(memory_space=pltpu.HBM)
ANY = pl.BlockSpec(memory_space=pl.ANY)


def call(kernel, name, **more):
    return pl.pallas_call(
        kernel,
        compiler_params=pltpu.CompilerParams(vmem_limit_bytes=VMEM_LIMIT),
        cost_estimate=pl.CostEstimate(flops=1024, bytes_accessed=1024, transcendentals=0),
        name=name,
        **more,
    )


def shift(piece, axis, step):
    count = lax.axis_size(axis)
    return lax.ppermute(piece, axis, [(i, (i + step) % count) for i in range(count)])


def wrap(index, count):
    return lax.rem(index + 2 * count, count)


def pick_up(at, slot_of, adapter_up, data_count):
    def kernel(at_ref, up_ref, *rest):
        out_refs, sems = rest[:data_count], rest[data_count]
        copies = []
        for k in range(data_count):
            data = wrap(at_ref[0] + k, data_count)
            slot = slot_of(at_ref, data, at_ref[3])
            copies.append(pltpu.make_async_copy(up_ref.at[slot], out_refs[k], sems.at[k]))
        for copy in copies:
            copy.start()
        for copy in copies:
            copy.wait()

    return call(
        kernel,
        "pick_up",
        out_shape=(jax.ShapeDtypeStruct(adapter_up.shape[1:], adapter_up.dtype),) * data_count,
        in_specs=[SMEM, HBM],
        out_specs=(VMEM,) * data_count,
        scratch_shapes=[pltpu.SemaphoreType.DMA((data_count,))],
    )(at, adapter_up)


def pick_down(at, slot_of, adapter_down, data_count, blocks_dev):
    def kernel(at_ref, down_ref, out_ref, sems):
        copies = [
            pltpu.make_async_copy(
                down_ref.at[slot_of(at_ref, data, block)], out_ref.at[data, block], sems.at[data, block]
            )
            for data in range(data_count)
            for block in range(blocks_dev)
        ]
        for copy in copies:
            copy.start()
        for copy in copies:
            copy.wait()

    return call(
        kernel,
        "pick_down",
        out_shape=jax.ShapeDtypeStruct(
            (data_count, blocks_dev) + adapter_down.shape[1:], adapter_down.dtype
        ),
        in_specs=[SMEM, HBM],
        out_specs=VMEM,
        scratch_shapes=[pltpu.SemaphoreType.DMA((data_count, blocks_dev))],
    )(at, adapter_down)


def base_product(at, tokens, weight, first, count):
    pipe_count, tensor_count, rows, depth = tokens.shape
    tile = 1024

    def kernel(at_ref, x_ref, w_ref, out_ref):
        x = x_ref[...].reshape(pipe_count * rows, depth)
        y = jnp.dot(x, w_ref[...], preferred_element_type=jnp.float32).astype(out_ref.dtype)
        for chip in range(pipe_count):
            out_ref[0, wrap(chip - at_ref[1], pipe_count)] = y[chip * rows : (chip + 1) * rows]

    return call(
        kernel,
        "base_product",
        grid_spec=pltpu.PrefetchScalarGridSpec(
            num_scalar_prefetch=1,
            grid=(WIDTH // tile, count),
            in_specs=[
                pl.BlockSpec(
                    (pipe_count, 1, rows, depth),
                    lambda n, s, at: (0, wrap(at[2] + s + first, tensor_count), 0, 0),
                ),
                pl.BlockSpec((depth, tile), lambda n, s, at: (0, n)),
            ],
            out_specs=pl.BlockSpec((1, pipe_count, rows, tile), lambda n, s, at: (s, 0, 0, n)),
        ),
        out_shape=jax.ShapeDtypeStruct((count, pipe_count, rows, WIDTH), jnp.bfloat16),
    )(at, tokens, weight)


def low_product(at, tokens, down, pipe_count, tensor_count):
    tok_dev, depth = tokens.shape
    rows = tok_dev // (pipe_count * tensor_count)

    def kernel(at_ref, x_ref, a_ref, out_ref):
        for block in range(tok_dev // BLOCK):
            a = a_ref[:, block].reshape(depth, RANKS)
            x = x_ref[block * BLOCK : (block + 1) * BLOCK]
            y = jnp.dot(x, a, preferred_element_type=jnp.float32).astype(out_ref.dtype)
            for part in range(BLOCK // rows):
                chip, core = divmod(block * (BLOCK // rows) + part, tensor_count)
                core = wrap(core - at_ref[2], tensor_count)
                out_ref[core, chip] = y[part * rows : (part + 1) * rows]

    return call(
        kernel,
        "low_product",
        in_specs=[SMEM, VMEM, VMEM],
        out_specs=VMEM,
        out_shape=jax.ShapeDtypeStruct((tensor_count, pipe_count, rows, RANKS), jnp.bfloat16),
    )(at, tokens, down)


def input_gradient(at, cot_pieces, weight, grad_pieces, down):
    data_count, blocks_dev, down_rows, _ = down.shape
    tensor_count, pipe_count = len(cot_pieces), len(cot_pieces[0])
    rows = cot_pieces[0][0].shape[0]
    depth = weight.shape[0]
    tok_dev = blocks_dev * BLOCK
    planes = next((n for n in range(1, data_count) if n * down_rows % 256 == 0), data_count)
    tile = planes * down_rows
    order = [(s, k) for s in range(tensor_count) for k in range(pipe_count)]

    def kernel(at_ref, w_ref, a_ref, *rest):
        grad_refs, rest = rest[:tensor_count], rest[tensor_count:]
        cot_refs, (out_ref, cot, grad, sems) = rest[: len(order)], rest[len(order) :]

        def first_row(s, k):
            chip = wrap(at_ref[1] - k, pipe_count)
            core = wrap(at_ref[2] - s, tensor_count)
            return pl.multiple_of((chip * tensor_count + core) * rows, rows)

        @pl.when(pl.program_id(0) == 0)
        def _():
            copies = [
                pltpu.make_async_copy(ref, cot.at[pl.ds(first_row(*at), rows)], sems.at[i])
                for i, (at, ref) in enumerate(zip(order, cot_refs))
            ]
            for copy in copies:
                copy.start()
            for s, k in order:
                grad[pl.ds(first_row(s, k), rows)] = grad_refs[s][k, 0]
            for copy in copies:
                copy.wait()

        base = lax.dot_general(cot[...], w_ref[...], LAST_BOTH, preferred_element_type=jnp.float32)
        for block in range(blocks_dev):
            at = slice(block * BLOCK, (block + 1) * BLOCK)
            a = a_ref[:, block].reshape(tile, RANKS)
            low = lax.dot_general(grad[at], a, LAST_BOTH, preferred_element_type=jnp.float32)
            out_ref[at] = (base[at] + low).astype(out_ref.dtype)

    grad_shape = (pipe_count, 1, rows, RANKS)
    return call(
        kernel,
        "input_gradient",
        grid=(data_count // planes,),
        in_specs=[
            SMEM,
            pl.BlockSpec((tile, WIDTH), lambda n: (n, 0)),
            pl.BlockSpec((planes, blocks_dev, down_rows, RANKS), lambda n: (n, 0, 0, 0)),
        ]
        + [pl.BlockSpec(grad_shape, lambda n: (0, 0, 0, 0))] * tensor_count
        + [ANY] * len(order),
        out_specs=pl.BlockSpec((tok_dev, tile), lambda n: (0, n)),
        out_shape=jax.ShapeDtypeStruct((tok_dev, depth), jnp.bfloat16),
        scratch_shapes=[
            pltpu.VMEM((tok_dev, WIDTH), jnp.bfloat16),
            pltpu.VMEM((tok_dev, RANKS), jnp.bfloat16),
            pltpu.SemaphoreType.DMA((len(order),)),
        ],
    )(at, weight, down, *grad_pieces, *[cot_pieces[s][k] for s, k in order])


def grad_down(at, slot_of, slots, x_features, grad_pieces):
    data_count, down_rows, tok_dev = x_features.shape
    tensor_count = len(grad_pieces)
    pipe_count, _, rows, _ = grad_pieces[0].shape
    blocks_dev = tok_dev // BLOCK

    def kernel(at_ref, x_ref, *rest):
        grad_refs, (out_ref, grad) = rest[:tensor_count], rest[tensor_count:]
        for s in range(tensor_count):
            core = wrap(at_ref[2] - s, tensor_count)
            for k in range(pipe_count):
                chip = wrap(at_ref[1] - k, pipe_count)
                first = pl.multiple_of((chip * tensor_count + core) * rows, rows)
                for m in range(data_count):
                    data = wrap(at_ref[0] - m, data_count)
                    grad[data, pl.ds(first, rows)] = grad_refs[s][k, m]
        out_ref[...] = jnp.zeros(out_ref.shape, out_ref.dtype)
        for data in range(data_count):
            for block in range(blocks_dev):
                slot = slot_of(at_ref, data, block)
                at = slice(block * BLOCK, (block + 1) * BLOCK)
                out_ref[slot] += jnp.dot(
                    x_ref[data, :, at], grad[data, at], preferred_element_type=jnp.float32
                )

    return call(
        kernel,
        "grad_down",
        in_specs=[SMEM, VMEM] + [VMEM] * tensor_count,
        out_specs=VMEM,
        out_shape=jax.ShapeDtypeStruct((slots, down_rows, RANKS), jnp.float32),
        scratch_shapes=[pltpu.VMEM((data_count, tok_dev, RANKS), jnp.bfloat16)],
    )(at, x_features, *grad_pieces)


def grad_up_pieces(at, low_pieces, cot_pieces, data_count, up_rows):
    tensor_count, pipe_count = len(cot_pieces), len(cot_pieces[0])
    group_count = tensor_count * pipe_count
    rows = cot_pieces[0][0].shape[0]
    cols = WIDTH // group_count
    tok_dev = group_count * rows
    blocks_dev = tok_dev // BLOCK
    group_half = group_count // 2
    order = [(s, k) for s in range(tensor_count) for k in range(pipe_count)]
    pieces = [cot_pieces[s][k] for s, k in order]
    in_kernel = cols % 128 == 0
    if not in_kernel:
        first_col = (at[1] * tensor_count + at[2]) * cols
        pieces = [lax.dynamic_slice_in_dim(piece, first_col, cols, 1) for piece in pieces]

    def kernel(at_ref, *rest):
        low_refs, rest = rest[:tensor_count], rest[tensor_count:]
        cot_refs, (out_ref, low, cot, sems) = rest[: len(order)], rest[len(order) :]
        my_group = at_ref[1] * tensor_count + at_ref[2]
        copies = []
        for i, (s, k) in enumerate(order):
            core = wrap(at_ref[2] - s, tensor_count)
            chip = wrap(at_ref[1] - k, pipe_count)
            first = pl.multiple_of((chip * tensor_count + core) * rows, rows)
            piece = cot_refs[i]
            if in_kernel:
                piece = piece.at[:, pl.ds(pl.multiple_of(my_group * cols, cols), cols)]
            copies.append(pltpu.make_async_copy(piece, cot.at[pl.ds(first, rows)], sems.at[i]))
        for copy in copies:
            copy.start()
        for s in range(tensor_count):
            core = wrap(at_ref[2] - s, tensor_count)
            for k in range(pipe_count):
                first = pl.multiple_of((k * tensor_count + core) * rows, rows)
                low[pl.ds(first, rows)] = low_refs[s][k]
        for copy in copies:
            copy.wait()
        for block in range(blocks_dev):
            at = slice(block * BLOCK, (block + 1) * BLOCK)
            both = lax.dot_general(low[at], cot[at], FIRST_BOTH, preferred_element_type=jnp.float32)
            half = jnp.where(my_group < group_half, both[:ADAPTER_RANK], both[ADAPTER_RANK:])
            half = half.astype(out_ref.dtype)
            for data in range(data_count):
                k = wrap(data - at_ref[0], data_count)
                out_ref[k, block] = half[data * up_rows : (data + 1) * up_rows]

    return call(
        kernel,
        "grad_up_pieces",
        in_specs=[SMEM] + [VMEM] * tensor_count + [ANY] * len(order),
        out_specs=VMEM,
        out_shape=jax.ShapeDtypeStruct((data_count, blocks_dev, up_rows, cols), jnp.bfloat16),
        scratch_shapes=[
            pltpu.VMEM((tok_dev, RANKS), jnp.bfloat16),
            pltpu.VMEM((tok_dev, cols), jnp.bfloat16),
            pltpu.SemaphoreType.DMA((len(order),)),
        ],
    )(at, *low_pieces, *pieces)


def grad_up(at, slot_of, slots, pieces):
    data_count = len(pieces)
    blocks_dev, up_rows, cols = pieces[0].shape

    def kernel(at_ref, *rest):
        piece_refs, out_ref = rest[:data_count], rest[data_count]
        out_ref[...] = jnp.zeros(out_ref.shape, out_ref.dtype)
        for k in range(data_count):
            data = wrap(at_ref[0] - k, data_count)
            for block in range(blocks_dev):
                slot = slot_of(at_ref, data, block)
                out_ref[slot] += piece_refs[k][block].astype(out_ref.dtype)

    return call(
        kernel,
        "grad_up",
        in_specs=[SMEM] + [VMEM] * data_count,
        out_specs=VMEM,
        out_shape=jax.ShapeDtypeStruct((slots, up_rows, cols), jnp.float32),
    )(at, *pieces)


def own_rows(at, up, cotangent):
    data_count = len(up)
    rows = cotangent.shape[0]

    def kernel(at_ref, cot_ref, *rest):
        up_refs, (b_ref, grad_ref) = rest[:data_count], rest[data_count:]
        pieces = []
        for data in range(data_count):
            came = wrap(at_ref[0] - data, data_count)
            piece = up_refs[0][...]
            for k in range(1, data_count):
                piece = jnp.where(came == k, up_refs[k][...], piece)
            pieces.append(piece)
        b = jnp.concatenate(pieces, axis=0)
        b_ref[...] = b
        cot = cot_ref[...]
        grad_ref[...] = jnp.concatenate(
            [
                lax.dot_general(cot[:, half], b[:, half], LAST_BOTH, preferred_element_type=jnp.float32)
                for half in (slice(0, KEY_WIDTH), slice(KEY_WIDTH, WIDTH))
            ],
            axis=1,
        ).astype(grad_ref.dtype)

    return call(
        kernel,
        "own_rows",
        in_specs=[SMEM, VMEM] + [VMEM] * data_count,
        out_specs=(VMEM, VMEM),
        out_shape=(
            jax.ShapeDtypeStruct((ADAPTER_RANK, WIDTH), jnp.bfloat16),
            jax.ShapeDtypeStruct((rows, RANKS), jnp.bfloat16),
        ),
    )(at, cotangent, *up)


def keys_and_values(at, base_pieces, low_sum, b_own):
    rows = base_pieces[0].shape[0]
    count = len(base_pieces)

    def kernel(at_ref, low_ref, b_ref, *rest):
        base_refs, out_ref = rest[:count], rest[count]
        low = low_ref[at_ref[1]]
        for first, ranks in ((0, slice(0, ADAPTER_RANK)), (KEY_WIDTH, slice(ADAPTER_RANK, RANKS))):
            at = slice(first, first + KEY_WIDTH)
            y = jnp.dot(low[:, ranks], b_ref[:, at], preferred_element_type=jnp.float32)
            for base_ref in base_refs:
                y += base_ref[:, at].astype(jnp.float32)
            out_ref[:, at] = y.astype(out_ref.dtype)

    return call(
        kernel,
        "keys_and_values",
        in_specs=[SMEM, VMEM, VMEM] + [VMEM] * count,
        out_specs=VMEM,
        out_shape=jax.ShapeDtypeStruct((rows, WIDTH), jnp.bfloat16),
    )(at, low_sum, b_own, *base_pieces)


def body(
    tokens, key_value_weight, adapter_down, adapter_up, tenant_of_block, slot_of_tenant, cotangent
):
    data_count = lax.axis_size("dp")
    pipe_count = lax.axis_size("pipe")
    tensor_count = lax.axis_size("tensor")
    group_count = pipe_count * tensor_count
    at_data, at_pipe, at_tensor = (lax.axis_index(a) for a in ("dp", "pipe", "tensor"))
    my_group = at_pipe * tensor_count + at_tensor
    tok_dev, feature_count = tokens.shape
    blocks_dev = tok_dev // BLOCK
    rows = tok_dev // group_count
    down_rows = adapter_down.shape[1]
    up_rows = adapter_up.shape[1]
    slots = adapter_down.shape[0]
    blocks = tenant_of_block.shape[0]

    own_block = my_group * rows // BLOCK
    at = jnp.stack([at_data, at_pipe, at_tensor, own_block]).astype(jnp.int32)
    at = jnp.concatenate([at, tenant_of_block, slot_of_tenant])

    def slot_of(at_ref, data, block):
        return at_ref[4 + blocks + at_ref[4 + data * blocks_dev + block]]

    b_send = pick_up(at, slot_of, adapter_up, data_count)
    b_came = [b_send[0]] + [shift(b_send[k], "dp", k) for k in range(1, data_count)]
    a_send = pick_down(at, slot_of, adapter_down, data_count, blocks_dev)
    a_send, b_came = lax.optimization_barrier((a_send, b_came))
    a_recv = lax.all_to_all(a_send, "dp", 0, 0, tiled=True)
    b_own, grad_rows = own_rows(at, b_came, cotangent)

    cot_send, a_send = lax.optimization_barrier((cotangent, a_send))
    cot_chips = [cotangent] + [shift(cot_send, "pipe", k) for k in range(1, pipe_count)]

    base_tokens, cot_chips[1] = lax.optimization_barrier((tokens, cot_chips[1]))
    tokens_by_group = base_tokens.reshape(pipe_count, tensor_count, rows, feature_count)
    base_send = base_product(at, tokens_by_group, key_value_weight, 1, tensor_count - 1)
    base_came = [shift(base_send[s - 1], "tensor", s) for s in range(1, tensor_count)]
    tokens_by_group, cot_chips = lax.optimization_barrier((tokens_by_group, cot_chips))
    base_keep = base_product(at, tokens_by_group, key_value_weight, 0, 1)[0]
    base_chip = [
        sum([base_keep[k].astype(jnp.float32)] + [b[k].astype(jnp.float32) for b in base_came])
        for k in range(pipe_count)
    ]
    base_chip_came = [
        shift(base_chip[k].astype(jnp.bfloat16), "pipe", k) for k in range(1, pipe_count)
    ]
    grad_rows, cot_chips, base_chip = lax.optimization_barrier((grad_rows, cot_chips, base_chip))
    grad_data = [grad_rows] + [shift(grad_rows, "dp", k) for k in range(1, data_count)]

    x_send = tokens.T.reshape(data_count, down_rows, tok_dev)
    a_recv, x_send, grad_data = lax.optimization_barrier((a_recv, x_send, grad_data))
    x_recv = lax.all_to_all(x_send, "dp", 0, 0, tiled=True)

    cot_pieces = [cot_chips] + [
        [shift(piece, "tensor", s) for piece in cot_chips] for s in range(1, tensor_count)
    ]
    grad_data = jnp.stack(grad_data)
    grad_chips = jnp.stack([grad_data] + [shift(grad_data, "pipe", k) for k in range(1, pipe_count)])
    grad_pieces = [grad_chips] + [shift(grad_chips, "tensor", s) for s in range(1, tensor_count)]

    low_part = low_product(at, tokens, a_recv, pipe_count, tensor_count)
    low_core = sum(
        [low_part[0].astype(jnp.float32)]
        + [shift(low_part[s], "tensor", s).astype(jnp.float32) for s in range(1, tensor_count)]
    ).astype(jnp.bfloat16)
    low_sum = sum(
        [low_core.astype(jnp.float32)]
        + [shift(low_core, "pipe", k).astype(jnp.float32) for k in range(1, pipe_count)]
    ).astype(jnp.bfloat16)
    low_pieces = [low_sum] + [shift(low_sum, "tensor", s) for s in range(1, tensor_count)]
    key_value = keys_and_values(at, base_chip[:1] + base_chip_came, low_sum, b_own)

    up_pieces = grad_up_pieces(at, low_pieces, cot_pieces, data_count, up_rows)
    up_came = [up_pieces[0]] + [shift(up_pieces[k], "dp", k) for k in range(1, data_count)]
    grad_b = grad_up(at, slot_of, slots, up_came)

    input_grad = input_gradient(at, cot_pieces, key_value_weight, grad_pieces, a_recv)
    grad_a = grad_down(at, slot_of, slots, x_recv, grad_pieces)
    return (key_value, input_grad, grad_a, grad_b)


def solution(mesh):
    atd = (
        P("dp", ("pipe", "tensor")),
        P(("pipe", "tensor"), None),
        P(None, ("pipe", "tensor", "dp"), None),
        P(None, "dp", None),
        P(),
        P(),
        P(("dp", "pipe", "tensor"), None),
    )
    return jax.shard_map(
        body,
        mesh=mesh,
        in_specs=atd,
        out_specs=(
            P(("dp", "pipe", "tensor"), None),
            P("dp", ("pipe", "tensor")),
            P(None, ("pipe", "tensor", "dp"), None),
            P(None, "dp", ("pipe", "tensor")),
        ),
        check_vma=False,
    )
```

time: 174 us -> 146 us (0.84)
  waiting for transfers between devices: 78.8 us -> 50.5 us
  starting transfers between devices: 41.2 us -> 45.9 us
  local copies, waits for them, and re-layouts: 10.1 us -> 8.14 us
    ppermute x29, waiting for transfers between devices: 78.8 us -> 50.5 us  [shift(): lax.ppermute(piece, axis, [(i, (i + step) % count) for i in range(count)])]
    ppermute x29, starting transfers between devices: 32.1 us -> 37 us  [shift(): lax.ppermute(piece, axis, [(i, (i + step) % count) for i in range(count)])]
    add x1 -> x0, other arithmetic: 3.6 us -> none  [body(): sum([base_keep[k].astype(jnp.float32)] + [b[k].astype(jnp.float32) for b...]
    unnamed x38 -> x30, local copies, waits for them, and re-layouts: 7.51 us -> 4.82 us
    convert_element_type x0 -> x1, other arithmetic: none -> 2.06 us  [body(): base_chip[k].astype(jnp.bfloat16)]
  transfers between devices with their start and end apart: 31 -> 31, of which waited for: 13 -> 10; matrix products, arithmetic and copies ran while one was open for 4% -> 4% of each run, Pallas kernels for 15% -> 22%
where the time goes in v4:
time: 146 us; the launch traced here: 145 us
  waiting for transfers between devices  50.5 us (35%)
  starting transfers between devices  45.9 us (31%)
  Pallas kernels  36.9 us (25%)
  local copies, waits for them, and re-layouts  8.14 us (6%)
  other arithmetic  3.03 us (2%)
    ppermute x29, waiting for transfers between devices, shift(): lax.ppermute(piece, axis, [(i, (i + step) % count) for i in range(count)])  50.5 us
    ppermute x29, starting transfers between devices, shift(): lax.ppermute(piece, axis, [(i, (i + step) % count) for i in range(count)])  37 us
    pallas_call x2, Pallas kernels, base_product(): call(kernel, 'base_product', grid_spec=pltpu.PrefetchScalarGridSpec(num_s...  9.67 us
    pallas_call x1, Pallas kernels, input_gradient(): call(kernel, 'input_gradient', grid=(data_count // planes,), in_specs=[SM...  9.41 us
    unnamed x30, local copies, waits for them, and re-layouts  4.82 us
    all_to_all x1, starting transfers between devices, body(): x_recv = lax.all_to_all(x_send, 'dp', 0, 0, tiled=True)  4.45 us
    all_to_all x1, starting transfers between devices, body(): a_recv = lax.all_to_all(a_send, 'dp', 0, 0, tiled=True)  4.45 us
    pallas_call x1, Pallas kernels, grad_down(): call(kernel, 'grad_down', in_specs=[SMEM, VMEM] + [VMEM] * tensor_count,...  4.31 us
  transfers between devices with their start and end apart: 31, of which 10 were waited for; matrix products, arithmetic and copies ran while one was open for 4% of the time, Pallas kernels for 22%

profile of v4, /device:TPU:0, one launch (start us, length us, event | category | flops | bytes accessed | tf_op | source)
XLA Modules:
  0.0 145.4 jit_solution(16205929325589170140)
XLA Ops:
  0.6 0.8 concatenate.3.at_ref
  1.4 1.4 copy-done.6
  2.8 0.9 pick_up.1
  3.8 0.0 copy-start.2
  3.8 3.1 %collective-permute-start = (bf16[16,2048]{1,0:T(8,128)(2,1)S(1)}, bf16[16,2048]{1,0:T(8,128)(2,1)S(1)}, u32[]{:S(2)}, u32[]{:S(2)}) collective-permute-start(bf16[16,2048]{1,0:T(8,128)(2,1)S(1)} %get-tuple-element.36), channel_id=1, source_target_pairs={{0,8},{8,16},{16,24},{24,0},{1,9},{9,17},{17,25},{25,1},{2,10},{10... | collective-permute-start | bytes 196616 | tf_op jit(solution)/shard_map/ppermute | solution.py:34
  6.8 2.6 %collective-permute-start.1 = (bf16[16,2048]{1,0:T(8,128)(2,1)S(1)}, bf16[16,2048]{1,0:T(8,128)(2,1)S(1)}, u32[]{:S(2)}, u32[]{:S(2)}) collective-permute-start(bf16[16,2048]{1,0:T(8,128)(2,1)S(1)} %get-tuple-element.37), channel_id=1, source_target_pairs={{0,16},{8,24},{16,0},{24,8},{1,17},{9,25},{17,1},{25,9},{2,18},{10... | collective-permute-start | bytes 196616 | tf_op jit(solution)/shard_map/ppermute | solution.py:34
  9.4 1.3 collective-permute-start.2
  10.8 3.7 %pick_down.1 = bf16[4,8,256,128]{3,2,1,0:T(8,128)(2,1)S(1)} custom-call(s32[60]{0:T(128)S(1)} %concatenate.3.at_ref, bf16[24,256,128]{2,1,0:T(8,128)(2,1)S(1)} %copy-done.7), custom_call_target="tpu_custom_call" | custom-call | flops 1024 | bytes 1024 | tf_op jit(solution)/shard_map/pick_down/pallas_call | solution.py:78
  14.5 0.0 copy-start.1
  14.5 1.3 copy-done.1
  15.8 0.6 copy-done.8
  16.4 0.6 copy-done.10
  17.1 1.5 %collective-permute-start.3 = (bf16[128,2048]{1,0:T(8,128)(2,1)S(1)}, bf16[128,2048]{1,0:T(8,128)(2,1)S(1)}, u32[]{:S(2)}, u32[]{:S(2)}) collective-permute-start(bf16[128,2048]{1,0:T(8,128)(2,1)S(1)} %copy-done.2), channel_id=1, source_target_pairs={{0,2},{2,4},{4,6},{6,0},{1,3},{3,5},{5,7},{7,1},{8,10},{10,12},{12... | collective-permute-start | bytes 1572872 | tf_op jit(solution)/shard_map/ppermute | solution.py:34
  18.6 4.4 %all-to-all-start = ((bf16[4,8,256,128]{3,2,1,0:T(8,128)(2,1)}), bf16[4,8,256,128]{3,2,1,0:T(8,128)(2,1)}, u32[]{:S(2)}, u32[]{:S(2)}) async-start(bf16[4,8,256,128]{3,2,1,0:T(8,128)(2,1)} %copy-done.1), calls=%async_computation | async-start | bytes 4194304 | tf_op jit(solution)/shard_map/all_to_all | solution.py:407
  23.0 7.8 %collective-permute-done.3.rest_3_ = bf16[128,2048]{1,0:T(8,128)(2,1)S(1)} collective-permute-done((bf16[128,2048]{1,0:T(8,128)(2,1)S(1)}, bf16[128,2048]{1,0:T(8,128)(2,1)S(1)}, u32[]{:S(2)}, u32[]{:S(2)}) %collective-permute-start.3) | collective-permute-done | bytes 524320 | tf_op jit(solution)/shard_map/ppermute | solution.py:34
  30.8 4.8 %base_product.3 = bf16[1,4,128,2048]{3,2,1,0:T(8,128)(2,1)S(1)} custom-call(s32[60]{0:T(128)S(1)} %concatenate.3.at_ref, bf16[4,2,128,1024]{3,2,1,0:T(8,128)(2,1)S(1)} %bitcast.84, bf16[1024,2048]{1,0:T(8,128)(2,1)} %w_ref.5), custom_call_target="tpu_custom_call" | custom-call | flops 1024 | bytes 1024 | tf_op jit(solution)/shard_map/base_product/pallas_call | solution.py:100
  35.6 0.1 collective-permute-start.6
  35.7 1.6 %collective-permute-start.4 = (bf16[128,2048]{1,0:T(8,128)(2,1)S(1)}, bf16[128,2048]{1,0:T(8,128)(2,1)S(1)}, u32[]{:S(2)}, u32[]{:S(2)}) collective-permute-start(bf16[128,2048]{1,0:T(8,128)(2,1)S(1)} %copy-done.2), channel_id=1, source_target_pairs={{0,4},{2,6},{4,0},{6,2},{1,5},{3,7},{5,1},{7,3},{8,12},{10,14},{12... | collective-permute-start | bytes 1572872 | tf_op jit(solution)/shard_map/ppermute | solution.py:34
  37.3 0.5 collective-permute-start.5
  37.9 1.5 %own_rows.1 = (bf16[64,2048]{1,0:T(8,128)(2,1)S(1)}, bf16[128,128]{1,0:T(8,128)(2,1)}) custom-call(s32[60]{0:T(128)S(1)} %concatenate.3.at_ref, bf16[128,2048]{1,0:T(8,128)(2,1)S(1)} %copy-done.2, bf16[16,2048]{1,0:T(8,128)(2,1)S(1)} %get-tuple-element.40.rest_0_, bf16[16,2048]{1,0:T(8,128)(2,1)S(1)} %collective-permute-done.rest_1_, ...), custom_call_target="tpu_custom_call" | custom-call | flops 1024 | bytes 1024 | tf_op jit(solution)/shard_map/own_rows/pallas_call | solution.py:344
  39.4 10.7 %collective-permute-done.4.rest_4_ = bf16[128,2048]{1,0:T(8,128)(2,1)S(1)} collective-permute-done((bf16[128,2048]{1,0:T(8,128)(2,1)S(1)}, bf16[128,2048]{1,0:T(8,128)(2,1)S(1)}, u32[]{:S(2)}, u32[]{:S(2)}) %collective-permute-start.4) | collective-permute-done | bytes 524320 | tf_op jit(solution)/shard_map/ppermute | solution.py:34
  50.1 0.8 copy-done.4
  50.9 0.6 collective-permute-done.5.rest_5_
  51.4 4.8 %base_product.2 = bf16[1,4,128,2048]{3,2,1,0:T(8,128)(2,1)S(1)} custom-call(s32[60]{0:T(128)S(1)} %concatenate.3.at_ref, bf16[4,2,128,1024]{3,2,1,0:T(8,128)(2,1)S(1)} %bitcast.85, bf16[1024,2048]{1,0:T(8,128)(2,1)} %w_ref.5), custom_call_target="tpu_custom_call" | custom-call | flops 1024 | bytes 1024 | tf_op jit(solution)/shard_map/base_product/pallas_call | solution.py:100
  56.3 2.1 %fusion.4 = (bf16[128,2048]{1,0:T(8,128)(2,1)}, bf16[128,2048]{1,0:T(8,128)(2,1)}, bf16[128,2048]{1,0:T(8,128)(2,1)}, f32[128,2048]{1,0:T(8,128)}) fusion(bf16[4,128,2048]{2,1,0:T(8,128)(2,1)S(1)} %collective-permute-done.6, bf16[1,4,128,2048]{3,2,1,0:T(8,128)(2,1)S(1)} %base_product.2), kind=kLoop, calls=%fused_computation.26 | loop fusion | flops 3932160 | bytes 6815744 | tf_op jit(solution)/shard_map/convert_element_type | solution.py:424
  58.3 0.7 collective-permute-start.7
  59.0 0.3 collective-permute-start.8
  59.3 2.8 %collective-permute-start.9 = (bf16[128,128]{1,0:T(8,128)(2,1)}, bf16[128,128]{1,0:T(8,128)(2,1)S(1)}, u32[]{:S(2)}, u32[]{:S(2)}) collective-permute-start(bf16[128,128]{1,0:T(8,128)(2,1)} %get-tuple-element.57), channel_id=1, source_target_pairs={{0,24},{8,0},{16,8},{24,16},{1,25},{9,1},{17,9},{25,17},{2,26},{10... | collective-permute-start | bytes 98312 | tf_op jit(solution)/shard_map/ppermute | solution.py:34
  62.2 2.5 %copy.11 = bf16[1024,1024]{1,0:T(8,128)(2,1)} copy(bf16[1024,1024]{0,1:T(8,128)(2,1)S(1)} %bitcast.86) | data formatting | bytes 4194304 | tf_op jit(solution)/shard_map/transpose | solution.py:429
  64.7 8.1 %collective-permute-done.8 = bf16[128,128]{1,0:T(8,128)(2,1)S(1)} collective-permute-done((bf16[128,128]{1,0:T(8,128)(2,1)}, bf16[128,128]{1,0:T(8,128)(2,1)S(1)}, u32[]{:S(2)}, u32[]{:S(2)}) %collective-permute-start.8) | collective-permute-done | bytes 32800 | tf_op jit(solution)/shard_map/ppermute | solution.py:34
  72.8 4.5 %all-to-all-start.1 = ((bf16[4,256,1024]{2,1,0:T(8,128)(2,1)}), bf16[4,256,1024]{2,1,0:T(8,128)(2,1)}, u32[]{:S(2)}, u32[]{:S(2)}) async-start(bf16[4,256,1024]{2,1,0:T(8,128)(2,1)} %bitcast.88), calls=%async_computation.1 | async-start | bytes 4194304 | tf_op jit(solution)/shard_map/all_to_all | solution.py:431
  77.3 0.1 collective-permute-start.21
  77.3 0.5 collective-permute-start.22
  77.8 0.1 collective-permute-start.23
  77.9 2.3 %low_product.1 = bf16[2,4,128,128]{3,2,1,0:T(8,128)(2,1)S(1)} custom-call(s32[60]{0:T(128)S(1)} %concatenate.3.at_ref, bf16[1024,1024]{1,0:T(8,128)(2,1)S(1)} %copy-done, bf16[4,8,256,128]{3,2,1,0:T(8,128)(2,1)} %all-to-all-done.a_ref), custom_call_target="tpu_custom_call" | custom-call | flops 1024 | bytes 1024 | tf_op jit(solution)/shard_map/low_product/pallas_call | solution.py:133
  80.3 0.5 collective-permute-start.10
  80.8 0.1 collective-permute-start.24
  80.9 0.8 fusion.1
  81.7 4.4 %collective-permute-start.19 = (bf16[4,128,128]{2,1,0:T(8,128)(2,1)S(1)}, bf16[4,128,128]{2,1,0:T(8,128)(2,1)S(1)}, u32[]{:S(2)}, u32[]{:S(2)}) collective-permute-start(bf16[4,128,128]{2,1,0:T(8,128)(2,1)S(1)} %get-tuple-element.75), channel_id=1, source_target_pairs={{0,6},{2,0},{4,2},{6,4},{1,7},{3,1},{5,3},{7,5},{8,14},{10,8},{12,... | collective-permute-start | bytes 393224 | tf_op jit(solution)/shard_map/ppermute | solution.py:34
  86.1 0.5 collective-permute-start.18
  86.6 0.1 collective-permute-start.17
  86.7 3.2 %collective-permute-done.19 = bf16[4,128,128]{2,1,0:T(8,128)(2,1)S(1)} collective-permute-done((bf16[4,128,128]{2,1,0:T(8,128)(2,1)S(1)}, bf16[4,128,128]{2,1,0:T(8,128)(2,1)S(1)}, u32[]{:S(2)}, u32[]{:S(2)}) %collective-permute-start.19) | collective-permute-done | bytes 131104 | tf_op jit(solution)/shard_map/ppermute | solution.py:34
  89.9 3.4 %collective-permute-start.13 = (bf16[4,128,128]{2,1,0:T(8,128)(2,1)S(1)}, bf16[4,128,128]{2,1,0:T(8,128)(2,1)S(1)}, u32[]{:S(2)}, u32[]{:S(2)}) collective-permute-start(bf16[4,128,128]{2,1,0:T(8,128)(2,1)S(1)} %fusion), channel_id=1, source_target_pairs={{0,6},{2,0},{4,2},{6,4},{1,7},{3,1},{5,3},{7,5},{8,14},{10,8},{12,... | collective-permute-start | bytes 393224 | tf_op jit(solution)/shard_map/ppermute | solution.py:34
  93.3 1.1 collective-permute-done.18
  94.4 0.5 collective-permute-start.12
  94.9 0.4 collective-permute-start.11
  95.4 0.1 pad_maximum_fusion.rest_0_
  95.5 2.6 %collective-permute-start.14 = (bf16[128,2048]{1,0:T(8,128)(2,1)S(1)}, bf16[128,2048]{1,0:T(8,128)(2,1)S(1)}, u32[]{:S(2)}, u32[]{:S(2)}) collective-permute-start(bf16[128,2048]{1,0:T(8,128)(2,1)S(1)} %copy-done.14), channel_id=1, source_target_pairs={{0,2},{2,4},{4,6},{6,0},{1,3},{3,5},{5,7},{7,1},{8,10},{10,12},{12... | collective-permute-start | bytes 1572872 | tf_op jit(solution)/shard_map/ppermute | solution.py:34
  98.1 0.5 collective-permute-start.15
  98.6 15.8 %collective-permute-done.12 = bf16[4,128,128]{2,1,0:T(8,128)(2,1)S(1)} collective-permute-done((bf16[4,128,128]{2,1,0:T(8,128)(2,1)S(1)}, bf16[4,128,128]{2,1,0:T(8,128)(2,1)S(1)}, u32[]{:S(2)}, u32[]{:S(2)}) %collective-permute-start.12) | collective-permute-done | bytes 131104 | tf_op jit(solution)/shard_map/ppermute | solution.py:34
  114.4 0.1 collective-permute-start.20
  114.5 0.1 add_convert_fusion.low_ref.rest_0_
  114.6 0.6 collective-permute-start.25
  115.1 1.4 collective-permute-done.25.rest_1_
  116.6 1.8 %grad_up_pieces.1 = bf16[4,8,16,256]{3,2,1,0:T(8,128)(2,1)S(1)} custom-call(s32[60]{0:T(128)S(1)} %concatenate.3.at_ref, bf16[4,128,128]{2,1,0:T(8,128)(2,1)S(1)} %add_convert_fusion.low_ref.rest_0_, bf16[4,128,128]{2,1,0:T(8,128)(2,1)S(1)} %collective-permute-done.25.rest_1_, bf16[128,2048]{1,0:T(8,128)(2,1)S(1)} %copy-done.2, ...), custom_call_target="tpu_custom_call" | custom-call | flops 1024 | bytes 1024 | tf_op jit(solution)/shard_map/grad_up_pieces/pallas_call | solution.py:284
  118.4 2.0 %collective-permute-start.26 = (bf16[8,16,256]{2,1,0:T(8,128)(2,1)S(1)}, bf16[8,16,256]{2,1,0:T(8,128)(2,1)S(1)}, u32[]{:S(2)}, u32[]{:S(2)}) collective-permute-start(bf16[8,16,256]{2,1,0:T(8,128)(2,1)S(1)} %get-tuple-element.72), channel_id=1, source_target_pairs={{0,8},{8,16},{16,24},{24,0},{1,9},{9,17},{17,25},{25,1},{2,10},{10... | collective-permute-start | bytes 196616 | tf_op jit(solution)/shard_map/ppermute | solution.py:34
  120.5 2.4 %collective-permute-start.27 = (bf16[8,16,256]{2,1,0:T(8,128)(2,1)S(1)}, bf16[8,16,256]{2,1,0:T(8,128)(2,1)S(1)}, u32[]{:S(2)}, u32[]{:S(2)}) collective-permute-start(bf16[8,16,256]{2,1,0:T(8,128)(2,1)S(1)} %get-tuple-element.71), channel_id=1, source_target_pairs={{0,16},{8,24},{16,0},{24,8},{1,17},{9,25},{17,1},{25,9},{2,18},{10... | collective-permute-start | bytes 196616 | tf_op jit(solution)/shard_map/ppermute | solution.py:34
  122.8 1.7 %collective-permute-done.15.rest_2_ = bf16[128,2048]{1,0:T(8,128)(2,1)S(1)} collective-permute-done((bf16[128,2048]{1,0:T(8,128)(2,1)S(1)}, bf16[128,2048]{1,0:T(8,128)(2,1)S(1)}, u32[]{:S(2)}, u32[]{:S(2)}) %collective-permute-start.15) | collective-permute-done | bytes 524320 | tf_op jit(solution)/shard_map/ppermute | solution.py:34
  124.6 3.8 %collective-permute-start.28 = (bf16[8,16,256]{2,1,0:T(8,128)(2,1)S(1)}, bf16[8,16,256]{2,1,0:T(8,128)(2,1)S(1)}, u32[]{:S(2)}, u32[]{:S(2)}) collective-permute-start(bf16[8,16,256]{2,1,0:T(8,128)(2,1)S(1)} %get-tuple-element.70), channel_id=1, source_target_pairs={{0,24},{8,0},{16,8},{24,16},{1,25},{9,1},{17,9},{25,17},{2,26},{10... | collective-permute-start | bytes 196616 | tf_op jit(solution)/shard_map/ppermute | solution.py:34
  128.3 1.8 %keys_and_values.1 = bf16[128,2048]{1,0:T(8,128)(2,1)} custom-call(s32[60]{0:T(128)S(1)} %concatenate.3.at_ref, bf16[4,128,128]{2,1,0:T(8,128)(2,1)S(1)} %add_convert_fusion.low_ref.rest_0_, bf16[64,2048]{1,0:T(8,128)(2,1)S(1)} %get-tuple-element.55.b_ref, f32[128,2048]{1,0:T(8,128)S(1)} %copy-done.3, bf16[128,2048]{1,0:T(8,128)(2,1)S(1)} %collective-permute-done.14.rest_1_, ...), custom_call_target="tpu_custom_call" | custom-call | flops 1024 | bytes 1024 | tf_op jit(solution)/shard_map/keys_and_values/pallas_call | solution.py:370
  130.1 0.1 collective-permute-done.28.rest_3_
  130.2 1.5 %grad_up.1 = f32[24,16,256]{2,1,0:T(8,128)} custom-call(s32[60]{0:T(128)S(1)} %concatenate.3.at_ref, bf16[8,16,256]{2,1,0:T(8,128)(2,1)S(1)} %get-tuple-element.73.rest_0_, bf16[8,16,256]{2,1,0:T(8,128)(2,1)S(1)} %collective-permute-done.26.rest_1_, bf16[8,16,256]{2,1,0:T(8,128)(2,1)S(1)} %collective-permute-done.27.rest_2_, ...), custom_call_target="tpu_custom_call" | custom-call | flops 1024 | bytes 1024 | tf_op jit(solution)/shard_map/grad_up/pallas_call | solution.py:311
  131.7 9.4 %input_gradient.1 = bf16[1024,1024]{1,0:T(8,128)(2,1)} custom-call(s32[60]{0:T(128)S(1)} %concatenate.3.at_ref, bf16[1024,2048]{1,0:T(8,128)(2,1)} %w_ref.5, bf16[4,8,256,128]{3,2,1,0:T(8,128)(2,1)} %all-to-all-done.a_ref, bf16[4,4,128,128]{3,2,1,0:T(8,128)(2,1)S(1)} %pad_maximum_fusion.rest_0_, ...), custom_call_target="tpu_custom_call" | custom-call | flops 1024 | bytes 1024 | tf_op jit(solution)/shard_map/input_gradient/pallas_call | solution.py:182
  141.1 4.3 %grad_down.1 = f32[24,256,128]{2,1,0:T(8,128)} custom-call(s32[60]{0:T(128)S(1)} %concatenate.3.at_ref, bf16[4,256,1024]{2,1,0:T(8,128)(2,1)} %all-to-all-done.1.x_ref, bf16[4,4,128,128]{3,2,1,0:T(8,128)(2,1)S(1)} %pad_maximum_fusion.rest_0_, bf16[4,4,128,128]{3,2,1,0:T(8,128)(2,1)S(1)} %collective-permute-done.20.rest_1_), custom_call_target="tpu_custom_call" | custom-call | flops 1024 | bytes 1024 | tf_op jit(solution)/shard_map/grad_down/pallas_call | solution.py:228
  (48 shorter events, 0.2 us)
Async XLA Ops:
  1.4 1.4 copy-start.6
  2.8 8.0 %copy-start.7 = (bf16[24,256,128]{2,1,0:T(8,128)(2,1)S(1)}, bf16[24,256,128]{2,1,0:T(8,128)(2,1)}, u32[]{:S(2)}) copy-start(bf16[24,256,128]{2,1,0:T(8,128)(2,1)} %down_ref.1) | copy-start | bytes 4718596
  3.8 13.3 %copy-start.2 = (bf16[128,2048]{1,0:T(8,128)(2,1)S(1)}, bf16[128,2048]{1,0:T(8,128)(2,1)}, u32[]{:S(2)}) copy-start(bf16[128,2048]{1,0:T(8,128)(2,1)} %rest_2_.1) | copy-start | bytes 1572868
  3.8 12.0 %collective-permute-start = (bf16[16,2048]{1,0:T(8,128)(2,1)S(1)}, bf16[16,2048]{1,0:T(8,128)(2,1)S(1)}, u32[]{:S(2)}, u32[]{:S(2)}) collective-permute-start(bf16[16,2048]{1,0:T(8,128)(2,1)S(1)} %get-tuple-element.36), channel_id=1, source_target_pairs={{0,8},{8,16},{16,24},{24,0},{1,9},{9,17},{17,25},{25,1},{2,10},{10... | collective-permute-start | bytes 196616 | tf_op jit(solution)/shard_map/ppermute | solution.py:34
  6.8 9.0 %collective-permute-start.1 = (bf16[16,2048]{1,0:T(8,128)(2,1)S(1)}, bf16[16,2048]{1,0:T(8,128)(2,1)S(1)}, u32[]{:S(2)}, u32[]{:S(2)}) collective-permute-start(bf16[16,2048]{1,0:T(8,128)(2,1)S(1)} %get-tuple-element.37), channel_id=1, source_target_pairs={{0,16},{8,24},{16,0},{24,8},{1,17},{9,25},{17,1},{25,9},{2,18},{10... | collective-permute-start | bytes 196616 | tf_op jit(solution)/shard_map/ppermute | solution.py:34
  9.4 7.0 %collective-permute-start.2 = (bf16[16,2048]{1,0:T(8,128)(2,1)S(1)}, bf16[16,2048]{1,0:T(8,128)(2,1)S(1)}, u32[]{:S(2)}, u32[]{:S(2)}) collective-permute-start(bf16[16,2048]{1,0:T(8,128)(2,1)S(1)} %get-tuple-element.38), channel_id=1, source_target_pairs={{0,24},{8,0},{16,8},{24,16},{1,25},{9,1},{17,9},{25,17},{2,26},{10... | collective-permute-start | bytes 196616 | tf_op jit(solution)/shard_map/ppermute | solution.py:34
  14.5 1.3 copy-start.1
  15.8 0.6 copy-start.8
  16.4 0.6 copy-start.10
  17.1 13.7 %copy-start = (bf16[1024,1024]{1,0:T(8,128)(2,1)S(1)}, bf16[1024,1024]{1,0:T(8,128)(2,1)}, u32[]{:S(2)}) copy-start(bf16[1024,1024]{1,0:T(8,128)(2,1)} %x_ref.1) | copy-start | bytes 6291460
  17.1 13.7 %collective-permute-start.3 = (bf16[128,2048]{1,0:T(8,128)(2,1)S(1)}, bf16[128,2048]{1,0:T(8,128)(2,1)S(1)}, u32[]{:S(2)}, u32[]{:S(2)}) collective-permute-start(bf16[128,2048]{1,0:T(8,128)(2,1)S(1)} %copy-done.2), channel_id=1, source_target_pairs={{0,2},{2,4},{4,6},{6,0},{1,3},{3,5},{5,7},{7,1},{8,10},{10,12},{12... | collective-permute-start | bytes 1572872 | tf_op jit(solution)/shard_map/ppermute | solution.py:34
  18.6 54.2 %all-to-all-start = ((bf16[4,8,256,128]{3,2,1,0:T(8,128)(2,1)}), bf16[4,8,256,128]{3,2,1,0:T(8,128)(2,1)}, u32[]{:S(2)}, u32[]{:S(2)}) async-start(bf16[4,8,256,128]{3,2,1,0:T(8,128)(2,1)} %copy-done.1), calls=%async_computation | async-start | bytes 4194304 | tf_op jit(solution)/shard_map/all_to_all | solution.py:407
  30.8 7.0 %copy-start.9 = (bf16[16,2048]{1,0:T(8,128)(2,1)S(1)}, bf16[16,2048]{1,0:T(8,128)(2,1)}, u32[]{:S(2)}) copy-start(bf16[16,2048]{1,0:T(8,128)(2,1)} %copy-done.8) | copy-start | bytes 196612
  30.8 7.0 %copy-start.11 = (bf16[16,2048]{1,0:T(8,128)(2,1)S(1)}, bf16[16,2048]{1,0:T(8,128)(2,1)}, u32[]{:S(2)}) copy-start(bf16[16,2048]{1,0:T(8,128)(2,1)} %copy-done.10) | copy-start | bytes 196612
  35.6 20.6 %collective-permute-start.6 = (bf16[4,128,2048]{2,1,0:T(8,128)(2,1)S(1)}, bf16[4,128,2048]{2,1,0:T(8,128)(2,1)S(1)}, u32[]{:S(2)}, u32[]{:S(2)}) collective-permute-start(bf16[4,128,2048]{2,1,0:T(8,128)(2,1)S(1)} %bitcast.87), channel_id=1, source_target_pairs={{0,1},{1,0},{2,3},{3,2},{4,5},{5,4},{6,7},{7,6},{8,9},{9,8},{10,11... | collective-permute-start | bytes 6291464 | tf_op jit(solution)/shard_map/ppermute | solution.py:34
  35.7 14.3 %collective-permute-start.4 = (bf16[128,2048]{1,0:T(8,128)(2,1)S(1)}, bf16[128,2048]{1,0:T(8,128)(2,1)S(1)}, u32[]{:S(2)}, u32[]{:S(2)}) collective-permute-start(bf16[128,2048]{1,0:T(8,128)(2,1)S(1)} %copy-done.2), channel_id=1, source_target_pairs={{0,4},{2,6},{4,0},{6,2},{1,5},{3,7},{5,1},{7,3},{8,12},{10,14},{12... | collective-permute-start | bytes 1572872 | tf_op jit(solution)/shard_map/ppermute | solution.py:34
  37.3 14.1 %collective-permute-start.5 = (bf16[128,2048]{1,0:T(8,128)(2,1)S(1)}, bf16[128,2048]{1,0:T(8,128)(2,1)}, u32[]{:S(2)}, u32[]{:S(2)}) collective-permute-start(bf16[128,2048]{1,0:T(8,128)(2,1)S(1)} %copy-done.2), channel_id=1, source_target_pairs={{0,6},{2,0},{4,2},{6,4},{1,7},{3,1},{5,3},{7,5},{8,14},{10,8},{12,... | collective-permute-start | bytes 1572872 | tf_op jit(solution)/shard_map/ppermute | solution.py:34
  50.1 0.8 copy-start.4
  58.3 6.4 %collective-permute-start.7 = (bf16[128,128]{1,0:T(8,128)(2,1)}, bf16[128,128]{1,0:T(8,128)(2,1)S(1)}, u32[]{:S(2)}, u32[]{:S(2)}) collective-permute-start(bf16[128,128]{1,0:T(8,128)(2,1)} %get-tuple-element.57), channel_id=1, source_target_pairs={{0,8},{8,16},{16,24},{24,0},{1,9},{9,17},{17,25},{25,1},{2,10},{10... | collective-permute-start | bytes 98312 | tf_op jit(solution)/shard_map/ppermute | solution.py:34
  59.0 13.8 %collective-permute-start.8 = (bf16[128,128]{1,0:T(8,128)(2,1)}, bf16[128,128]{1,0:T(8,128)(2,1)S(1)}, u32[]{:S(2)}, u32[]{:S(2)}) collective-permute-start(bf16[128,128]{1,0:T(8,128)(2,1)} %get-tuple-element.57), channel_id=1, source_target_pairs={{0,16},{8,24},{16,0},{24,8},{1,17},{9,25},{17,1},{25,9},{2,18},{10... | collective-permute-start | bytes 98312 | tf_op jit(solution)/shard_map/ppermute | solution.py:34
  59.3 13.4 %collective-permute-start.9 = (bf16[128,128]{1,0:T(8,128)(2,1)}, bf16[128,128]{1,0:T(8,128)(2,1)S(1)}, u32[]{:S(2)}, u32[]{:S(2)}) collective-permute-start(bf16[128,128]{1,0:T(8,128)(2,1)} %get-tuple-element.57), channel_id=1, source_target_pairs={{0,24},{8,0},{16,8},{24,16},{1,25},{9,1},{17,9},{25,17},{2,26},{10... | collective-permute-start | bytes 98312 | tf_op jit(solution)/shard_map/ppermute | solution.py:34
  72.8 68.3 %all-to-all-start.1 = ((bf16[4,256,1024]{2,1,0:T(8,128)(2,1)}), bf16[4,256,1024]{2,1,0:T(8,128)(2,1)}, u32[]{:S(2)}, u32[]{:S(2)}) async-start(bf16[4,256,1024]{2,1,0:T(8,128)(2,1)} %bitcast.88), calls=%async_computation.1 | async-start | bytes 4194304 | tf_op jit(solution)/shard_map/all_to_all | solution.py:431
  77.3 4.4 %collective-permute-start.21 = (bf16[128,2048]{1,0:T(8,128)(2,1)S(1)}, bf16[128,2048]{1,0:T(8,128)(2,1)S(1)}, u32[]{:S(2)}, u32[]{:S(2)}) collective-permute-start(bf16[128,2048]{1,0:T(8,128)(2,1)S(1)} %copy-done.2), channel_id=1, source_target_pairs={{0,1},{1,0},{2,3},{3,2},{4,5},{5,4},{6,7},{7,6},{8,9},{9,8},{10,11... | collective-permute-start | bytes 1572872 | tf_op jit(solution)/shard_map/ppermute | solution.py:34
  77.3 8.7 %collective-permute-start.22 = (bf16[128,2048]{1,0:T(8,128)(2,1)S(1)}, bf16[128,2048]{1,0:T(8,128)(2,1)S(1)}, u32[]{:S(2)}, u32[]{:S(2)}) collective-permute-start(bf16[128,2048]{1,0:T(8,128)(2,1)S(1)} %collective-permute-done.3.rest_3_), channel_id=1, source_target_pairs={{0,1},{1,0},{2,3},{3,2},{4,5},{5,4},{6,7},{7,6},{8,9},{9,8},{10,11... | collective-permute-start | bytes 1572872 | tf_op jit(solution)/shard_map/ppermute | solution.py:34
  77.8 17.6 %collective-permute-start.23 = (bf16[128,2048]{1,0:T(8,128)(2,1)}, bf16[128,2048]{1,0:T(8,128)(2,1)S(1)}, u32[]{:S(2)}, u32[]{:S(2)}) collective-permute-start(bf16[128,2048]{1,0:T(8,128)(2,1)} %copy-done.4), channel_id=1, source_target_pairs={{0,1},{1,0},{2,3},{3,2},{4,5},{5,4},{6,7},{7,6},{8,9},{9,8},{10,11... | collective-permute-start | bytes 1572872 | tf_op jit(solution)/shard_map/ppermute | solution.py:34
  80.2 15.2 %copy-start.14 = (bf16[128,2048]{1,0:T(8,128)(2,1)S(1)}, bf16[128,2048]{1,0:T(8,128)(2,1)}, u32[]{:S(2)}) copy-start(bf16[128,2048]{1,0:T(8,128)(2,1)} %get-tuple-element.67) | copy-start | bytes 1572868
  80.3 17.8 %copy-start.13 = (bf16[128,2048]{1,0:T(8,128)(2,1)S(1)}, bf16[128,2048]{1,0:T(8,128)(2,1)}, u32[]{:S(2)}) copy-start(bf16[128,2048]{1,0:T(8,128)(2,1)} %get-tuple-element.68) | copy-start | bytes 1572868
  80.3 34.1 %copy-start.12 = (bf16[128,2048]{1,0:T(8,128)(2,1)S(1)}, bf16[128,2048]{1,0:T(8,128)(2,1)}, u32[]{:S(2)}) copy-start(bf16[128,2048]{1,0:T(8,128)(2,1)} %get-tuple-element.66) | copy-start | bytes 1572868
  80.3 36.3 %copy-start.5 = (bf16[128,2048]{1,0:T(8,128)(2,1)S(1)}, bf16[128,2048]{1,0:T(8,128)(2,1)}, u32[]{:S(2)}) copy-start(bf16[128,2048]{1,0:T(8,128)(2,1)} %copy-done.4) | copy-start | bytes 1572868
  80.3 6.3 %collective-permute-start.10 = (bf16[4,128,128]{2,1,0:T(8,128)(2,1)S(1)}, bf16[4,128,128]{2,1,0:T(8,128)(2,1)S(1)}, u32[]{:S(2)}, u32[]{:S(2)}) collective-permute-start(bf16[4,128,128]{2,1,0:T(8,128)(2,1)S(1)} %slice_bitcast_fusion.8), channel_id=1, source_target_pairs={{0,1},{1,0},{2,3},{3,2},{4,5},{5,4},{6,7},{7,6},{8,9},{9,8},{10,11... | collective-permute-start | bytes 393224 | tf_op jit(solution)/shard_map/ppermute | solution.py:34
  80.8 33.8 %collective-permute-start.24 = (bf16[128,2048]{1,0:T(8,128)(2,1)}, bf16[128,2048]{1,0:T(8,128)(2,1)S(1)}, u32[]{:S(2)}, u32[]{:S(2)}) collective-permute-start(bf16[128,2048]{1,0:T(8,128)(2,1)} %collective-permute-done.5.rest_5_), channel_id=1, source_target_pairs={{0,1},{1,0},{2,3},{3,2},{4,5},{5,4},{6,7},{7,6},{8,9},{9,8},{10,11... | collective-permute-start | bytes 1572872 | tf_op jit(solution)/shard_map/ppermute | solution.py:34
  81.7 8.2 %collective-permute-start.19 = (bf16[4,128,128]{2,1,0:T(8,128)(2,1)S(1)}, bf16[4,128,128]{2,1,0:T(8,128)(2,1)S(1)}, u32[]{:S(2)}, u32[]{:S(2)}) collective-permute-start(bf16[4,128,128]{2,1,0:T(8,128)(2,1)S(1)} %get-tuple-element.75), channel_id=1, source_target_pairs={{0,6},{2,0},{4,2},{6,4},{1,7},{3,1},{5,3},{7,5},{8,14},{10,8},{12,... | collective-permute-start | bytes 393224 | tf_op jit(solution)/shard_map/ppermute | solution.py:34
  86.1 8.4 %collective-permute-start.18 = (bf16[4,128,128]{2,1,0:T(8,128)(2,1)S(1)}, bf16[4,128,128]{2,1,0:T(8,128)(2,1)S(1)}, u32[]{:S(2)}, u32[]{:S(2)}) collective-permute-start(bf16[4,128,128]{2,1,0:T(8,128)(2,1)S(1)} %get-tuple-element.75), channel_id=1, source_target_pairs={{0,4},{2,6},{4,0},{6,2},{1,5},{3,7},{5,1},{7,3},{8,12},{10,14},{12... | collective-permute-start | bytes 393224 | tf_op jit(solution)/shard_map/ppermute | solution.py:34
  86.6 8.4 %collective-permute-start.17 = (bf16[4,128,128]{2,1,0:T(8,128)(2,1)S(1)}, bf16[4,128,128]{2,1,0:T(8,128)(2,1)S(1)}, u32[]{:S(2)}, u32[]{:S(2)}) collective-permute-start(bf16[4,128,128]{2,1,0:T(8,128)(2,1)S(1)} %get-tuple-element.75), channel_id=1, source_target_pairs={{0,2},{2,4},{4,6},{6,0},{1,3},{3,5},{5,7},{7,1},{8,10},{10,12},{12... | collective-permute-start | bytes 393224 | tf_op jit(solution)/shard_map/ppermute | solution.py:34
  89.9 8.2 %collective-permute-start.13 = (bf16[4,128,128]{2,1,0:T(8,128)(2,1)S(1)}, bf16[4,128,128]{2,1,0:T(8,128)(2,1)S(1)}, u32[]{:S(2)}, u32[]{:S(2)}) collective-permute-start(bf16[4,128,128]{2,1,0:T(8,128)(2,1)S(1)} %fusion), channel_id=1, source_target_pairs={{0,6},{2,0},{4,2},{6,4},{1,7},{3,1},{5,3},{7,5},{8,14},{10,8},{12,... | collective-permute-start | bytes 393224 | tf_op jit(solution)/shard_map/ppermute | solution.py:34
  94.4 20.0 %collective-permute-start.12 = (bf16[4,128,128]{2,1,0:T(8,128)(2,1)S(1)}, bf16[4,128,128]{2,1,0:T(8,128)(2,1)S(1)}, u32[]{:S(2)}, u32[]{:S(2)}) collective-permute-start(bf16[4,128,128]{2,1,0:T(8,128)(2,1)S(1)} %fusion), channel_id=1, source_target_pairs={{0,4},{2,6},{4,0},{6,2},{1,5},{3,7},{5,1},{7,3},{8,12},{10,14},{12... | collective-permute-start | bytes 393224 | tf_op jit(solution)/shard_map/ppermute | solution.py:34
  94.9 19.5 %collective-permute-start.11 = (bf16[4,128,128]{2,1,0:T(8,128)(2,1)S(1)}, bf16[4,128,128]{2,1,0:T(8,128)(2,1)S(1)}, u32[]{:S(2)}, u32[]{:S(2)}) collective-permute-start(bf16[4,128,128]{2,1,0:T(8,128)(2,1)S(1)} %fusion), channel_id=1, source_target_pairs={{0,2},{2,4},{4,6},{6,0},{1,3},{3,5},{5,7},{7,1},{8,10},{10,12},{12... | collective-permute-start | bytes 393224 | tf_op jit(solution)/shard_map/ppermute | solution.py:34
  95.5 25.0 %collective-permute-start.14 = (bf16[128,2048]{1,0:T(8,128)(2,1)S(1)}, bf16[128,2048]{1,0:T(8,128)(2,1)S(1)}, u32[]{:S(2)}, u32[]{:S(2)}) collective-permute-start(bf16[128,2048]{1,0:T(8,128)(2,1)S(1)} %copy-done.14), channel_id=1, source_target_pairs={{0,2},{2,4},{4,6},{6,0},{1,3},{3,5},{5,7},{7,1},{8,10},{10,12},{12... | collective-permute-start | bytes 1572872 | tf_op jit(solution)/shard_map/ppermute | solution.py:34
  98.1 26.5 %collective-permute-start.15 = (bf16[128,2048]{1,0:T(8,128)(2,1)S(1)}, bf16[128,2048]{1,0:T(8,128)(2,1)S(1)}, u32[]{:S(2)}, u32[]{:S(2)}) collective-permute-start(bf16[128,2048]{1,0:T(8,128)(2,1)S(1)} %copy-done.13), channel_id=1, source_target_pairs={{0,4},{2,6},{4,0},{6,2},{1,5},{3,7},{5,1},{7,3},{8,12},{10,14},{12... | collective-permute-start | bytes 1572872 | tf_op jit(solution)/shard_map/ppermute | solution.py:34
  114.4 13.9 %collective-permute-start.16 = (bf16[128,2048]{1,0:T(8,128)(2,1)S(1)}, bf16[128,2048]{1,0:T(8,128)(2,1)S(1)}, u32[]{:S(2)}, u32[]{:S(2)}) collective-permute-start(bf16[128,2048]{1,0:T(8,128)(2,1)S(1)} %copy-done.12), channel_id=1, source_target_pairs={{0,6},{2,0},{4,2},{6,4},{1,7},{3,1},{5,3},{7,5},{8,14},{10,8},{12,... | collective-permute-start | bytes 1572872 | tf_op jit(solution)/shard_map/ppermute | solution.py:34
  114.4 17.3 %collective-permute-start.20 = (bf16[4,4,128,128]{3,2,1,0:T(8,128)(2,1)S(1)}, bf16[4,4,128,128]{3,2,1,0:T(8,128)(2,1)S(1)}, u32[]{:S(2)}, u32[]{:S(2)}) collective-permute-start(bf16[4,4,128,128]{3,2,1,0:T(8,128)(2,1)S(1)} %pad_maximum_fusion.rest_0_), channel_id=1, source_target_pairs={{0,1},{1,0},{2,3},{3,2},{4,5},{5,4},{6,7},{7,6},{8,9},{9,8},{10,11... | collective-permute-start | bytes 1572872 | tf_op jit(solution)/shard_map/ppermute | solution.py:34
  114.6 13.8 %copy-start.3 = (f32[128,2048]{1,0:T(8,128)S(1)}, f32[128,2048]{1,0:T(8,128)}, u32[]{:S(2)}) copy-start(f32[128,2048]{1,0:T(8,128)} %get-tuple-element.56.rest_0_) | copy-start | bytes 3145732
  114.6 2.0 %collective-permute-start.25 = (bf16[4,128,128]{2,1,0:T(8,128)(2,1)S(1)}, bf16[4,128,128]{2,1,0:T(8,128)(2,1)S(1)}, u32[]{:S(2)}, u32[]{:S(2)}) collective-permute-start(bf16[4,128,128]{2,1,0:T(8,128)(2,1)S(1)} %add_convert_fusion.low_ref.rest_0_), channel_id=1, source_target_pairs={{0,1},{1,0},{2,3},{3,2},{4,5},{5,4},{6,7},{7,6},{8,9},{9,8},{10,11... | collective-permute-start | bytes 393224 | tf_op jit(solution)/shard_map/ppermute | solution.py:34
  118.4 11.7 %collective-permute-start.26 = (bf16[8,16,256]{2,1,0:T(8,128)(2,1)S(1)}, bf16[8,16,256]{2,1,0:T(8,128)(2,1)S(1)}, u32[]{:S(2)}, u32[]{:S(2)}) collective-permute-start(bf16[8,16,256]{2,1,0:T(8,128)(2,1)S(1)} %get-tuple-element.72), channel_id=1, source_target_pairs={{0,8},{8,16},{16,24},{24,0},{1,9},{9,17},{17,25},{25,1},{2,10},{10... | collective-permute-start | bytes 196616 | tf_op jit(solution)/shard_map/ppermute | solution.py:34
  120.5 9.6 %collective-permute-start.27 = (bf16[8,16,256]{2,1,0:T(8,128)(2,1)S(1)}, bf16[8,16,256]{2,1,0:T(8,128)(2,1)S(1)}, u32[]{:S(2)}, u32[]{:S(2)}) collective-permute-start(bf16[8,16,256]{2,1,0:T(8,128)(2,1)S(1)} %get-tuple-element.71), channel_id=1, source_target_pairs={{0,16},{8,24},{16,0},{24,8},{1,17},{9,25},{17,1},{25,9},{2,18},{10... | collective-permute-start | bytes 196616 | tf_op jit(solution)/shard_map/ppermute | solution.py:34
  124.6 5.7 %collective-permute-start.28 = (bf16[8,16,256]{2,1,0:T(8,128)(2,1)S(1)}, bf16[8,16,256]{2,1,0:T(8,128)(2,1)S(1)}, u32[]{:S(2)}, u32[]{:S(2)}) collective-permute-start(bf16[8,16,256]{2,1,0:T(8,128)(2,1)S(1)} %get-tuple-element.70), channel_id=1, source_target_pairs={{0,24},{8,0},{16,8},{24,16},{1,25},{9,1},{17,9},{25,17},{2,26},{10... | collective-permute-start | bytes 196616 | tf_op jit(solution)/shard_map/ppermute | solution.py:34

commit v5 on v4

--- a/solution.py
+++ b/solution.py
@@ -10,7 +10,8 @@
 BLOCK = 128
 RANKS = 2 * ADAPTER_RANK
 WIDTH = 2 * KEY_WIDTH
-VMEM_LIMIT = 48 * 1024 * 1024
+VMEM_LIMIT = 24 * 1024 * 1024
+VMEM_MOST = 60 * 1024 * 1024
 LAST_BOTH = (((1,), (1,)), ((), ()))
 FIRST_BOTH = (((0,), (0,)), ((), ()))
 SMEM = pl.BlockSpec(memory_space=pltpu.SMEM)
@@ -19,10 +20,10 @@
 ANY = pl.BlockSpec(memory_space=pl.ANY)
 
 
-def call(kernel, name, **more):
+def call(kernel, name, vmem=VMEM_LIMIT, **more):
     return pl.pallas_call(
         kernel,
-        compiler_params=pltpu.CompilerParams(vmem_limit_bytes=VMEM_LIMIT),
+        compiler_params=pltpu.CompilerParams(vmem_limit_bytes=vmem),
         cost_estimate=pl.CostEstimate(flops=1024, bytes_accessed=1024, transcendentals=0),
         name=name,
         **more,
@@ -54,6 +55,7 @@
     return call(
         kernel,
         "pick_up",
+        VMEM_MOST,
         out_shape=(jax.ShapeDtypeStruct(adapter_up.shape[1:], adapter_up.dtype),) * data_count,
         in_specs=[SMEM, HBM],
         out_specs=(VMEM,) * data_count,
@@ -62,28 +64,20 @@
 
 
 def pick_down(at, slot_of, adapter_down, data_count, blocks_dev):
-    def kernel(at_ref, down_ref, out_ref, sems):
-        copies = [
-            pltpu.make_async_copy(
-                down_ref.at[slot_of(at_ref, data, block)], out_ref.at[data, block], sems.at[data, block]
-            )
-            for data in range(data_count)
-            for block in range(blocks_dev)
-        ]
-        for copy in copies:
-            copy.start()
-        for copy in copies:
-            copy.wait()
+    rows, ranks = adapter_down.shape[1:]
+
+    def kernel(at_ref, down_ref, out_ref):
+        data = pl.program_id(0)
+        for block in range(blocks_dev):
+            out_ref[0, block] = down_ref[slot_of(at_ref, data, block)]
 
     return call(
         kernel,
         "pick_down",
-        out_shape=jax.ShapeDtypeStruct(
-            (data_count, blocks_dev) + adapter_down.shape[1:], adapter_down.dtype
-        ),
-        in_specs=[SMEM, HBM],
-        out_specs=VMEM,
-        scratch_shapes=[pltpu.SemaphoreType.DMA((data_count, blocks_dev))],
+        grid=(data_count,),
+        out_shape=jax.ShapeDtypeStruct((data_count, blocks_dev, rows, ranks), adapter_down.dtype),
+        in_specs=[SMEM, VMEM],
+        out_specs=pl.BlockSpec((1, blocks_dev, rows, ranks), lambda d: (d, 0, 0, 0)),
     )(at, adapter_down)
 
 
@@ -408,22 +402,23 @@
     b_own, grad_rows = own_rows(at, b_came, cotangent)
 
     cot_send, a_send = lax.optimization_barrier((cotangent, a_send))
-    cot_chips = [cotangent] + [shift(cot_send, "pipe", k) for k in range(1, pipe_count)]
-
-    base_tokens, cot_chips[1] = lax.optimization_barrier((tokens, cot_chips[1]))
+    cot_cores = [shift(cot_send, "tensor", s) for s in range(1, tensor_count)]
+
+    base_tokens, cot_cores = lax.optimization_barrier((tokens, cot_cores))
     tokens_by_group = base_tokens.reshape(pipe_count, tensor_count, rows, feature_count)
     base_send = base_product(at, tokens_by_group, key_value_weight, 1, tensor_count - 1)
     base_came = [shift(base_send[s - 1], "tensor", s) for s in range(1, tensor_count)]
-    tokens_by_group, cot_chips = lax.optimization_barrier((tokens_by_group, cot_chips))
     base_keep = base_product(at, tokens_by_group, key_value_weight, 0, 1)[0]
     base_chip = [
         sum([base_keep[k].astype(jnp.float32)] + [b[k].astype(jnp.float32) for b in base_came])
         for k in range(pipe_count)
     ]
-    base_chip_came = [
-        shift(base_chip[k].astype(jnp.bfloat16), "pipe", k) for k in range(1, pipe_count)
-    ]
-    grad_rows, cot_chips, base_chip = lax.optimization_barrier((grad_rows, cot_chips, base_chip))
+    base_chip[1:] = [piece.astype(jnp.bfloat16) for piece in base_chip[1:]]
+    base_chip_came = [shift(base_chip[k], "pipe", k) for k in range(1, pipe_count)]
+
+    cot_send, base_chip = lax.optimization_barrier((cot_send, base_chip))
+    cot_chips = [cotangent] + [shift(cot_send, "pipe", k) for k in range(1, pipe_count)]
+    grad_rows, base_chip_came = lax.optimization_barrier((grad_rows, base_chip_came))
     grad_data = [grad_rows] + [shift(grad_rows, "dp", k) for k in range(1, data_count)]
 
     x_send = tokens.T.reshape(data_count, down_rows, tok_dev)
@@ -431,21 +426,23 @@
     x_recv = lax.all_to_all(x_send, "dp", 0, 0, tiled=True)
 
     cot_pieces = [cot_chips] + [
-        [shift(piece, "tensor", s) for piece in cot_chips] for s in range(1, tensor_count)
+        [cot_cores[s - 1]] + [shift(piece, "tensor", s) for piece in cot_chips[1:]]
+        for s in range(1, tensor_count)
     ]
     grad_data = jnp.stack(grad_data)
     grad_chips = jnp.stack([grad_data] + [shift(grad_data, "pipe", k) for k in range(1, pipe_count)])
     grad_pieces = [grad_chips] + [shift(grad_chips, "tensor", s) for s in range(1, tensor_count)]
+    input_grad = input_gradient(at, cot_pieces, key_value_weight, grad_pieces, a_recv)
 
     low_part = low_product(at, tokens, a_recv, pipe_count, tensor_count)
     low_core = sum(
         [low_part[0].astype(jnp.float32)]
         + [shift(low_part[s], "tensor", s).astype(jnp.float32) for s in range(1, tensor_count)]
     ).astype(jnp.bfloat16)
-    low_sum = sum(
-        [low_core.astype(jnp.float32)]
-        + [shift(low_core, "pipe", k).astype(jnp.float32) for k in range(1, pipe_count)]
-    ).astype(jnp.bfloat16)
+    low_came = [shift(low_core, "pipe", k) for k in range(1, pipe_count)]
+    low_came, input_grad = lax.optimization_barrier((low_came, input_grad))
+    low_sum = sum([piece.astype(jnp.float32) for piece in [low_core] + low_came])
+    low_sum = low_sum.astype(jnp.bfloat16)
     low_pieces = [low_sum] + [shift(low_sum, "tensor", s) for s in range(1, tensor_count)]
     key_value = keys_and_values(at, base_chip[:1] + base_chip_came, low_sum, b_own)
 
@@ -453,7 +450,6 @@
     up_came = [up_pieces[0]] + [shift(up_pieces[k], "dp", k) for k in range(1, data_count)]
     grad_b = grad_up(at, slot_of, slots, up_came)
 
-    input_grad = input_gradient(at, cot_pieces, key_value_weight, grad_pieces, a_recv)
     grad_a = grad_down(at, slot_of, slots, x_recv, grad_pieces)
     return (key_value, input_grad, grad_a, grad_b)
 

time: 146 us -> 150 us (1.027)
  local copies, waits for them, and re-layouts: 8.14 us -> 14.6 us
  Pallas kernels: 36.9 us -> 31.9 us
  waiting for transfers between devices: 50.5 us -> 54.1 us
  starting transfers between devices: 45.9 us -> 43.2 us
    all_to_all x1, waiting for transfers between devices: 0.01 us -> 6.71 us  [body(): a_recv = lax.all_to_all(a_send, 'dp', 0, 0, tiled=True)]
    unnamed x30 -> x38, local copies, waits for them, and re-layouts: 4.82 us -> 10.8 us
    add x0 -> x1, other arithmetic: none -> 3.4 us  [body(): sum([base_keep[k].astype(jnp.float32)] + [b[k].astype(jnp.float32) for b...]
    ppermute x29, waiting for transfers between devices: 50.5 us -> 47.4 us  [shift(): lax.ppermute(piece, axis, [(i, (i + step) % count) for i in range(count)])]
    ppermute x29, starting transfers between devices: 37 us -> 34.3 us  [shift(): lax.ppermute(piece, axis, [(i, (i + step) % count) for i in range(count)])]
    convert_element_type x2 -> x1, other arithmetic: 2.14 us -> 0.08 us  [body(): low_sum = low_sum.astype(jnp.bfloat16)]
    pallas_call x2, Pallas kernels: 9.67 us -> 8.03 us  [base_product(): call(kernel, 'base_product', grid_spec=pltpu.PrefetchScalarGridSpec(num_s...]
  transfers between devices with their start and end apart: 31 -> 31, of which waited for: 10 -> 15; matrix products, arithmetic and copies ran while one was open for 4% -> 5% of each run, Pallas kernels for 22% -> 14%
where the time goes in v5:
time: 150 us; the launch traced here: 149 us
  waiting for transfers between devices  54.1 us (36%)
  starting transfers between devices  43.2 us (29%)
  Pallas kernels  31.9 us (21%)
  local copies, waits for them, and re-layouts  14.6 us (10%)
  other arithmetic  4.36 us (3%)
    ppermute x29, waiting for transfers between devices, shift(): lax.ppermute(piece, axis, [(i, (i + step) % count) for i in range(count)])  47.4 us
    ppermute x29, starting transfers between devices, shift(): lax.ppermute(piece, axis, [(i, (i + step) % count) for i in range(count)])  34.3 us
    unnamed x38, local copies, waits for them, and re-layouts  10.8 us
    pallas_call x1, Pallas kernels, input_gradient(): call(kernel, 'input_gradient', grid=(data_count // planes,), in_specs=[SM...  8.21 us
    pallas_call x2, Pallas kernels, base_product(): call(kernel, 'base_product', grid_spec=pltpu.PrefetchScalarGridSpec(num_s...  8.03 us
    all_to_all x1, waiting for transfers between devices, body(): a_recv = lax.all_to_all(a_send, 'dp', 0, 0, tiled=True)  6.71 us
    all_to_all x1, starting transfers between devices, body(): a_recv = lax.all_to_all(a_send, 'dp', 0, 0, tiled=True)  4.46 us
    all_to_all x1, starting transfers between devices, body(): x_recv = lax.all_to_all(x_send, 'dp', 0, 0, tiled=True)  4.45 us
  transfers between devices with their start and end apart: 31, of which 15 were waited for; matrix products, arithmetic and copies ran while one was open for 5% of the time, Pallas kernels for 14%

profile of v5, /device:TPU:0, one launch (start us, length us, event | category | flops | bytes accessed | tf_op | source)
XLA Modules:
  0.0 149.1 jit_solution(17596872745959017499)
XLA Ops:
  0.6 1.2 concatenate.3.at_ref
  1.9 2.4 %pick_up.1 = (bf16[16,2048]{1,0:T(8,128)(2,1)}, bf16[16,2048]{1,0:T(8,128)(2,1)}, bf16[16,2048]{1,0:T(8,128)(2,1)}, bf16[16,2048]{1,0:T(8,128)(2,1)}) custom-call(s32[60]{0:T(128)} %concatenate.3.at_ref, bf16[24,16,2048]{2,1,0:T(8,128)(2,1)} %up_ref.1), custom_call_target="tpu_custom_call" | custom-call | flops 1024 | bytes 1024 | tf_op jit(solution)/shard_map/pick_up/pallas_call | solution.py:55
  4.3 3.1 %collective-permute-start = (bf16[16,2048]{1,0:T(8,128)(2,1)}, bf16[16,2048]{1,0:T(8,128)(2,1)S(1)}, u32[]{:S(2)}, u32[]{:S(2)}) collective-permute-start(bf16[16,2048]{1,0:T(8,128)(2,1)} %get-tuple-element.35), channel_id=1, source_target_pairs={{0,8},{8,16},{16,24},{24,0},{1,9},{9,17},{17,25},{25,1},{2,10},{10... | collective-permute-start | bytes 196616 | tf_op jit(solution)/shard_map/ppermute | solution.py:35
  7.4 2.6 %collective-permute-start.1 = (bf16[16,2048]{1,0:T(8,128)(2,1)}, bf16[16,2048]{1,0:T(8,128)(2,1)S(1)}, u32[]{:S(2)}, u32[]{:S(2)}) collective-permute-start(bf16[16,2048]{1,0:T(8,128)(2,1)} %get-tuple-element.36), channel_id=1, source_target_pairs={{0,16},{8,24},{16,0},{24,8},{1,17},{9,25},{17,1},{25,9},{2,18},{10... | collective-permute-start | bytes 196616 | tf_op jit(solution)/shard_map/ppermute | solution.py:35
  10.0 1.3 collective-permute-start.2
  11.4 1.4 copy-done.7
  12.8 0.6 copy-done.14
  13.3 0.8 pick_down.1
  14.1 1.3 copy-done.4
  15.5 0.6 copy-done.17
  16.1 1.9 %collective-permute-done.3.rest_6_ = bf16[128,2048]{1,0:T(8,128)(2,1)S(1)} collective-permute-done((bf16[128,2048]{1,0:T(8,128)(2,1)S(1)}, bf16[128,2048]{1,0:T(8,128)(2,1)S(1)}, u32[]{:S(2)}, u32[]{:S(2)}) %collective-permute-start.3) | collective-permute-done | bytes 524320 | tf_op jit(solution)/shard_map/ppermute | solution.py:35
  18.0 2.2 %copy-done = bf16[1024,2048]{1,0:T(8,128)(2,1)S(1)} copy-done((bf16[1024,2048]{1,0:T(8,128)(2,1)S(1)}, bf16[1024,2048]{1,0:T(8,128)(2,1)}, u32[]{:S(2)}) %copy-start) | copy-done | bytes 4194328
  20.2 4.4 %base_product.3 = bf16[1,4,128,2048]{3,2,1,0:T(8,128)(2,1)} custom-call(s32[60]{0:T(128)S(1)} %copy-done.15, bf16[4,2,128,1024]{3,2,1,0:T(8,128)(2,1)S(1)} %bitcast.72, bf16[1024,2048]{1,0:T(8,128)(2,1)S(1)} %copy-done), custom_call_target="tpu_custom_call" | custom-call | flops 1024 | bytes 1024 | tf_op jit(solution)/shard_map/base_product/pallas_call | solution.py:94
  24.6 0.1 collective-permute-start.4
  24.8 4.5 %all-to-all-start = ((bf16[4,8,256,128]{3,2,1,0:T(8,128)(2,1)}), bf16[4,8,256,128]{3,2,1,0:T(8,128)(2,1)}, u32[]{:S(2)}, u32[]{:S(2)}) async-start(bf16[4,8,256,128]{3,2,1,0:T(8,128)(2,1)} %copy-done.4), calls=%async_computation | async-start | bytes 4194304 | tf_op jit(solution)/shard_map/all_to_all | solution.py:401
  29.2 2.2 %copy-done.1 = bf16[1024,2048]{1,0:T(8,128)(2,1)S(1)} copy-done((bf16[1024,2048]{1,0:T(8,128)(2,1)S(1)}, bf16[1024,2048]{1,0:T(8,128)(2,1)}, u32[]{:S(2)}) %copy-start.1) | copy-done | bytes 4194328
  31.4 3.6 %base_product.2 = bf16[1,4,128,2048]{3,2,1,0:T(8,128)(2,1)S(1)} custom-call(s32[60]{0:T(128)S(1)} %copy-done.15, bf16[4,2,128,1024]{3,2,1,0:T(8,128)(2,1)S(1)} %bitcast.73, bf16[1024,2048]{1,0:T(8,128)(2,1)S(1)} %copy-done.1), custom_call_target="tpu_custom_call" | custom-call | flops 1024 | bytes 1024 | tf_op jit(solution)/shard_map/base_product/pallas_call | solution.py:94
  35.1 3.4 %convert_add_fusion = (f32[128,2048]{1,0:T(8,128)}, bf16[128,2048]{1,0:T(8,128)(2,1)S(1)}, bf16[128,2048]{1,0:T(8,128)(2,1)S(1)}, bf16[128,2048]{1,0:T(8,128)(2,1)S(1)}) fusion(bf16[4,128,2048]{2,1,0:T(8,128)(2,1)} %collective-permute-done.4, bf16[1,4,128,2048]{3,2,1,0:T(8,128)(2,1)S(1)} %base_product.2), kind=kLoop, calls=%fused_computation | loop fusion | flops 3932160 | bytes 6815744 | tf_op jit(solution)/shard_map/add | solution.py:413
  38.5 1.5 %collective-permute-start.5 = (bf16[128,2048]{1,0:T(8,128)(2,1)S(1)}, bf16[128,2048]{1,0:T(8,128)(2,1)S(1)}, u32[]{:S(2)}, u32[]{:S(2)}) collective-permute-start(bf16[128,2048]{1,0:T(8,128)(2,1)S(1)} %get-tuple-element.67), channel_id=1, source_target_pairs={{0,2},{2,4},{4,6},{6,0},{1,3},{3,5},{5,7},{7,1},{8,10},{10,12},{12... | collective-permute-start | bytes 1572872 | tf_op jit(solution)/shard_map/ppermute | solution.py:35
  40.0 1.5 %collective-permute-start.6 = (bf16[128,2048]{1,0:T(8,128)(2,1)S(1)}, bf16[128,2048]{1,0:T(8,128)(2,1)S(1)}, u32[]{:S(2)}, u32[]{:S(2)}) collective-permute-start(bf16[128,2048]{1,0:T(8,128)(2,1)S(1)} %get-tuple-element.66), channel_id=1, source_target_pairs={{0,4},{2,6},{4,0},{6,2},{1,5},{3,7},{5,1},{7,3},{8,12},{10,14},{12... | collective-permute-start | bytes 1572872 | tf_op jit(solution)/shard_map/ppermute | solution.py:35
  41.5 1.4 collective-permute-start.7
  42.9 1.5 %own_rows.1 = (bf16[64,2048]{1,0:T(8,128)(2,1)S(1)}, bf16[128,128]{1,0:T(8,128)(2,1)}) custom-call(s32[60]{0:T(128)S(1)} %copy-done.15, bf16[128,2048]{1,0:T(8,128)(2,1)S(1)} %copy-done.5, bf16[16,2048]{1,0:T(8,128)(2,1)S(1)} %copy-done.16, bf16[16,2048]{1,0:T(8,128)(2,1)S(1)} %collective-permute-done.rest_1_, ...), custom_call_target="tpu_custom_call" | custom-call | flops 1024 | bytes 1024 | tf_op jit(solution)/shard_map/own_rows/pallas_call | solution.py:338
  44.5 9.7 %collective-permute-done.5.rest_1_ = bf16[128,2048]{1,0:T(8,128)(2,1)S(1)} collective-permute-done((bf16[128,2048]{1,0:T(8,128)(2,1)S(1)}, bf16[128,2048]{1,0:T(8,128)(2,1)S(1)}, u32[]{:S(2)}, u32[]{:S(2)}) %collective-permute-start.5) | collective-permute-done | bytes 524320 | tf_op jit(solution)/shard_map/ppermute | solution.py:35
  54.2 0.8 copy-done.8
  55.0 9.8 %collective-permute-done.6.rest_2_ = bf16[128,2048]{1,0:T(8,128)(2,1)S(1)} collective-permute-done((bf16[128,2048]{1,0:T(8,128)(2,1)S(1)}, bf16[128,2048]{1,0:T(8,128)(2,1)S(1)}, u32[]{:S(2)}, u32[]{:S(2)}) %collective-permute-start.6) | collective-permute-done | bytes 524320 | tf_op jit(solution)/shard_map/ppermute | solution.py:35
  64.8 0.8 copy-done.10
  65.6 0.8 copy-done.12
  66.4 3.5 %collective-permute-start.10 = (bf16[128,128]{1,0:T(8,128)(2,1)}, bf16[128,128]{1,0:T(8,128)(2,1)S(1)}, u32[]{:S(2)}, u32[]{:S(2)}) collective-permute-start(bf16[128,128]{1,0:T(8,128)(2,1)} %get-tuple-element.48), channel_id=1, source_target_pairs={{0,24},{8,0},{16,8},{24,16},{1,25},{9,1},{17,9},{25,17},{2,26},{10... | collective-permute-start | bytes 98312 | tf_op jit(solution)/shard_map/ppermute | solution.py:35
  69.9 1.1 collective-permute-start.9
  71.1 2.5 %copy.11 = bf16[1024,1024]{1,0:T(8,128)(2,1)} copy(bf16[1024,1024]{0,1:T(8,128)(2,1)S(1)} %bitcast.74) | data formatting | bytes 4194304 | tf_op jit(solution)/shard_map/transpose | solution.py:424
  73.6 6.7 %all-to-all-done.a_ref = bf16[4,8,256,128]{3,2,1,0:T(8,128)(2,1)} async-done(((bf16[4,8,256,128]{3,2,1,0:T(8,128)(2,1)}), bf16[4,8,256,128]{3,2,1,0:T(8,128)(2,1)}, u32[]{:S(2)}, u32[]{:S(2)}) %all-to-all-start) | async-done | bytes 2097184 | tf_op jit(solution)/shard_map/all_to_all | solution.py:401
  80.3 0.7 collective-permute-done.9
  81.1 4.5 %all-to-all-start.1 = ((bf16[4,256,1024]{2,1,0:T(8,128)(2,1)}), bf16[4,256,1024]{2,1,0:T(8,128)(2,1)}, u32[]{:S(2)}, u32[]{:S(2)}) async-start(bf16[4,256,1024]{2,1,0:T(8,128)(2,1)} %bitcast.75), calls=%async_computation.1 | async-start | bytes 4194304 | tf_op jit(solution)/shard_map/all_to_all | solution.py:426
  85.5 1.5 %collective-permute-start.19 = (bf16[128,2048]{1,0:T(8,128)(2,1)S(1)}, bf16[128,2048]{1,0:T(8,128)(2,1)S(1)}, u32[]{:S(2)}, u32[]{:S(2)}) collective-permute-start(bf16[128,2048]{1,0:T(8,128)(2,1)S(1)} %copy-done.5), channel_id=1, source_target_pairs={{0,2},{2,4},{4,6},{6,0},{1,3},{3,5},{5,7},{7,1},{8,10},{10,12},{12... | collective-permute-start | bytes 1572872 | tf_op jit(solution)/shard_map/ppermute | solution.py:35
  87.1 1.5 %collective-permute-start.20 = (bf16[128,2048]{1,0:T(8,128)(2,1)S(1)}, bf16[128,2048]{1,0:T(8,128)(2,1)S(1)}, u32[]{:S(2)}, u32[]{:S(2)}) collective-permute-start(bf16[128,2048]{1,0:T(8,128)(2,1)S(1)} %copy-done.5), channel_id=1, source_target_pairs={{0,4},{2,6},{4,0},{6,2},{1,5},{3,7},{5,1},{7,3},{8,12},{10,14},{12... | collective-permute-start | bytes 1572872 | tf_op jit(solution)/shard_map/ppermute | solution.py:35
  88.6 1.4 collective-permute-start.21
  90.0 0.8 fusion.4
  90.8 0.6 collective-permute-start.15
  91.5 0.5 collective-permute-start.16
  92.0 9.4 %collective-permute-done.19.rest_3_ = bf16[128,2048]{1,0:T(8,128)(2,1)S(1)} collective-permute-done((bf16[128,2048]{1,0:T(8,128)(2,1)S(1)}, bf16[128,2048]{1,0:T(8,128)(2,1)S(1)}, u32[]{:S(2)}, u32[]{:S(2)}) %collective-permute-start.19) | collective-permute-done | bytes 524320 | tf_op jit(solution)/shard_map/ppermute | solution.py:35
  101.4 1.5 %collective-permute-start.17 = (bf16[4,128,128]{2,1,0:T(8,128)(2,1)S(1)}, bf16[4,128,128]{2,1,0:T(8,128)(2,1)S(1)}, u32[]{:S(2)}, u32[]{:S(2)}) collective-permute-start(bf16[4,128,128]{2,1,0:T(8,128)(2,1)S(1)} %get-tuple-element.73), channel_id=1, source_target_pairs={{0,6},{2,0},{4,2},{6,4},{1,7},{3,1},{5,3},{7,5},{8,14},{10,8},{12,... | collective-permute-start | bytes 393224 | tf_op jit(solution)/shard_map/ppermute | solution.py:35
  102.9 2.3 %low_product.1 = bf16[2,4,128,128]{3,2,1,0:T(8,128)(2,1)S(1)} custom-call(s32[60]{0:T(128)S(1)} %copy-done.15, bf16[1024,1024]{1,0:T(8,128)(2,1)S(1)} %copy-done.3, bf16[4,8,256,128]{3,2,1,0:T(8,128)(2,1)} %all-to-all-done.a_ref), custom_call_target="tpu_custom_call" | custom-call | flops 1024 | bytes 1024 | tf_op jit(solution)/shard_map/low_product/pallas_call | solution.py:127
  105.2 7.2 %collective-permute-done.20.rest_4_ = bf16[128,2048]{1,0:T(8,128)(2,1)S(1)} collective-permute-done((bf16[128,2048]{1,0:T(8,128)(2,1)S(1)}, bf16[128,2048]{1,0:T(8,128)(2,1)S(1)}, u32[]{:S(2)}, u32[]{:S(2)}) %collective-permute-start.20) | collective-permute-done | bytes 524320 | tf_op jit(solution)/shard_map/ppermute | solution.py:35
  112.4 0.3 collective-permute-done.21.rest_5_
  112.7 0.2 collective-permute-start.23
  112.9 2.3 %collective-permute-done.15 = bf16[4,128,128]{2,1,0:T(8,128)(2,1)S(1)} collective-permute-done((bf16[4,128,128]{2,1,0:T(8,128)(2,1)S(1)}, bf16[4,128,128]{2,1,0:T(8,128)(2,1)S(1)}, u32[]{:S(2)}, u32[]{:S(2)}) %collective-permute-start.15) | collective-permute-done | bytes 131104 | tf_op jit(solution)/shard_map/ppermute | solution.py:35
  115.3 1.3 collective-permute-done.16
  116.5 0.1 collective-permute-done.17
  116.8 0.6 collective-permute-start.11
  117.3 1.5 %collective-permute-done.11 = bf16[4,128,128]{2,1,0:T(8,128)(2,1)S(1)} collective-permute-done((bf16[4,128,128]{2,1,0:T(8,128)(2,1)S(1)}, bf16[4,128,128]{2,1,0:T(8,128)(2,1)S(1)}, u32[]{:S(2)}, u32[]{:S(2)}) %collective-permute-start.11) | collective-permute-done | bytes 131104 | tf_op jit(solution)/shard_map/ppermute | solution.py:35
  118.9 1.8 %collective-permute-start.12 = (bf16[4,128,128]{2,1,0:T(8,128)(2,1)S(1)}, bf16[4,128,128]{2,1,0:T(8,128)(2,1)S(1)}, u32[]{:S(2)}, u32[]{:S(2)}) collective-permute-start(bf16[4,128,128]{2,1,0:T(8,128)(2,1)S(1)} %fusion.3), channel_id=1, source_target_pairs={{0,2},{2,4},{4,6},{6,0},{1,3},{3,5},{5,7},{7,1},{8,10},{10,12},{12... | collective-permute-start | bytes 393224 | tf_op jit(solution)/shard_map/ppermute | solution.py:35
  120.7 0.5 collective-permute-start.13
  121.2 2.1 %collective-permute-start.14 = (bf16[4,128,128]{2,1,0:T(8,128)(2,1)S(1)}, bf16[4,128,128]{2,1,0:T(8,128)(2,1)S(1)}, u32[]{:S(2)}, u32[]{:S(2)}) collective-permute-start(bf16[4,128,128]{2,1,0:T(8,128)(2,1)S(1)} %fusion.3), channel_id=1, source_target_pairs={{0,6},{2,0},{4,2},{6,4},{1,7},{3,1},{5,3},{7,5},{8,14},{10,8},{12,... | collective-permute-start | bytes 393224 | tf_op jit(solution)/shard_map/ppermute | solution.py:35
  123.3 8.2 %input_gradient.1 = bf16[1024,1024]{1,0:T(8,128)(2,1)} custom-call(s32[60]{0:T(128)S(1)} %copy-done.15, bf16[1024,2048]{1,0:T(8,128)(2,1)S(1)} %copy-done.2, bf16[4,8,256,128]{3,2,1,0:T(8,128)(2,1)} %all-to-all-done.a_ref, bf16[4,4,128,128]{3,2,1,0:T(8,128)(2,1)S(1)} %pad_maximum_fusion.rest_0_, ...), custom_call_target="tpu_custom_call" | custom-call | flops 1024 | bytes 1024 | tf_op jit(solution)/shard_map/input_gradient/pallas_call | solution.py:176
  131.8 1.3 collective-permute-done.25.rest_1_
  133.1 1.1 grad_up_pieces.1
  134.2 1.7 %collective-permute-start.26 = (bf16[8,16,256]{2,1,0:T(8,128)(2,1)S(1)}, bf16[8,16,256]{2,1,0:T(8,128)(2,1)S(1)}, u32[]{:S(2)}, u32[]{:S(2)}) collective-permute-start(bf16[8,16,256]{2,1,0:T(8,128)(2,1)S(1)} %get-tuple-element.70), channel_id=1, source_target_pairs={{0,8},{8,16},{16,24},{24,0},{1,9},{9,17},{17,25},{25,1},{2,10},{10... | collective-permute-start | bytes 196616 | tf_op jit(solution)/shard_map/ppermute | solution.py:35
  135.9 2.4 %collective-permute-start.27 = (bf16[8,16,256]{2,1,0:T(8,128)(2,1)S(1)}, bf16[8,16,256]{2,1,0:T(8,128)(2,1)S(1)}, u32[]{:S(2)}, u32[]{:S(2)}) collective-permute-start(bf16[8,16,256]{2,1,0:T(8,128)(2,1)S(1)} %get-tuple-element.69), channel_id=1, source_target_pairs={{0,16},{8,24},{16,0},{24,8},{1,17},{9,25},{17,1},{25,9},{2,18},{10... | collective-permute-start | bytes 196616 | tf_op jit(solution)/shard_map/ppermute | solution.py:35
  138.3 1.5 collective-permute-start.28
  139.8 1.8 %keys_and_values.1 = bf16[128,2048]{1,0:T(8,128)(2,1)} custom-call(s32[60]{0:T(128)S(1)} %copy-done.15, bf16[4,128,128]{2,1,0:T(8,128)(2,1)S(1)} %add_convert_fusion.low_ref.rest_0_, bf16[64,2048]{1,0:T(8,128)(2,1)S(1)} %get-tuple-element.57.b_ref, f32[128,2048]{1,0:T(8,128)S(1)} %copy-done.6, bf16[128,2048]{1,0:T(8,128)(2,1)S(1)} %copy-done.9, ...), custom_call_target="tpu_custom_call" | custom-call | flops 1024 | bytes 1024 | tf_op jit(solution)/shard_map/keys_and_values/pallas_call | solution.py:364
  141.5 1.6 %collective-permute-done.27.rest_2_ = bf16[8,16,256]{2,1,0:T(8,128)(2,1)S(1)} collective-permute-done((bf16[8,16,256]{2,1,0:T(8,128)(2,1)S(1)}, bf16[8,16,256]{2,1,0:T(8,128)(2,1)S(1)}, u32[]{:S(2)}, u32[]{:S(2)}) %collective-permute-start.27) | collective-permute-done | bytes 65568 | tf_op jit(solution)/shard_map/ppermute | solution.py:35
  143.1 0.2 collective-permute-done.28.rest_3_
  143.3 1.5 grad_up.1
  144.8 4.3 %grad_down.1 = f32[24,256,128]{2,1,0:T(8,128)} custom-call(s32[60]{0:T(128)S(1)} %copy-done.15, bf16[4,256,1024]{2,1,0:T(8,128)(2,1)} %all-to-all-done.1.x_ref, bf16[4,4,128,128]{3,2,1,0:T(8,128)(2,1)S(1)} %pad_maximum_fusion.rest_0_, bf16[4,4,128,128]{3,2,1,0:T(8,128)(2,1)S(1)} %collective-permute-done.18.rest_1_), custom_call_target="tpu_custom_call" | custom-call | flops 1024 | bytes 1024 | tf_op jit(solution)/shard_map/grad_down/pallas_call | solution.py:222
  (56 shorter events, 0.5 us)
Async XLA Ops:
  1.9 16.1 %copy-start.15 = (s32[60]{0:T(128)S(1)}, s32[60]{0:T(128)}, u32[]{:S(2)}) copy-start(s32[60]{0:T(128)} %concatenate.3.at_ref) | copy-start | bytes 724
  4.3 11.8 %copy-start.5 = (bf16[128,2048]{1,0:T(8,128)(2,1)S(1)}, bf16[128,2048]{1,0:T(8,128)(2,1)}, u32[]{:S(2)}) copy-start(bf16[128,2048]{1,0:T(8,128)(2,1)} %rest_2_.3) | copy-start | bytes 1572868
  4.3 13.7 %copy-start.3 = (bf16[1024,1024]{1,0:T(8,128)(2,1)S(1)}, bf16[1024,1024]{1,0:T(8,128)(2,1)}, u32[]{:S(2)}) copy-start(bf16[1024,1024]{1,0:T(8,128)(2,1)} %x_ref.1) | copy-start | bytes 6291460
  4.3 11.1 %collective-permute-start = (bf16[16,2048]{1,0:T(8,128)(2,1)}, bf16[16,2048]{1,0:T(8,128)(2,1)S(1)}, u32[]{:S(2)}, u32[]{:S(2)}) collective-permute-start(bf16[16,2048]{1,0:T(8,128)(2,1)} %get-tuple-element.35), channel_id=1, source_target_pairs={{0,8},{8,16},{16,24},{24,0},{1,9},{9,17},{17,25},{25,1},{2,10},{10... | collective-permute-start | bytes 196616 | tf_op jit(solution)/shard_map/ppermute | solution.py:35
  7.4 8.0 %collective-permute-start.1 = (bf16[16,2048]{1,0:T(8,128)(2,1)}, bf16[16,2048]{1,0:T(8,128)(2,1)S(1)}, u32[]{:S(2)}, u32[]{:S(2)}) collective-permute-start(bf16[16,2048]{1,0:T(8,128)(2,1)} %get-tuple-element.36), channel_id=1, source_target_pairs={{0,16},{8,24},{16,0},{24,8},{1,17},{9,25},{17,1},{25,9},{2,18},{10... | collective-permute-start | bytes 196616 | tf_op jit(solution)/shard_map/ppermute | solution.py:35
  10.0 5.5 %collective-permute-start.2 = (bf16[16,2048]{1,0:T(8,128)(2,1)}, bf16[16,2048]{1,0:T(8,128)(2,1)S(1)}, u32[]{:S(2)}, u32[]{:S(2)}) collective-permute-start(bf16[16,2048]{1,0:T(8,128)(2,1)} %get-tuple-element.37), channel_id=1, source_target_pairs={{0,24},{8,0},{16,8},{24,16},{1,25},{9,1},{17,9},{25,17},{2,26},{10... | collective-permute-start | bytes 196616 | tf_op jit(solution)/shard_map/ppermute | solution.py:35
  11.4 1.4 copy-start.7
  12.8 0.6 copy-start.14
  14.1 1.3 copy-start.4
  15.5 0.6 copy-start.17
  16.1 1.9 %collective-permute-start.3 = (bf16[128,2048]{1,0:T(8,128)(2,1)S(1)}, bf16[128,2048]{1,0:T(8,128)(2,1)S(1)}, u32[]{:S(2)}, u32[]{:S(2)}) collective-permute-start(bf16[128,2048]{1,0:T(8,128)(2,1)S(1)} %copy-done.5), channel_id=1, source_target_pairs={{0,1},{1,0},{2,3},{3,2},{4,5},{5,4},{6,7},{7,6},{8,9},{9,8},{10,11... | collective-permute-start | bytes 1572872 | tf_op jit(solution)/shard_map/ppermute | solution.py:35
  18.0 2.2 %copy-start = (bf16[1024,2048]{1,0:T(8,128)(2,1)S(1)}, bf16[1024,2048]{1,0:T(8,128)(2,1)}, u32[]{:S(2)}) copy-start(bf16[1024,2048]{1,0:T(8,128)(2,1)} %w_ref.5) | copy-start | bytes 12582916
  24.6 10.4 %collective-permute-start.4 = (bf16[4,128,2048]{2,1,0:T(8,128)(2,1)}, bf16[4,128,2048]{2,1,0:T(8,128)(2,1)}, u32[]{:S(2)}, u32[]{:S(2)}) collective-permute-start(bf16[4,128,2048]{2,1,0:T(8,128)(2,1)} %bitcast.8), channel_id=1, source_target_pairs={{0,1},{1,0},{2,3},{3,2},{4,5},{5,4},{6,7},{7,6},{8,9},{9,8},{10,11... | collective-permute-start | bytes 6291464 | tf_op jit(solution)/shard_map/ppermute | solution.py:35
  24.8 55.5 %all-to-all-start = ((bf16[4,8,256,128]{3,2,1,0:T(8,128)(2,1)}), bf16[4,8,256,128]{3,2,1,0:T(8,128)(2,1)}, u32[]{:S(2)}, u32[]{:S(2)}) async-start(bf16[4,8,256,128]{3,2,1,0:T(8,128)(2,1)} %copy-done.4), calls=%async_computation | async-start | bytes 4194304 | tf_op jit(solution)/shard_map/all_to_all | solution.py:401
  29.2 2.2 %copy-start.1 = (bf16[1024,2048]{1,0:T(8,128)(2,1)S(1)}, bf16[1024,2048]{1,0:T(8,128)(2,1)}, u32[]{:S(2)}) copy-start(bf16[1024,2048]{1,0:T(8,128)(2,1)} %w_ref.5) | copy-start | bytes 12582916
  35.0 7.9 %copy-start.16 = (bf16[16,2048]{1,0:T(8,128)(2,1)S(1)}, bf16[16,2048]{1,0:T(8,128)(2,1)}, u32[]{:S(2)}) copy-start(bf16[16,2048]{1,0:T(8,128)(2,1)} %get-tuple-element.39.rest_0_) | copy-start | bytes 196612
  35.1 7.9 %copy-start.18 = (bf16[16,2048]{1,0:T(8,128)(2,1)S(1)}, bf16[16,2048]{1,0:T(8,128)(2,1)}, u32[]{:S(2)}) copy-start(bf16[16,2048]{1,0:T(8,128)(2,1)} %copy-done.17) | copy-start | bytes 196612
  38.5 15.7 %collective-permute-start.5 = (bf16[128,2048]{1,0:T(8,128)(2,1)S(1)}, bf16[128,2048]{1,0:T(8,128)(2,1)S(1)}, u32[]{:S(2)}, u32[]{:S(2)}) collective-permute-start(bf16[128,2048]{1,0:T(8,128)(2,1)S(1)} %get-tuple-element.67), channel_id=1, source_target_pairs={{0,2},{2,4},{4,6},{6,0},{1,3},{3,5},{5,7},{7,1},{8,10},{10,12},{12... | collective-permute-start | bytes 1572872 | tf_op jit(solution)/shard_map/ppermute | solution.py:35
  40.0 24.8 %collective-permute-start.6 = (bf16[128,2048]{1,0:T(8,128)(2,1)S(1)}, bf16[128,2048]{1,0:T(8,128)(2,1)S(1)}, u32[]{:S(2)}, u32[]{:S(2)}) collective-permute-start(bf16[128,2048]{1,0:T(8,128)(2,1)S(1)} %get-tuple-element.66), channel_id=1, source_target_pairs={{0,4},{2,6},{4,0},{6,2},{1,5},{3,7},{5,1},{7,3},{8,12},{10,14},{12... | collective-permute-start | bytes 1572872 | tf_op jit(solution)/shard_map/ppermute | solution.py:35
  41.5 24.1 %collective-permute-start.7 = (bf16[128,2048]{1,0:T(8,128)(2,1)S(1)}, bf16[128,2048]{1,0:T(8,128)(2,1)S(1)}, u32[]{:S(2)}, u32[]{:S(2)}) collective-permute-start(bf16[128,2048]{1,0:T(8,128)(2,1)S(1)} %get-tuple-element.65), channel_id=1, source_target_pairs={{0,6},{2,0},{4,2},{6,4},{1,7},{3,1},{5,3},{7,5},{8,14},{10,8},{12,... | collective-permute-start | bytes 1572872 | tf_op jit(solution)/shard_map/ppermute | solution.py:35
  54.2 0.8 copy-start.8
  64.8 0.8 copy-start.10
  65.6 0.8 copy-start.12
  66.4 13.9 %collective-permute-start.10 = (bf16[128,128]{1,0:T(8,128)(2,1)}, bf16[128,128]{1,0:T(8,128)(2,1)S(1)}, u32[]{:S(2)}, u32[]{:S(2)}) collective-permute-start(bf16[128,128]{1,0:T(8,128)(2,1)} %get-tuple-element.48), channel_id=1, source_target_pairs={{0,24},{8,0},{16,8},{24,16},{1,25},{9,1},{17,9},{25,17},{2,26},{10... | collective-permute-start | bytes 98312 | tf_op jit(solution)/shard_map/ppermute | solution.py:35
  69.9 10.4 %collective-permute-start.8 = (bf16[128,128]{1,0:T(8,128)(2,1)}, bf16[128,128]{1,0:T(8,128)(2,1)S(1)}, u32[]{:S(2)}, u32[]{:S(2)}) collective-permute-start(bf16[128,128]{1,0:T(8,128)(2,1)} %get-tuple-element.48), channel_id=1, source_target_pairs={{0,8},{8,16},{16,24},{24,0},{1,9},{9,17},{17,25},{25,1},{2,10},{10... | collective-permute-start | bytes 98312 | tf_op jit(solution)/shard_map/ppermute | solution.py:35
  69.9 11.1 %collective-permute-start.9 = (bf16[128,128]{1,0:T(8,128)(2,1)}, bf16[128,128]{1,0:T(8,128)(2,1)S(1)}, u32[]{:S(2)}, u32[]{:S(2)}) collective-permute-start(bf16[128,128]{1,0:T(8,128)(2,1)} %get-tuple-element.48), channel_id=1, source_target_pairs={{0,16},{8,24},{16,0},{24,8},{1,17},{9,25},{17,1},{25,9},{2,18},{10... | collective-permute-start | bytes 98312 | tf_op jit(solution)/shard_map/ppermute | solution.py:35
  81.1 63.7 %all-to-all-start.1 = ((bf16[4,256,1024]{2,1,0:T(8,128)(2,1)}), bf16[4,256,1024]{2,1,0:T(8,128)(2,1)}, u32[]{:S(2)}, u32[]{:S(2)}) async-start(bf16[4,256,1024]{2,1,0:T(8,128)(2,1)} %bitcast.75), calls=%async_computation.1 | async-start | bytes 4194304 | tf_op jit(solution)/shard_map/all_to_all | solution.py:426
  85.5 15.9 %collective-permute-start.19 = (bf16[128,2048]{1,0:T(8,128)(2,1)S(1)}, bf16[128,2048]{1,0:T(8,128)(2,1)S(1)}, u32[]{:S(2)}, u32[]{:S(2)}) collective-permute-start(bf16[128,2048]{1,0:T(8,128)(2,1)S(1)} %copy-done.5), channel_id=1, source_target_pairs={{0,2},{2,4},{4,6},{6,0},{1,3},{3,5},{5,7},{7,1},{8,10},{10,12},{12... | collective-permute-start | bytes 1572872 | tf_op jit(solution)/shard_map/ppermute | solution.py:35
  87.1 25.3 %collective-permute-start.20 = (bf16[128,2048]{1,0:T(8,128)(2,1)S(1)}, bf16[128,2048]{1,0:T(8,128)(2,1)S(1)}, u32[]{:S(2)}, u32[]{:S(2)}) collective-permute-start(bf16[128,2048]{1,0:T(8,128)(2,1)S(1)} %copy-done.5), channel_id=1, source_target_pairs={{0,4},{2,6},{4,0},{6,2},{1,5},{3,7},{5,1},{7,3},{8,12},{10,14},{12... | collective-permute-start | bytes 1572872 | tf_op jit(solution)/shard_map/ppermute | solution.py:35
  88.6 24.1 %collective-permute-start.21 = (bf16[128,2048]{1,0:T(8,128)(2,1)S(1)}, bf16[128,2048]{1,0:T(8,128)(2,1)S(1)}, u32[]{:S(2)}, u32[]{:S(2)}) collective-permute-start(bf16[128,2048]{1,0:T(8,128)(2,1)S(1)} %copy-done.5), channel_id=1, source_target_pairs={{0,6},{2,0},{4,2},{6,4},{1,7},{3,1},{5,3},{7,5},{8,14},{10,8},{12,... | collective-permute-start | bytes 1572872 | tf_op jit(solution)/shard_map/ppermute | solution.py:35
  90.8 32.5 %copy-start.2 = (bf16[1024,2048]{1,0:T(8,128)(2,1)S(1)}, bf16[1024,2048]{1,0:T(8,128)(2,1)}, u32[]{:S(2)}) copy-start(bf16[1024,2048]{1,0:T(8,128)(2,1)} %w_ref.5) | copy-start | bytes 12582916
  90.8 24.5 %collective-permute-start.15 = (bf16[4,128,128]{2,1,0:T(8,128)(2,1)S(1)}, bf16[4,128,128]{2,1,0:T(8,128)(2,1)S(1)}, u32[]{:S(2)}, u32[]{:S(2)}) collective-permute-start(bf16[4,128,128]{2,1,0:T(8,128)(2,1)S(1)} %get-tuple-element.73), channel_id=1, source_target_pairs={{0,2},{2,4},{4,6},{6,0},{1,3},{3,5},{5,7},{7,1},{8,10},{10,12},{12... | collective-permute-start | bytes 393224 | tf_op jit(solution)/shard_map/ppermute | solution.py:35
  91.5 25.1 %collective-permute-start.16 = (bf16[4,128,128]{2,1,0:T(8,128)(2,1)S(1)}, bf16[4,128,128]{2,1,0:T(8,128)(2,1)S(1)}, u32[]{:S(2)}, u32[]{:S(2)}) collective-permute-start(bf16[4,128,128]{2,1,0:T(8,128)(2,1)S(1)} %get-tuple-element.73), channel_id=1, source_target_pairs={{0,4},{2,6},{4,0},{6,2},{1,5},{3,7},{5,1},{7,3},{8,12},{10,14},{12... | collective-permute-start | bytes 393224 | tf_op jit(solution)/shard_map/ppermute | solution.py:35
  101.4 15.2 %collective-permute-start.17 = (bf16[4,128,128]{2,1,0:T(8,128)(2,1)S(1)}, bf16[4,128,128]{2,1,0:T(8,128)(2,1)S(1)}, u32[]{:S(2)}, u32[]{:S(2)}) collective-permute-start(bf16[4,128,128]{2,1,0:T(8,128)(2,1)S(1)} %get-tuple-element.73), channel_id=1, source_target_pairs={{0,6},{2,0},{4,2},{6,4},{1,7},{3,1},{5,3},{7,5},{8,14},{10,8},{12,... | collective-permute-start | bytes 393224 | tf_op jit(solution)/shard_map/ppermute | solution.py:35
  112.4 8.3 %collective-permute-start.22 = (bf16[128,2048]{1,0:T(8,128)(2,1)S(1)}, bf16[128,2048]{1,0:T(8,128)(2,1)S(1)}, u32[]{:S(2)}, u32[]{:S(2)}) collective-permute-start(bf16[128,2048]{1,0:T(8,128)(2,1)S(1)} %collective-permute-done.19.rest_3_), channel_id=1, source_target_pairs={{0,1},{1,0},{2,3},{3,2},{4,5},{5,4},{6,7},{7,6},{8,9},{9,8},{10,11... | collective-permute-start | bytes 1572872 | tf_op jit(solution)/shard_map/ppermute | solution.py:35
  112.7 8.5 %collective-permute-start.23 = (bf16[128,2048]{1,0:T(8,128)(2,1)S(1)}, bf16[128,2048]{1,0:T(8,128)(2,1)S(1)}, u32[]{:S(2)}, u32[]{:S(2)}) collective-permute-start(bf16[128,2048]{1,0:T(8,128)(2,1)S(1)} %collective-permute-done.20.rest_4_), channel_id=1, source_target_pairs={{0,1},{1,0},{2,3},{3,2},{4,5},{5,4},{6,7},{7,6},{8,9},{9,8},{10,11... | collective-permute-start | bytes 1572872 | tf_op jit(solution)/shard_map/ppermute | solution.py:35
  115.3 8.0 %collective-permute-start.24 = (bf16[128,2048]{1,0:T(8,128)(2,1)S(1)}, bf16[128,2048]{1,0:T(8,128)(2,1)S(1)}, u32[]{:S(2)}, u32[]{:S(2)}) collective-permute-start(bf16[128,2048]{1,0:T(8,128)(2,1)S(1)} %collective-permute-done.21.rest_5_), channel_id=1, source_target_pairs={{0,1},{1,0},{2,3},{3,2},{4,5},{5,4},{6,7},{7,6},{8,9},{9,8},{10,11... | collective-permute-start | bytes 1572872 | tf_op jit(solution)/shard_map/ppermute | solution.py:35
  116.7 6.6 %collective-permute-start.18 = (bf16[4,4,128,128]{3,2,1,0:T(8,128)(2,1)S(1)}, bf16[4,4,128,128]{3,2,1,0:T(8,128)(2,1)S(1)}, u32[]{:S(2)}, u32[]{:S(2)}) collective-permute-start(bf16[4,4,128,128]{3,2,1,0:T(8,128)(2,1)S(1)} %pad_maximum_fusion.rest_0_), channel_id=1, source_target_pairs={{0,1},{1,0},{2,3},{3,2},{4,5},{5,4},{6,7},{7,6},{8,9},{9,8},{10,11... | collective-permute-start | bytes 1572872 | tf_op jit(solution)/shard_map/ppermute | solution.py:35
  116.8 2.1 %collective-permute-start.11 = (bf16[4,128,128]{2,1,0:T(8,128)(2,1)S(1)}, bf16[4,128,128]{2,1,0:T(8,128)(2,1)S(1)}, u32[]{:S(2)}, u32[]{:S(2)}) collective-permute-start(bf16[4,128,128]{2,1,0:T(8,128)(2,1)S(1)} %slice_bitcast_fusion.8), channel_id=1, source_target_pairs={{0,1},{1,0},{2,3},{3,2},{4,5},{5,4},{6,7},{7,6},{8,9},{9,8},{10,11... | collective-permute-start | bytes 393224 | tf_op jit(solution)/shard_map/ppermute | solution.py:35
  118.9 12.6 %collective-permute-start.12 = (bf16[4,128,128]{2,1,0:T(8,128)(2,1)S(1)}, bf16[4,128,128]{2,1,0:T(8,128)(2,1)S(1)}, u32[]{:S(2)}, u32[]{:S(2)}) collective-permute-start(bf16[4,128,128]{2,1,0:T(8,128)(2,1)S(1)} %fusion.3), channel_id=1, source_target_pairs={{0,2},{2,4},{4,6},{6,0},{1,3},{3,5},{5,7},{7,1},{8,10},{10,12},{12... | collective-permute-start | bytes 393224 | tf_op jit(solution)/shard_map/ppermute | solution.py:35
  120.7 10.9 %collective-permute-start.13 = (bf16[4,128,128]{2,1,0:T(8,128)(2,1)S(1)}, bf16[4,128,128]{2,1,0:T(8,128)(2,1)S(1)}, u32[]{:S(2)}, u32[]{:S(2)}) collective-permute-start(bf16[4,128,128]{2,1,0:T(8,128)(2,1)S(1)} %fusion.3), channel_id=1, source_target_pairs={{0,4},{2,6},{4,0},{6,2},{1,5},{3,7},{5,1},{7,3},{8,12},{10,14},{12... | collective-permute-start | bytes 393224 | tf_op jit(solution)/shard_map/ppermute | solution.py:35
  121.2 10.4 %collective-permute-start.14 = (bf16[4,128,128]{2,1,0:T(8,128)(2,1)S(1)}, bf16[4,128,128]{2,1,0:T(8,128)(2,1)S(1)}, u32[]{:S(2)}, u32[]{:S(2)}) collective-permute-start(bf16[4,128,128]{2,1,0:T(8,128)(2,1)S(1)} %fusion.3), channel_id=1, source_target_pairs={{0,6},{2,0},{4,2},{6,4},{1,7},{3,1},{5,3},{7,5},{8,14},{10,8},{12,... | collective-permute-start | bytes 393224 | tf_op jit(solution)/shard_map/ppermute | solution.py:35
  131.7 8.1 %copy-start.6 = (f32[128,2048]{1,0:T(8,128)S(1)}, f32[128,2048]{1,0:T(8,128)}, u32[]{:S(2)}) copy-start(f32[128,2048]{1,0:T(8,128)} %get-tuple-element.58.rest_0_) | copy-start | bytes 3145732
  131.7 8.1 %copy-start.9 = (bf16[128,2048]{1,0:T(8,128)(2,1)S(1)}, bf16[128,2048]{1,0:T(8,128)(2,1)}, u32[]{:S(2)}) copy-start(bf16[128,2048]{1,0:T(8,128)(2,1)} %copy-done.8) | copy-start | bytes 1572868
  131.7 8.1 %copy-start.11 = (bf16[128,2048]{1,0:T(8,128)(2,1)S(1)}, bf16[128,2048]{1,0:T(8,128)(2,1)}, u32[]{:S(2)}) copy-start(bf16[128,2048]{1,0:T(8,128)(2,1)} %copy-done.10) | copy-start | bytes 1572868
  131.7 8.1 %copy-start.13 = (bf16[128,2048]{1,0:T(8,128)(2,1)S(1)}, bf16[128,2048]{1,0:T(8,128)(2,1)}, u32[]{:S(2)}) copy-start(bf16[128,2048]{1,0:T(8,128)(2,1)} %copy-done.12) | copy-start | bytes 1572868
  131.7 1.4 collective-permute-start.25
  134.2 7.3 %collective-permute-start.26 = (bf16[8,16,256]{2,1,0:T(8,128)(2,1)S(1)}, bf16[8,16,256]{2,1,0:T(8,128)(2,1)S(1)}, u32[]{:S(2)}, u32[]{:S(2)}) collective-permute-start(bf16[8,16,256]{2,1,0:T(8,128)(2,1)S(1)} %get-tuple-element.70), channel_id=1, source_target_pairs={{0,8},{8,16},{16,24},{24,0},{1,9},{9,17},{17,25},{25,1},{2,10},{10... | collective-permute-start | bytes 196616 | tf_op jit(solution)/shard_map/ppermute | solution.py:35
  135.9 7.2 %collective-permute-start.27 = (bf16[8,16,256]{2,1,0:T(8,128)(2,1)S(1)}, bf16[8,16,256]{2,1,0:T(8,128)(2,1)S(1)}, u32[]{:S(2)}, u32[]{:S(2)}) collective-permute-start(bf16[8,16,256]{2,1,0:T(8,128)(2,1)S(1)} %get-tuple-element.69), channel_id=1, source_target_pairs={{0,16},{8,24},{16,0},{24,8},{1,17},{9,25},{17,1},{25,9},{2,18},{10... | collective-permute-start | bytes 196616 | tf_op jit(solution)/shard_map/ppermute | solution.py:35
  138.3 5.0 %collective-permute-start.28 = (bf16[8,16,256]{2,1,0:T(8,128)(2,1)S(1)}, bf16[8,16,256]{2,1,0:T(8,128)(2,1)S(1)}, u32[]{:S(2)}, u32[]{:S(2)}) collective-permute-start(bf16[8,16,256]{2,1,0:T(8,128)(2,1)S(1)} %get-tuple-element.68), channel_id=1, source_target_pairs={{0,24},{8,0},{16,8},{24,16},{1,25},{9,1},{17,9},{25,17},{2,26},{10... | collective-permute-start | bytes 196616 | tf_op jit(solution)/shard_map/ppermute | solution.py:35

commit v6 on v5

--- a/solution.py
+++ b/solution.py
@@ -11,7 +11,6 @@
 RANKS = 2 * ADAPTER_RANK
 WIDTH = 2 * KEY_WIDTH
 VMEM_LIMIT = 24 * 1024 * 1024
-VMEM_MOST = 60 * 1024 * 1024
 LAST_BOTH = (((1,), (1,)), ((), ()))
 FIRST_BOTH = (((0,), (0,)), ((), ()))
 SMEM = pl.BlockSpec(memory_space=pltpu.SMEM)
@@ -20,10 +19,10 @@
 ANY = pl.BlockSpec(memory_space=pl.ANY)
 
 
-def call(kernel, name, vmem=VMEM_LIMIT, **more):
+def call(kernel, name, **more):
     return pl.pallas_call(
         kernel,
-        compiler_params=pltpu.CompilerParams(vmem_limit_bytes=vmem),
+        compiler_params=pltpu.CompilerParams(vmem_limit_bytes=VMEM_LIMIT),
         cost_estimate=pl.CostEstimate(flops=1024, bytes_accessed=1024, transcendentals=0),
         name=name,
         **more,
@@ -55,7 +54,6 @@
     return call(
         kernel,
         "pick_up",
-        VMEM_MOST,
         out_shape=(jax.ShapeDtypeStruct(adapter_up.shape[1:], adapter_up.dtype),) * data_count,
         in_specs=[SMEM, HBM],
         out_specs=(VMEM,) * data_count,
@@ -63,22 +61,26 @@
     )(at, adapter_up)
 
 
-def pick_down(at, slot_of, adapter_down, data_count, blocks_dev):
-    rows, ranks = adapter_down.shape[1:]
-
-    def kernel(at_ref, down_ref, out_ref):
+def pick_down(at, slot_of, adapter_down, grad_rows, data_count, blocks_dev):
+    down_rows, ranks = adapter_down.shape[1:]
+    rows = grad_rows.shape[0]
+    first_grad = blocks_dev * down_rows
+
+    def kernel(at_ref, down_ref, grad_ref, out_ref):
         data = pl.program_id(0)
         for block in range(blocks_dev):
-            out_ref[0, block] = down_ref[slot_of(at_ref, data, block)]
+            here = slice(block * down_rows, (block + 1) * down_rows)
+            out_ref[0, here] = down_ref[slot_of(at_ref, data, block)]
+        out_ref[0, first_grad:] = grad_ref[...]
 
     return call(
         kernel,
         "pick_down",
         grid=(data_count,),
-        out_shape=jax.ShapeDtypeStruct((data_count, blocks_dev, rows, ranks), adapter_down.dtype),
-        in_specs=[SMEM, VMEM],
-        out_specs=pl.BlockSpec((1, blocks_dev, rows, ranks), lambda d: (d, 0, 0, 0)),
-    )(at, adapter_down)
+        out_shape=pltpu.HBM((data_count, first_grad + rows, ranks), adapter_down.dtype),
+        in_specs=[SMEM, VMEM, VMEM],
+        out_specs=pl.BlockSpec((1, first_grad + rows, ranks), lambda d: (d, 0, 0)),
+    )(at, adapter_down, grad_rows)
 
 
 def base_product(at, tokens, weight, first, count):
@@ -112,11 +114,12 @@
 
 def low_product(at, tokens, down, pipe_count, tensor_count):
     tok_dev, depth = tokens.shape
+    down_rows = depth // down.shape[0]
     rows = tok_dev // (pipe_count * tensor_count)
 
     def kernel(at_ref, x_ref, a_ref, out_ref):
         for block in range(tok_dev // BLOCK):
-            a = a_ref[:, block].reshape(depth, RANKS)
+            a = a_ref[:, block * down_rows : (block + 1) * down_rows].reshape(depth, RANKS)
             x = x_ref[block * BLOCK : (block + 1) * BLOCK]
             y = jnp.dot(x, a, preferred_element_type=jnp.float32).astype(out_ref.dtype)
             for part in range(BLOCK // rows):
@@ -134,11 +137,13 @@
 
 
 def input_gradient(at, cot_pieces, weight, grad_pieces, down):
-    data_count, blocks_dev, down_rows, _ = down.shape
+    data_count, all_rows, _ = down.shape
     tensor_count, pipe_count = len(cot_pieces), len(cot_pieces[0])
     rows = cot_pieces[0][0].shape[0]
     depth = weight.shape[0]
-    tok_dev = blocks_dev * BLOCK
+    down_rows = depth // data_count
+    tok_dev = tensor_count * pipe_count * rows
+    blocks_dev = tok_dev // BLOCK
     planes = next((n for n in range(1, data_count) if n * down_rows % 256 == 0), data_count)
     tile = planes * down_rows
     order = [(s, k) for s in range(tensor_count) for k in range(pipe_count)]
@@ -161,18 +166,18 @@
             for copy in copies:
                 copy.start()
             for s, k in order:
-                grad[pl.ds(first_row(s, k), rows)] = grad_refs[s][k, 0]
+                grad[pl.ds(first_row(s, k), rows)] = grad_refs[s][k, at_ref[0]]
             for copy in copies:
                 copy.wait()
 
         base = lax.dot_general(cot[...], w_ref[...], LAST_BOTH, preferred_element_type=jnp.float32)
         for block in range(blocks_dev):
             at = slice(block * BLOCK, (block + 1) * BLOCK)
-            a = a_ref[:, block].reshape(tile, RANKS)
+            a = a_ref[:, block * down_rows : (block + 1) * down_rows].reshape(tile, RANKS)
             low = lax.dot_general(grad[at], a, LAST_BOTH, preferred_element_type=jnp.float32)
             out_ref[at] = (base[at] + low).astype(out_ref.dtype)
 
-    grad_shape = (pipe_count, 1, rows, RANKS)
+    grad_shape = (pipe_count, data_count, rows, RANKS)
     return call(
         kernel,
         "input_gradient",
@@ -180,7 +185,7 @@
         in_specs=[
             SMEM,
             pl.BlockSpec((tile, WIDTH), lambda n: (n, 0)),
-            pl.BlockSpec((planes, blocks_dev, down_rows, RANKS), lambda n: (n, 0, 0, 0)),
+            pl.BlockSpec((planes, all_rows, RANKS), lambda n: (n, 0, 0)),
         ]
         + [pl.BlockSpec(grad_shape, lambda n: (0, 0, 0, 0))] * tensor_count
         + [ANY] * len(order),
@@ -207,9 +212,8 @@
             for k in range(pipe_count):
                 chip = wrap(at_ref[1] - k, pipe_count)
                 first = pl.multiple_of((chip * tensor_count + core) * rows, rows)
-                for m in range(data_count):
-                    data = wrap(at_ref[0] - m, data_count)
-                    grad[data, pl.ds(first, rows)] = grad_refs[s][k, m]
+                for data in range(data_count):
+                    grad[data, pl.ds(first, rows)] = grad_refs[s][k, data]
         out_ref[...] = jnp.zeros(out_ref.shape, out_ref.dtype)
         for data in range(data_count):
             for block in range(blocks_dev):
@@ -396,15 +400,15 @@
 
     b_send = pick_up(at, slot_of, adapter_up, data_count)
     b_came = [b_send[0]] + [shift(b_send[k], "dp", k) for k in range(1, data_count)]
-    a_send = pick_down(at, slot_of, adapter_down, data_count, blocks_dev)
-    a_send, b_came = lax.optimization_barrier((a_send, b_came))
+    b_own, grad_rows = own_rows(at, b_came, cotangent)
+
+    a_send = pick_down(at, slot_of, adapter_down, grad_rows, data_count, blocks_dev)
     a_recv = lax.all_to_all(a_send, "dp", 0, 0, tiled=True)
-    b_own, grad_rows = own_rows(at, b_came, cotangent)
 
     cot_send, a_send = lax.optimization_barrier((cotangent, a_send))
-    cot_cores = [shift(cot_send, "tensor", s) for s in range(1, tensor_count)]
-
-    base_tokens, cot_cores = lax.optimization_barrier((tokens, cot_cores))
+    cot_chips = [cotangent] + [shift(cot_send, "pipe", k) for k in range(1, pipe_count)]
+
+    base_tokens, cot_chips[1] = lax.optimization_barrier((tokens, cot_chips[1]))
     tokens_by_group = base_tokens.reshape(pipe_count, tensor_count, rows, feature_count)
     base_send = base_product(at, tokens_by_group, key_value_weight, 1, tensor_count - 1)
     base_came = [shift(base_send[s - 1], "tensor", s) for s in range(1, tensor_count)]
@@ -416,20 +420,17 @@
     base_chip[1:] = [piece.astype(jnp.bfloat16) for piece in base_chip[1:]]
     base_chip_came = [shift(base_chip[k], "pipe", k) for k in range(1, pipe_count)]
 
-    cot_send, base_chip = lax.optimization_barrier((cot_send, base_chip))
-    cot_chips = [cotangent] + [shift(cot_send, "pipe", k) for k in range(1, pipe_count)]
-    grad_rows, base_chip_came = lax.optimization_barrier((grad_rows, base_chip_came))
-    grad_data = [grad_rows] + [shift(grad_rows, "dp", k) for k in range(1, data_count)]
-
-    x_send = tokens.T.reshape(data_count, down_rows, tok_dev)
-    a_recv, x_send, grad_data = lax.optimization_barrier((a_recv, x_send, grad_data))
+    x_tokens, base_chip = lax.optimization_barrier((tokens, base_chip))
+    x_send = x_tokens.T.reshape(data_count, down_rows, tok_dev)
+    a_recv, x_send, cot_chips, base_chip_came = lax.optimization_barrier(
+        (a_recv, x_send, cot_chips, base_chip_came)
+    )
     x_recv = lax.all_to_all(x_send, "dp", 0, 0, tiled=True)
 
     cot_pieces = [cot_chips] + [
-        [cot_cores[s - 1]] + [shift(piece, "tensor", s) for piece in cot_chips[1:]]
-        for s in range(1, tensor_count)
+        [shift(piece, "tensor", s) for piece in cot_chips] for s in range(1, tensor_count)
     ]
-    grad_data = jnp.stack(grad_data)
+    grad_data = a_recv[:, blocks_dev * down_rows :]
     grad_chips = jnp.stack([grad_data] + [shift(grad_data, "pipe", k) for k in range(1, pipe_count)])
     grad_pieces = [grad_chips] + [shift(grad_chips, "tensor", s) for s in range(1, tensor_count)]
     input_grad = input_gradient(at, cot_pieces, key_value_weight, grad_pieces, a_recv)

time: 150 us -> 148 us (0.987)
  the two profiles are of different devices: /device:TPU:0 before, /device:TPU:6 now
where the time goes in v6:
time: 148 us; the launch traced here: 147 us
  waiting for transfers between devices  68.4 us (46%)
  starting transfers between devices  33.5 us (23%)
  Pallas kernels  33.2 us (22%)
  local copies, waits for them, and re-layouts  8.94 us (6%)
  other arithmetic  2.23 us (2%)
    ppermute x26, waiting for transfers between devices, shift(): lax.ppermute(piece, axis, [(i, (i + step) % count) for i in range(count)])  68.4 us
    ppermute x26, starting transfers between devices, shift(): lax.ppermute(piece, axis, [(i, (i + step) % count) for i in range(count)])  24.5 us
    pallas_call x1, Pallas kernels, input_gradient(): call(kernel, 'input_gradient', grid=(data_count // planes,), in_specs=[SM...  9.13 us
    pallas_call x2, Pallas kernels, base_product(): call(kernel, 'base_product', grid_spec=pltpu.PrefetchScalarGridSpec(num_s...  7.23 us
    unnamed x16, local copies, waits for them, and re-layouts  4.66 us
    all_to_all x1, starting transfers between devices, body(): a_recv = lax.all_to_all(a_send, 'dp', 0, 0, tiled=True)  4.61 us
    all_to_all x1, starting transfers between devices, body(): x_recv = lax.all_to_all(x_send, 'dp', 0, 0, tiled=True)  4.46 us
    pallas_call x1, Pallas kernels, grad_down(): call(kernel, 'grad_down', in_specs=[SMEM, VMEM] + [VMEM] * tensor_count,...  4.25 us
  transfers between devices with their start and end apart: 28, of which 11 were waited for; matrix products, arithmetic and copies ran while one was open for 4% of the time, Pallas kernels for 17%

profile of v6, /device:TPU:6, one launch (start us, length us, event | category | flops | bytes accessed | tf_op | source)
XLA Modules:
  0.0 147.2 jit_solution(1074731232381534242)
XLA Ops:
  0.6 0.8 concatenate.3.at_ref
  1.4 1.4 copy-done.6
  2.8 0.9 pick_up.1
  3.8 1.6 %collective-permute-start = (bf16[16,2048]{1,0:T(8,128)(2,1)S(1)}, bf16[16,2048]{1,0:T(8,128)(2,1)S(1)}, u32[]{:S(2)}, u32[]{:S(2)}) collective-permute-start(bf16[16,2048]{1,0:T(8,128)(2,1)S(1)} %get-tuple-element.29), channel_id=1, source_target_pairs={{0,8},{8,16},{16,24},{24,0},{1,9},{9,17},{17,25},{25,1},{2,10},{10... | collective-permute-start | bytes 196616 | tf_op jit(solution)/shard_map/ppermute | solution.py:34
  5.4 2.6 %collective-permute-start.1 = (bf16[16,2048]{1,0:T(8,128)(2,1)S(1)}, bf16[16,2048]{1,0:T(8,128)(2,1)S(1)}, u32[]{:S(2)}, u32[]{:S(2)}) collective-permute-start(bf16[16,2048]{1,0:T(8,128)(2,1)S(1)} %get-tuple-element.30), channel_id=1, source_target_pairs={{0,16},{8,24},{16,0},{24,8},{1,17},{9,25},{17,1},{25,9},{2,18},{10... | collective-permute-start | bytes 196616 | tf_op jit(solution)/shard_map/ppermute | solution.py:34
  8.0 1.3 collective-permute-start.2
  9.3 1.0 collective-permute-done.rest_1_
  10.3 2.4 %collective-permute-done.1.rest_2_ = bf16[16,2048]{1,0:T(8,128)(2,1)S(1)} collective-permute-done((bf16[16,2048]{1,0:T(8,128)(2,1)S(1)}, bf16[16,2048]{1,0:T(8,128)(2,1)S(1)}, u32[]{:S(2)}, u32[]{:S(2)}) %collective-permute-start.1) | collective-permute-done | bytes 65568 | tf_op jit(solution)/shard_map/ppermute | solution.py:34
  12.7 0.0 collective-permute-done.2.rest_3_
  12.7 1.0 copy-done.3
  13.8 0.9 own_rows.1
  14.7 0.0 copy-start.4
  14.7 2.4 %pick_down.1 = bf16[4,2176,128]{2,1,0:T(8,128)(2,1)} custom-call(s32[60]{0:T(128)S(1)} %concatenate.3.at_ref, bf16[24,256,128]{2,1,0:T(8,128)(2,1)S(1)} %copy-done.7, bf16[128,128]{1,0:T(8,128)(2,1)S(1)} %get-tuple-element.32.grad_ref), custom_call_target="tpu_custom_call" | custom-call | flops 1024 | bytes 1024 | tf_op jit(solution)/shard_map/pick_down/pallas_call | solution.py:76
  17.2 0.4 collective-permute-start.3
  17.6 4.6 %all-to-all-start = ((bf16[4,2176,128]{2,1,0:T(8,128)(2,1)}), bf16[4,2176,128]{2,1,0:T(8,128)(2,1)}, u32[]{:S(2)}, u32[]{:S(2)}) async-start(bf16[4,2176,128]{2,1,0:T(8,128)(2,1)} %pick_down.1), calls=%async_computation | async-start | bytes 4456448 | tf_op jit(solution)/shard_map/all_to_all | solution.py:406
  22.2 7.6 %collective-permute-done.3.rest_3_ = bf16[128,2048]{1,0:T(8,128)(2,1)S(1)} collective-permute-done((bf16[128,2048]{1,0:T(8,128)(2,1)S(1)}, bf16[128,2048]{1,0:T(8,128)(2,1)S(1)}, u32[]{:S(2)}, u32[]{:S(2)}) %collective-permute-start.3) | collective-permute-done | bytes 524320 | tf_op jit(solution)/shard_map/ppermute | solution.py:34
  29.8 2.2 %copy-done = bf16[1024,2048]{1,0:T(8,128)(2,1)S(1)} copy-done((bf16[1024,2048]{1,0:T(8,128)(2,1)S(1)}, bf16[1024,2048]{1,0:T(8,128)(2,1)}, u32[]{:S(2)}) %copy-start) | copy-done | bytes 4194328
  32.0 3.6 %base_product.3 = bf16[1,4,128,2048]{3,2,1,0:T(8,128)(2,1)S(1)} custom-call(s32[60]{0:T(128)S(1)} %concatenate.3.at_ref, bf16[4,2,128,1024]{3,2,1,0:T(8,128)(2,1)S(1)} %bitcast.68, bf16[1024,2048]{1,0:T(8,128)(2,1)S(1)} %copy-done), custom_call_target="tpu_custom_call" | custom-call | flops 1024 | bytes 1024 | tf_op jit(solution)/shard_map/base_product/pallas_call | solution.py:96
  35.6 0.1 collective-permute-start.4
  35.7 0.6 collective-permute-start.5
  36.3 2.2 %collective-permute-start.6 = (bf16[128,2048]{1,0:T(8,128)(2,1)S(1)}, bf16[128,2048]{1,0:T(8,128)(2,1)}, u32[]{:S(2)}, u32[]{:S(2)}) collective-permute-start(bf16[128,2048]{1,0:T(8,128)(2,1)S(1)} %copy-done.4), channel_id=1, source_target_pairs={{0,6},{2,0},{4,2},{6,4},{1,7},{3,1},{5,3},{7,5},{8,14},{10,8},{12,... | collective-permute-start | bytes 1572872 | tf_op jit(solution)/shard_map/ppermute | solution.py:34
  38.4 3.6 %base_product.2 = bf16[1,4,128,2048]{3,2,1,0:T(8,128)(2,1)S(1)} custom-call(s32[60]{0:T(128)S(1)} %concatenate.3.at_ref, bf16[4,2,128,1024]{3,2,1,0:T(8,128)(2,1)S(1)} %bitcast.69, bf16[1024,2048]{1,0:T(8,128)(2,1)S(1)} %copy-done), custom_call_target="tpu_custom_call" | custom-call | flops 1024 | bytes 1024 | tf_op jit(solution)/shard_map/base_product/pallas_call | solution.py:96
  42.1 2.0 %fusion = (bf16[128,2048]{1,0:T(8,128)(2,1)}, bf16[128,2048]{1,0:T(8,128)(2,1)}, bf16[128,2048]{1,0:T(8,128)(2,1)}, f32[128,2048]{1,0:T(8,128)}) fusion(bf16[4,128,2048]{2,1,0:T(8,128)(2,1)S(1)} %collective-permute-done.4, bf16[1,4,128,2048]{3,2,1,0:T(8,128)(2,1)S(1)} %base_product.2), kind=kLoop, calls=%fused_computation.1 | loop fusion | flops 3932160 | bytes 6815744 | tf_op jit(solution)/shard_map/convert_element_type | solution.py:420
  44.1 0.8 collective-permute-start.7
  44.9 1.5 %collective-permute-start.8 = (bf16[128,2048]{1,0:T(8,128)(2,1)}, bf16[128,2048]{1,0:T(8,128)(2,1)}, u32[]{:S(2)}, u32[]{:S(2)}) collective-permute-start(bf16[128,2048]{1,0:T(8,128)(2,1)} %get-tuple-element.53), channel_id=1, source_target_pairs={{0,4},{2,6},{4,0},{6,2},{1,5},{3,7},{5,1},{7,3},{8,12},{10,14},{12... | collective-permute-start | bytes 1572872 | tf_op jit(solution)/shard_map/ppermute | solution.py:34
  46.4 0.5 collective-permute-start.9
  46.9 2.5 %copy.11 = bf16[1024,1024]{1,0:T(8,128)(2,1)} copy(bf16[1024,1024]{0,1:T(8,128)(2,1)S(1)} %bitcast.70) | data formatting | bytes 4194304 | tf_op jit(solution)/shard_map/transpose | solution.py:424
  49.5 12.4 %collective-permute-done.5.rest_4_ = bf16[128,2048]{1,0:T(8,128)(2,1)} collective-permute-done((bf16[128,2048]{1,0:T(8,128)(2,1)S(1)}, bf16[128,2048]{1,0:T(8,128)(2,1)}, u32[]{:S(2)}, u32[]{:S(2)}) %collective-permute-start.5) | collective-permute-done | bytes 524320 | tf_op jit(solution)/shard_map/ppermute | solution.py:34
  61.9 0.0 collective-permute-done.6.rest_5_
  61.9 1.5 %collective-permute-done.7.rest_1_ = bf16[128,2048]{1,0:T(8,128)(2,1)} collective-permute-done((bf16[128,2048]{1,0:T(8,128)(2,1)}, bf16[128,2048]{1,0:T(8,128)(2,1)}, u32[]{:S(2)}, u32[]{:S(2)}) %collective-permute-start.7) | collective-permute-done | bytes 524320 | tf_op jit(solution)/shard_map/ppermute | solution.py:34
  63.4 20.5 %collective-permute-done.8.rest_2_ = bf16[128,2048]{1,0:T(8,128)(2,1)} collective-permute-done((bf16[128,2048]{1,0:T(8,128)(2,1)}, bf16[128,2048]{1,0:T(8,128)(2,1)}, u32[]{:S(2)}, u32[]{:S(2)}) %collective-permute-start.8) | collective-permute-done | bytes 524320 | tf_op jit(solution)/shard_map/ppermute | solution.py:34
  83.9 0.0 collective-permute-done.9.rest_3_
  83.9 0.0 all-to-all-done.a_ref
  83.9 4.5 %all-to-all-start.1 = ((bf16[4,256,1024]{2,1,0:T(8,128)(2,1)}), bf16[4,256,1024]{2,1,0:T(8,128)(2,1)}, u32[]{:S(2)}, u32[]{:S(2)}) async-start(bf16[4,256,1024]{2,1,0:T(8,128)(2,1)} %bitcast.72), calls=%async_computation.1 | async-start | bytes 4194304 | tf_op jit(solution)/shard_map/all_to_all | solution.py:428
  88.3 0.9 slice_bitcast_fusion.14
  89.3 0.0 copy-start.1
  89.3 0.1 collective-permute-start.14
  89.4 0.6 collective-permute-start.15
  89.9 1.9 %collective-permute-start.16 = (bf16[4,128,128]{2,1,0:T(8,128)(2,1)S(1)}, bf16[4,128,128]{2,1,0:T(8,128)(2,1)S(1)}, u32[]{:S(2)}, u32[]{:S(2)}) collective-permute-start(bf16[4,128,128]{2,1,0:T(8,128)(2,1)S(1)} %get-tuple-element.57), channel_id=1, source_target_pairs={{0,6},{2,0},{4,2},{6,4},{1,7},{3,1},{5,3},{7,5},{8,14},{10,8},{12,... | collective-permute-start | bytes 393224 | tf_op jit(solution)/shard_map/ppermute | solution.py:34
  91.9 2.4 %low_product.1 = bf16[2,4,128,128]{3,2,1,0:T(8,128)(2,1)S(1)} custom-call(s32[60]{0:T(128)S(1)} %concatenate.3.at_ref, bf16[1024,1024]{1,0:T(8,128)(2,1)S(1)} %copy-done.2, bf16[4,2176,128]{2,1,0:T(8,128)(2,1)} %all-to-all-done.a_ref), custom_call_target="tpu_custom_call" | custom-call | flops 1024 | bytes 1024 | tf_op jit(solution)/shard_map/low_product/pallas_call | solution.py:130
  94.2 0.1 collective-permute-start.18
  94.3 0.6 collective-permute-start.10
  94.9 0.9 collective-permute-done.14
  95.8 1.5 %collective-permute-done.15 = bf16[4,128,128]{2,1,0:T(8,128)(2,1)S(1)} collective-permute-done((bf16[4,128,128]{2,1,0:T(8,128)(2,1)S(1)}, bf16[4,128,128]{2,1,0:T(8,128)(2,1)S(1)}, u32[]{:S(2)}, u32[]{:S(2)}) %collective-permute-start.15) | collective-permute-done | bytes 131104 | tf_op jit(solution)/shard_map/ppermute | solution.py:34
  97.3 0.5 collective-permute-start.21
  97.8 0.1 pad_maximum_fusion.rest_0_
  97.9 0.0 collective-permute-done.10
  97.9 0.1 collective-permute-start.17
  98.0 1.2 collective-permute-start.11
  99.2 0.5 collective-permute-start.12
  99.7 1.7 %collective-permute-start.13 = (bf16[4,128,128]{2,1,0:T(8,128)(2,1)S(1)}, bf16[4,128,128]{2,1,0:T(8,128)(2,1)S(1)}, u32[]{:S(2)}, u32[]{:S(2)}) collective-permute-start(bf16[4,128,128]{2,1,0:T(8,128)(2,1)S(1)} %fusion.3), channel_id=1, source_target_pairs={{0,6},{2,0},{4,2},{6,4},{1,7},{3,1},{5,3},{7,5},{8,14},{10,8},{12,... | collective-permute-start | bytes 393224 | tf_op jit(solution)/shard_map/ppermute | solution.py:34
  101.5 9.1 %input_gradient.1 = bf16[1024,1024]{1,0:T(8,128)(2,1)} custom-call(s32[60]{0:T(128)S(1)} %concatenate.3.at_ref, bf16[1024,2048]{1,0:T(8,128)(2,1)S(1)} %copy-done.1, bf16[4,2176,128]{2,1,0:T(8,128)(2,1)} %all-to-all-done.a_ref, bf16[4,4,128,128]{3,2,1,0:T(8,128)(2,1)S(1)} %pad_maximum_fusion.rest_0_, ...), custom_call_target="tpu_custom_call" | custom-call | flops 1024 | bytes 1024 | tf_op jit(solution)/shard_map/input_gradient/pallas_call | solution.py:181
  110.7 0.1 add_convert_fusion.low_ref.rest_0_
  110.8 0.1 collective-permute-start.22
  110.8 1.3 collective-permute-done.22.rest_1_
  112.2 1.9 %grad_up_pieces.1 = bf16[4,8,16,256]{3,2,1,0:T(8,128)(2,1)S(1)} custom-call(s32[60]{0:T(128)S(1)} %concatenate.3.at_ref, bf16[4,128,128]{2,1,0:T(8,128)(2,1)S(1)} %add_convert_fusion.low_ref.rest_0_, bf16[4,128,128]{2,1,0:T(8,128)(2,1)S(1)} %collective-permute-done.22.rest_1_, bf16[128,2048]{1,0:T(8,128)(2,1)S(1)} %copy-done.4, ...), custom_call_target="tpu_custom_call" | custom-call | flops 1024 | bytes 1024 | tf_op jit(solution)/shard_map/grad_up_pieces/pallas_call | solution.py:282
  114.1 2.5 %collective-permute-start.23 = (bf16[8,16,256]{2,1,0:T(8,128)(2,1)S(1)}, bf16[8,16,256]{2,1,0:T(8,128)(2,1)S(1)}, u32[]{:S(2)}, u32[]{:S(2)}) collective-permute-start(bf16[8,16,256]{2,1,0:T(8,128)(2,1)S(1)} %get-tuple-element.60), channel_id=1, source_target_pairs={{0,8},{8,16},{16,24},{24,0},{1,9},{9,17},{17,25},{25,1},{2,10},{10... | collective-permute-start | bytes 196616 | tf_op jit(solution)/shard_map/ppermute | solution.py:34
  116.5 1.6 %collective-permute-start.24 = (bf16[8,16,256]{2,1,0:T(8,128)(2,1)S(1)}, bf16[8,16,256]{2,1,0:T(8,128)(2,1)S(1)}, u32[]{:S(2)}, u32[]{:S(2)}) collective-permute-start(bf16[8,16,256]{2,1,0:T(8,128)(2,1)S(1)} %get-tuple-element.59), channel_id=1, source_target_pairs={{0,16},{8,24},{16,0},{24,8},{1,17},{9,25},{17,1},{25,9},{2,18},{10... | collective-permute-start | bytes 196616 | tf_op jit(solution)/shard_map/ppermute | solution.py:34
  118.2 1.5 collective-permute-start.25
  119.6 2.6 %keys_and_values.1 = bf16[128,2048]{1,0:T(8,128)(2,1)} custom-call(s32[60]{0:T(128)S(1)} %concatenate.3.at_ref, bf16[4,128,128]{2,1,0:T(8,128)(2,1)S(1)} %add_convert_fusion.low_ref.rest_0_, bf16[64,2048]{1,0:T(8,128)(2,1)S(1)} %get-tuple-element.45.b_ref, f32[128,2048]{1,0:T(8,128)S(1)} %copy-done.5, bf16[128,2048]{1,0:T(8,128)(2,1)} %collective-permute-done.7.rest_1_, ...), custom_call_target="tpu_custom_call" | custom-call | flops 1024 | bytes 1024 | tf_op jit(solution)/shard_map/keys_and_values/pallas_call | solution.py:368
  122.2 6.8 %collective-permute-done.23.rest_1_ = bf16[8,16,256]{2,1,0:T(8,128)(2,1)S(1)} collective-permute-done((bf16[8,16,256]{2,1,0:T(8,128)(2,1)S(1)}, bf16[8,16,256]{2,1,0:T(8,128)(2,1)S(1)}, u32[]{:S(2)}, u32[]{:S(2)}) %collective-permute-start.23) | collective-permute-done | bytes 65568 | tf_op jit(solution)/shard_map/ppermute | solution.py:34
  129.1 12.5 %collective-permute-done.24.rest_2_ = bf16[8,16,256]{2,1,0:T(8,128)(2,1)S(1)} collective-permute-done((bf16[8,16,256]{2,1,0:T(8,128)(2,1)S(1)}, bf16[8,16,256]{2,1,0:T(8,128)(2,1)S(1)}, u32[]{:S(2)}, u32[]{:S(2)}) %collective-permute-start.24) | collective-permute-done | bytes 65568 | tf_op jit(solution)/shard_map/ppermute | solution.py:34
  141.5 1.5 grad_up.1
  143.0 4.3 %grad_down.1 = f32[24,256,128]{2,1,0:T(8,128)} custom-call(s32[60]{0:T(128)S(1)} %concatenate.3.at_ref, bf16[4,256,1024]{2,1,0:T(8,128)(2,1)} %all-to-all-done.1.x_ref, bf16[4,4,128,128]{3,2,1,0:T(8,128)(2,1)S(1)} %pad_maximum_fusion.rest_0_, bf16[4,4,128,128]{3,2,1,0:T(8,128)(2,1)S(1)} %collective-permute-done.17.rest_1_), custom_call_target="tpu_custom_call" | custom-call | flops 1024 | bytes 1024 | tf_op jit(solution)/shard_map/grad_down/pallas_call | solution.py:226
  (28 shorter events, 0.1 us)
Async XLA Ops:
  1.4 1.4 copy-start.6
  2.8 11.9 %copy-start.7 = (bf16[24,256,128]{2,1,0:T(8,128)(2,1)S(1)}, bf16[24,256,128]{2,1,0:T(8,128)(2,1)}, u32[]{:S(2)}) copy-start(bf16[24,256,128]{2,1,0:T(8,128)(2,1)} %down_ref.1) | copy-start | bytes 4718596
  3.8 6.5 %collective-permute-start = (bf16[16,2048]{1,0:T(8,128)(2,1)S(1)}, bf16[16,2048]{1,0:T(8,128)(2,1)S(1)}, u32[]{:S(2)}, u32[]{:S(2)}) collective-permute-start(bf16[16,2048]{1,0:T(8,128)(2,1)S(1)} %get-tuple-element.29), channel_id=1, source_target_pairs={{0,8},{8,16},{16,24},{24,0},{1,9},{9,17},{17,25},{25,1},{2,10},{10... | collective-permute-start | bytes 196616 | tf_op jit(solution)/shard_map/ppermute | solution.py:34
  5.4 7.3 %collective-permute-start.1 = (bf16[16,2048]{1,0:T(8,128)(2,1)S(1)}, bf16[16,2048]{1,0:T(8,128)(2,1)S(1)}, u32[]{:S(2)}, u32[]{:S(2)}) collective-permute-start(bf16[16,2048]{1,0:T(8,128)(2,1)S(1)} %get-tuple-element.30), channel_id=1, source_target_pairs={{0,16},{8,24},{16,0},{24,8},{1,17},{9,25},{17,1},{25,9},{2,18},{10... | collective-permute-start | bytes 196616 | tf_op jit(solution)/shard_map/ppermute | solution.py:34
  8.0 4.8 %collective-permute-start.2 = (bf16[16,2048]{1,0:T(8,128)(2,1)S(1)}, bf16[16,2048]{1,0:T(8,128)(2,1)S(1)}, u32[]{:S(2)}, u32[]{:S(2)}) collective-permute-start(bf16[16,2048]{1,0:T(8,128)(2,1)S(1)} %get-tuple-element.31), channel_id=1, source_target_pairs={{0,24},{8,0},{16,8},{24,16},{1,25},{9,1},{17,9},{25,17},{2,26},{10... | collective-permute-start | bytes 196616 | tf_op jit(solution)/shard_map/ppermute | solution.py:34
  12.7 1.0 copy-start.3
  14.7 2.5 %copy-start.4 = (bf16[128,2048]{1,0:T(8,128)(2,1)S(1)}, bf16[128,2048]{1,0:T(8,128)(2,1)}, u32[]{:S(2)}) copy-start(bf16[128,2048]{1,0:T(8,128)(2,1)} %rest_2_.1) | copy-start | bytes 1572868
  17.2 12.7 %copy-start.2 = (bf16[1024,1024]{1,0:T(8,128)(2,1)S(1)}, bf16[1024,1024]{1,0:T(8,128)(2,1)}, u32[]{:S(2)}) copy-start(bf16[1024,1024]{1,0:T(8,128)(2,1)} %x_ref.1) | copy-start | bytes 6291460
  17.2 12.6 %collective-permute-start.3 = (bf16[128,2048]{1,0:T(8,128)(2,1)S(1)}, bf16[128,2048]{1,0:T(8,128)(2,1)S(1)}, u32[]{:S(2)}, u32[]{:S(2)}) collective-permute-start(bf16[128,2048]{1,0:T(8,128)(2,1)S(1)} %copy-done.4), channel_id=1, source_target_pairs={{0,2},{2,4},{4,6},{6,0},{1,3},{3,5},{5,7},{7,1},{8,10},{10,12},{12... | collective-permute-start | bytes 1572872 | tf_op jit(solution)/shard_map/ppermute | solution.py:34
  17.6 66.3 %all-to-all-start = ((bf16[4,2176,128]{2,1,0:T(8,128)(2,1)}), bf16[4,2176,128]{2,1,0:T(8,128)(2,1)}, u32[]{:S(2)}, u32[]{:S(2)}) async-start(bf16[4,2176,128]{2,1,0:T(8,128)(2,1)} %pick_down.1), calls=%async_computation | async-start | bytes 4456448 | tf_op jit(solution)/shard_map/all_to_all | solution.py:406
  29.8 2.2 %copy-start = (bf16[1024,2048]{1,0:T(8,128)(2,1)S(1)}, bf16[1024,2048]{1,0:T(8,128)(2,1)}, u32[]{:S(2)}) copy-start(bf16[1024,2048]{1,0:T(8,128)(2,1)} %w_ref.5) | copy-start | bytes 12582916
  35.6 6.4 %collective-permute-start.4 = (bf16[4,128,2048]{2,1,0:T(8,128)(2,1)S(1)}, bf16[4,128,2048]{2,1,0:T(8,128)(2,1)S(1)}, u32[]{:S(2)}, u32[]{:S(2)}) collective-permute-start(bf16[4,128,2048]{2,1,0:T(8,128)(2,1)S(1)} %bitcast.71), channel_id=1, source_target_pairs={{0,1},{1,0},{2,3},{3,2},{4,5},{5,4},{6,7},{7,6},{8,9},{9,8},{10,11... | collective-permute-start | bytes 6291464 | tf_op jit(solution)/shard_map/ppermute | solution.py:34
  35.7 26.2 %collective-permute-start.5 = (bf16[128,2048]{1,0:T(8,128)(2,1)S(1)}, bf16[128,2048]{1,0:T(8,128)(2,1)}, u32[]{:S(2)}, u32[]{:S(2)}) collective-permute-start(bf16[128,2048]{1,0:T(8,128)(2,1)S(1)} %copy-done.4), channel_id=1, source_target_pairs={{0,4},{2,6},{4,0},{6,2},{1,5},{3,7},{5,1},{7,3},{8,12},{10,14},{12... | collective-permute-start | bytes 1572872 | tf_op jit(solution)/shard_map/ppermute | solution.py:34
  36.3 25.6 %collective-permute-start.6 = (bf16[128,2048]{1,0:T(8,128)(2,1)S(1)}, bf16[128,2048]{1,0:T(8,128)(2,1)}, u32[]{:S(2)}, u32[]{:S(2)}) collective-permute-start(bf16[128,2048]{1,0:T(8,128)(2,1)S(1)} %copy-done.4), channel_id=1, source_target_pairs={{0,6},{2,0},{4,2},{6,4},{1,7},{3,1},{5,3},{7,5},{8,14},{10,8},{12,... | collective-permute-start | bytes 1572872 | tf_op jit(solution)/shard_map/ppermute | solution.py:34
  44.1 19.3 %collective-permute-start.7 = (bf16[128,2048]{1,0:T(8,128)(2,1)}, bf16[128,2048]{1,0:T(8,128)(2,1)}, u32[]{:S(2)}, u32[]{:S(2)}) collective-permute-start(bf16[128,2048]{1,0:T(8,128)(2,1)} %get-tuple-element.54), channel_id=1, source_target_pairs={{0,2},{2,4},{4,6},{6,0},{1,3},{3,5},{5,7},{7,1},{8,10},{10,12},{12... | collective-permute-start | bytes 1572872 | tf_op jit(solution)/shard_map/ppermute | solution.py:34
  44.9 39.0 %collective-permute-start.8 = (bf16[128,2048]{1,0:T(8,128)(2,1)}, bf16[128,2048]{1,0:T(8,128)(2,1)}, u32[]{:S(2)}, u32[]{:S(2)}) collective-permute-start(bf16[128,2048]{1,0:T(8,128)(2,1)} %get-tuple-element.53), channel_id=1, source_target_pairs={{0,4},{2,6},{4,0},{6,2},{1,5},{3,7},{5,1},{7,3},{8,12},{10,14},{12... | collective-permute-start | bytes 1572872 | tf_op jit(solution)/shard_map/ppermute | solution.py:34
  46.4 37.5 %collective-permute-start.9 = (bf16[128,2048]{1,0:T(8,128)(2,1)}, bf16[128,2048]{1,0:T(8,128)(2,1)}, u32[]{:S(2)}, u32[]{:S(2)}) collective-permute-start(bf16[128,2048]{1,0:T(8,128)(2,1)} %get-tuple-element.52), channel_id=1, source_target_pairs={{0,6},{2,0},{4,2},{6,4},{1,7},{3,1},{5,3},{7,5},{8,14},{10,8},{12,... | collective-permute-start | bytes 1572872 | tf_op jit(solution)/shard_map/ppermute | solution.py:34
  83.9 59.1 %all-to-all-start.1 = ((bf16[4,256,1024]{2,1,0:T(8,128)(2,1)}), bf16[4,256,1024]{2,1,0:T(8,128)(2,1)}, u32[]{:S(2)}, u32[]{:S(2)}) async-start(bf16[4,256,1024]{2,1,0:T(8,128)(2,1)} %bitcast.72), calls=%async_computation.1 | async-start | bytes 4194304 | tf_op jit(solution)/shard_map/all_to_all | solution.py:428
  89.3 12.2 %copy-start.1 = (bf16[1024,2048]{1,0:T(8,128)(2,1)S(1)}, bf16[1024,2048]{1,0:T(8,128)(2,1)}, u32[]{:S(2)}) copy-start(bf16[1024,2048]{1,0:T(8,128)(2,1)} %w_ref.5) | copy-start | bytes 12582916
  89.3 6.5 %collective-permute-start.14 = (bf16[4,128,128]{2,1,0:T(8,128)(2,1)S(1)}, bf16[4,128,128]{2,1,0:T(8,128)(2,1)S(1)}, u32[]{:S(2)}, u32[]{:S(2)}) collective-permute-start(bf16[4,128,128]{2,1,0:T(8,128)(2,1)S(1)} %get-tuple-element.57), channel_id=1, source_target_pairs={{0,2},{2,4},{4,6},{6,0},{1,3},{3,5},{5,7},{7,1},{8,10},{10,12},{12... | collective-permute-start | bytes 393224 | tf_op jit(solution)/shard_map/ppermute | solution.py:34
  89.4 7.9 %collective-permute-start.15 = (bf16[4,128,128]{2,1,0:T(8,128)(2,1)S(1)}, bf16[4,128,128]{2,1,0:T(8,128)(2,1)S(1)}, u32[]{:S(2)}, u32[]{:S(2)}) collective-permute-start(bf16[4,128,128]{2,1,0:T(8,128)(2,1)S(1)} %get-tuple-element.57), channel_id=1, source_target_pairs={{0,4},{2,6},{4,0},{6,2},{1,5},{3,7},{5,1},{7,3},{8,12},{10,14},{12... | collective-permute-start | bytes 393224 | tf_op jit(solution)/shard_map/ppermute | solution.py:34
  89.9 7.4 %collective-permute-start.16 = (bf16[4,128,128]{2,1,0:T(8,128)(2,1)S(1)}, bf16[4,128,128]{2,1,0:T(8,128)(2,1)S(1)}, u32[]{:S(2)}, u32[]{:S(2)}) collective-permute-start(bf16[4,128,128]{2,1,0:T(8,128)(2,1)S(1)} %get-tuple-element.57), channel_id=1, source_target_pairs={{0,6},{2,0},{4,2},{6,4},{1,7},{3,1},{5,3},{7,5},{8,14},{10,8},{12,... | collective-permute-start | bytes 393224 | tf_op jit(solution)/shard_map/ppermute | solution.py:34
  94.2 3.8 %collective-permute-start.18 = (bf16[128,2048]{1,0:T(8,128)(2,1)S(1)}, bf16[128,2048]{1,0:T(8,128)(2,1)S(1)}, u32[]{:S(2)}, u32[]{:S(2)}) collective-permute-start(bf16[128,2048]{1,0:T(8,128)(2,1)S(1)} %copy-done.4), channel_id=1, source_target_pairs={{0,1},{1,0},{2,3},{3,2},{4,5},{5,4},{6,7},{7,6},{8,9},{9,8},{10,11... | collective-permute-start | bytes 1572872 | tf_op jit(solution)/shard_map/ppermute | solution.py:34
  94.3 3.5 %collective-permute-start.10 = (bf16[4,128,128]{2,1,0:T(8,128)(2,1)S(1)}, bf16[4,128,128]{2,1,0:T(8,128)(2,1)S(1)}, u32[]{:S(2)}, u32[]{:S(2)}) collective-permute-start(bf16[4,128,128]{2,1,0:T(8,128)(2,1)S(1)} %slice_bitcast_fusion.8), channel_id=1, source_target_pairs={{0,1},{1,0},{2,3},{3,2},{4,5},{5,4},{6,7},{7,6},{8,9},{9,8},{10,11... | collective-permute-start | bytes 393224 | tf_op jit(solution)/shard_map/ppermute | solution.py:34
  95.8 3.5 %collective-permute-start.19 = (bf16[128,2048]{1,0:T(8,128)(2,1)S(1)}, bf16[128,2048]{1,0:T(8,128)(2,1)S(1)}, u32[]{:S(2)}, u32[]{:S(2)}) collective-permute-start(bf16[128,2048]{1,0:T(8,128)(2,1)S(1)} %collective-permute-done.3.rest_3_), channel_id=1, source_target_pairs={{0,1},{1,0},{2,3},{3,2},{4,5},{5,4},{6,7},{7,6},{8,9},{9,8},{10,11... | collective-permute-start | bytes 1572872 | tf_op jit(solution)/shard_map/ppermute | solution.py:34
  97.3 2.4 %collective-permute-start.20 = (bf16[128,2048]{1,0:T(8,128)(2,1)}, bf16[128,2048]{1,0:T(8,128)(2,1)S(1)}, u32[]{:S(2)}, u32[]{:S(2)}) collective-permute-start(bf16[128,2048]{1,0:T(8,128)(2,1)} %collective-permute-done.5.rest_4_), channel_id=1, source_target_pairs={{0,1},{1,0},{2,3},{3,2},{4,5},{5,4},{6,7},{7,6},{8,9},{9,8},{10,11... | collective-permute-start | bytes 1572872 | tf_op jit(solution)/shard_map/ppermute | solution.py:34
  97.3 4.2 %collective-permute-start.21 = (bf16[128,2048]{1,0:T(8,128)(2,1)}, bf16[128,2048]{1,0:T(8,128)(2,1)S(1)}, u32[]{:S(2)}, u32[]{:S(2)}) collective-permute-start(bf16[128,2048]{1,0:T(8,128)(2,1)} %collective-permute-done.6.rest_5_), channel_id=1, source_target_pairs={{0,1},{1,0},{2,3},{3,2},{4,5},{5,4},{6,7},{7,6},{8,9},{9,8},{10,11... | collective-permute-start | bytes 1572872 | tf_op jit(solution)/shard_map/ppermute | solution.py:34
  97.9 3.6 %collective-permute-start.17 = (bf16[4,4,128,128]{3,2,1,0:T(8,128)(2,1)S(1)}, bf16[4,4,128,128]{3,2,1,0:T(8,128)(2,1)S(1)}, u32[]{:S(2)}, u32[]{:S(2)}) collective-permute-start(bf16[4,4,128,128]{3,2,1,0:T(8,128)(2,1)S(1)} %pad_maximum_fusion.rest_0_), channel_id=1, source_target_pairs={{0,1},{1,0},{2,3},{3,2},{4,5},{5,4},{6,7},{7,6},{8,9},{9,8},{10,11... | collective-permute-start | bytes 1572872 | tf_op jit(solution)/shard_map/ppermute | solution.py:34
  98.0 12.6 %collective-permute-start.11 = (bf16[4,128,128]{2,1,0:T(8,128)(2,1)S(1)}, bf16[4,128,128]{2,1,0:T(8,128)(2,1)S(1)}, u32[]{:S(2)}, u32[]{:S(2)}) collective-permute-start(bf16[4,128,128]{2,1,0:T(8,128)(2,1)S(1)} %fusion.3), channel_id=1, source_target_pairs={{0,2},{2,4},{4,6},{6,0},{1,3},{3,5},{5,7},{7,1},{8,10},{10,12},{12... | collective-permute-start | bytes 393224 | tf_op jit(solution)/shard_map/ppermute | solution.py:34
  99.2 11.4 %collective-permute-start.12 = (bf16[4,128,128]{2,1,0:T(8,128)(2,1)S(1)}, bf16[4,128,128]{2,1,0:T(8,128)(2,1)S(1)}, u32[]{:S(2)}, u32[]{:S(2)}) collective-permute-start(bf16[4,128,128]{2,1,0:T(8,128)(2,1)S(1)} %fusion.3), channel_id=1, source_target_pairs={{0,4},{2,6},{4,0},{6,2},{1,5},{3,7},{5,1},{7,3},{8,12},{10,14},{12... | collective-permute-start | bytes 393224 | tf_op jit(solution)/shard_map/ppermute | solution.py:34
  99.7 10.9 %collective-permute-start.13 = (bf16[4,128,128]{2,1,0:T(8,128)(2,1)S(1)}, bf16[4,128,128]{2,1,0:T(8,128)(2,1)S(1)}, u32[]{:S(2)}, u32[]{:S(2)}) collective-permute-start(bf16[4,128,128]{2,1,0:T(8,128)(2,1)S(1)} %fusion.3), channel_id=1, source_target_pairs={{0,6},{2,0},{4,2},{6,4},{1,7},{3,1},{5,3},{7,5},{8,14},{10,8},{12,... | collective-permute-start | bytes 393224 | tf_op jit(solution)/shard_map/ppermute | solution.py:34
  110.7 8.9 %copy-start.5 = (f32[128,2048]{1,0:T(8,128)S(1)}, f32[128,2048]{1,0:T(8,128)}, u32[]{:S(2)}) copy-start(f32[128,2048]{1,0:T(8,128)} %get-tuple-element.46.rest_0_) | copy-start | bytes 3145732
  110.8 1.4 collective-permute-start.22
  114.1 15.0 %collective-permute-start.23 = (bf16[8,16,256]{2,1,0:T(8,128)(2,1)S(1)}, bf16[8,16,256]{2,1,0:T(8,128)(2,1)S(1)}, u32[]{:S(2)}, u32[]{:S(2)}) collective-permute-start(bf16[8,16,256]{2,1,0:T(8,128)(2,1)S(1)} %get-tuple-element.60), channel_id=1, source_target_pairs={{0,8},{8,16},{16,24},{24,0},{1,9},{9,17},{17,25},{25,1},{2,10},{10... | collective-permute-start | bytes 196616 | tf_op jit(solution)/shard_map/ppermute | solution.py:34
  116.5 25.0 %collective-permute-start.24 = (bf16[8,16,256]{2,1,0:T(8,128)(2,1)S(1)}, bf16[8,16,256]{2,1,0:T(8,128)(2,1)S(1)}, u32[]{:S(2)}, u32[]{:S(2)}) collective-permute-start(bf16[8,16,256]{2,1,0:T(8,128)(2,1)S(1)} %get-tuple-element.59), channel_id=1, source_target_pairs={{0,16},{8,24},{16,0},{24,8},{1,17},{9,25},{17,1},{25,9},{2,18},{10... | collective-permute-start | bytes 196616 | tf_op jit(solution)/shard_map/ppermute | solution.py:34
  118.2 23.4 %collective-permute-start.25 = (bf16[8,16,256]{2,1,0:T(8,128)(2,1)S(1)}, bf16[8,16,256]{2,1,0:T(8,128)(2,1)S(1)}, u32[]{:S(2)}, u32[]{:S(2)}) collective-permute-start(bf16[8,16,256]{2,1,0:T(8,128)(2,1)S(1)} %get-tuple-element.58), channel_id=1, source_target_pairs={{0,24},{8,0},{16,8},{24,16},{1,25},{9,1},{17,9},{25,17},{2,26},{10... | collective-permute-start | bytes 196616 | tf_op jit(solution)/shard_map/ppermute | solution.py:34

commit v7 on v6

--- a/solution.py
+++ b/solution.py
@@ -29,13 +29,34 @@
     )
 
 
-def shift(piece, axis, step):
-    count = lax.axis_size(axis)
-    return lax.ppermute(piece, axis, [(i, (i + step) % count) for i in range(count)])
-
-
 def wrap(index, count):
     return lax.rem(index + 2 * count, count)
+
+
+def shift(piece, axis, k):
+    count = lax.axis_size(axis)
+    return lax.ppermute(piece, axis, [(i, (i + k) % count) for i in range(count)])
+
+
+def paired(count):
+    return count & (count - 1) == 0
+
+
+def partner(index, k, count):
+    return index ^ k if paired(count) else (index + k) % count
+
+
+def came_from(index, k, count):
+    return index ^ k if paired(count) else wrap(index - k, count)
+
+
+def which_partner(other, index, count):
+    return other ^ index if paired(count) else wrap(other - index, count)
+
+
+def swap(piece, axis, k):
+    count = lax.axis_size(axis)
+    return lax.ppermute(piece, axis, [(i, partner(i, k, count)) for i in range(count)])
 
 
 def pick_up(at, slot_of, adapter_up, data_count):
@@ -83,6 +104,29 @@
     )(at, adapter_down, grad_rows)
 
 
+def features(at, tokens, k, data_count):
+    tok_dev, depth = tokens.shape
+    count = depth // data_count
+    if count % 128:
+        return lax.dynamic_slice_in_dim(tokens, wrap(at[0] + k, data_count) * count, count, 1).T
+
+    def kernel(at_ref, x_ref, out_ref):
+        out_ref[...] = x_ref[...].T
+
+    tile = 256 if tok_dev % 256 == 0 else tok_dev
+    return call(
+        kernel,
+        "features",
+        grid_spec=pltpu.PrefetchScalarGridSpec(
+            num_scalar_prefetch=1,
+            grid=(tok_dev // tile,),
+            in_specs=[pl.BlockSpec((tile, count), lambda n, at: (n, wrap(at[0] + k, data_count)))],
+            out_specs=pl.BlockSpec((count, tile), lambda n, at: (0, n)),
+        ),
+        out_shape=jax.ShapeDtypeStruct((count, tok_dev), tokens.dtype),
+    )(at, tokens)
+
+
 def base_product(at, tokens, weight, first, count):
     pipe_count, tensor_count, rows, depth = tokens.shape
     tile = 1024
@@ -91,7 +135,7 @@
         x = x_ref[...].reshape(pipe_count * rows, depth)
         y = jnp.dot(x, w_ref[...], preferred_element_type=jnp.float32).astype(out_ref.dtype)
         for chip in range(pipe_count):
-            out_ref[0, wrap(chip - at_ref[1], pipe_count)] = y[chip * rows : (chip + 1) * rows]
+            out_ref[0, which_partner(chip, at_ref[1], pipe_count)] = y[chip * rows : (chip + 1) * rows]
 
     return call(
         kernel,
@@ -102,7 +146,7 @@
             in_specs=[
                 pl.BlockSpec(
                     (pipe_count, 1, rows, depth),
-                    lambda n, s, at: (0, wrap(at[2] + s + first, tensor_count), 0, 0),
+                    lambda n, s, at: (0, partner(at[2], s + first, tensor_count), 0, 0),
                 ),
                 pl.BlockSpec((depth, tile), lambda n, s, at: (0, n)),
             ],
@@ -124,7 +168,7 @@
             y = jnp.dot(x, a, preferred_element_type=jnp.float32).astype(out_ref.dtype)
             for part in range(BLOCK // rows):
                 chip, core = divmod(block * (BLOCK // rows) + part, tensor_count)
-                core = wrap(core - at_ref[2], tensor_count)
+                core = which_partner(core, at_ref[2], tensor_count)
                 out_ref[core, chip] = y[part * rows : (part + 1) * rows]
 
     return call(
@@ -136,46 +180,76 @@
     )(at, tokens, down)
 
 
-def input_gradient(at, cot_pieces, weight, grad_pieces, down):
-    data_count, all_rows, _ = down.shape
+def cotangent_product(at, cot_pieces, weight):
     tensor_count, pipe_count = len(cot_pieces), len(cot_pieces[0])
     rows = cot_pieces[0][0].shape[0]
     depth = weight.shape[0]
+    tok_dev = tensor_count * pipe_count * rows
+    tile = 256 if depth % 256 == 0 else depth
+    order = [(s, k) for s in range(tensor_count) for k in range(pipe_count)]
+
+    def kernel(at_ref, w_ref, *rest):
+        cot_refs, (out_ref, cot, sems) = rest[: len(order)], rest[len(order) :]
+
+        @pl.when(pl.program_id(0) == 0)
+        def _():
+            copies = []
+            for i, (s, k) in enumerate(order):
+                chip = came_from(at_ref[1], k, pipe_count)
+                core = came_from(at_ref[2], s, tensor_count)
+                first = pl.multiple_of((chip * tensor_count + core) * rows, rows)
+                copies.append(
+                    pltpu.make_async_copy(cot_refs[i], cot.at[pl.ds(first, rows)], sems.at[i])
+                )
+            for copy in copies:
+                copy.start()
+            for copy in copies:
+                copy.wait()
+
+        out_ref[...] = lax.dot_general(
+            cot[...], w_ref[...], LAST_BOTH, preferred_element_type=jnp.float32
+        )
+
+    return call(
+        kernel,
+        "cotangent_product",
+        grid=(depth // tile,),
+        in_specs=[SMEM, pl.BlockSpec((tile, WIDTH), lambda n: (n, 0))] + [ANY] * len(order),
+        out_specs=pl.BlockSpec((tok_dev, tile), lambda n: (0, n)),
+        out_shape=jax.ShapeDtypeStruct((tok_dev, depth), jnp.float32),
+        scratch_shapes=[
+            pltpu.VMEM((tok_dev, WIDTH), jnp.bfloat16),
+            pltpu.SemaphoreType.DMA((len(order),)),
+        ],
+    )(at, weight, *[cot_pieces[s][k] for s, k in order])
+
+
+def input_gradient(at, base, grad_pieces, down):
+    data_count, all_rows, _ = down.shape
+    tensor_count = len(grad_pieces)
+    pipe_count, _, rows, _ = grad_pieces[0].shape
+    tok_dev, depth = base.shape
     down_rows = depth // data_count
-    tok_dev = tensor_count * pipe_count * rows
-    blocks_dev = tok_dev // BLOCK
     planes = next((n for n in range(1, data_count) if n * down_rows % 256 == 0), data_count)
     tile = planes * down_rows
-    order = [(s, k) for s in range(tensor_count) for k in range(pipe_count)]
-
-    def kernel(at_ref, w_ref, a_ref, *rest):
-        grad_refs, rest = rest[:tensor_count], rest[tensor_count:]
-        cot_refs, (out_ref, cot, grad, sems) = rest[: len(order)], rest[len(order) :]
-
-        def first_row(s, k):
-            chip = wrap(at_ref[1] - k, pipe_count)
-            core = wrap(at_ref[2] - s, tensor_count)
-            return pl.multiple_of((chip * tensor_count + core) * rows, rows)
+
+    def kernel(at_ref, base_ref, a_ref, *rest):
+        grad_refs, (out_ref, grad) = rest[:tensor_count], rest[tensor_count:]
 
         @pl.when(pl.program_id(0) == 0)
         def _():
-            copies = [
-                pltpu.make_async_copy(ref, cot.at[pl.ds(first_row(*at), rows)], sems.at[i])
-                for i, (at, ref) in enumerate(zip(order, cot_refs))
-            ]
-            for copy in copies:
-                copy.start()
-            for s, k in order:
-                grad[pl.ds(first_row(s, k), rows)] = grad_refs[s][k, at_ref[0]]
-            for copy in copies:
-                copy.wait()
-
-        base = lax.dot_general(cot[...], w_ref[...], LAST_BOTH, preferred_element_type=jnp.float32)
-        for block in range(blocks_dev):
-            at = slice(block * BLOCK, (block + 1) * BLOCK)
+            for s in range(tensor_count):
+                core = came_from(at_ref[2], s, tensor_count)
+                for k in range(pipe_count):
+                    chip = came_from(at_ref[1], k, pipe_count)
+                    first = pl.multiple_of((chip * tensor_count + core) * rows, rows)
+                    grad[pl.ds(first, rows)] = grad_refs[s][k, at_ref[0]]
+
+        for block in range(tok_dev // BLOCK):
+            here = slice(block * BLOCK, (block + 1) * BLOCK)
             a = a_ref[:, block * down_rows : (block + 1) * down_rows].reshape(tile, RANKS)
-            low = lax.dot_general(grad[at], a, LAST_BOTH, preferred_element_type=jnp.float32)
-            out_ref[at] = (base[at] + low).astype(out_ref.dtype)
+            low = lax.dot_general(grad[here], a, LAST_BOTH, preferred_element_type=jnp.float32)
+            out_ref[here] = (base_ref[here] + low).astype(out_ref.dtype)
 
     grad_shape = (pipe_count, data_count, rows, RANKS)
     return call(
@@ -184,53 +258,56 @@
         grid=(data_count // planes,),
         in_specs=[
             SMEM,
-            pl.BlockSpec((tile, WIDTH), lambda n: (n, 0)),
+            pl.BlockSpec((tok_dev, tile), lambda n: (0, n)),
             pl.BlockSpec((planes, all_rows, RANKS), lambda n: (n, 0, 0)),
         ]
-        + [pl.BlockSpec(grad_shape, lambda n: (0, 0, 0, 0))] * tensor_count
-        + [ANY] * len(order),
+        + [pl.BlockSpec(grad_shape, lambda n: (0, 0, 0, 0))] * tensor_count,
         out_specs=pl.BlockSpec((tok_dev, tile), lambda n: (0, n)),
         out_shape=jax.ShapeDtypeStruct((tok_dev, depth), jnp.bfloat16),
-        scratch_shapes=[
-            pltpu.VMEM((tok_dev, WIDTH), jnp.bfloat16),
-            pltpu.VMEM((tok_dev, RANKS), jnp.bfloat16),
-            pltpu.SemaphoreType.DMA((len(order),)),
-        ],
-    )(at, weight, down, *grad_pieces, *[cot_pieces[s][k] for s, k in order])
+        scratch_shapes=[pltpu.VMEM((tok_dev, RANKS), jnp.bfloat16)],
+    )(at, base, down, *grad_pieces)
 
 
 def grad_down(at, slot_of, slots, x_features, grad_pieces):
-    data_count, down_rows, tok_dev = x_features.shape
+    data_count = len(x_features)
+    down_rows = sum(part.shape[0] for part in x_features[0])
+    tok_dev = x_features[0][0].shape[1]
+    parts = [(k, part) for k in range(data_count) for part in x_features[k]]
     tensor_count = len(grad_pieces)
     pipe_count, _, rows, _ = grad_pieces[0].shape
     blocks_dev = tok_dev // BLOCK
 
-    def kernel(at_ref, x_ref, *rest):
+    def kernel(at_ref, *rest):
+        x_refs, rest = rest[: len(parts)], rest[len(parts) :]
         grad_refs, (out_ref, grad) = rest[:tensor_count], rest[tensor_count:]
         for s in range(tensor_count):
-            core = wrap(at_ref[2] - s, tensor_count)
+            core = came_from(at_ref[2], s, tensor_count)
             for k in range(pipe_count):
-                chip = wrap(at_ref[1] - k, pipe_count)
+                chip = came_from(at_ref[1], k, pipe_count)
                 first = pl.multiple_of((chip * tensor_count + core) * rows, rows)
                 for data in range(data_count):
                     grad[data, pl.ds(first, rows)] = grad_refs[s][k, data]
         out_ref[...] = jnp.zeros(out_ref.shape, out_ref.dtype)
-        for data in range(data_count):
+        first = 0
+        for (k, part), x_ref in zip(parts, x_refs):
+            data = wrap(at_ref[0] - k, data_count)
+            features_at = slice(first, first + part.shape[0])
+            first = features_at.stop % down_rows
             for block in range(blocks_dev):
                 slot = slot_of(at_ref, data, block)
-                at = slice(block * BLOCK, (block + 1) * BLOCK)
-                out_ref[slot] += jnp.dot(
-                    x_ref[data, :, at], grad[data, at], preferred_element_type=jnp.float32
+                here = slice(block * BLOCK, (block + 1) * BLOCK)
+                out_ref[slot, features_at] += jnp.dot(
+                    x_ref[:, here], grad[data, here], preferred_element_type=jnp.float32
                 )
 
     return call(
         kernel,
         "grad_down",
-        in_specs=[SMEM, VMEM] + [VMEM] * tensor_count,
+        in_specs=[SMEM] + [VMEM] * (len(parts) + tensor_count),
         out_specs=VMEM,
         out_shape=jax.ShapeDtypeStruct((slots, down_rows, RANKS), jnp.float32),
         scratch_shapes=[pltpu.VMEM((data_count, tok_dev, RANKS), jnp.bfloat16)],
-    )(at, x_features, *grad_pieces)
+    )(at, *[part for _, part in parts], *grad_pieces)
 
 
 def grad_up_pieces(at, low_pieces, cot_pieces, data_count, up_rows):
@@ -254,8 +331,8 @@
         my_group = at_ref[1] * tensor_count + at_ref[2]
         copies = []
         for i, (s, k) in enumerate(order):
-            core = wrap(at_ref[2] - s, tensor_count)
-            chip = wrap(at_ref[1] - k, pipe_count)
+            core = came_from(at_ref[2], s, tensor_count)
+            chip = came_from(at_ref[1], k, pipe_count)
             first = pl.multiple_of((chip * tensor_count + core) * rows, rows)
             piece = cot_refs[i]
             if in_kernel:
@@ -264,7 +341,7 @@
         for copy in copies:
             copy.start()
         for s in range(tensor_count):
-            core = wrap(at_ref[2] - s, tensor_count)
+            core = came_from(at_ref[2], s, tensor_count)
             for k in range(pipe_count):
                 first = pl.multiple_of((k * tensor_count + core) * rows, rows)
                 low[pl.ds(first, rows)] = low_refs[s][k]
@@ -398,60 +475,74 @@
     def slot_of(at_ref, data, block):
         return at_ref[4 + blocks + at_ref[4 + data * blocks_dev + block]]
 
+    x_came = [[features(at, tokens, 0, data_count)]]
+    x_came += [[shift(features(at, tokens, 1, data_count), "dp", 1)]] if data_count > 1 else []
+
     b_send = pick_up(at, slot_of, adapter_up, data_count)
     b_came = [b_send[0]] + [shift(b_send[k], "dp", k) for k in range(1, data_count)]
+    b_came, x_came[1:] = lax.optimization_barrier((b_came, x_came[1:]))
     b_own, grad_rows = own_rows(at, b_came, cotangent)
 
     a_send = pick_down(at, slot_of, adapter_down, grad_rows, data_count, blocks_dev)
     a_recv = lax.all_to_all(a_send, "dp", 0, 0, tiled=True)
 
+    cot_send, b_send = lax.optimization_barrier((cotangent, b_send))
+    cot_chips = [cotangent] + [swap(cot_send, "pipe", k) for k in range(1, pipe_count - 1)]
     cot_send, a_send = lax.optimization_barrier((cotangent, a_send))
-    cot_chips = [cotangent] + [shift(cot_send, "pipe", k) for k in range(1, pipe_count)]
-
-    base_tokens, cot_chips[1] = lax.optimization_barrier((tokens, cot_chips[1]))
+    cot_chips += [swap(cot_send, "pipe", pipe_count - 1)]
+
+    base_tokens, cot_chips[-1] = lax.optimization_barrier((tokens, cot_chips[-1]))
     tokens_by_group = base_tokens.reshape(pipe_count, tensor_count, rows, feature_count)
     base_send = base_product(at, tokens_by_group, key_value_weight, 1, tensor_count - 1)
-    base_came = [shift(base_send[s - 1], "tensor", s) for s in range(1, tensor_count)]
+    base_came = [swap(base_send[s - 1], "tensor", s) for s in range(1, tensor_count)]
     base_keep = base_product(at, tokens_by_group, key_value_weight, 0, 1)[0]
     base_chip = [
         sum([base_keep[k].astype(jnp.float32)] + [b[k].astype(jnp.float32) for b in base_came])
         for k in range(pipe_count)
     ]
     base_chip[1:] = [piece.astype(jnp.bfloat16) for piece in base_chip[1:]]
-    base_chip_came = [shift(base_chip[k], "pipe", k) for k in range(1, pipe_count)]
+    base_chip_came = [swap(base_chip[k], "pipe", k) for k in range(1, pipe_count)]
+
+    cot_pieces = [cot_chips] + [
+        [swap(piece, "tensor", s) for piece in cot_chips] for s in range(1, tensor_count)
+    ]
+    input_base = cotangent_product(at, cot_pieces, key_value_weight)
 
     x_tokens, base_chip = lax.optimization_barrier((tokens, base_chip))
-    x_send = x_tokens.T.reshape(data_count, down_rows, tok_dev)
-    a_recv, x_send, cot_chips, base_chip_came = lax.optimization_barrier(
-        (a_recv, x_send, cot_chips, base_chip_came)
+    x_send = [[features(at, x_tokens, k, data_count)] for k in range(2, data_count)]
+    if down_rows % 256 == 0:
+        x_send[:-1] = [jnp.split(whole, 2) for (whole,) in x_send[:-1]]
+    a_recv, x_send, input_base, base_chip_came[:1] = lax.optimization_barrier(
+        (a_recv, x_send, input_base, base_chip_came[:1])
     )
-    x_recv = lax.all_to_all(x_send, "dp", 0, 0, tiled=True)
-
-    cot_pieces = [cot_chips] + [
-        [shift(piece, "tensor", s) for piece in cot_chips] for s in range(1, tensor_count)
-    ]
+    x_came += [[shift(part, "dp", k + 2) for part in parts] for k, parts in enumerate(x_send)]
+
     grad_data = a_recv[:, blocks_dev * down_rows :]
-    grad_chips = jnp.stack([grad_data] + [shift(grad_data, "pipe", k) for k in range(1, pipe_count)])
-    grad_pieces = [grad_chips] + [shift(grad_chips, "tensor", s) for s in range(1, tensor_count)]
-    input_grad = input_gradient(at, cot_pieces, key_value_weight, grad_pieces, a_recv)
-
-    low_part = low_product(at, tokens, a_recv, pipe_count, tensor_count)
+    grad_chips = jnp.stack([grad_data] + [swap(grad_data, "pipe", k) for k in range(1, pipe_count)])
+    grad_pieces = [grad_chips] + [swap(grad_chips, "tensor", s) for s in range(1, tensor_count)]
+    input_grad = input_gradient(at, input_base, grad_pieces, a_recv)
+
+    x_first = [parts[0] for parts in x_came[2:-1]]
+    low_down, base_chip_came, x_first = lax.optimization_barrier((a_recv, base_chip_came, x_first))
+    low_part = low_product(at, tokens, low_down, pipe_count, tensor_count)
     low_core = sum(
         [low_part[0].astype(jnp.float32)]
-        + [shift(low_part[s], "tensor", s).astype(jnp.float32) for s in range(1, tensor_count)]
+        + [swap(low_part[s], "tensor", s).astype(jnp.float32) for s in range(1, tensor_count)]
     ).astype(jnp.bfloat16)
-    low_came = [shift(low_core, "pipe", k) for k in range(1, pipe_count)]
-    low_came, input_grad = lax.optimization_barrier((low_came, input_grad))
+    low_came = [swap(low_core, "pipe", k) for k in range(1, pipe_count)]
+    x_rest = [parts[1:] for parts in x_came[2:-1]]
+    low_came, x_rest = lax.optimization_barrier((low_came, x_rest))
     low_sum = sum([piece.astype(jnp.float32) for piece in [low_core] + low_came])
     low_sum = low_sum.astype(jnp.bfloat16)
-    low_pieces = [low_sum] + [shift(low_sum, "tensor", s) for s in range(1, tensor_count)]
+    low_pieces = [low_sum] + [swap(low_sum, "tensor", s) for s in range(1, tensor_count)]
     key_value = keys_and_values(at, base_chip[:1] + base_chip_came, low_sum, b_own)
 
     up_pieces = grad_up_pieces(at, low_pieces, cot_pieces, data_count, up_rows)
     up_came = [up_pieces[0]] + [shift(up_pieces[k], "dp", k) for k in range(1, data_count)]
     grad_b = grad_up(at, slot_of, slots, up_came)
 
-    grad_a = grad_down(at, slot_of, slots, x_recv, grad_pieces)
+    x_came[2:-1] = [[part] + rest for part, rest in zip(x_first, x_rest)]
+    grad_a = grad_down(at, slot_of, slots, x_came, grad_pieces)
     return (key_value, input_grad, grad_a, grad_b)
 
 

time: 148 us -> 152 us (1.027)
  the two profiles are of different devices: /device:TPU:6 before, /device:TPU:0 now
where the time goes in v7:
time: 152 us
  waiting for transfers between devices  57.7 us (38%)
  starting transfers between devices  45.5 us (30%)
  Pallas kernels  37.9 us (25%)
  local copies, waits for them, and re-layouts  7.56 us (5%)
  other arithmetic  2.04 us (1%)
    ppermute x20, waiting for transfers between devices, swap(): lax.ppermute(piece, axis, [(i, partner(i, k, count)) for i in range(count)])  37.5 us
    ppermute x10, starting transfers between devices, shift(): lax.ppermute(piece, axis, [(i, (i + k) % count) for i in range(count)])  25.1 us
    ppermute x10, waiting for transfers between devices, shift(): lax.ppermute(piece, axis, [(i, (i + k) % count) for i in range(count)])  19.9 us
    ppermute x20, starting transfers between devices, swap(): lax.ppermute(piece, axis, [(i, partner(i, k, count)) for i in range(count)])  15.9 us
    pallas_call x2, Pallas kernels, base_product(): call(kernel, 'base_product', grid_spec=pltpu.PrefetchScalarGridSpec(num_s...  7.22 us
    pallas_call x1, Pallas kernels, cotangent_product(): call(kernel, 'cotangent_product', grid=(depth // tile,), in_specs=[SMEM,...  6.58 us
    unnamed x58, local copies, waits for them, and re-layouts  4.76 us
    pallas_call x1, Pallas kernels, input_gradient(): call(kernel, 'input_gradient', grid=(data_count // planes,), in_specs=[SM...  4.61 us
  transfers between devices with their start and end apart: 31, of which 14 were waited for; matrix products, arithmetic and copies ran while one was open for 3% of the time, Pallas kernels for 19%

profile of v7, /device:TPU:0, one launch (start us, length us, event | category | flops | bytes accessed | tf_op | source)
XLA Modules:
  0.0 151.8 jit_solution(514334302480508099)
XLA Ops:
  0.6 0.8 concatenate.3.at_ref
  1.4 1.6 %copy-done = bf16[1024,1024]{1,0:T(8,128)(2,1)S(1)} copy-done((bf16[1024,1024]{1,0:T(8,128)(2,1)S(1)}, bf16[1024,1024]{1,0:T(8,128)(2,1)}, u32[]{:S(2)}) %copy-start) | copy-done | bytes 2097176
  3.0 1.1 features.4
  4.1 3.1 %collective-permute-start.3 = (bf16[256,1024]{1,0:T(8,128)(2,1)S(1)}, bf16[256,1024]{1,0:T(8,128)(2,1)S(1)}, u32[]{:S(2)}, u32[]{:S(2)}) collective-permute-start(bf16[256,1024]{1,0:T(8,128)(2,1)S(1)} %features.4), channel_id=1, source_target_pairs={{0,8},{8,16},{16,24},{24,0},{1,9},{9,17},{17,25},{25,1},{2,10},{10... | collective-permute-start | bytes 1572872 | tf_op jit(solution)/shard_map/ppermute | solution.py:38
  7.2 0.9 pick_up.1
  8.1 1.6 %collective-permute-start = (bf16[16,2048]{1,0:T(8,128)(2,1)S(1)}, bf16[16,2048]{1,0:T(8,128)(2,1)S(1)}, u32[]{:S(2)}, u32[]{:S(2)}) collective-permute-start(bf16[16,2048]{1,0:T(8,128)(2,1)S(1)} %get-tuple-element.37), channel_id=1, source_target_pairs={{0,8},{8,16},{16,24},{24,0},{1,9},{9,17},{17,25},{25,1},{2,10},{10... | collective-permute-start | bytes 196616 | tf_op jit(solution)/shard_map/ppermute | solution.py:38
  9.8 1.2 collective-permute-start.1
  11.0 2.7 %collective-permute-start.2 = (bf16[16,2048]{1,0:T(8,128)(2,1)S(1)}, bf16[16,2048]{1,0:T(8,128)(2,1)S(1)}, u32[]{:S(2)}, u32[]{:S(2)}) collective-permute-start(bf16[16,2048]{1,0:T(8,128)(2,1)S(1)} %get-tuple-element.39), channel_id=1, source_target_pairs={{0,24},{8,0},{16,8},{24,16},{1,25},{9,1},{17,9},{25,17},{2,26},{10... | collective-permute-start | bytes 196616 | tf_op jit(solution)/shard_map/ppermute | solution.py:38
  13.7 9.8 %collective-permute-done.rest_1_ = bf16[16,2048]{1,0:T(8,128)(2,1)S(1)} collective-permute-done((bf16[16,2048]{1,0:T(8,128)(2,1)S(1)}, bf16[16,2048]{1,0:T(8,128)(2,1)S(1)}, u32[]{:S(2)}, u32[]{:S(2)}) %collective-permute-start) | collective-permute-done | bytes 65568 | tf_op jit(solution)/shard_map/ppermute | solution.py:38
  23.5 2.0 %collective-permute-done.1.rest_2_ = bf16[16,2048]{1,0:T(8,128)(2,1)S(1)} collective-permute-done((bf16[16,2048]{1,0:T(8,128)(2,1)S(1)}, bf16[16,2048]{1,0:T(8,128)(2,1)S(1)}, u32[]{:S(2)}, u32[]{:S(2)}) %collective-permute-start.1) | collective-permute-done | bytes 65568 | tf_op jit(solution)/shard_map/ppermute | solution.py:38
  25.5 0.9 own_rows.1
  26.4 2.4 %pick_down.1 = bf16[4,2176,128]{2,1,0:T(8,128)(2,1)} custom-call(s32[60]{0:T(128)S(1)} %concatenate.3.at_ref, bf16[24,256,128]{2,1,0:T(8,128)(2,1)S(1)} %copy-done.21, bf16[128,128]{1,0:T(8,128)(2,1)S(1)} %get-tuple-element.44.grad_ref), custom_call_target="tpu_custom_call" | custom-call | flops 1024 | bytes 1024 | tf_op jit(solution)/shard_map/pick_down/pallas_call | solution.py:97
  28.9 2.5 %collective-permute-start.4 = (bf16[128,2048]{1,0:T(8,128)(2,1)S(1)}, bf16[128,2048]{1,0:T(8,128)(2,1)S(1)}, u32[]{:S(2)}, u32[]{:S(2)}) collective-permute-start(bf16[128,2048]{1,0:T(8,128)(2,1)S(1)} %copy-done.6), channel_id=1, source_target_pairs={{0,6},{2,4},{4,2},{6,0},{1,7},{3,5},{5,3},{7,1},{8,14},{10,12},{12... | collective-permute-start | bytes 1572872 | tf_op jit(solution)/shard_map/ppermute | solution.py:59
  31.3 4.5 %all-to-all-start = ((bf16[4,2176,128]{2,1,0:T(8,128)(2,1)}), bf16[4,2176,128]{2,1,0:T(8,128)(2,1)}, u32[]{:S(2)}, u32[]{:S(2)}) async-start(bf16[4,2176,128]{2,1,0:T(8,128)(2,1)} %pick_down.1), calls=%async_computation | async-start | bytes 4456448 | tf_op jit(solution)/shard_map/all_to_all | solution.py:487
  35.8 7.7 %collective-permute-done.4.rest_3_.rest_5_ = bf16[128,2048]{1,0:T(8,128)(2,1)S(1)} collective-permute-done((bf16[128,2048]{1,0:T(8,128)(2,1)S(1)}, bf16[128,2048]{1,0:T(8,128)(2,1)S(1)}, u32[]{:S(2)}, u32[]{:S(2)}) %collective-permute-start.4) | collective-permute-done | bytes 524320 | tf_op jit(solution)/shard_map/ppermute | solution.py:59
  43.6 2.2 %copy-done.2 = bf16[1024,2048]{1,0:T(8,128)(2,1)S(1)} copy-done((bf16[1024,2048]{1,0:T(8,128)(2,1)S(1)}, bf16[1024,2048]{1,0:T(8,128)(2,1)}, u32[]{:S(2)}) %copy-start.2) | copy-done | bytes 4194328
  45.7 3.6 %base_product.3 = bf16[1,4,128,2048]{3,2,1,0:T(8,128)(2,1)S(1)} custom-call(s32[60]{0:T(128)S(1)} %concatenate.3.at_ref, bf16[4,2,128,1024]{3,2,1,0:T(8,128)(2,1)S(1)} %bitcast.66, bf16[1024,2048]{1,0:T(8,128)(2,1)S(1)} %copy-done.2), custom_call_target="tpu_custom_call" | custom-call | flops 1024 | bytes 1024 | tf_op jit(solution)/shard_map/base_product/pallas_call | solution.py:140
  49.4 0.1 collective-permute-start.5
  49.4 1.6 %collective-permute-start.6 = (bf16[128,2048]{1,0:T(8,128)(2,1)S(1)}, bf16[128,2048]{1,0:T(8,128)(2,1)S(1)}, u32[]{:S(2)}, u32[]{:S(2)}) collective-permute-start(bf16[128,2048]{1,0:T(8,128)(2,1)S(1)} %copy-done.6), channel_id=1, source_target_pairs={{0,2},{2,0},{4,6},{6,4},{1,3},{3,1},{5,7},{7,5},{8,10},{10,8},{12,... | collective-permute-start | bytes 1572872 | tf_op jit(solution)/shard_map/ppermute | solution.py:59
  51.0 1.5 %collective-permute-start.7 = (bf16[128,2048]{1,0:T(8,128)(2,1)S(1)}, bf16[128,2048]{1,0:T(8,128)(2,1)S(1)}, u32[]{:S(2)}, u32[]{:S(2)}) collective-permute-start(bf16[128,2048]{1,0:T(8,128)(2,1)S(1)} %copy-done.6), channel_id=1, source_target_pairs={{0,4},{2,6},{4,0},{6,2},{1,5},{3,7},{5,1},{7,3},{8,12},{10,14},{12... | collective-permute-start | bytes 1572872 | tf_op jit(solution)/shard_map/ppermute | solution.py:59
  52.5 11.3 %collective-permute-done.6.rest_1_.rest_3_ = bf16[128,2048]{1,0:T(8,128)(2,1)S(1)} collective-permute-done((bf16[128,2048]{1,0:T(8,128)(2,1)S(1)}, bf16[128,2048]{1,0:T(8,128)(2,1)S(1)}, u32[]{:S(2)}, u32[]{:S(2)}) %collective-permute-start.6) | collective-permute-done | bytes 524320 | tf_op jit(solution)/shard_map/ppermute | solution.py:59
  63.8 1.2 collective-permute-done.7.rest_2_.rest_4_
  65.0 3.6 %base_product.2 = bf16[1,4,128,2048]{3,2,1,0:T(8,128)(2,1)S(1)} custom-call(s32[60]{0:T(128)S(1)} %concatenate.3.at_ref, bf16[4,2,128,1024]{3,2,1,0:T(8,128)(2,1)S(1)} %bitcast.67, bf16[1024,2048]{1,0:T(8,128)(2,1)S(1)} %copy-done.2), custom_call_target="tpu_custom_call" | custom-call | flops 1024 | bytes 1024 | tf_op jit(solution)/shard_map/base_product/pallas_call | solution.py:140
  68.6 0.6 collective-permute-start.11
  69.2 1.9 %fusion = (bf16[128,2048]{1,0:T(8,128)(2,1)}, bf16[128,2048]{1,0:T(8,128)(2,1)}, bf16[128,2048]{1,0:T(8,128)(2,1)S(1)}, f32[128,2048]{1,0:T(8,128)}) fusion(bf16[4,128,2048]{2,1,0:T(8,128)(2,1)S(1)} %collective-permute-done.5, bf16[1,4,128,2048]{3,2,1,0:T(8,128)(2,1)S(1)} %base_product.2), kind=kLoop, calls=%fused_computation.1 | loop fusion | flops 3932160 | bytes 6815744 | tf_op jit(solution)/shard_map/convert_element_type | solution.py:503
  71.1 0.5 collective-permute-start.12
  71.6 1.5 collective-permute-start.13
  73.1 1.4 collective-permute-start.14
  74.6 6.6 %cotangent_product.1.base_ref = f32[1024,1024]{1,0:T(8,128)S(1)} custom-call(s32[60]{0:T(128)S(1)} %concatenate.3.at_ref, bf16[1024,2048]{1,0:T(8,128)(2,1)S(1)} %copy-done.3, bf16[128,2048]{1,0:T(8,128)(2,1)S(1)} %copy-done.6, bf16[128,2048]{1,0:T(8,128)(2,1)S(1)} %collective-permute-done.6.rest_1_.rest_3_, ...), custom_call_target="tpu_custom_call" | custom-call | flops 1024 | bytes 1024 | tf_op jit(solution)/shard_map/cotangent_product/pallas_call | solution.py:213
  81.3 1.1 features.5
  82.4 1.1 features.6
  83.5 0.9 fusion.4
  84.4 0.1 copy-done.24
  84.5 1.3 collective-permute-done.12.rest_1_
  85.8 0.8 copy-done.26
  86.7 0.3 all-to-all-done.a_ref
  87.0 0.6 collective-permute-start.15
  87.6 8.4 %collective-permute-done.13.rest_2_ = bf16[128,2048]{1,0:T(8,128)(2,1)} collective-permute-done((bf16[128,2048]{1,0:T(8,128)(2,1)}, bf16[128,2048]{1,0:T(8,128)(2,1)}, u32[]{:S(2)}, u32[]{:S(2)}) %collective-permute-start.13) | collective-permute-done | bytes 524320 | tf_op jit(solution)/shard_map/ppermute | solution.py:59
  96.0 1.2 collective-permute-done.14.rest_3_
  97.2 3.8 %collective-permute-done.15.rest_2_ = bf16[128,1024]{1,0:T(8,128)(2,1)S(1)} collective-permute-done((bf16[128,1024]{1,0:T(8,128)(2,1)}, bf16[128,1024]{1,0:T(8,128)(2,1)S(1)}, u32[]{:S(2)}, u32[]{:S(2)}) %collective-permute-start.15) | collective-permute-done | bytes 262176 | tf_op jit(solution)/shard_map/ppermute | solution.py:38
  101.0 2.4 %low_product.1 = bf16[2,4,128,128]{3,2,1,0:T(8,128)(2,1)S(1)} custom-call(s32[60]{0:T(128)S(1)} %concatenate.3.at_ref, bf16[1024,1024]{1,0:T(8,128)(2,1)S(1)} %copy-done.1, bf16[4,2176,128]{2,1,0:T(8,128)(2,1)} %all-to-all-done.a_ref), custom_call_target="tpu_custom_call" | custom-call | flops 1024 | bytes 1024 | tf_op jit(solution)/shard_map/low_product/pallas_call | solution.py:174
  103.5 0.1 collective-permute-start.16
  103.6 1.1 slice_bitcast_fusion.14
  104.7 1.0 collective-permute-start.23
  105.7 1.0 collective-permute-start.22
  106.7 1.5 collective-permute-start.21
  108.3 0.6 collective-permute-start.17
  108.9 3.1 %collective-permute-done.23 = bf16[4,128,128]{2,1,0:T(8,128)(2,1)S(1)} collective-permute-done((bf16[4,128,128]{2,1,0:T(8,128)(2,1)S(1)}, bf16[4,128,128]{2,1,0:T(8,128)(2,1)S(1)}, u32[]{:S(2)}, u32[]{:S(2)}) %collective-permute-start.23) | collective-permute-done | bytes 131104 | tf_op jit(solution)/shard_map/ppermute | solution.py:59
  112.0 0.5 collective-permute-start.18
  112.5 1.8 %collective-permute-done.22 = bf16[4,128,128]{2,1,0:T(8,128)(2,1)S(1)} collective-permute-done((bf16[4,128,128]{2,1,0:T(8,128)(2,1)S(1)}, bf16[4,128,128]{2,1,0:T(8,128)(2,1)S(1)}, u32[]{:S(2)}, u32[]{:S(2)}) %collective-permute-start.22) | collective-permute-done | bytes 131104 | tf_op jit(solution)/shard_map/ppermute | solution.py:59
  114.3 0.9 collective-permute-start.19
  115.2 1.6 %collective-permute-start.25 = (bf16[256,1024]{1,0:T(8,128)(2,1)S(1)}, bf16[256,1024]{1,0:T(8,128)(2,1)S(1)}, u32[]{:S(2)}, u32[]{:S(2)}) collective-permute-start(bf16[256,1024]{1,0:T(8,128)(2,1)S(1)} %copy-done.25), channel_id=1, source_target_pairs={{0,24},{8,0},{16,8},{24,16},{1,25},{9,1},{17,9},{25,17},{2,26},{10... | collective-permute-start | bytes 1572872 | tf_op jit(solution)/shard_map/ppermute | solution.py:38
  117.0 4.3 %collective-permute-done.20.rest_3_ = bf16[128,1024]{1,0:T(8,128)(2,1)S(1)} collective-permute-done((bf16[128,1024]{1,0:T(8,128)(2,1)S(1)}, bf16[128,1024]{1,0:T(8,128)(2,1)S(1)}, u32[]{:S(2)}, u32[]{:S(2)}) %collective-permute-start.20) | collective-permute-done | bytes 262176 | tf_op jit(solution)/shard_map/ppermute | solution.py:38
  121.3 0.1 add_convert_fusion.low_ref.rest_0_
  121.4 0.6 collective-permute-start.26
  122.0 1.4 collective-permute-done.26.rest_1_
  123.4 1.1 grad_up_pieces.1
  124.6 10.8 %collective-permute-start.27 = (bf16[8,16,256]{2,1,0:T(8,128)(2,1)S(1)}, bf16[8,16,256]{2,1,0:T(8,128)(2,1)S(1)}, u32[]{:S(2)}, u32[]{:S(2)}) collective-permute-start(bf16[8,16,256]{2,1,0:T(8,128)(2,1)S(1)} %get-tuple-element.78), channel_id=1, source_target_pairs={{0,8},{8,16},{16,24},{24,0},{1,9},{9,17},{17,25},{25,1},{2,10},{10... | collective-permute-start | bytes 196616 | tf_op jit(solution)/shard_map/ppermute | solution.py:38
  135.4 3.4 %collective-permute-start.28 = (bf16[8,16,256]{2,1,0:T(8,128)(2,1)S(1)}, bf16[8,16,256]{2,1,0:T(8,128)(2,1)S(1)}, u32[]{:S(2)}, u32[]{:S(2)}) collective-permute-start(bf16[8,16,256]{2,1,0:T(8,128)(2,1)S(1)} %get-tuple-element.77), channel_id=1, source_target_pairs={{0,16},{8,24},{16,0},{24,8},{1,17},{9,25},{17,1},{25,9},{2,18},{10... | collective-permute-start | bytes 196616 | tf_op jit(solution)/shard_map/ppermute | solution.py:38
  138.8 1.1 features.7.rest_0_
  139.9 2.6 %keys_and_values.1 = bf16[128,2048]{1,0:T(8,128)(2,1)} custom-call(s32[60]{0:T(128)S(1)} %concatenate.3.at_ref, bf16[4,128,128]{2,1,0:T(8,128)(2,1)S(1)} %add_convert_fusion.low_ref.rest_0_, bf16[64,2048]{1,0:T(8,128)(2,1)S(1)} %get-tuple-element.58.b_ref, f32[128,2048]{1,0:T(8,128)S(1)} %copy-done.7, bf16[128,2048]{1,0:T(8,128)(2,1)S(1)} %copy-done.27, ...), custom_call_target="tpu_custom_call" | custom-call | flops 1024 | bytes 1024 | tf_op jit(solution)/shard_map/keys_and_values/pallas_call | solution.py:445
  142.5 4.6 %input_gradient.1 = bf16[1024,1024]{1,0:T(8,128)(2,1)} custom-call(s32[60]{0:T(128)S(1)} %concatenate.3.at_ref, f32[1024,1024]{1,0:T(8,128)S(1)} %copy-done.5, bf16[4,2176,128]{2,1,0:T(8,128)(2,1)} %all-to-all-done.a_ref, bf16[4,4,128,128]{3,2,1,0:T(8,128)(2,1)S(1)} %pad_maximum_fusion.rest_0_.rest_5_, ...), custom_call_target="tpu_custom_call" | custom-call | flops 1024 | bytes 1024 | tf_op jit(solution)/shard_map/input_gradient/pallas_call | solution.py:255
  147.1 3.2 %grad_down.1 = f32[24,256,128]{2,1,0:T(8,128)} custom-call(s32[60]{0:T(128)S(1)} %concatenate.3.at_ref, bf16[256,1024]{1,0:T(8,128)(2,1)S(1)} %features.7.rest_0_, bf16[256,1024]{1,0:T(8,128)(2,1)S(1)} %copy-done.23, bf16[128,1024]{1,0:T(8,128)(2,1)S(1)} %collective-permute-done.15.rest_2_, bf16[128,1024]{1,0:T(8,128)(2,1)S(1)} %collective-permute-done.20.rest_3_, ...), custom_call_target="tpu_custom_call" | custom-call | flops 1024 | bytes 1024 | tf_op jit(solution)/shard_map/grad_down/pallas_call | solution.py:303
  150.3 1.5 grad_up.1
  (81 shorter events, 0.3 us)
Async XLA Ops:
  1.4 1.6 %copy-start = (bf16[1024,1024]{1,0:T(8,128)(2,1)S(1)}, bf16[1024,1024]{1,0:T(8,128)(2,1)}, u32[]{:S(2)}) copy-start(bf16[1024,1024]{1,0:T(8,128)(2,1)} %x_ref.7) | copy-start | bytes 6291460
  3.0 4.2 %copy-start.20 = (bf16[24,16,2048]{2,1,0:T(8,128)(2,1)S(1)}, bf16[24,16,2048]{2,1,0:T(8,128)(2,1)}, u32[]{:S(2)}) copy-start(bf16[24,16,2048]{2,1,0:T(8,128)(2,1)} %up_ref.1) | copy-start | bytes 4718596
  3.0 22.5 %copy-start.6 = (bf16[128,2048]{1,0:T(8,128)(2,1)S(1)}, bf16[128,2048]{1,0:T(8,128)(2,1)}, u32[]{:S(2)}) copy-start(bf16[128,2048]{1,0:T(8,128)(2,1)} %rest_2_.1) | copy-start | bytes 1572868
  3.0 23.4 %copy-start.21 = (bf16[24,256,128]{2,1,0:T(8,128)(2,1)S(1)}, bf16[24,256,128]{2,1,0:T(8,128)(2,1)}, u32[]{:S(2)}) copy-start(bf16[24,256,128]{2,1,0:T(8,128)(2,1)} %down_ref.1) | copy-start | bytes 4718596
  4.1 21.4 %collective-permute-start.3 = (bf16[256,1024]{1,0:T(8,128)(2,1)S(1)}, bf16[256,1024]{1,0:T(8,128)(2,1)S(1)}, u32[]{:S(2)}, u32[]{:S(2)}) collective-permute-start(bf16[256,1024]{1,0:T(8,128)(2,1)S(1)} %features.4), channel_id=1, source_target_pairs={{0,8},{8,16},{16,24},{24,0},{1,9},{9,17},{17,25},{25,1},{2,10},{10... | collective-permute-start | bytes 1572872 | tf_op jit(solution)/shard_map/ppermute | solution.py:38
  8.1 15.3 %collective-permute-start = (bf16[16,2048]{1,0:T(8,128)(2,1)S(1)}, bf16[16,2048]{1,0:T(8,128)(2,1)S(1)}, u32[]{:S(2)}, u32[]{:S(2)}) collective-permute-start(bf16[16,2048]{1,0:T(8,128)(2,1)S(1)} %get-tuple-element.37), channel_id=1, source_target_pairs={{0,8},{8,16},{16,24},{24,0},{1,9},{9,17},{17,25},{25,1},{2,10},{10... | collective-permute-start | bytes 196616 | tf_op jit(solution)/shard_map/ppermute | solution.py:38
  9.8 15.7 %collective-permute-start.1 = (bf16[16,2048]{1,0:T(8,128)(2,1)S(1)}, bf16[16,2048]{1,0:T(8,128)(2,1)S(1)}, u32[]{:S(2)}, u32[]{:S(2)}) collective-permute-start(bf16[16,2048]{1,0:T(8,128)(2,1)S(1)} %get-tuple-element.38), channel_id=1, source_target_pairs={{0,16},{8,24},{16,0},{24,8},{1,17},{9,25},{17,1},{25,9},{2,18},{10... | collective-permute-start | bytes 196616 | tf_op jit(solution)/shard_map/ppermute | solution.py:38
  11.0 14.5 %collective-permute-start.2 = (bf16[16,2048]{1,0:T(8,128)(2,1)S(1)}, bf16[16,2048]{1,0:T(8,128)(2,1)S(1)}, u32[]{:S(2)}, u32[]{:S(2)}) collective-permute-start(bf16[16,2048]{1,0:T(8,128)(2,1)S(1)} %get-tuple-element.39), channel_id=1, source_target_pairs={{0,24},{8,0},{16,8},{24,16},{1,25},{9,1},{17,9},{25,17},{2,26},{10... | collective-permute-start | bytes 196616 | tf_op jit(solution)/shard_map/ppermute | solution.py:38
  25.5 3.4 %copy-start.22 = (bf16[256,1024]{1,0:T(8,128)(2,1)}, bf16[256,1024]{1,0:T(8,128)(2,1)S(1)}, u32[]{:S(2)}) copy-start(bf16[256,1024]{1,0:T(8,128)(2,1)S(1)} %collective-permute-done.3.rest_1_) | copy-start | bytes 1572868
  28.9 14.7 %copy-start.1 = (bf16[1024,1024]{1,0:T(8,128)(2,1)S(1)}, bf16[1024,1024]{1,0:T(8,128)(2,1)}, u32[]{:S(2)}) copy-start(bf16[1024,1024]{1,0:T(8,128)(2,1)} %x_ref.7) | copy-start | bytes 6291460
  28.9 14.7 %collective-permute-start.4 = (bf16[128,2048]{1,0:T(8,128)(2,1)S(1)}, bf16[128,2048]{1,0:T(8,128)(2,1)S(1)}, u32[]{:S(2)}, u32[]{:S(2)}) collective-permute-start(bf16[128,2048]{1,0:T(8,128)(2,1)S(1)} %copy-done.6), channel_id=1, source_target_pairs={{0,6},{2,4},{4,2},{6,0},{1,7},{3,5},{5,3},{7,1},{8,14},{10,12},{12... | collective-permute-start | bytes 1572872 | tf_op jit(solution)/shard_map/ppermute | solution.py:59
  31.3 55.6 %all-to-all-start = ((bf16[4,2176,128]{2,1,0:T(8,128)(2,1)}), bf16[4,2176,128]{2,1,0:T(8,128)(2,1)}, u32[]{:S(2)}, u32[]{:S(2)}) async-start(bf16[4,2176,128]{2,1,0:T(8,128)(2,1)} %pick_down.1), calls=%async_computation | async-start | bytes 4456448 | tf_op jit(solution)/shard_map/all_to_all | solution.py:487
  43.6 2.2 %copy-start.2 = (bf16[1024,2048]{1,0:T(8,128)(2,1)S(1)}, bf16[1024,2048]{1,0:T(8,128)(2,1)}, u32[]{:S(2)}) copy-start(bf16[1024,2048]{1,0:T(8,128)(2,1)} %w_ref.5) | copy-start | bytes 12582916
  49.4 19.8 %collective-permute-start.5 = (bf16[4,128,2048]{2,1,0:T(8,128)(2,1)S(1)}, bf16[4,128,2048]{2,1,0:T(8,128)(2,1)S(1)}, u32[]{:S(2)}, u32[]{:S(2)}) collective-permute-start(bf16[4,128,2048]{2,1,0:T(8,128)(2,1)S(1)} %bitcast.68), channel_id=1, source_target_pairs={{0,1},{1,0},{2,3},{3,2},{4,5},{5,4},{6,7},{7,6},{8,9},{9,8},{10,11... | collective-permute-start | bytes 6291464 | tf_op jit(solution)/shard_map/ppermute | solution.py:59
  49.4 14.3 %collective-permute-start.6 = (bf16[128,2048]{1,0:T(8,128)(2,1)S(1)}, bf16[128,2048]{1,0:T(8,128)(2,1)S(1)}, u32[]{:S(2)}, u32[]{:S(2)}) collective-permute-start(bf16[128,2048]{1,0:T(8,128)(2,1)S(1)} %copy-done.6), channel_id=1, source_target_pairs={{0,2},{2,0},{4,6},{6,4},{1,3},{3,1},{5,7},{7,5},{8,10},{10,8},{12,... | collective-permute-start | bytes 1572872 | tf_op jit(solution)/shard_map/ppermute | solution.py:59
  51.0 14.0 %collective-permute-start.7 = (bf16[128,2048]{1,0:T(8,128)(2,1)S(1)}, bf16[128,2048]{1,0:T(8,128)(2,1)S(1)}, u32[]{:S(2)}, u32[]{:S(2)}) collective-permute-start(bf16[128,2048]{1,0:T(8,128)(2,1)S(1)} %copy-done.6), channel_id=1, source_target_pairs={{0,4},{2,6},{4,0},{6,2},{1,5},{3,7},{5,1},{7,3},{8,12},{10,14},{12... | collective-permute-start | bytes 1572872 | tf_op jit(solution)/shard_map/ppermute | solution.py:59
  52.5 19.1 %collective-permute-start.8 = (bf16[128,2048]{1,0:T(8,128)(2,1)S(1)}, bf16[128,2048]{1,0:T(8,128)(2,1)S(1)}, u32[]{:S(2)}, u32[]{:S(2)}) collective-permute-start(bf16[128,2048]{1,0:T(8,128)(2,1)S(1)} %copy-done.6), channel_id=1, source_target_pairs={{0,1},{1,0},{2,3},{3,2},{4,5},{5,4},{6,7},{7,6},{8,9},{9,8},{10,11... | collective-permute-start | bytes 1572872 | tf_op jit(solution)/shard_map/ppermute | solution.py:59
  63.8 10.8 %copy-start.8 = (bf16[128,2048]{1,0:T(8,128)(2,1)}, bf16[128,2048]{1,0:T(8,128)(2,1)S(1)}, u32[]{:S(2)}) copy-start(bf16[128,2048]{1,0:T(8,128)(2,1)S(1)} %collective-permute-done.6.rest_1_.rest_3_) | copy-start | bytes 1572868
  63.8 9.3 %collective-permute-start.9 = (bf16[128,2048]{1,0:T(8,128)(2,1)S(1)}, bf16[128,2048]{1,0:T(8,128)(2,1)S(1)}, u32[]{:S(2)}, u32[]{:S(2)}) collective-permute-start(bf16[128,2048]{1,0:T(8,128)(2,1)S(1)} %collective-permute-done.6.rest_1_.rest_3_), channel_id=1, source_target_pairs={{0,1},{1,0},{2,3},{3,2},{4,5},{5,4},{6,7},{7,6},{8,9},{9,8},{10,11... | collective-permute-start | bytes 1572872 | tf_op jit(solution)/shard_map/ppermute | solution.py:59
  65.0 9.6 %copy-start.10 = (bf16[128,2048]{1,0:T(8,128)(2,1)}, bf16[128,2048]{1,0:T(8,128)(2,1)S(1)}, u32[]{:S(2)}) copy-start(bf16[128,2048]{1,0:T(8,128)(2,1)S(1)} %collective-permute-done.7.rest_2_.rest_4_) | copy-start | bytes 1572868
  65.0 9.6 %collective-permute-start.10 = (bf16[128,2048]{1,0:T(8,128)(2,1)S(1)}, bf16[128,2048]{1,0:T(8,128)(2,1)S(1)}, u32[]{:S(2)}, u32[]{:S(2)}) collective-permute-start(bf16[128,2048]{1,0:T(8,128)(2,1)S(1)} %collective-permute-done.7.rest_2_.rest_4_), channel_id=1, source_target_pairs={{0,1},{1,0},{2,3},{3,2},{4,5},{5,4},{6,7},{7,6},{8,9},{9,8},{10,11... | collective-permute-start | bytes 1572872 | tf_op jit(solution)/shard_map/ppermute | solution.py:59
  68.6 6.0 %copy-start.3 = (bf16[1024,2048]{1,0:T(8,128)(2,1)S(1)}, bf16[1024,2048]{1,0:T(8,128)(2,1)}, u32[]{:S(2)}) copy-start(bf16[1024,2048]{1,0:T(8,128)(2,1)} %w_ref.5) | copy-start | bytes 12582916
  68.6 5.9 %collective-permute-start.11 = (bf16[128,2048]{1,0:T(8,128)(2,1)S(1)}, bf16[128,2048]{1,0:T(8,128)(2,1)S(1)}, u32[]{:S(2)}, u32[]{:S(2)}) collective-permute-start(bf16[128,2048]{1,0:T(8,128)(2,1)S(1)} %collective-permute-done.4.rest_3_.rest_5_), channel_id=1, source_target_pairs={{0,1},{1,0},{2,3},{3,2},{4,5},{5,4},{6,7},{7,6},{8,9},{9,8},{10,11... | collective-permute-start | bytes 1572872 | tf_op jit(solution)/shard_map/ppermute | solution.py:59
  71.1 14.8 %collective-permute-start.12 = (bf16[128,2048]{1,0:T(8,128)(2,1)S(1)}, bf16[128,2048]{1,0:T(8,128)(2,1)S(1)}, u32[]{:S(2)}, u32[]{:S(2)}) collective-permute-start(bf16[128,2048]{1,0:T(8,128)(2,1)S(1)} %get-tuple-element.70), channel_id=1, source_target_pairs={{0,2},{2,0},{4,6},{6,4},{1,3},{3,1},{5,7},{7,5},{8,10},{10,8},{12,... | collective-permute-start | bytes 1572872 | tf_op jit(solution)/shard_map/ppermute | solution.py:59
  71.6 9.6 %copy-start.12 = (bf16[128,2048]{1,0:T(8,128)(2,1)}, bf16[128,2048]{1,0:T(8,128)(2,1)S(1)}, u32[]{:S(2)}) copy-start(bf16[128,2048]{1,0:T(8,128)(2,1)S(1)} %collective-permute-done.8.rest_4_.rest_6_) | copy-start | bytes 1572868
  71.6 24.4 %collective-permute-start.13 = (bf16[128,2048]{1,0:T(8,128)(2,1)}, bf16[128,2048]{1,0:T(8,128)(2,1)}, u32[]{:S(2)}, u32[]{:S(2)}) collective-permute-start(bf16[128,2048]{1,0:T(8,128)(2,1)} %get-tuple-element.69), channel_id=1, source_target_pairs={{0,4},{2,6},{4,0},{6,2},{1,5},{3,7},{5,1},{7,3},{8,12},{10,14},{12... | collective-permute-start | bytes 1572872 | tf_op jit(solution)/shard_map/ppermute | solution.py:59
  73.1 8.1 %copy-start.14 = (bf16[128,2048]{1,0:T(8,128)(2,1)}, bf16[128,2048]{1,0:T(8,128)(2,1)S(1)}, u32[]{:S(2)}) copy-start(bf16[128,2048]{1,0:T(8,128)(2,1)S(1)} %collective-permute-done.9.rest_5_.rest_7_) | copy-start | bytes 1572868
  73.1 24.1 %collective-permute-start.14 = (bf16[128,2048]{1,0:T(8,128)(2,1)}, bf16[128,2048]{1,0:T(8,128)(2,1)}, u32[]{:S(2)}, u32[]{:S(2)}) collective-permute-start(bf16[128,2048]{1,0:T(8,128)(2,1)} %get-tuple-element.68), channel_id=1, source_target_pairs={{0,6},{2,4},{4,2},{6,0},{1,7},{3,5},{5,3},{7,1},{8,14},{10,12},{12... | collective-permute-start | bytes 1572872 | tf_op jit(solution)/shard_map/ppermute | solution.py:59
  74.6 6.7 %copy-start.16 = (bf16[128,2048]{1,0:T(8,128)(2,1)}, bf16[128,2048]{1,0:T(8,128)(2,1)S(1)}, u32[]{:S(2)}) copy-start(bf16[128,2048]{1,0:T(8,128)(2,1)S(1)} %collective-permute-done.10.rest_6_.rest_8_) | copy-start | bytes 1572868
  74.6 6.6 %copy-start.18 = (bf16[128,2048]{1,0:T(8,128)(2,1)}, bf16[128,2048]{1,0:T(8,128)(2,1)S(1)}, u32[]{:S(2)}) copy-start(bf16[128,2048]{1,0:T(8,128)(2,1)S(1)} %collective-permute-done.11.rest_7_.rest_9_) | copy-start | bytes 1572868
  81.2 2.3 %copy-start.4 = (f32[1024,1024]{1,0:T(8,128)}, f32[1024,1024]{1,0:T(8,128)S(1)}, u32[]{:S(2)}) copy-start(f32[1024,1024]{1,0:T(8,128)S(1)} %cotangent_product.1.base_ref) | copy-start | bytes 12582916
  83.5 1.0 copy-start.24
  85.8 0.8 copy-start.26
  87.0 21.2 %copy-start.28 = (bf16[128,1024]{1,0:T(8,128)(2,1)S(1)}, bf16[128,1024]{1,0:T(8,128)(2,1)}, u32[]{:S(2)}) copy-start(bf16[128,1024]{1,0:T(8,128)(2,1)} %get-tuple-element.54) | copy-start | bytes 786436
  87.0 28.2 %copy-start.25 = (bf16[256,1024]{1,0:T(8,128)(2,1)S(1)}, bf16[256,1024]{1,0:T(8,128)(2,1)}, u32[]{:S(2)}) copy-start(bf16[256,1024]{1,0:T(8,128)(2,1)} %copy-done.24) | copy-start | bytes 1572868
  87.0 14.0 %collective-permute-start.15 = (bf16[128,1024]{1,0:T(8,128)(2,1)}, bf16[128,1024]{1,0:T(8,128)(2,1)S(1)}, u32[]{:S(2)}, u32[]{:S(2)}) collective-permute-start(bf16[128,1024]{1,0:T(8,128)(2,1)} %get-tuple-element.52), channel_id=1, source_target_pairs={{0,16},{8,24},{16,0},{24,8},{1,17},{9,25},{17,1},{25,9},{2,18},{10... | collective-permute-start | bytes 786440 | tf_op jit(solution)/shard_map/ppermute | solution.py:38
  101.0 22.4 %copy-start.19 = (bf16[128,2048]{1,0:T(8,128)(2,1)S(1)}, bf16[128,2048]{1,0:T(8,128)(2,1)}, u32[]{:S(2)}) copy-start(bf16[128,2048]{1,0:T(8,128)(2,1)} %copy-done.18) | copy-start | bytes 1572868
  103.4 20.0 %copy-start.9 = (bf16[128,2048]{1,0:T(8,128)(2,1)S(1)}, bf16[128,2048]{1,0:T(8,128)(2,1)}, u32[]{:S(2)}) copy-start(bf16[128,2048]{1,0:T(8,128)(2,1)} %copy-done.8) | copy-start | bytes 1572868
  103.4 20.0 %copy-start.11 = (bf16[128,2048]{1,0:T(8,128)(2,1)S(1)}, bf16[128,2048]{1,0:T(8,128)(2,1)}, u32[]{:S(2)}) copy-start(bf16[128,2048]{1,0:T(8,128)(2,1)} %copy-done.10) | copy-start | bytes 1572868
  103.4 20.0 %copy-start.13 = (bf16[128,2048]{1,0:T(8,128)(2,1)S(1)}, bf16[128,2048]{1,0:T(8,128)(2,1)}, u32[]{:S(2)}) copy-start(bf16[128,2048]{1,0:T(8,128)(2,1)} %copy-done.12) | copy-start | bytes 1572868
  103.5 20.0 %copy-start.15 = (bf16[128,2048]{1,0:T(8,128)(2,1)S(1)}, bf16[128,2048]{1,0:T(8,128)(2,1)}, u32[]{:S(2)}) copy-start(bf16[128,2048]{1,0:T(8,128)(2,1)} %copy-done.14) | copy-start | bytes 1572868
  103.5 20.0 %copy-start.17 = (bf16[128,2048]{1,0:T(8,128)(2,1)S(1)}, bf16[128,2048]{1,0:T(8,128)(2,1)}, u32[]{:S(2)}) copy-start(bf16[128,2048]{1,0:T(8,128)(2,1)} %copy-done.16) | copy-start | bytes 1572868
  103.5 4.7 %collective-permute-start.16 = (bf16[4,128,128]{2,1,0:T(8,128)(2,1)S(1)}, bf16[4,128,128]{2,1,0:T(8,128)(2,1)S(1)}, u32[]{:S(2)}, u32[]{:S(2)}) collective-permute-start(bf16[4,128,128]{2,1,0:T(8,128)(2,1)S(1)} %slice_bitcast_fusion.8), channel_id=1, source_target_pairs={{0,1},{1,0},{2,3},{3,2},{4,5},{5,4},{6,7},{7,6},{8,9},{9,8},{10,11... | collective-permute-start | bytes 393224 | tf_op jit(solution)/shard_map/ppermute | solution.py:59
  104.7 7.3 %collective-permute-start.23 = (bf16[4,128,128]{2,1,0:T(8,128)(2,1)S(1)}, bf16[4,128,128]{2,1,0:T(8,128)(2,1)S(1)}, u32[]{:S(2)}, u32[]{:S(2)}) collective-permute-start(bf16[4,128,128]{2,1,0:T(8,128)(2,1)S(1)} %get-tuple-element.73), channel_id=1, source_target_pairs={{0,6},{2,4},{4,2},{6,0},{1,7},{3,5},{5,3},{7,1},{8,14},{10,12},{12... | collective-permute-start | bytes 393224 | tf_op jit(solution)/shard_map/ppermute | solution.py:59
  105.7 8.6 %collective-permute-start.22 = (bf16[4,128,128]{2,1,0:T(8,128)(2,1)S(1)}, bf16[4,128,128]{2,1,0:T(8,128)(2,1)S(1)}, u32[]{:S(2)}, u32[]{:S(2)}) collective-permute-start(bf16[4,128,128]{2,1,0:T(8,128)(2,1)S(1)} %get-tuple-element.73), channel_id=1, source_target_pairs={{0,4},{2,6},{4,0},{6,2},{1,5},{3,7},{5,1},{7,3},{8,12},{10,14},{12... | collective-permute-start | bytes 393224 | tf_op jit(solution)/shard_map/ppermute | solution.py:59
  106.7 8.5 %collective-permute-start.21 = (bf16[4,128,128]{2,1,0:T(8,128)(2,1)S(1)}, bf16[4,128,128]{2,1,0:T(8,128)(2,1)S(1)}, u32[]{:S(2)}, u32[]{:S(2)}) collective-permute-start(bf16[4,128,128]{2,1,0:T(8,128)(2,1)S(1)} %get-tuple-element.73), channel_id=1, source_target_pairs={{0,2},{2,0},{4,6},{6,4},{1,3},{3,1},{5,7},{7,5},{8,10},{10,8},{12,... | collective-permute-start | bytes 393224 | tf_op jit(solution)/shard_map/ppermute | solution.py:59
  108.2 13.1 %collective-permute-start.20 = (bf16[128,1024]{1,0:T(8,128)(2,1)S(1)}, bf16[128,1024]{1,0:T(8,128)(2,1)S(1)}, u32[]{:S(2)}, u32[]{:S(2)}) collective-permute-start(bf16[128,1024]{1,0:T(8,128)(2,1)S(1)} %copy-done.28), channel_id=1, source_target_pairs={{0,16},{8,24},{16,0},{24,8},{1,17},{9,25},{17,1},{25,9},{2,18},{10... | collective-permute-start | bytes 786440 | tf_op jit(solution)/shard_map/ppermute | solution.py:38
  108.3 13.0 %collective-permute-start.17 = (bf16[4,128,128]{2,1,0:T(8,128)(2,1)S(1)}, bf16[4,128,128]{2,1,0:T(8,128)(2,1)S(1)}, u32[]{:S(2)}, u32[]{:S(2)}) collective-permute-start(bf16[4,128,128]{2,1,0:T(8,128)(2,1)S(1)} %fusion.3), channel_id=1, source_target_pairs={{0,2},{2,0},{4,6},{6,4},{1,3},{3,1},{5,7},{7,5},{8,10},{10,8},{12,... | collective-permute-start | bytes 393224 | tf_op jit(solution)/shard_map/ppermute | solution.py:59
  112.0 9.3 %collective-permute-start.18 = (bf16[4,128,128]{2,1,0:T(8,128)(2,1)S(1)}, bf16[4,128,128]{2,1,0:T(8,128)(2,1)S(1)}, u32[]{:S(2)}, u32[]{:S(2)}) collective-permute-start(bf16[4,128,128]{2,1,0:T(8,128)(2,1)S(1)} %fusion.3), channel_id=1, source_target_pairs={{0,4},{2,6},{4,0},{6,2},{1,5},{3,7},{5,1},{7,3},{8,12},{10,14},{12... | collective-permute-start | bytes 393224 | tf_op jit(solution)/shard_map/ppermute | solution.py:59
  114.3 7.0 %collective-permute-start.19 = (bf16[4,128,128]{2,1,0:T(8,128)(2,1)S(1)}, bf16[4,128,128]{2,1,0:T(8,128)(2,1)S(1)}, u32[]{:S(2)}, u32[]{:S(2)}) collective-permute-start(bf16[4,128,128]{2,1,0:T(8,128)(2,1)S(1)} %fusion.3), channel_id=1, source_target_pairs={{0,6},{2,4},{4,2},{6,0},{1,7},{3,5},{5,3},{7,1},{8,14},{10,12},{12... | collective-permute-start | bytes 393224 | tf_op jit(solution)/shard_map/ppermute | solution.py:59
  115.2 31.9 %collective-permute-start.25 = (bf16[256,1024]{1,0:T(8,128)(2,1)S(1)}, bf16[256,1024]{1,0:T(8,128)(2,1)S(1)}, u32[]{:S(2)}, u32[]{:S(2)}) collective-permute-start(bf16[256,1024]{1,0:T(8,128)(2,1)S(1)} %copy-done.25), channel_id=1, source_target_pairs={{0,24},{8,0},{16,8},{24,16},{1,25},{9,1},{17,9},{25,17},{2,26},{10... | collective-permute-start | bytes 1572872 | tf_op jit(solution)/shard_map/ppermute | solution.py:38
  121.3 21.2 %collective-permute-start.24 = (bf16[4,4,128,128]{3,2,1,0:T(8,128)(2,1)S(1)}, bf16[4,4,128,128]{3,2,1,0:T(8,128)(2,1)S(1)}, u32[]{:S(2)}, u32[]{:S(2)}) collective-permute-start(bf16[4,4,128,128]{3,2,1,0:T(8,128)(2,1)S(1)} %pad_maximum_fusion.rest_0_.rest_5_), channel_id=1, source_target_pairs={{0,1},{1,0},{2,3},{3,2},{4,5},{5,4},{6,7},{7,6},{8,9},{9,8},{10,11... | collective-permute-start | bytes 1572872 | tf_op jit(solution)/shard_map/ppermute | solution.py:59
  121.4 2.0 %collective-permute-start.26 = (bf16[4,128,128]{2,1,0:T(8,128)(2,1)S(1)}, bf16[4,128,128]{2,1,0:T(8,128)(2,1)S(1)}, u32[]{:S(2)}, u32[]{:S(2)}) collective-permute-start(bf16[4,128,128]{2,1,0:T(8,128)(2,1)S(1)} %add_convert_fusion.low_ref.rest_0_), channel_id=1, source_target_pairs={{0,1},{1,0},{2,3},{3,2},{4,5},{5,4},{6,7},{7,6},{8,9},{9,8},{10,11... | collective-permute-start | bytes 393224 | tf_op jit(solution)/shard_map/ppermute | solution.py:59
  124.5 15.4 %copy-start.7 = (f32[128,2048]{1,0:T(8,128)S(1)}, f32[128,2048]{1,0:T(8,128)}, u32[]{:S(2)}) copy-start(f32[128,2048]{1,0:T(8,128)} %get-tuple-element.59.rest_0_) | copy-start | bytes 3145732
  124.5 15.4 %copy-start.27 = (bf16[128,2048]{1,0:T(8,128)(2,1)S(1)}, bf16[128,2048]{1,0:T(8,128)(2,1)}, u32[]{:S(2)}) copy-start(bf16[128,2048]{1,0:T(8,128)(2,1)} %copy-done.26) | copy-start | bytes 1572868
  124.6 25.7 %collective-permute-start.27 = (bf16[8,16,256]{2,1,0:T(8,128)(2,1)S(1)}, bf16[8,16,256]{2,1,0:T(8,128)(2,1)S(1)}, u32[]{:S(2)}, u32[]{:S(2)}) collective-permute-start(bf16[8,16,256]{2,1,0:T(8,128)(2,1)S(1)} %get-tuple-element.78), channel_id=1, source_target_pairs={{0,8},{8,16},{16,24},{24,0},{1,9},{9,17},{17,25},{25,1},{2,10},{10... | collective-permute-start | bytes 196616 | tf_op jit(solution)/shard_map/ppermute | solution.py:38
  135.4 14.9 %collective-permute-start.28 = (bf16[8,16,256]{2,1,0:T(8,128)(2,1)S(1)}, bf16[8,16,256]{2,1,0:T(8,128)(2,1)S(1)}, u32[]{:S(2)}, u32[]{:S(2)}) collective-permute-start(bf16[8,16,256]{2,1,0:T(8,128)(2,1)S(1)} %get-tuple-element.77), channel_id=1, source_target_pairs={{0,16},{8,24},{16,0},{24,8},{1,17},{9,25},{17,1},{25,9},{2,18},{10... | collective-permute-start | bytes 196616 | tf_op jit(solution)/shard_map/ppermute | solution.py:38
  138.8 11.5 %collective-permute-start.29 = (bf16[8,16,256]{2,1,0:T(8,128)(2,1)S(1)}, bf16[8,16,256]{2,1,0:T(8,128)(2,1)S(1)}, u32[]{:S(2)}, u32[]{:S(2)}) collective-permute-start(bf16[8,16,256]{2,1,0:T(8,128)(2,1)S(1)} %get-tuple-element.76), channel_id=1, source_target_pairs={{0,24},{8,0},{16,8},{24,16},{1,25},{9,1},{17,9},{25,17},{2,26},{10... | collective-permute-start | bytes 196616 | tf_op jit(solution)/shard_map/ppermute | solution.py:38
  138.8 3.7 %copy-start.5 = (f32[1024,1024]{1,0:T(8,128)S(1)}, f32[1024,1024]{1,0:T(8,128)}, u32[]{:S(2)}) copy-start(f32[1024,1024]{1,0:T(8,128)} %copy-done.4) | copy-start | bytes 12582916
  142.5 4.6 %copy-start.23 = (bf16[256,1024]{1,0:T(8,128)(2,1)S(1)}, bf16[256,1024]{1,0:T(8,128)(2,1)}, u32[]{:S(2)}) copy-start(bf16[256,1024]{1,0:T(8,128)(2,1)} %copy-done.22) | copy-start | bytes 1572868

commit v8 on v7

--- a/solution.py
+++ b/solution.py
@@ -59,72 +59,41 @@
     return lax.ppermute(piece, axis, [(i, partner(i, k, count)) for i in range(count)])
 
 
-def pick_up(at, slot_of, adapter_up, data_count):
-    def kernel(at_ref, up_ref, *rest):
-        out_refs, sems = rest[:data_count], rest[data_count]
-        copies = []
-        for k in range(data_count):
-            data = wrap(at_ref[0] + k, data_count)
-            slot = slot_of(at_ref, data, at_ref[3])
-            copies.append(pltpu.make_async_copy(up_ref.at[slot], out_refs[k], sems.at[k]))
-        for copy in copies:
-            copy.start()
-        for copy in copies:
-            copy.wait()
-
-    return call(
-        kernel,
-        "pick_up",
-        out_shape=(jax.ShapeDtypeStruct(adapter_up.shape[1:], adapter_up.dtype),) * data_count,
-        in_specs=[SMEM, HBM],
-        out_specs=(VMEM,) * data_count,
-        scratch_shapes=[pltpu.SemaphoreType.DMA((data_count,))],
-    )(at, adapter_up)
-
-
-def pick_down(at, slot_of, adapter_down, grad_rows, data_count, blocks_dev):
+def up_rides(adapter_up):
+    return adapter_up.shape[1] % 16 == 0
+
+
+def pick(at, slot_of, adapter_down, adapter_up, data_count, blocks_dev):
     down_rows, ranks = adapter_down.shape[1:]
-    rows = grad_rows.shape[0]
-    first_grad = blocks_dev * down_rows
-
-    def kernel(at_ref, down_ref, grad_ref, out_ref):
+    up_rows, width = adapter_up.shape[1:]
+    first_up = blocks_dev * down_rows
+    rides = up_rides(adapter_up)
+    total = first_up + (up_rows * width // ranks if rides else 0)
+
+    def kernel(at_ref, down_ref, up_ref, out_ref):
         data = pl.program_id(0)
         for block in range(blocks_dev):
             here = slice(block * down_rows, (block + 1) * down_rows)
             out_ref[0, here] = down_ref[slot_of(at_ref, data, block)]
-        out_ref[0, first_grad:] = grad_ref[...]
-
-    return call(
-        kernel,
-        "pick_down",
+        if rides:
+            slot = slot_of(at_ref, data, at_ref[3])
+            for n in range(width // ranks):
+                first = first_up + n * up_rows
+                out_ref[0, first : first + up_rows] = up_ref[slot, :, n * ranks : (n + 1) * ranks]
+
+    return call(
+        kernel,
+        "pick_rows",
         grid=(data_count,),
-        out_shape=pltpu.HBM((data_count, first_grad + rows, ranks), adapter_down.dtype),
+        out_shape=pltpu.HBM((data_count, total, ranks), adapter_down.dtype),
         in_specs=[SMEM, VMEM, VMEM],
-        out_specs=pl.BlockSpec((1, first_grad + rows, ranks), lambda d: (d, 0, 0)),
-    )(at, adapter_down, grad_rows)
-
-
-def features(at, tokens, k, data_count):
-    tok_dev, depth = tokens.shape
-    count = depth // data_count
-    if count % 128:
-        return lax.dynamic_slice_in_dim(tokens, wrap(at[0] + k, data_count) * count, count, 1).T
-
-    def kernel(at_ref, x_ref, out_ref):
-        out_ref[...] = x_ref[...].T
-
-    tile = 256 if tok_dev % 256 == 0 else tok_dev
-    return call(
-        kernel,
-        "features",
-        grid_spec=pltpu.PrefetchScalarGridSpec(
-            num_scalar_prefetch=1,
-            grid=(tok_dev // tile,),
-            in_specs=[pl.BlockSpec((tile, count), lambda n, at: (n, wrap(at[0] + k, data_count)))],
-            out_specs=pl.BlockSpec((count, tile), lambda n, at: (0, n)),
-        ),
-        out_shape=jax.ShapeDtypeStruct((count, tok_dev), tokens.dtype),
-    )(at, tokens)
+        out_specs=pl.BlockSpec((1, total, ranks), lambda d: (d, 0, 0)),
+    )(at, adapter_down, adapter_up)
+
+
+def pick_up(at, slot_of, adapter_up, data_count):
+    slots = jnp.stack([slot_of(at, data, at[3]) for data in range(data_count)])
+    return jnp.take(adapter_up, slots, axis=0)
 
 
 def base_product(at, tokens, weight, first, count):
@@ -243,7 +212,7 @@
                 for k in range(pipe_count):
                     chip = came_from(at_ref[1], k, pipe_count)
                     first = pl.multiple_of((chip * tensor_count + core) * rows, rows)
-                    grad[pl.ds(first, rows)] = grad_refs[s][k, at_ref[0]]
+                    grad[pl.ds(first, rows)] = grad_refs[s][k, 0]
 
         for block in range(tok_dev // BLOCK):
             here = slice(block * BLOCK, (block + 1) * BLOCK)
@@ -269,45 +238,38 @@
 
 
 def grad_down(at, slot_of, slots, x_features, grad_pieces):
-    data_count = len(x_features)
-    down_rows = sum(part.shape[0] for part in x_features[0])
-    tok_dev = x_features[0][0].shape[1]
-    parts = [(k, part) for k in range(data_count) for part in x_features[k]]
+    data_count, down_rows, tok_dev = x_features.shape
     tensor_count = len(grad_pieces)
     pipe_count, _, rows, _ = grad_pieces[0].shape
     blocks_dev = tok_dev // BLOCK
 
-    def kernel(at_ref, *rest):
-        x_refs, rest = rest[: len(parts)], rest[len(parts) :]
+    def kernel(at_ref, x_ref, *rest):
         grad_refs, (out_ref, grad) = rest[:tensor_count], rest[tensor_count:]
         for s in range(tensor_count):
             core = came_from(at_ref[2], s, tensor_count)
             for k in range(pipe_count):
                 chip = came_from(at_ref[1], k, pipe_count)
                 first = pl.multiple_of((chip * tensor_count + core) * rows, rows)
-                for data in range(data_count):
-                    grad[data, pl.ds(first, rows)] = grad_refs[s][k, data]
+                for m in range(data_count):
+                    data = wrap(at_ref[0] - m, data_count)
+                    grad[data, pl.ds(first, rows)] = grad_refs[s][k, m]
         out_ref[...] = jnp.zeros(out_ref.shape, out_ref.dtype)
-        first = 0
-        for (k, part), x_ref in zip(parts, x_refs):
-            data = wrap(at_ref[0] - k, data_count)
-            features_at = slice(first, first + part.shape[0])
-            first = features_at.stop % down_rows
+        for data in range(data_count):
             for block in range(blocks_dev):
                 slot = slot_of(at_ref, data, block)
                 here = slice(block * BLOCK, (block + 1) * BLOCK)
-                out_ref[slot, features_at] += jnp.dot(
-                    x_ref[:, here], grad[data, here], preferred_element_type=jnp.float32
+                out_ref[slot] += jnp.dot(
+                    x_ref[data, :, here], grad[data, here], preferred_element_type=jnp.float32
                 )
 
     return call(
         kernel,
         "grad_down",
-        in_specs=[SMEM] + [VMEM] * (len(parts) + tensor_count),
+        in_specs=[SMEM, VMEM] + [VMEM] * tensor_count,
         out_specs=VMEM,
         out_shape=jax.ShapeDtypeStruct((slots, down_rows, RANKS), jnp.float32),
         scratch_shapes=[pltpu.VMEM((data_count, tok_dev, RANKS), jnp.bfloat16)],
-    )(at, *[part for _, part in parts], *grad_pieces)
+    )(at, x_features, *grad_pieces)
 
 
 def grad_up_pieces(at, low_pieces, cot_pieces, data_count, up_rows):
@@ -392,22 +354,24 @@
     )(at, *pieces)
 
 
-def own_rows(at, up, cotangent):
-    data_count = len(up)
+def own_rows(came, up, cotangent, first_up):
     rows = cotangent.shape[0]
-
-    def kernel(at_ref, cot_ref, *rest):
-        up_refs, (b_ref, grad_ref) = rest[:data_count], rest[data_count:]
-        pieces = []
-        for data in range(data_count):
-            came = wrap(at_ref[0] - data, data_count)
-            piece = up_refs[0][...]
-            for k in range(1, data_count):
-                piece = jnp.where(came == k, up_refs[k][...], piece)
-            pieces.append(piece)
-        b = jnp.concatenate(pieces, axis=0)
-        b_ref[...] = b
-        cot = cot_ref[...]
+    data_count = came.shape[0]
+    up_rows = ADAPTER_RANK // data_count
+
+    def kernel(cot_ref, came_ref, b_ref, grad_ref, tiles, sem):
+        if up is None:
+            copy = pltpu.make_async_copy(came_ref.at[:, pl.ds(first_up, tiles.shape[1])], tiles, sem)
+            copy.start()
+            copy.wait()
+            for data in range(data_count):
+                for n in range(WIDTH // RANKS):
+                    b_ref[
+                        data * up_rows : (data + 1) * up_rows, n * RANKS : (n + 1) * RANKS
+                    ] = tiles[data, n * up_rows : (n + 1) * up_rows]
+        else:
+            b_ref[...] = came_ref[...]
+        cot, b = cot_ref[...], b_ref[...]
         grad_ref[...] = jnp.concatenate(
             [
                 lax.dot_general(cot[:, half], b[:, half], LAST_BOTH, preferred_element_type=jnp.float32)
@@ -416,16 +380,21 @@
             axis=1,
         ).astype(grad_ref.dtype)
 
+    tile_rows = up_rows * WIDTH // RANKS
     return call(
         kernel,
         "own_rows",
-        in_specs=[SMEM, VMEM] + [VMEM] * data_count,
+        in_specs=[VMEM, ANY if up is None else VMEM],
         out_specs=(VMEM, VMEM),
         out_shape=(
             jax.ShapeDtypeStruct((ADAPTER_RANK, WIDTH), jnp.bfloat16),
             jax.ShapeDtypeStruct((rows, RANKS), jnp.bfloat16),
         ),
-    )(at, cotangent, *up)
+        scratch_shapes=[
+            pltpu.VMEM((data_count, tile_rows, RANKS), jnp.bfloat16),
+            pltpu.SemaphoreType.DMA,
+        ],
+    )(cotangent, came if up is None else up)
 
 
 def keys_and_values(at, base_pieces, low_sum, b_own):
@@ -475,23 +444,17 @@
     def slot_of(at_ref, data, block):
         return at_ref[4 + blocks + at_ref[4 + data * blocks_dev + block]]
 
-    x_came = [[features(at, tokens, 0, data_count)]]
-    x_came += [[shift(features(at, tokens, 1, data_count), "dp", 1)]] if data_count > 1 else []
-
-    b_send = pick_up(at, slot_of, adapter_up, data_count)
-    b_came = [b_send[0]] + [shift(b_send[k], "dp", k) for k in range(1, data_count)]
-    b_came, x_came[1:] = lax.optimization_barrier((b_came, x_came[1:]))
-    b_own, grad_rows = own_rows(at, b_came, cotangent)
-
-    a_send = pick_down(at, slot_of, adapter_down, grad_rows, data_count, blocks_dev)
+    a_send = pick(at, slot_of, adapter_down, adapter_up, data_count, blocks_dev)
     a_recv = lax.all_to_all(a_send, "dp", 0, 0, tiled=True)
-
-    cot_send, b_send = lax.optimization_barrier((cotangent, b_send))
-    cot_chips = [cotangent] + [swap(cot_send, "pipe", k) for k in range(1, pipe_count - 1)]
+    up = None
+    if not up_rides(adapter_up):
+        up = lax.all_to_all(pick_up(at, slot_of, adapter_up, data_count), "dp", 0, 0, tiled=True)
+        up = up.reshape(ADAPTER_RANK, WIDTH)
+
     cot_send, a_send = lax.optimization_barrier((cotangent, a_send))
-    cot_chips += [swap(cot_send, "pipe", pipe_count - 1)]
-
-    base_tokens, cot_chips[-1] = lax.optimization_barrier((tokens, cot_chips[-1]))
+    cot_chips = [cotangent] + [swap(cot_send, "pipe", k) for k in range(1, pipe_count)]
+
+    base_tokens, cot_chips = lax.optimization_barrier((tokens, cot_chips))
     tokens_by_group = base_tokens.reshape(pipe_count, tensor_count, rows, feature_count)
     base_send = base_product(at, tokens_by_group, key_value_weight, 1, tensor_count - 1)
     base_came = [swap(base_send[s - 1], "tensor", s) for s in range(1, tensor_count)]
@@ -509,29 +472,28 @@
     input_base = cotangent_product(at, cot_pieces, key_value_weight)
 
     x_tokens, base_chip = lax.optimization_barrier((tokens, base_chip))
-    x_send = [[features(at, x_tokens, k, data_count)] for k in range(2, data_count)]
-    if down_rows % 256 == 0:
-        x_send[:-1] = [jnp.split(whole, 2) for (whole,) in x_send[:-1]]
-    a_recv, x_send, input_base, base_chip_came[:1] = lax.optimization_barrier(
-        (a_recv, x_send, input_base, base_chip_came[:1])
-    )
-    x_came += [[shift(part, "dp", k + 2) for part in parts] for k, parts in enumerate(x_send)]
-
-    grad_data = a_recv[:, blocks_dev * down_rows :]
-    grad_chips = jnp.stack([grad_data] + [swap(grad_data, "pipe", k) for k in range(1, pipe_count)])
+    x_send = x_tokens.T.reshape(data_count, down_rows, tok_dev)
+
+    a_recv, x_send, input_base = lax.optimization_barrier((a_recv, x_send, input_base))
+    b_own, grad_rows = own_rows(a_recv, up, cotangent, blocks_dev * down_rows)
+    grad_data = [grad_rows] + [shift(grad_rows, "dp", k) for k in range(1, data_count)]
+    x_send, grad_data = lax.optimization_barrier((x_send, grad_data))
+    x_recv = lax.all_to_all(x_send, "dp", 0, 0, tiled=True)
+
+    grad_all = jnp.stack(grad_data)
+    grad_chips = jnp.stack([grad_all] + [swap(grad_all, "pipe", k) for k in range(1, pipe_count)])
     grad_pieces = [grad_chips] + [swap(grad_chips, "tensor", s) for s in range(1, tensor_count)]
     input_grad = input_gradient(at, input_base, grad_pieces, a_recv)
 
-    x_first = [parts[0] for parts in x_came[2:-1]]
-    low_down, base_chip_came, x_first = lax.optimization_barrier((a_recv, base_chip_came, x_first))
+    low_down, base_chip_came, grad_data = lax.optimization_barrier(
+        (a_recv, base_chip_came, grad_data)
+    )
     low_part = low_product(at, tokens, low_down, pipe_count, tensor_count)
     low_core = sum(
         [low_part[0].astype(jnp.float32)]
         + [swap(low_part[s], "tensor", s).astype(jnp.float32) for s in range(1, tensor_count)]
     ).astype(jnp.bfloat16)
     low_came = [swap(low_core, "pipe", k) for k in range(1, pipe_count)]
-    x_rest = [parts[1:] for parts in x_came[2:-1]]
-    low_came, x_rest = lax.optimization_barrier((low_came, x_rest))
     low_sum = sum([piece.astype(jnp.float32) for piece in [low_core] + low_came])
     low_sum = low_sum.astype(jnp.bfloat16)
     low_pieces = [low_sum] + [swap(low_sum, "tensor", s) for s in range(1, tensor_count)]
@@ -539,10 +501,9 @@
 
     up_pieces = grad_up_pieces(at, low_pieces, cot_pieces, data_count, up_rows)
     up_came = [up_pieces[0]] + [shift(up_pieces[k], "dp", k) for k in range(1, data_count)]
+    grad_a = grad_down(at, slot_of, slots, x_recv, grad_pieces)
+    up_came, grad_a = lax.optimization_barrier((up_came, grad_a))
     grad_b = grad_up(at, slot_of, slots, up_came)
-
-    x_came[2:-1] = [[part] + rest for part, rest in zip(x_first, x_rest)]
-    grad_a = grad_down(at, slot_of, slots, x_came, grad_pieces)
     return (key_value, input_grad, grad_a, grad_b)
 
 

time: 152 us -> 145 us (0.954)
  starting transfers between devices: 45.5 us -> 37.3 us
  Pallas kernels: 37.9 us -> 29.7 us
  local copies, waits for them, and re-layouts: 7.56 us -> 15.6 us
    ppermute x20, waiting for transfers between devices: 37.5 us -> 56 us  [swap(): lax.ppermute(piece, axis, [(i, partner(i, k, count)) for i in range(count)])]
    ppermute x10 -> x6, waiting for transfers between devices: 19.9 us -> 2.46 us  [shift(): lax.ppermute(piece, axis, [(i, (i + k) % count) for i in range(count)])]
    ppermute x10 -> x6, starting transfers between devices: 25.1 us -> 11.1 us  [shift(): lax.ppermute(piece, axis, [(i, (i + k) % count) for i in range(count)])]
    unnamed x58, local copies, waits for them, and re-layouts: 4.76 us -> 10.8 us
    pallas_call x8 -> x3, Pallas kernels: 11.9 us -> 7.13 us  [the longest x1 4.24 us: grad_down(): call(kernel, 'grad_down', in_specs=[SMEM, VMEM] + [VMEM] * tensor_count,...]
    all_to_all x0 -> x1, starting transfers between devices: none -> 4.53 us  [body(): x_recv = lax.all_to_all(x_send, 'dp', 0, 0, tiled=True)]
    transpose x0 -> x1, local copies, waits for them, and re-layouts: none -> 4.02 us  [body(): x_send = x_tokens.T.reshape(data_count, down_rows, tok_dev)]
    all_to_all x1, starting transfers between devices: 4.49 us -> 6.45 us  [body(): a_recv = lax.all_to_all(a_send, 'dp', 0, 0, tiled=True)]
  transfers between devices with their start and end apart: 31 -> 28, of which waited for: 14 -> 17; matrix products, arithmetic and copies ran while one was open for 3% -> 5% of each run, Pallas kernels for 19% -> 18%
where the time goes in v8:
time: 145 us
  waiting for transfers between devices  58.5 us (40%)
  starting transfers between devices  37.3 us (26%)
  Pallas kernels  29.7 us (20%)
  local copies, waits for them, and re-layouts  15.6 us (11%)
  other arithmetic  2.65 us (2%)
    ppermute x20, waiting for transfers between devices, swap(): lax.ppermute(piece, axis, [(i, partner(i, k, count)) for i in range(count)])  56 us
    ppermute x20, starting transfers between devices, swap(): lax.ppermute(piece, axis, [(i, partner(i, k, count)) for i in range(count)])  15.2 us
    ppermute x6, starting transfers between devices, shift(): lax.ppermute(piece, axis, [(i, (i + k) % count) for i in range(count)])  11.1 us
    unnamed x58, local copies, waits for them, and re-layouts  10.8 us
    pallas_call x2, Pallas kernels, base_product(): call(kernel, 'base_product', grid_spec=pltpu.PrefetchScalarGridSpec(num_s...  7.22 us
    pallas_call x1, Pallas kernels, cotangent_product(): call(kernel, 'cotangent_product', grid=(depth // tile,), in_specs=[SMEM,...  6.52 us
    all_to_all x1, starting transfers between devices, body(): a_recv = lax.all_to_all(a_send, 'dp', 0, 0, tiled=True)  6.45 us
    all_to_all x1, starting transfers between devices, body(): x_recv = lax.all_to_all(x_send, 'dp', 0, 0, tiled=True)  4.53 us
  transfers between devices with their start and end apart: 28, of which 17 were waited for; matrix products, arithmetic and copies ran while one was open for 5% of the time, Pallas kernels for 18%

profile of v8, /device:TPU:0, one launch (start us, length us, event | category | flops | bytes accessed | tf_op | source)
XLA Modules:
  0.0 144.8 jit_solution(15855134952394576456)
XLA Ops:
  0.6 0.8 concatenate.3.at_ref
  1.4 1.4 copy-done.25
  2.8 1.4 copy-done.26
  4.2 2.5 %pick_rows.1 = bf16[4,2304,128]{2,1,0:T(8,128)(2,1)} custom-call(s32[60]{0:T(128)S(1)} %concatenate.3.at_ref, bf16[24,256,128]{2,1,0:T(8,128)(2,1)S(1)} %copy-done.25, bf16[24,16,2048]{2,1,0:T(8,128)(2,1)S(1)} %copy-done.26), custom_call_target="tpu_custom_call" | custom-call | flops 1024 | bytes 1024 | tf_op jit(solution)/shard_map/pick_rows/pallas_call | solution.py:84
  6.7 6.4 %all-to-all-start = ((bf16[4,2304,128]{2,1,0:T(8,128)(2,1)}), bf16[4,2304,128]{2,1,0:T(8,128)(2,1)S(1)}, u32[]{:S(2)}, u32[]{:S(2)}) async-start(bf16[4,2304,128]{2,1,0:T(8,128)(2,1)} %pick_rows.1), calls=%async_computation | async-start | bytes 4718592 | tf_op jit(solution)/shard_map/all_to_all | solution.py:448
  13.2 1.5 %collective-permute-start = (bf16[128,2048]{1,0:T(8,128)(2,1)S(1)}, bf16[128,2048]{1,0:T(8,128)(2,1)S(1)}, u32[]{:S(2)}, u32[]{:S(2)}) collective-permute-start(bf16[128,2048]{1,0:T(8,128)(2,1)S(1)} %copy-done.7), channel_id=1, source_target_pairs={{0,2},{2,0},{4,6},{6,4},{1,3},{3,1},{5,7},{7,5},{8,10},{10,8},{12,... | collective-permute-start | bytes 1572872 | tf_op jit(solution)/shard_map/ppermute | solution.py:59
  14.6 1.5 %collective-permute-start.1 = (bf16[128,2048]{1,0:T(8,128)(2,1)S(1)}, bf16[128,2048]{1,0:T(8,128)(2,1)S(1)}, u32[]{:S(2)}, u32[]{:S(2)}) collective-permute-start(bf16[128,2048]{1,0:T(8,128)(2,1)S(1)} %copy-done.7), channel_id=1, source_target_pairs={{0,4},{2,6},{4,0},{6,2},{1,5},{3,7},{5,1},{7,3},{8,12},{10,14},{12... | collective-permute-start | bytes 1572872 | tf_op jit(solution)/shard_map/ppermute | solution.py:59
  16.2 0.5 collective-permute-start.2
  16.6 11.4 %collective-permute-done.rest_1_.rest_3_ = bf16[128,2048]{1,0:T(8,128)(2,1)S(1)} collective-permute-done((bf16[128,2048]{1,0:T(8,128)(2,1)S(1)}, bf16[128,2048]{1,0:T(8,128)(2,1)S(1)}, u32[]{:S(2)}, u32[]{:S(2)}) %collective-permute-start) | collective-permute-done | bytes 524320 | tf_op jit(solution)/shard_map/ppermute | solution.py:59
  28.0 11.0 %collective-permute-done.1.rest_2_.rest_4_ = bf16[128,2048]{1,0:T(8,128)(2,1)S(1)} collective-permute-done((bf16[128,2048]{1,0:T(8,128)(2,1)S(1)}, bf16[128,2048]{1,0:T(8,128)(2,1)S(1)}, u32[]{:S(2)}, u32[]{:S(2)}) %collective-permute-start.1) | collective-permute-done | bytes 524320 | tf_op jit(solution)/shard_map/ppermute | solution.py:59
  39.0 2.6 %copy-done = bf16[1024,2048]{1,0:T(8,128)(2,1)S(1)} copy-done((bf16[1024,2048]{1,0:T(8,128)(2,1)S(1)}, bf16[1024,2048]{1,0:T(8,128)(2,1)}, u32[]{:S(2)}) %copy-start) | copy-done | bytes 4194328
  41.6 1.6 %copy-done.2 = bf16[1024,1024]{1,0:T(8,128)(2,1)S(1)} copy-done((bf16[1024,1024]{1,0:T(8,128)(2,1)S(1)}, bf16[1024,1024]{1,0:T(8,128)(2,1)}, u32[]{:S(2)}) %copy-start.2) | copy-done | bytes 2097176
  43.1 3.6 %base_product.3 = bf16[1,4,128,2048]{3,2,1,0:T(8,128)(2,1)S(1)} custom-call(s32[60]{0:T(128)S(1)} %concatenate.3.at_ref, bf16[4,2,128,1024]{3,2,1,0:T(8,128)(2,1)S(1)} %bitcast.73, bf16[1024,2048]{1,0:T(8,128)(2,1)S(1)} %copy-done), custom_call_target="tpu_custom_call" | custom-call | flops 1024 | bytes 1024 | tf_op jit(solution)/shard_map/base_product/pallas_call | solution.py:109
  46.8 0.5 collective-permute-start.4
  47.3 0.1 collective-permute-start.5
  47.4 0.4 collective-permute-start.6
  47.9 0.1 collective-permute-start.7
  47.9 3.6 %base_product.2 = bf16[1,4,128,2048]{3,2,1,0:T(8,128)(2,1)S(1)} custom-call(s32[60]{0:T(128)S(1)} %concatenate.3.at_ref, bf16[4,2,128,1024]{3,2,1,0:T(8,128)(2,1)S(1)} %bitcast.74, bf16[1024,2048]{1,0:T(8,128)(2,1)S(1)} %copy-done), custom_call_target="tpu_custom_call" | custom-call | flops 1024 | bytes 1024 | tf_op jit(solution)/shard_map/base_product/pallas_call | solution.py:109
  51.6 0.2 collective-permute-done.4.rest_4_.rest_6_
  51.7 0.7 collective-permute-done.5.rest_5_.rest_7_
  52.5 0.7 collective-permute-done.6.rest_6_.rest_8_
  53.2 0.7 collective-permute-done.7.rest_7_.rest_9_
  54.0 6.5 %cotangent_product.1.base_ref = f32[1024,1024]{1,0:T(8,128)S(1)} custom-call(s32[60]{0:T(128)S(1)} %concatenate.3.at_ref, bf16[1024,2048]{1,0:T(8,128)(2,1)S(1)} %copy-done.1, bf16[128,2048]{1,0:T(8,128)(2,1)S(1)} %copy-done.7, bf16[128,2048]{1,0:T(8,128)(2,1)S(1)} %collective-permute-done.rest_1_.rest_3_, ...), custom_call_target="tpu_custom_call" | custom-call | flops 1024 | bytes 1024 | tf_op jit(solution)/shard_map/cotangent_product/pallas_call | solution.py:182
  60.6 2.4 %fusion = (bf16[128,2048]{1,0:T(8,128)(2,1)}, bf16[128,2048]{1,0:T(8,128)(2,1)}, bf16[128,2048]{1,0:T(8,128)(2,1)}, f32[128,2048]{1,0:T(8,128)}) fusion(bf16[4,128,2048]{2,1,0:T(8,128)(2,1)S(1)} %collective-permute-done.3, bf16[1,4,128,2048]{3,2,1,0:T(8,128)(2,1)S(1)} %base_product.2), kind=kLoop, calls=%fused_computation.1 | loop fusion | flops 3932160 | bytes 6815744 | tf_op jit(solution)/shard_map/convert_element_type | solution.py:466
  63.1 0.3 copy-done.5
  63.4 4.0 %copy.11 = bf16[1024,1024]{1,0:T(8,128)(2,1)} copy(bf16[1024,1024]{0,1:T(8,128)(2,1)} %bitcast.72) | data formatting | bytes 4194304 | tf_op jit(solution)/shard_map/transpose | solution.py:475
  67.4 0.4 own_rows.1
  67.8 1.8 %collective-permute-start.11 = (bf16[128,128]{1,0:T(8,128)(2,1)S(1)}, bf16[128,128]{1,0:T(8,128)(2,1)S(1)}, u32[]{:S(2)}, u32[]{:S(2)}) collective-permute-start(bf16[128,128]{1,0:T(8,128)(2,1)S(1)} %get-tuple-element.41), channel_id=1, source_target_pairs={{0,8},{8,16},{16,24},{24,0},{1,9},{9,17},{17,25},{25,1},{2,10},{10... | collective-permute-start | bytes 98312 | tf_op jit(solution)/shard_map/ppermute | solution.py:38
  69.6 2.4 %collective-permute-start.12 = (bf16[128,128]{1,0:T(8,128)(2,1)S(1)}, bf16[128,128]{1,0:T(8,128)(2,1)S(1)}, u32[]{:S(2)}, u32[]{:S(2)}) collective-permute-start(bf16[128,128]{1,0:T(8,128)(2,1)S(1)} %get-tuple-element.41), channel_id=1, source_target_pairs={{0,16},{8,24},{16,0},{24,8},{1,17},{9,25},{17,1},{25,9},{2,18},{10... | collective-permute-start | bytes 98312 | tf_op jit(solution)/shard_map/ppermute | solution.py:38
  72.0 1.5 %collective-permute-start.13 = (bf16[128,128]{1,0:T(8,128)(2,1)S(1)}, bf16[128,128]{1,0:T(8,128)(2,1)S(1)}, u32[]{:S(2)}, u32[]{:S(2)}) collective-permute-start(bf16[128,128]{1,0:T(8,128)(2,1)S(1)} %get-tuple-element.41), channel_id=1, source_target_pairs={{0,24},{8,0},{16,8},{24,16},{1,25},{9,1},{17,9},{25,17},{2,26},{10... | collective-permute-start | bytes 98312 | tf_op jit(solution)/shard_map/ppermute | solution.py:38
  73.4 0.2 collective-permute-done.11
  73.7 1.2 collective-permute-done.12
  74.9 1.0 collective-permute-done.13
  75.9 4.5 %all-to-all-start.1 = ((bf16[4,256,1024]{2,1,0:T(8,128)(2,1)}), bf16[4,256,1024]{2,1,0:T(8,128)(2,1)}, u32[]{:S(2)}, u32[]{:S(2)}) async-start(bf16[4,256,1024]{2,1,0:T(8,128)(2,1)} %bitcast.77), calls=%async_computation.1 | async-start | bytes 4194304 | tf_op jit(solution)/shard_map/all_to_all | solution.py:481
  80.4 1.1 collective-permute-start.8
  81.5 1.0 collective-permute-start.9
  82.5 1.4 collective-permute-start.10
  83.9 11.6 %collective-permute-done.8.rest_1_ = bf16[128,2048]{1,0:T(8,128)(2,1)S(1)} collective-permute-done((bf16[128,2048]{1,0:T(8,128)(2,1)}, bf16[128,2048]{1,0:T(8,128)(2,1)S(1)}, u32[]{:S(2)}, u32[]{:S(2)}) %collective-permute-start.8) | collective-permute-done | bytes 524320 | tf_op jit(solution)/shard_map/ppermute | solution.py:59
  95.5 8.6 %collective-permute-done.9.rest_2_ = bf16[128,2048]{1,0:T(8,128)(2,1)S(1)} collective-permute-done((bf16[128,2048]{1,0:T(8,128)(2,1)}, bf16[128,2048]{1,0:T(8,128)(2,1)S(1)}, u32[]{:S(2)}, u32[]{:S(2)}) %collective-permute-start.9) | collective-permute-done | bytes 524320 | tf_op jit(solution)/shard_map/ppermute | solution.py:59
  104.1 1.5 %collective-permute-done.10.rest_3_ = bf16[128,2048]{1,0:T(8,128)(2,1)S(1)} collective-permute-done((bf16[128,2048]{1,0:T(8,128)(2,1)}, bf16[128,2048]{1,0:T(8,128)(2,1)S(1)}, u32[]{:S(2)}, u32[]{:S(2)}) %collective-permute-start.10) | collective-permute-done | bytes 524320 | tf_op jit(solution)/shard_map/ppermute | solution.py:59
  105.6 1.6 %copy-done.4 = bf16[1024,1024]{1,0:T(8,128)(2,1)S(1)} copy-done((bf16[1024,1024]{1,0:T(8,128)(2,1)S(1)}, bf16[1024,1024]{1,0:T(8,128)(2,1)}, u32[]{:S(2)}) %copy-start.4) | copy-done | bytes 2097176
  107.2 1.3 low_product.1
  108.7 1.8 %collective-permute-start.20 = (bf16[4,128,128]{2,1,0:T(8,128)(2,1)S(1)}, bf16[4,128,128]{2,1,0:T(8,128)(2,1)S(1)}, u32[]{:S(2)}, u32[]{:S(2)}) collective-permute-start(bf16[4,128,128]{2,1,0:T(8,128)(2,1)S(1)} %get-tuple-element.67), channel_id=1, source_target_pairs={{0,6},{2,4},{4,2},{6,0},{1,7},{3,5},{5,3},{7,1},{8,14},{10,12},{12... | collective-permute-start | bytes 393224 | tf_op jit(solution)/shard_map/ppermute | solution.py:59
  110.5 0.5 collective-permute-start.19
  111.0 1.2 collective-permute-start.18
  112.3 1.8 %collective-permute-start.17 = (bf16[4,128,128]{2,1,0:T(8,128)(2,1)S(1)}, bf16[4,128,128]{2,1,0:T(8,128)(2,1)S(1)}, u32[]{:S(2)}, u32[]{:S(2)}) collective-permute-start(bf16[4,128,128]{2,1,0:T(8,128)(2,1)S(1)} %fusion.3), channel_id=1, source_target_pairs={{0,6},{2,4},{4,2},{6,0},{1,7},{3,5},{5,3},{7,1},{8,14},{10,12},{12... | collective-permute-start | bytes 393224 | tf_op jit(solution)/shard_map/ppermute | solution.py:59
  114.1 0.5 collective-permute-start.16
  114.6 1.4 collective-permute-done.20
  116.0 0.8 collective-permute-start.15
  116.8 2.0 %collective-permute-done.19 = bf16[4,128,128]{2,1,0:T(8,128)(2,1)S(1)} collective-permute-done((bf16[4,128,128]{2,1,0:T(8,128)(2,1)S(1)}, bf16[4,128,128]{2,1,0:T(8,128)(2,1)S(1)}, u32[]{:S(2)}, u32[]{:S(2)}) %collective-permute-start.19) | collective-permute-done | bytes 131104 | tf_op jit(solution)/shard_map/ppermute | solution.py:59
  119.0 2.7 %collective-permute-done.17 = bf16[4,128,128]{2,1,0:T(8,128)(2,1)S(1)} collective-permute-done((bf16[4,128,128]{2,1,0:T(8,128)(2,1)S(1)}, bf16[4,128,128]{2,1,0:T(8,128)(2,1)S(1)}, u32[]{:S(2)}, u32[]{:S(2)}) %collective-permute-start.17) | collective-permute-done | bytes 131104 | tf_op jit(solution)/shard_map/ppermute | solution.py:59
  121.6 2.3 %collective-permute-done.16 = bf16[4,128,128]{2,1,0:T(8,128)(2,1)S(1)} collective-permute-done((bf16[4,128,128]{2,1,0:T(8,128)(2,1)S(1)}, bf16[4,128,128]{2,1,0:T(8,128)(2,1)S(1)}, u32[]{:S(2)}, u32[]{:S(2)}) %collective-permute-start.16) | collective-permute-done | bytes 131104 | tf_op jit(solution)/shard_map/ppermute | solution.py:59
  124.1 0.2 collective-permute-start.22
  124.3 1.2 collective-permute-done.22.rest_1_
  125.5 1.1 grad_up_pieces.1
  126.6 1.7 %collective-permute-start.23 = (bf16[8,16,256]{2,1,0:T(8,128)(2,1)S(1)}, bf16[8,16,256]{2,1,0:T(8,128)(2,1)S(1)}, u32[]{:S(2)}, u32[]{:S(2)}) collective-permute-start(bf16[8,16,256]{2,1,0:T(8,128)(2,1)S(1)} %get-tuple-element.64), channel_id=1, source_target_pairs={{0,8},{8,16},{16,24},{24,0},{1,9},{9,17},{17,25},{25,1},{2,10},{10... | collective-permute-start | bytes 196616 | tf_op jit(solution)/shard_map/ppermute | solution.py:38
  128.3 2.4 %collective-permute-start.24 = (bf16[8,16,256]{2,1,0:T(8,128)(2,1)S(1)}, bf16[8,16,256]{2,1,0:T(8,128)(2,1)S(1)}, u32[]{:S(2)}, u32[]{:S(2)}) collective-permute-start(bf16[8,16,256]{2,1,0:T(8,128)(2,1)S(1)} %get-tuple-element.63), channel_id=1, source_target_pairs={{0,16},{8,24},{16,0},{24,8},{1,17},{9,25},{17,1},{25,9},{2,18},{10... | collective-permute-start | bytes 196616 | tf_op jit(solution)/shard_map/ppermute | solution.py:38
  130.7 1.5 %collective-permute-start.25 = (bf16[8,16,256]{2,1,0:T(8,128)(2,1)S(1)}, bf16[8,16,256]{2,1,0:T(8,128)(2,1)S(1)}, u32[]{:S(2)}, u32[]{:S(2)}) collective-permute-start(bf16[8,16,256]{2,1,0:T(8,128)(2,1)S(1)} %get-tuple-element.62), channel_id=1, source_target_pairs={{0,24},{8,0},{16,8},{24,16},{1,25},{9,1},{17,9},{25,17},{2,26},{10... | collective-permute-start | bytes 196616 | tf_op jit(solution)/shard_map/ppermute | solution.py:38
  132.2 1.7 %keys_and_values.1 = bf16[128,2048]{1,0:T(8,128)(2,1)} custom-call(s32[60]{0:T(128)S(1)} %concatenate.3.at_ref, bf16[4,128,128]{2,1,0:T(8,128)(2,1)S(1)} %add_convert_fusion.low_ref.rest_0_, bf16[64,2048]{1,0:T(8,128)(2,1)S(1)} %copy-done.28, f32[128,2048]{1,0:T(8,128)S(1)} %copy-done.8, bf16[128,2048]{1,0:T(8,128)(2,1)S(1)} %collective-permute-done.8.rest_1_, ...), custom_call_target="tpu_custom_call" | custom-call | flops 1024 | bytes 1024 | tf_op jit(solution)/shard_map/keys_and_values/pallas_call | solution.py:414
  133.9 3.3 %input_gradient.1 = bf16[1024,1024]{1,0:T(8,128)(2,1)} custom-call(s32[60]{0:T(128)S(1)} %concatenate.3.at_ref, f32[1024,1024]{1,0:T(8,128)S(1)} %copy-done.6, bf16[4,2304,128]{2,1,0:T(8,128)(2,1)S(1)} %all-to-all-done.came_ref.a_ref, bf16[4,4,128,128]{3,2,1,0:T(8,128)(2,1)S(1)} %pad_maximum_fusion.rest_0_, ...), custom_call_target="tpu_custom_call" | custom-call | flops 1024 | bytes 1024 | tf_op jit(solution)/shard_map/input_gradient/pallas_call | solution.py:224
  137.2 0.8 copy-done.23
  138.0 1.0 copy-done.24
  139.1 4.2 %grad_down.1 = f32[24,256,128]{2,1,0:T(8,128)} custom-call(s32[60]{0:T(128)S(1)} %concatenate.3.at_ref, bf16[4,256,1024]{2,1,0:T(8,128)(2,1)} %all-to-all-done.1.x_ref, bf16[4,4,128,128]{3,2,1,0:T(8,128)(2,1)S(1)} %pad_maximum_fusion.rest_0_, bf16[4,4,128,128]{3,2,1,0:T(8,128)(2,1)S(1)} %copy-done.24), custom_call_target="tpu_custom_call" | custom-call | flops 1024 | bytes 1024 | tf_op jit(solution)/shard_map/grad_down/pallas_call | solution.py:265
  143.3 1.5 %grad_up.1 = f32[24,16,256]{2,1,0:T(8,128)} custom-call(s32[60]{0:T(128)S(1)} %concatenate.3.at_ref, bf16[8,16,256]{2,1,0:T(8,128)(2,1)S(1)} %get-tuple-element.54.rest_0_, bf16[8,16,256]{2,1,0:T(8,128)(2,1)S(1)} %collective-permute-done.23.rest_1_, bf16[8,16,256]{2,1,0:T(8,128)(2,1)S(1)} %collective-permute-done.24.rest_2_, ...), custom_call_target="tpu_custom_call" | custom-call | flops 1024 | bytes 1024 | tf_op jit(solution)/shard_map/grad_up/pallas_call | solution.py:348
  (70 shorter events, 0.6 us)
Async XLA Ops:
  1.4 1.4 copy-start.25
  2.8 1.4 copy-start.26
  6.7 6.5 %copy-start.7 = (bf16[128,2048]{1,0:T(8,128)(2,1)S(1)}, bf16[128,2048]{1,0:T(8,128)(2,1)}, u32[]{:S(2)}) copy-start(bf16[128,2048]{1,0:T(8,128)(2,1)} %rest_2_) | copy-start | bytes 1572868
  6.7 60.7 %all-to-all-start = ((bf16[4,2304,128]{2,1,0:T(8,128)(2,1)}), bf16[4,2304,128]{2,1,0:T(8,128)(2,1)S(1)}, u32[]{:S(2)}, u32[]{:S(2)}) async-start(bf16[4,2304,128]{2,1,0:T(8,128)(2,1)} %pick_rows.1), calls=%async_computation | async-start | bytes 4718592 | tf_op jit(solution)/shard_map/all_to_all | solution.py:448
  13.2 14.8 %collective-permute-start = (bf16[128,2048]{1,0:T(8,128)(2,1)S(1)}, bf16[128,2048]{1,0:T(8,128)(2,1)S(1)}, u32[]{:S(2)}, u32[]{:S(2)}) collective-permute-start(bf16[128,2048]{1,0:T(8,128)(2,1)S(1)} %copy-done.7), channel_id=1, source_target_pairs={{0,2},{2,0},{4,6},{6,4},{1,3},{3,1},{5,7},{7,5},{8,10},{10,8},{12,... | collective-permute-start | bytes 1572872 | tf_op jit(solution)/shard_map/ppermute | solution.py:59
  14.6 24.3 %collective-permute-start.1 = (bf16[128,2048]{1,0:T(8,128)(2,1)S(1)}, bf16[128,2048]{1,0:T(8,128)(2,1)S(1)}, u32[]{:S(2)}, u32[]{:S(2)}) collective-permute-start(bf16[128,2048]{1,0:T(8,128)(2,1)S(1)} %copy-done.7), channel_id=1, source_target_pairs={{0,4},{2,6},{4,0},{6,2},{1,5},{3,7},{5,1},{7,3},{8,12},{10,14},{12... | collective-permute-start | bytes 1572872 | tf_op jit(solution)/shard_map/ppermute | solution.py:59
  16.2 22.8 %collective-permute-start.2 = (bf16[128,2048]{1,0:T(8,128)(2,1)S(1)}, bf16[128,2048]{1,0:T(8,128)(2,1)S(1)}, u32[]{:S(2)}, u32[]{:S(2)}) collective-permute-start(bf16[128,2048]{1,0:T(8,128)(2,1)S(1)} %copy-done.7), channel_id=1, source_target_pairs={{0,6},{2,4},{4,2},{6,0},{1,7},{3,5},{5,3},{7,1},{8,14},{10,12},{12... | collective-permute-start | bytes 1572872 | tf_op jit(solution)/shard_map/ppermute | solution.py:59
  28.0 26.0 %copy-start.9 = (bf16[128,2048]{1,0:T(8,128)(2,1)}, bf16[128,2048]{1,0:T(8,128)(2,1)S(1)}, u32[]{:S(2)}) copy-start(bf16[128,2048]{1,0:T(8,128)(2,1)S(1)} %collective-permute-done.rest_1_.rest_3_) | copy-start | bytes 1572868
  39.0 15.0 %copy-start.11 = (bf16[128,2048]{1,0:T(8,128)(2,1)}, bf16[128,2048]{1,0:T(8,128)(2,1)S(1)}, u32[]{:S(2)}) copy-start(bf16[128,2048]{1,0:T(8,128)(2,1)S(1)} %collective-permute-done.1.rest_2_.rest_4_) | copy-start | bytes 1572868
  39.0 15.0 %copy-start.13 = (bf16[128,2048]{1,0:T(8,128)(2,1)}, bf16[128,2048]{1,0:T(8,128)(2,1)S(1)}, u32[]{:S(2)}) copy-start(bf16[128,2048]{1,0:T(8,128)(2,1)S(1)} %collective-permute-done.2.rest_3_.rest_5_) | copy-start | bytes 1572868
  39.0 2.6 %copy-start = (bf16[1024,2048]{1,0:T(8,128)(2,1)S(1)}, bf16[1024,2048]{1,0:T(8,128)(2,1)}, u32[]{:S(2)}) copy-start(bf16[1024,2048]{1,0:T(8,128)(2,1)} %w_ref.5) | copy-start | bytes 12582916
  41.6 1.6 %copy-start.2 = (bf16[1024,1024]{1,0:T(8,128)(2,1)S(1)}, bf16[1024,1024]{1,0:T(8,128)(2,1)}, u32[]{:S(2)}) copy-start(bf16[1024,1024]{1,0:T(8,128)(2,1)} %x_ref.1) | copy-start | bytes 6291460
  43.1 4.8 %copy-start.3 = (bf16[1024,1024]{1,0:T(8,128)(2,1)S(1)}, bf16[1024,1024]{1,0:T(8,128)(2,1)}, u32[]{:S(2)}) copy-start(bf16[1024,1024]{1,0:T(8,128)(2,1)} %x_ref.1) | copy-start | bytes 6291460
  46.8 13.8 %collective-permute-start.3 = (bf16[4,128,2048]{2,1,0:T(8,128)(2,1)S(1)}, bf16[4,128,2048]{2,1,0:T(8,128)(2,1)S(1)}, u32[]{:S(2)}, u32[]{:S(2)}) collective-permute-start(bf16[4,128,2048]{2,1,0:T(8,128)(2,1)S(1)} %bitcast.75), channel_id=1, source_target_pairs={{0,1},{1,0},{2,3},{3,2},{4,5},{5,4},{6,7},{7,6},{8,9},{9,8},{10,11... | collective-permute-start | bytes 6291464 | tf_op jit(solution)/shard_map/ppermute | solution.py:59
  46.8 4.9 %collective-permute-start.4 = (bf16[128,2048]{1,0:T(8,128)(2,1)S(1)}, bf16[128,2048]{1,0:T(8,128)(2,1)S(1)}, u32[]{:S(2)}, u32[]{:S(2)}) collective-permute-start(bf16[128,2048]{1,0:T(8,128)(2,1)S(1)} %copy-done.7), channel_id=1, source_target_pairs={{0,1},{1,0},{2,3},{3,2},{4,5},{5,4},{6,7},{7,6},{8,9},{9,8},{10,11... | collective-permute-start | bytes 1572872 | tf_op jit(solution)/shard_map/ppermute | solution.py:59
  47.3 5.1 %collective-permute-start.5 = (bf16[128,2048]{1,0:T(8,128)(2,1)S(1)}, bf16[128,2048]{1,0:T(8,128)(2,1)S(1)}, u32[]{:S(2)}, u32[]{:S(2)}) collective-permute-start(bf16[128,2048]{1,0:T(8,128)(2,1)S(1)} %collective-permute-done.rest_1_.rest_3_), channel_id=1, source_target_pairs={{0,1},{1,0},{2,3},{3,2},{4,5},{5,4},{6,7},{7,6},{8,9},{9,8},{10,11... | collective-permute-start | bytes 1572872 | tf_op jit(solution)/shard_map/ppermute | solution.py:59
  47.4 5.8 %collective-permute-start.6 = (bf16[128,2048]{1,0:T(8,128)(2,1)S(1)}, bf16[128,2048]{1,0:T(8,128)(2,1)S(1)}, u32[]{:S(2)}, u32[]{:S(2)}) collective-permute-start(bf16[128,2048]{1,0:T(8,128)(2,1)S(1)} %collective-permute-done.1.rest_2_.rest_4_), channel_id=1, source_target_pairs={{0,1},{1,0},{2,3},{3,2},{4,5},{5,4},{6,7},{7,6},{8,9},{9,8},{10,11... | collective-permute-start | bytes 1572872 | tf_op jit(solution)/shard_map/ppermute | solution.py:59
  47.9 6.1 %collective-permute-start.7 = (bf16[128,2048]{1,0:T(8,128)(2,1)S(1)}, bf16[128,2048]{1,0:T(8,128)(2,1)S(1)}, u32[]{:S(2)}, u32[]{:S(2)}) collective-permute-start(bf16[128,2048]{1,0:T(8,128)(2,1)S(1)} %collective-permute-done.2.rest_3_.rest_5_), channel_id=1, source_target_pairs={{0,1},{1,0},{2,3},{3,2},{4,5},{5,4},{6,7},{7,6},{8,9},{9,8},{10,11... | collective-permute-start | bytes 1572872 | tf_op jit(solution)/shard_map/ppermute | solution.py:59
  47.9 6.1 %copy-start.1 = (bf16[1024,2048]{1,0:T(8,128)(2,1)S(1)}, bf16[1024,2048]{1,0:T(8,128)(2,1)}, u32[]{:S(2)}) copy-start(bf16[1024,2048]{1,0:T(8,128)(2,1)} %w_ref.5) | copy-start | bytes 12582916
  51.7 8.8 %copy-start.15 = (bf16[128,2048]{1,0:T(8,128)(2,1)}, bf16[128,2048]{1,0:T(8,128)(2,1)S(1)}, u32[]{:S(2)}) copy-start(bf16[128,2048]{1,0:T(8,128)(2,1)S(1)} %collective-permute-done.4.rest_4_.rest_6_) | copy-start | bytes 1572868
  52.5 8.1 %copy-start.17 = (bf16[128,2048]{1,0:T(8,128)(2,1)}, bf16[128,2048]{1,0:T(8,128)(2,1)S(1)}, u32[]{:S(2)}) copy-start(bf16[128,2048]{1,0:T(8,128)(2,1)S(1)} %collective-permute-done.5.rest_5_.rest_7_) | copy-start | bytes 1572868
  53.2 7.3 %copy-start.19 = (bf16[128,2048]{1,0:T(8,128)(2,1)}, bf16[128,2048]{1,0:T(8,128)(2,1)S(1)}, u32[]{:S(2)}) copy-start(bf16[128,2048]{1,0:T(8,128)(2,1)S(1)} %collective-permute-done.6.rest_6_.rest_8_) | copy-start | bytes 1572868
  54.0 6.6 %copy-start.21 = (bf16[128,2048]{1,0:T(8,128)(2,1)}, bf16[128,2048]{1,0:T(8,128)(2,1)S(1)}, u32[]{:S(2)}) copy-start(bf16[128,2048]{1,0:T(8,128)(2,1)S(1)} %collective-permute-done.7.rest_7_.rest_9_) | copy-start | bytes 1572868
  60.6 2.8 %copy-start.5 = (f32[1024,1024]{1,0:T(8,128)}, f32[1024,1024]{1,0:T(8,128)S(1)}, u32[]{:S(2)}) copy-start(f32[1024,1024]{1,0:T(8,128)S(1)} %cotangent_product.1.base_ref) | copy-start | bytes 12582916
  67.8 8.1 %copy-start.27 = (bf16[64,2048]{1,0:T(8,128)(2,1)}, bf16[64,2048]{1,0:T(8,128)(2,1)S(1)}, u32[]{:S(2)}) copy-start(bf16[64,2048]{1,0:T(8,128)(2,1)S(1)} %get-tuple-element.46.b_ref) | copy-start | bytes 786436
  67.8 5.8 %collective-permute-start.11 = (bf16[128,128]{1,0:T(8,128)(2,1)S(1)}, bf16[128,128]{1,0:T(8,128)(2,1)S(1)}, u32[]{:S(2)}, u32[]{:S(2)}) collective-permute-start(bf16[128,128]{1,0:T(8,128)(2,1)S(1)} %get-tuple-element.41), channel_id=1, source_target_pairs={{0,8},{8,16},{16,24},{24,0},{1,9},{9,17},{17,25},{25,1},{2,10},{10... | collective-permute-start | bytes 98312 | tf_op jit(solution)/shard_map/ppermute | solution.py:38
  69.6 5.3 %collective-permute-start.12 = (bf16[128,128]{1,0:T(8,128)(2,1)S(1)}, bf16[128,128]{1,0:T(8,128)(2,1)S(1)}, u32[]{:S(2)}, u32[]{:S(2)}) collective-permute-start(bf16[128,128]{1,0:T(8,128)(2,1)S(1)} %get-tuple-element.41), channel_id=1, source_target_pairs={{0,16},{8,24},{16,0},{24,8},{1,17},{9,25},{17,1},{25,9},{2,18},{10... | collective-permute-start | bytes 98312 | tf_op jit(solution)/shard_map/ppermute | solution.py:38
  72.0 3.9 %collective-permute-start.13 = (bf16[128,128]{1,0:T(8,128)(2,1)S(1)}, bf16[128,128]{1,0:T(8,128)(2,1)S(1)}, u32[]{:S(2)}, u32[]{:S(2)}) collective-permute-start(bf16[128,128]{1,0:T(8,128)(2,1)S(1)} %get-tuple-element.41), channel_id=1, source_target_pairs={{0,24},{8,0},{16,8},{24,16},{1,25},{9,1},{17,9},{25,17},{2,26},{10... | collective-permute-start | bytes 98312 | tf_op jit(solution)/shard_map/ppermute | solution.py:38
  75.9 62.1 %all-to-all-start.1 = ((bf16[4,256,1024]{2,1,0:T(8,128)(2,1)}), bf16[4,256,1024]{2,1,0:T(8,128)(2,1)}, u32[]{:S(2)}, u32[]{:S(2)}) async-start(bf16[4,256,1024]{2,1,0:T(8,128)(2,1)} %bitcast.77), calls=%async_computation.1 | async-start | bytes 4194304 | tf_op jit(solution)/shard_map/all_to_all | solution.py:481
  80.4 15.1 %collective-permute-start.8 = (bf16[128,2048]{1,0:T(8,128)(2,1)}, bf16[128,2048]{1,0:T(8,128)(2,1)S(1)}, u32[]{:S(2)}, u32[]{:S(2)}) collective-permute-start(bf16[128,2048]{1,0:T(8,128)(2,1)} %get-tuple-element.60), channel_id=1, source_target_pairs={{0,2},{2,0},{4,6},{6,4},{1,3},{3,1},{5,7},{7,5},{8,10},{10,8},{12,... | collective-permute-start | bytes 1572872 | tf_op jit(solution)/shard_map/ppermute | solution.py:59
  81.5 22.6 %collective-permute-start.9 = (bf16[128,2048]{1,0:T(8,128)(2,1)}, bf16[128,2048]{1,0:T(8,128)(2,1)S(1)}, u32[]{:S(2)}, u32[]{:S(2)}) collective-permute-start(bf16[128,2048]{1,0:T(8,128)(2,1)} %get-tuple-element.59), channel_id=1, source_target_pairs={{0,4},{2,6},{4,0},{6,2},{1,5},{3,7},{5,1},{7,3},{8,12},{10,14},{12... | collective-permute-start | bytes 1572872 | tf_op jit(solution)/shard_map/ppermute | solution.py:59
  82.5 23.1 %collective-permute-start.10 = (bf16[128,2048]{1,0:T(8,128)(2,1)}, bf16[128,2048]{1,0:T(8,128)(2,1)S(1)}, u32[]{:S(2)}, u32[]{:S(2)}) collective-permute-start(bf16[128,2048]{1,0:T(8,128)(2,1)} %get-tuple-element.58), channel_id=1, source_target_pairs={{0,6},{2,4},{4,2},{6,0},{1,7},{3,5},{5,3},{7,1},{8,14},{10,12},{12... | collective-permute-start | bytes 1572872 | tf_op jit(solution)/shard_map/ppermute | solution.py:59
  105.6 1.6 %copy-start.4 = (bf16[1024,1024]{1,0:T(8,128)(2,1)S(1)}, bf16[1024,1024]{1,0:T(8,128)(2,1)}, u32[]{:S(2)}) copy-start(bf16[1024,1024]{1,0:T(8,128)(2,1)} %x_ref.1) | copy-start | bytes 6291460
  107.2 18.3 %copy-start.20 = (bf16[128,2048]{1,0:T(8,128)(2,1)S(1)}, bf16[128,2048]{1,0:T(8,128)(2,1)}, u32[]{:S(2)}) copy-start(bf16[128,2048]{1,0:T(8,128)(2,1)} %copy-done.19) | copy-start | bytes 1572868
  107.2 18.3 %copy-start.22 = (bf16[128,2048]{1,0:T(8,128)(2,1)S(1)}, bf16[128,2048]{1,0:T(8,128)(2,1)}, u32[]{:S(2)}) copy-start(bf16[128,2048]{1,0:T(8,128)(2,1)} %copy-done.21) | copy-start | bytes 1572868
  108.5 17.0 %copy-start.10 = (bf16[128,2048]{1,0:T(8,128)(2,1)S(1)}, bf16[128,2048]{1,0:T(8,128)(2,1)}, u32[]{:S(2)}) copy-start(bf16[128,2048]{1,0:T(8,128)(2,1)} %copy-done.9) | copy-start | bytes 1572868
  108.5 17.0 %copy-start.12 = (bf16[128,2048]{1,0:T(8,128)(2,1)S(1)}, bf16[128,2048]{1,0:T(8,128)(2,1)}, u32[]{:S(2)}) copy-start(bf16[128,2048]{1,0:T(8,128)(2,1)} %copy-done.11) | copy-start | bytes 1572868
  108.5 17.0 %copy-start.14 = (bf16[128,2048]{1,0:T(8,128)(2,1)S(1)}, bf16[128,2048]{1,0:T(8,128)(2,1)}, u32[]{:S(2)}) copy-start(bf16[128,2048]{1,0:T(8,128)(2,1)} %copy-done.13) | copy-start | bytes 1572868
  108.5 17.0 %copy-start.16 = (bf16[128,2048]{1,0:T(8,128)(2,1)S(1)}, bf16[128,2048]{1,0:T(8,128)(2,1)}, u32[]{:S(2)}) copy-start(bf16[128,2048]{1,0:T(8,128)(2,1)} %copy-done.15) | copy-start | bytes 1572868
  108.5 17.0 %copy-start.18 = (bf16[128,2048]{1,0:T(8,128)(2,1)S(1)}, bf16[128,2048]{1,0:T(8,128)(2,1)}, u32[]{:S(2)}) copy-start(bf16[128,2048]{1,0:T(8,128)(2,1)} %copy-done.17) | copy-start | bytes 1572868
  108.6 3.7 %collective-permute-start.14 = (bf16[4,128,128]{2,1,0:T(8,128)(2,1)S(1)}, bf16[4,128,128]{2,1,0:T(8,128)(2,1)S(1)}, u32[]{:S(2)}, u32[]{:S(2)}) collective-permute-start(bf16[4,128,128]{2,1,0:T(8,128)(2,1)S(1)} %slice_bitcast_fusion.8), channel_id=1, source_target_pairs={{0,1},{1,0},{2,3},{3,2},{4,5},{5,4},{6,7},{7,6},{8,9},{9,8},{10,11... | collective-permute-start | bytes 393224 | tf_op jit(solution)/shard_map/ppermute | solution.py:59
  108.7 7.3 %collective-permute-start.20 = (bf16[4,128,128]{2,1,0:T(8,128)(2,1)S(1)}, bf16[4,128,128]{2,1,0:T(8,128)(2,1)S(1)}, u32[]{:S(2)}, u32[]{:S(2)}) collective-permute-start(bf16[4,128,128]{2,1,0:T(8,128)(2,1)S(1)} %get-tuple-element.67), channel_id=1, source_target_pairs={{0,6},{2,4},{4,2},{6,0},{1,7},{3,5},{5,3},{7,1},{8,14},{10,12},{12... | collective-permute-start | bytes 393224 | tf_op jit(solution)/shard_map/ppermute | solution.py:59
  110.5 8.3 %collective-permute-start.19 = (bf16[4,128,128]{2,1,0:T(8,128)(2,1)S(1)}, bf16[4,128,128]{2,1,0:T(8,128)(2,1)S(1)}, u32[]{:S(2)}, u32[]{:S(2)}) collective-permute-start(bf16[4,128,128]{2,1,0:T(8,128)(2,1)S(1)} %get-tuple-element.67), channel_id=1, source_target_pairs={{0,4},{2,6},{4,0},{6,2},{1,5},{3,7},{5,1},{7,3},{8,12},{10,14},{12... | collective-permute-start | bytes 393224 | tf_op jit(solution)/shard_map/ppermute | solution.py:59
  111.0 7.8 %collective-permute-start.18 = (bf16[4,128,128]{2,1,0:T(8,128)(2,1)S(1)}, bf16[4,128,128]{2,1,0:T(8,128)(2,1)S(1)}, u32[]{:S(2)}, u32[]{:S(2)}) collective-permute-start(bf16[4,128,128]{2,1,0:T(8,128)(2,1)S(1)} %get-tuple-element.67), channel_id=1, source_target_pairs={{0,2},{2,0},{4,6},{6,4},{1,3},{3,1},{5,7},{7,5},{8,10},{10,8},{12,... | collective-permute-start | bytes 393224 | tf_op jit(solution)/shard_map/ppermute | solution.py:59
  112.3 9.4 %collective-permute-start.17 = (bf16[4,128,128]{2,1,0:T(8,128)(2,1)S(1)}, bf16[4,128,128]{2,1,0:T(8,128)(2,1)S(1)}, u32[]{:S(2)}, u32[]{:S(2)}) collective-permute-start(bf16[4,128,128]{2,1,0:T(8,128)(2,1)S(1)} %fusion.3), channel_id=1, source_target_pairs={{0,6},{2,4},{4,2},{6,0},{1,7},{3,5},{5,3},{7,1},{8,14},{10,12},{12... | collective-permute-start | bytes 393224 | tf_op jit(solution)/shard_map/ppermute | solution.py:59
  114.1 9.9 %collective-permute-start.16 = (bf16[4,128,128]{2,1,0:T(8,128)(2,1)S(1)}, bf16[4,128,128]{2,1,0:T(8,128)(2,1)S(1)}, u32[]{:S(2)}, u32[]{:S(2)}) collective-permute-start(bf16[4,128,128]{2,1,0:T(8,128)(2,1)S(1)} %fusion.3), channel_id=1, source_target_pairs={{0,4},{2,6},{4,0},{6,2},{1,5},{3,7},{5,1},{7,3},{8,12},{10,14},{12... | collective-permute-start | bytes 393224 | tf_op jit(solution)/shard_map/ppermute | solution.py:59
  116.0 8.0 %collective-permute-start.15 = (bf16[4,128,128]{2,1,0:T(8,128)(2,1)S(1)}, bf16[4,128,128]{2,1,0:T(8,128)(2,1)S(1)}, u32[]{:S(2)}, u32[]{:S(2)}) collective-permute-start(bf16[4,128,128]{2,1,0:T(8,128)(2,1)S(1)} %fusion.3), channel_id=1, source_target_pairs={{0,2},{2,0},{4,6},{6,4},{1,3},{3,1},{5,7},{7,5},{8,10},{10,8},{12,... | collective-permute-start | bytes 393224 | tf_op jit(solution)/shard_map/ppermute | solution.py:59
  118.9 15.0 %collective-permute-start.21 = (bf16[4,4,128,128]{3,2,1,0:T(8,128)(2,1)S(1)}, bf16[4,4,128,128]{3,2,1,0:T(8,128)(2,1)S(1)}, u32[]{:S(2)}, u32[]{:S(2)}) collective-permute-start(bf16[4,4,128,128]{3,2,1,0:T(8,128)(2,1)S(1)} %pad_maximum_fusion.rest_0_), channel_id=1, source_target_pairs={{0,1},{1,0},{2,3},{3,2},{4,5},{5,4},{6,7},{7,6},{8,9},{9,8},{10,11... | collective-permute-start | bytes 1572872 | tf_op jit(solution)/shard_map/ppermute | solution.py:59
  124.0 8.1 %copy-start.8 = (f32[128,2048]{1,0:T(8,128)S(1)}, f32[128,2048]{1,0:T(8,128)}, u32[]{:S(2)}) copy-start(f32[128,2048]{1,0:T(8,128)} %get-tuple-element.47.rest_0_) | copy-start | bytes 3145732
  124.0 8.1 %copy-start.28 = (bf16[64,2048]{1,0:T(8,128)(2,1)S(1)}, bf16[64,2048]{1,0:T(8,128)(2,1)}, u32[]{:S(2)}) copy-start(bf16[64,2048]{1,0:T(8,128)(2,1)} %copy-done.27) | copy-start | bytes 786436
  124.1 1.4 collective-permute-start.22
  125.5 8.4 %copy-start.6 = (f32[1024,1024]{1,0:T(8,128)S(1)}, f32[1024,1024]{1,0:T(8,128)}, u32[]{:S(2)}) copy-start(f32[1024,1024]{1,0:T(8,128)} %copy-done.5) | copy-start | bytes 12582916
  126.6 16.7 %collective-permute-start.23 = (bf16[8,16,256]{2,1,0:T(8,128)(2,1)S(1)}, bf16[8,16,256]{2,1,0:T(8,128)(2,1)S(1)}, u32[]{:S(2)}, u32[]{:S(2)}) collective-permute-start(bf16[8,16,256]{2,1,0:T(8,128)(2,1)S(1)} %get-tuple-element.64), channel_id=1, source_target_pairs={{0,8},{8,16},{16,24},{24,0},{1,9},{9,17},{17,25},{25,1},{2,10},{10... | collective-permute-start | bytes 196616 | tf_op jit(solution)/shard_map/ppermute | solution.py:38
  128.3 15.0 %collective-permute-start.24 = (bf16[8,16,256]{2,1,0:T(8,128)(2,1)S(1)}, bf16[8,16,256]{2,1,0:T(8,128)(2,1)S(1)}, u32[]{:S(2)}, u32[]{:S(2)}) collective-permute-start(bf16[8,16,256]{2,1,0:T(8,128)(2,1)S(1)} %get-tuple-element.63), channel_id=1, source_target_pairs={{0,16},{8,24},{16,0},{24,8},{1,17},{9,25},{17,1},{25,9},{2,18},{10... | collective-permute-start | bytes 196616 | tf_op jit(solution)/shard_map/ppermute | solution.py:38
  130.7 12.6 %collective-permute-start.25 = (bf16[8,16,256]{2,1,0:T(8,128)(2,1)S(1)}, bf16[8,16,256]{2,1,0:T(8,128)(2,1)S(1)}, u32[]{:S(2)}, u32[]{:S(2)}) collective-permute-start(bf16[8,16,256]{2,1,0:T(8,128)(2,1)S(1)} %get-tuple-element.62), channel_id=1, source_target_pairs={{0,24},{8,0},{16,8},{24,16},{1,25},{9,1},{17,9},{25,17},{2,26},{10... | collective-permute-start | bytes 196616 | tf_op jit(solution)/shard_map/ppermute | solution.py:38
  137.2 0.8 copy-start.23
  138.0 1.0 copy-start.24

commit v9 on v8

--- a/solution.py
+++ b/solution.py
@@ -57,6 +57,18 @@
 def swap(piece, axis, k):
     count = lax.axis_size(axis)
     return lax.ppermute(piece, axis, [(i, partner(i, k, count)) for i in range(count)])
+
+
+def gather_chips(piece, behind):
+    count = lax.axis_size("pipe")
+    in_halves = count == 4 and piece.shape[0] % 32 == 0
+    came = [swap(piece, "pipe", k) for k in range(1, 3 if in_halves else count)]
+    came, one, two = lax.optimization_barrier((came, behind, behind))
+    if in_halves:
+        half = piece.shape[0] // 2
+        third = [swap(came[1][:half], "pipe", 1), swap(came[0][half:], "pipe", 2)]
+        came = came + [jnp.concatenate(third)]
+    return came, one, two
 
 
 def up_rides(adapter_up):
@@ -452,9 +464,9 @@
         up = up.reshape(ADAPTER_RANK, WIDTH)
 
     cot_send, a_send = lax.optimization_barrier((cotangent, a_send))
-    cot_chips = [cotangent] + [swap(cot_send, "pipe", k) for k in range(1, pipe_count)]
-
-    base_tokens, cot_chips = lax.optimization_barrier((tokens, cot_chips))
+    cot_chips, base_tokens, x_tokens = gather_chips(cot_send, tokens)
+    cot_chips = [cotangent] + cot_chips
+
     tokens_by_group = base_tokens.reshape(pipe_count, tensor_count, rows, feature_count)
     base_send = base_product(at, tokens_by_group, key_value_weight, 1, tensor_count - 1)
     base_came = [swap(base_send[s - 1], "tensor", s) for s in range(1, tensor_count)]
@@ -471,10 +483,11 @@
     ]
     input_base = cotangent_product(at, cot_pieces, key_value_weight)
 
-    x_tokens, base_chip = lax.optimization_barrier((tokens, base_chip))
     x_send = x_tokens.T.reshape(data_count, down_rows, tok_dev)
 
-    a_recv, x_send, input_base = lax.optimization_barrier((a_recv, x_send, input_base))
+    a_recv, x_send, input_base, base_chip_came[:2] = lax.optimization_barrier(
+        (a_recv, x_send, input_base, base_chip_came[:2])
+    )
     b_own, grad_rows = own_rows(a_recv, up, cotangent, blocks_dev * down_rows)
     grad_data = [grad_rows] + [shift(grad_rows, "dp", k) for k in range(1, data_count)]
     x_send, grad_data = lax.optimization_barrier((x_send, grad_data))

time: 145 us -> 139 us (0.959)
  waiting for transfers between devices: 58.5 us -> 46.7 us
  local copies, waits for them, and re-layouts: 15.6 us -> 23.2 us
  starting transfers between devices: 37.3 us -> 31.8 us
  Pallas kernels: 29.7 us -> 32.9 us
    ppermute x20 -> x21, waiting for transfers between devices: 56 us -> 30.7 us  [swap(): lax.ppermute(piece, axis, [(i, partner(i, k, count)) for i in range(count)])]
    unnamed x58 -> x39, local copies, waits for them, and re-layouts: 10.8 us -> 16.8 us
    all_to_all x1, waiting for transfers between devices: 0.01 us -> 5.9 us  [body(): a_recv = lax.all_to_all(a_send, 'dp', 0, 0, tiled=True)]
    all_to_all x1, waiting for transfers between devices: 0.01 us -> 5.04 us  [body(): x_recv = lax.all_to_all(x_send, 'dp', 0, 0, tiled=True)]
    ppermute x6, starting transfers between devices: 11.1 us -> 6.76 us  [shift(): lax.ppermute(piece, axis, [(i, (i + k) % count) for i in range(count)])]
    ppermute x6, waiting for transfers between devices: 2.46 us -> 5.08 us  [shift(): lax.ppermute(piece, axis, [(i, (i + k) % count) for i in range(count)])]
    convert_element_type x1 -> x0, other arithmetic: 2.45 us -> none  [body(): base_chip[1:] = [piece.astype(jnp.bfloat16) for piece in base_chip[1:]]]
    add x0 -> x1, other arithmetic: none -> 2.04 us  [body(): sum([base_keep[k].astype(jnp.float32)] + [b[k].astype(jnp.float32) for b...]
  transfers between devices with their start and end apart: 28 -> 29, of which waited for: 17 -> 16; matrix products, arithmetic and copies ran while one was open for 5% -> 6% of each run, Pallas kernels for 18% -> 21%
where the time goes in v9:
time: 139 us; the launch traced here: 138 us
  waiting for transfers between devices  46.7 us (34%)
  Pallas kernels  32.9 us (24%)
  starting transfers between devices  31.8 us (23%)
  local copies, waits for them, and re-layouts  23.2 us (17%)
  other arithmetic  2.25 us (2%)
    ppermute x21, waiting for transfers between devices, swap(): lax.ppermute(piece, axis, [(i, partner(i, k, count)) for i in range(count)])  30.7 us
    unnamed x39, local copies, waits for them, and re-layouts  16.8 us
    ppermute x21, starting transfers between devices, swap(): lax.ppermute(piece, axis, [(i, partner(i, k, count)) for i in range(count)])  15.7 us
    pallas_call x1, Pallas kernels, cotangent_product(): call(kernel, 'cotangent_product', grid=(depth // tile,), in_specs=[SMEM,...  7.91 us
    pallas_call x2, Pallas kernels, base_product(): call(kernel, 'base_product', grid_spec=pltpu.PrefetchScalarGridSpec(num_s...  7.22 us
    ppermute x6, starting transfers between devices, shift(): lax.ppermute(piece, axis, [(i, (i + k) % count) for i in range(count)])  6.76 us
    all_to_all x1, waiting for transfers between devices, body(): a_recv = lax.all_to_all(a_send, 'dp', 0, 0, tiled=True)  5.9 us
    ppermute x6, waiting for transfers between devices, shift(): lax.ppermute(piece, axis, [(i, (i + k) % count) for i in range(count)])  5.08 us
  transfers between devices with their start and end apart: 29, of which 16 were waited for; matrix products, arithmetic and copies ran while one was open for 6% of the time, Pallas kernels for 21%

profile of v9, /device:TPU:0, one launch (start us, length us, event | category | flops | bytes accessed | tf_op | source)
XLA Modules:
  0.0 137.9 jit_solution(8737137465992646740)
XLA Ops:
  0.6 0.8 concatenate.6.at_ref
  1.4 1.4 %copy-done.15 = bf16[24,256,128]{2,1,0:T(8,128)(2,1)S(1)} copy-done((bf16[24,256,128]{2,1,0:T(8,128)(2,1)S(1)}, bf16[24,256,128]{2,1,0:T(8,128)(2,1)}, u32[]{:S(2)}) %copy-start.15) | copy-done | bytes 1572888
  2.8 1.4 %copy-done.16 = bf16[24,16,2048]{2,1,0:T(8,128)(2,1)S(1)} copy-done((bf16[24,16,2048]{2,1,0:T(8,128)(2,1)S(1)}, bf16[24,16,2048]{2,1,0:T(8,128)(2,1)}, u32[]{:S(2)}) %copy-start.16) | copy-done | bytes 1572888
  4.2 2.5 %pick_rows.1 = bf16[4,2304,128]{2,1,0:T(8,128)(2,1)} custom-call(s32[60]{0:T(128)S(1)} %concatenate.6.at_ref, bf16[24,256,128]{2,1,0:T(8,128)(2,1)S(1)} %copy-done.15, bf16[24,16,2048]{2,1,0:T(8,128)(2,1)S(1)} %copy-done.16), custom_call_target="tpu_custom_call" | custom-call | flops 1024 | bytes 1024 | tf_op jit(solution)/shard_map/pick_rows/pallas_call | solution.py:96
  6.7 3.0 %collective-permute-start.1 = (bf16[128,2048]{1,0:T(8,128)(2,1)S(1)}, bf16[128,2048]{1,0:T(8,128)(2,1)S(1)}, u32[]{:S(2)}, u32[]{:S(2)}) collective-permute-start(bf16[128,2048]{1,0:T(8,128)(2,1)S(1)} %copy-done.6), channel_id=1, source_target_pairs={{0,4},{2,6},{4,0},{6,2},{1,5},{3,7},{5,1},{7,3},{8,12},{10,14},{12... | collective-permute-start | bytes 1572872 | tf_op jit(solution)/shard_map/ppermute | solution.py:59
  9.7 1.5 %collective-permute-start = (bf16[128,2048]{1,0:T(8,128)(2,1)S(1)}, bf16[128,2048]{1,0:T(8,128)(2,1)}, u32[]{:S(2)}, u32[]{:S(2)}) collective-permute-start(bf16[128,2048]{1,0:T(8,128)(2,1)S(1)} %copy-done.6), channel_id=1, source_target_pairs={{0,2},{2,0},{4,6},{6,4},{1,3},{3,1},{5,7},{7,5},{8,10},{10,8},{12,... | collective-permute-start | bytes 1572872 | tf_op jit(solution)/shard_map/ppermute | solution.py:59
  11.2 4.9 %all-to-all-start = ((bf16[4,2304,128]{2,1,0:T(8,128)(2,1)}), bf16[4,2304,128]{2,1,0:T(8,128)(2,1)S(1)}, u32[]{:S(2)}, u32[]{:S(2)}) async-start(bf16[4,2304,128]{2,1,0:T(8,128)(2,1)} %pick_rows.1), calls=%async_computation | async-start | bytes 4718592 | tf_op jit(solution)/shard_map/all_to_all | solution.py:460
  16.0 5.6 %collective-permute-done.1.rest_2_.rest_4_ = bf16[128,2048]{1,0:T(8,128)(2,1)S(1)} collective-permute-done((bf16[128,2048]{1,0:T(8,128)(2,1)S(1)}, bf16[128,2048]{1,0:T(8,128)(2,1)S(1)}, u32[]{:S(2)}, u32[]{:S(2)}) %collective-permute-start.1) | collective-permute-done | bytes 524320 | tf_op jit(solution)/shard_map/ppermute | solution.py:59
  21.6 1.6 %collective-permute-done.rest_1_.rest_3_ = bf16[128,2048]{1,0:T(8,128)(2,1)} collective-permute-done((bf16[128,2048]{1,0:T(8,128)(2,1)S(1)}, bf16[128,2048]{1,0:T(8,128)(2,1)}, u32[]{:S(2)}, u32[]{:S(2)}) %collective-permute-start) | collective-permute-done | bytes 524320 | tf_op jit(solution)/shard_map/ppermute | solution.py:59
  23.2 2.2 %copy-done = bf16[1024,2048]{1,0:T(8,128)(2,1)S(1)} copy-done((bf16[1024,2048]{1,0:T(8,128)(2,1)S(1)}, bf16[1024,2048]{1,0:T(8,128)(2,1)}, u32[]{:S(2)}) %copy-start) | copy-done | bytes 4194328
  25.3 1.6 %copy-done.2 = bf16[1024,1024]{1,0:T(8,128)(2,1)S(1)} copy-done((bf16[1024,1024]{1,0:T(8,128)(2,1)S(1)}, bf16[1024,1024]{1,0:T(8,128)(2,1)}, u32[]{:S(2)}) %copy-start.2) | copy-done | bytes 2097176
  26.9 3.6 %base_product.3 = bf16[1,4,128,2048]{3,2,1,0:T(8,128)(2,1)S(1)} custom-call(s32[60]{0:T(128)S(1)} %concatenate.6.at_ref, bf16[4,2,128,1024]{3,2,1,0:T(8,128)(2,1)S(1)} %bitcast.73, bf16[1024,2048]{1,0:T(8,128)(2,1)S(1)} %copy-done), custom_call_target="tpu_custom_call" | custom-call | flops 1024 | bytes 1024 | tf_op jit(solution)/shard_map/base_product/pallas_call | solution.py:121
  30.7 1.6 %collective-permute-start.2 = (bf16[64,2048]{1,0:T(8,128)(2,1)S(1)}, bf16[64,2048]{1,0:T(8,128)(2,1)S(1)}, u32[]{:S(2)}, u32[]{:S(2)}) collective-permute-start(bf16[64,2048]{1,0:T(8,128)(2,1)S(1)} %slice.52), channel_id=1, source_target_pairs={{0,2},{2,0},{4,6},{6,4},{1,3},{3,1},{5,7},{7,5},{8,10},{10,8},{12,... | collective-permute-start | bytes 786440 | tf_op jit(solution)/shard_map/ppermute | solution.py:59
  32.2 1.0 slice.53
  33.2 0.6 collective-permute-start.3
  33.8 0.5 collective-permute-start.5
  34.3 3.6 %base_product.2 = bf16[1,4,128,2048]{3,2,1,0:T(8,128)(2,1)S(1)} custom-call(s32[60]{0:T(128)S(1)} %concatenate.6.at_ref, bf16[4,2,128,1024]{3,2,1,0:T(8,128)(2,1)S(1)} %bitcast.74, bf16[1024,2048]{1,0:T(8,128)(2,1)S(1)} %copy-done), custom_call_target="tpu_custom_call" | custom-call | flops 1024 | bytes 1024 | tf_op jit(solution)/shard_map/base_product/pallas_call | solution.py:121
  37.9 1.5 %collective-permute-done.2 = bf16[64,2048]{1,0:T(8,128)(2,1)S(1)} collective-permute-done((bf16[64,2048]{1,0:T(8,128)(2,1)S(1)}, bf16[64,2048]{1,0:T(8,128)(2,1)S(1)}, u32[]{:S(2)}, u32[]{:S(2)}) %collective-permute-start.2) | collective-permute-done | bytes 262176 | tf_op jit(solution)/shard_map/ppermute | solution.py:59
  39.4 0.7 constant_dynamic-update-slice_fusion.1
  40.2 1.5 %collective-permute-done.3 = bf16[64,2048]{1,0:T(8,128)(2,1)S(1)} collective-permute-done((bf16[64,2048]{1,0:T(8,128)(2,1)S(1)}, bf16[64,2048]{1,0:T(8,128)(2,1)S(1)}, u32[]{:S(2)}, u32[]{:S(2)}) %collective-permute-start.3) | collective-permute-done | bytes 262176 | tf_op jit(solution)/shard_map/ppermute | solution.py:59
  41.7 0.7 constant_dynamic-update-slice_fusion.rest_3_.rest_5_
  42.4 2.0 %convert_add_fusion = (f32[128,2048]{1,0:T(8,128)}, bf16[128,2048]{1,0:T(8,128)(2,1)}, bf16[128,2048]{1,0:T(8,128)(2,1)}, bf16[128,2048]{1,0:T(8,128)(2,1)}) fusion(bf16[4,128,2048]{2,1,0:T(8,128)(2,1)S(1)} %collective-permute-done.8, bf16[1,4,128,2048]{3,2,1,0:T(8,128)(2,1)S(1)} %base_product.2), kind=kLoop, calls=%fused_computation | loop fusion | flops 3932160 | bytes 6815744 | tf_op jit(solution)/shard_map/add | solution.py:475
  44.4 0.5 collective-permute-start.10
  45.0 0.8 copy-done.10
  45.8 0.5 collective-permute-start.9
  46.3 3.9 %copy.11 = bf16[1024,1024]{1,0:T(8,128)(2,1)} copy(bf16[1024,1024]{0,1:T(8,128)(2,1)} %bitcast.72) | data formatting | bytes 4194304 | tf_op jit(solution)/shard_map/transpose | solution.py:486
  50.3 2.2 %copy-done.1 = bf16[1024,2048]{1,0:T(8,128)(2,1)S(1)} copy-done((bf16[1024,2048]{1,0:T(8,128)(2,1)S(1)}, bf16[1024,2048]{1,0:T(8,128)(2,1)}, u32[]{:S(2)}) %copy-start.1) | copy-done | bytes 4194328
  52.4 1.0 copy-done.11
  53.5 7.9 %cotangent_product.1.base_ref = f32[1024,1024]{1,0:T(8,128)S(1)} custom-call(s32[60]{0:T(128)S(1)} %concatenate.6.at_ref, bf16[1024,2048]{1,0:T(8,128)(2,1)S(1)} %copy-done.1, bf16[128,2048]{1,0:T(8,128)(2,1)S(1)} %copy-done.6, bf16[128,2048]{1,0:T(8,128)(2,1)} %collective-permute-done.rest_1_.rest_3_, ...), custom_call_target="tpu_custom_call" | custom-call | flops 1024 | bytes 1024 | tf_op jit(solution)/shard_map/cotangent_product/pallas_call | solution.py:194
  61.4 2.0 %copy-done.4 = f32[1024,1024]{1,0:T(8,128)} copy-done((f32[1024,1024]{1,0:T(8,128)}, f32[1024,1024]{1,0:T(8,128)S(1)}, u32[]{:S(2)}) %copy-start.4) | copy-done | bytes 4194328
  63.4 5.9 %all-to-all-done.came_ref.a_ref = bf16[4,2304,128]{2,1,0:T(8,128)(2,1)S(1)} async-done(((bf16[4,2304,128]{2,1,0:T(8,128)(2,1)}), bf16[4,2304,128]{2,1,0:T(8,128)(2,1)S(1)}, u32[]{:S(2)}, u32[]{:S(2)}) %all-to-all-start) | async-done | bytes 2359328 | tf_op jit(solution)/shard_map/all_to_all | solution.py:460
  69.3 0.4 own_rows.1
  69.7 1.5 %collective-permute-start.14 = (bf16[128,128]{1,0:T(8,128)(2,1)S(1)}, bf16[128,128]{1,0:T(8,128)(2,1)S(1)}, u32[]{:S(2)}, u32[]{:S(2)}) collective-permute-start(bf16[128,128]{1,0:T(8,128)(2,1)S(1)} %get-tuple-element.40), channel_id=1, source_target_pairs={{0,24},{8,0},{16,8},{24,16},{1,25},{9,1},{17,9},{25,17},{2,26},{10... | collective-permute-start | bytes 98312 | tf_op jit(solution)/shard_map/ppermute | solution.py:38
  71.2 0.6 collective-permute-start.12
  71.9 1.8 %collective-permute-done.14 = bf16[128,128]{1,0:T(8,128)(2,1)S(1)} collective-permute-done((bf16[128,128]{1,0:T(8,128)(2,1)S(1)}, bf16[128,128]{1,0:T(8,128)(2,1)S(1)}, u32[]{:S(2)}, u32[]{:S(2)}) %collective-permute-start.14) | collective-permute-done | bytes 32800 | tf_op jit(solution)/shard_map/ppermute | solution.py:38
  73.7 2.7 %collective-permute-done.13 = bf16[128,128]{1,0:T(8,128)(2,1)S(1)} collective-permute-done((bf16[128,128]{1,0:T(8,128)(2,1)S(1)}, bf16[128,128]{1,0:T(8,128)(2,1)S(1)}, u32[]{:S(2)}, u32[]{:S(2)}) %collective-permute-start.13) | collective-permute-done | bytes 32800 | tf_op jit(solution)/shard_map/ppermute | solution.py:38
  76.4 0.6 collective-permute-done.12
  77.0 4.5 %all-to-all-start.1 = ((bf16[4,256,1024]{2,1,0:T(8,128)(2,1)}), bf16[4,256,1024]{2,1,0:T(8,128)(2,1)}, u32[]{:S(2)}, u32[]{:S(2)}) async-start(bf16[4,256,1024]{2,1,0:T(8,128)(2,1)} %bitcast.77), calls=%async_computation.1 | async-start | bytes 4194304 | tf_op jit(solution)/shard_map/all_to_all | solution.py:494
  81.4 0.5 collective-permute-start.11
  82.0 11.5 %collective-permute-done.11.rest_3_ = bf16[128,2048]{1,0:T(8,128)(2,1)S(1)} collective-permute-done((bf16[128,2048]{1,0:T(8,128)(2,1)}, bf16[128,2048]{1,0:T(8,128)(2,1)S(1)}, u32[]{:S(2)}, u32[]{:S(2)}) %collective-permute-start.11) | collective-permute-done | bytes 524320 | tf_op jit(solution)/shard_map/ppermute | solution.py:59
  93.5 1.6 %copy-done.3 = bf16[1024,1024]{1,0:T(8,128)(2,1)S(1)} copy-done((bf16[1024,1024]{1,0:T(8,128)(2,1)S(1)}, bf16[1024,1024]{1,0:T(8,128)(2,1)}, u32[]{:S(2)}) %copy-start.3) | copy-done | bytes 2097176
  95.1 1.3 low_product.1
  96.5 0.6 collective-permute-start.20
  97.1 0.5 collective-permute-start.19
  97.6 2.4 %collective-permute-start.21 = (bf16[4,128,128]{2,1,0:T(8,128)(2,1)S(1)}, bf16[4,128,128]{2,1,0:T(8,128)(2,1)S(1)}, u32[]{:S(2)}, u32[]{:S(2)}) collective-permute-start(bf16[4,128,128]{2,1,0:T(8,128)(2,1)S(1)} %get-tuple-element.65), channel_id=1, source_target_pairs={{0,6},{2,4},{4,2},{6,0},{1,7},{3,5},{5,3},{7,1},{8,14},{10,12},{12... | collective-permute-start | bytes 393224 | tf_op jit(solution)/shard_map/ppermute | solution.py:59
  100.1 0.5 collective-permute-start.18
  100.6 1.5 %collective-permute-start.17 = (bf16[4,128,128]{2,1,0:T(8,128)(2,1)S(1)}, bf16[4,128,128]{2,1,0:T(8,128)(2,1)S(1)}, u32[]{:S(2)}, u32[]{:S(2)}) collective-permute-start(bf16[4,128,128]{2,1,0:T(8,128)(2,1)S(1)} %fusion.3), channel_id=1, source_target_pairs={{0,4},{2,6},{4,0},{6,2},{1,5},{3,7},{5,1},{7,3},{8,12},{10,14},{12... | collective-permute-start | bytes 393224 | tf_op jit(solution)/shard_map/ppermute | solution.py:59
  102.2 0.3 collective-permute-done.20
  102.4 1.2 collective-permute-start.16
  103.7 3.6 %collective-permute-done.21 = bf16[4,128,128]{2,1,0:T(8,128)(2,1)S(1)} collective-permute-done((bf16[4,128,128]{2,1,0:T(8,128)(2,1)S(1)}, bf16[4,128,128]{2,1,0:T(8,128)(2,1)S(1)}, u32[]{:S(2)}, u32[]{:S(2)}) %collective-permute-start.21) | collective-permute-done | bytes 131104 | tf_op jit(solution)/shard_map/ppermute | solution.py:59
  107.4 2.6 %collective-permute-done.18 = bf16[4,128,128]{2,1,0:T(8,128)(2,1)S(1)} collective-permute-done((bf16[4,128,128]{2,1,0:T(8,128)(2,1)S(1)}, bf16[4,128,128]{2,1,0:T(8,128)(2,1)S(1)}, u32[]{:S(2)}, u32[]{:S(2)}) %collective-permute-start.18) | collective-permute-done | bytes 131104 | tf_op jit(solution)/shard_map/ppermute | solution.py:59
  110.0 1.0 collective-permute-done.17
  111.0 0.1 collective-permute-done.16
  111.3 1.3 collective-permute-done.23.rest_1_
  112.7 2.2 %grad_up_pieces.1 = bf16[4,8,16,256]{3,2,1,0:T(8,128)(2,1)S(1)} custom-call(s32[60]{0:T(128)S(1)} %concatenate.6.at_ref, bf16[4,128,128]{2,1,0:T(8,128)(2,1)S(1)} %add_convert_fusion.low_ref.rest_0_, bf16[4,128,128]{2,1,0:T(8,128)(2,1)S(1)} %collective-permute-done.23.rest_1_, bf16[128,2048]{1,0:T(8,128)(2,1)S(1)} %copy-done.6, ...), custom_call_target="tpu_custom_call" | custom-call | flops 1024 | bytes 1024 | tf_op jit(solution)/shard_map/grad_up_pieces/pallas_call | solution.py:333
  114.9 3.5 %collective-permute-start.26 = (bf16[8,16,256]{2,1,0:T(8,128)(2,1)S(1)}, bf16[8,16,256]{2,1,0:T(8,128)(2,1)S(1)}, u32[]{:S(2)}, u32[]{:S(2)}) collective-permute-start(bf16[8,16,256]{2,1,0:T(8,128)(2,1)S(1)} %get-tuple-element.60), channel_id=1, source_target_pairs={{0,24},{8,0},{16,8},{24,16},{1,25},{9,1},{17,9},{25,17},{2,26},{10... | collective-permute-start | bytes 196616 | tf_op jit(solution)/shard_map/ppermute | solution.py:38
  118.4 1.1 collective-permute-start.24
  119.5 2.4 %keys_and_values.1 = bf16[128,2048]{1,0:T(8,128)(2,1)} custom-call(s32[60]{0:T(128)S(1)} %concatenate.6.at_ref, bf16[4,128,128]{2,1,0:T(8,128)(2,1)S(1)} %add_convert_fusion.low_ref.rest_0_, bf16[64,2048]{1,0:T(8,128)(2,1)S(1)} %copy-done.18, f32[128,2048]{1,0:T(8,128)S(1)} %copy-done.7, bf16[128,2048]{1,0:T(8,128)(2,1)} %collective-permute-done.9.rest_1_, ...), custom_call_target="tpu_custom_call" | custom-call | flops 1024 | bytes 1024 | tf_op jit(solution)/shard_map/keys_and_values/pallas_call | solution.py:426
  121.9 3.3 %input_gradient.1 = bf16[1024,1024]{1,0:T(8,128)(2,1)} custom-call(s32[60]{0:T(128)S(1)} %concatenate.6.at_ref, f32[1024,1024]{1,0:T(8,128)S(1)} %copy-done.5, bf16[4,2304,128]{2,1,0:T(8,128)(2,1)S(1)} %all-to-all-done.came_ref.a_ref, bf16[4,4,128,128]{3,2,1,0:T(8,128)(2,1)S(1)} %pad_maximum_fusion.rest_0_, ...), custom_call_target="tpu_custom_call" | custom-call | flops 1024 | bytes 1024 | tf_op jit(solution)/shard_map/input_gradient/pallas_call | solution.py:236
  125.3 0.8 copy-done.13
  126.1 5.0 %all-to-all-done.1.x_ref = bf16[4,256,1024]{2,1,0:T(8,128)(2,1)} async-done(((bf16[4,256,1024]{2,1,0:T(8,128)(2,1)}), bf16[4,256,1024]{2,1,0:T(8,128)(2,1)}, u32[]{:S(2)}, u32[]{:S(2)}) %all-to-all-start.1) | async-done | bytes 2097184 | tf_op jit(solution)/shard_map/all_to_all | solution.py:494
  131.1 1.0 copy-done.14
  132.1 4.2 %grad_down.1 = f32[24,256,128]{2,1,0:T(8,128)} custom-call(s32[60]{0:T(128)S(1)} %concatenate.6.at_ref, bf16[4,256,1024]{2,1,0:T(8,128)(2,1)} %all-to-all-done.1.x_ref, bf16[4,4,128,128]{3,2,1,0:T(8,128)(2,1)S(1)} %pad_maximum_fusion.rest_0_, bf16[4,4,128,128]{3,2,1,0:T(8,128)(2,1)S(1)} %copy-done.14), custom_call_target="tpu_custom_call" | custom-call | flops 1024 | bytes 1024 | tf_op jit(solution)/shard_map/grad_down/pallas_call | solution.py:277
  136.4 1.5 %grad_up.1 = f32[24,16,256]{2,1,0:T(8,128)} custom-call(s32[60]{0:T(128)S(1)} %concatenate.6.at_ref, bf16[8,16,256]{2,1,0:T(8,128)(2,1)S(1)} %get-tuple-element.52.rest_0_, bf16[8,16,256]{2,1,0:T(8,128)(2,1)S(1)} %collective-permute-done.24.rest_1_, bf16[8,16,256]{2,1,0:T(8,128)(2,1)S(1)} %collective-permute-done.25.rest_2_, ...), custom_call_target="tpu_custom_call" | custom-call | flops 1024 | bytes 1024 | tf_op jit(solution)/shard_map/grad_up/pallas_call | solution.py:360
  (56 shorter events, 0.6 us)
Async XLA Ops:
  1.4 1.4 %copy-start.15 = (bf16[24,256,128]{2,1,0:T(8,128)(2,1)S(1)}, bf16[24,256,128]{2,1,0:T(8,128)(2,1)}, u32[]{:S(2)}) copy-start(bf16[24,256,128]{2,1,0:T(8,128)(2,1)} %down_ref.1) | copy-start | bytes 4718596
  2.8 1.4 %copy-start.16 = (bf16[24,16,2048]{2,1,0:T(8,128)(2,1)S(1)}, bf16[24,16,2048]{2,1,0:T(8,128)(2,1)}, u32[]{:S(2)}) copy-start(bf16[24,16,2048]{2,1,0:T(8,128)(2,1)} %up_ref.1) | copy-start | bytes 4718596
  4.2 2.5 %copy-start.6 = (bf16[128,2048]{1,0:T(8,128)(2,1)S(1)}, bf16[128,2048]{1,0:T(8,128)(2,1)}, u32[]{:S(2)}) copy-start(bf16[128,2048]{1,0:T(8,128)(2,1)} %rest_2_.1) | copy-start | bytes 1572868
  6.7 14.9 %collective-permute-start.1 = (bf16[128,2048]{1,0:T(8,128)(2,1)S(1)}, bf16[128,2048]{1,0:T(8,128)(2,1)S(1)}, u32[]{:S(2)}, u32[]{:S(2)}) collective-permute-start(bf16[128,2048]{1,0:T(8,128)(2,1)S(1)} %copy-done.6), channel_id=1, source_target_pairs={{0,4},{2,6},{4,0},{6,2},{1,5},{3,7},{5,1},{7,3},{8,12},{10,14},{12... | collective-permute-start | bytes 1572872 | tf_op jit(solution)/shard_map/ppermute | solution.py:59
  9.7 13.5 %collective-permute-start = (bf16[128,2048]{1,0:T(8,128)(2,1)S(1)}, bf16[128,2048]{1,0:T(8,128)(2,1)}, u32[]{:S(2)}, u32[]{:S(2)}) collective-permute-start(bf16[128,2048]{1,0:T(8,128)(2,1)S(1)} %copy-done.6), channel_id=1, source_target_pairs={{0,2},{2,0},{4,6},{6,4},{1,3},{3,1},{5,7},{7,5},{8,10},{10,8},{12,... | collective-permute-start | bytes 1572872 | tf_op jit(solution)/shard_map/ppermute | solution.py:59
  11.2 58.1 %all-to-all-start = ((bf16[4,2304,128]{2,1,0:T(8,128)(2,1)}), bf16[4,2304,128]{2,1,0:T(8,128)(2,1)S(1)}, u32[]{:S(2)}, u32[]{:S(2)}) async-start(bf16[4,2304,128]{2,1,0:T(8,128)(2,1)} %pick_rows.1), calls=%async_computation | async-start | bytes 4718592 | tf_op jit(solution)/shard_map/all_to_all | solution.py:460
  21.6 28.6 %copy-start.8 = (bf16[128,2048]{1,0:T(8,128)(2,1)}, bf16[128,2048]{1,0:T(8,128)(2,1)S(1)}, u32[]{:S(2)}) copy-start(bf16[128,2048]{1,0:T(8,128)(2,1)S(1)} %collective-permute-done.1.rest_2_.rest_4_) | copy-start | bytes 1572868
  23.2 2.2 %copy-start = (bf16[1024,2048]{1,0:T(8,128)(2,1)S(1)}, bf16[1024,2048]{1,0:T(8,128)(2,1)}, u32[]{:S(2)}) copy-start(bf16[1024,2048]{1,0:T(8,128)(2,1)} %w_ref.5) | copy-start | bytes 12582916
  25.3 1.6 %copy-start.2 = (bf16[1024,1024]{1,0:T(8,128)(2,1)S(1)}, bf16[1024,1024]{1,0:T(8,128)(2,1)}, u32[]{:S(2)}) copy-start(bf16[1024,1024]{1,0:T(8,128)(2,1)} %x_ref.1) | copy-start | bytes 6291460
  30.6 11.8 %collective-permute-start.8 = (bf16[4,128,2048]{2,1,0:T(8,128)(2,1)S(1)}, bf16[4,128,2048]{2,1,0:T(8,128)(2,1)S(1)}, u32[]{:S(2)}, u32[]{:S(2)}) collective-permute-start(bf16[4,128,2048]{2,1,0:T(8,128)(2,1)S(1)} %bitcast.75), channel_id=1, source_target_pairs={{0,1},{1,0},{2,3},{3,2},{4,5},{5,4},{6,7},{7,6},{8,9},{9,8},{10,11... | collective-permute-start | bytes 6291464 | tf_op jit(solution)/shard_map/ppermute | solution.py:59
  30.7 8.8 %collective-permute-start.2 = (bf16[64,2048]{1,0:T(8,128)(2,1)S(1)}, bf16[64,2048]{1,0:T(8,128)(2,1)S(1)}, u32[]{:S(2)}, u32[]{:S(2)}) collective-permute-start(bf16[64,2048]{1,0:T(8,128)(2,1)S(1)} %slice.52), channel_id=1, source_target_pairs={{0,2},{2,0},{4,6},{6,4},{1,3},{3,1},{5,7},{7,5},{8,10},{10,8},{12,... | collective-permute-start | bytes 786440 | tf_op jit(solution)/shard_map/ppermute | solution.py:59
  33.2 8.5 %collective-permute-start.3 = (bf16[64,2048]{1,0:T(8,128)(2,1)S(1)}, bf16[64,2048]{1,0:T(8,128)(2,1)S(1)}, u32[]{:S(2)}, u32[]{:S(2)}) collective-permute-start(bf16[64,2048]{1,0:T(8,128)(2,1)S(1)} %slice.53), channel_id=1, source_target_pairs={{0,4},{2,6},{4,0},{6,2},{1,5},{3,7},{5,1},{7,3},{8,12},{10,14},{12... | collective-permute-start | bytes 786440 | tf_op jit(solution)/shard_map/ppermute | solution.py:59
  33.8 11.2 %collective-permute-start.4 = (bf16[128,2048]{1,0:T(8,128)(2,1)S(1)}, bf16[128,2048]{1,0:T(8,128)(2,1)S(1)}, u32[]{:S(2)}, u32[]{:S(2)}) collective-permute-start(bf16[128,2048]{1,0:T(8,128)(2,1)S(1)} %copy-done.6), channel_id=1, source_target_pairs={{0,1},{1,0},{2,3},{3,2},{4,5},{5,4},{6,7},{7,6},{8,9},{9,8},{10,11... | collective-permute-start | bytes 1572872 | tf_op jit(solution)/shard_map/ppermute | solution.py:59
  33.8 16.5 %collective-permute-start.5 = (bf16[128,2048]{1,0:T(8,128)(2,1)}, bf16[128,2048]{1,0:T(8,128)(2,1)}, u32[]{:S(2)}, u32[]{:S(2)}) collective-permute-start(bf16[128,2048]{1,0:T(8,128)(2,1)} %collective-permute-done.rest_1_.rest_3_), channel_id=1, source_target_pairs={{0,1},{1,0},{2,3},{3,2},{4,5},{5,4},{6,7},{7,6},{8,9},{9,8},{10,11... | collective-permute-start | bytes 1572872 | tf_op jit(solution)/shard_map/ppermute | solution.py:59
  39.4 10.8 %collective-permute-start.6 = (bf16[128,2048]{1,0:T(8,128)(2,1)S(1)}, bf16[128,2048]{1,0:T(8,128)(2,1)}, u32[]{:S(2)}, u32[]{:S(2)}) collective-permute-start(bf16[128,2048]{1,0:T(8,128)(2,1)S(1)} %collective-permute-done.1.rest_2_.rest_4_), channel_id=1, source_target_pairs={{0,1},{1,0},{2,3},{3,2},{4,5},{5,4},{6,7},{7,6},{8,9},{9,8},{10,11... | collective-permute-start | bytes 1572872 | tf_op jit(solution)/shard_map/ppermute | solution.py:59
  42.4 7.8 %collective-permute-start.7 = (bf16[128,2048]{1,0:T(8,128)(2,1)}, bf16[128,2048]{1,0:T(8,128)(2,1)}, u32[]{:S(2)}, u32[]{:S(2)}) collective-permute-start(bf16[128,2048]{1,0:T(8,128)(2,1)} %constant_dynamic-update-slice_fusion.rest_3_.rest_5_), channel_id=1, source_target_pairs={{0,1},{1,0},{2,3},{3,2},{4,5},{5,4},{6,7},{7,6},{8,9},{9,8},{10,11... | collective-permute-start | bytes 1572872 | tf_op jit(solution)/shard_map/ppermute | solution.py:59
  44.4 18.9 %collective-permute-start.10 = (bf16[128,2048]{1,0:T(8,128)(2,1)}, bf16[128,2048]{1,0:T(8,128)(2,1)}, u32[]{:S(2)}, u32[]{:S(2)}) collective-permute-start(bf16[128,2048]{1,0:T(8,128)(2,1)} %get-tuple-element.58), channel_id=1, source_target_pairs={{0,4},{2,6},{4,0},{6,2},{1,5},{3,7},{5,1},{7,3},{8,12},{10,14},{12... | collective-permute-start | bytes 1572872 | tf_op jit(solution)/shard_map/ppermute | solution.py:59
  45.0 0.8 copy-start.10
  45.8 17.6 %collective-permute-start.9 = (bf16[128,2048]{1,0:T(8,128)(2,1)}, bf16[128,2048]{1,0:T(8,128)(2,1)}, u32[]{:S(2)}, u32[]{:S(2)}) collective-permute-start(bf16[128,2048]{1,0:T(8,128)(2,1)} %get-tuple-element.59), channel_id=1, source_target_pairs={{0,2},{2,0},{4,6},{6,4},{1,3},{3,1},{5,7},{7,5},{8,10},{10,8},{12,... | collective-permute-start | bytes 1572872 | tf_op jit(solution)/shard_map/ppermute | solution.py:59
  50.2 2.2 %copy-start.1 = (bf16[1024,2048]{1,0:T(8,128)(2,1)S(1)}, bf16[1024,2048]{1,0:T(8,128)(2,1)}, u32[]{:S(2)}) copy-start(bf16[1024,2048]{1,0:T(8,128)(2,1)} %w_ref.5) | copy-start | bytes 12582916
  52.4 1.0 copy-start.11
  61.4 2.0 %copy-start.4 = (f32[1024,1024]{1,0:T(8,128)}, f32[1024,1024]{1,0:T(8,128)S(1)}, u32[]{:S(2)}) copy-start(f32[1024,1024]{1,0:T(8,128)S(1)} %cotangent_product.1.base_ref) | copy-start | bytes 12582916
  69.7 7.2 %copy-start.17 = (bf16[64,2048]{1,0:T(8,128)(2,1)}, bf16[64,2048]{1,0:T(8,128)(2,1)S(1)}, u32[]{:S(2)}) copy-start(bf16[64,2048]{1,0:T(8,128)(2,1)S(1)} %get-tuple-element.45.b_ref) | copy-start | bytes 786436
  69.7 4.0 %collective-permute-start.14 = (bf16[128,128]{1,0:T(8,128)(2,1)S(1)}, bf16[128,128]{1,0:T(8,128)(2,1)S(1)}, u32[]{:S(2)}, u32[]{:S(2)}) collective-permute-start(bf16[128,128]{1,0:T(8,128)(2,1)S(1)} %get-tuple-element.40), channel_id=1, source_target_pairs={{0,24},{8,0},{16,8},{24,16},{1,25},{9,1},{17,9},{25,17},{2,26},{10... | collective-permute-start | bytes 98312 | tf_op jit(solution)/shard_map/ppermute | solution.py:38
  71.2 5.2 %collective-permute-start.13 = (bf16[128,128]{1,0:T(8,128)(2,1)S(1)}, bf16[128,128]{1,0:T(8,128)(2,1)S(1)}, u32[]{:S(2)}, u32[]{:S(2)}) collective-permute-start(bf16[128,128]{1,0:T(8,128)(2,1)S(1)} %get-tuple-element.40), channel_id=1, source_target_pairs={{0,16},{8,24},{16,0},{24,8},{1,17},{9,25},{17,1},{25,9},{2,18},{10... | collective-permute-start | bytes 98312 | tf_op jit(solution)/shard_map/ppermute | solution.py:38
  71.2 5.7 %collective-permute-start.12 = (bf16[128,128]{1,0:T(8,128)(2,1)S(1)}, bf16[128,128]{1,0:T(8,128)(2,1)S(1)}, u32[]{:S(2)}, u32[]{:S(2)}) collective-permute-start(bf16[128,128]{1,0:T(8,128)(2,1)S(1)} %get-tuple-element.40), channel_id=1, source_target_pairs={{0,8},{8,16},{16,24},{24,0},{1,9},{9,17},{17,25},{25,1},{2,10},{10... | collective-permute-start | bytes 98312 | tf_op jit(solution)/shard_map/ppermute | solution.py:38
  77.0 54.1 %all-to-all-start.1 = ((bf16[4,256,1024]{2,1,0:T(8,128)(2,1)}), bf16[4,256,1024]{2,1,0:T(8,128)(2,1)}, u32[]{:S(2)}, u32[]{:S(2)}) async-start(bf16[4,256,1024]{2,1,0:T(8,128)(2,1)} %bitcast.77), calls=%async_computation.1 | async-start | bytes 4194304 | tf_op jit(solution)/shard_map/all_to_all | solution.py:494
  81.4 12.1 %collective-permute-start.11 = (bf16[128,2048]{1,0:T(8,128)(2,1)}, bf16[128,2048]{1,0:T(8,128)(2,1)S(1)}, u32[]{:S(2)}, u32[]{:S(2)}) collective-permute-start(bf16[128,2048]{1,0:T(8,128)(2,1)} %get-tuple-element.57), channel_id=1, source_target_pairs={{0,6},{2,4},{4,2},{6,0},{1,7},{3,5},{5,3},{7,1},{8,14},{10,12},{12... | collective-permute-start | bytes 1572872 | tf_op jit(solution)/shard_map/ppermute | solution.py:59
  93.5 1.6 %copy-start.3 = (bf16[1024,1024]{1,0:T(8,128)(2,1)S(1)}, bf16[1024,1024]{1,0:T(8,128)(2,1)}, u32[]{:S(2)}) copy-start(bf16[1024,1024]{1,0:T(8,128)(2,1)} %x_ref.1) | copy-start | bytes 6291460
  96.3 16.3 %copy-start.9 = (bf16[128,2048]{1,0:T(8,128)(2,1)S(1)}, bf16[128,2048]{1,0:T(8,128)(2,1)}, u32[]{:S(2)}) copy-start(bf16[128,2048]{1,0:T(8,128)(2,1)} %copy-done.8) | copy-start | bytes 1572868
  96.3 16.3 %copy-start.12 = (bf16[128,2048]{1,0:T(8,128)(2,1)S(1)}, bf16[128,2048]{1,0:T(8,128)(2,1)}, u32[]{:S(2)}) copy-start(bf16[128,2048]{1,0:T(8,128)(2,1)} %copy-done.10) | copy-start | bytes 1572868
  96.4 3.7 %collective-permute-start.15 = (bf16[4,128,128]{2,1,0:T(8,128)(2,1)S(1)}, bf16[4,128,128]{2,1,0:T(8,128)(2,1)S(1)}, u32[]{:S(2)}, u32[]{:S(2)}) collective-permute-start(bf16[4,128,128]{2,1,0:T(8,128)(2,1)S(1)} %slice_bitcast_fusion.8), channel_id=1, source_target_pairs={{0,1},{1,0},{2,3},{3,2},{4,5},{5,4},{6,7},{7,6},{8,9},{9,8},{10,11... | collective-permute-start | bytes 393224 | tf_op jit(solution)/shard_map/ppermute | solution.py:59
  96.5 6.0 %collective-permute-start.20 = (bf16[4,128,128]{2,1,0:T(8,128)(2,1)S(1)}, bf16[4,128,128]{2,1,0:T(8,128)(2,1)S(1)}, u32[]{:S(2)}, u32[]{:S(2)}) collective-permute-start(bf16[4,128,128]{2,1,0:T(8,128)(2,1)S(1)} %get-tuple-element.65), channel_id=1, source_target_pairs={{0,4},{2,6},{4,0},{6,2},{1,5},{3,7},{5,1},{7,3},{8,12},{10,14},{12... | collective-permute-start | bytes 393224 | tf_op jit(solution)/shard_map/ppermute | solution.py:59
  97.1 6.6 %collective-permute-start.19 = (bf16[4,128,128]{2,1,0:T(8,128)(2,1)S(1)}, bf16[4,128,128]{2,1,0:T(8,128)(2,1)S(1)}, u32[]{:S(2)}, u32[]{:S(2)}) collective-permute-start(bf16[4,128,128]{2,1,0:T(8,128)(2,1)S(1)} %get-tuple-element.65), channel_id=1, source_target_pairs={{0,2},{2,0},{4,6},{6,4},{1,3},{3,1},{5,7},{7,5},{8,10},{10,8},{12,... | collective-permute-start | bytes 393224 | tf_op jit(solution)/shard_map/ppermute | solution.py:59
  97.6 9.7 %collective-permute-start.21 = (bf16[4,128,128]{2,1,0:T(8,128)(2,1)S(1)}, bf16[4,128,128]{2,1,0:T(8,128)(2,1)S(1)}, u32[]{:S(2)}, u32[]{:S(2)}) collective-permute-start(bf16[4,128,128]{2,1,0:T(8,128)(2,1)S(1)} %get-tuple-element.65), channel_id=1, source_target_pairs={{0,6},{2,4},{4,2},{6,0},{1,7},{3,5},{5,3},{7,1},{8,14},{10,12},{12... | collective-permute-start | bytes 393224 | tf_op jit(solution)/shard_map/ppermute | solution.py:59
  100.1 9.9 %collective-permute-start.18 = (bf16[4,128,128]{2,1,0:T(8,128)(2,1)S(1)}, bf16[4,128,128]{2,1,0:T(8,128)(2,1)S(1)}, u32[]{:S(2)}, u32[]{:S(2)}) collective-permute-start(bf16[4,128,128]{2,1,0:T(8,128)(2,1)S(1)} %fusion.3), channel_id=1, source_target_pairs={{0,6},{2,4},{4,2},{6,0},{1,7},{3,5},{5,3},{7,1},{8,14},{10,12},{12... | collective-permute-start | bytes 393224 | tf_op jit(solution)/shard_map/ppermute | solution.py:59
  100.6 10.4 %collective-permute-start.17 = (bf16[4,128,128]{2,1,0:T(8,128)(2,1)S(1)}, bf16[4,128,128]{2,1,0:T(8,128)(2,1)S(1)}, u32[]{:S(2)}, u32[]{:S(2)}) collective-permute-start(bf16[4,128,128]{2,1,0:T(8,128)(2,1)S(1)} %fusion.3), channel_id=1, source_target_pairs={{0,4},{2,6},{4,0},{6,2},{1,5},{3,7},{5,1},{7,3},{8,12},{10,14},{12... | collective-permute-start | bytes 393224 | tf_op jit(solution)/shard_map/ppermute | solution.py:59
  102.4 8.7 %collective-permute-start.16 = (bf16[4,128,128]{2,1,0:T(8,128)(2,1)S(1)}, bf16[4,128,128]{2,1,0:T(8,128)(2,1)S(1)}, u32[]{:S(2)}, u32[]{:S(2)}) collective-permute-start(bf16[4,128,128]{2,1,0:T(8,128)(2,1)S(1)} %fusion.3), channel_id=1, source_target_pairs={{0,2},{2,0},{4,6},{6,4},{1,3},{3,1},{5,7},{7,5},{8,10},{10,8},{12,... | collective-permute-start | bytes 393224 | tf_op jit(solution)/shard_map/ppermute | solution.py:59
  107.3 14.6 %collective-permute-start.22 = (bf16[4,4,128,128]{3,2,1,0:T(8,128)(2,1)S(1)}, bf16[4,4,128,128]{3,2,1,0:T(8,128)(2,1)S(1)}, u32[]{:S(2)}, u32[]{:S(2)}) collective-permute-start(bf16[4,4,128,128]{3,2,1,0:T(8,128)(2,1)S(1)} %pad_maximum_fusion.rest_0_), channel_id=1, source_target_pairs={{0,1},{1,0},{2,3},{3,2},{4,5},{5,4},{6,7},{7,6},{8,9},{9,8},{10,11... | collective-permute-start | bytes 1572872 | tf_op jit(solution)/shard_map/ppermute | solution.py:59
  111.2 8.3 %copy-start.7 = (f32[128,2048]{1,0:T(8,128)S(1)}, f32[128,2048]{1,0:T(8,128)}, u32[]{:S(2)}) copy-start(f32[128,2048]{1,0:T(8,128)} %get-tuple-element.56.rest_0_) | copy-start | bytes 3145732
  111.2 8.3 %copy-start.18 = (bf16[64,2048]{1,0:T(8,128)(2,1)S(1)}, bf16[64,2048]{1,0:T(8,128)(2,1)}, u32[]{:S(2)}) copy-start(bf16[64,2048]{1,0:T(8,128)(2,1)} %copy-done.17) | copy-start | bytes 786436
  111.3 1.4 %collective-permute-start.23 = (bf16[4,128,128]{2,1,0:T(8,128)(2,1)S(1)}, bf16[4,128,128]{2,1,0:T(8,128)(2,1)S(1)}, u32[]{:S(2)}, u32[]{:S(2)}) collective-permute-start(bf16[4,128,128]{2,1,0:T(8,128)(2,1)S(1)} %add_convert_fusion.low_ref.rest_0_), channel_id=1, source_target_pairs={{0,1},{1,0},{2,3},{3,2},{4,5},{5,4},{6,7},{7,6},{8,9},{9,8},{10,11... | collective-permute-start | bytes 393224 | tf_op jit(solution)/shard_map/ppermute | solution.py:59
  112.7 9.3 %copy-start.5 = (f32[1024,1024]{1,0:T(8,128)S(1)}, f32[1024,1024]{1,0:T(8,128)}, u32[]{:S(2)}) copy-start(f32[1024,1024]{1,0:T(8,128)} %copy-done.4) | copy-start | bytes 12582916
  114.9 21.5 %collective-permute-start.26 = (bf16[8,16,256]{2,1,0:T(8,128)(2,1)S(1)}, bf16[8,16,256]{2,1,0:T(8,128)(2,1)S(1)}, u32[]{:S(2)}, u32[]{:S(2)}) collective-permute-start(bf16[8,16,256]{2,1,0:T(8,128)(2,1)S(1)} %get-tuple-element.60), channel_id=1, source_target_pairs={{0,24},{8,0},{16,8},{24,16},{1,25},{9,1},{17,9},{25,17},{2,26},{10... | collective-permute-start | bytes 196616 | tf_op jit(solution)/shard_map/ppermute | solution.py:38
  118.4 18.0 %collective-permute-start.25 = (bf16[8,16,256]{2,1,0:T(8,128)(2,1)S(1)}, bf16[8,16,256]{2,1,0:T(8,128)(2,1)S(1)}, u32[]{:S(2)}, u32[]{:S(2)}) collective-permute-start(bf16[8,16,256]{2,1,0:T(8,128)(2,1)S(1)} %get-tuple-element.61), channel_id=1, source_target_pairs={{0,16},{8,24},{16,0},{24,8},{1,17},{9,25},{17,1},{25,9},{2,18},{10... | collective-permute-start | bytes 196616 | tf_op jit(solution)/shard_map/ppermute | solution.py:38
  118.4 18.0 %collective-permute-start.24 = (bf16[8,16,256]{2,1,0:T(8,128)(2,1)S(1)}, bf16[8,16,256]{2,1,0:T(8,128)(2,1)S(1)}, u32[]{:S(2)}, u32[]{:S(2)}) collective-permute-start(bf16[8,16,256]{2,1,0:T(8,128)(2,1)S(1)} %get-tuple-element.62), channel_id=1, source_target_pairs={{0,8},{8,16},{16,24},{24,0},{1,9},{9,17},{17,25},{25,1},{2,10},{10... | collective-permute-start | bytes 196616 | tf_op jit(solution)/shard_map/ppermute | solution.py:38
  125.3 0.8 copy-start.13
  131.1 1.0 copy-start.14

commit v10 on v9

--- a/solution.py
+++ b/solution.py
@@ -11,6 +11,7 @@
 RANKS = 2 * ADAPTER_RANK
 WIDTH = 2 * KEY_WIDTH
 VMEM_LIMIT = 24 * 1024 * 1024
+VMEM_MOST = 60 * 1024 * 1024
 LAST_BOTH = (((1,), (1,)), ((), ()))
 FIRST_BOTH = (((0,), (0,)), ((), ()))
 SMEM = pl.BlockSpec(memory_space=pltpu.SMEM)
@@ -19,10 +20,10 @@
 ANY = pl.BlockSpec(memory_space=pl.ANY)
 
 
-def call(kernel, name, **more):
+def call(kernel, name, vmem=VMEM_LIMIT, **more):
     return pl.pallas_call(
         kernel,
-        compiler_params=pltpu.CompilerParams(vmem_limit_bytes=VMEM_LIMIT),
+        compiler_params=pltpu.CompilerParams(vmem_limit_bytes=vmem),
         cost_estimate=pl.CostEstimate(flops=1024, bytes_accessed=1024, transcendentals=0),
         name=name,
         **more,
@@ -82,24 +83,46 @@
     rides = up_rides(adapter_up)
     total = first_up + (up_rows * width // ranks if rides else 0)
 
-    def kernel(at_ref, down_ref, up_ref, out_ref):
-        data = pl.program_id(0)
-        for block in range(blocks_dev):
-            here = slice(block * down_rows, (block + 1) * down_rows)
-            out_ref[0, here] = down_ref[slot_of(at_ref, data, block)]
-        if rides:
-            slot = slot_of(at_ref, data, at_ref[3])
-            for n in range(width // ranks):
+    def kernel(at_ref, down_ref, up_ref, out_ref, rows, tiles, down_sem, up_sem, out_sem):
+        downs, ups, outs = [], [], []
+        for data in range(data_count):
+            downs.append([])
+            for block in range(blocks_dev):
+                here = rows.at[data, pl.ds(block * down_rows, down_rows)]
+                slot = slot_of(at_ref, data, block)
+                downs[data].append(
+                    pltpu.make_async_copy(down_ref.at[slot], here, down_sem.at[data, block])
+                )
+            if rides:
+                slot = slot_of(at_ref, data, at_ref[3])
+                ups.append(pltpu.make_async_copy(up_ref.at[slot], tiles.at[data], up_sem.at[data]))
+            outs.append(pltpu.make_async_copy(rows.at[data], out_ref.at[data], out_sem.at[data]))
+            for copy in downs[data] + ups[data:]:
+                copy.start()
+        for data in range(data_count):
+            for copy in downs[data] + ups[data : data + 1]:
+                copy.wait()
+            for n in range(width // ranks if rides else 0):
                 first = first_up + n * up_rows
-                out_ref[0, first : first + up_rows] = up_ref[slot, :, n * ranks : (n + 1) * ranks]
+                rows[data, first : first + up_rows] = tiles[data, :, n * ranks : (n + 1) * ranks]
+            outs[data].start()
+        for copy in outs:
+            copy.wait()
 
     return call(
         kernel,
         "pick_rows",
-        grid=(data_count,),
+        VMEM_MOST,
         out_shape=pltpu.HBM((data_count, total, ranks), adapter_down.dtype),
-        in_specs=[SMEM, VMEM, VMEM],
-        out_specs=pl.BlockSpec((1, total, ranks), lambda d: (d, 0, 0)),
+        in_specs=[SMEM, HBM, HBM],
+        out_specs=HBM,
+        scratch_shapes=[
+            pltpu.VMEM((data_count, total, ranks), adapter_down.dtype),
+            pltpu.VMEM((data_count, up_rows, width), adapter_up.dtype),
+            pltpu.SemaphoreType.DMA((data_count, blocks_dev)),
+            pltpu.SemaphoreType.DMA((data_count,)),
+            pltpu.SemaphoreType.DMA((data_count,)),
+        ],
     )(at, adapter_down, adapter_up)
 
 
@@ -256,7 +279,13 @@
     blocks_dev = tok_dev // BLOCK
 
     def kernel(at_ref, x_ref, *rest):
-        grad_refs, (out_ref, grad) = rest[:tensor_count], rest[tensor_count:]
+        grad_refs, (out_ref, grad, x, sems) = rest[:tensor_count], rest[tensor_count:]
+        copies = [
+            pltpu.make_async_copy(x_ref.at[data], x.at[data], sems.at[data])
+            for data in range(data_count)
+        ]
+        for copy in copies:
+            copy.start()
         for s in range(tensor_count):
             core = came_from(at_ref[2], s, tensor_count)
             for k in range(pipe_count):
@@ -267,20 +296,26 @@
                     grad[data, pl.ds(first, rows)] = grad_refs[s][k, m]
         out_ref[...] = jnp.zeros(out_ref.shape, out_ref.dtype)
         for data in range(data_count):
+            copies[data].wait()
             for block in range(blocks_dev):
                 slot = slot_of(at_ref, data, block)
                 here = slice(block * BLOCK, (block + 1) * BLOCK)
                 out_ref[slot] += jnp.dot(
-                    x_ref[data, :, here], grad[data, here], preferred_element_type=jnp.float32
+                    x[data, :, here], grad[data, here], preferred_element_type=jnp.float32
                 )
 
     return call(
         kernel,
         "grad_down",
-        in_specs=[SMEM, VMEM] + [VMEM] * tensor_count,
+        VMEM_MOST,
+        in_specs=[SMEM, HBM] + [VMEM] * tensor_count,
         out_specs=VMEM,
         out_shape=jax.ShapeDtypeStruct((slots, down_rows, RANKS), jnp.float32),
-        scratch_shapes=[pltpu.VMEM((data_count, tok_dev, RANKS), jnp.bfloat16)],
+        scratch_shapes=[
+            pltpu.VMEM((data_count, tok_dev, RANKS), jnp.bfloat16),
+            pltpu.VMEM(x_features.shape, jnp.bfloat16),
+            pltpu.SemaphoreType.DMA((data_count,)),
+        ],
     )(at, x_features, *grad_pieces)
 
 
@@ -463,8 +498,8 @@
         up = lax.all_to_all(pick_up(at, slot_of, adapter_up, data_count), "dp", 0, 0, tiled=True)
         up = up.reshape(ADAPTER_RANK, WIDTH)
 
-    cot_send, a_send = lax.optimization_barrier((cotangent, a_send))
-    cot_chips, base_tokens, x_tokens = gather_chips(cot_send, tokens)
+    behind, a_send = lax.optimization_barrier((tokens, a_send))
+    cot_chips, base_tokens, x_tokens = gather_chips(cotangent, behind)
     cot_chips = [cotangent] + cot_chips
 
     tokens_by_group = base_tokens.reshape(pipe_count, tensor_count, rows, feature_count)

time: 139 us -> 138 us (level)
  local copies, waits for them, and re-layouts: 23.2 us -> 19.9 us
  Pallas kernels: 32.9 us -> 35.6 us
    all_to_all x1, waiting for transfers between devices: 5.9 us -> 11.4 us  [body(): a_recv = lax.all_to_all(a_send, 'dp', 0, 0, tiled=True)]
    ppermute x21, waiting for transfers between devices: 30.7 us -> 25.3 us  [swap(): lax.ppermute(piece, axis, [(i, partner(i, k, count)) for i in range(count)])]
    unnamed x39, local copies, waits for them, and re-layouts: 16.8 us -> 12.9 us
    pallas_call x2, Pallas kernels: 6.72 us -> 9.36 us  [the longest x1 5.14 us: grad_down(): call(kernel, 'grad_down', VMEM_MOST, in_specs=[SMEM, HBM] + [VMEM] * tens...]
  transfers between devices with their start and end apart: 29 -> 29, of which waited for: 16 -> 16; matrix products, arithmetic and copies ran while one was open for 6% -> 7% of each run, Pallas kernels for 21% -> 25%
where the time goes in v10:
time: 138 us; the launch traced here: 137 us
  waiting for transfers between devices  46.8 us (34%)
  Pallas kernels  35.6 us (26%)
  starting transfers between devices  31.9 us (23%)
  local copies, waits for them, and re-layouts  19.9 us (14%)
  other arithmetic  2.25 us (2%)
    ppermute x21, waiting for transfers between devices, swap(): lax.ppermute(piece, axis, [(i, partner(i, k, count)) for i in range(count)])  25.3 us
    ppermute x21, starting transfers between devices, swap(): lax.ppermute(piece, axis, [(i, partner(i, k, count)) for i in range(count)])  15.8 us
    unnamed x39, local copies, waits for them, and re-layouts  12.9 us
    all_to_all x1, waiting for transfers between devices, body(): a_recv = lax.all_to_all(a_send, 'dp', 0, 0, tiled=True)  11.4 us
    pallas_call x1, Pallas kernels, cotangent_product(): call(kernel, 'cotangent_product', grid=(depth // tile,), in_specs=[SMEM,...  7.92 us
    pallas_call x2, Pallas kernels, base_product(): call(kernel, 'base_product', grid_spec=pltpu.PrefetchScalarGridSpec(num_s...  7.22 us
    ppermute x6, starting transfers between devices, shift(): lax.ppermute(piece, axis, [(i, (i + k) % count) for i in range(count)])  6.77 us
    pallas_call x1, Pallas kernels, grad_down(): call(kernel, 'grad_down', VMEM_MOST, in_specs=[SMEM, HBM] + [VMEM] * tens...  5.14 us
  transfers between devices with their start and end apart: 29, of which 16 were waited for; matrix products, arithmetic and copies ran while one was open for 7% of the time, Pallas kernels for 25%

profile of v10, /device:TPU:0, one launch (start us, length us, event | category | flops | bytes accessed | tf_op | source)
XLA Modules:
  0.0 137.3 jit_solution(12591568670460039207)
XLA Ops:
  0.6 3.0 %collective-permute-start.1 = (bf16[128,2048]{1,0:T(8,128)(2,1)}, bf16[128,2048]{1,0:T(8,128)(2,1)S(1)}, u32[]{:S(2)}, u32[]{:S(2)}) collective-permute-start(bf16[128,2048]{1,0:T(8,128)(2,1)} %rest_2_.1), channel_id=1, source_target_pairs={{0,4},{2,6},{4,0},{6,2},{1,5},{3,7},{5,1},{7,3},{8,12},{10,14},{12... | collective-permute-start | bytes 1572872 | tf_op jit(solution)/shard_map/ppermute | solution.py:60
  3.7 1.5 %collective-permute-start = (bf16[128,2048]{1,0:T(8,128)(2,1)}, bf16[128,2048]{1,0:T(8,128)(2,1)}, u32[]{:S(2)}, u32[]{:S(2)}) collective-permute-start(bf16[128,2048]{1,0:T(8,128)(2,1)} %rest_2_.1), channel_id=1, source_target_pairs={{0,2},{2,0},{4,6},{6,4},{1,3},{3,1},{5,7},{7,5},{8,10},{10,8},{12,... | collective-permute-start | bytes 1572872 | tf_op jit(solution)/shard_map/ppermute | solution.py:60
  5.2 1.3 concatenate.6.at_ref
  6.5 4.2 %pick_rows.1 = bf16[4,2304,128]{2,1,0:T(8,128)(2,1)} custom-call(s32[60]{0:T(128)} %concatenate.6.at_ref, bf16[24,256,128]{2,1,0:T(8,128)(2,1)} %down_ref.1, bf16[24,16,2048]{2,1,0:T(8,128)(2,1)} %up_ref.1), custom_call_target="tpu_custom_call" | custom-call | flops 1024 | bytes 1024 | tf_op jit(solution)/shard_map/pick_rows/pallas_call | solution.py:112
  10.7 4.9 %all-to-all-start = ((bf16[4,2304,128]{2,1,0:T(8,128)(2,1)}), bf16[4,2304,128]{2,1,0:T(8,128)(2,1)S(1)}, u32[]{:S(2)}, u32[]{:S(2)}) async-start(bf16[4,2304,128]{2,1,0:T(8,128)(2,1)} %pick_rows.1), calls=%async_computation | async-start | bytes 4718592 | tf_op jit(solution)/shard_map/all_to_all | solution.py:495
  15.6 0.2 collective-permute-done.1.rest_2_.rest_4_
  15.8 1.6 %collective-permute-done.rest_1_.rest_3_ = bf16[128,2048]{1,0:T(8,128)(2,1)} collective-permute-done((bf16[128,2048]{1,0:T(8,128)(2,1)}, bf16[128,2048]{1,0:T(8,128)(2,1)}, u32[]{:S(2)}, u32[]{:S(2)}) %collective-permute-start) | collective-permute-done | bytes 524320 | tf_op jit(solution)/shard_map/ppermute | solution.py:60
  17.4 2.2 %copy-done = bf16[1024,2048]{1,0:T(8,128)(2,1)S(1)} copy-done((bf16[1024,2048]{1,0:T(8,128)(2,1)S(1)}, bf16[1024,2048]{1,0:T(8,128)(2,1)}, u32[]{:S(2)}) %copy-start) | copy-done | bytes 4194328
  19.6 1.6 %copy-done.2 = bf16[1024,1024]{1,0:T(8,128)(2,1)S(1)} copy-done((bf16[1024,1024]{1,0:T(8,128)(2,1)S(1)}, bf16[1024,1024]{1,0:T(8,128)(2,1)}, u32[]{:S(2)}) %copy-start.2) | copy-done | bytes 2097176
  21.1 3.6 %base_product.3 = bf16[1,4,128,2048]{3,2,1,0:T(8,128)(2,1)S(1)} custom-call(s32[60]{0:T(128)S(1)} %copy-done.17, bf16[4,2,128,1024]{3,2,1,0:T(8,128)(2,1)S(1)} %bitcast.73, bf16[1024,2048]{1,0:T(8,128)(2,1)S(1)} %copy-done), custom_call_target="tpu_custom_call" | custom-call | flops 1024 | bytes 1024 | tf_op jit(solution)/shard_map/base_product/pallas_call | solution.py:144
  24.8 0.1 collective-permute-start.8
  24.9 1.6 %collective-permute-start.2 = (bf16[64,2048]{1,0:T(8,128)(2,1)S(1)}, bf16[64,2048]{1,0:T(8,128)(2,1)S(1)}, u32[]{:S(2)}, u32[]{:S(2)}) collective-permute-start(bf16[64,2048]{1,0:T(8,128)(2,1)S(1)} %slice.52), channel_id=1, source_target_pairs={{0,2},{2,0},{4,6},{6,4},{1,3},{3,1},{5,7},{7,5},{8,10},{10,8},{12,... | collective-permute-start | bytes 786440 | tf_op jit(solution)/shard_map/ppermute | solution.py:60
  26.4 1.0 slice.53
  27.4 0.6 collective-permute-start.3
  28.0 0.5 collective-permute-start.5
  28.5 3.6 %base_product.2 = bf16[1,4,128,2048]{3,2,1,0:T(8,128)(2,1)S(1)} custom-call(s32[60]{0:T(128)S(1)} %copy-done.17, bf16[4,2,128,1024]{3,2,1,0:T(8,128)(2,1)S(1)} %bitcast.74, bf16[1024,2048]{1,0:T(8,128)(2,1)S(1)} %copy-done), custom_call_target="tpu_custom_call" | custom-call | flops 1024 | bytes 1024 | tf_op jit(solution)/shard_map/base_product/pallas_call | solution.py:144
  32.1 1.5 %collective-permute-done.2 = bf16[64,2048]{1,0:T(8,128)(2,1)S(1)} collective-permute-done((bf16[64,2048]{1,0:T(8,128)(2,1)S(1)}, bf16[64,2048]{1,0:T(8,128)(2,1)S(1)}, u32[]{:S(2)}, u32[]{:S(2)}) %collective-permute-start.2) | collective-permute-done | bytes 262176 | tf_op jit(solution)/shard_map/ppermute | solution.py:60
  33.6 0.7 constant_dynamic-update-slice_fusion.1
  34.4 1.5 %collective-permute-done.3 = bf16[64,2048]{1,0:T(8,128)(2,1)S(1)} collective-permute-done((bf16[64,2048]{1,0:T(8,128)(2,1)S(1)}, bf16[64,2048]{1,0:T(8,128)(2,1)S(1)}, u32[]{:S(2)}, u32[]{:S(2)}) %collective-permute-start.3) | collective-permute-done | bytes 262176 | tf_op jit(solution)/shard_map/ppermute | solution.py:60
  35.9 0.7 constant_dynamic-update-slice_fusion.rest_3_.rest_5_
  36.6 2.0 %convert_add_fusion = (f32[128,2048]{1,0:T(8,128)}, bf16[128,2048]{1,0:T(8,128)(2,1)}, bf16[128,2048]{1,0:T(8,128)(2,1)}, bf16[128,2048]{1,0:T(8,128)(2,1)}) fusion(bf16[4,128,2048]{2,1,0:T(8,128)(2,1)S(1)} %collective-permute-done.8, bf16[1,4,128,2048]{3,2,1,0:T(8,128)(2,1)S(1)} %base_product.2), kind=kLoop, calls=%fused_computation | loop fusion | flops 3932160 | bytes 6815744 | tf_op jit(solution)/shard_map/add | solution.py:510
  38.6 0.5 collective-permute-start.10
  39.2 0.8 copy-done.11
  40.0 0.5 collective-permute-start.9
  40.4 3.9 %copy.11 = bf16[1024,1024]{1,0:T(8,128)(2,1)} copy(bf16[1024,1024]{0,1:T(8,128)(2,1)} %bitcast.72) | data formatting | bytes 4194304 | tf_op jit(solution)/shard_map/transpose | solution.py:521
  44.4 2.2 %copy-done.1 = bf16[1024,2048]{1,0:T(8,128)(2,1)S(1)} copy-done((bf16[1024,2048]{1,0:T(8,128)(2,1)S(1)}, bf16[1024,2048]{1,0:T(8,128)(2,1)}, u32[]{:S(2)}) %copy-start.1) | copy-done | bytes 4194328
  46.6 1.0 copy-done.12
  47.6 7.9 %cotangent_product.1.base_ref = f32[1024,1024]{1,0:T(8,128)S(1)} custom-call(s32[60]{0:T(128)S(1)} %copy-done.17, bf16[1024,2048]{1,0:T(8,128)(2,1)S(1)} %copy-done.1, bf16[128,2048]{1,0:T(8,128)(2,1)S(1)} %copy-done.7, bf16[128,2048]{1,0:T(8,128)(2,1)} %collective-permute-done.rest_1_.rest_3_, bf16[128,2048]{1,0:T(8,128)(2,1)S(1)} %collective-permute-done.1.rest_2_.rest_4_, ...), custom_call_target="tpu_custom_call" | custom-call | flops 1024 | bytes 1024 | tf_op jit(solution)/shard_map/cotangent_product/pallas_call | solution.py:217
  55.5 2.0 %copy-done.4 = f32[1024,1024]{1,0:T(8,128)} copy-done((f32[1024,1024]{1,0:T(8,128)}, f32[1024,1024]{1,0:T(8,128)S(1)}, u32[]{:S(2)}) %copy-start.4) | copy-done | bytes 4194328
  57.5 11.4 %all-to-all-done.came_ref.a_ref = bf16[4,2304,128]{2,1,0:T(8,128)(2,1)S(1)} async-done(((bf16[4,2304,128]{2,1,0:T(8,128)(2,1)}), bf16[4,2304,128]{2,1,0:T(8,128)(2,1)S(1)}, u32[]{:S(2)}, u32[]{:S(2)}) %all-to-all-start) | async-done | bytes 2359328 | tf_op jit(solution)/shard_map/all_to_all | solution.py:495
  68.9 0.4 own_rows.1
  69.3 1.5 %collective-permute-start.14 = (bf16[128,128]{1,0:T(8,128)(2,1)S(1)}, bf16[128,128]{1,0:T(8,128)(2,1)S(1)}, u32[]{:S(2)}, u32[]{:S(2)}) collective-permute-start(bf16[128,128]{1,0:T(8,128)(2,1)S(1)} %get-tuple-element.40), channel_id=1, source_target_pairs={{0,24},{8,0},{16,8},{24,16},{1,25},{9,1},{17,9},{25,17},{2,26},{10... | collective-permute-start | bytes 98312 | tf_op jit(solution)/shard_map/ppermute | solution.py:39
  70.8 0.6 collective-permute-start.12
  71.5 1.8 %collective-permute-done.14 = bf16[128,128]{1,0:T(8,128)(2,1)S(1)} collective-permute-done((bf16[128,128]{1,0:T(8,128)(2,1)S(1)}, bf16[128,128]{1,0:T(8,128)(2,1)S(1)}, u32[]{:S(2)}, u32[]{:S(2)}) %collective-permute-start.14) | collective-permute-done | bytes 32800 | tf_op jit(solution)/shard_map/ppermute | solution.py:39
  73.3 2.7 %collective-permute-done.13 = bf16[128,128]{1,0:T(8,128)(2,1)S(1)} collective-permute-done((bf16[128,128]{1,0:T(8,128)(2,1)S(1)}, bf16[128,128]{1,0:T(8,128)(2,1)S(1)}, u32[]{:S(2)}, u32[]{:S(2)}) %collective-permute-start.13) | collective-permute-done | bytes 32800 | tf_op jit(solution)/shard_map/ppermute | solution.py:39
  76.0 0.6 collective-permute-done.12
  76.5 4.5 %all-to-all-start.1 = ((bf16[4,256,1024]{2,1,0:T(8,128)(2,1)}), bf16[4,256,1024]{2,1,0:T(8,128)(2,1)}, u32[]{:S(2)}, u32[]{:S(2)}) async-start(bf16[4,256,1024]{2,1,0:T(8,128)(2,1)} %bitcast.77), calls=%async_computation.1 | async-start | bytes 4194304 | tf_op jit(solution)/shard_map/all_to_all | solution.py:529
  81.0 0.5 collective-permute-start.11
  81.5 11.5 %collective-permute-done.11.rest_3_ = bf16[128,2048]{1,0:T(8,128)(2,1)S(1)} collective-permute-done((bf16[128,2048]{1,0:T(8,128)(2,1)}, bf16[128,2048]{1,0:T(8,128)(2,1)S(1)}, u32[]{:S(2)}, u32[]{:S(2)}) %collective-permute-start.11) | collective-permute-done | bytes 524320 | tf_op jit(solution)/shard_map/ppermute | solution.py:60
  93.1 1.6 %copy-done.3 = bf16[1024,1024]{1,0:T(8,128)(2,1)S(1)} copy-done((bf16[1024,1024]{1,0:T(8,128)(2,1)S(1)}, bf16[1024,1024]{1,0:T(8,128)(2,1)}, u32[]{:S(2)}) %copy-start.3) | copy-done | bytes 2097176
  94.7 1.3 low_product.1
  96.0 0.1 collective-permute-start.15
  96.1 0.6 collective-permute-start.20
  96.6 0.5 collective-permute-start.19
  97.2 2.4 %collective-permute-start.21 = (bf16[4,128,128]{2,1,0:T(8,128)(2,1)S(1)}, bf16[4,128,128]{2,1,0:T(8,128)(2,1)S(1)}, u32[]{:S(2)}, u32[]{:S(2)}) collective-permute-start(bf16[4,128,128]{2,1,0:T(8,128)(2,1)S(1)} %get-tuple-element.65), channel_id=1, source_target_pairs={{0,6},{2,4},{4,2},{6,0},{1,7},{3,5},{5,3},{7,1},{8,14},{10,12},{12... | collective-permute-start | bytes 393224 | tf_op jit(solution)/shard_map/ppermute | solution.py:60
  99.7 0.5 collective-permute-start.18
  100.2 1.5 %collective-permute-start.17 = (bf16[4,128,128]{2,1,0:T(8,128)(2,1)S(1)}, bf16[4,128,128]{2,1,0:T(8,128)(2,1)S(1)}, u32[]{:S(2)}, u32[]{:S(2)}) collective-permute-start(bf16[4,128,128]{2,1,0:T(8,128)(2,1)S(1)} %fusion.3), channel_id=1, source_target_pairs={{0,4},{2,6},{4,0},{6,2},{1,5},{3,7},{5,1},{7,3},{8,12},{10,14},{12... | collective-permute-start | bytes 393224 | tf_op jit(solution)/shard_map/ppermute | solution.py:60
  101.7 0.3 collective-permute-done.20
  102.0 1.2 collective-permute-start.16
  103.2 3.6 %collective-permute-done.21 = bf16[4,128,128]{2,1,0:T(8,128)(2,1)S(1)} collective-permute-done((bf16[4,128,128]{2,1,0:T(8,128)(2,1)S(1)}, bf16[4,128,128]{2,1,0:T(8,128)(2,1)S(1)}, u32[]{:S(2)}, u32[]{:S(2)}) %collective-permute-start.21) | collective-permute-done | bytes 131104 | tf_op jit(solution)/shard_map/ppermute | solution.py:60
  107.0 2.6 %collective-permute-done.18 = bf16[4,128,128]{2,1,0:T(8,128)(2,1)S(1)} collective-permute-done((bf16[4,128,128]{2,1,0:T(8,128)(2,1)S(1)}, bf16[4,128,128]{2,1,0:T(8,128)(2,1)S(1)}, u32[]{:S(2)}, u32[]{:S(2)}) %collective-permute-start.18) | collective-permute-done | bytes 131104 | tf_op jit(solution)/shard_map/ppermute | solution.py:60
  109.6 1.0 collective-permute-done.17
  110.6 0.1 collective-permute-done.16
  110.7 0.1 add_convert_fusion.low_ref.rest_0_
  110.9 1.3 collective-permute-done.23.rest_1_
  112.2 2.2 %grad_up_pieces.1 = bf16[4,8,16,256]{3,2,1,0:T(8,128)(2,1)S(1)} custom-call(s32[60]{0:T(128)S(1)} %copy-done.17, bf16[4,128,128]{2,1,0:T(8,128)(2,1)S(1)} %add_convert_fusion.low_ref.rest_0_, bf16[4,128,128]{2,1,0:T(8,128)(2,1)S(1)} %collective-permute-done.23.rest_1_, bf16[128,2048]{1,0:T(8,128)(2,1)S(1)} %copy-done.7, ...), custom_call_target="tpu_custom_call" | custom-call | flops 1024 | bytes 1024 | tf_op jit(solution)/shard_map/grad_up_pieces/pallas_call | solution.py:368
  114.5 3.5 %collective-permute-start.26 = (bf16[8,16,256]{2,1,0:T(8,128)(2,1)S(1)}, bf16[8,16,256]{2,1,0:T(8,128)(2,1)S(1)}, u32[]{:S(2)}, u32[]{:S(2)}) collective-permute-start(bf16[8,16,256]{2,1,0:T(8,128)(2,1)S(1)} %get-tuple-element.60), channel_id=1, source_target_pairs={{0,24},{8,0},{16,8},{24,16},{1,25},{9,1},{17,9},{25,17},{2,26},{10... | collective-permute-start | bytes 196616 | tf_op jit(solution)/shard_map/ppermute | solution.py:39
  118.0 1.1 collective-permute-start.24
  119.1 2.4 %keys_and_values.1 = bf16[128,2048]{1,0:T(8,128)(2,1)} custom-call(s32[60]{0:T(128)S(1)} %copy-done.17, bf16[4,128,128]{2,1,0:T(8,128)(2,1)S(1)} %add_convert_fusion.low_ref.rest_0_, bf16[64,2048]{1,0:T(8,128)(2,1)S(1)} %copy-done.16, f32[128,2048]{1,0:T(8,128)S(1)} %copy-done.8, bf16[128,2048]{1,0:T(8,128)(2,1)} %collective-permute-done.9.rest_1_, ...), custom_call_target="tpu_custom_call" | custom-call | flops 1024 | bytes 1024 | tf_op jit(solution)/shard_map/keys_and_values/pallas_call | solution.py:461
  121.5 3.3 %input_gradient.1 = bf16[1024,1024]{1,0:T(8,128)(2,1)} custom-call(s32[60]{0:T(128)S(1)} %copy-done.17, f32[1024,1024]{1,0:T(8,128)S(1)} %copy-done.5, bf16[4,2304,128]{2,1,0:T(8,128)(2,1)S(1)} %all-to-all-done.came_ref.a_ref, bf16[4,4,128,128]{3,2,1,0:T(8,128)(2,1)S(1)} %pad_maximum_fusion.rest_0_, bf16[4,4,128,128]{3,2,1,0:T(8,128)(2,1)S(1)} %collective-permute-done.22.rest_1_), custom_call_target="tpu_custom_call" | custom-call | flops 1024 | bytes 1024 | tf_op jit(solution)/shard_map/input_gradient/pallas_call | solution.py:259
  124.9 0.8 copy-done.14
  125.7 5.0 %all-to-all-done.1.x_ref = bf16[4,256,1024]{2,1,0:T(8,128)(2,1)} async-done(((bf16[4,256,1024]{2,1,0:T(8,128)(2,1)}), bf16[4,256,1024]{2,1,0:T(8,128)(2,1)}, u32[]{:S(2)}, u32[]{:S(2)}) %all-to-all-start.1) | async-done | bytes 2097184 | tf_op jit(solution)/shard_map/all_to_all | solution.py:529
  130.7 5.1 %grad_down.1 = f32[24,256,128]{2,1,0:T(8,128)} custom-call(s32[60]{0:T(128)} %concatenate.6.at_ref, bf16[4,256,1024]{2,1,0:T(8,128)(2,1)} %all-to-all-done.1.x_ref, bf16[4,4,128,128]{3,2,1,0:T(8,128)(2,1)} %copy-done.6, bf16[4,4,128,128]{3,2,1,0:T(8,128)(2,1)} %copy-done.14), custom_call_target="tpu_custom_call" | custom-call | flops 1024 | bytes 1024 | tf_op jit(solution)/shard_map/grad_down/pallas_call | solution.py:307
  135.9 1.5 %grad_up.1 = f32[24,16,256]{2,1,0:T(8,128)} custom-call(s32[60]{0:T(128)S(1)} %copy-done.18, bf16[8,16,256]{2,1,0:T(8,128)(2,1)S(1)} %get-tuple-element.52.rest_0_, bf16[8,16,256]{2,1,0:T(8,128)(2,1)S(1)} %collective-permute-done.24.rest_1_, bf16[8,16,256]{2,1,0:T(8,128)(2,1)S(1)} %collective-permute-done.25.rest_2_, ...), custom_call_target="tpu_custom_call" | custom-call | flops 1024 | bytes 1024 | tf_op jit(solution)/shard_map/grad_up/pallas_call | solution.py:395
  (56 shorter events, 0.4 us)
Async XLA Ops:
  0.6 15.2 %collective-permute-start.1 = (bf16[128,2048]{1,0:T(8,128)(2,1)}, bf16[128,2048]{1,0:T(8,128)(2,1)S(1)}, u32[]{:S(2)}, u32[]{:S(2)}) collective-permute-start(bf16[128,2048]{1,0:T(8,128)(2,1)} %rest_2_.1), channel_id=1, source_target_pairs={{0,4},{2,6},{4,0},{6,2},{1,5},{3,7},{5,1},{7,3},{8,12},{10,14},{12... | collective-permute-start | bytes 1572872 | tf_op jit(solution)/shard_map/ppermute | solution.py:60
  3.7 13.7 %collective-permute-start = (bf16[128,2048]{1,0:T(8,128)(2,1)}, bf16[128,2048]{1,0:T(8,128)(2,1)}, u32[]{:S(2)}, u32[]{:S(2)}) collective-permute-start(bf16[128,2048]{1,0:T(8,128)(2,1)} %rest_2_.1), channel_id=1, source_target_pairs={{0,2},{2,0},{4,6},{6,4},{1,3},{3,1},{5,7},{7,5},{8,10},{10,8},{12,... | collective-permute-start | bytes 1572872 | tf_op jit(solution)/shard_map/ppermute | solution.py:60
  10.7 6.6 %copy-start.17 = (s32[60]{0:T(128)S(1)}, s32[60]{0:T(128)}, u32[]{:S(2)}) copy-start(s32[60]{0:T(128)} %concatenate.6.at_ref) | copy-start | bytes 724
  10.7 58.1 %all-to-all-start = ((bf16[4,2304,128]{2,1,0:T(8,128)(2,1)}), bf16[4,2304,128]{2,1,0:T(8,128)(2,1)S(1)}, u32[]{:S(2)}, u32[]{:S(2)}) async-start(bf16[4,2304,128]{2,1,0:T(8,128)(2,1)} %pick_rows.1), calls=%async_computation | async-start | bytes 4718592 | tf_op jit(solution)/shard_map/all_to_all | solution.py:495
  15.8 28.6 %copy-start.9 = (bf16[128,2048]{1,0:T(8,128)(2,1)}, bf16[128,2048]{1,0:T(8,128)(2,1)S(1)}, u32[]{:S(2)}) copy-start(bf16[128,2048]{1,0:T(8,128)(2,1)S(1)} %collective-permute-done.1.rest_2_.rest_4_) | copy-start | bytes 1572868
  17.4 2.2 %copy-start = (bf16[1024,2048]{1,0:T(8,128)(2,1)S(1)}, bf16[1024,2048]{1,0:T(8,128)(2,1)}, u32[]{:S(2)}) copy-start(bf16[1024,2048]{1,0:T(8,128)(2,1)} %w_ref.5) | copy-start | bytes 12582916
  19.6 1.6 %copy-start.2 = (bf16[1024,1024]{1,0:T(8,128)(2,1)S(1)}, bf16[1024,1024]{1,0:T(8,128)(2,1)}, u32[]{:S(2)}) copy-start(bf16[1024,1024]{1,0:T(8,128)(2,1)} %x_ref.1) | copy-start | bytes 6291460
  21.1 6.8 %copy-start.7 = (bf16[128,2048]{1,0:T(8,128)(2,1)S(1)}, bf16[128,2048]{1,0:T(8,128)(2,1)}, u32[]{:S(2)}) copy-start(bf16[128,2048]{1,0:T(8,128)(2,1)} %rest_2_.1) | copy-start | bytes 1572868
  24.8 11.8 %collective-permute-start.8 = (bf16[4,128,2048]{2,1,0:T(8,128)(2,1)S(1)}, bf16[4,128,2048]{2,1,0:T(8,128)(2,1)S(1)}, u32[]{:S(2)}, u32[]{:S(2)}) collective-permute-start(bf16[4,128,2048]{2,1,0:T(8,128)(2,1)S(1)} %bitcast.75), channel_id=1, source_target_pairs={{0,1},{1,0},{2,3},{3,2},{4,5},{5,4},{6,7},{7,6},{8,9},{9,8},{10,11... | collective-permute-start | bytes 6291464 | tf_op jit(solution)/shard_map/ppermute | solution.py:60
  24.9 8.8 %collective-permute-start.2 = (bf16[64,2048]{1,0:T(8,128)(2,1)S(1)}, bf16[64,2048]{1,0:T(8,128)(2,1)S(1)}, u32[]{:S(2)}, u32[]{:S(2)}) collective-permute-start(bf16[64,2048]{1,0:T(8,128)(2,1)S(1)} %slice.52), channel_id=1, source_target_pairs={{0,2},{2,0},{4,6},{6,4},{1,3},{3,1},{5,7},{7,5},{8,10},{10,8},{12,... | collective-permute-start | bytes 786440 | tf_op jit(solution)/shard_map/ppermute | solution.py:60
  27.4 8.5 %collective-permute-start.3 = (bf16[64,2048]{1,0:T(8,128)(2,1)S(1)}, bf16[64,2048]{1,0:T(8,128)(2,1)S(1)}, u32[]{:S(2)}, u32[]{:S(2)}) collective-permute-start(bf16[64,2048]{1,0:T(8,128)(2,1)S(1)} %slice.53), channel_id=1, source_target_pairs={{0,4},{2,6},{4,0},{6,2},{1,5},{3,7},{5,1},{7,3},{8,12},{10,14},{12... | collective-permute-start | bytes 786440 | tf_op jit(solution)/shard_map/ppermute | solution.py:60
  28.0 11.2 %collective-permute-start.4 = (bf16[128,2048]{1,0:T(8,128)(2,1)S(1)}, bf16[128,2048]{1,0:T(8,128)(2,1)S(1)}, u32[]{:S(2)}, u32[]{:S(2)}) collective-permute-start(bf16[128,2048]{1,0:T(8,128)(2,1)S(1)} %copy-done.7), channel_id=1, source_target_pairs={{0,1},{1,0},{2,3},{3,2},{4,5},{5,4},{6,7},{7,6},{8,9},{9,8},{10,11... | collective-permute-start | bytes 1572872 | tf_op jit(solution)/shard_map/ppermute | solution.py:60
  28.0 16.4 %collective-permute-start.5 = (bf16[128,2048]{1,0:T(8,128)(2,1)}, bf16[128,2048]{1,0:T(8,128)(2,1)}, u32[]{:S(2)}, u32[]{:S(2)}) collective-permute-start(bf16[128,2048]{1,0:T(8,128)(2,1)} %collective-permute-done.rest_1_.rest_3_), channel_id=1, source_target_pairs={{0,1},{1,0},{2,3},{3,2},{4,5},{5,4},{6,7},{7,6},{8,9},{9,8},{10,11... | collective-permute-start | bytes 1572872 | tf_op jit(solution)/shard_map/ppermute | solution.py:60
  33.6 10.7 %collective-permute-start.6 = (bf16[128,2048]{1,0:T(8,128)(2,1)S(1)}, bf16[128,2048]{1,0:T(8,128)(2,1)}, u32[]{:S(2)}, u32[]{:S(2)}) collective-permute-start(bf16[128,2048]{1,0:T(8,128)(2,1)S(1)} %collective-permute-done.1.rest_2_.rest_4_), channel_id=1, source_target_pairs={{0,1},{1,0},{2,3},{3,2},{4,5},{5,4},{6,7},{7,6},{8,9},{9,8},{10,11... | collective-permute-start | bytes 1572872 | tf_op jit(solution)/shard_map/ppermute | solution.py:60
  36.6 7.8 %collective-permute-start.7 = (bf16[128,2048]{1,0:T(8,128)(2,1)}, bf16[128,2048]{1,0:T(8,128)(2,1)}, u32[]{:S(2)}, u32[]{:S(2)}) collective-permute-start(bf16[128,2048]{1,0:T(8,128)(2,1)} %constant_dynamic-update-slice_fusion.rest_3_.rest_5_), channel_id=1, source_target_pairs={{0,1},{1,0},{2,3},{3,2},{4,5},{5,4},{6,7},{7,6},{8,9},{9,8},{10,11... | collective-permute-start | bytes 1572872 | tf_op jit(solution)/shard_map/ppermute | solution.py:60
  38.6 18.9 %collective-permute-start.10 = (bf16[128,2048]{1,0:T(8,128)(2,1)}, bf16[128,2048]{1,0:T(8,128)(2,1)}, u32[]{:S(2)}, u32[]{:S(2)}) collective-permute-start(bf16[128,2048]{1,0:T(8,128)(2,1)} %get-tuple-element.58), channel_id=1, source_target_pairs={{0,4},{2,6},{4,0},{6,2},{1,5},{3,7},{5,1},{7,3},{8,12},{10,14},{12... | collective-permute-start | bytes 1572872 | tf_op jit(solution)/shard_map/ppermute | solution.py:60
  39.1 0.8 copy-start.11
  40.0 17.6 %collective-permute-start.9 = (bf16[128,2048]{1,0:T(8,128)(2,1)}, bf16[128,2048]{1,0:T(8,128)(2,1)}, u32[]{:S(2)}, u32[]{:S(2)}) collective-permute-start(bf16[128,2048]{1,0:T(8,128)(2,1)} %get-tuple-element.59), channel_id=1, source_target_pairs={{0,2},{2,0},{4,6},{6,4},{1,3},{3,1},{5,7},{7,5},{8,10},{10,8},{12,... | collective-permute-start | bytes 1572872 | tf_op jit(solution)/shard_map/ppermute | solution.py:60
  44.4 2.2 %copy-start.1 = (bf16[1024,2048]{1,0:T(8,128)(2,1)S(1)}, bf16[1024,2048]{1,0:T(8,128)(2,1)}, u32[]{:S(2)}) copy-start(bf16[1024,2048]{1,0:T(8,128)(2,1)} %w_ref.5) | copy-start | bytes 12582916
  46.6 1.0 copy-start.12
  55.5 2.0 %copy-start.4 = (f32[1024,1024]{1,0:T(8,128)}, f32[1024,1024]{1,0:T(8,128)S(1)}, u32[]{:S(2)}) copy-start(f32[1024,1024]{1,0:T(8,128)S(1)} %cotangent_product.1.base_ref) | copy-start | bytes 12582916
  69.3 7.2 %copy-start.15 = (bf16[64,2048]{1,0:T(8,128)(2,1)}, bf16[64,2048]{1,0:T(8,128)(2,1)S(1)}, u32[]{:S(2)}) copy-start(bf16[64,2048]{1,0:T(8,128)(2,1)S(1)} %get-tuple-element.45.b_ref) | copy-start | bytes 786436
  69.3 4.0 %collective-permute-start.14 = (bf16[128,128]{1,0:T(8,128)(2,1)S(1)}, bf16[128,128]{1,0:T(8,128)(2,1)S(1)}, u32[]{:S(2)}, u32[]{:S(2)}) collective-permute-start(bf16[128,128]{1,0:T(8,128)(2,1)S(1)} %get-tuple-element.40), channel_id=1, source_target_pairs={{0,24},{8,0},{16,8},{24,16},{1,25},{9,1},{17,9},{25,17},{2,26},{10... | collective-permute-start | bytes 98312 | tf_op jit(solution)/shard_map/ppermute | solution.py:39
  70.8 5.2 %collective-permute-start.13 = (bf16[128,128]{1,0:T(8,128)(2,1)S(1)}, bf16[128,128]{1,0:T(8,128)(2,1)S(1)}, u32[]{:S(2)}, u32[]{:S(2)}) collective-permute-start(bf16[128,128]{1,0:T(8,128)(2,1)S(1)} %get-tuple-element.40), channel_id=1, source_target_pairs={{0,16},{8,24},{16,0},{24,8},{1,17},{9,25},{17,1},{25,9},{2,18},{10... | collective-permute-start | bytes 98312 | tf_op jit(solution)/shard_map/ppermute | solution.py:39
  70.8 5.7 %collective-permute-start.12 = (bf16[128,128]{1,0:T(8,128)(2,1)S(1)}, bf16[128,128]{1,0:T(8,128)(2,1)S(1)}, u32[]{:S(2)}, u32[]{:S(2)}) collective-permute-start(bf16[128,128]{1,0:T(8,128)(2,1)S(1)} %get-tuple-element.40), channel_id=1, source_target_pairs={{0,8},{8,16},{16,24},{24,0},{1,9},{9,17},{17,25},{25,1},{2,10},{10... | collective-permute-start | bytes 98312 | tf_op jit(solution)/shard_map/ppermute | solution.py:39
  76.5 54.1 %all-to-all-start.1 = ((bf16[4,256,1024]{2,1,0:T(8,128)(2,1)}), bf16[4,256,1024]{2,1,0:T(8,128)(2,1)}, u32[]{:S(2)}, u32[]{:S(2)}) async-start(bf16[4,256,1024]{2,1,0:T(8,128)(2,1)} %bitcast.77), calls=%async_computation.1 | async-start | bytes 4194304 | tf_op jit(solution)/shard_map/all_to_all | solution.py:529
  81.0 12.1 %collective-permute-start.11 = (bf16[128,2048]{1,0:T(8,128)(2,1)}, bf16[128,2048]{1,0:T(8,128)(2,1)S(1)}, u32[]{:S(2)}, u32[]{:S(2)}) collective-permute-start(bf16[128,2048]{1,0:T(8,128)(2,1)} %get-tuple-element.57), channel_id=1, source_target_pairs={{0,6},{2,4},{4,2},{6,0},{1,7},{3,5},{5,3},{7,1},{8,14},{10,12},{12... | collective-permute-start | bytes 1572872 | tf_op jit(solution)/shard_map/ppermute | solution.py:60
  93.1 1.6 %copy-start.3 = (bf16[1024,1024]{1,0:T(8,128)(2,1)S(1)}, bf16[1024,1024]{1,0:T(8,128)(2,1)}, u32[]{:S(2)}) copy-start(bf16[1024,1024]{1,0:T(8,128)(2,1)} %x_ref.1) | copy-start | bytes 6291460
  95.9 16.3 %copy-start.10 = (bf16[128,2048]{1,0:T(8,128)(2,1)S(1)}, bf16[128,2048]{1,0:T(8,128)(2,1)}, u32[]{:S(2)}) copy-start(bf16[128,2048]{1,0:T(8,128)(2,1)} %copy-done.9) | copy-start | bytes 1572868
  95.9 16.3 %copy-start.13 = (bf16[128,2048]{1,0:T(8,128)(2,1)S(1)}, bf16[128,2048]{1,0:T(8,128)(2,1)}, u32[]{:S(2)}) copy-start(bf16[128,2048]{1,0:T(8,128)(2,1)} %copy-done.11) | copy-start | bytes 1572868
  96.0 3.7 %collective-permute-start.15 = (bf16[4,128,128]{2,1,0:T(8,128)(2,1)S(1)}, bf16[4,128,128]{2,1,0:T(8,128)(2,1)S(1)}, u32[]{:S(2)}, u32[]{:S(2)}) collective-permute-start(bf16[4,128,128]{2,1,0:T(8,128)(2,1)S(1)} %slice_bitcast_fusion.8), channel_id=1, source_target_pairs={{0,1},{1,0},{2,3},{3,2},{4,5},{5,4},{6,7},{7,6},{8,9},{9,8},{10,11... | collective-permute-start | bytes 393224 | tf_op jit(solution)/shard_map/ppermute | solution.py:60
  96.1 6.0 %collective-permute-start.20 = (bf16[4,128,128]{2,1,0:T(8,128)(2,1)S(1)}, bf16[4,128,128]{2,1,0:T(8,128)(2,1)S(1)}, u32[]{:S(2)}, u32[]{:S(2)}) collective-permute-start(bf16[4,128,128]{2,1,0:T(8,128)(2,1)S(1)} %get-tuple-element.65), channel_id=1, source_target_pairs={{0,4},{2,6},{4,0},{6,2},{1,5},{3,7},{5,1},{7,3},{8,12},{10,14},{12... | collective-permute-start | bytes 393224 | tf_op jit(solution)/shard_map/ppermute | solution.py:60
  96.6 6.6 %collective-permute-start.19 = (bf16[4,128,128]{2,1,0:T(8,128)(2,1)S(1)}, bf16[4,128,128]{2,1,0:T(8,128)(2,1)S(1)}, u32[]{:S(2)}, u32[]{:S(2)}) collective-permute-start(bf16[4,128,128]{2,1,0:T(8,128)(2,1)S(1)} %get-tuple-element.65), channel_id=1, source_target_pairs={{0,2},{2,0},{4,6},{6,4},{1,3},{3,1},{5,7},{7,5},{8,10},{10,8},{12,... | collective-permute-start | bytes 393224 | tf_op jit(solution)/shard_map/ppermute | solution.py:60
  97.2 9.7 %collective-permute-start.21 = (bf16[4,128,128]{2,1,0:T(8,128)(2,1)S(1)}, bf16[4,128,128]{2,1,0:T(8,128)(2,1)S(1)}, u32[]{:S(2)}, u32[]{:S(2)}) collective-permute-start(bf16[4,128,128]{2,1,0:T(8,128)(2,1)S(1)} %get-tuple-element.65), channel_id=1, source_target_pairs={{0,6},{2,4},{4,2},{6,0},{1,7},{3,5},{5,3},{7,1},{8,14},{10,12},{12... | collective-permute-start | bytes 393224 | tf_op jit(solution)/shard_map/ppermute | solution.py:60
  99.7 9.9 %collective-permute-start.18 = (bf16[4,128,128]{2,1,0:T(8,128)(2,1)S(1)}, bf16[4,128,128]{2,1,0:T(8,128)(2,1)S(1)}, u32[]{:S(2)}, u32[]{:S(2)}) collective-permute-start(bf16[4,128,128]{2,1,0:T(8,128)(2,1)S(1)} %fusion.3), channel_id=1, source_target_pairs={{0,6},{2,4},{4,2},{6,0},{1,7},{3,5},{5,3},{7,1},{8,14},{10,12},{12... | collective-permute-start | bytes 393224 | tf_op jit(solution)/shard_map/ppermute | solution.py:60
  100.2 10.4 %collective-permute-start.17 = (bf16[4,128,128]{2,1,0:T(8,128)(2,1)S(1)}, bf16[4,128,128]{2,1,0:T(8,128)(2,1)S(1)}, u32[]{:S(2)}, u32[]{:S(2)}) collective-permute-start(bf16[4,128,128]{2,1,0:T(8,128)(2,1)S(1)} %fusion.3), channel_id=1, source_target_pairs={{0,4},{2,6},{4,0},{6,2},{1,5},{3,7},{5,1},{7,3},{8,12},{10,14},{12... | collective-permute-start | bytes 393224 | tf_op jit(solution)/shard_map/ppermute | solution.py:60
  102.0 8.7 %collective-permute-start.16 = (bf16[4,128,128]{2,1,0:T(8,128)(2,1)S(1)}, bf16[4,128,128]{2,1,0:T(8,128)(2,1)S(1)}, u32[]{:S(2)}, u32[]{:S(2)}) collective-permute-start(bf16[4,128,128]{2,1,0:T(8,128)(2,1)S(1)} %fusion.3), channel_id=1, source_target_pairs={{0,2},{2,0},{4,6},{6,4},{1,3},{3,1},{5,7},{7,5},{8,10},{10,8},{12,... | collective-permute-start | bytes 393224 | tf_op jit(solution)/shard_map/ppermute | solution.py:60
  106.9 14.6 %copy-start.6 = (bf16[4,4,128,128]{3,2,1,0:T(8,128)(2,1)}, bf16[4,4,128,128]{3,2,1,0:T(8,128)(2,1)S(1)}, u32[]{:S(2)}) copy-start(bf16[4,4,128,128]{3,2,1,0:T(8,128)(2,1)S(1)} %pad_maximum_fusion.rest_0_) | copy-start | bytes 1572868
  106.9 14.6 %collective-permute-start.22 = (bf16[4,4,128,128]{3,2,1,0:T(8,128)(2,1)S(1)}, bf16[4,4,128,128]{3,2,1,0:T(8,128)(2,1)S(1)}, u32[]{:S(2)}, u32[]{:S(2)}) collective-permute-start(bf16[4,4,128,128]{3,2,1,0:T(8,128)(2,1)S(1)} %pad_maximum_fusion.rest_0_), channel_id=1, source_target_pairs={{0,1},{1,0},{2,3},{3,2},{4,5},{5,4},{6,7},{7,6},{8,9},{9,8},{10,11... | collective-permute-start | bytes 1572872 | tf_op jit(solution)/shard_map/ppermute | solution.py:60
  110.8 8.3 %copy-start.8 = (f32[128,2048]{1,0:T(8,128)S(1)}, f32[128,2048]{1,0:T(8,128)}, u32[]{:S(2)}) copy-start(f32[128,2048]{1,0:T(8,128)} %get-tuple-element.56.rest_0_) | copy-start | bytes 3145732
  110.8 8.3 %copy-start.16 = (bf16[64,2048]{1,0:T(8,128)(2,1)S(1)}, bf16[64,2048]{1,0:T(8,128)(2,1)}, u32[]{:S(2)}) copy-start(bf16[64,2048]{1,0:T(8,128)(2,1)} %copy-done.15) | copy-start | bytes 786436
  110.8 1.4 %collective-permute-start.23 = (bf16[4,128,128]{2,1,0:T(8,128)(2,1)S(1)}, bf16[4,128,128]{2,1,0:T(8,128)(2,1)S(1)}, u32[]{:S(2)}, u32[]{:S(2)}) collective-permute-start(bf16[4,128,128]{2,1,0:T(8,128)(2,1)S(1)} %add_convert_fusion.low_ref.rest_0_), channel_id=1, source_target_pairs={{0,1},{1,0},{2,3},{3,2},{4,5},{5,4},{6,7},{7,6},{8,9},{9,8},{10,11... | collective-permute-start | bytes 393224 | tf_op jit(solution)/shard_map/ppermute | solution.py:60
  112.2 9.3 %copy-start.5 = (f32[1024,1024]{1,0:T(8,128)S(1)}, f32[1024,1024]{1,0:T(8,128)}, u32[]{:S(2)}) copy-start(f32[1024,1024]{1,0:T(8,128)} %copy-done.4) | copy-start | bytes 12582916
  114.5 21.3 %collective-permute-start.26 = (bf16[8,16,256]{2,1,0:T(8,128)(2,1)S(1)}, bf16[8,16,256]{2,1,0:T(8,128)(2,1)S(1)}, u32[]{:S(2)}, u32[]{:S(2)}) collective-permute-start(bf16[8,16,256]{2,1,0:T(8,128)(2,1)S(1)} %get-tuple-element.60), channel_id=1, source_target_pairs={{0,24},{8,0},{16,8},{24,16},{1,25},{9,1},{17,9},{25,17},{2,26},{10... | collective-permute-start | bytes 196616 | tf_op jit(solution)/shard_map/ppermute | solution.py:39
  118.0 17.9 %collective-permute-start.25 = (bf16[8,16,256]{2,1,0:T(8,128)(2,1)S(1)}, bf16[8,16,256]{2,1,0:T(8,128)(2,1)S(1)}, u32[]{:S(2)}, u32[]{:S(2)}) collective-permute-start(bf16[8,16,256]{2,1,0:T(8,128)(2,1)S(1)} %get-tuple-element.61), channel_id=1, source_target_pairs={{0,16},{8,24},{16,0},{24,8},{1,17},{9,25},{17,1},{25,9},{2,18},{10... | collective-permute-start | bytes 196616 | tf_op jit(solution)/shard_map/ppermute | solution.py:39
  118.0 17.9 %collective-permute-start.24 = (bf16[8,16,256]{2,1,0:T(8,128)(2,1)S(1)}, bf16[8,16,256]{2,1,0:T(8,128)(2,1)S(1)}, u32[]{:S(2)}, u32[]{:S(2)}) collective-permute-start(bf16[8,16,256]{2,1,0:T(8,128)(2,1)S(1)} %get-tuple-element.62), channel_id=1, source_target_pairs={{0,8},{8,16},{16,24},{24,0},{1,9},{9,17},{17,25},{25,1},{2,10},{10... | collective-permute-start | bytes 196616 | tf_op jit(solution)/shard_map/ppermute | solution.py:39
  124.8 0.8 copy-start.14
  125.7 10.2 %copy-start.18 = (s32[60]{0:T(128)S(1)}, s32[60]{0:T(128)}, u32[]{:S(2)}) copy-start(s32[60]{0:T(128)} %concatenate.6.at_ref) | copy-start | bytes 724

commit v11 on v10

--- a/solution.py
+++ b/solution.py
@@ -72,19 +72,35 @@
     return came, one, two
 
 
-def up_rides(adapter_up):
-    return adapter_up.shape[1] % 16 == 0
-
-
-def pick(at, slot_of, adapter_down, adapter_up, data_count, blocks_dev):
+def pick_up(at, slot_of, adapter_up, data_count):
+    def kernel(at_ref, up_ref, *rest):
+        out_refs, sems = rest[:data_count], rest[data_count]
+        copies = []
+        for k in range(data_count):
+            data = wrap(at_ref[0] + k, data_count)
+            slot = slot_of(at_ref, data, at_ref[3])
+            copies.append(pltpu.make_async_copy(up_ref.at[slot], out_refs[k], sems.at[k]))
+        for copy in copies:
+            copy.start()
+        for copy in copies:
+            copy.wait()
+
+    return call(
+        kernel,
+        "pick_up",
+        out_shape=(jax.ShapeDtypeStruct(adapter_up.shape[1:], adapter_up.dtype),) * data_count,
+        in_specs=[SMEM, HBM],
+        out_specs=(VMEM,) * data_count,
+        scratch_shapes=[pltpu.SemaphoreType.DMA((data_count,))],
+    )(at, adapter_up)
+
+
+def pick_down(at, slot_of, adapter_down, data_count, blocks_dev, spare):
     down_rows, ranks = adapter_down.shape[1:]
-    up_rows, width = adapter_up.shape[1:]
-    first_up = blocks_dev * down_rows
-    rides = up_rides(adapter_up)
-    total = first_up + (up_rows * width // ranks if rides else 0)
-
-    def kernel(at_ref, down_ref, up_ref, out_ref, rows, tiles, down_sem, up_sem, out_sem):
-        downs, ups, outs = [], [], []
+    used = blocks_dev * down_rows
+
+    def kernel(at_ref, down_ref, out_ref, rows, down_sem, out_sem):
+        downs, outs = [], []
         for data in range(data_count):
             downs.append([])
             for block in range(blocks_dev):
@@ -93,42 +109,30 @@
                 downs[data].append(
                     pltpu.make_async_copy(down_ref.at[slot], here, down_sem.at[data, block])
                 )
-            if rides:
-                slot = slot_of(at_ref, data, at_ref[3])
-                ups.append(pltpu.make_async_copy(up_ref.at[slot], tiles.at[data], up_sem.at[data]))
-            outs.append(pltpu.make_async_copy(rows.at[data], out_ref.at[data], out_sem.at[data]))
-            for copy in downs[data] + ups[data:]:
+            there = out_ref.at[data, pl.ds(0, used)]
+            outs.append(pltpu.make_async_copy(rows.at[data], there, out_sem.at[data]))
+            for copy in downs[data]:
                 copy.start()
         for data in range(data_count):
-            for copy in downs[data] + ups[data : data + 1]:
+            for copy in downs[data]:
                 copy.wait()
-            for n in range(width // ranks if rides else 0):
-                first = first_up + n * up_rows
-                rows[data, first : first + up_rows] = tiles[data, :, n * ranks : (n + 1) * ranks]
             outs[data].start()
         for copy in outs:
             copy.wait()
 
     return call(
         kernel,
-        "pick_rows",
+        "pick_down",
         VMEM_MOST,
-        out_shape=pltpu.HBM((data_count, total, ranks), adapter_down.dtype),
-        in_specs=[SMEM, HBM, HBM],
+        out_shape=pltpu.HBM((data_count, used + spare, ranks), adapter_down.dtype),
+        in_specs=[SMEM, HBM],
         out_specs=HBM,
         scratch_shapes=[
-            pltpu.VMEM((data_count, total, ranks), adapter_down.dtype),
-            pltpu.VMEM((data_count, up_rows, width), adapter_up.dtype),
+            pltpu.VMEM((data_count, used, ranks), adapter_down.dtype),
             pltpu.SemaphoreType.DMA((data_count, blocks_dev)),
             pltpu.SemaphoreType.DMA((data_count,)),
-            pltpu.SemaphoreType.DMA((data_count,)),
         ],
-    )(at, adapter_down, adapter_up)
-
-
-def pick_up(at, slot_of, adapter_up, data_count):
-    slots = jnp.stack([slot_of(at, data, at[3]) for data in range(data_count)])
-    return jnp.take(adapter_up, slots, axis=0)
+    )(at, adapter_down)
 
 
 def base_product(at, tokens, weight, first, count):
@@ -247,7 +251,7 @@
                 for k in range(pipe_count):
                     chip = came_from(at_ref[1], k, pipe_count)
                     first = pl.multiple_of((chip * tensor_count + core) * rows, rows)
-                    grad[pl.ds(first, rows)] = grad_refs[s][k, 0]
+                    grad[pl.ds(first, rows)] = grad_refs[s][k, at_ref[0]]
 
         for block in range(tok_dev // BLOCK):
             here = slice(block * BLOCK, (block + 1) * BLOCK)
@@ -279,7 +283,7 @@
     blocks_dev = tok_dev // BLOCK
 
     def kernel(at_ref, x_ref, *rest):
-        grad_refs, (out_ref, grad, x, sems) = rest[:tensor_count], rest[tensor_count:]
+        grad_refs, (out_ref, grad, x, products, sems) = rest[:tensor_count], rest[tensor_count:]
         copies = [
             pltpu.make_async_copy(x_ref.at[data], x.at[data], sems.at[data])
             for data in range(data_count)
@@ -291,18 +295,19 @@
             for k in range(pipe_count):
                 chip = came_from(at_ref[1], k, pipe_count)
                 first = pl.multiple_of((chip * tensor_count + core) * rows, rows)
-                for m in range(data_count):
-                    data = wrap(at_ref[0] - m, data_count)
-                    grad[data, pl.ds(first, rows)] = grad_refs[s][k, m]
+                for data in range(data_count):
+                    grad[data, pl.ds(first, rows)] = grad_refs[s][k, data]
         out_ref[...] = jnp.zeros(out_ref.shape, out_ref.dtype)
         for data in range(data_count):
             copies[data].wait()
             for block in range(blocks_dev):
-                slot = slot_of(at_ref, data, block)
                 here = slice(block * BLOCK, (block + 1) * BLOCK)
-                out_ref[slot] += jnp.dot(
+                products[data % 2, block] = jnp.dot(
                     x[data, :, here], grad[data, here], preferred_element_type=jnp.float32
                 )
+            for block in range(blocks_dev):
+                slot = slot_of(at_ref, data, block)
+                out_ref[slot] += products[data % 2, block]
 
     return call(
         kernel,
@@ -314,6 +319,7 @@
         scratch_shapes=[
             pltpu.VMEM((data_count, tok_dev, RANKS), jnp.bfloat16),
             pltpu.VMEM(x_features.shape, jnp.bfloat16),
+            pltpu.VMEM((2, blocks_dev, down_rows, RANKS), jnp.float32),
             pltpu.SemaphoreType.DMA((data_count,)),
         ],
     )(at, x_features, *grad_pieces)
@@ -401,47 +407,55 @@
     )(at, *pieces)
 
 
-def own_rows(came, up, cotangent, first_up):
+def own_rows(at, up, cotangent, a_send):
+    data_count = len(up)
     rows = cotangent.shape[0]
-    data_count = came.shape[0]
-    up_rows = ADAPTER_RANK // data_count
-
-    def kernel(cot_ref, came_ref, b_ref, grad_ref, tiles, sem):
-        if up is None:
-            copy = pltpu.make_async_copy(came_ref.at[:, pl.ds(first_up, tiles.shape[1])], tiles, sem)
-            copy.start()
-            copy.wait()
-            for data in range(data_count):
-                for n in range(WIDTH // RANKS):
-                    b_ref[
-                        data * up_rows : (data + 1) * up_rows, n * RANKS : (n + 1) * RANKS
-                    ] = tiles[data, n * up_rows : (n + 1) * up_rows]
-        else:
-            b_ref[...] = came_ref[...]
-        cot, b = cot_ref[...], b_ref[...]
-        grad_ref[...] = jnp.concatenate(
+    used = a_send.shape[1] - rows
+
+    def kernel(at_ref, cot_ref, send_in_ref, *rest):
+        del send_in_ref
+        up_refs, (b_ref, send_ref, grad, sems) = rest[:data_count], rest[data_count:]
+        pieces = []
+        for data in range(data_count):
+            came = wrap(at_ref[0] - data, data_count)
+            piece = up_refs[0][...]
+            for k in range(1, data_count):
+                piece = jnp.where(came == k, up_refs[k][...], piece)
+            pieces.append(piece)
+        b = jnp.concatenate(pieces, axis=0)
+        cot = cot_ref[...]
+        grad[...] = jnp.concatenate(
             [
                 lax.dot_general(cot[:, half], b[:, half], LAST_BOTH, preferred_element_type=jnp.float32)
                 for half in (slice(0, KEY_WIDTH), slice(KEY_WIDTH, WIDTH))
             ],
             axis=1,
-        ).astype(grad_ref.dtype)
-
-    tile_rows = up_rows * WIDTH // RANKS
+        ).astype(grad.dtype)
+        copies = [
+            pltpu.make_async_copy(grad, send_ref.at[data, pl.ds(used, rows)], sems.at[data])
+            for data in range(data_count)
+        ]
+        for copy in copies:
+            copy.start()
+        b_ref[...] = b
+        for copy in copies:
+            copy.wait()
+
     return call(
         kernel,
         "own_rows",
-        in_specs=[VMEM, ANY if up is None else VMEM],
-        out_specs=(VMEM, VMEM),
+        in_specs=[SMEM, VMEM, HBM] + [VMEM] * data_count,
+        out_specs=(VMEM, HBM),
         out_shape=(
             jax.ShapeDtypeStruct((ADAPTER_RANK, WIDTH), jnp.bfloat16),
-            jax.ShapeDtypeStruct((rows, RANKS), jnp.bfloat16),
+            pltpu.HBM(a_send.shape, a_send.dtype),
         ),
+        input_output_aliases={2: 1},
         scratch_shapes=[
-            pltpu.VMEM((data_count, tile_rows, RANKS), jnp.bfloat16),
-            pltpu.SemaphoreType.DMA,
+            pltpu.VMEM((rows, RANKS), jnp.bfloat16),
+            pltpu.SemaphoreType.DMA((data_count,)),
         ],
-    )(cotangent, came if up is None else up)
+    )(at, cotangent, a_send, *up)
 
 
 def keys_and_values(at, base_pieces, low_sum, b_own):
@@ -491,15 +505,17 @@
     def slot_of(at_ref, data, block):
         return at_ref[4 + blocks + at_ref[4 + data * blocks_dev + block]]
 
-    a_send = pick(at, slot_of, adapter_down, adapter_up, data_count, blocks_dev)
+    b_send = pick_up(at, slot_of, adapter_up, data_count)
+    b_came = [b_send[0]] + [shift(b_send[k], "dp", k) for k in range(1, data_count)]
+
+    adapter_down, b_send = lax.optimization_barrier((adapter_down, b_send))
+    a_send = pick_down(at, slot_of, adapter_down, data_count, blocks_dev, rows)
+    a_send, cot_send = lax.optimization_barrier((a_send, cotangent))
+    b_own, a_send = own_rows(at, b_came, cotangent, a_send)
     a_recv = lax.all_to_all(a_send, "dp", 0, 0, tiled=True)
-    up = None
-    if not up_rides(adapter_up):
-        up = lax.all_to_all(pick_up(at, slot_of, adapter_up, data_count), "dp", 0, 0, tiled=True)
-        up = up.reshape(ADAPTER_RANK, WIDTH)
 
     behind, a_send = lax.optimization_barrier((tokens, a_send))
-    cot_chips, base_tokens, x_tokens = gather_chips(cotangent, behind)
+    cot_chips, base_tokens, x_tokens = gather_chips(cot_send, behind)
     cot_chips = [cotangent] + cot_chips
 
     tokens_by_group = base_tokens.reshape(pipe_count, tensor_count, rows, feature_count)
@@ -523,19 +539,14 @@
     a_recv, x_send, input_base, base_chip_came[:2] = lax.optimization_barrier(
         (a_recv, x_send, input_base, base_chip_came[:2])
     )
-    b_own, grad_rows = own_rows(a_recv, up, cotangent, blocks_dev * down_rows)
-    grad_data = [grad_rows] + [shift(grad_rows, "dp", k) for k in range(1, data_count)]
-    x_send, grad_data = lax.optimization_barrier((x_send, grad_data))
     x_recv = lax.all_to_all(x_send, "dp", 0, 0, tiled=True)
 
-    grad_all = jnp.stack(grad_data)
-    grad_chips = jnp.stack([grad_all] + [swap(grad_all, "pipe", k) for k in range(1, pipe_count)])
+    grad_data = a_recv[:, blocks_dev * down_rows :]
+    grad_chips = jnp.stack([grad_data] + [swap(grad_data, "pipe", k) for k in range(1, pipe_count)])
     grad_pieces = [grad_chips] + [swap(grad_chips, "tensor", s) for s in range(1, tensor_count)]
     input_grad = input_gradient(at, input_base, grad_pieces, a_recv)
 
-    low_down, base_chip_came, grad_data = lax.optimization_barrier(
-        (a_recv, base_chip_came, grad_data)
-    )
+    low_down, base_chip_came = lax.optimization_barrier((a_recv, base_chip_came))
     low_part = low_product(at, tokens, low_down, pipe_count, tensor_count)
     low_core = sum(
         [low_part[0].astype(jnp.float32)]

time: 138 us -> 142 us (1.029)
  Pallas kernels: 35.6 us -> 40 us
  starting transfers between devices: 31.9 us -> 34.8 us
  local copies, waits for them, and re-layouts: 19.9 us -> 17.1 us
    ppermute x6, starting transfers between devices: 6.77 us -> 10.1 us  [shift(): lax.ppermute(piece, axis, [(i, (i + k) % count) for i in range(count)])]
    unnamed x39 -> x35, local copies, waits for them, and re-layouts: 12.9 us -> 11 us
    pallas_call x2 -> x3, Pallas kernels: 4.63 us -> 6.52 us  [the longest x1 3.99 us: pick_down(): call(kernel, 'pick_down', VMEM_MOST, out_shape=pltpu.HBM((data_count, use...]
    ppermute x6, waiting for transfers between devices: 5.08 us -> 3.32 us  [shift(): lax.ppermute(piece, axis, [(i, (i + k) % count) for i in range(count)])]
  transfers between devices with their start and end apart: 29 -> 29, of which waited for: 16 -> 14; matrix products, arithmetic and copies ran while one was open for 7% -> 6% of each run, Pallas kernels for 25% -> 24%
where the time goes in v11:
time: 142 us; the launch traced here: 141 us
  waiting for transfers between devices  45.7 us (32%)
  Pallas kernels  40 us (28%)
  starting transfers between devices  34.8 us (25%)
  local copies, waits for them, and re-layouts  17.1 us (12%)
  other arithmetic  2.21 us (2%)
    ppermute x21, waiting for transfers between devices, swap(): lax.ppermute(piece, axis, [(i, partner(i, k, count)) for i in range(count)])  25.7 us
    ppermute x21, starting transfers between devices, swap(): lax.ppermute(piece, axis, [(i, partner(i, k, count)) for i in range(count)])  15.6 us
    all_to_all x1, waiting for transfers between devices, body(): a_recv = lax.all_to_all(a_send, 'dp', 0, 0, tiled=True)  12.6 us
    unnamed x35, local copies, waits for them, and re-layouts  11 us
    ppermute x6, starting transfers between devices, shift(): lax.ppermute(piece, axis, [(i, (i + k) % count) for i in range(count)])  10.1 us
    pallas_call x1, Pallas kernels, cotangent_product(): call(kernel, 'cotangent_product', grid=(depth // tile,), in_specs=[SMEM,...  7.96 us
    pallas_call x2, Pallas kernels, base_product(): call(kernel, 'base_product', grid_spec=pltpu.PrefetchScalarGridSpec(num_s...  7.22 us
    pallas_call x1, Pallas kernels, grad_down(): call(kernel, 'grad_down', VMEM_MOST, in_specs=[SMEM, HBM] + [VMEM] * tens...  5.15 us
  transfers between devices with their start and end apart: 29, of which 14 were waited for; matrix products, arithmetic and copies ran while one was open for 6% of the time, Pallas kernels for 24%

profile of v11, /device:TPU:0, one launch (start us, length us, event | category | flops | bytes accessed | tf_op | source)
XLA Modules:
  0.0 140.8 jit_solution(2487747504512715882)
XLA Ops:
  0.6 0.8 concatenate.6.at_ref
  1.4 1.4 copy-done.12
  2.8 0.9 pick_up.1
  3.8 4.0 %pick_down.1.send_in_ref = bf16[4,2176,128]{2,1,0:T(8,128)(2,1)} custom-call(s32[60]{0:T(128)} %copy-done.13, bf16[24,256,128]{2,1,0:T(8,128)(2,1)} %down_ref), custom_call_target="tpu_custom_call" | custom-call | flops 1024 | bytes 1024 | tf_op jit(solution)/shard_map/pick_down/pallas_call | solution.py:123
  7.8 3.0 %collective-permute-start.4 = (bf16[128,2048]{1,0:T(8,128)(2,1)S(1)}, bf16[128,2048]{1,0:T(8,128)(2,1)S(1)}, u32[]{:S(2)}, u32[]{:S(2)}) collective-permute-start(bf16[128,2048]{1,0:T(8,128)(2,1)S(1)} %copy-done.5), channel_id=1, source_target_pairs={{0,4},{2,6},{4,0},{6,2},{1,5},{3,7},{5,1},{7,3},{8,12},{10,14},{12... | collective-permute-start | bytes 1572872 | tf_op jit(solution)/shard_map/ppermute | solution.py:60
  10.8 1.5 %collective-permute-start.3 = (bf16[128,2048]{1,0:T(8,128)(2,1)S(1)}, bf16[128,2048]{1,0:T(8,128)(2,1)}, u32[]{:S(2)}, u32[]{:S(2)}) collective-permute-start(bf16[128,2048]{1,0:T(8,128)(2,1)S(1)} %copy-done.5), channel_id=1, source_target_pairs={{0,2},{2,0},{4,6},{6,4},{1,3},{3,1},{5,7},{7,5},{8,10},{10,8},{12,... | collective-permute-start | bytes 1572872 | tf_op jit(solution)/shard_map/ppermute | solution.py:60
  12.3 1.6 %collective-permute-start = (bf16[16,2048]{1,0:T(8,128)(2,1)S(1)}, bf16[16,2048]{1,0:T(8,128)(2,1)S(1)}, u32[]{:S(2)}, u32[]{:S(2)}) collective-permute-start(bf16[16,2048]{1,0:T(8,128)(2,1)S(1)} %get-tuple-element.33), channel_id=1, source_target_pairs={{0,8},{8,16},{16,24},{24,0},{1,9},{9,17},{17,25},{25,1},{2,10},{10... | collective-permute-start | bytes 196616 | tf_op jit(solution)/shard_map/ppermute | solution.py:39
  13.9 2.6 %collective-permute-start.1 = (bf16[16,2048]{1,0:T(8,128)(2,1)S(1)}, bf16[16,2048]{1,0:T(8,128)(2,1)S(1)}, u32[]{:S(2)}, u32[]{:S(2)}) collective-permute-start(bf16[16,2048]{1,0:T(8,128)(2,1)S(1)} %get-tuple-element.34), channel_id=1, source_target_pairs={{0,16},{8,24},{16,0},{24,8},{1,17},{9,25},{17,1},{25,9},{2,18},{10... | collective-permute-start | bytes 196616 | tf_op jit(solution)/shard_map/ppermute | solution.py:39
  16.5 1.3 collective-permute-start.2
  17.8 1.3 collective-permute-done.rest_1_
  19.1 1.9 %collective-permute-done.1.rest_2_ = bf16[16,2048]{1,0:T(8,128)(2,1)S(1)} collective-permute-done((bf16[16,2048]{1,0:T(8,128)(2,1)S(1)}, bf16[16,2048]{1,0:T(8,128)(2,1)S(1)}, u32[]{:S(2)}, u32[]{:S(2)}) %collective-permute-start.1) | collective-permute-done | bytes 65568 | tf_op jit(solution)/shard_map/ppermute | solution.py:39
  21.1 0.1 collective-permute-done.2.rest_3_
  21.1 0.7 copy-done.14
  21.8 1.6 %own_rows.1 = (bf16[64,2048]{1,0:T(8,128)(2,1)S(1)}, bf16[4,2176,128]{2,1,0:T(8,128)(2,1)}) custom-call(s32[60]{0:T(128)S(1)} %copy-done.14, bf16[128,2048]{1,0:T(8,128)(2,1)S(1)} %copy-done.5, bf16[4,2176,128]{2,1,0:T(8,128)(2,1)} %pick_down.1.send_in_ref, bf16[16,2048]{1,0:T(8,128)(2,1)S(1)} %get-tuple-element.32.rest_0_, ...), custom_call_target="tpu_custom_call", output_to_operand_aliasing={{1}: (2, {})} | custom-call | flops 1024 | bytes 1024 | tf_op jit(solution)/shard_map/own_rows/pallas_call | solution.py:444
  23.4 4.6 %all-to-all-start = ((bf16[4,2176,128]{2,1,0:T(8,128)(2,1)}), bf16[4,2176,128]{2,1,0:T(8,128)(2,1)}, u32[]{:S(2)}, u32[]{:S(2)}) async-start(bf16[4,2176,128]{2,1,0:T(8,128)(2,1)} %get-tuple-element.38), calls=%async_computation | async-start | bytes 4456448 | tf_op jit(solution)/shard_map/all_to_all | solution.py:515
  28.1 2.2 %copy-done = bf16[1024,2048]{1,0:T(8,128)(2,1)S(1)} copy-done((bf16[1024,2048]{1,0:T(8,128)(2,1)S(1)}, bf16[1024,2048]{1,0:T(8,128)(2,1)}, u32[]{:S(2)}) %copy-start) | copy-done | bytes 4194328
  30.3 3.6 %base_product.3 = bf16[1,4,128,2048]{3,2,1,0:T(8,128)(2,1)S(1)} custom-call(s32[60]{0:T(128)S(1)} %copy-done.15, bf16[4,2,128,1024]{3,2,1,0:T(8,128)(2,1)S(1)} %bitcast.68, bf16[1024,2048]{1,0:T(8,128)(2,1)S(1)} %copy-done), custom_call_target="tpu_custom_call" | custom-call | flops 1024 | bytes 1024 | tf_op jit(solution)/shard_map/base_product/pallas_call | solution.py:148
  33.9 0.1 collective-permute-start.11
  34.0 0.6 collective-permute-start.5
  34.6 1.0 slice.56
  35.6 0.5 collective-permute-start.6
  36.1 0.5 collective-permute-start.8
  36.6 3.6 %base_product.2 = bf16[1,4,128,2048]{3,2,1,0:T(8,128)(2,1)S(1)} custom-call(s32[60]{0:T(128)S(1)} %copy-done.15, bf16[4,2,128,1024]{3,2,1,0:T(8,128)(2,1)S(1)} %bitcast.69, bf16[1024,2048]{1,0:T(8,128)(2,1)S(1)} %copy-done), custom_call_target="tpu_custom_call" | custom-call | flops 1024 | bytes 1024 | tf_op jit(solution)/shard_map/base_product/pallas_call | solution.py:148
  40.2 2.6 %collective-permute-done.5 = bf16[64,2048]{1,0:T(8,128)(2,1)S(1)} collective-permute-done((bf16[64,2048]{1,0:T(8,128)(2,1)S(1)}, bf16[64,2048]{1,0:T(8,128)(2,1)S(1)}, u32[]{:S(2)}, u32[]{:S(2)}) %collective-permute-start.5) | collective-permute-done | bytes 262176 | tf_op jit(solution)/shard_map/ppermute | solution.py:60
  42.8 0.7 constant_dynamic-update-slice_fusion.1
  43.5 0.6 collective-permute-done.6
  44.1 0.7 constant_dynamic-update-slice_fusion.rest_3_.rest_5_
  44.8 2.0 %convert_add_fusion = (f32[128,2048]{1,0:T(8,128)}, bf16[128,2048]{1,0:T(8,128)(2,1)}, bf16[128,2048]{1,0:T(8,128)(2,1)}, bf16[128,2048]{1,0:T(8,128)(2,1)}) fusion(bf16[4,128,2048]{2,1,0:T(8,128)(2,1)S(1)} %collective-permute-done.11, bf16[1,4,128,2048]{3,2,1,0:T(8,128)(2,1)S(1)} %base_product.2), kind=kLoop, calls=%fused_computation | loop fusion | flops 3932160 | bytes 6815744 | tf_op jit(solution)/shard_map/add | solution.py:526
  46.8 0.5 collective-permute-start.13
  47.3 0.8 copy-done.8
  48.1 1.5 %collective-permute-start.12 = (bf16[128,2048]{1,0:T(8,128)(2,1)}, bf16[128,2048]{1,0:T(8,128)(2,1)}, u32[]{:S(2)}, u32[]{:S(2)}) collective-permute-start(bf16[128,2048]{1,0:T(8,128)(2,1)} %get-tuple-element.63), channel_id=1, source_target_pairs={{0,2},{2,0},{4,6},{6,4},{1,3},{3,1},{5,7},{7,5},{8,10},{10,8},{12,... | collective-permute-start | bytes 1572872 | tf_op jit(solution)/shard_map/ppermute | solution.py:60
  49.6 2.6 %copy.12 = bf16[1024,1024]{1,0:T(8,128)(2,1)} copy(bf16[1024,1024]{0,1:T(8,128)(2,1)S(1)} %bitcast.70) | data formatting | bytes 4194304 | tf_op jit(solution)/shard_map/transpose | solution.py:537
  52.3 2.2 %copy-done.1 = bf16[1024,2048]{1,0:T(8,128)(2,1)S(1)} copy-done((bf16[1024,2048]{1,0:T(8,128)(2,1)S(1)}, bf16[1024,2048]{1,0:T(8,128)(2,1)}, u32[]{:S(2)}) %copy-start.1) | copy-done | bytes 4194328
  54.5 1.0 copy-done.9
  55.5 8.0 %cotangent_product.1.base_ref = f32[1024,1024]{1,0:T(8,128)S(1)} custom-call(s32[60]{0:T(128)S(1)} %copy-done.15, bf16[1024,2048]{1,0:T(8,128)(2,1)S(1)} %copy-done.1, bf16[128,2048]{1,0:T(8,128)(2,1)S(1)} %copy-done.5, bf16[128,2048]{1,0:T(8,128)(2,1)} %collective-permute-done.3.rest_1_.rest_3_, ...), custom_call_target="tpu_custom_call" | custom-call | flops 1024 | bytes 1024 | tf_op jit(solution)/shard_map/cotangent_product/pallas_call | solution.py:221
  63.5 2.0 %copy-done.3 = f32[1024,1024]{1,0:T(8,128)} copy-done((f32[1024,1024]{1,0:T(8,128)}, f32[1024,1024]{1,0:T(8,128)S(1)}, u32[]{:S(2)}) %copy-start.3) | copy-done | bytes 4194328
  65.4 12.6 %all-to-all-done.a_ref = bf16[4,2176,128]{2,1,0:T(8,128)(2,1)} async-done(((bf16[4,2176,128]{2,1,0:T(8,128)(2,1)}), bf16[4,2176,128]{2,1,0:T(8,128)(2,1)}, u32[]{:S(2)}, u32[]{:S(2)}) %all-to-all-start) | async-done | bytes 2228256 | tf_op jit(solution)/shard_map/all_to_all | solution.py:515
  78.1 4.4 %all-to-all-start.1 = ((bf16[4,256,1024]{2,1,0:T(8,128)(2,1)}), bf16[4,256,1024]{2,1,0:T(8,128)(2,1)}, u32[]{:S(2)}, u32[]{:S(2)}) async-start(bf16[4,256,1024]{2,1,0:T(8,128)(2,1)} %bitcast.72), calls=%async_computation.1 | async-start | bytes 4194304 | tf_op jit(solution)/shard_map/all_to_all | solution.py:542
  82.5 0.3 collective-permute-start.14
  82.9 13.7 %collective-permute-done.14.rest_3_ = bf16[128,2048]{1,0:T(8,128)(2,1)S(1)} collective-permute-done((bf16[128,2048]{1,0:T(8,128)(2,1)}, bf16[128,2048]{1,0:T(8,128)(2,1)S(1)}, u32[]{:S(2)}, u32[]{:S(2)}) %collective-permute-start.14) | collective-permute-done | bytes 524320 | tf_op jit(solution)/shard_map/ppermute | solution.py:60
  96.6 2.4 %low_product.1 = bf16[2,4,128,128]{3,2,1,0:T(8,128)(2,1)S(1)} custom-call(s32[60]{0:T(128)S(1)} %copy-done.15, bf16[1024,1024]{1,0:T(8,128)(2,1)S(1)} %copy-done.2, bf16[4,2176,128]{2,1,0:T(8,128)(2,1)} %all-to-all-done.a_ref), custom_call_target="tpu_custom_call" | custom-call | flops 1024 | bytes 1024 | tf_op jit(solution)/shard_map/low_product/pallas_call | solution.py:182
  99.1 1.0 slice_bitcast_fusion.14
  100.0 0.6 collective-permute-start.20
  100.6 0.3 collective-permute-start.19
  101.0 2.6 %collective-permute-start.21 = (bf16[4,128,128]{2,1,0:T(8,128)(2,1)S(1)}, bf16[4,128,128]{2,1,0:T(8,128)(2,1)S(1)}, u32[]{:S(2)}, u32[]{:S(2)}) collective-permute-start(bf16[4,128,128]{2,1,0:T(8,128)(2,1)S(1)} %get-tuple-element.65), channel_id=1, source_target_pairs={{0,6},{2,4},{4,2},{6,0},{1,7},{3,5},{5,3},{7,1},{8,14},{10,12},{12... | collective-permute-start | bytes 393224 | tf_op jit(solution)/shard_map/ppermute | solution.py:60
  103.6 0.4 collective-permute-start.18
  104.0 1.7 %collective-permute-start.17 = (bf16[4,128,128]{2,1,0:T(8,128)(2,1)S(1)}, bf16[4,128,128]{2,1,0:T(8,128)(2,1)S(1)}, u32[]{:S(2)}, u32[]{:S(2)}) collective-permute-start(bf16[4,128,128]{2,1,0:T(8,128)(2,1)S(1)} %fusion.3), channel_id=1, source_target_pairs={{0,4},{2,6},{4,0},{6,2},{1,5},{3,7},{5,1},{7,3},{8,12},{10,14},{12... | collective-permute-start | bytes 393224 | tf_op jit(solution)/shard_map/ppermute | solution.py:60
  105.7 0.2 collective-permute-done.20
  106.0 1.2 collective-permute-start.16
  107.2 3.6 %collective-permute-done.21 = bf16[4,128,128]{2,1,0:T(8,128)(2,1)S(1)} collective-permute-done((bf16[4,128,128]{2,1,0:T(8,128)(2,1)S(1)}, bf16[4,128,128]{2,1,0:T(8,128)(2,1)S(1)}, u32[]{:S(2)}, u32[]{:S(2)}) %collective-permute-start.21) | collective-permute-done | bytes 131104 | tf_op jit(solution)/shard_map/ppermute | solution.py:60
  110.9 0.1 collective-permute-start.22
  111.0 2.6 %collective-permute-done.18 = bf16[4,128,128]{2,1,0:T(8,128)(2,1)S(1)} collective-permute-done((bf16[4,128,128]{2,1,0:T(8,128)(2,1)S(1)}, bf16[4,128,128]{2,1,0:T(8,128)(2,1)S(1)}, u32[]{:S(2)}, u32[]{:S(2)}) %collective-permute-start.18) | collective-permute-done | bytes 131104 | tf_op jit(solution)/shard_map/ppermute | solution.py:60
  113.6 0.8 collective-permute-done.17
  114.4 0.2 collective-permute-done.16
  114.7 0.1 add_convert_fusion.low_ref.rest_0_
  114.8 1.3 collective-permute-done.23.rest_1_
  116.2 2.2 %grad_up_pieces.1 = bf16[4,8,16,256]{3,2,1,0:T(8,128)(2,1)S(1)} custom-call(s32[60]{0:T(128)S(1)} %copy-done.15, bf16[4,128,128]{2,1,0:T(8,128)(2,1)S(1)} %add_convert_fusion.low_ref.rest_0_, bf16[4,128,128]{2,1,0:T(8,128)(2,1)S(1)} %collective-permute-done.23.rest_1_, bf16[128,2048]{1,0:T(8,128)(2,1)S(1)} %copy-done.5, ...), custom_call_target="tpu_custom_call" | custom-call | flops 1024 | bytes 1024 | tf_op jit(solution)/shard_map/grad_up_pieces/pallas_call | solution.py:374
  118.4 3.5 %collective-permute-start.26 = (bf16[8,16,256]{2,1,0:T(8,128)(2,1)S(1)}, bf16[8,16,256]{2,1,0:T(8,128)(2,1)S(1)}, u32[]{:S(2)}, u32[]{:S(2)}) collective-permute-start(bf16[8,16,256]{2,1,0:T(8,128)(2,1)S(1)} %get-tuple-element.66), channel_id=1, source_target_pairs={{0,24},{8,0},{16,8},{24,16},{1,25},{9,1},{17,9},{25,17},{2,26},{10... | collective-permute-start | bytes 196616 | tf_op jit(solution)/shard_map/ppermute | solution.py:39
  121.9 1.1 collective-permute-start.24
  123.0 2.5 %keys_and_values.1 = bf16[128,2048]{1,0:T(8,128)(2,1)} custom-call(s32[60]{0:T(128)S(1)} %copy-done.15, bf16[4,128,128]{2,1,0:T(8,128)(2,1)S(1)} %add_convert_fusion.low_ref.rest_0_, bf16[64,2048]{1,0:T(8,128)(2,1)S(1)} %get-tuple-element.49.b_ref, f32[128,2048]{1,0:T(8,128)S(1)} %copy-done.7, bf16[128,2048]{1,0:T(8,128)(2,1)} %collective-permute-done.12.rest_1_, ...), custom_call_target="tpu_custom_call" | custom-call | flops 1024 | bytes 1024 | tf_op jit(solution)/shard_map/keys_and_values/pallas_call | solution.py:475
  125.5 4.7 %input_gradient.1 = bf16[1024,1024]{1,0:T(8,128)(2,1)} custom-call(s32[60]{0:T(128)S(1)} %copy-done.15, f32[1024,1024]{1,0:T(8,128)S(1)} %copy-done.4, bf16[4,2176,128]{2,1,0:T(8,128)(2,1)} %all-to-all-done.a_ref, bf16[4,4,128,128]{3,2,1,0:T(8,128)(2,1)S(1)} %pad_maximum_fusion.rest_0_, bf16[4,4,128,128]{3,2,1,0:T(8,128)(2,1)S(1)} %collective-permute-done.22.rest_1_), custom_call_target="tpu_custom_call" | custom-call | flops 1024 | bytes 1024 | tf_op jit(solution)/shard_map/input_gradient/pallas_call | solution.py:263
  130.2 4.0 %all-to-all-done.1.x_ref = bf16[4,256,1024]{2,1,0:T(8,128)(2,1)} async-done(((bf16[4,256,1024]{2,1,0:T(8,128)(2,1)}), bf16[4,256,1024]{2,1,0:T(8,128)(2,1)}, u32[]{:S(2)}, u32[]{:S(2)}) %all-to-all-start.1) | async-done | bytes 2097184 | tf_op jit(solution)/shard_map/all_to_all | solution.py:542
  134.2 5.2 %grad_down.1 = f32[24,256,128]{2,1,0:T(8,128)} custom-call(s32[60]{0:T(128)} %copy-done.13, bf16[4,256,1024]{2,1,0:T(8,128)(2,1)} %all-to-all-done.1.x_ref, bf16[4,4,128,128]{3,2,1,0:T(8,128)(2,1)} %copy-done.6, bf16[4,4,128,128]{3,2,1,0:T(8,128)(2,1)} %copy-done.11), custom_call_target="tpu_custom_call" | custom-call | flops 1024 | bytes 1024 | tf_op jit(solution)/shard_map/grad_down/pallas_call | solution.py:312
  139.4 1.5 %grad_up.1 = f32[24,16,256]{2,1,0:T(8,128)} custom-call(s32[60]{0:T(128)S(1)} %copy-done.16, bf16[8,16,256]{2,1,0:T(8,128)(2,1)S(1)} %get-tuple-element.56.rest_0_, bf16[8,16,256]{2,1,0:T(8,128)(2,1)S(1)} %collective-permute-done.24.rest_1_, bf16[8,16,256]{2,1,0:T(8,128)(2,1)S(1)} %collective-permute-done.25.rest_2_, ...), custom_call_target="tpu_custom_call" | custom-call | flops 1024 | bytes 1024 | tf_op jit(solution)/shard_map/grad_up/pallas_call | solution.py:401
  (53 shorter events, 0.4 us)
Async XLA Ops:
  1.4 1.4 %copy-start.12 = (bf16[24,16,2048]{2,1,0:T(8,128)(2,1)S(1)}, bf16[24,16,2048]{2,1,0:T(8,128)(2,1)}, u32[]{:S(2)}) copy-start(bf16[24,16,2048]{2,1,0:T(8,128)(2,1)} %up_ref.1) | copy-start | bytes 4718596
  2.8 1.0 copy-start.13
  3.8 4.0 %copy-start.5 = (bf16[128,2048]{1,0:T(8,128)(2,1)S(1)}, bf16[128,2048]{1,0:T(8,128)(2,1)}, u32[]{:S(2)}) copy-start(bf16[128,2048]{1,0:T(8,128)(2,1)} %rest_2_.1) | copy-start | bytes 1572868
  7.8 20.3 %collective-permute-start.4 = (bf16[128,2048]{1,0:T(8,128)(2,1)S(1)}, bf16[128,2048]{1,0:T(8,128)(2,1)S(1)}, u32[]{:S(2)}, u32[]{:S(2)}) collective-permute-start(bf16[128,2048]{1,0:T(8,128)(2,1)S(1)} %copy-done.5), channel_id=1, source_target_pairs={{0,4},{2,6},{4,0},{6,2},{1,5},{3,7},{5,1},{7,3},{8,12},{10,14},{12... | collective-permute-start | bytes 1572872 | tf_op jit(solution)/shard_map/ppermute | solution.py:60
  10.8 17.2 %collective-permute-start.3 = (bf16[128,2048]{1,0:T(8,128)(2,1)S(1)}, bf16[128,2048]{1,0:T(8,128)(2,1)}, u32[]{:S(2)}, u32[]{:S(2)}) collective-permute-start(bf16[128,2048]{1,0:T(8,128)(2,1)S(1)} %copy-done.5), channel_id=1, source_target_pairs={{0,2},{2,0},{4,6},{6,4},{1,3},{3,1},{5,7},{7,5},{8,10},{10,8},{12,... | collective-permute-start | bytes 1572872 | tf_op jit(solution)/shard_map/ppermute | solution.py:60
  12.3 6.8 %collective-permute-start = (bf16[16,2048]{1,0:T(8,128)(2,1)S(1)}, bf16[16,2048]{1,0:T(8,128)(2,1)S(1)}, u32[]{:S(2)}, u32[]{:S(2)}) collective-permute-start(bf16[16,2048]{1,0:T(8,128)(2,1)S(1)} %get-tuple-element.33), channel_id=1, source_target_pairs={{0,8},{8,16},{16,24},{24,0},{1,9},{9,17},{17,25},{25,1},{2,10},{10... | collective-permute-start | bytes 196616 | tf_op jit(solution)/shard_map/ppermute | solution.py:39
  13.9 7.2 %collective-permute-start.1 = (bf16[16,2048]{1,0:T(8,128)(2,1)S(1)}, bf16[16,2048]{1,0:T(8,128)(2,1)S(1)}, u32[]{:S(2)}, u32[]{:S(2)}) collective-permute-start(bf16[16,2048]{1,0:T(8,128)(2,1)S(1)} %get-tuple-element.34), channel_id=1, source_target_pairs={{0,16},{8,24},{16,0},{24,8},{1,17},{9,25},{17,1},{25,9},{2,18},{10... | collective-permute-start | bytes 196616 | tf_op jit(solution)/shard_map/ppermute | solution.py:39
  16.5 4.7 %collective-permute-start.2 = (bf16[16,2048]{1,0:T(8,128)(2,1)S(1)}, bf16[16,2048]{1,0:T(8,128)(2,1)S(1)}, u32[]{:S(2)}, u32[]{:S(2)}) collective-permute-start(bf16[16,2048]{1,0:T(8,128)(2,1)S(1)} %get-tuple-element.35), channel_id=1, source_target_pairs={{0,24},{8,0},{16,8},{24,16},{1,25},{9,1},{17,9},{25,17},{2,26},{10... | collective-permute-start | bytes 196616 | tf_op jit(solution)/shard_map/ppermute | solution.py:39
  21.1 0.7 copy-start.14
  23.4 4.7 %copy-start.2 = (bf16[1024,1024]{1,0:T(8,128)(2,1)S(1)}, bf16[1024,1024]{1,0:T(8,128)(2,1)}, u32[]{:S(2)}) copy-start(bf16[1024,1024]{1,0:T(8,128)(2,1)} %x_ref.1) | copy-start | bytes 6291460
  23.4 4.7 %copy-start.15 = (s32[60]{0:T(128)S(1)}, s32[60]{0:T(128)}, u32[]{:S(2)}) copy-start(s32[60]{0:T(128)} %copy-done.13) | copy-start | bytes 724
  23.4 54.7 %all-to-all-start = ((bf16[4,2176,128]{2,1,0:T(8,128)(2,1)}), bf16[4,2176,128]{2,1,0:T(8,128)(2,1)}, u32[]{:S(2)}, u32[]{:S(2)}) async-start(bf16[4,2176,128]{2,1,0:T(8,128)(2,1)} %get-tuple-element.38), calls=%async_computation | async-start | bytes 4456448 | tf_op jit(solution)/shard_map/all_to_all | solution.py:515
  28.1 2.2 %copy-start = (bf16[1024,2048]{1,0:T(8,128)(2,1)S(1)}, bf16[1024,2048]{1,0:T(8,128)(2,1)}, u32[]{:S(2)}) copy-start(bf16[1024,2048]{1,0:T(8,128)(2,1)} %w_ref.5) | copy-start | bytes 12582916
  33.9 10.9 %collective-permute-start.11 = (bf16[4,128,2048]{2,1,0:T(8,128)(2,1)S(1)}, bf16[4,128,2048]{2,1,0:T(8,128)(2,1)S(1)}, u32[]{:S(2)}, u32[]{:S(2)}) collective-permute-start(bf16[4,128,2048]{2,1,0:T(8,128)(2,1)S(1)} %bitcast.71), channel_id=1, source_target_pairs={{0,1},{1,0},{2,3},{3,2},{4,5},{5,4},{6,7},{7,6},{8,9},{9,8},{10,11... | collective-permute-start | bytes 6291464 | tf_op jit(solution)/shard_map/ppermute | solution.py:60
  34.0 8.8 %collective-permute-start.5 = (bf16[64,2048]{1,0:T(8,128)(2,1)S(1)}, bf16[64,2048]{1,0:T(8,128)(2,1)S(1)}, u32[]{:S(2)}, u32[]{:S(2)}) collective-permute-start(bf16[64,2048]{1,0:T(8,128)(2,1)S(1)} %slice.55), channel_id=1, source_target_pairs={{0,2},{2,0},{4,6},{6,4},{1,3},{3,1},{5,7},{7,5},{8,10},{10,8},{12,... | collective-permute-start | bytes 786440 | tf_op jit(solution)/shard_map/ppermute | solution.py:60
  35.6 8.5 %collective-permute-start.6 = (bf16[64,2048]{1,0:T(8,128)(2,1)S(1)}, bf16[64,2048]{1,0:T(8,128)(2,1)S(1)}, u32[]{:S(2)}, u32[]{:S(2)}) collective-permute-start(bf16[64,2048]{1,0:T(8,128)(2,1)S(1)} %slice.56), channel_id=1, source_target_pairs={{0,4},{2,6},{4,0},{6,2},{1,5},{3,7},{5,1},{7,3},{8,12},{10,14},{12... | collective-permute-start | bytes 786440 | tf_op jit(solution)/shard_map/ppermute | solution.py:60
  36.1 11.2 %collective-permute-start.7 = (bf16[128,2048]{1,0:T(8,128)(2,1)S(1)}, bf16[128,2048]{1,0:T(8,128)(2,1)S(1)}, u32[]{:S(2)}, u32[]{:S(2)}) collective-permute-start(bf16[128,2048]{1,0:T(8,128)(2,1)S(1)} %copy-done.5), channel_id=1, source_target_pairs={{0,1},{1,0},{2,3},{3,2},{4,5},{5,4},{6,7},{7,6},{8,9},{9,8},{10,11... | collective-permute-start | bytes 1572872 | tf_op jit(solution)/shard_map/ppermute | solution.py:60
  36.1 16.2 %collective-permute-start.8 = (bf16[128,2048]{1,0:T(8,128)(2,1)}, bf16[128,2048]{1,0:T(8,128)(2,1)}, u32[]{:S(2)}, u32[]{:S(2)}) collective-permute-start(bf16[128,2048]{1,0:T(8,128)(2,1)} %collective-permute-done.3.rest_1_.rest_3_), channel_id=1, source_target_pairs={{0,1},{1,0},{2,3},{3,2},{4,5},{5,4},{6,7},{7,6},{8,9},{9,8},{10,11... | collective-permute-start | bytes 1572872 | tf_op jit(solution)/shard_map/ppermute | solution.py:60
  42.8 9.5 %collective-permute-start.9 = (bf16[128,2048]{1,0:T(8,128)(2,1)S(1)}, bf16[128,2048]{1,0:T(8,128)(2,1)}, u32[]{:S(2)}, u32[]{:S(2)}) collective-permute-start(bf16[128,2048]{1,0:T(8,128)(2,1)S(1)} %collective-permute-done.4.rest_2_.rest_4_), channel_id=1, source_target_pairs={{0,1},{1,0},{2,3},{3,2},{4,5},{5,4},{6,7},{7,6},{8,9},{9,8},{10,11... | collective-permute-start | bytes 1572872 | tf_op jit(solution)/shard_map/ppermute | solution.py:60
  44.8 7.5 %collective-permute-start.10 = (bf16[128,2048]{1,0:T(8,128)(2,1)}, bf16[128,2048]{1,0:T(8,128)(2,1)}, u32[]{:S(2)}, u32[]{:S(2)}) collective-permute-start(bf16[128,2048]{1,0:T(8,128)(2,1)} %constant_dynamic-update-slice_fusion.rest_3_.rest_5_), channel_id=1, source_target_pairs={{0,1},{1,0},{2,3},{3,2},{4,5},{5,4},{6,7},{7,6},{8,9},{9,8},{10,11... | collective-permute-start | bytes 1572872 | tf_op jit(solution)/shard_map/ppermute | solution.py:60
  46.8 18.6 %collective-permute-start.13 = (bf16[128,2048]{1,0:T(8,128)(2,1)}, bf16[128,2048]{1,0:T(8,128)(2,1)}, u32[]{:S(2)}, u32[]{:S(2)}) collective-permute-start(bf16[128,2048]{1,0:T(8,128)(2,1)} %get-tuple-element.62), channel_id=1, source_target_pairs={{0,4},{2,6},{4,0},{6,2},{1,5},{3,7},{5,1},{7,3},{8,12},{10,14},{12... | collective-permute-start | bytes 1572872 | tf_op jit(solution)/shard_map/ppermute | solution.py:60
  47.3 0.8 copy-start.8
  48.1 17.3 %collective-permute-start.12 = (bf16[128,2048]{1,0:T(8,128)(2,1)}, bf16[128,2048]{1,0:T(8,128)(2,1)}, u32[]{:S(2)}, u32[]{:S(2)}) collective-permute-start(bf16[128,2048]{1,0:T(8,128)(2,1)} %get-tuple-element.63), channel_id=1, source_target_pairs={{0,2},{2,0},{4,6},{6,4},{1,3},{3,1},{5,7},{7,5},{8,10},{10,8},{12,... | collective-permute-start | bytes 1572872 | tf_op jit(solution)/shard_map/ppermute | solution.py:60
  52.3 2.2 %copy-start.1 = (bf16[1024,2048]{1,0:T(8,128)(2,1)S(1)}, bf16[1024,2048]{1,0:T(8,128)(2,1)}, u32[]{:S(2)}) copy-start(bf16[1024,2048]{1,0:T(8,128)(2,1)} %w_ref.5) | copy-start | bytes 12582916
  54.5 1.0 copy-start.9
  63.5 2.0 %copy-start.3 = (f32[1024,1024]{1,0:T(8,128)}, f32[1024,1024]{1,0:T(8,128)S(1)}, u32[]{:S(2)}) copy-start(f32[1024,1024]{1,0:T(8,128)S(1)} %cotangent_product.1.base_ref) | copy-start | bytes 12582916
  78.1 56.1 %all-to-all-start.1 = ((bf16[4,256,1024]{2,1,0:T(8,128)(2,1)}), bf16[4,256,1024]{2,1,0:T(8,128)(2,1)}, u32[]{:S(2)}, u32[]{:S(2)}) async-start(bf16[4,256,1024]{2,1,0:T(8,128)(2,1)} %bitcast.72), calls=%async_computation.1 | async-start | bytes 4194304 | tf_op jit(solution)/shard_map/all_to_all | solution.py:542
  82.5 14.0 %collective-permute-start.14 = (bf16[128,2048]{1,0:T(8,128)(2,1)}, bf16[128,2048]{1,0:T(8,128)(2,1)S(1)}, u32[]{:S(2)}, u32[]{:S(2)}) collective-permute-start(bf16[128,2048]{1,0:T(8,128)(2,1)} %get-tuple-element.61), channel_id=1, source_target_pairs={{0,6},{2,4},{4,2},{6,0},{1,7},{3,5},{5,3},{7,1},{8,14},{10,12},{12... | collective-permute-start | bytes 1572872 | tf_op jit(solution)/shard_map/ppermute | solution.py:60
  98.9 17.2 %copy-start.10 = (bf16[128,2048]{1,0:T(8,128)(2,1)S(1)}, bf16[128,2048]{1,0:T(8,128)(2,1)}, u32[]{:S(2)}) copy-start(bf16[128,2048]{1,0:T(8,128)(2,1)} %copy-done.8) | copy-start | bytes 1572868
  99.0 4.6 %collective-permute-start.15 = (bf16[4,128,128]{2,1,0:T(8,128)(2,1)S(1)}, bf16[4,128,128]{2,1,0:T(8,128)(2,1)S(1)}, u32[]{:S(2)}, u32[]{:S(2)}) collective-permute-start(bf16[4,128,128]{2,1,0:T(8,128)(2,1)S(1)} %slice_bitcast_fusion.8), channel_id=1, source_target_pairs={{0,1},{1,0},{2,3},{3,2},{4,5},{5,4},{6,7},{7,6},{8,9},{9,8},{10,11... | collective-permute-start | bytes 393224 | tf_op jit(solution)/shard_map/ppermute | solution.py:60
  100.0 5.9 %collective-permute-start.20 = (bf16[4,128,128]{2,1,0:T(8,128)(2,1)S(1)}, bf16[4,128,128]{2,1,0:T(8,128)(2,1)S(1)}, u32[]{:S(2)}, u32[]{:S(2)}) collective-permute-start(bf16[4,128,128]{2,1,0:T(8,128)(2,1)S(1)} %get-tuple-element.65), channel_id=1, source_target_pairs={{0,4},{2,6},{4,0},{6,2},{1,5},{3,7},{5,1},{7,3},{8,12},{10,14},{12... | collective-permute-start | bytes 393224 | tf_op jit(solution)/shard_map/ppermute | solution.py:60
  100.6 6.6 %collective-permute-start.19 = (bf16[4,128,128]{2,1,0:T(8,128)(2,1)S(1)}, bf16[4,128,128]{2,1,0:T(8,128)(2,1)S(1)}, u32[]{:S(2)}, u32[]{:S(2)}) collective-permute-start(bf16[4,128,128]{2,1,0:T(8,128)(2,1)S(1)} %get-tuple-element.65), channel_id=1, source_target_pairs={{0,2},{2,0},{4,6},{6,4},{1,3},{3,1},{5,7},{7,5},{8,10},{10,8},{12,... | collective-permute-start | bytes 393224 | tf_op jit(solution)/shard_map/ppermute | solution.py:60
  101.0 9.9 %collective-permute-start.21 = (bf16[4,128,128]{2,1,0:T(8,128)(2,1)S(1)}, bf16[4,128,128]{2,1,0:T(8,128)(2,1)S(1)}, u32[]{:S(2)}, u32[]{:S(2)}) collective-permute-start(bf16[4,128,128]{2,1,0:T(8,128)(2,1)S(1)} %get-tuple-element.65), channel_id=1, source_target_pairs={{0,6},{2,4},{4,2},{6,0},{1,7},{3,5},{5,3},{7,1},{8,14},{10,12},{12... | collective-permute-start | bytes 393224 | tf_op jit(solution)/shard_map/ppermute | solution.py:60
  103.6 9.9 %collective-permute-start.18 = (bf16[4,128,128]{2,1,0:T(8,128)(2,1)S(1)}, bf16[4,128,128]{2,1,0:T(8,128)(2,1)S(1)}, u32[]{:S(2)}, u32[]{:S(2)}) collective-permute-start(bf16[4,128,128]{2,1,0:T(8,128)(2,1)S(1)} %fusion.3), channel_id=1, source_target_pairs={{0,6},{2,4},{4,2},{6,0},{1,7},{3,5},{5,3},{7,1},{8,14},{10,12},{12... | collective-permute-start | bytes 393224 | tf_op jit(solution)/shard_map/ppermute | solution.py:60
  104.0 10.4 %collective-permute-start.17 = (bf16[4,128,128]{2,1,0:T(8,128)(2,1)S(1)}, bf16[4,128,128]{2,1,0:T(8,128)(2,1)S(1)}, u32[]{:S(2)}, u32[]{:S(2)}) collective-permute-start(bf16[4,128,128]{2,1,0:T(8,128)(2,1)S(1)} %fusion.3), channel_id=1, source_target_pairs={{0,4},{2,6},{4,0},{6,2},{1,5},{3,7},{5,1},{7,3},{8,12},{10,14},{12... | collective-permute-start | bytes 393224 | tf_op jit(solution)/shard_map/ppermute | solution.py:60
  106.0 8.7 %collective-permute-start.16 = (bf16[4,128,128]{2,1,0:T(8,128)(2,1)S(1)}, bf16[4,128,128]{2,1,0:T(8,128)(2,1)S(1)}, u32[]{:S(2)}, u32[]{:S(2)}) collective-permute-start(bf16[4,128,128]{2,1,0:T(8,128)(2,1)S(1)} %fusion.3), channel_id=1, source_target_pairs={{0,2},{2,0},{4,6},{6,4},{1,3},{3,1},{5,7},{7,5},{8,10},{10,8},{12,... | collective-permute-start | bytes 393224 | tf_op jit(solution)/shard_map/ppermute | solution.py:60
  110.9 14.6 %copy-start.6 = (bf16[4,4,128,128]{3,2,1,0:T(8,128)(2,1)}, bf16[4,4,128,128]{3,2,1,0:T(8,128)(2,1)S(1)}, u32[]{:S(2)}) copy-start(bf16[4,4,128,128]{3,2,1,0:T(8,128)(2,1)S(1)} %pad_maximum_fusion.rest_0_) | copy-start | bytes 1572868
  110.9 14.6 %collective-permute-start.22 = (bf16[4,4,128,128]{3,2,1,0:T(8,128)(2,1)S(1)}, bf16[4,4,128,128]{3,2,1,0:T(8,128)(2,1)S(1)}, u32[]{:S(2)}, u32[]{:S(2)}) collective-permute-start(bf16[4,4,128,128]{3,2,1,0:T(8,128)(2,1)S(1)} %pad_maximum_fusion.rest_0_), channel_id=1, source_target_pairs={{0,1},{1,0},{2,3},{3,2},{4,5},{5,4},{6,7},{7,6},{8,9},{9,8},{10,11... | collective-permute-start | bytes 1572872 | tf_op jit(solution)/shard_map/ppermute | solution.py:60
  114.7 8.3 %copy-start.7 = (f32[128,2048]{1,0:T(8,128)S(1)}, f32[128,2048]{1,0:T(8,128)}, u32[]{:S(2)}) copy-start(f32[128,2048]{1,0:T(8,128)} %get-tuple-element.60.rest_0_) | copy-start | bytes 3145732
  114.7 1.4 %collective-permute-start.23 = (bf16[4,128,128]{2,1,0:T(8,128)(2,1)S(1)}, bf16[4,128,128]{2,1,0:T(8,128)(2,1)S(1)}, u32[]{:S(2)}, u32[]{:S(2)}) collective-permute-start(bf16[4,128,128]{2,1,0:T(8,128)(2,1)S(1)} %add_convert_fusion.low_ref.rest_0_), channel_id=1, source_target_pairs={{0,1},{1,0},{2,3},{3,2},{4,5},{5,4},{6,7},{7,6},{8,9},{9,8},{10,11... | collective-permute-start | bytes 393224 | tf_op jit(solution)/shard_map/ppermute | solution.py:60
  116.2 9.3 %copy-start.4 = (f32[1024,1024]{1,0:T(8,128)S(1)}, f32[1024,1024]{1,0:T(8,128)}, u32[]{:S(2)}) copy-start(f32[1024,1024]{1,0:T(8,128)} %copy-done.3) | copy-start | bytes 12582916
  118.4 20.9 %collective-permute-start.26 = (bf16[8,16,256]{2,1,0:T(8,128)(2,1)S(1)}, bf16[8,16,256]{2,1,0:T(8,128)(2,1)S(1)}, u32[]{:S(2)}, u32[]{:S(2)}) collective-permute-start(bf16[8,16,256]{2,1,0:T(8,128)(2,1)S(1)} %get-tuple-element.66), channel_id=1, source_target_pairs={{0,24},{8,0},{16,8},{24,16},{1,25},{9,1},{17,9},{25,17},{2,26},{10... | collective-permute-start | bytes 196616 | tf_op jit(solution)/shard_map/ppermute | solution.py:39
  121.9 17.5 %collective-permute-start.25 = (bf16[8,16,256]{2,1,0:T(8,128)(2,1)S(1)}, bf16[8,16,256]{2,1,0:T(8,128)(2,1)S(1)}, u32[]{:S(2)}, u32[]{:S(2)}) collective-permute-start(bf16[8,16,256]{2,1,0:T(8,128)(2,1)S(1)} %get-tuple-element.67), channel_id=1, source_target_pairs={{0,16},{8,24},{16,0},{24,8},{1,17},{9,25},{17,1},{25,9},{2,18},{10... | collective-permute-start | bytes 196616 | tf_op jit(solution)/shard_map/ppermute | solution.py:39
  121.9 17.5 %collective-permute-start.24 = (bf16[8,16,256]{2,1,0:T(8,128)(2,1)S(1)}, bf16[8,16,256]{2,1,0:T(8,128)(2,1)S(1)}, u32[]{:S(2)}, u32[]{:S(2)}) collective-permute-start(bf16[8,16,256]{2,1,0:T(8,128)(2,1)S(1)} %get-tuple-element.68), channel_id=1, source_target_pairs={{0,8},{8,16},{16,24},{24,0},{1,9},{9,17},{17,25},{25,1},{2,10},{10... | collective-permute-start | bytes 196616 | tf_op jit(solution)/shard_map/ppermute | solution.py:39
  125.5 4.7 %copy-start.11 = (bf16[4,4,128,128]{3,2,1,0:T(8,128)(2,1)}, bf16[4,4,128,128]{3,2,1,0:T(8,128)(2,1)S(1)}, u32[]{:S(2)}) copy-start(bf16[4,4,128,128]{3,2,1,0:T(8,128)(2,1)S(1)} %collective-permute-done.22.rest_1_) | copy-start | bytes 1572868
  130.2 9.2 %copy-start.16 = (s32[60]{0:T(128)S(1)}, s32[60]{0:T(128)}, u32[]{:S(2)}) copy-start(s32[60]{0:T(128)} %copy-done.13) | copy-start | bytes 724

commit v12 on v11

--- a/solution.py
+++ b/solution.py
@@ -72,67 +72,56 @@
     return came, one, two
 
 
-def pick_up(at, slot_of, adapter_up, data_count):
-    def kernel(at_ref, up_ref, *rest):
-        out_refs, sems = rest[:data_count], rest[data_count]
-        copies = []
-        for k in range(data_count):
-            data = wrap(at_ref[0] + k, data_count)
-            slot = slot_of(at_ref, data, at_ref[3])
-            copies.append(pltpu.make_async_copy(up_ref.at[slot], out_refs[k], sems.at[k]))
-        for copy in copies:
-            copy.start()
-        for copy in copies:
-            copy.wait()
-
-    return call(
-        kernel,
-        "pick_up",
-        out_shape=(jax.ShapeDtypeStruct(adapter_up.shape[1:], adapter_up.dtype),) * data_count,
-        in_specs=[SMEM, HBM],
-        out_specs=(VMEM,) * data_count,
-        scratch_shapes=[pltpu.SemaphoreType.DMA((data_count,))],
-    )(at, adapter_up)
-
-
-def pick_down(at, slot_of, adapter_down, data_count, blocks_dev, spare):
+def pick(tenant_of_block, slot_of_tenant, adapter_down, adapter_up, group_rows, spare):
+    data_count = lax.axis_size("dp")
+    blocks_dev = tenant_of_block.shape[0] // data_count
     down_rows, ranks = adapter_down.shape[1:]
     used = blocks_dev * down_rows
 
-    def kernel(at_ref, down_ref, out_ref, rows, down_sem, out_sem):
-        downs, outs = [], []
+    def kernel(tenant_ref, slot_ref, down_ref, up_ref, *rest):
+        up_refs, (out_ref, rows, up_sem, down_sem, out_sem) = rest[:data_count], rest[data_count:]
+        own_block = lax.axis_index(("pipe", "tensor")) * group_rows // BLOCK
+        ups, downs, outs = [], [], []
+        for k in range(data_count):
+            data = wrap(lax.axis_index("dp") + k, data_count)
+            slot = slot_ref[tenant_ref[data * blocks_dev + own_block]]
+            ups.append(pltpu.make_async_copy(up_ref.at[slot], up_refs[k], up_sem.at[k]))
+            ups[-1].start()
         for data in range(data_count):
             downs.append([])
             for block in range(blocks_dev):
                 here = rows.at[data, pl.ds(block * down_rows, down_rows)]
-                slot = slot_of(at_ref, data, block)
+                slot = slot_ref[tenant_ref[data * blocks_dev + block]]
                 downs[data].append(
                     pltpu.make_async_copy(down_ref.at[slot], here, down_sem.at[data, block])
                 )
+                downs[data][-1].start()
             there = out_ref.at[data, pl.ds(0, used)]
             outs.append(pltpu.make_async_copy(rows.at[data], there, out_sem.at[data]))
-            for copy in downs[data]:
-                copy.start()
         for data in range(data_count):
             for copy in downs[data]:
                 copy.wait()
             outs[data].start()
-        for copy in outs:
+        for copy in ups + outs:
             copy.wait()
 
-    return call(
-        kernel,
-        "pick_down",
+    up_shape = jax.ShapeDtypeStruct(adapter_up.shape[1:], adapter_up.dtype)
+    out = call(
+        kernel,
+        "pick_rows",
         VMEM_MOST,
-        out_shape=pltpu.HBM((data_count, used + spare, ranks), adapter_down.dtype),
-        in_specs=[SMEM, HBM],
-        out_specs=HBM,
+        out_shape=(up_shape,) * data_count
+        + (pltpu.HBM((data_count, used + spare, ranks), adapter_down.dtype),),
+        in_specs=[SMEM, SMEM, HBM, HBM],
+        out_specs=(VMEM,) * data_count + (HBM,),
         scratch_shapes=[
             pltpu.VMEM((data_count, used, ranks), adapter_down.dtype),
+            pltpu.SemaphoreType.DMA((data_count,)),
             pltpu.SemaphoreType.DMA((data_count, blocks_dev)),
             pltpu.SemaphoreType.DMA((data_count,)),
         ],
-    )(at, adapter_down)
+    )(tenant_of_block, slot_of_tenant, adapter_down, adapter_up)
+    return out[:data_count], out[data_count]
 
 
 def base_product(at, tokens, weight, first, count):
@@ -282,45 +271,64 @@
     pipe_count, _, rows, _ = grad_pieces[0].shape
     blocks_dev = tok_dev // BLOCK
 
+    parts = 2 if down_rows % 256 == 0 else 1
+    part_rows = down_rows // parts
+
     def kernel(at_ref, x_ref, *rest):
-        grad_refs, (out_ref, grad, x, products, sems) = rest[:tensor_count], rest[tensor_count:]
-        copies = [
-            pltpu.make_async_copy(x_ref.at[data], x.at[data], sems.at[data])
-            for data in range(data_count)
-        ]
-        for copy in copies:
-            copy.start()
+        grad_refs, rest = rest[:tensor_count], rest[tensor_count:]
+        out_ref, grad, x, total, products, x_sem, grad_sem, out_sem = rest
+        copies = []
         for s in range(tensor_count):
             core = came_from(at_ref[2], s, tensor_count)
             for k in range(pipe_count):
                 chip = came_from(at_ref[1], k, pipe_count)
                 first = pl.multiple_of((chip * tensor_count + core) * rows, rows)
-                for data in range(data_count):
-                    grad[data, pl.ds(first, rows)] = grad_refs[s][k, data]
-        out_ref[...] = jnp.zeros(out_ref.shape, out_ref.dtype)
-        for data in range(data_count):
-            copies[data].wait()
-            for block in range(blocks_dev):
-                here = slice(block * BLOCK, (block + 1) * BLOCK)
-                products[data % 2, block] = jnp.dot(
-                    x[data, :, here], grad[data, here], preferred_element_type=jnp.float32
-                )
-            for block in range(blocks_dev):
-                slot = slot_of(at_ref, data, block)
-                out_ref[slot] += products[data % 2, block]
+                there = grad.at[:, pl.ds(first, rows)]
+                copies.append(pltpu.make_async_copy(grad_refs[s].at[k], there, grad_sem.at[s, k]))
+        x_copies = [
+            pltpu.make_async_copy(x_ref.at[data], x.at[data], x_sem.at[data])
+            for data in range(data_count)
+        ]
+        for copy in copies + x_copies:
+            copy.start()
+        total[...] = jnp.zeros(total.shape, total.dtype)
+        for copy in copies:
+            copy.wait()
+        outs = []
+        for part in range(parts):
+            at = slice(part * part_rows, (part + 1) * part_rows)
+            for data in range(data_count):
+                if part == 0:
+                    x_copies[data].wait()
+                for block in range(blocks_dev):
+                    here = slice(block * BLOCK, (block + 1) * BLOCK)
+                    products[data % 2, block] = jnp.dot(
+                        x[data, at, here], grad[data, here], preferred_element_type=jnp.float32
+                    )
+                for block in range(blocks_dev):
+                    slot = slot_of(at_ref, data, block)
+                    total[part, slot] += products[data % 2, block]
+            there = out_ref.at[:, pl.ds(part * part_rows, part_rows)]
+            outs.append(pltpu.make_async_copy(total.at[part], there, out_sem.at[part]))
+            outs[-1].start()
+        for copy in outs:
+            copy.wait()
 
     return call(
         kernel,
         "grad_down",
         VMEM_MOST,
-        in_specs=[SMEM, HBM] + [VMEM] * tensor_count,
-        out_specs=VMEM,
-        out_shape=jax.ShapeDtypeStruct((slots, down_rows, RANKS), jnp.float32),
+        in_specs=[SMEM, HBM] + [HBM] * tensor_count,
+        out_specs=HBM,
+        out_shape=pltpu.HBM((slots, down_rows, RANKS), jnp.float32),
         scratch_shapes=[
             pltpu.VMEM((data_count, tok_dev, RANKS), jnp.bfloat16),
             pltpu.VMEM(x_features.shape, jnp.bfloat16),
-            pltpu.VMEM((2, blocks_dev, down_rows, RANKS), jnp.float32),
+            pltpu.VMEM((parts, slots, part_rows, RANKS), jnp.float32),
+            pltpu.VMEM((2, blocks_dev, part_rows, RANKS), jnp.float32),
             pltpu.SemaphoreType.DMA((data_count,)),
+            pltpu.SemaphoreType.DMA((tensor_count, pipe_count)),
+            pltpu.SemaphoreType.DMA((parts,)),
         ],
     )(at, x_features, *grad_pieces)
 
@@ -498,24 +506,22 @@
     slots = adapter_down.shape[0]
     blocks = tenant_of_block.shape[0]
 
-    own_block = my_group * rows // BLOCK
-    at = jnp.stack([at_data, at_pipe, at_tensor, own_block]).astype(jnp.int32)
+    at = jnp.stack([at_data, at_pipe, at_tensor]).astype(jnp.int32)
     at = jnp.concatenate([at, tenant_of_block, slot_of_tenant])
 
     def slot_of(at_ref, data, block):
-        return at_ref[4 + blocks + at_ref[4 + data * blocks_dev + block]]
-
-    b_send = pick_up(at, slot_of, adapter_up, data_count)
+        return at_ref[3 + blocks + at_ref[3 + data * blocks_dev + block]]
+
+    b_send, a_send = pick(
+        tenant_of_block, slot_of_tenant, adapter_down, adapter_up, rows, rows
+    )
     b_came = [b_send[0]] + [shift(b_send[k], "dp", k) for k in range(1, data_count)]
 
-    adapter_down, b_send = lax.optimization_barrier((adapter_down, b_send))
-    a_send = pick_down(at, slot_of, adapter_down, data_count, blocks_dev, rows)
-    a_send, cot_send = lax.optimization_barrier((a_send, cotangent))
     b_own, a_send = own_rows(at, b_came, cotangent, a_send)
     a_recv = lax.all_to_all(a_send, "dp", 0, 0, tiled=True)
 
     behind, a_send = lax.optimization_barrier((tokens, a_send))
-    cot_chips, base_tokens, x_tokens = gather_chips(cot_send, behind)
+    cot_chips, base_tokens, x_tokens = gather_chips(cotangent, behind)
     cot_chips = [cotangent] + cot_chips
 
     tokens_by_group = base_tokens.reshape(pipe_count, tensor_count, rows, feature_count)

time: 142 us -> 140 us (0.986)
  local copies, waits for them, and re-layouts: 17.1 us -> 15.2 us
    pallas_call x3 -> x2, Pallas kernels: 10.1 us -> 9.87 us  [the longest x1 5.05 us: grad_down(): call(kernel, 'grad_down', VMEM_MOST, in_specs=[SMEM, HBM] + [HBM] * tenso...]
  transfers between devices with their start and end apart: 29 -> 29, of which waited for: 14 -> 13; matrix products, arithmetic and copies ran while one was open for 6% -> 6% of each run, Pallas kernels for 24% -> 28%
where the time goes in v12:
time: 140 us; the launch traced here: 139 us
  waiting for transfers between devices  45.7 us (33%)
  Pallas kernels  39.8 us (28%)
  starting transfers between devices  34.9 us (25%)
  local copies, waits for them, and re-layouts  15.2 us (11%)
  other arithmetic  2.21 us (2%)
    ppermute x21, waiting for transfers between devices, swap(): lax.ppermute(piece, axis, [(i, partner(i, k, count)) for i in range(count)])  25.7 us
    ppermute x21, starting transfers between devices, swap(): lax.ppermute(piece, axis, [(i, partner(i, k, count)) for i in range(count)])  15.7 us
    all_to_all x1, waiting for transfers between devices, body(): a_recv = lax.all_to_all(a_send, 'dp', 0, 0, tiled=True)  12.6 us
    ppermute x6, starting transfers between devices, shift(): lax.ppermute(piece, axis, [(i, (i + k) % count) for i in range(count)])  10.2 us
    unnamed x35, local copies, waits for them, and re-layouts  9.79 us
    pallas_call x1, Pallas kernels, cotangent_product(): call(kernel, 'cotangent_product', grid=(depth // tile,), in_specs=[SMEM,...  7.96 us
    pallas_call x2, Pallas kernels, base_product(): call(kernel, 'base_product', grid_spec=pltpu.PrefetchScalarGridSpec(num_s...  7.22 us
    pallas_call x1, Pallas kernels, grad_down(): call(kernel, 'grad_down', VMEM_MOST, in_specs=[SMEM, HBM] + [HBM] * tenso...  5.05 us
  transfers between devices with their start and end apart: 29, of which 13 were waited for; matrix products, arithmetic and copies ran while one was open for 6% of the time, Pallas kernels for 28%

profile of v12, /device:TPU:0, one launch (start us, length us, event | category | flops | bytes accessed | tf_op | source)
XLA Modules:
  0.0 138.8 jit_solution(13681237292711966047)
XLA Ops:
  0.7 3.0 %collective-permute-start.4 = (bf16[128,2048]{1,0:T(8,128)(2,1)}, bf16[128,2048]{1,0:T(8,128)(2,1)S(1)}, u32[]{:S(2)}, u32[]{:S(2)}) collective-permute-start(bf16[128,2048]{1,0:T(8,128)(2,1)} %rest_2_.1), channel_id=1, source_target_pairs={{0,4},{2,6},{4,0},{6,2},{1,5},{3,7},{5,1},{7,3},{8,12},{10,14},{12... | collective-permute-start | bytes 1572872 | tf_op jit(solution)/shard_map/ppermute | solution.py:60
  3.7 1.5 %collective-permute-start.3 = (bf16[128,2048]{1,0:T(8,128)(2,1)}, bf16[128,2048]{1,0:T(8,128)(2,1)}, u32[]{:S(2)}, u32[]{:S(2)}) collective-permute-start(bf16[128,2048]{1,0:T(8,128)(2,1)} %rest_2_.1), channel_id=1, source_target_pairs={{0,2},{2,0},{4,6},{6,4},{1,3},{3,1},{5,7},{7,5},{8,10},{10,8},{12,... | collective-permute-start | bytes 1572872 | tf_op jit(solution)/shard_map/ppermute | solution.py:60
  5.2 4.8 %pick_rows.1 = (bf16[16,2048]{1,0:T(8,128)(2,1)}, bf16[16,2048]{1,0:T(8,128)(2,1)}, bf16[16,2048]{1,0:T(8,128)(2,1)}, bf16[16,2048]{1,0:T(8,128)(2,1)}, bf16[4,2176,128]{2,1,0:T(8,128)(2,1)}) custom-call(s32[32]{0:T(128)} %tenant_ref.1, s32[24]{0:T(128)} %slot_ref.1, bf16[24,256,128]{2,1,0:T(8,128)(2,1)} %down_ref.1, bf16[24,16,2048]{2,1,0:T(8,128)(2,1)} %up_ref.1), custom_call_target="tpu_custom_call" | custom-call | flops 1024 | bytes 1024 | tf_op jit(solution)/shard_map/pick_rows/pallas_call | solution.py:109
  10.0 1.6 %collective-permute-start = (bf16[16,2048]{1,0:T(8,128)(2,1)}, bf16[16,2048]{1,0:T(8,128)(2,1)S(1)}, u32[]{:S(2)}, u32[]{:S(2)}) collective-permute-start(bf16[16,2048]{1,0:T(8,128)(2,1)} %get-tuple-element.32), channel_id=1, source_target_pairs={{0,8},{8,16},{16,24},{24,0},{1,9},{9,17},{17,25},{25,1},{2,10},{10... | collective-permute-start | bytes 196616 | tf_op jit(solution)/shard_map/ppermute | solution.py:39
  11.6 2.6 %collective-permute-start.1 = (bf16[16,2048]{1,0:T(8,128)(2,1)}, bf16[16,2048]{1,0:T(8,128)(2,1)S(1)}, u32[]{:S(2)}, u32[]{:S(2)}) collective-permute-start(bf16[16,2048]{1,0:T(8,128)(2,1)} %get-tuple-element.33), channel_id=1, source_target_pairs={{0,16},{8,24},{16,0},{24,8},{1,17},{9,25},{17,1},{25,9},{2,18},{10... | collective-permute-start | bytes 196616 | tf_op jit(solution)/shard_map/ppermute | solution.py:39
  14.2 1.4 collective-permute-start.2
  15.6 0.1 concatenate.6.at_ref
  15.7 1.4 %collective-permute-done.rest_1_ = bf16[16,2048]{1,0:T(8,128)(2,1)S(1)} collective-permute-done((bf16[16,2048]{1,0:T(8,128)(2,1)}, bf16[16,2048]{1,0:T(8,128)(2,1)S(1)}, u32[]{:S(2)}, u32[]{:S(2)}) %collective-permute-start) | collective-permute-done | bytes 65568 | tf_op jit(solution)/shard_map/ppermute | solution.py:39
  17.1 2.0 %collective-permute-done.1.rest_2_ = bf16[16,2048]{1,0:T(8,128)(2,1)S(1)} collective-permute-done((bf16[16,2048]{1,0:T(8,128)(2,1)}, bf16[16,2048]{1,0:T(8,128)(2,1)S(1)}, u32[]{:S(2)}, u32[]{:S(2)}) %collective-permute-start.1) | collective-permute-done | bytes 65568 | tf_op jit(solution)/shard_map/ppermute | solution.py:39
  19.1 0.8 copy-done.12
  19.9 1.6 %own_rows.1 = (bf16[64,2048]{1,0:T(8,128)(2,1)S(1)}, bf16[4,2176,128]{2,1,0:T(8,128)(2,1)}) custom-call(s32[59]{0:T(128)S(1)} %concatenate.6.at_ref, bf16[128,2048]{1,0:T(8,128)(2,1)S(1)} %copy-done.5, bf16[4,2176,128]{2,1,0:T(8,128)(2,1)} %get-tuple-element.30.send_in_ref, bf16[16,2048]{1,0:T(8,128)(2,1)S(1)} %copy-done.12, ...), custom_call_target="tpu_custom_call", output_to_operand_aliasing={{1}: (2, {})} | custom-call | flops 1024 | bytes 1024 | tf_op jit(solution)/shard_map/own_rows/pallas_call | solution.py:452
  21.6 4.6 %all-to-all-start = ((bf16[4,2176,128]{2,1,0:T(8,128)(2,1)}), bf16[4,2176,128]{2,1,0:T(8,128)(2,1)}, u32[]{:S(2)}, u32[]{:S(2)}) async-start(bf16[4,2176,128]{2,1,0:T(8,128)(2,1)} %get-tuple-element.35), calls=%async_computation | async-start | bytes 4456448 | tf_op jit(solution)/shard_map/all_to_all | solution.py:521
  26.2 2.2 %copy-done = bf16[1024,2048]{1,0:T(8,128)(2,1)S(1)} copy-done((bf16[1024,2048]{1,0:T(8,128)(2,1)S(1)}, bf16[1024,2048]{1,0:T(8,128)(2,1)}, u32[]{:S(2)}) %copy-start) | copy-done | bytes 4194328
  28.4 3.6 %base_product.3 = bf16[1,4,128,2048]{3,2,1,0:T(8,128)(2,1)S(1)} custom-call(s32[59]{0:T(128)S(1)} %concatenate.6.at_ref, bf16[4,2,128,1024]{3,2,1,0:T(8,128)(2,1)S(1)} %bitcast.67, bf16[1024,2048]{1,0:T(8,128)(2,1)S(1)} %copy-done), custom_call_target="tpu_custom_call" | custom-call | flops 1024 | bytes 1024 | tf_op jit(solution)/shard_map/base_product/pallas_call | solution.py:137
  32.0 0.1 collective-permute-start.11
  32.1 0.6 collective-permute-start.5
  32.7 1.0 slice.56
  33.6 0.6 collective-permute-start.6
  34.2 0.5 collective-permute-start.8
  34.7 3.6 %base_product.2 = bf16[1,4,128,2048]{3,2,1,0:T(8,128)(2,1)S(1)} custom-call(s32[59]{0:T(128)S(1)} %concatenate.6.at_ref, bf16[4,2,128,1024]{3,2,1,0:T(8,128)(2,1)S(1)} %bitcast.68, bf16[1024,2048]{1,0:T(8,128)(2,1)S(1)} %copy-done), custom_call_target="tpu_custom_call" | custom-call | flops 1024 | bytes 1024 | tf_op jit(solution)/shard_map/base_product/pallas_call | solution.py:137
  38.3 2.6 %collective-permute-done.5 = bf16[64,2048]{1,0:T(8,128)(2,1)S(1)} collective-permute-done((bf16[64,2048]{1,0:T(8,128)(2,1)S(1)}, bf16[64,2048]{1,0:T(8,128)(2,1)S(1)}, u32[]{:S(2)}, u32[]{:S(2)}) %collective-permute-start.5) | collective-permute-done | bytes 262176 | tf_op jit(solution)/shard_map/ppermute | solution.py:60
  40.9 0.7 constant_dynamic-update-slice_fusion.1
  41.6 0.5 collective-permute-done.6
  42.1 0.7 constant_dynamic-update-slice_fusion.rest_3_.rest_5_
  42.9 2.0 %convert_add_fusion = (f32[128,2048]{1,0:T(8,128)}, bf16[128,2048]{1,0:T(8,128)(2,1)}, bf16[128,2048]{1,0:T(8,128)(2,1)}, bf16[128,2048]{1,0:T(8,128)(2,1)}) fusion(bf16[4,128,2048]{2,1,0:T(8,128)(2,1)S(1)} %collective-permute-done.11, bf16[1,4,128,2048]{3,2,1,0:T(8,128)(2,1)S(1)} %base_product.2), kind=kLoop, calls=%fused_computation | loop fusion | flops 3932160 | bytes 6815744 | tf_op jit(solution)/shard_map/add | solution.py:532
  44.9 0.5 collective-permute-start.13
  45.4 0.8 copy-done.8
  46.2 1.5 %collective-permute-start.12 = (bf16[128,2048]{1,0:T(8,128)(2,1)}, bf16[128,2048]{1,0:T(8,128)(2,1)}, u32[]{:S(2)}, u32[]{:S(2)}) collective-permute-start(bf16[128,2048]{1,0:T(8,128)(2,1)} %get-tuple-element.59), channel_id=1, source_target_pairs={{0,2},{2,0},{4,6},{6,4},{1,3},{3,1},{5,7},{7,5},{8,10},{10,8},{12,... | collective-permute-start | bytes 1572872 | tf_op jit(solution)/shard_map/ppermute | solution.py:60
  47.7 2.6 %copy.12 = bf16[1024,1024]{1,0:T(8,128)(2,1)} copy(bf16[1024,1024]{0,1:T(8,128)(2,1)S(1)} %bitcast.69) | data formatting | bytes 4194304 | tf_op jit(solution)/shard_map/transpose | solution.py:543
  50.4 2.2 %copy-done.1 = bf16[1024,2048]{1,0:T(8,128)(2,1)S(1)} copy-done((bf16[1024,2048]{1,0:T(8,128)(2,1)S(1)}, bf16[1024,2048]{1,0:T(8,128)(2,1)}, u32[]{:S(2)}) %copy-start.1) | copy-done | bytes 4194328
  52.6 1.0 copy-done.9
  53.6 8.0 %cotangent_product.1.base_ref = f32[1024,1024]{1,0:T(8,128)S(1)} custom-call(s32[59]{0:T(128)S(1)} %concatenate.6.at_ref, bf16[1024,2048]{1,0:T(8,128)(2,1)S(1)} %copy-done.1, bf16[128,2048]{1,0:T(8,128)(2,1)S(1)} %copy-done.5, bf16[128,2048]{1,0:T(8,128)(2,1)} %collective-permute-done.3.rest_1_.rest_3_, ...), custom_call_target="tpu_custom_call" | custom-call | flops 1024 | bytes 1024 | tf_op jit(solution)/shard_map/cotangent_product/pallas_call | solution.py:210
  61.6 2.0 %copy-done.3 = f32[1024,1024]{1,0:T(8,128)} copy-done((f32[1024,1024]{1,0:T(8,128)}, f32[1024,1024]{1,0:T(8,128)S(1)}, u32[]{:S(2)}) %copy-start.3) | copy-done | bytes 4194328
  63.5 12.6 %all-to-all-done.a_ref = bf16[4,2176,128]{2,1,0:T(8,128)(2,1)} async-done(((bf16[4,2176,128]{2,1,0:T(8,128)(2,1)}), bf16[4,2176,128]{2,1,0:T(8,128)(2,1)}, u32[]{:S(2)}, u32[]{:S(2)}) %all-to-all-start) | async-done | bytes 2228256 | tf_op jit(solution)/shard_map/all_to_all | solution.py:521
  76.1 4.4 %all-to-all-start.1 = ((bf16[4,256,1024]{2,1,0:T(8,128)(2,1)}), bf16[4,256,1024]{2,1,0:T(8,128)(2,1)}, u32[]{:S(2)}, u32[]{:S(2)}) async-start(bf16[4,256,1024]{2,1,0:T(8,128)(2,1)} %bitcast.71), calls=%async_computation.1 | async-start | bytes 4194304 | tf_op jit(solution)/shard_map/all_to_all | solution.py:548
  80.6 0.4 collective-permute-start.14
  80.9 13.7 %collective-permute-done.14.rest_3_ = bf16[128,2048]{1,0:T(8,128)(2,1)S(1)} collective-permute-done((bf16[128,2048]{1,0:T(8,128)(2,1)}, bf16[128,2048]{1,0:T(8,128)(2,1)S(1)}, u32[]{:S(2)}, u32[]{:S(2)}) %collective-permute-start.14) | collective-permute-done | bytes 524320 | tf_op jit(solution)/shard_map/ppermute | solution.py:60
  94.6 2.4 %low_product.1 = bf16[2,4,128,128]{3,2,1,0:T(8,128)(2,1)S(1)} custom-call(s32[59]{0:T(128)S(1)} %concatenate.6.at_ref, bf16[1024,1024]{1,0:T(8,128)(2,1)S(1)} %copy-done.2, bf16[4,2176,128]{2,1,0:T(8,128)(2,1)} %all-to-all-done.a_ref), custom_call_target="tpu_custom_call" | custom-call | flops 1024 | bytes 1024 | tf_op jit(solution)/shard_map/low_product/pallas_call | solution.py:171
  97.0 0.1 collective-permute-start.15
  97.1 1.0 slice_bitcast_fusion.14
  98.1 0.6 collective-permute-start.20
  98.7 0.3 collective-permute-start.19
  99.0 2.6 %collective-permute-start.21 = (bf16[4,128,128]{2,1,0:T(8,128)(2,1)S(1)}, bf16[4,128,128]{2,1,0:T(8,128)(2,1)S(1)}, u32[]{:S(2)}, u32[]{:S(2)}) collective-permute-start(bf16[4,128,128]{2,1,0:T(8,128)(2,1)S(1)} %get-tuple-element.61), channel_id=1, source_target_pairs={{0,6},{2,4},{4,2},{6,0},{1,7},{3,5},{5,3},{7,1},{8,14},{10,12},{12... | collective-permute-start | bytes 393224 | tf_op jit(solution)/shard_map/ppermute | solution.py:60
  101.7 0.4 collective-permute-start.18
  102.0 1.7 %collective-permute-start.17 = (bf16[4,128,128]{2,1,0:T(8,128)(2,1)S(1)}, bf16[4,128,128]{2,1,0:T(8,128)(2,1)S(1)}, u32[]{:S(2)}, u32[]{:S(2)}) collective-permute-start(bf16[4,128,128]{2,1,0:T(8,128)(2,1)S(1)} %fusion.3), channel_id=1, source_target_pairs={{0,4},{2,6},{4,0},{6,2},{1,5},{3,7},{5,1},{7,3},{8,12},{10,14},{12... | collective-permute-start | bytes 393224 | tf_op jit(solution)/shard_map/ppermute | solution.py:60
  103.8 0.2 collective-permute-done.20
  104.0 1.2 collective-permute-start.16
  105.3 3.6 %collective-permute-done.21 = bf16[4,128,128]{2,1,0:T(8,128)(2,1)S(1)} collective-permute-done((bf16[4,128,128]{2,1,0:T(8,128)(2,1)S(1)}, bf16[4,128,128]{2,1,0:T(8,128)(2,1)S(1)}, u32[]{:S(2)}, u32[]{:S(2)}) %collective-permute-start.21) | collective-permute-done | bytes 131104 | tf_op jit(solution)/shard_map/ppermute | solution.py:60
  108.9 0.1 pad_maximum_fusion.rest_0_
  108.9 0.1 collective-permute-start.22
  109.0 2.6 %collective-permute-done.18 = bf16[4,128,128]{2,1,0:T(8,128)(2,1)S(1)} collective-permute-done((bf16[4,128,128]{2,1,0:T(8,128)(2,1)S(1)}, bf16[4,128,128]{2,1,0:T(8,128)(2,1)S(1)}, u32[]{:S(2)}, u32[]{:S(2)}) %collective-permute-start.18) | collective-permute-done | bytes 131104 | tf_op jit(solution)/shard_map/ppermute | solution.py:60
  111.6 0.8 collective-permute-done.17
  112.5 0.3 collective-permute-done.16
  112.7 0.1 add_convert_fusion.low_ref.rest_0_
  112.8 0.1 collective-permute-start.23
  112.9 1.3 collective-permute-done.23.rest_1_
  114.2 2.2 %grad_up_pieces.1 = bf16[4,8,16,256]{3,2,1,0:T(8,128)(2,1)S(1)} custom-call(s32[59]{0:T(128)S(1)} %concatenate.6.at_ref, bf16[4,128,128]{2,1,0:T(8,128)(2,1)S(1)} %add_convert_fusion.low_ref.rest_0_, bf16[4,128,128]{2,1,0:T(8,128)(2,1)S(1)} %collective-permute-done.23.rest_1_, bf16[128,2048]{1,0:T(8,128)(2,1)S(1)} %copy-done.5, ...), custom_call_target="tpu_custom_call" | custom-call | flops 1024 | bytes 1024 | tf_op jit(solution)/shard_map/grad_up_pieces/pallas_call | solution.py:382
  116.5 3.5 %collective-permute-start.26 = (bf16[8,16,256]{2,1,0:T(8,128)(2,1)S(1)}, bf16[8,16,256]{2,1,0:T(8,128)(2,1)S(1)}, u32[]{:S(2)}, u32[]{:S(2)}) collective-permute-start(bf16[8,16,256]{2,1,0:T(8,128)(2,1)S(1)} %get-tuple-element.62), channel_id=1, source_target_pairs={{0,24},{8,0},{16,8},{24,16},{1,25},{9,1},{17,9},{25,17},{2,26},{10... | collective-permute-start | bytes 196616 | tf_op jit(solution)/shard_map/ppermute | solution.py:39
  120.0 1.1 collective-permute-start.24
  121.1 2.5 %keys_and_values.1 = bf16[128,2048]{1,0:T(8,128)(2,1)} custom-call(s32[59]{0:T(128)S(1)} %concatenate.6.at_ref, bf16[4,128,128]{2,1,0:T(8,128)(2,1)S(1)} %add_convert_fusion.low_ref.rest_0_, bf16[64,2048]{1,0:T(8,128)(2,1)S(1)} %get-tuple-element.45.b_ref, f32[128,2048]{1,0:T(8,128)S(1)} %copy-done.7, bf16[128,2048]{1,0:T(8,128)(2,1)} %collective-permute-done.12.rest_1_, ...), custom_call_target="tpu_custom_call" | custom-call | flops 1024 | bytes 1024 | tf_op jit(solution)/shard_map/keys_and_values/pallas_call | solution.py:483
  123.6 4.7 %input_gradient.1 = bf16[1024,1024]{1,0:T(8,128)(2,1)} custom-call(s32[59]{0:T(128)S(1)} %concatenate.6.at_ref, f32[1024,1024]{1,0:T(8,128)S(1)} %copy-done.4, bf16[4,2176,128]{2,1,0:T(8,128)(2,1)} %all-to-all-done.a_ref, bf16[4,4,128,128]{3,2,1,0:T(8,128)(2,1)S(1)} %pad_maximum_fusion.rest_0_, bf16[4,4,128,128]{3,2,1,0:T(8,128)(2,1)S(1)} %collective-permute-done.22.rest_1_), custom_call_target="tpu_custom_call" | custom-call | flops 1024 | bytes 1024 | tf_op jit(solution)/shard_map/input_gradient/pallas_call | solution.py:252
  128.2 4.0 %all-to-all-done.1.x_ref = bf16[4,256,1024]{2,1,0:T(8,128)(2,1)} async-done(((bf16[4,256,1024]{2,1,0:T(8,128)(2,1)}), bf16[4,256,1024]{2,1,0:T(8,128)(2,1)}, u32[]{:S(2)}, u32[]{:S(2)}) %all-to-all-start.1) | async-done | bytes 2097184 | tf_op jit(solution)/shard_map/all_to_all | solution.py:548
  132.2 5.0 %grad_down.1 = f32[24,256,128]{2,1,0:T(8,128)} custom-call(s32[59]{0:T(128)} %copy-done.13, bf16[4,256,1024]{2,1,0:T(8,128)(2,1)} %all-to-all-done.1.x_ref, bf16[4,4,128,128]{3,2,1,0:T(8,128)(2,1)} %copy-done.6, bf16[4,4,128,128]{3,2,1,0:T(8,128)(2,1)} %copy-done.11), custom_call_target="tpu_custom_call" | custom-call | flops 1024 | bytes 1024 | tf_op jit(solution)/shard_map/grad_down/pallas_call | solution.py:317
  137.3 1.5 %grad_up.1 = f32[24,16,256]{2,1,0:T(8,128)} custom-call(s32[59]{0:T(128)S(1)} %copy-done.14, bf16[8,16,256]{2,1,0:T(8,128)(2,1)S(1)} %get-tuple-element.52.rest_0_, bf16[8,16,256]{2,1,0:T(8,128)(2,1)S(1)} %collective-permute-done.24.rest_1_, bf16[8,16,256]{2,1,0:T(8,128)(2,1)S(1)} %collective-permute-done.25.rest_2_, ...), custom_call_target="tpu_custom_call" | custom-call | flops 1024 | bytes 1024 | tf_op jit(solution)/shard_map/grad_up/pallas_call | solution.py:409
  (52 shorter events, 0.2 us)
Async XLA Ops:
  0.6 18.5 %copy-start.5 = (bf16[128,2048]{1,0:T(8,128)(2,1)S(1)}, bf16[128,2048]{1,0:T(8,128)(2,1)}, u32[]{:S(2)}) copy-start(bf16[128,2048]{1,0:T(8,128)(2,1)} %rest_2_.1) | copy-start | bytes 1572868
  0.6 15.0 %copy-start.16 = (s32[24]{0:T(128)S(1)}, s32[24]{0:T(128)}, u32[]{:S(2)}) copy-start(s32[24]{0:T(128)} %slot_ref.1) | copy-start | bytes 292
  0.7 15.0 %copy-start.15 = (s32[32]{0:T(128)S(1)}, s32[32]{0:T(128)}, u32[]{:S(2)}) copy-start(s32[32]{0:T(128)} %tenant_ref.1) | copy-start | bytes 388
  0.7 25.5 %collective-permute-start.4 = (bf16[128,2048]{1,0:T(8,128)(2,1)}, bf16[128,2048]{1,0:T(8,128)(2,1)S(1)}, u32[]{:S(2)}, u32[]{:S(2)}) collective-permute-start(bf16[128,2048]{1,0:T(8,128)(2,1)} %rest_2_.1), channel_id=1, source_target_pairs={{0,4},{2,6},{4,0},{6,2},{1,5},{3,7},{5,1},{7,3},{8,12},{10,14},{12... | collective-permute-start | bytes 1572872 | tf_op jit(solution)/shard_map/ppermute | solution.py:60
  3.7 22.5 %collective-permute-start.3 = (bf16[128,2048]{1,0:T(8,128)(2,1)}, bf16[128,2048]{1,0:T(8,128)(2,1)}, u32[]{:S(2)}, u32[]{:S(2)}) collective-permute-start(bf16[128,2048]{1,0:T(8,128)(2,1)} %rest_2_.1), channel_id=1, source_target_pairs={{0,2},{2,0},{4,6},{6,4},{1,3},{3,1},{5,7},{7,5},{8,10},{10,8},{12,... | collective-permute-start | bytes 1572872 | tf_op jit(solution)/shard_map/ppermute | solution.py:60
  10.0 7.1 %collective-permute-start = (bf16[16,2048]{1,0:T(8,128)(2,1)}, bf16[16,2048]{1,0:T(8,128)(2,1)S(1)}, u32[]{:S(2)}, u32[]{:S(2)}) collective-permute-start(bf16[16,2048]{1,0:T(8,128)(2,1)} %get-tuple-element.32), channel_id=1, source_target_pairs={{0,8},{8,16},{16,24},{24,0},{1,9},{9,17},{17,25},{25,1},{2,10},{10... | collective-permute-start | bytes 196616 | tf_op jit(solution)/shard_map/ppermute | solution.py:39
  11.6 7.4 %collective-permute-start.1 = (bf16[16,2048]{1,0:T(8,128)(2,1)}, bf16[16,2048]{1,0:T(8,128)(2,1)S(1)}, u32[]{:S(2)}, u32[]{:S(2)}) collective-permute-start(bf16[16,2048]{1,0:T(8,128)(2,1)} %get-tuple-element.33), channel_id=1, source_target_pairs={{0,16},{8,24},{16,0},{24,8},{1,17},{9,25},{17,1},{25,9},{2,18},{10... | collective-permute-start | bytes 196616 | tf_op jit(solution)/shard_map/ppermute | solution.py:39
  14.2 4.9 %collective-permute-start.2 = (bf16[16,2048]{1,0:T(8,128)(2,1)}, bf16[16,2048]{1,0:T(8,128)(2,1)S(1)}, u32[]{:S(2)}, u32[]{:S(2)}) collective-permute-start(bf16[16,2048]{1,0:T(8,128)(2,1)} %get-tuple-element.34), channel_id=1, source_target_pairs={{0,24},{8,0},{16,8},{24,16},{1,25},{9,1},{17,9},{25,17},{2,26},{10... | collective-permute-start | bytes 196616 | tf_op jit(solution)/shard_map/ppermute | solution.py:39
  15.7 107.9 %copy-start.13 = (s32[59]{0:T(128)}, s32[59]{0:T(128)S(1)}, u32[]{:S(2)}) copy-start(s32[59]{0:T(128)S(1)} %concatenate.6.at_ref) | copy-start | bytes 712
  19.1 0.8 copy-start.12
  21.5 4.7 %copy-start.2 = (bf16[1024,1024]{1,0:T(8,128)(2,1)S(1)}, bf16[1024,1024]{1,0:T(8,128)(2,1)}, u32[]{:S(2)}) copy-start(bf16[1024,1024]{1,0:T(8,128)(2,1)} %x_ref.1) | copy-start | bytes 6291460
  21.6 54.6 %all-to-all-start = ((bf16[4,2176,128]{2,1,0:T(8,128)(2,1)}), bf16[4,2176,128]{2,1,0:T(8,128)(2,1)}, u32[]{:S(2)}, u32[]{:S(2)}) async-start(bf16[4,2176,128]{2,1,0:T(8,128)(2,1)} %get-tuple-element.35), calls=%async_computation | async-start | bytes 4456448 | tf_op jit(solution)/shard_map/all_to_all | solution.py:521
  26.2 2.2 %copy-start = (bf16[1024,2048]{1,0:T(8,128)(2,1)S(1)}, bf16[1024,2048]{1,0:T(8,128)(2,1)}, u32[]{:S(2)}) copy-start(bf16[1024,2048]{1,0:T(8,128)(2,1)} %w_ref.5) | copy-start | bytes 12582916
  32.0 10.9 %collective-permute-start.11 = (bf16[4,128,2048]{2,1,0:T(8,128)(2,1)S(1)}, bf16[4,128,2048]{2,1,0:T(8,128)(2,1)S(1)}, u32[]{:S(2)}, u32[]{:S(2)}) collective-permute-start(bf16[4,128,2048]{2,1,0:T(8,128)(2,1)S(1)} %bitcast.70), channel_id=1, source_target_pairs={{0,1},{1,0},{2,3},{3,2},{4,5},{5,4},{6,7},{7,6},{8,9},{9,8},{10,11... | collective-permute-start | bytes 6291464 | tf_op jit(solution)/shard_map/ppermute | solution.py:60
  32.1 8.8 %collective-permute-start.5 = (bf16[64,2048]{1,0:T(8,128)(2,1)S(1)}, bf16[64,2048]{1,0:T(8,128)(2,1)S(1)}, u32[]{:S(2)}, u32[]{:S(2)}) collective-permute-start(bf16[64,2048]{1,0:T(8,128)(2,1)S(1)} %slice.55), channel_id=1, source_target_pairs={{0,2},{2,0},{4,6},{6,4},{1,3},{3,1},{5,7},{7,5},{8,10},{10,8},{12,... | collective-permute-start | bytes 786440 | tf_op jit(solution)/shard_map/ppermute | solution.py:60
  33.6 8.5 %collective-permute-start.6 = (bf16[64,2048]{1,0:T(8,128)(2,1)S(1)}, bf16[64,2048]{1,0:T(8,128)(2,1)S(1)}, u32[]{:S(2)}, u32[]{:S(2)}) collective-permute-start(bf16[64,2048]{1,0:T(8,128)(2,1)S(1)} %slice.56), channel_id=1, source_target_pairs={{0,4},{2,6},{4,0},{6,2},{1,5},{3,7},{5,1},{7,3},{8,12},{10,14},{12... | collective-permute-start | bytes 786440 | tf_op jit(solution)/shard_map/ppermute | solution.py:60
  34.2 11.2 %collective-permute-start.7 = (bf16[128,2048]{1,0:T(8,128)(2,1)S(1)}, bf16[128,2048]{1,0:T(8,128)(2,1)S(1)}, u32[]{:S(2)}, u32[]{:S(2)}) collective-permute-start(bf16[128,2048]{1,0:T(8,128)(2,1)S(1)} %copy-done.5), channel_id=1, source_target_pairs={{0,1},{1,0},{2,3},{3,2},{4,5},{5,4},{6,7},{7,6},{8,9},{9,8},{10,11... | collective-permute-start | bytes 1572872 | tf_op jit(solution)/shard_map/ppermute | solution.py:60
  34.2 16.1 %collective-permute-start.8 = (bf16[128,2048]{1,0:T(8,128)(2,1)}, bf16[128,2048]{1,0:T(8,128)(2,1)}, u32[]{:S(2)}, u32[]{:S(2)}) collective-permute-start(bf16[128,2048]{1,0:T(8,128)(2,1)} %collective-permute-done.3.rest_1_.rest_3_), channel_id=1, source_target_pairs={{0,1},{1,0},{2,3},{3,2},{4,5},{5,4},{6,7},{7,6},{8,9},{9,8},{10,11... | collective-permute-start | bytes 1572872 | tf_op jit(solution)/shard_map/ppermute | solution.py:60
  40.9 9.5 %collective-permute-start.9 = (bf16[128,2048]{1,0:T(8,128)(2,1)S(1)}, bf16[128,2048]{1,0:T(8,128)(2,1)}, u32[]{:S(2)}, u32[]{:S(2)}) collective-permute-start(bf16[128,2048]{1,0:T(8,128)(2,1)S(1)} %collective-permute-done.4.rest_2_.rest_4_), channel_id=1, source_target_pairs={{0,1},{1,0},{2,3},{3,2},{4,5},{5,4},{6,7},{7,6},{8,9},{9,8},{10,11... | collective-permute-start | bytes 1572872 | tf_op jit(solution)/shard_map/ppermute | solution.py:60
  42.9 7.5 %collective-permute-start.10 = (bf16[128,2048]{1,0:T(8,128)(2,1)}, bf16[128,2048]{1,0:T(8,128)(2,1)}, u32[]{:S(2)}, u32[]{:S(2)}) collective-permute-start(bf16[128,2048]{1,0:T(8,128)(2,1)} %constant_dynamic-update-slice_fusion.rest_3_.rest_5_), channel_id=1, source_target_pairs={{0,1},{1,0},{2,3},{3,2},{4,5},{5,4},{6,7},{7,6},{8,9},{9,8},{10,11... | collective-permute-start | bytes 1572872 | tf_op jit(solution)/shard_map/ppermute | solution.py:60
  44.9 18.6 %collective-permute-start.13 = (bf16[128,2048]{1,0:T(8,128)(2,1)}, bf16[128,2048]{1,0:T(8,128)(2,1)}, u32[]{:S(2)}, u32[]{:S(2)}) collective-permute-start(bf16[128,2048]{1,0:T(8,128)(2,1)} %get-tuple-element.58), channel_id=1, source_target_pairs={{0,4},{2,6},{4,0},{6,2},{1,5},{3,7},{5,1},{7,3},{8,12},{10,14},{12... | collective-permute-start | bytes 1572872 | tf_op jit(solution)/shard_map/ppermute | solution.py:60
  45.4 0.8 copy-start.8
  46.2 17.3 %collective-permute-start.12 = (bf16[128,2048]{1,0:T(8,128)(2,1)}, bf16[128,2048]{1,0:T(8,128)(2,1)}, u32[]{:S(2)}, u32[]{:S(2)}) collective-permute-start(bf16[128,2048]{1,0:T(8,128)(2,1)} %get-tuple-element.59), channel_id=1, source_target_pairs={{0,2},{2,0},{4,6},{6,4},{1,3},{3,1},{5,7},{7,5},{8,10},{10,8},{12,... | collective-permute-start | bytes 1572872 | tf_op jit(solution)/shard_map/ppermute | solution.py:60
  50.4 2.2 %copy-start.1 = (bf16[1024,2048]{1,0:T(8,128)(2,1)S(1)}, bf16[1024,2048]{1,0:T(8,128)(2,1)}, u32[]{:S(2)}) copy-start(bf16[1024,2048]{1,0:T(8,128)(2,1)} %w_ref.5) | copy-start | bytes 12582916
  52.5 1.0 copy-start.9
  61.6 2.0 %copy-start.3 = (f32[1024,1024]{1,0:T(8,128)}, f32[1024,1024]{1,0:T(8,128)S(1)}, u32[]{:S(2)}) copy-start(f32[1024,1024]{1,0:T(8,128)S(1)} %cotangent_product.1.base_ref) | copy-start | bytes 12582916
  76.1 56.1 %all-to-all-start.1 = ((bf16[4,256,1024]{2,1,0:T(8,128)(2,1)}), bf16[4,256,1024]{2,1,0:T(8,128)(2,1)}, u32[]{:S(2)}, u32[]{:S(2)}) async-start(bf16[4,256,1024]{2,1,0:T(8,128)(2,1)} %bitcast.71), calls=%async_computation.1 | async-start | bytes 4194304 | tf_op jit(solution)/shard_map/all_to_all | solution.py:548
  80.6 14.0 %collective-permute-start.14 = (bf16[128,2048]{1,0:T(8,128)(2,1)}, bf16[128,2048]{1,0:T(8,128)(2,1)S(1)}, u32[]{:S(2)}, u32[]{:S(2)}) collective-permute-start(bf16[128,2048]{1,0:T(8,128)(2,1)} %get-tuple-element.57), channel_id=1, source_target_pairs={{0,6},{2,4},{4,2},{6,0},{1,7},{3,5},{5,3},{7,1},{8,14},{10,12},{12... | collective-permute-start | bytes 1572872 | tf_op jit(solution)/shard_map/ppermute | solution.py:60
  97.0 17.2 %copy-start.10 = (bf16[128,2048]{1,0:T(8,128)(2,1)S(1)}, bf16[128,2048]{1,0:T(8,128)(2,1)}, u32[]{:S(2)}) copy-start(bf16[128,2048]{1,0:T(8,128)(2,1)} %copy-done.8) | copy-start | bytes 1572868
  97.0 4.6 %collective-permute-start.15 = (bf16[4,128,128]{2,1,0:T(8,128)(2,1)S(1)}, bf16[4,128,128]{2,1,0:T(8,128)(2,1)S(1)}, u32[]{:S(2)}, u32[]{:S(2)}) collective-permute-start(bf16[4,128,128]{2,1,0:T(8,128)(2,1)S(1)} %slice_bitcast_fusion.8), channel_id=1, source_target_pairs={{0,1},{1,0},{2,3},{3,2},{4,5},{5,4},{6,7},{7,6},{8,9},{9,8},{10,11... | collective-permute-start | bytes 393224 | tf_op jit(solution)/shard_map/ppermute | solution.py:60
  98.1 5.9 %collective-permute-start.20 = (bf16[4,128,128]{2,1,0:T(8,128)(2,1)S(1)}, bf16[4,128,128]{2,1,0:T(8,128)(2,1)S(1)}, u32[]{:S(2)}, u32[]{:S(2)}) collective-permute-start(bf16[4,128,128]{2,1,0:T(8,128)(2,1)S(1)} %get-tuple-element.61), channel_id=1, source_target_pairs={{0,4},{2,6},{4,0},{6,2},{1,5},{3,7},{5,1},{7,3},{8,12},{10,14},{12... | collective-permute-start | bytes 393224 | tf_op jit(solution)/shard_map/ppermute | solution.py:60
  98.7 6.6 %collective-permute-start.19 = (bf16[4,128,128]{2,1,0:T(8,128)(2,1)S(1)}, bf16[4,128,128]{2,1,0:T(8,128)(2,1)S(1)}, u32[]{:S(2)}, u32[]{:S(2)}) collective-permute-start(bf16[4,128,128]{2,1,0:T(8,128)(2,1)S(1)} %get-tuple-element.61), channel_id=1, source_target_pairs={{0,2},{2,0},{4,6},{6,4},{1,3},{3,1},{5,7},{7,5},{8,10},{10,8},{12,... | collective-permute-start | bytes 393224 | tf_op jit(solution)/shard_map/ppermute | solution.py:60
  99.0 9.9 %collective-permute-start.21 = (bf16[4,128,128]{2,1,0:T(8,128)(2,1)S(1)}, bf16[4,128,128]{2,1,0:T(8,128)(2,1)S(1)}, u32[]{:S(2)}, u32[]{:S(2)}) collective-permute-start(bf16[4,128,128]{2,1,0:T(8,128)(2,1)S(1)} %get-tuple-element.61), channel_id=1, source_target_pairs={{0,6},{2,4},{4,2},{6,0},{1,7},{3,5},{5,3},{7,1},{8,14},{10,12},{12... | collective-permute-start | bytes 393224 | tf_op jit(solution)/shard_map/ppermute | solution.py:60
  101.7 9.9 %collective-permute-start.18 = (bf16[4,128,128]{2,1,0:T(8,128)(2,1)S(1)}, bf16[4,128,128]{2,1,0:T(8,128)(2,1)S(1)}, u32[]{:S(2)}, u32[]{:S(2)}) collective-permute-start(bf16[4,128,128]{2,1,0:T(8,128)(2,1)S(1)} %fusion.3), channel_id=1, source_target_pairs={{0,6},{2,4},{4,2},{6,0},{1,7},{3,5},{5,3},{7,1},{8,14},{10,12},{12... | collective-permute-start | bytes 393224 | tf_op jit(solution)/shard_map/ppermute | solution.py:60
  102.0 10.4 %collective-permute-start.17 = (bf16[4,128,128]{2,1,0:T(8,128)(2,1)S(1)}, bf16[4,128,128]{2,1,0:T(8,128)(2,1)S(1)}, u32[]{:S(2)}, u32[]{:S(2)}) collective-permute-start(bf16[4,128,128]{2,1,0:T(8,128)(2,1)S(1)} %fusion.3), channel_id=1, source_target_pairs={{0,4},{2,6},{4,0},{6,2},{1,5},{3,7},{5,1},{7,3},{8,12},{10,14},{12... | collective-permute-start | bytes 393224 | tf_op jit(solution)/shard_map/ppermute | solution.py:60
  104.0 8.7 %collective-permute-start.16 = (bf16[4,128,128]{2,1,0:T(8,128)(2,1)S(1)}, bf16[4,128,128]{2,1,0:T(8,128)(2,1)S(1)}, u32[]{:S(2)}, u32[]{:S(2)}) collective-permute-start(bf16[4,128,128]{2,1,0:T(8,128)(2,1)S(1)} %fusion.3), channel_id=1, source_target_pairs={{0,2},{2,0},{4,6},{6,4},{1,3},{3,1},{5,7},{7,5},{8,10},{10,8},{12,... | collective-permute-start | bytes 393224 | tf_op jit(solution)/shard_map/ppermute | solution.py:60
  108.9 14.6 %copy-start.6 = (bf16[4,4,128,128]{3,2,1,0:T(8,128)(2,1)}, bf16[4,4,128,128]{3,2,1,0:T(8,128)(2,1)S(1)}, u32[]{:S(2)}) copy-start(bf16[4,4,128,128]{3,2,1,0:T(8,128)(2,1)S(1)} %pad_maximum_fusion.rest_0_) | copy-start | bytes 1572868
  108.9 14.6 %collective-permute-start.22 = (bf16[4,4,128,128]{3,2,1,0:T(8,128)(2,1)S(1)}, bf16[4,4,128,128]{3,2,1,0:T(8,128)(2,1)S(1)}, u32[]{:S(2)}, u32[]{:S(2)}) collective-permute-start(bf16[4,4,128,128]{3,2,1,0:T(8,128)(2,1)S(1)} %pad_maximum_fusion.rest_0_), channel_id=1, source_target_pairs={{0,1},{1,0},{2,3},{3,2},{4,5},{5,4},{6,7},{7,6},{8,9},{9,8},{10,11... | collective-permute-start | bytes 1572872 | tf_op jit(solution)/shard_map/ppermute | solution.py:60
  112.8 8.3 %copy-start.7 = (f32[128,2048]{1,0:T(8,128)S(1)}, f32[128,2048]{1,0:T(8,128)}, u32[]{:S(2)}) copy-start(f32[128,2048]{1,0:T(8,128)} %get-tuple-element.56.rest_0_) | copy-start | bytes 3145732
  112.8 1.4 %collective-permute-start.23 = (bf16[4,128,128]{2,1,0:T(8,128)(2,1)S(1)}, bf16[4,128,128]{2,1,0:T(8,128)(2,1)S(1)}, u32[]{:S(2)}, u32[]{:S(2)}) collective-permute-start(bf16[4,128,128]{2,1,0:T(8,128)(2,1)S(1)} %add_convert_fusion.low_ref.rest_0_), channel_id=1, source_target_pairs={{0,1},{1,0},{2,3},{3,2},{4,5},{5,4},{6,7},{7,6},{8,9},{9,8},{10,11... | collective-permute-start | bytes 393224 | tf_op jit(solution)/shard_map/ppermute | solution.py:60
  114.2 9.3 %copy-start.4 = (f32[1024,1024]{1,0:T(8,128)S(1)}, f32[1024,1024]{1,0:T(8,128)}, u32[]{:S(2)}) copy-start(f32[1024,1024]{1,0:T(8,128)} %copy-done.3) | copy-start | bytes 12582916
  116.5 20.8 %collective-permute-start.26 = (bf16[8,16,256]{2,1,0:T(8,128)(2,1)S(1)}, bf16[8,16,256]{2,1,0:T(8,128)(2,1)S(1)}, u32[]{:S(2)}, u32[]{:S(2)}) collective-permute-start(bf16[8,16,256]{2,1,0:T(8,128)(2,1)S(1)} %get-tuple-element.62), channel_id=1, source_target_pairs={{0,24},{8,0},{16,8},{24,16},{1,25},{9,1},{17,9},{25,17},{2,26},{10... | collective-permute-start | bytes 196616 | tf_op jit(solution)/shard_map/ppermute | solution.py:39
  120.0 17.3 %collective-permute-start.25 = (bf16[8,16,256]{2,1,0:T(8,128)(2,1)S(1)}, bf16[8,16,256]{2,1,0:T(8,128)(2,1)S(1)}, u32[]{:S(2)}, u32[]{:S(2)}) collective-permute-start(bf16[8,16,256]{2,1,0:T(8,128)(2,1)S(1)} %get-tuple-element.63), channel_id=1, source_target_pairs={{0,16},{8,24},{16,0},{24,8},{1,17},{9,25},{17,1},{25,9},{2,18},{10... | collective-permute-start | bytes 196616 | tf_op jit(solution)/shard_map/ppermute | solution.py:39
  120.0 17.3 %collective-permute-start.24 = (bf16[8,16,256]{2,1,0:T(8,128)(2,1)S(1)}, bf16[8,16,256]{2,1,0:T(8,128)(2,1)S(1)}, u32[]{:S(2)}, u32[]{:S(2)}) collective-permute-start(bf16[8,16,256]{2,1,0:T(8,128)(2,1)S(1)} %get-tuple-element.64), channel_id=1, source_target_pairs={{0,8},{8,16},{16,24},{24,0},{1,9},{9,17},{17,25},{25,1},{2,10},{10... | collective-permute-start | bytes 196616 | tf_op jit(solution)/shard_map/ppermute | solution.py:39
  123.6 4.7 %copy-start.11 = (bf16[4,4,128,128]{3,2,1,0:T(8,128)(2,1)}, bf16[4,4,128,128]{3,2,1,0:T(8,128)(2,1)S(1)}, u32[]{:S(2)}) copy-start(bf16[4,4,128,128]{3,2,1,0:T(8,128)(2,1)S(1)} %collective-permute-done.22.rest_1_) | copy-start | bytes 1572868
  128.2 9.1 %copy-start.14 = (s32[59]{0:T(128)S(1)}, s32[59]{0:T(128)}, u32[]{:S(2)}) copy-start(s32[59]{0:T(128)} %copy-done.13) | copy-start | bytes 712

commit v13 on v12

--- a/solution.py
+++ b/solution.py
@@ -72,7 +72,7 @@
     return came, one, two
 
 
-def pick(tenant_of_block, slot_of_tenant, adapter_down, adapter_up, group_rows, spare):
+def pick(tenant_of_block, slot_of_tenant, adapter_down, adapter_up, group_rows):
     data_count = lax.axis_size("dp")
     blocks_dev = tenant_of_block.shape[0] // data_count
     down_rows, ranks = adapter_down.shape[1:]
@@ -96,8 +96,7 @@
                     pltpu.make_async_copy(down_ref.at[slot], here, down_sem.at[data, block])
                 )
                 downs[data][-1].start()
-            there = out_ref.at[data, pl.ds(0, used)]
-            outs.append(pltpu.make_async_copy(rows.at[data], there, out_sem.at[data]))
+            outs.append(pltpu.make_async_copy(rows.at[data], out_ref.at[data], out_sem.at[data]))
         for data in range(data_count):
             for copy in downs[data]:
                 copy.wait()
@@ -111,7 +110,7 @@
         "pick_rows",
         VMEM_MOST,
         out_shape=(up_shape,) * data_count
-        + (pltpu.HBM((data_count, used + spare, ranks), adapter_down.dtype),),
+        + (pltpu.HBM((data_count, used, ranks), adapter_down.dtype),),
         in_specs=[SMEM, SMEM, HBM, HBM],
         out_specs=(VMEM,) * data_count + (HBM,),
         scratch_shapes=[
@@ -224,7 +223,7 @@
 def input_gradient(at, base, grad_pieces, down):
     data_count, all_rows, _ = down.shape
     tensor_count = len(grad_pieces)
-    pipe_count, _, rows, _ = grad_pieces[0].shape
+    pipe_count, rows, _ = grad_pieces[0].shape
     tok_dev, depth = base.shape
     down_rows = depth // data_count
     planes = next((n for n in range(1, data_count) if n * down_rows % 256 == 0), data_count)
@@ -240,7 +239,7 @@
                 for k in range(pipe_count):
                     chip = came_from(at_ref[1], k, pipe_count)
                     first = pl.multiple_of((chip * tensor_count + core) * rows, rows)
-                    grad[pl.ds(first, rows)] = grad_refs[s][k, at_ref[0]]
+                    grad[pl.ds(first, rows)] = grad_refs[s][k]
 
         for block in range(tok_dev // BLOCK):
             here = slice(block * BLOCK, (block + 1) * BLOCK)
@@ -248,7 +247,6 @@
             low = lax.dot_general(grad[here], a, LAST_BOTH, preferred_element_type=jnp.float32)
             out_ref[here] = (base_ref[here] + low).astype(out_ref.dtype)
 
-    grad_shape = (pipe_count, data_count, rows, RANKS)
     return call(
         kernel,
         "input_gradient",
@@ -258,56 +256,77 @@
             pl.BlockSpec((tok_dev, tile), lambda n: (0, n)),
             pl.BlockSpec((planes, all_rows, RANKS), lambda n: (n, 0, 0)),
         ]
-        + [pl.BlockSpec(grad_shape, lambda n: (0, 0, 0, 0))] * tensor_count,
+        + [VMEM] * tensor_count,
         out_specs=pl.BlockSpec((tok_dev, tile), lambda n: (0, n)),
         out_shape=jax.ShapeDtypeStruct((tok_dev, depth), jnp.bfloat16),
         scratch_shapes=[pltpu.VMEM((tok_dev, RANKS), jnp.bfloat16)],
     )(at, base, down, *grad_pieces)
 
 
-def grad_down(at, slot_of, slots, x_features, grad_pieces):
+def grad_down_pieces(at, x_features, grad_pieces):
     data_count, down_rows, tok_dev = x_features.shape
     tensor_count = len(grad_pieces)
-    pipe_count, _, rows, _ = grad_pieces[0].shape
+    pipe_count, rows, _ = grad_pieces[0].shape
     blocks_dev = tok_dev // BLOCK
 
+    def kernel(at_ref, x_ref, *rest):
+        grad_refs, (out_ref, grad) = rest[:tensor_count], rest[tensor_count:]
+
+        @pl.when(pl.program_id(0) == 0)
+        def _():
+            for s in range(tensor_count):
+                core = came_from(at_ref[2], s, tensor_count)
+                for k in range(pipe_count):
+                    chip = came_from(at_ref[1], k, pipe_count)
+                    first = pl.multiple_of((chip * tensor_count + core) * rows, rows)
+                    grad[pl.ds(first, rows)] = grad_refs[s][k]
+
+        for block in range(blocks_dev):
+            here = slice(block * BLOCK, (block + 1) * BLOCK)
+            out_ref[0, block] = jnp.dot(
+                x_ref[0, :, here], grad[here], preferred_element_type=jnp.float32
+            ).astype(out_ref.dtype)
+
+    return call(
+        kernel,
+        "grad_down_pieces",
+        grid=(data_count,),
+        in_specs=[SMEM, pl.BlockSpec((1, down_rows, tok_dev), lambda d: (d, 0, 0))]
+        + [VMEM] * tensor_count,
+        out_specs=pl.BlockSpec((1, blocks_dev, down_rows, RANKS), lambda d: (d, 0, 0, 0)),
+        out_shape=pltpu.HBM((data_count, blocks_dev, down_rows, RANKS), jnp.bfloat16),
+        scratch_shapes=[pltpu.VMEM((tok_dev, RANKS), jnp.bfloat16)],
+    )(at, x_features, *grad_pieces)
+
+
+def grad_down(at, slot_of, slots, pieces):
+    data_count, blocks_dev, down_rows, _ = pieces.shape
     parts = 2 if down_rows % 256 == 0 else 1
     part_rows = down_rows // parts
 
-    def kernel(at_ref, x_ref, *rest):
-        grad_refs, rest = rest[:tensor_count], rest[tensor_count:]
-        out_ref, grad, x, total, products, x_sem, grad_sem, out_sem = rest
-        copies = []
-        for s in range(tensor_count):
-            core = came_from(at_ref[2], s, tensor_count)
-            for k in range(pipe_count):
-                chip = came_from(at_ref[1], k, pipe_count)
-                first = pl.multiple_of((chip * tensor_count + core) * rows, rows)
-                there = grad.at[:, pl.ds(first, rows)]
-                copies.append(pltpu.make_async_copy(grad_refs[s].at[k], there, grad_sem.at[s, k]))
-        x_copies = [
-            pltpu.make_async_copy(x_ref.at[data], x.at[data], x_sem.at[data])
+    def kernel(at_ref, piece_ref, out_ref, piece, total, piece_sem, out_sem):
+        copies = [
+            [
+                pltpu.make_async_copy(
+                    piece_ref.at[data, block], piece.at[data, block], piece_sem.at[data, block]
+                )
+                for block in range(blocks_dev)
+            ]
             for data in range(data_count)
         ]
-        for copy in copies + x_copies:
-            copy.start()
+        for some in copies:
+            for copy in some:
+                copy.start()
         total[...] = jnp.zeros(total.shape, total.dtype)
-        for copy in copies:
-            copy.wait()
         outs = []
         for part in range(parts):
-            at = slice(part * part_rows, (part + 1) * part_rows)
+            here = slice(part * part_rows, (part + 1) * part_rows)
             for data in range(data_count):
-                if part == 0:
-                    x_copies[data].wait()
                 for block in range(blocks_dev):
-                    here = slice(block * BLOCK, (block + 1) * BLOCK)
-                    products[data % 2, block] = jnp.dot(
-                        x[data, at, here], grad[data, here], preferred_element_type=jnp.float32
-                    )
-                for block in range(blocks_dev):
+                    if part == 0:
+                        copies[data][block].wait()
                     slot = slot_of(at_ref, data, block)
-                    total[part, slot] += products[data % 2, block]
+                    total[part, slot] += piece[data, block, here].astype(total.dtype)
             there = out_ref.at[:, pl.ds(part * part_rows, part_rows)]
             outs.append(pltpu.make_async_copy(total.at[part], there, out_sem.at[part]))
             outs[-1].start()
@@ -318,19 +337,16 @@
         kernel,
         "grad_down",
         VMEM_MOST,
-        in_specs=[SMEM, HBM] + [HBM] * tensor_count,
+        in_specs=[SMEM, HBM],
         out_specs=HBM,
         out_shape=pltpu.HBM((slots, down_rows, RANKS), jnp.float32),
         scratch_shapes=[
-            pltpu.VMEM((data_count, tok_dev, RANKS), jnp.bfloat16),
-            pltpu.VMEM(x_features.shape, jnp.bfloat16),
+            pltpu.VMEM(pieces.shape, jnp.bfloat16),
             pltpu.VMEM((parts, slots, part_rows, RANKS), jnp.float32),
-            pltpu.VMEM((2, blocks_dev, part_rows, RANKS), jnp.float32),
-            pltpu.SemaphoreType.DMA((data_count,)),
-            pltpu.SemaphoreType.DMA((tensor_count, pipe_count)),
+            pltpu.SemaphoreType.DMA((data_count, blocks_dev)),
             pltpu.SemaphoreType.DMA((parts,)),
         ],
-    )(at, x_features, *grad_pieces)
+    )(at, pieces)
 
 
 def grad_up_pieces(at, low_pieces, cot_pieces, data_count, up_rows):
@@ -415,14 +431,12 @@
     )(at, *pieces)
 
 
-def own_rows(at, up, cotangent, a_send):
+def own_rows(at, up, cotangent):
     data_count = len(up)
     rows = cotangent.shape[0]
-    used = a_send.shape[1] - rows
-
-    def kernel(at_ref, cot_ref, send_in_ref, *rest):
-        del send_in_ref
-        up_refs, (b_ref, send_ref, grad, sems) = rest[:data_count], rest[data_count:]
+
+    def kernel(at_ref, cot_ref, *rest):
+        up_refs, (b_ref, grad_ref) = rest[:data_count], rest[data_count:]
         pieces = []
         for data in range(data_count):
             came = wrap(at_ref[0] - data, data_count)
@@ -431,39 +445,26 @@
                 piece = jnp.where(came == k, up_refs[k][...], piece)
             pieces.append(piece)
         b = jnp.concatenate(pieces, axis=0)
+        b_ref[...] = b
         cot = cot_ref[...]
-        grad[...] = jnp.concatenate(
+        grad_ref[...] = jnp.concatenate(
             [
                 lax.dot_general(cot[:, half], b[:, half], LAST_BOTH, preferred_element_type=jnp.float32)
                 for half in (slice(0, KEY_WIDTH), slice(KEY_WIDTH, WIDTH))
             ],
             axis=1,
-        ).astype(grad.dtype)
-        copies = [
-            pltpu.make_async_copy(grad, send_ref.at[data, pl.ds(used, rows)], sems.at[data])
-            for data in range(data_count)
-        ]
-        for copy in copies:
-            copy.start()
-        b_ref[...] = b
-        for copy in copies:
-            copy.wait()
+        ).astype(grad_ref.dtype)
 
     return call(
         kernel,
         "own_rows",
-        in_specs=[SMEM, VMEM, HBM] + [VMEM] * data_count,
-        out_specs=(VMEM, HBM),
+        in_specs=[SMEM, VMEM] + [VMEM] * data_count,
+        out_specs=(VMEM, VMEM),
         out_shape=(
             jax.ShapeDtypeStruct((ADAPTER_RANK, WIDTH), jnp.bfloat16),
-            pltpu.HBM(a_send.shape, a_send.dtype),
+            jax.ShapeDtypeStruct((rows, RANKS), jnp.bfloat16),
         ),
-        input_output_aliases={2: 1},
-        scratch_shapes=[
-            pltpu.VMEM((rows, RANKS), jnp.bfloat16),
-            pltpu.SemaphoreType.DMA((data_count,)),
-        ],
-    )(at, cotangent, a_send, *up)
+    )(at, cotangent, *up)
 
 
 def keys_and_values(at, base_pieces, low_sum, b_own):
@@ -512,12 +513,11 @@
     def slot_of(at_ref, data, block):
         return at_ref[3 + blocks + at_ref[3 + data * blocks_dev + block]]
 
-    b_send, a_send = pick(
-        tenant_of_block, slot_of_tenant, adapter_down, adapter_up, rows, rows
-    )
+    b_send, a_send = pick(tenant_of_block, slot_of_tenant, adapter_down, adapter_up, rows)
     b_came = [b_send[0]] + [shift(b_send[k], "dp", k) for k in range(1, data_count)]
-
-    b_own, a_send = own_rows(at, b_came, cotangent, a_send)
+    b_own, grad_rows = own_rows(at, b_came, cotangent)
+
+    a_send, b_came = lax.optimization_barrier((a_send, b_came))
     a_recv = lax.all_to_all(a_send, "dp", 0, 0, tiled=True)
 
     behind, a_send = lax.optimization_barrier((tokens, a_send))
@@ -540,16 +540,15 @@
     ]
     input_base = cotangent_product(at, cot_pieces, key_value_weight)
 
-    x_send = x_tokens.T.reshape(data_count, down_rows, tok_dev)
-
-    a_recv, x_send, input_base, base_chip_came[:2] = lax.optimization_barrier(
-        (a_recv, x_send, input_base, base_chip_came[:2])
+    grad_chips = jnp.stack([grad_rows] + [swap(grad_rows, "pipe", k) for k in range(1, pipe_count)])
+    grad_pieces = [grad_chips] + [swap(grad_chips, "tensor", s) for s in range(1, tensor_count)]
+    x_features = x_tokens.T.reshape(data_count, down_rows, tok_dev)
+    down_send = grad_down_pieces(at, x_features, grad_pieces)
+
+    a_recv, down_send, input_base, base_chip_came[:2] = lax.optimization_barrier(
+        (a_recv, down_send, input_base, base_chip_came[:2])
     )
-    x_recv = lax.all_to_all(x_send, "dp", 0, 0, tiled=True)
-
-    grad_data = a_recv[:, blocks_dev * down_rows :]
-    grad_chips = jnp.stack([grad_data] + [swap(grad_data, "pipe", k) for k in range(1, pipe_count)])
-    grad_pieces = [grad_chips] + [swap(grad_chips, "tensor", s) for s in range(1, tensor_count)]
+    down_recv = lax.all_to_all(down_send, "dp", 0, 0, tiled=True)
     input_grad = input_gradient(at, input_base, grad_pieces, a_recv)
 
     low_down, base_chip_came = lax.optimization_barrier((a_recv, base_chip_came))
@@ -566,7 +565,7 @@
 
     up_pieces = grad_up_pieces(at, low_pieces, cot_pieces, data_count, up_rows)
     up_came = [up_pieces[0]] + [shift(up_pieces[k], "dp", k) for k in range(1, data_count)]
-    grad_a = grad_down(at, slot_of, slots, x_recv, grad_pieces)
+    grad_a = grad_down(at, slot_of, slots, down_recv)
     up_came, grad_a = lax.optimization_barrier((up_came, grad_a))
     grad_b = grad_up(at, slot_of, slots, up_came)
     return (key_value, input_grad, grad_a, grad_b)

time: 140 us -> 143 us (1.021)
  waiting for transfers between devices: 45.7 us -> 43.6 us
  starting transfers between devices: 34.9 us -> 36.8 us
  Pallas kernels: 39.8 us -> 41.5 us
  other arithmetic: 2.21 us -> 3.74 us
    all_to_all x1, waiting for transfers between devices: 12.6 us -> 4.78 us  [body(): a_recv = lax.all_to_all(a_send, 'dp', 0, 0, tiled=True)]
    all_to_all x1, waiting for transfers between devices: 4 us -> 10.1 us  [body(): down_recv = lax.all_to_all(down_send, 'dp', 0, 0, tiled=True)]
    ppermute x21, starting transfers between devices: 15.7 us -> 17.6 us  [swap(): lax.ppermute(piece, axis, [(i, partner(i, k, count)) for i in range(count)])]
    add x1, other arithmetic: 2.03 us -> 3.61 us  [body(): sum([base_keep[k].astype(jnp.float32)] + [b[k].astype(jnp.float32) for b...]
    pallas_call x2 -> x3, Pallas kernels: 6.64 us -> 8.16 us  [the longest x1 4.18 us: grad_down(): call(kernel, 'grad_down', VMEM_MOST, in_specs=[SMEM, HBM], out_specs=HBM,...]
    unnamed x35 -> x39, local copies, waits for them, and re-layouts: 9.79 us -> 10.5 us
  transfers between devices with their start and end apart: 29 -> 29, of which waited for: 13 -> 11; matrix products, arithmetic and copies ran while one was open for 6% -> 6% of each run, Pallas kernels for 28% -> 25%
where the time goes in v13:
time: 143 us; the launch traced here: 142 us
  waiting for transfers between devices  43.6 us (30%)
  Pallas kernels  41.5 us (29%)
  starting transfers between devices  36.8 us (26%)
  local copies, waits for them, and re-layouts  14.9 us (10%)
  other arithmetic  3.74 us (3%)
    ppermute x21, waiting for transfers between devices, swap(): lax.ppermute(piece, axis, [(i, partner(i, k, count)) for i in range(count)])  25.4 us
    ppermute x21, starting transfers between devices, swap(): lax.ppermute(piece, axis, [(i, partner(i, k, count)) for i in range(count)])  17.6 us
    unnamed x39, local copies, waits for them, and re-layouts  10.5 us
    ppermute x6, starting transfers between devices, shift(): lax.ppermute(piece, axis, [(i, (i + k) % count) for i in range(count)])  10.2 us
    all_to_all x1, waiting for transfers between devices, body(): down_recv = lax.all_to_all(down_send, 'dp', 0, 0, tiled=True)  10.1 us
    pallas_call x2, Pallas kernels, base_product(): call(kernel, 'base_product', grid_spec=pltpu.PrefetchScalarGridSpec(num_s...  8.03 us
    pallas_call x1, Pallas kernels, cotangent_product(): call(kernel, 'cotangent_product', grid=(depth // tile,), in_specs=[SMEM,...  7.95 us
    all_to_all x1, waiting for transfers between devices, body(): a_recv = lax.all_to_all(a_send, 'dp', 0, 0, tiled=True)  4.78 us
  transfers between devices with their start and end apart: 29, of which 11 were waited for; matrix products, arithmetic and copies ran while one was open for 6% of the time, Pallas kernels for 25%

profile of v13, /device:TPU:0, one launch (start us, length us, event | category | flops | bytes accessed | tf_op | source)
XLA Modules:
  0.0 141.5 jit_solution(10385942986643956005)
XLA Ops:
  0.7 3.0 %collective-permute-start.4 = (bf16[128,2048]{1,0:T(8,128)(2,1)}, bf16[128,2048]{1,0:T(8,128)(2,1)S(1)}, u32[]{:S(2)}, u32[]{:S(2)}) collective-permute-start(bf16[128,2048]{1,0:T(8,128)(2,1)} %rest_2_.1), channel_id=1, source_target_pairs={{0,4},{2,6},{4,0},{6,2},{1,5},{3,7},{5,1},{7,3},{8,12},{10,14},{12... | collective-permute-start | bytes 1572872 | tf_op jit(solution)/shard_map/ppermute | solution.py:60
  3.7 1.5 %collective-permute-start.3 = (bf16[128,2048]{1,0:T(8,128)(2,1)}, bf16[128,2048]{1,0:T(8,128)(2,1)}, u32[]{:S(2)}, u32[]{:S(2)}) collective-permute-start(bf16[128,2048]{1,0:T(8,128)(2,1)} %rest_2_.1), channel_id=1, source_target_pairs={{0,2},{2,0},{4,6},{6,4},{1,3},{3,1},{5,7},{7,5},{8,10},{10,8},{12,... | collective-permute-start | bytes 1572872 | tf_op jit(solution)/shard_map/ppermute | solution.py:60
  5.2 4.7 %pick_rows.1 = (bf16[16,2048]{1,0:T(8,128)(2,1)}, bf16[16,2048]{1,0:T(8,128)(2,1)}, bf16[16,2048]{1,0:T(8,128)(2,1)}, bf16[16,2048]{1,0:T(8,128)(2,1)}, bf16[4,2048,128]{2,1,0:T(8,128)(2,1)}) custom-call(s32[32]{0:T(128)} %tenant_ref.1, s32[24]{0:T(128)} %slot_ref.1, bf16[24,256,128]{2,1,0:T(8,128)(2,1)} %down_ref.1, bf16[24,16,2048]{2,1,0:T(8,128)(2,1)} %up_ref.1), custom_call_target="tpu_custom_call" | custom-call | flops 1024 | bytes 1024 | tf_op jit(solution)/shard_map/pick_rows/pallas_call | solution.py:108
  9.9 1.6 %collective-permute-start = (bf16[16,2048]{1,0:T(8,128)(2,1)}, bf16[16,2048]{1,0:T(8,128)(2,1)S(1)}, u32[]{:S(2)}, u32[]{:S(2)}) collective-permute-start(bf16[16,2048]{1,0:T(8,128)(2,1)} %get-tuple-element.33), channel_id=1, source_target_pairs={{0,8},{8,16},{16,24},{24,0},{1,9},{9,17},{17,25},{25,1},{2,10},{10... | collective-permute-start | bytes 196616 | tf_op jit(solution)/shard_map/ppermute | solution.py:39
  11.5 2.6 %collective-permute-start.1 = (bf16[16,2048]{1,0:T(8,128)(2,1)}, bf16[16,2048]{1,0:T(8,128)(2,1)S(1)}, u32[]{:S(2)}, u32[]{:S(2)}) collective-permute-start(bf16[16,2048]{1,0:T(8,128)(2,1)} %get-tuple-element.34), channel_id=1, source_target_pairs={{0,16},{8,24},{16,0},{24,8},{1,17},{9,25},{17,1},{25,9},{2,18},{10... | collective-permute-start | bytes 196616 | tf_op jit(solution)/shard_map/ppermute | solution.py:39
  14.1 1.4 collective-permute-start.2
  15.5 0.1 concatenate.6.at_ref
  15.5 1.4 collective-permute-done.rest_1_
  16.9 2.0 %collective-permute-done.1.rest_2_ = bf16[16,2048]{1,0:T(8,128)(2,1)S(1)} collective-permute-done((bf16[16,2048]{1,0:T(8,128)(2,1)}, bf16[16,2048]{1,0:T(8,128)(2,1)S(1)}, u32[]{:S(2)}, u32[]{:S(2)}) %collective-permute-start.1) | collective-permute-done | bytes 65568 | tf_op jit(solution)/shard_map/ppermute | solution.py:39
  18.9 0.1 collective-permute-done.2.rest_3_
  19.0 0.0 copy-start
  19.0 2.2 %copy-done = bf16[1024,2048]{1,0:T(8,128)(2,1)S(1)} copy-done((bf16[1024,2048]{1,0:T(8,128)(2,1)S(1)}, bf16[1024,2048]{1,0:T(8,128)(2,1)}, u32[]{:S(2)}) %copy-start) | copy-done | bytes 4194328
  21.2 4.4 %base_product.3 = bf16[1,4,128,2048]{3,2,1,0:T(8,128)(2,1)} custom-call(s32[59]{0:T(128)S(1)} %concatenate.6.at_ref, bf16[4,2,128,1024]{3,2,1,0:T(8,128)(2,1)S(1)} %bitcast.66, bf16[1024,2048]{1,0:T(8,128)(2,1)S(1)} %copy-done), custom_call_target="tpu_custom_call" | custom-call | flops 1024 | bytes 1024 | tf_op jit(solution)/shard_map/base_product/pallas_call | solution.py:136
  25.6 4.6 %all-to-all-start = ((bf16[4,2048,128]{2,1,0:T(8,128)(2,1)}), bf16[4,2048,128]{2,1,0:T(8,128)(2,1)}, u32[]{:S(2)}, u32[]{:S(2)}) async-start(bf16[4,2048,128]{2,1,0:T(8,128)(2,1)} %get-tuple-element.36), calls=%async_computation | async-start | bytes 4194304 | tf_op jit(solution)/shard_map/all_to_all | solution.py:521
  30.2 0.6 collective-permute-start.9
  30.8 0.9 own_rows.1
  31.8 0.0 copy-start.12
  31.8 1.5 %collective-permute-start.7 = (bf16[128,128]{1,0:T(8,128)(2,1)S(1)}, bf16[128,128]{1,0:T(8,128)(2,1)S(1)}, u32[]{:S(2)}, u32[]{:S(2)}) collective-permute-start(bf16[128,128]{1,0:T(8,128)(2,1)S(1)} %get-tuple-element.39), channel_id=1, source_target_pairs={{0,6},{2,4},{4,2},{6,0},{1,7},{3,5},{5,3},{7,1},{8,14},{10,12},{12... | collective-permute-start | bytes 98312 | tf_op jit(solution)/shard_map/ppermute | solution.py:60
  33.3 1.5 %collective-permute-start.6 = (bf16[128,128]{1,0:T(8,128)(2,1)S(1)}, bf16[128,128]{1,0:T(8,128)(2,1)S(1)}, u32[]{:S(2)}, u32[]{:S(2)}) collective-permute-start(bf16[128,128]{1,0:T(8,128)(2,1)S(1)} %get-tuple-element.39), channel_id=1, source_target_pairs={{0,4},{2,6},{4,0},{6,2},{1,5},{3,7},{5,1},{7,3},{8,12},{10,14},{12... | collective-permute-start | bytes 98312 | tf_op jit(solution)/shard_map/ppermute | solution.py:60
  34.8 0.5 collective-permute-start.5
  35.3 1.0 slice.53
  36.3 3.6 %collective-permute-done.7 = bf16[128,128]{1,0:T(8,128)(2,1)S(1)} collective-permute-done((bf16[128,128]{1,0:T(8,128)(2,1)S(1)}, bf16[128,128]{1,0:T(8,128)(2,1)S(1)}, u32[]{:S(2)}, u32[]{:S(2)}) %collective-permute-start.7) | collective-permute-done | bytes 32800 | tf_op jit(solution)/shard_map/ppermute | solution.py:60
  39.9 1.5 %collective-permute-start.10 = (bf16[64,2048]{1,0:T(8,128)(2,1)S(1)}, bf16[64,2048]{1,0:T(8,128)(2,1)S(1)}, u32[]{:S(2)}, u32[]{:S(2)}) collective-permute-start(bf16[64,2048]{1,0:T(8,128)(2,1)S(1)} %slice.53), channel_id=1, source_target_pairs={{0,4},{2,6},{4,0},{6,2},{1,5},{3,7},{5,1},{7,3},{8,12},{10,14},{12... | collective-permute-start | bytes 786440 | tf_op jit(solution)/shard_map/ppermute | solution.py:60
  41.4 0.3 collective-permute-start.8
  41.7 2.2 %copy-done.1 = bf16[1024,2048]{1,0:T(8,128)(2,1)S(1)} copy-done((bf16[1024,2048]{1,0:T(8,128)(2,1)S(1)}, bf16[1024,2048]{1,0:T(8,128)(2,1)}, u32[]{:S(2)}) %copy-start.1) | copy-done | bytes 4194328
  43.9 3.6 %base_product.2 = bf16[1,4,128,2048]{3,2,1,0:T(8,128)(2,1)S(1)} custom-call(s32[59]{0:T(128)S(1)} %concatenate.6.at_ref, bf16[4,2,128,1024]{3,2,1,0:T(8,128)(2,1)S(1)} %bitcast.67, bf16[1024,2048]{1,0:T(8,128)(2,1)S(1)} %copy-done.1), custom_call_target="tpu_custom_call" | custom-call | flops 1024 | bytes 1024 | tf_op jit(solution)/shard_map/base_product/pallas_call | solution.py:136
  47.5 0.3 collective-permute-start.12
  47.9 0.7 constant_dynamic-update-slice_fusion.1
  48.6 0.2 collective-permute-start.13
  48.8 0.7 constant_dynamic-update-slice_fusion.rest_3_.rest_5_
  49.5 0.3 collective-permute-start.14
  49.8 3.6 %convert_add_fusion = (f32[128,2048]{1,0:T(8,128)}, bf16[128,2048]{1,0:T(8,128)(2,1)}, bf16[128,2048]{1,0:T(8,128)(2,1)}, bf16[128,2048]{1,0:T(8,128)(2,1)}) fusion(bf16[4,128,2048]{2,1,0:T(8,128)(2,1)} %collective-permute-done.15, bf16[1,4,128,2048]{3,2,1,0:T(8,128)(2,1)S(1)} %base_product.2), kind=kLoop, calls=%fused_computation | loop fusion | flops 3932160 | bytes 6815744 | tf_op jit(solution)/shard_map/add | solution.py:532
  53.4 1.5 %collective-permute-start.17 = (bf16[128,2048]{1,0:T(8,128)(2,1)}, bf16[128,2048]{1,0:T(8,128)(2,1)}, u32[]{:S(2)}, u32[]{:S(2)}) collective-permute-start(bf16[128,2048]{1,0:T(8,128)(2,1)} %get-tuple-element.60), channel_id=1, source_target_pairs={{0,4},{2,6},{4,0},{6,2},{1,5},{3,7},{5,1},{7,3},{8,12},{10,14},{12... | collective-permute-start | bytes 1572872 | tf_op jit(solution)/shard_map/ppermute | solution.py:60
  54.9 0.8 copy-done.9
  55.7 0.5 collective-permute-start.16
  56.3 2.5 %copy.11 = bf16[1024,1024]{1,0:T(8,128)(2,1)} copy(bf16[1024,1024]{0,1:T(8,128)(2,1)S(1)} %bitcast.68) | data formatting | bytes 4194304 | tf_op jit(solution)/shard_map/transpose | solution.py:545
  58.8 1.6 %copy-done.6 = bf16[1024,1024]{1,0:T(8,128)(2,1)S(1)} copy-done((bf16[1024,1024]{1,0:T(8,128)(2,1)S(1)}, bf16[1024,1024]{1,0:T(8,128)(2,1)}, u32[]{:S(2)}) %copy-start.6) | copy-done | bytes 2097176
  60.4 3.1 %grad_down_pieces.1 = bf16[4,8,256,128]{3,2,1,0:T(8,128)(2,1)} custom-call(s32[59]{0:T(128)S(1)} %concatenate.6.at_ref, bf16[4,256,1024]{2,1,0:T(8,128)(2,1)S(1)} %bitcast.69, bf16[4,128,128]{2,1,0:T(8,128)(2,1)S(1)} %pad_maximum_fusion.rest_0_, bf16[4,128,128]{2,1,0:T(8,128)(2,1)S(1)} %collective-permute-done.8.rest_1_), custom_call_target="tpu_custom_call" | custom-call | flops 1024 | bytes 1024 | tf_op jit(solution)/shard_map/grad_down_pieces/pallas_call | solution.py:290
  63.5 1.0 copy-done.10
  64.5 8.0 %cotangent_product.1.base_ref = f32[1024,1024]{1,0:T(8,128)S(1)} custom-call(s32[59]{0:T(128)S(1)} %concatenate.6.at_ref, bf16[1024,2048]{1,0:T(8,128)(2,1)S(1)} %copy-done.2, bf16[128,2048]{1,0:T(8,128)(2,1)S(1)} %copy-done.7, bf16[128,2048]{1,0:T(8,128)(2,1)} %collective-permute-done.3.rest_1_.rest_3_, ...), custom_call_target="tpu_custom_call" | custom-call | flops 1024 | bytes 1024 | tf_op jit(solution)/shard_map/cotangent_product/pallas_call | solution.py:209
  72.5 2.0 %copy-done.4 = f32[1024,1024]{1,0:T(8,128)} copy-done((f32[1024,1024]{1,0:T(8,128)}, f32[1024,1024]{1,0:T(8,128)S(1)}, u32[]{:S(2)}) %copy-start.4) | copy-done | bytes 4194328
  74.5 4.8 %all-to-all-done.a_ref = bf16[4,2048,128]{2,1,0:T(8,128)(2,1)} async-done(((bf16[4,2048,128]{2,1,0:T(8,128)(2,1)}), bf16[4,2048,128]{2,1,0:T(8,128)(2,1)}, u32[]{:S(2)}, u32[]{:S(2)}) %all-to-all-start) | async-done | bytes 2097184 | tf_op jit(solution)/shard_map/all_to_all | solution.py:521
  79.3 4.5 %all-to-all-start.1 = ((bf16[4,8,256,128]{3,2,1,0:T(8,128)(2,1)}), bf16[4,8,256,128]{3,2,1,0:T(8,128)(2,1)}, u32[]{:S(2)}, u32[]{:S(2)}) async-start(bf16[4,8,256,128]{3,2,1,0:T(8,128)(2,1)} %grad_down_pieces.1), calls=%async_computation.1 | async-start | bytes 4194304 | tf_op jit(solution)/shard_map/all_to_all | solution.py:551
  83.7 0.5 collective-permute-start.18
  84.3 14.0 %collective-permute-done.18.rest_3_ = bf16[128,2048]{1,0:T(8,128)(2,1)S(1)} collective-permute-done((bf16[128,2048]{1,0:T(8,128)(2,1)}, bf16[128,2048]{1,0:T(8,128)(2,1)S(1)}, u32[]{:S(2)}, u32[]{:S(2)}) %collective-permute-start.18) | collective-permute-done | bytes 524320 | tf_op jit(solution)/shard_map/ppermute | solution.py:60
  98.3 2.3 %low_product.1 = bf16[2,4,128,128]{3,2,1,0:T(8,128)(2,1)S(1)} custom-call(s32[59]{0:T(128)S(1)} %concatenate.6.at_ref, bf16[1024,1024]{1,0:T(8,128)(2,1)S(1)} %copy-done.3, bf16[4,2048,128]{2,1,0:T(8,128)(2,1)} %all-to-all-done.a_ref), custom_call_target="tpu_custom_call" | custom-call | flops 1024 | bytes 1024 | tf_op jit(solution)/shard_map/low_product/pallas_call | solution.py:170
  100.6 0.1 collective-permute-start.19
  100.7 1.3 collective-permute-done.19
  102.1 0.5 collective-permute-start.22
  102.6 1.5 %collective-permute-start.21 = (bf16[4,128,128]{2,1,0:T(8,128)(2,1)S(1)}, bf16[4,128,128]{2,1,0:T(8,128)(2,1)S(1)}, u32[]{:S(2)}, u32[]{:S(2)}) collective-permute-start(bf16[4,128,128]{2,1,0:T(8,128)(2,1)S(1)} %fusion.3), channel_id=1, source_target_pairs={{0,4},{2,6},{4,0},{6,2},{1,5},{3,7},{5,1},{7,3},{8,12},{10,14},{12... | collective-permute-start | bytes 393224 | tf_op jit(solution)/shard_map/ppermute | solution.py:60
  104.1 1.5 %collective-permute-start.20 = (bf16[4,128,128]{2,1,0:T(8,128)(2,1)S(1)}, bf16[4,128,128]{2,1,0:T(8,128)(2,1)S(1)}, u32[]{:S(2)}, u32[]{:S(2)}) collective-permute-start(bf16[4,128,128]{2,1,0:T(8,128)(2,1)S(1)} %fusion.3), channel_id=1, source_target_pairs={{0,2},{2,0},{4,6},{6,4},{1,3},{3,1},{5,7},{7,5},{8,10},{10,8},{12,... | collective-permute-start | bytes 393224 | tf_op jit(solution)/shard_map/ppermute | solution.py:60
  105.6 3.8 %collective-permute-done.22 = bf16[4,128,128]{2,1,0:T(8,128)(2,1)S(1)} collective-permute-done((bf16[4,128,128]{2,1,0:T(8,128)(2,1)S(1)}, bf16[4,128,128]{2,1,0:T(8,128)(2,1)S(1)}, u32[]{:S(2)}, u32[]{:S(2)}) %collective-permute-start.22) | collective-permute-done | bytes 131104 | tf_op jit(solution)/shard_map/ppermute | solution.py:60
  109.4 1.2 collective-permute-done.21
  110.7 0.1 add_convert_fusion.low_ref.rest_0_
  110.8 0.1 collective-permute-start.23
  110.9 1.3 collective-permute-done.23.rest_1_
  112.2 1.9 %grad_up_pieces.1 = bf16[4,8,16,256]{3,2,1,0:T(8,128)(2,1)S(1)} custom-call(s32[59]{0:T(128)S(1)} %concatenate.6.at_ref, bf16[4,128,128]{2,1,0:T(8,128)(2,1)S(1)} %add_convert_fusion.low_ref.rest_0_, bf16[4,128,128]{2,1,0:T(8,128)(2,1)S(1)} %collective-permute-done.23.rest_1_, bf16[128,2048]{1,0:T(8,128)(2,1)S(1)} %copy-done.7, ...), custom_call_target="tpu_custom_call" | custom-call | flops 1024 | bytes 1024 | tf_op jit(solution)/shard_map/grad_up_pieces/pallas_call | solution.py:398
  114.2 3.5 %collective-permute-start.26 = (bf16[8,16,256]{2,1,0:T(8,128)(2,1)S(1)}, bf16[8,16,256]{2,1,0:T(8,128)(2,1)S(1)}, u32[]{:S(2)}, u32[]{:S(2)}) collective-permute-start(bf16[8,16,256]{2,1,0:T(8,128)(2,1)S(1)} %get-tuple-element.62), channel_id=1, source_target_pairs={{0,24},{8,0},{16,8},{24,16},{1,25},{9,1},{17,9},{25,17},{2,26},{10... | collective-permute-start | bytes 196616 | tf_op jit(solution)/shard_map/ppermute | solution.py:39
  117.7 1.1 collective-permute-start.24
  118.8 4.5 %input_gradient.1 = bf16[1024,1024]{1,0:T(8,128)(2,1)} custom-call(s32[59]{0:T(128)S(1)} %concatenate.6.at_ref, f32[1024,1024]{1,0:T(8,128)S(1)} %copy-done.5, bf16[4,2048,128]{2,1,0:T(8,128)(2,1)} %all-to-all-done.a_ref, bf16[4,128,128]{2,1,0:T(8,128)(2,1)S(1)} %pad_maximum_fusion.rest_0_, bf16[4,128,128]{2,1,0:T(8,128)(2,1)S(1)} %collective-permute-done.8.rest_1_), custom_call_target="tpu_custom_call" | custom-call | flops 1024 | bytes 1024 | tf_op jit(solution)/shard_map/input_gradient/pallas_call | solution.py:250
  123.3 2.5 %keys_and_values.1 = bf16[128,2048]{1,0:T(8,128)(2,1)} custom-call(s32[59]{0:T(128)S(1)} %concatenate.6.at_ref, bf16[4,128,128]{2,1,0:T(8,128)(2,1)S(1)} %add_convert_fusion.low_ref.rest_0_, bf16[64,2048]{1,0:T(8,128)(2,1)S(1)} %copy-done.13, f32[128,2048]{1,0:T(8,128)S(1)} %copy-done.8, bf16[128,2048]{1,0:T(8,128)(2,1)} %collective-permute-done.16.rest_1_, ...), custom_call_target="tpu_custom_call" | custom-call | flops 1024 | bytes 1024 | tf_op jit(solution)/shard_map/keys_and_values/pallas_call | solution.py:484
  125.8 10.1 %all-to-all-done.1.piece_ref = bf16[4,8,256,128]{3,2,1,0:T(8,128)(2,1)} async-done(((bf16[4,8,256,128]{3,2,1,0:T(8,128)(2,1)}), bf16[4,8,256,128]{3,2,1,0:T(8,128)(2,1)}, u32[]{:S(2)}, u32[]{:S(2)}) %all-to-all-start.1) | async-done | bytes 2097184 | tf_op jit(solution)/shard_map/all_to_all | solution.py:551
  135.8 4.2 %grad_down.1 = f32[24,256,128]{2,1,0:T(8,128)} custom-call(s32[59]{0:T(128)} %copy-done.14, bf16[4,8,256,128]{3,2,1,0:T(8,128)(2,1)} %all-to-all-done.1.piece_ref), custom_call_target="tpu_custom_call" | custom-call | flops 1024 | bytes 1024 | tf_op jit(solution)/shard_map/grad_down/pallas_call | solution.py:336
  140.1 1.5 %grad_up.1 = f32[24,16,256]{2,1,0:T(8,128)} custom-call(s32[59]{0:T(128)S(1)} %copy-done.15, bf16[8,16,256]{2,1,0:T(8,128)(2,1)S(1)} %get-tuple-element.54.rest_0_, bf16[8,16,256]{2,1,0:T(8,128)(2,1)S(1)} %collective-permute-done.24.rest_1_, bf16[8,16,256]{2,1,0:T(8,128)(2,1)S(1)} %collective-permute-done.25.rest_2_, ...), custom_call_target="tpu_custom_call" | custom-call | flops 1024 | bytes 1024 | tf_op jit(solution)/shard_map/grad_up/pallas_call | solution.py:425
  (56 shorter events, 0.2 us)
Async XLA Ops:
  0.6 14.8 %copy-start.18 = (s32[24]{0:T(128)S(1)}, s32[24]{0:T(128)}, u32[]{:S(2)}) copy-start(s32[24]{0:T(128)} %slot_ref.1) | copy-start | bytes 292
  0.6 14.8 %copy-start.17 = (s32[32]{0:T(128)S(1)}, s32[32]{0:T(128)}, u32[]{:S(2)}) copy-start(s32[32]{0:T(128)} %tenant_ref.1) | copy-start | bytes 388
  0.7 18.3 %copy-start.3 = (bf16[1024,1024]{1,0:T(8,128)(2,1)S(1)}, bf16[1024,1024]{1,0:T(8,128)(2,1)}, u32[]{:S(2)}) copy-start(bf16[1024,1024]{1,0:T(8,128)(2,1)} %x_ref.1) | copy-start | bytes 6291460
  0.7 18.3 %collective-permute-start.4 = (bf16[128,2048]{1,0:T(8,128)(2,1)}, bf16[128,2048]{1,0:T(8,128)(2,1)S(1)}, u32[]{:S(2)}, u32[]{:S(2)}) collective-permute-start(bf16[128,2048]{1,0:T(8,128)(2,1)} %rest_2_.1), channel_id=1, source_target_pairs={{0,4},{2,6},{4,0},{6,2},{1,5},{3,7},{5,1},{7,3},{8,12},{10,14},{12... | collective-permute-start | bytes 1572872 | tf_op jit(solution)/shard_map/ppermute | solution.py:60
  3.7 15.3 %collective-permute-start.3 = (bf16[128,2048]{1,0:T(8,128)(2,1)}, bf16[128,2048]{1,0:T(8,128)(2,1)}, u32[]{:S(2)}, u32[]{:S(2)}) collective-permute-start(bf16[128,2048]{1,0:T(8,128)(2,1)} %rest_2_.1), channel_id=1, source_target_pairs={{0,2},{2,0},{4,6},{6,4},{1,3},{3,1},{5,7},{7,5},{8,10},{10,8},{12,... | collective-permute-start | bytes 1572872 | tf_op jit(solution)/shard_map/ppermute | solution.py:60
  9.9 7.0 %collective-permute-start = (bf16[16,2048]{1,0:T(8,128)(2,1)}, bf16[16,2048]{1,0:T(8,128)(2,1)S(1)}, u32[]{:S(2)}, u32[]{:S(2)}) collective-permute-start(bf16[16,2048]{1,0:T(8,128)(2,1)} %get-tuple-element.33), channel_id=1, source_target_pairs={{0,8},{8,16},{16,24},{24,0},{1,9},{9,17},{17,25},{25,1},{2,10},{10... | collective-permute-start | bytes 196616 | tf_op jit(solution)/shard_map/ppermute | solution.py:39
  11.5 7.4 %collective-permute-start.1 = (bf16[16,2048]{1,0:T(8,128)(2,1)}, bf16[16,2048]{1,0:T(8,128)(2,1)S(1)}, u32[]{:S(2)}, u32[]{:S(2)}) collective-permute-start(bf16[16,2048]{1,0:T(8,128)(2,1)} %get-tuple-element.34), channel_id=1, source_target_pairs={{0,16},{8,24},{16,0},{24,8},{1,17},{9,25},{17,1},{25,9},{2,18},{10... | collective-permute-start | bytes 196616 | tf_op jit(solution)/shard_map/ppermute | solution.py:39
  14.1 4.9 %collective-permute-start.2 = (bf16[16,2048]{1,0:T(8,128)(2,1)}, bf16[16,2048]{1,0:T(8,128)(2,1)S(1)}, u32[]{:S(2)}, u32[]{:S(2)}) collective-permute-start(bf16[16,2048]{1,0:T(8,128)(2,1)} %get-tuple-element.35), channel_id=1, source_target_pairs={{0,24},{8,0},{16,8},{24,16},{1,25},{9,1},{17,9},{25,17},{2,26},{10... | collective-permute-start | bytes 196616 | tf_op jit(solution)/shard_map/ppermute | solution.py:39
  15.5 107.8 %copy-start.14 = (s32[59]{0:T(128)}, s32[59]{0:T(128)S(1)}, u32[]{:S(2)}) copy-start(s32[59]{0:T(128)S(1)} %concatenate.6.at_ref) | copy-start | bytes 712
  19.0 2.2 %copy-start = (bf16[1024,2048]{1,0:T(8,128)(2,1)S(1)}, bf16[1024,2048]{1,0:T(8,128)(2,1)}, u32[]{:S(2)}) copy-start(bf16[1024,2048]{1,0:T(8,128)(2,1)} %w_ref.5) | copy-start | bytes 12582916
  25.6 5.2 %copy-start.7 = (bf16[128,2048]{1,0:T(8,128)(2,1)S(1)}, bf16[128,2048]{1,0:T(8,128)(2,1)}, u32[]{:S(2)}) copy-start(bf16[128,2048]{1,0:T(8,128)(2,1)} %rest_2_.1) | copy-start | bytes 1572868
  25.6 5.2 %copy-start.16 = (bf16[16,2048]{1,0:T(8,128)(2,1)S(1)}, bf16[16,2048]{1,0:T(8,128)(2,1)}, u32[]{:S(2)}) copy-start(bf16[16,2048]{1,0:T(8,128)(2,1)} %get-tuple-element.32.rest_0_) | copy-start | bytes 196612
  25.6 23.9 %collective-permute-start.15 = (bf16[4,128,2048]{2,1,0:T(8,128)(2,1)}, bf16[4,128,2048]{2,1,0:T(8,128)(2,1)}, u32[]{:S(2)}, u32[]{:S(2)}) collective-permute-start(bf16[4,128,2048]{2,1,0:T(8,128)(2,1)} %bitcast.11), channel_id=1, source_target_pairs={{0,1},{1,0},{2,3},{3,2},{4,5},{5,4},{6,7},{7,6},{8,9},{9,8},{10,11... | collective-permute-start | bytes 6291464 | tf_op jit(solution)/shard_map/ppermute | solution.py:60
  25.6 53.7 %all-to-all-start = ((bf16[4,2048,128]{2,1,0:T(8,128)(2,1)}), bf16[4,2048,128]{2,1,0:T(8,128)(2,1)}, u32[]{:S(2)}, u32[]{:S(2)}) async-start(bf16[4,2048,128]{2,1,0:T(8,128)(2,1)} %get-tuple-element.36), calls=%async_computation | async-start | bytes 4194304 | tf_op jit(solution)/shard_map/all_to_all | solution.py:521
  30.2 17.3 %collective-permute-start.9 = (bf16[64,2048]{1,0:T(8,128)(2,1)S(1)}, bf16[64,2048]{1,0:T(8,128)(2,1)S(1)}, u32[]{:S(2)}, u32[]{:S(2)}) collective-permute-start(bf16[64,2048]{1,0:T(8,128)(2,1)S(1)} %slice.52), channel_id=1, source_target_pairs={{0,2},{2,0},{4,6},{6,4},{1,3},{3,1},{5,7},{7,5},{8,10},{10,8},{12,... | collective-permute-start | bytes 786440 | tf_op jit(solution)/shard_map/ppermute | solution.py:60
  31.8 9.7 %copy-start.12 = (bf16[64,2048]{1,0:T(8,128)(2,1)}, bf16[64,2048]{1,0:T(8,128)(2,1)S(1)}, u32[]{:S(2)}) copy-start(bf16[64,2048]{1,0:T(8,128)(2,1)S(1)} %get-tuple-element.47.b_ref) | copy-start | bytes 786436
  31.8 8.1 %collective-permute-start.7 = (bf16[128,128]{1,0:T(8,128)(2,1)S(1)}, bf16[128,128]{1,0:T(8,128)(2,1)S(1)}, u32[]{:S(2)}, u32[]{:S(2)}) collective-permute-start(bf16[128,128]{1,0:T(8,128)(2,1)S(1)} %get-tuple-element.39), channel_id=1, source_target_pairs={{0,6},{2,4},{4,2},{6,0},{1,7},{3,5},{5,3},{7,1},{8,14},{10,12},{12... | collective-permute-start | bytes 98312 | tf_op jit(solution)/shard_map/ppermute | solution.py:60
  33.3 6.6 %collective-permute-start.6 = (bf16[128,128]{1,0:T(8,128)(2,1)S(1)}, bf16[128,128]{1,0:T(8,128)(2,1)S(1)}, u32[]{:S(2)}, u32[]{:S(2)}) collective-permute-start(bf16[128,128]{1,0:T(8,128)(2,1)S(1)} %get-tuple-element.39), channel_id=1, source_target_pairs={{0,4},{2,6},{4,0},{6,2},{1,5},{3,7},{5,1},{7,3},{8,12},{10,14},{12... | collective-permute-start | bytes 98312 | tf_op jit(solution)/shard_map/ppermute | solution.py:60
  34.8 6.6 %collective-permute-start.5 = (bf16[128,128]{1,0:T(8,128)(2,1)S(1)}, bf16[128,128]{1,0:T(8,128)(2,1)S(1)}, u32[]{:S(2)}, u32[]{:S(2)}) collective-permute-start(bf16[128,128]{1,0:T(8,128)(2,1)S(1)} %get-tuple-element.39), channel_id=1, source_target_pairs={{0,2},{2,0},{4,6},{6,4},{1,3},{3,1},{5,7},{7,5},{8,10},{10,8},{12,... | collective-permute-start | bytes 98312 | tf_op jit(solution)/shard_map/ppermute | solution.py:60
  39.9 15.1 %collective-permute-start.11 = (bf16[128,2048]{1,0:T(8,128)(2,1)S(1)}, bf16[128,2048]{1,0:T(8,128)(2,1)S(1)}, u32[]{:S(2)}, u32[]{:S(2)}) collective-permute-start(bf16[128,2048]{1,0:T(8,128)(2,1)S(1)} %copy-done.7), channel_id=1, source_target_pairs={{0,1},{1,0},{2,3},{3,2},{4,5},{5,4},{6,7},{7,6},{8,9},{9,8},{10,11... | collective-permute-start | bytes 1572872 | tf_op jit(solution)/shard_map/ppermute | solution.py:60
  39.9 8.7 %collective-permute-start.10 = (bf16[64,2048]{1,0:T(8,128)(2,1)S(1)}, bf16[64,2048]{1,0:T(8,128)(2,1)S(1)}, u32[]{:S(2)}, u32[]{:S(2)}) collective-permute-start(bf16[64,2048]{1,0:T(8,128)(2,1)S(1)} %slice.53), channel_id=1, source_target_pairs={{0,4},{2,6},{4,0},{6,2},{1,5},{3,7},{5,1},{7,3},{8,12},{10,14},{12... | collective-permute-start | bytes 786440 | tf_op jit(solution)/shard_map/ppermute | solution.py:60
  41.4 12.0 %collective-permute-start.8 = (bf16[4,128,128]{2,1,0:T(8,128)(2,1)S(1)}, bf16[4,128,128]{2,1,0:T(8,128)(2,1)S(1)}, u32[]{:S(2)}, u32[]{:S(2)}) collective-permute-start(bf16[4,128,128]{2,1,0:T(8,128)(2,1)S(1)} %pad_maximum_fusion.rest_0_), channel_id=1, source_target_pairs={{0,1},{1,0},{2,3},{3,2},{4,5},{5,4},{6,7},{7,6},{8,9},{9,8},{10,11... | collective-permute-start | bytes 393224 | tf_op jit(solution)/shard_map/ppermute | solution.py:60
  41.7 2.2 %copy-start.1 = (bf16[1024,2048]{1,0:T(8,128)(2,1)S(1)}, bf16[1024,2048]{1,0:T(8,128)(2,1)}, u32[]{:S(2)}) copy-start(bf16[1024,2048]{1,0:T(8,128)(2,1)} %w_ref.5) | copy-start | bytes 12582916
  47.5 15.9 %collective-permute-start.12 = (bf16[128,2048]{1,0:T(8,128)(2,1)}, bf16[128,2048]{1,0:T(8,128)(2,1)}, u32[]{:S(2)}, u32[]{:S(2)}) collective-permute-start(bf16[128,2048]{1,0:T(8,128)(2,1)} %collective-permute-done.3.rest_1_.rest_3_), channel_id=1, source_target_pairs={{0,1},{1,0},{2,3},{3,2},{4,5},{5,4},{6,7},{7,6},{8,9},{9,8},{10,11... | collective-permute-start | bytes 1572872 | tf_op jit(solution)/shard_map/ppermute | solution.py:60
  48.6 14.9 %collective-permute-start.13 = (bf16[128,2048]{1,0:T(8,128)(2,1)S(1)}, bf16[128,2048]{1,0:T(8,128)(2,1)}, u32[]{:S(2)}, u32[]{:S(2)}) collective-permute-start(bf16[128,2048]{1,0:T(8,128)(2,1)S(1)} %collective-permute-done.4.rest_2_.rest_4_), channel_id=1, source_target_pairs={{0,1},{1,0},{2,3},{3,2},{4,5},{5,4},{6,7},{7,6},{8,9},{9,8},{10,11... | collective-permute-start | bytes 1572872 | tf_op jit(solution)/shard_map/ppermute | solution.py:60
  49.5 13.9 %collective-permute-start.14 = (bf16[128,2048]{1,0:T(8,128)(2,1)}, bf16[128,2048]{1,0:T(8,128)(2,1)}, u32[]{:S(2)}, u32[]{:S(2)}) collective-permute-start(bf16[128,2048]{1,0:T(8,128)(2,1)} %constant_dynamic-update-slice_fusion.rest_3_.rest_5_), channel_id=1, source_target_pairs={{0,1},{1,0},{2,3},{3,2},{4,5},{5,4},{6,7},{7,6},{8,9},{9,8},{10,11... | collective-permute-start | bytes 1572872 | tf_op jit(solution)/shard_map/ppermute | solution.py:60
  53.4 21.1 %collective-permute-start.17 = (bf16[128,2048]{1,0:T(8,128)(2,1)}, bf16[128,2048]{1,0:T(8,128)(2,1)}, u32[]{:S(2)}, u32[]{:S(2)}) collective-permute-start(bf16[128,2048]{1,0:T(8,128)(2,1)} %get-tuple-element.60), channel_id=1, source_target_pairs={{0,4},{2,6},{4,0},{6,2},{1,5},{3,7},{5,1},{7,3},{8,12},{10,14},{12... | collective-permute-start | bytes 1572872 | tf_op jit(solution)/shard_map/ppermute | solution.py:60
  54.9 0.8 copy-start.9
  55.7 18.7 %collective-permute-start.16 = (bf16[128,2048]{1,0:T(8,128)(2,1)}, bf16[128,2048]{1,0:T(8,128)(2,1)}, u32[]{:S(2)}, u32[]{:S(2)}) collective-permute-start(bf16[128,2048]{1,0:T(8,128)(2,1)} %get-tuple-element.61), channel_id=1, source_target_pairs={{0,2},{2,0},{4,6},{6,4},{1,3},{3,1},{5,7},{7,5},{8,10},{10,8},{12,... | collective-permute-start | bytes 1572872 | tf_op jit(solution)/shard_map/ppermute | solution.py:60
  58.8 1.6 %copy-start.6 = (bf16[1024,1024]{1,0:T(8,128)(2,1)S(1)}, bf16[1024,1024]{1,0:T(8,128)(2,1)}, u32[]{:S(2)}) copy-start(bf16[1024,1024]{1,0:T(8,128)(2,1)} %copy.11) | copy-start | bytes 6291460
  60.4 3.1 %copy-start.2 = (bf16[1024,2048]{1,0:T(8,128)(2,1)S(1)}, bf16[1024,2048]{1,0:T(8,128)(2,1)}, u32[]{:S(2)}) copy-start(bf16[1024,2048]{1,0:T(8,128)(2,1)} %w_ref.5) | copy-start | bytes 12582916
  63.5 1.0 copy-start.10
  72.5 2.0 %copy-start.4 = (f32[1024,1024]{1,0:T(8,128)}, f32[1024,1024]{1,0:T(8,128)S(1)}, u32[]{:S(2)}) copy-start(f32[1024,1024]{1,0:T(8,128)S(1)} %cotangent_product.1.base_ref) | copy-start | bytes 12582916
  79.3 56.6 %all-to-all-start.1 = ((bf16[4,8,256,128]{3,2,1,0:T(8,128)(2,1)}), bf16[4,8,256,128]{3,2,1,0:T(8,128)(2,1)}, u32[]{:S(2)}, u32[]{:S(2)}) async-start(bf16[4,8,256,128]{3,2,1,0:T(8,128)(2,1)} %grad_down_pieces.1), calls=%async_computation.1 | async-start | bytes 4194304 | tf_op jit(solution)/shard_map/all_to_all | solution.py:551
  83.7 28.5 %copy-start.11 = (bf16[128,2048]{1,0:T(8,128)(2,1)S(1)}, bf16[128,2048]{1,0:T(8,128)(2,1)}, u32[]{:S(2)}) copy-start(bf16[128,2048]{1,0:T(8,128)(2,1)} %copy-done.9) | copy-start | bytes 1572868
  83.7 14.6 %collective-permute-start.18 = (bf16[128,2048]{1,0:T(8,128)(2,1)}, bf16[128,2048]{1,0:T(8,128)(2,1)S(1)}, u32[]{:S(2)}, u32[]{:S(2)}) collective-permute-start(bf16[128,2048]{1,0:T(8,128)(2,1)} %get-tuple-element.59), channel_id=1, source_target_pairs={{0,6},{2,4},{4,2},{6,0},{1,7},{3,5},{5,3},{7,1},{8,14},{10,12},{12... | collective-permute-start | bytes 1572872 | tf_op jit(solution)/shard_map/ppermute | solution.py:60
  100.6 1.4 collective-permute-start.19
  102.1 7.4 %collective-permute-start.22 = (bf16[4,128,128]{2,1,0:T(8,128)(2,1)S(1)}, bf16[4,128,128]{2,1,0:T(8,128)(2,1)S(1)}, u32[]{:S(2)}, u32[]{:S(2)}) collective-permute-start(bf16[4,128,128]{2,1,0:T(8,128)(2,1)S(1)} %fusion.3), channel_id=1, source_target_pairs={{0,6},{2,4},{4,2},{6,0},{1,7},{3,5},{5,3},{7,1},{8,14},{10,12},{12... | collective-permute-start | bytes 393224 | tf_op jit(solution)/shard_map/ppermute | solution.py:60
  102.6 8.1 %collective-permute-start.21 = (bf16[4,128,128]{2,1,0:T(8,128)(2,1)S(1)}, bf16[4,128,128]{2,1,0:T(8,128)(2,1)S(1)}, u32[]{:S(2)}, u32[]{:S(2)}) collective-permute-start(bf16[4,128,128]{2,1,0:T(8,128)(2,1)S(1)} %fusion.3), channel_id=1, source_target_pairs={{0,4},{2,6},{4,0},{6,2},{1,5},{3,7},{5,1},{7,3},{8,12},{10,14},{12... | collective-permute-start | bytes 393224 | tf_op jit(solution)/shard_map/ppermute | solution.py:60
  104.1 6.5 %collective-permute-start.20 = (bf16[4,128,128]{2,1,0:T(8,128)(2,1)S(1)}, bf16[4,128,128]{2,1,0:T(8,128)(2,1)S(1)}, u32[]{:S(2)}, u32[]{:S(2)}) collective-permute-start(bf16[4,128,128]{2,1,0:T(8,128)(2,1)S(1)} %fusion.3), channel_id=1, source_target_pairs={{0,2},{2,0},{4,6},{6,4},{1,3},{3,1},{5,7},{7,5},{8,10},{10,8},{12,... | collective-permute-start | bytes 393224 | tf_op jit(solution)/shard_map/ppermute | solution.py:60
  110.8 8.0 %copy-start.5 = (f32[1024,1024]{1,0:T(8,128)S(1)}, f32[1024,1024]{1,0:T(8,128)}, u32[]{:S(2)}) copy-start(f32[1024,1024]{1,0:T(8,128)} %copy-done.4) | copy-start | bytes 12582916
  110.8 1.4 collective-permute-start.23
  114.2 25.9 %collective-permute-start.26 = (bf16[8,16,256]{2,1,0:T(8,128)(2,1)S(1)}, bf16[8,16,256]{2,1,0:T(8,128)(2,1)S(1)}, u32[]{:S(2)}, u32[]{:S(2)}) collective-permute-start(bf16[8,16,256]{2,1,0:T(8,128)(2,1)S(1)} %get-tuple-element.62), channel_id=1, source_target_pairs={{0,24},{8,0},{16,8},{24,16},{1,25},{9,1},{17,9},{25,17},{2,26},{10... | collective-permute-start | bytes 196616 | tf_op jit(solution)/shard_map/ppermute | solution.py:39
  117.6 22.4 %collective-permute-start.25 = (bf16[8,16,256]{2,1,0:T(8,128)(2,1)S(1)}, bf16[8,16,256]{2,1,0:T(8,128)(2,1)S(1)}, u32[]{:S(2)}, u32[]{:S(2)}) collective-permute-start(bf16[8,16,256]{2,1,0:T(8,128)(2,1)S(1)} %get-tuple-element.63), channel_id=1, source_target_pairs={{0,16},{8,24},{16,0},{24,8},{1,17},{9,25},{17,1},{25,9},{2,18},{10... | collective-permute-start | bytes 196616 | tf_op jit(solution)/shard_map/ppermute | solution.py:39
  117.7 5.7 %copy-start.8 = (f32[128,2048]{1,0:T(8,128)S(1)}, f32[128,2048]{1,0:T(8,128)}, u32[]{:S(2)}) copy-start(f32[128,2048]{1,0:T(8,128)} %get-tuple-element.58.rest_0_) | copy-start | bytes 3145732
  117.7 5.7 %copy-start.13 = (bf16[64,2048]{1,0:T(8,128)(2,1)S(1)}, bf16[64,2048]{1,0:T(8,128)(2,1)}, u32[]{:S(2)}) copy-start(bf16[64,2048]{1,0:T(8,128)(2,1)} %copy-done.12) | copy-start | bytes 786436
  117.7 22.4 %collective-permute-start.24 = (bf16[8,16,256]{2,1,0:T(8,128)(2,1)S(1)}, bf16[8,16,256]{2,1,0:T(8,128)(2,1)S(1)}, u32[]{:S(2)}, u32[]{:S(2)}) collective-permute-start(bf16[8,16,256]{2,1,0:T(8,128)(2,1)S(1)} %get-tuple-element.64), channel_id=1, source_target_pairs={{0,8},{8,16},{16,24},{24,0},{1,9},{9,17},{17,25},{25,1},{2,10},{10... | collective-permute-start | bytes 196616 | tf_op jit(solution)/shard_map/ppermute | solution.py:39
  125.8 14.3 %copy-start.15 = (s32[59]{0:T(128)S(1)}, s32[59]{0:T(128)}, u32[]{:S(2)}) copy-start(s32[59]{0:T(128)} %copy-done.14) | copy-start | bytes 712

commit v14 on v13

--- a/solution.py
+++ b/solution.py
@@ -60,10 +60,10 @@
     return lax.ppermute(piece, axis, [(i, partner(i, k, count)) for i in range(count)])
 
 
-def gather_chips(piece, behind):
+def gather_chips(piece, later, behind):
     count = lax.axis_size("pipe")
     in_halves = count == 4 and piece.shape[0] % 32 == 0
-    came = [swap(piece, "pipe", k) for k in range(1, 3 if in_halves else count)]
+    came = [swap(piece if k == 1 else later, "pipe", k) for k in range(1, 3 if in_halves else count)]
     came, one, two = lax.optimization_barrier((came, behind, behind))
     if in_halves:
         half = piece.shape[0] // 2
@@ -136,6 +136,7 @@
     return call(
         kernel,
         "base_product",
+        VMEM_MOST,
         grid_spec=pltpu.PrefetchScalarGridSpec(
             num_scalar_prefetch=1,
             grid=(WIDTH // tile, count),
@@ -209,6 +210,7 @@
     return call(
         kernel,
         "cotangent_product",
+        VMEM_MOST,
         grid=(depth // tile,),
         in_specs=[SMEM, pl.BlockSpec((tile, WIDTH), lambda n: (n, 0))] + [ANY] * len(order),
         out_specs=pl.BlockSpec((tok_dev, tile), lambda n: (0, n)),
@@ -520,8 +522,8 @@
     a_send, b_came = lax.optimization_barrier((a_send, b_came))
     a_recv = lax.all_to_all(a_send, "dp", 0, 0, tiled=True)
 
-    behind, a_send = lax.optimization_barrier((tokens, a_send))
-    cot_chips, base_tokens, x_tokens = gather_chips(cotangent, behind)
+    behind, cot_later, a_send = lax.optimization_barrier((tokens, cotangent, a_send))
+    cot_chips, base_tokens, x_tokens = gather_chips(cotangent, cot_later, behind)
     cot_chips = [cotangent] + cot_chips
 
     tokens_by_group = base_tokens.reshape(pipe_count, tensor_count, rows, feature_count)
@@ -545,13 +547,15 @@
     x_features = x_tokens.T.reshape(data_count, down_rows, tok_dev)
     down_send = grad_down_pieces(at, x_features, grad_pieces)
 
-    a_recv, down_send, input_base, base_chip_came[:2] = lax.optimization_barrier(
-        (a_recv, down_send, input_base, base_chip_came[:2])
+    a_recv, down_send, base_chip_came[:2] = lax.optimization_barrier(
+        (a_recv, down_send, base_chip_came[:2])
     )
     down_recv = lax.all_to_all(down_send, "dp", 0, 0, tiled=True)
+
+    low_down, base_chip_came, input_base = lax.optimization_barrier(
+        (a_recv, base_chip_came, input_base)
+    )
     input_grad = input_gradient(at, input_base, grad_pieces, a_recv)
-
-    low_down, base_chip_came = lax.optimization_barrier((a_recv, base_chip_came))
     low_part = low_product(at, tokens, low_down, pipe_count, tensor_count)
     low_core = sum(
         [low_part[0].astype(jnp.float32)]

time: 143 us -> 155 us (1.084)
  waiting for transfers between devices: 43.6 us -> 52.6 us
  Pallas kernels: 41.5 us -> 48.4 us
  local copies, waits for them, and re-layouts: 14.9 us -> 9.07 us
  starting transfers between devices: 36.8 us -> 38.7 us
    all_to_all x1, waiting for transfers between devices: 4.78 us -> 15 us  [body(): a_recv = lax.all_to_all(a_send, 'dp', 0, 0, tiled=True)]
    ppermute x21, waiting for transfers between devices: 25.4 us -> 35.5 us  [swap(): lax.ppermute(piece, axis, [(i, partner(i, k, count)) for i in range(count)])]
    all_to_all x1, waiting for transfers between devices: 10.1 us -> 0.01 us  [body(): down_recv = lax.all_to_all(down_send, 'dp', 0, 0, tiled=True)]
    pallas_call x3, Pallas kernels: 16 us -> 22.3 us  [the longest x2 12.1 us: base_product(): call(kernel, 'base_product', VMEM_MOST, grid_spec=pltpu.PrefetchScalarGri...]
    unnamed x39 -> x53, local copies, waits for them, and re-layouts: 10.5 us -> 4.8 us
    ppermute x6, starting transfers between devices: 10.2 us -> 12.6 us  [shift(): lax.ppermute(piece, axis, [(i, (i + k) % count) for i in range(count)])]
  transfers between devices with their start and end apart: 29 -> 29, of which waited for: 11 -> 14; matrix products, arithmetic and copies ran while one was open for 6% -> 6% of each run, Pallas kernels for 25% -> 23%
where the time goes in v14:
time: 155 us; the launch traced here: 154 us
  waiting for transfers between devices  52.6 us (34%)
  Pallas kernels  48.4 us (31%)
  starting transfers between devices  38.7 us (25%)
  local copies, waits for them, and re-layouts  9.07 us (6%)
  other arithmetic  4.48 us (3%)
    ppermute x21, waiting for transfers between devices, swap(): lax.ppermute(piece, axis, [(i, partner(i, k, count)) for i in range(count)])  35.5 us
    ppermute x21, starting transfers between devices, swap(): lax.ppermute(piece, axis, [(i, partner(i, k, count)) for i in range(count)])  17.2 us
    all_to_all x1, waiting for transfers between devices, body(): a_recv = lax.all_to_all(a_send, 'dp', 0, 0, tiled=True)  15 us
    ppermute x6, starting transfers between devices, shift(): lax.ppermute(piece, axis, [(i, (i + k) % count) for i in range(count)])  12.6 us
    pallas_call x2, Pallas kernels, base_product(): call(kernel, 'base_product', VMEM_MOST, grid_spec=pltpu.PrefetchScalarGri...  12.1 us
    pallas_call x1, Pallas kernels, cotangent_product(): call(kernel, 'cotangent_product', VMEM_MOST, grid=(depth // tile,), in_sp...  10.2 us
    pallas_call x1, Pallas kernels, pick(): call(kernel, 'pick_rows', VMEM_MOST, out_shape=(up_shape,) * data_count +...  5.06 us
    unnamed x53, local copies, waits for them, and re-layouts  4.8 us
  transfers between devices with their start and end apart: 29, of which 14 were waited for; matrix products, arithmetic and copies ran while one was open for 6% of the time, Pallas kernels for 23%

profile of v14, /device:TPU:0, one launch (start us, length us, event | category | flops | bytes accessed | tf_op | source)
XLA Modules:
  0.0 154.1 jit_solution(7340929002487765149)
XLA Ops:
  0.7 5.1 %pick_rows.1 = (bf16[16,2048]{1,0:T(8,128)(2,1)}, bf16[16,2048]{1,0:T(8,128)(2,1)}, bf16[16,2048]{1,0:T(8,128)(2,1)}, bf16[16,2048]{1,0:T(8,128)(2,1)}, bf16[4,2048,128]{2,1,0:T(8,128)(2,1)}) custom-call(s32[32]{0:T(128)} %tenant_ref.1, s32[24]{0:T(128)} %slot_ref.1, bf16[24,256,128]{2,1,0:T(8,128)(2,1)} %down_ref.1, bf16[24,16,2048]{2,1,0:T(8,128)(2,1)} %up_ref.1), custom_call_target="tpu_custom_call" | custom-call | flops 1024 | bytes 1024 | tf_op jit(solution)/shard_map/pick_rows/pallas_call | solution.py:108
  5.7 3.1 %collective-permute-start = (bf16[16,2048]{1,0:T(8,128)(2,1)}, bf16[16,2048]{1,0:T(8,128)(2,1)S(1)}, u32[]{:S(2)}, u32[]{:S(2)}) collective-permute-start(bf16[16,2048]{1,0:T(8,128)(2,1)} %get-tuple-element.34), channel_id=1, source_target_pairs={{0,8},{8,16},{16,24},{24,0},{1,9},{9,17},{17,25},{25,1},{2,10},{10... | collective-permute-start | bytes 196616 | tf_op jit(solution)/shard_map/ppermute | solution.py:39
  8.8 2.6 %collective-permute-start.1 = (bf16[16,2048]{1,0:T(8,128)(2,1)}, bf16[16,2048]{1,0:T(8,128)(2,1)S(1)}, u32[]{:S(2)}, u32[]{:S(2)}) collective-permute-start(bf16[16,2048]{1,0:T(8,128)(2,1)} %get-tuple-element.35), channel_id=1, source_target_pairs={{0,16},{8,24},{16,0},{24,8},{1,17},{9,25},{17,1},{25,9},{2,18},{10... | collective-permute-start | bytes 196616 | tf_op jit(solution)/shard_map/ppermute | solution.py:39
  11.4 1.3 collective-permute-start.2
  12.8 1.5 collective-permute-start.3
  14.3 1.9 %collective-permute-done.1.rest_2_ = bf16[16,2048]{1,0:T(8,128)(2,1)S(1)} collective-permute-done((bf16[16,2048]{1,0:T(8,128)(2,1)}, bf16[16,2048]{1,0:T(8,128)(2,1)S(1)}, u32[]{:S(2)}, u32[]{:S(2)}) %collective-permute-start.1) | collective-permute-done | bytes 65568 | tf_op jit(solution)/shard_map/ppermute | solution.py:39
  16.1 0.2 collective-permute-done.2.rest_3_
  16.3 1.6 %collective-permute-start.4 = (bf16[128,2048]{1,0:T(8,128)(2,1)S(1)}, bf16[128,2048]{1,0:T(8,128)(2,1)S(1)}, u32[]{:S(2)}, u32[]{:S(2)}) collective-permute-start(bf16[128,2048]{1,0:T(8,128)(2,1)S(1)} %copy-done.3), channel_id=1, source_target_pairs={{0,4},{2,6},{4,0},{6,2},{1,5},{3,7},{5,1},{7,3},{8,12},{10,14},{12... | collective-permute-start | bytes 1572872 | tf_op jit(solution)/shard_map/ppermute | solution.py:60
  17.9 0.7 concatenate.6.at_ref
  18.6 7.0 %collective-permute-done.3.rest_1_.rest_3_ = bf16[128,2048]{1,0:T(8,128)(2,1)S(1)} collective-permute-done((bf16[128,2048]{1,0:T(8,128)(2,1)S(1)}, bf16[128,2048]{1,0:T(8,128)(2,1)S(1)}, u32[]{:S(2)}, u32[]{:S(2)}) %collective-permute-start.3) | collective-permute-done | bytes 524320 | tf_op jit(solution)/shard_map/ppermute | solution.py:60
  25.6 4.2 %collective-permute-done.4.rest_2_.rest_4_ = bf16[128,2048]{1,0:T(8,128)(2,1)S(1)} collective-permute-done((bf16[128,2048]{1,0:T(8,128)(2,1)S(1)}, bf16[128,2048]{1,0:T(8,128)(2,1)S(1)}, u32[]{:S(2)}, u32[]{:S(2)}) %collective-permute-start.4) | collective-permute-done | bytes 524320 | tf_op jit(solution)/shard_map/ppermute | solution.py:60
  29.8 6.0 %base_product.3 = bf16[1,4,128,2048]{3,2,1,0:T(8,128)(2,1)} custom-call(s32[59]{0:T(128)} %concatenate.6.at_ref, bf16[4,2,128,1024]{3,2,1,0:T(8,128)(2,1)} %bitcast.66, bf16[1024,2048]{1,0:T(8,128)(2,1)} %w_ref.5), custom_call_target="tpu_custom_call" | custom-call | flops 1024 | bytes 1024 | tf_op jit(solution)/shard_map/base_product/pallas_call | solution.py:136
  35.8 4.5 %all-to-all-start = ((bf16[4,2048,128]{2,1,0:T(8,128)(2,1)}), bf16[4,2048,128]{2,1,0:T(8,128)(2,1)}, u32[]{:S(2)}, u32[]{:S(2)}) async-start(bf16[4,2048,128]{2,1,0:T(8,128)(2,1)} %get-tuple-element.37), calls=%async_computation | async-start | bytes 4194304 | tf_op jit(solution)/shard_map/all_to_all | solution.py:523
  40.3 6.1 %base_product.2 = bf16[1,4,128,2048]{3,2,1,0:T(8,128)(2,1)} custom-call(s32[59]{0:T(128)} %concatenate.6.at_ref, bf16[4,2,128,1024]{3,2,1,0:T(8,128)(2,1)} %bitcast.67, bf16[1024,2048]{1,0:T(8,128)(2,1)} %w_ref.5), custom_call_target="tpu_custom_call" | custom-call | flops 1024 | bytes 1024 | tf_op jit(solution)/shard_map/base_product/pallas_call | solution.py:136
  46.4 0.0 copy-start
  46.4 4.4 %convert_add_fusion = (f32[128,2048]{1,0:T(8,128)}, bf16[128,2048]{1,0:T(8,128)(2,1)}, bf16[128,2048]{1,0:T(8,128)(2,1)}, bf16[128,2048]{1,0:T(8,128)(2,1)}) fusion(bf16[4,128,2048]{2,1,0:T(8,128)(2,1)} %collective-permute-done.9, bf16[1,4,128,2048]{3,2,1,0:T(8,128)(2,1)} %base_product.2), kind=kLoop, calls=%fused_computation | loop fusion | flops 3932160 | bytes 6815744 | tf_op jit(solution)/shard_map/add | solution.py:534
  50.7 0.7 collective-permute-start.10
  51.4 1.4 collective-permute-start.11
  52.9 0.9 own_rows.1
  53.8 0.7 copy-done.18
  54.5 1.3 collective-permute-start.7
  55.8 0.9 collective-permute-start.6
  56.7 1.3 collective-permute-start.5
  58.0 8.7 %collective-permute-done.7 = bf16[128,128]{1,0:T(8,128)(2,1)S(1)} collective-permute-done((bf16[128,128]{1,0:T(8,128)(2,1)S(1)}, bf16[128,128]{1,0:T(8,128)(2,1)S(1)}, u32[]{:S(2)}, u32[]{:S(2)}) %collective-permute-start.7) | collective-permute-done | bytes 32800 | tf_op jit(solution)/shard_map/ppermute | solution.py:60
  66.7 0.4 collective-permute-done.6
  67.1 0.1 collective-permute-start.8
  67.2 2.6 %copy.11 = bf16[1024,1024]{1,0:T(8,128)(2,1)} copy(bf16[1024,1024]{0,1:T(8,128)(2,1)S(1)} %bitcast.68) | data formatting | bytes 4194304 | tf_op jit(solution)/shard_map/transpose | solution.py:547
  69.8 1.6 %copy-done.2 = bf16[1024,1024]{1,0:T(8,128)(2,1)S(1)} copy-done((bf16[1024,1024]{1,0:T(8,128)(2,1)S(1)}, bf16[1024,1024]{1,0:T(8,128)(2,1)}, u32[]{:S(2)}) %copy-start.2) | copy-done | bytes 2097176
  71.4 3.1 %grad_down_pieces.1 = bf16[4,8,256,128]{3,2,1,0:T(8,128)(2,1)} custom-call(s32[59]{0:T(128)S(1)} %copy-done.20, bf16[4,256,1024]{2,1,0:T(8,128)(2,1)S(1)} %bitcast.69, bf16[4,128,128]{2,1,0:T(8,128)(2,1)S(1)} %pad_maximum_fusion.rest_0_, bf16[4,128,128]{2,1,0:T(8,128)(2,1)S(1)} %collective-permute-done.8.rest_1_), custom_call_target="tpu_custom_call" | custom-call | flops 1024 | bytes 1024 | tf_op jit(solution)/shard_map/grad_down_pieces/pallas_call | solution.py:292
  74.4 15.0 %all-to-all-done.a_ref = bf16[4,2048,128]{2,1,0:T(8,128)(2,1)} async-done(((bf16[4,2048,128]{2,1,0:T(8,128)(2,1)}), bf16[4,2048,128]{2,1,0:T(8,128)(2,1)}, u32[]{:S(2)}, u32[]{:S(2)}) %all-to-all-start) | async-done | bytes 2097184 | tf_op jit(solution)/shard_map/all_to_all | solution.py:523
  89.5 4.5 %all-to-all-start.1 = ((bf16[4,8,256,128]{3,2,1,0:T(8,128)(2,1)}), bf16[4,8,256,128]{3,2,1,0:T(8,128)(2,1)}, u32[]{:S(2)}, u32[]{:S(2)}) async-start(bf16[4,8,256,128]{3,2,1,0:T(8,128)(2,1)} %grad_down_pieces.1), calls=%async_computation.1 | async-start | bytes 4194304 | tf_op jit(solution)/shard_map/all_to_all | solution.py:553
  93.9 1.0 slice.58
  94.9 0.8 collective-permute-start.13
  95.7 1.5 collective-permute-start.14
  97.2 0.5 collective-permute-start.16
  97.7 5.2 %collective-permute-done.13 = bf16[64,2048]{1,0:T(8,128)(2,1)S(1)} collective-permute-done((bf16[64,2048]{1,0:T(8,128)(2,1)S(1)}, bf16[64,2048]{1,0:T(8,128)(2,1)S(1)}, u32[]{:S(2)}, u32[]{:S(2)}) %collective-permute-start.13) | collective-permute-done | bytes 262176 | tf_op jit(solution)/shard_map/ppermute | solution.py:60
  102.9 0.5 collective-permute-done.14
  103.5 0.1 collective-permute-start.18
  103.6 1.7 %collective-permute-start.12 = (bf16[128,2048]{1,0:T(8,128)(2,1)}, bf16[128,2048]{1,0:T(8,128)(2,1)}, u32[]{:S(2)}, u32[]{:S(2)}) collective-permute-start(bf16[128,2048]{1,0:T(8,128)(2,1)} %get-tuple-element.61), channel_id=1, source_target_pairs={{0,6},{2,4},{4,2},{6,0},{1,7},{3,5},{5,3},{7,1},{8,14},{10,12},{12... | collective-permute-start | bytes 1572872 | tf_op jit(solution)/shard_map/ppermute | solution.py:60
  105.3 0.8 copy-done.12
  106.1 0.8 copy-done.14
  106.9 0.8 copy-done.16
  107.7 10.2 %cotangent_product.1.base_ref = f32[1024,1024]{1,0:T(8,128)} custom-call(s32[59]{0:T(128)} %concatenate.6.at_ref, bf16[1024,2048]{1,0:T(8,128)(2,1)} %w_ref.5, bf16[128,2048]{1,0:T(8,128)(2,1)} %rest_2_.1, bf16[128,2048]{1,0:T(8,128)(2,1)} %copy-done.6, bf16[128,2048]{1,0:T(8,128)(2,1)} %copy-done.8, bf16[128,2048]{1,0:T(8,128)(2,1)} %copy-done.10, ...), custom_call_target="tpu_custom_call" | custom-call | flops 1024 | bytes 1024 | tf_op jit(solution)/shard_map/cotangent_product/pallas_call | solution.py:210
  118.0 1.1 collective-permute-done.12.rest_3_
  119.1 2.3 %low_product.1 = bf16[2,4,128,128]{3,2,1,0:T(8,128)(2,1)S(1)} custom-call(s32[59]{0:T(128)S(1)} %copy-done.21, bf16[1024,1024]{1,0:T(8,128)(2,1)S(1)} %copy-done, bf16[4,2048,128]{2,1,0:T(8,128)(2,1)} %all-to-all-done.a_ref), custom_call_target="tpu_custom_call" | custom-call | flops 1024 | bytes 1024 | tf_op jit(solution)/shard_map/low_product/pallas_call | solution.py:171
  121.4 0.1 collective-permute-start.19
  121.5 1.3 collective-permute-done.19
  122.9 1.7 %collective-permute-start.22 = (bf16[4,128,128]{2,1,0:T(8,128)(2,1)S(1)}, bf16[4,128,128]{2,1,0:T(8,128)(2,1)S(1)}, u32[]{:S(2)}, u32[]{:S(2)}) collective-permute-start(bf16[4,128,128]{2,1,0:T(8,128)(2,1)S(1)} %fusion.3), channel_id=1, source_target_pairs={{0,6},{2,4},{4,2},{6,0},{1,7},{3,5},{5,3},{7,1},{8,14},{10,12},{12... | collective-permute-start | bytes 393224 | tf_op jit(solution)/shard_map/ppermute | solution.py:60
  124.6 1.1 collective-permute-start.21
  125.7 0.7 collective-permute-start.20
  126.4 3.8 %collective-permute-done.22 = bf16[4,128,128]{2,1,0:T(8,128)(2,1)S(1)} collective-permute-done((bf16[4,128,128]{2,1,0:T(8,128)(2,1)S(1)}, bf16[4,128,128]{2,1,0:T(8,128)(2,1)S(1)}, u32[]{:S(2)}, u32[]{:S(2)}) %collective-permute-start.22) | collective-permute-done | bytes 131104 | tf_op jit(solution)/shard_map/ppermute | solution.py:60
  130.2 2.0 %collective-permute-done.21 = bf16[4,128,128]{2,1,0:T(8,128)(2,1)S(1)} collective-permute-done((bf16[4,128,128]{2,1,0:T(8,128)(2,1)S(1)}, bf16[4,128,128]{2,1,0:T(8,128)(2,1)S(1)}, u32[]{:S(2)}, u32[]{:S(2)}) %collective-permute-start.21) | collective-permute-done | bytes 131104 | tf_op jit(solution)/shard_map/ppermute | solution.py:60
  132.2 0.0 collective-permute-done.20
  132.2 0.1 add_convert_fusion.low_ref.rest_0_
  132.3 0.2 collective-permute-start.23
  132.5 1.2 collective-permute-done.23.rest_1_
  133.8 1.9 %grad_up_pieces.1 = bf16[4,8,16,256]{3,2,1,0:T(8,128)(2,1)S(1)} custom-call(s32[59]{0:T(128)S(1)} %copy-done.21, bf16[4,128,128]{2,1,0:T(8,128)(2,1)S(1)} %add_convert_fusion.low_ref.rest_0_, bf16[4,128,128]{2,1,0:T(8,128)(2,1)S(1)} %collective-permute-done.23.rest_1_, bf16[128,2048]{1,0:T(8,128)(2,1)S(1)} %copy-done.4, bf16[128,2048]{1,0:T(8,128)(2,1)S(1)} %copy-done.7, ...), custom_call_target="tpu_custom_call" | custom-call | flops 1024 | bytes 1024 | tf_op jit(solution)/shard_map/grad_up_pieces/pallas_call | solution.py:400
  135.7 1.7 %collective-permute-start.24 = (bf16[8,16,256]{2,1,0:T(8,128)(2,1)S(1)}, bf16[8,16,256]{2,1,0:T(8,128)(2,1)S(1)}, u32[]{:S(2)}, u32[]{:S(2)}) collective-permute-start(bf16[8,16,256]{2,1,0:T(8,128)(2,1)S(1)} %get-tuple-element.66), channel_id=1, source_target_pairs={{0,8},{8,16},{16,24},{24,0},{1,9},{9,17},{17,25},{25,1},{2,10},{10... | collective-permute-start | bytes 196616 | tf_op jit(solution)/shard_map/ppermute | solution.py:39
  137.4 2.4 %collective-permute-start.25 = (bf16[8,16,256]{2,1,0:T(8,128)(2,1)S(1)}, bf16[8,16,256]{2,1,0:T(8,128)(2,1)S(1)}, u32[]{:S(2)}, u32[]{:S(2)}) collective-permute-start(bf16[8,16,256]{2,1,0:T(8,128)(2,1)S(1)} %get-tuple-element.65), channel_id=1, source_target_pairs={{0,16},{8,24},{16,0},{24,8},{1,17},{9,25},{17,1},{25,9},{2,18},{10... | collective-permute-start | bytes 196616 | tf_op jit(solution)/shard_map/ppermute | solution.py:39
  139.8 1.5 collective-permute-start.26
  141.3 4.5 %input_gradient.1 = bf16[1024,1024]{1,0:T(8,128)(2,1)} custom-call(s32[59]{0:T(128)S(1)} %copy-done.21, f32[1024,1024]{1,0:T(8,128)S(1)} %copy-done.1, bf16[4,2048,128]{2,1,0:T(8,128)(2,1)} %all-to-all-done.a_ref, bf16[4,128,128]{2,1,0:T(8,128)(2,1)S(1)} %pad_maximum_fusion.rest_0_, bf16[4,128,128]{2,1,0:T(8,128)(2,1)S(1)} %collective-permute-done.8.rest_1_), custom_call_target="tpu_custom_call" | custom-call | flops 1024 | bytes 1024 | tf_op jit(solution)/shard_map/input_gradient/pallas_call | solution.py:252
  145.8 2.6 %keys_and_values.1 = bf16[128,2048]{1,0:T(8,128)(2,1)} custom-call(s32[59]{0:T(128)S(1)} %copy-done.21, bf16[4,128,128]{2,1,0:T(8,128)(2,1)S(1)} %add_convert_fusion.low_ref.rest_0_, bf16[64,2048]{1,0:T(8,128)(2,1)S(1)} %copy-done.19, f32[128,2048]{1,0:T(8,128)S(1)} %copy-done.5, bf16[128,2048]{1,0:T(8,128)(2,1)} %collective-permute-done.10.rest_1_, ...), custom_call_target="tpu_custom_call" | custom-call | flops 1024 | bytes 1024 | tf_op jit(solution)/shard_map/keys_and_values/pallas_call | solution.py:486
  148.4 4.3 %grad_down.1 = f32[24,256,128]{2,1,0:T(8,128)} custom-call(s32[59]{0:T(128)} %concatenate.6.at_ref, bf16[4,8,256,128]{3,2,1,0:T(8,128)(2,1)} %all-to-all-done.1.piece_ref), custom_call_target="tpu_custom_call" | custom-call | flops 1024 | bytes 1024 | tf_op jit(solution)/shard_map/grad_down/pallas_call | solution.py:338
  152.7 1.5 grad_up.1
  (70 shorter events, 0.3 us)
Async XLA Ops:
  0.6 17.3 %copy-start.24 = (s32[32]{0:T(128)S(1)}, s32[32]{0:T(128)}, u32[]{:S(2)}) copy-start(s32[32]{0:T(128)} %tenant_ref.1) | copy-start | bytes 388
  0.6 17.3 %copy-start.25 = (s32[24]{0:T(128)S(1)}, s32[24]{0:T(128)}, u32[]{:S(2)}) copy-start(s32[24]{0:T(128)} %slot_ref.1) | copy-start | bytes 292
  0.7 12.1 %copy-start.3 = (bf16[128,2048]{1,0:T(8,128)(2,1)S(1)}, bf16[128,2048]{1,0:T(8,128)(2,1)}, u32[]{:S(2)}) copy-start(bf16[128,2048]{1,0:T(8,128)(2,1)} %rest_2_.1) | copy-start | bytes 1572868
  5.7 8.5 %collective-permute-start = (bf16[16,2048]{1,0:T(8,128)(2,1)}, bf16[16,2048]{1,0:T(8,128)(2,1)S(1)}, u32[]{:S(2)}, u32[]{:S(2)}) collective-permute-start(bf16[16,2048]{1,0:T(8,128)(2,1)} %get-tuple-element.34), channel_id=1, source_target_pairs={{0,8},{8,16},{16,24},{24,0},{1,9},{9,17},{17,25},{25,1},{2,10},{10... | collective-permute-start | bytes 196616 | tf_op jit(solution)/shard_map/ppermute | solution.py:39
  8.8 7.3 %collective-permute-start.1 = (bf16[16,2048]{1,0:T(8,128)(2,1)}, bf16[16,2048]{1,0:T(8,128)(2,1)S(1)}, u32[]{:S(2)}, u32[]{:S(2)}) collective-permute-start(bf16[16,2048]{1,0:T(8,128)(2,1)} %get-tuple-element.35), channel_id=1, source_target_pairs={{0,16},{8,24},{16,0},{24,8},{1,17},{9,25},{17,1},{25,9},{2,18},{10... | collective-permute-start | bytes 196616 | tf_op jit(solution)/shard_map/ppermute | solution.py:39
  11.4 4.9 %collective-permute-start.2 = (bf16[16,2048]{1,0:T(8,128)(2,1)}, bf16[16,2048]{1,0:T(8,128)(2,1)S(1)}, u32[]{:S(2)}, u32[]{:S(2)}) collective-permute-start(bf16[16,2048]{1,0:T(8,128)(2,1)} %get-tuple-element.36), channel_id=1, source_target_pairs={{0,24},{8,0},{16,8},{24,16},{1,25},{9,1},{17,9},{25,17},{2,26},{10... | collective-permute-start | bytes 196616 | tf_op jit(solution)/shard_map/ppermute | solution.py:39
  12.8 12.8 %collective-permute-start.3 = (bf16[128,2048]{1,0:T(8,128)(2,1)S(1)}, bf16[128,2048]{1,0:T(8,128)(2,1)S(1)}, u32[]{:S(2)}, u32[]{:S(2)}) collective-permute-start(bf16[128,2048]{1,0:T(8,128)(2,1)S(1)} %copy-done.3), channel_id=1, source_target_pairs={{0,2},{2,0},{4,6},{6,4},{1,3},{3,1},{5,7},{7,5},{8,10},{10,8},{12,... | collective-permute-start | bytes 1572872 | tf_op jit(solution)/shard_map/ppermute | solution.py:60
  16.3 13.4 %collective-permute-start.4 = (bf16[128,2048]{1,0:T(8,128)(2,1)S(1)}, bf16[128,2048]{1,0:T(8,128)(2,1)S(1)}, u32[]{:S(2)}, u32[]{:S(2)}) collective-permute-start(bf16[128,2048]{1,0:T(8,128)(2,1)S(1)} %copy-done.3), channel_id=1, source_target_pairs={{0,4},{2,6},{4,0},{6,2},{1,5},{3,7},{5,1},{7,3},{8,12},{10,14},{12... | collective-permute-start | bytes 1572872 | tf_op jit(solution)/shard_map/ppermute | solution.py:60
  25.6 71.6 %copy-start.6 = (bf16[128,2048]{1,0:T(8,128)(2,1)}, bf16[128,2048]{1,0:T(8,128)(2,1)S(1)}, u32[]{:S(2)}) copy-start(bf16[128,2048]{1,0:T(8,128)(2,1)S(1)} %collective-permute-done.3.rest_1_.rest_3_) | copy-start | bytes 1572868
  29.7 6.0 %copy-start.8 = (bf16[128,2048]{1,0:T(8,128)(2,1)}, bf16[128,2048]{1,0:T(8,128)(2,1)S(1)}, u32[]{:S(2)}) copy-start(bf16[128,2048]{1,0:T(8,128)(2,1)S(1)} %collective-permute-done.4.rest_2_.rest_4_) | copy-start | bytes 1572868
  35.8 10.6 %collective-permute-start.9 = (bf16[4,128,2048]{2,1,0:T(8,128)(2,1)}, bf16[4,128,2048]{2,1,0:T(8,128)(2,1)}, u32[]{:S(2)}, u32[]{:S(2)}) collective-permute-start(bf16[4,128,2048]{2,1,0:T(8,128)(2,1)} %bitcast.71), channel_id=1, source_target_pairs={{0,1},{1,0},{2,3},{3,2},{4,5},{5,4},{6,7},{7,6},{8,9},{9,8},{10,11... | collective-permute-start | bytes 6291464 | tf_op jit(solution)/shard_map/ppermute | solution.py:60
  35.8 53.7 %all-to-all-start = ((bf16[4,2048,128]{2,1,0:T(8,128)(2,1)}), bf16[4,2048,128]{2,1,0:T(8,128)(2,1)}, u32[]{:S(2)}, u32[]{:S(2)}) async-start(bf16[4,2048,128]{2,1,0:T(8,128)(2,1)} %get-tuple-element.37), calls=%async_computation | async-start | bytes 4194304 | tf_op jit(solution)/shard_map/all_to_all | solution.py:523
  46.3 6.5 %copy-start.20 = (s32[59]{0:T(128)S(1)}, s32[59]{0:T(128)}, u32[]{:S(2)}) copy-start(s32[59]{0:T(128)} %concatenate.6.at_ref) | copy-start | bytes 712
  46.3 6.5 %copy-start.23 = (bf16[16,2048]{1,0:T(8,128)(2,1)S(1)}, bf16[16,2048]{1,0:T(8,128)(2,1)}, u32[]{:S(2)}) copy-start(bf16[16,2048]{1,0:T(8,128)(2,1)} %get-tuple-element.33.rest_0_) | copy-start | bytes 196612
  46.4 20.9 %copy-start = (bf16[1024,1024]{1,0:T(8,128)(2,1)S(1)}, bf16[1024,1024]{1,0:T(8,128)(2,1)}, u32[]{:S(2)}) copy-start(bf16[1024,1024]{1,0:T(8,128)(2,1)} %x_ref.1) | copy-start | bytes 6291460
  50.7 38.7 %collective-permute-start.10 = (bf16[128,2048]{1,0:T(8,128)(2,1)}, bf16[128,2048]{1,0:T(8,128)(2,1)}, u32[]{:S(2)}, u32[]{:S(2)}) collective-permute-start(bf16[128,2048]{1,0:T(8,128)(2,1)} %get-tuple-element.63), channel_id=1, source_target_pairs={{0,2},{2,0},{4,6},{6,4},{1,3},{3,1},{5,7},{7,5},{8,10},{10,8},{12,... | collective-permute-start | bytes 1572872 | tf_op jit(solution)/shard_map/ppermute | solution.py:60
  51.4 38.0 %collective-permute-start.11 = (bf16[128,2048]{1,0:T(8,128)(2,1)}, bf16[128,2048]{1,0:T(8,128)(2,1)}, u32[]{:S(2)}, u32[]{:S(2)}) collective-permute-start(bf16[128,2048]{1,0:T(8,128)(2,1)} %get-tuple-element.62), channel_id=1, source_target_pairs={{0,4},{2,6},{4,0},{6,2},{1,5},{3,7},{5,1},{7,3},{8,12},{10,14},{12... | collective-permute-start | bytes 1572872 | tf_op jit(solution)/shard_map/ppermute | solution.py:60
  53.8 0.7 copy-start.18
  54.5 12.2 %collective-permute-start.7 = (bf16[128,128]{1,0:T(8,128)(2,1)S(1)}, bf16[128,128]{1,0:T(8,128)(2,1)S(1)}, u32[]{:S(2)}, u32[]{:S(2)}) collective-permute-start(bf16[128,128]{1,0:T(8,128)(2,1)S(1)} %get-tuple-element.41), channel_id=1, source_target_pairs={{0,6},{2,4},{4,2},{6,0},{1,7},{3,5},{5,3},{7,1},{8,14},{10,12},{12... | collective-permute-start | bytes 98312 | tf_op jit(solution)/shard_map/ppermute | solution.py:60
  55.8 11.3 %collective-permute-start.6 = (bf16[128,128]{1,0:T(8,128)(2,1)S(1)}, bf16[128,128]{1,0:T(8,128)(2,1)S(1)}, u32[]{:S(2)}, u32[]{:S(2)}) collective-permute-start(bf16[128,128]{1,0:T(8,128)(2,1)S(1)} %get-tuple-element.41), channel_id=1, source_target_pairs={{0,4},{2,6},{4,0},{6,2},{1,5},{3,7},{5,1},{7,3},{8,12},{10,14},{12... | collective-permute-start | bytes 98312 | tf_op jit(solution)/shard_map/ppermute | solution.py:60
  56.7 10.4 %collective-permute-start.5 = (bf16[128,128]{1,0:T(8,128)(2,1)S(1)}, bf16[128,128]{1,0:T(8,128)(2,1)S(1)}, u32[]{:S(2)}, u32[]{:S(2)}) collective-permute-start(bf16[128,128]{1,0:T(8,128)(2,1)S(1)} %get-tuple-element.41), channel_id=1, source_target_pairs={{0,2},{2,0},{4,6},{6,4},{1,3},{3,1},{5,7},{7,5},{8,10},{10,8},{12,... | collective-permute-start | bytes 98312 | tf_op jit(solution)/shard_map/ppermute | solution.py:60
  67.1 2.7 %collective-permute-start.8 = (bf16[4,128,128]{2,1,0:T(8,128)(2,1)S(1)}, bf16[4,128,128]{2,1,0:T(8,128)(2,1)S(1)}, u32[]{:S(2)}, u32[]{:S(2)}) collective-permute-start(bf16[4,128,128]{2,1,0:T(8,128)(2,1)S(1)} %pad_maximum_fusion.rest_0_), channel_id=1, source_target_pairs={{0,1},{1,0},{2,3},{3,2},{4,5},{5,4},{6,7},{7,6},{8,9},{9,8},{10,11... | collective-permute-start | bytes 393224 | tf_op jit(solution)/shard_map/ppermute | solution.py:60
  69.8 1.6 %copy-start.2 = (bf16[1024,1024]{1,0:T(8,128)(2,1)S(1)}, bf16[1024,1024]{1,0:T(8,128)(2,1)}, u32[]{:S(2)}) copy-start(bf16[1024,1024]{1,0:T(8,128)(2,1)} %copy.11) | copy-start | bytes 6291460
  89.5 58.9 %all-to-all-start.1 = ((bf16[4,8,256,128]{3,2,1,0:T(8,128)(2,1)}), bf16[4,8,256,128]{3,2,1,0:T(8,128)(2,1)}, u32[]{:S(2)}, u32[]{:S(2)}) async-start(bf16[4,8,256,128]{3,2,1,0:T(8,128)(2,1)} %grad_down_pieces.1), calls=%async_computation.1 | async-start | bytes 4194304 | tf_op jit(solution)/shard_map/all_to_all | solution.py:553
  94.9 8.0 %collective-permute-start.13 = (bf16[64,2048]{1,0:T(8,128)(2,1)S(1)}, bf16[64,2048]{1,0:T(8,128)(2,1)S(1)}, u32[]{:S(2)}, u32[]{:S(2)}) collective-permute-start(bf16[64,2048]{1,0:T(8,128)(2,1)S(1)} %slice.58), channel_id=1, source_target_pairs={{0,2},{2,0},{4,6},{6,4},{1,3},{3,1},{5,7},{7,5},{8,10},{10,8},{12,... | collective-permute-start | bytes 786440 | tf_op jit(solution)/shard_map/ppermute | solution.py:60
  95.7 7.7 %collective-permute-start.14 = (bf16[64,2048]{1,0:T(8,128)(2,1)S(1)}, bf16[64,2048]{1,0:T(8,128)(2,1)S(1)}, u32[]{:S(2)}, u32[]{:S(2)}) collective-permute-start(bf16[64,2048]{1,0:T(8,128)(2,1)S(1)} %slice.59), channel_id=1, source_target_pairs={{0,4},{2,6},{4,0},{6,2},{1,5},{3,7},{5,1},{7,3},{8,12},{10,14},{12... | collective-permute-start | bytes 786440 | tf_op jit(solution)/shard_map/ppermute | solution.py:60
  97.2 8.0 %collective-permute-start.15 = (bf16[128,2048]{1,0:T(8,128)(2,1)S(1)}, bf16[128,2048]{1,0:T(8,128)(2,1)S(1)}, u32[]{:S(2)}, u32[]{:S(2)}) collective-permute-start(bf16[128,2048]{1,0:T(8,128)(2,1)S(1)} %copy-done.3), channel_id=1, source_target_pairs={{0,1},{1,0},{2,3},{3,2},{4,5},{5,4},{6,7},{7,6},{8,9},{9,8},{10,11... | collective-permute-start | bytes 1572872 | tf_op jit(solution)/shard_map/ppermute | solution.py:60
  97.2 8.0 %collective-permute-start.16 = (bf16[128,2048]{1,0:T(8,128)(2,1)S(1)}, bf16[128,2048]{1,0:T(8,128)(2,1)S(1)}, u32[]{:S(2)}, u32[]{:S(2)}) collective-permute-start(bf16[128,2048]{1,0:T(8,128)(2,1)S(1)} %collective-permute-done.3.rest_1_.rest_3_), channel_id=1, source_target_pairs={{0,1},{1,0},{2,3},{3,2},{4,5},{5,4},{6,7},{7,6},{8,9},{9,8},{10,11... | collective-permute-start | bytes 1572872 | tf_op jit(solution)/shard_map/ppermute | solution.py:60
  97.7 8.3 %collective-permute-start.17 = (bf16[128,2048]{1,0:T(8,128)(2,1)}, bf16[128,2048]{1,0:T(8,128)(2,1)S(1)}, u32[]{:S(2)}, u32[]{:S(2)}) collective-permute-start(bf16[128,2048]{1,0:T(8,128)(2,1)} %copy-done.8), channel_id=1, source_target_pairs={{0,1},{1,0},{2,3},{3,2},{4,5},{5,4},{6,7},{7,6},{8,9},{9,8},{10,11... | collective-permute-start | bytes 1572872 | tf_op jit(solution)/shard_map/ppermute | solution.py:60
  103.5 4.2 %copy-start.10 = (bf16[128,2048]{1,0:T(8,128)(2,1)}, bf16[128,2048]{1,0:T(8,128)(2,1)S(1)}, u32[]{:S(2)}) copy-start(bf16[128,2048]{1,0:T(8,128)(2,1)S(1)} %constant_dynamic-update-slice_fusion.rest_3_.rest_5_) | copy-start | bytes 1572868
  103.5 4.2 %collective-permute-start.18 = (bf16[128,2048]{1,0:T(8,128)(2,1)S(1)}, bf16[128,2048]{1,0:T(8,128)(2,1)}, u32[]{:S(2)}, u32[]{:S(2)}) collective-permute-start(bf16[128,2048]{1,0:T(8,128)(2,1)S(1)} %constant_dynamic-update-slice_fusion.rest_3_.rest_5_), channel_id=1, source_target_pairs={{0,1},{1,0},{2,3},{3,2},{4,5},{5,4},{6,7},{7,6},{8,9},{9,8},{10,11... | collective-permute-start | bytes 1572872 | tf_op jit(solution)/shard_map/ppermute | solution.py:60
  103.6 15.6 %copy-start.21 = (s32[59]{0:T(128)S(1)}, s32[59]{0:T(128)}, u32[]{:S(2)}) copy-start(s32[59]{0:T(128)} %concatenate.6.at_ref) | copy-start | bytes 712
  103.6 15.5 %collective-permute-start.12 = (bf16[128,2048]{1,0:T(8,128)(2,1)}, bf16[128,2048]{1,0:T(8,128)(2,1)}, u32[]{:S(2)}, u32[]{:S(2)}) collective-permute-start(bf16[128,2048]{1,0:T(8,128)(2,1)} %get-tuple-element.61), channel_id=1, source_target_pairs={{0,6},{2,4},{4,2},{6,0},{1,7},{3,5},{5,3},{7,1},{8,14},{10,12},{12... | collective-permute-start | bytes 1572872 | tf_op jit(solution)/shard_map/ppermute | solution.py:60
  105.3 0.8 copy-start.12
  106.1 0.8 copy-start.14
  106.9 0.8 copy-start.16
  117.9 15.8 %copy-start.4 = (bf16[128,2048]{1,0:T(8,128)(2,1)S(1)}, bf16[128,2048]{1,0:T(8,128)(2,1)}, u32[]{:S(2)}) copy-start(bf16[128,2048]{1,0:T(8,128)(2,1)} %rest_2_.1) | copy-start | bytes 1572868
  117.9 15.8 %copy-start.7 = (bf16[128,2048]{1,0:T(8,128)(2,1)S(1)}, bf16[128,2048]{1,0:T(8,128)(2,1)}, u32[]{:S(2)}) copy-start(bf16[128,2048]{1,0:T(8,128)(2,1)} %copy-done.6) | copy-start | bytes 1572868
  117.9 15.8 %copy-start.9 = (bf16[128,2048]{1,0:T(8,128)(2,1)S(1)}, bf16[128,2048]{1,0:T(8,128)(2,1)}, u32[]{:S(2)}) copy-start(bf16[128,2048]{1,0:T(8,128)(2,1)} %copy-done.8) | copy-start | bytes 1572868
  117.9 15.8 %copy-start.11 = (bf16[128,2048]{1,0:T(8,128)(2,1)S(1)}, bf16[128,2048]{1,0:T(8,128)(2,1)}, u32[]{:S(2)}) copy-start(bf16[128,2048]{1,0:T(8,128)(2,1)} %copy-done.10) | copy-start | bytes 1572868
  118.0 15.8 %copy-start.13 = (bf16[128,2048]{1,0:T(8,128)(2,1)S(1)}, bf16[128,2048]{1,0:T(8,128)(2,1)}, u32[]{:S(2)}) copy-start(bf16[128,2048]{1,0:T(8,128)(2,1)} %copy-done.12) | copy-start | bytes 1572868
  118.0 15.8 %copy-start.15 = (bf16[128,2048]{1,0:T(8,128)(2,1)S(1)}, bf16[128,2048]{1,0:T(8,128)(2,1)}, u32[]{:S(2)}) copy-start(bf16[128,2048]{1,0:T(8,128)(2,1)} %copy-done.14) | copy-start | bytes 1572868
  118.0 15.8 %copy-start.17 = (bf16[128,2048]{1,0:T(8,128)(2,1)S(1)}, bf16[128,2048]{1,0:T(8,128)(2,1)}, u32[]{:S(2)}) copy-start(bf16[128,2048]{1,0:T(8,128)(2,1)} %copy-done.16) | copy-start | bytes 1572868
  121.4 1.4 collective-permute-start.19
  122.9 7.3 %collective-permute-start.22 = (bf16[4,128,128]{2,1,0:T(8,128)(2,1)S(1)}, bf16[4,128,128]{2,1,0:T(8,128)(2,1)S(1)}, u32[]{:S(2)}, u32[]{:S(2)}) collective-permute-start(bf16[4,128,128]{2,1,0:T(8,128)(2,1)S(1)} %fusion.3), channel_id=1, source_target_pairs={{0,6},{2,4},{4,2},{6,0},{1,7},{3,5},{5,3},{7,1},{8,14},{10,12},{12... | collective-permute-start | bytes 393224 | tf_op jit(solution)/shard_map/ppermute | solution.py:60
  124.6 7.6 %collective-permute-start.21 = (bf16[4,128,128]{2,1,0:T(8,128)(2,1)S(1)}, bf16[4,128,128]{2,1,0:T(8,128)(2,1)S(1)}, u32[]{:S(2)}, u32[]{:S(2)}) collective-permute-start(bf16[4,128,128]{2,1,0:T(8,128)(2,1)S(1)} %fusion.3), channel_id=1, source_target_pairs={{0,4},{2,6},{4,0},{6,2},{1,5},{3,7},{5,1},{7,3},{8,12},{10,14},{12... | collective-permute-start | bytes 393224 | tf_op jit(solution)/shard_map/ppermute | solution.py:60
  125.7 6.5 %collective-permute-start.20 = (bf16[4,128,128]{2,1,0:T(8,128)(2,1)S(1)}, bf16[4,128,128]{2,1,0:T(8,128)(2,1)S(1)}, u32[]{:S(2)}, u32[]{:S(2)}) collective-permute-start(bf16[4,128,128]{2,1,0:T(8,128)(2,1)S(1)} %fusion.3), channel_id=1, source_target_pairs={{0,2},{2,0},{4,6},{6,4},{1,3},{3,1},{5,7},{7,5},{8,10},{10,8},{12,... | collective-permute-start | bytes 393224 | tf_op jit(solution)/shard_map/ppermute | solution.py:60
  132.3 9.0 %copy-start.1 = (f32[1024,1024]{1,0:T(8,128)S(1)}, f32[1024,1024]{1,0:T(8,128)}, u32[]{:S(2)}) copy-start(f32[1024,1024]{1,0:T(8,128)} %cotangent_product.1.base_ref) | copy-start | bytes 12582916
  132.3 1.4 collective-permute-start.23
  135.7 16.9 %collective-permute-start.24 = (bf16[8,16,256]{2,1,0:T(8,128)(2,1)S(1)}, bf16[8,16,256]{2,1,0:T(8,128)(2,1)S(1)}, u32[]{:S(2)}, u32[]{:S(2)}) collective-permute-start(bf16[8,16,256]{2,1,0:T(8,128)(2,1)S(1)} %get-tuple-element.66), channel_id=1, source_target_pairs={{0,8},{8,16},{16,24},{24,0},{1,9},{9,17},{17,25},{25,1},{2,10},{10... | collective-permute-start | bytes 196616 | tf_op jit(solution)/shard_map/ppermute | solution.py:39
  137.4 15.2 %collective-permute-start.25 = (bf16[8,16,256]{2,1,0:T(8,128)(2,1)S(1)}, bf16[8,16,256]{2,1,0:T(8,128)(2,1)S(1)}, u32[]{:S(2)}, u32[]{:S(2)}) collective-permute-start(bf16[8,16,256]{2,1,0:T(8,128)(2,1)S(1)} %get-tuple-element.65), channel_id=1, source_target_pairs={{0,16},{8,24},{16,0},{24,8},{1,17},{9,25},{17,1},{25,9},{2,18},{10... | collective-permute-start | bytes 196616 | tf_op jit(solution)/shard_map/ppermute | solution.py:39
  139.8 6.0 %copy-start.5 = (f32[128,2048]{1,0:T(8,128)S(1)}, f32[128,2048]{1,0:T(8,128)}, u32[]{:S(2)}) copy-start(f32[128,2048]{1,0:T(8,128)} %get-tuple-element.60.rest_0_) | copy-start | bytes 3145732
  139.8 6.0 %copy-start.19 = (bf16[64,2048]{1,0:T(8,128)(2,1)S(1)}, bf16[64,2048]{1,0:T(8,128)(2,1)}, u32[]{:S(2)}) copy-start(bf16[64,2048]{1,0:T(8,128)(2,1)} %copy-done.18) | copy-start | bytes 786436
  139.8 12.8 %collective-permute-start.26 = (bf16[8,16,256]{2,1,0:T(8,128)(2,1)S(1)}, bf16[8,16,256]{2,1,0:T(8,128)(2,1)S(1)}, u32[]{:S(2)}, u32[]{:S(2)}) collective-permute-start(bf16[8,16,256]{2,1,0:T(8,128)(2,1)S(1)} %get-tuple-element.64), channel_id=1, source_target_pairs={{0,24},{8,0},{16,8},{24,16},{1,25},{9,1},{17,9},{25,17},{2,26},{10... | collective-permute-start | bytes 196616 | tf_op jit(solution)/shard_map/ppermute | solution.py:39
  148.4 4.3 %copy-start.22 = (s32[59]{0:T(128)S(1)}, s32[59]{0:T(128)}, u32[]{:S(2)}) copy-start(s32[59]{0:T(128)} %concatenate.6.at_ref) | copy-start | bytes 712

commit v15 on v13

--- a/solution.py
+++ b/solution.py
@@ -517,7 +517,7 @@
     b_came = [b_send[0]] + [shift(b_send[k], "dp", k) for k in range(1, data_count)]
     b_own, grad_rows = own_rows(at, b_came, cotangent)
 
-    a_send, b_came = lax.optimization_barrier((a_send, b_came))
+    a_send, grad_rows = lax.optimization_barrier((a_send, grad_rows))
     a_recv = lax.all_to_all(a_send, "dp", 0, 0, tiled=True)
 
     behind, a_send = lax.optimization_barrier((tokens, a_send))

time: 143 us -> 145 us (1.014)
  transfers between devices with their start and end apart: 29 -> 29, of which waited for: 11 -> 10; matrix products, arithmetic and copies ran while one was open for 6% -> 6% of each run, Pallas kernels for 25% -> 25%
where the time goes in v15:
time: 145 us; the launch traced here: 144 us
  waiting for transfers between devices  44.9 us (31%)
  Pallas kernels  41.6 us (29%)
  starting transfers between devices  36.6 us (25%)
  local copies, waits for them, and re-layouts  15.8 us (11%)
  other arithmetic  3.74 us (3%)
    ppermute x21, waiting for transfers between devices, swap(): lax.ppermute(piece, axis, [(i, partner(i, k, count)) for i in range(count)])  26.7 us
    ppermute x21, starting transfers between devices, swap(): lax.ppermute(piece, axis, [(i, partner(i, k, count)) for i in range(count)])  17.6 us
    unnamed x39, local copies, waits for them, and re-layouts  11.4 us
    ppermute x6, starting transfers between devices, shift(): lax.ppermute(piece, axis, [(i, (i + k) % count) for i in range(count)])  10.2 us
    all_to_all x1, waiting for transfers between devices, body(): down_recv = lax.all_to_all(down_send, 'dp', 0, 0, tiled=True)  10 us
    pallas_call x2, Pallas kernels, base_product(): call(kernel, 'base_product', grid_spec=pltpu.PrefetchScalarGridSpec(num_s...  8.03 us
    pallas_call x1, Pallas kernels, cotangent_product(): call(kernel, 'cotangent_product', grid=(depth // tile,), in_specs=[SMEM,...  7.96 us
    pallas_call x1, Pallas kernels, pick(): call(kernel, 'pick_rows', VMEM_MOST, out_shape=(up_shape,) * data_count +...  4.76 us
  transfers between devices with their start and end apart: 29, of which 10 were waited for; matrix products, arithmetic and copies ran while one was open for 6% of the time, Pallas kernels for 25%

profile of v15, /device:TPU:0, one launch (start us, length us, event | category | flops | bytes accessed | tf_op | source)
XLA Modules:
  0.0 143.6 jit_solution(15615644522055241672)
XLA Ops:
  0.7 3.0 %collective-permute-start.4 = (bf16[128,2048]{1,0:T(8,128)(2,1)}, bf16[128,2048]{1,0:T(8,128)(2,1)S(1)}, u32[]{:S(2)}, u32[]{:S(2)}) collective-permute-start(bf16[128,2048]{1,0:T(8,128)(2,1)} %rest_2_.1), channel_id=1, source_target_pairs={{0,4},{2,6},{4,0},{6,2},{1,5},{3,7},{5,1},{7,3},{8,12},{10,14},{12... | collective-permute-start | bytes 1572872 | tf_op jit(solution)/shard_map/ppermute | solution.py:60
  3.7 1.5 %collective-permute-start.3 = (bf16[128,2048]{1,0:T(8,128)(2,1)}, bf16[128,2048]{1,0:T(8,128)(2,1)}, u32[]{:S(2)}, u32[]{:S(2)}) collective-permute-start(bf16[128,2048]{1,0:T(8,128)(2,1)} %rest_2_.1), channel_id=1, source_target_pairs={{0,2},{2,0},{4,6},{6,4},{1,3},{3,1},{5,7},{7,5},{8,10},{10,8},{12,... | collective-permute-start | bytes 1572872 | tf_op jit(solution)/shard_map/ppermute | solution.py:60
  5.2 4.8 %pick_rows.1 = (bf16[16,2048]{1,0:T(8,128)(2,1)}, bf16[16,2048]{1,0:T(8,128)(2,1)}, bf16[16,2048]{1,0:T(8,128)(2,1)}, bf16[16,2048]{1,0:T(8,128)(2,1)}, bf16[4,2048,128]{2,1,0:T(8,128)(2,1)}) custom-call(s32[32]{0:T(128)} %tenant_ref.1, s32[24]{0:T(128)} %slot_ref.1, bf16[24,256,128]{2,1,0:T(8,128)(2,1)} %down_ref.1, bf16[24,16,2048]{2,1,0:T(8,128)(2,1)} %up_ref.1), custom_call_target="tpu_custom_call" | custom-call | flops 1024 | bytes 1024 | tf_op jit(solution)/shard_map/pick_rows/pallas_call | solution.py:108
  10.0 1.6 %collective-permute-start = (bf16[16,2048]{1,0:T(8,128)(2,1)}, bf16[16,2048]{1,0:T(8,128)(2,1)S(1)}, u32[]{:S(2)}, u32[]{:S(2)}) collective-permute-start(bf16[16,2048]{1,0:T(8,128)(2,1)} %get-tuple-element.34), channel_id=1, source_target_pairs={{0,8},{8,16},{16,24},{24,0},{1,9},{9,17},{17,25},{25,1},{2,10},{10... | collective-permute-start | bytes 196616 | tf_op jit(solution)/shard_map/ppermute | solution.py:39
  11.6 2.6 %collective-permute-start.1 = (bf16[16,2048]{1,0:T(8,128)(2,1)}, bf16[16,2048]{1,0:T(8,128)(2,1)S(1)}, u32[]{:S(2)}, u32[]{:S(2)}) collective-permute-start(bf16[16,2048]{1,0:T(8,128)(2,1)} %get-tuple-element.35), channel_id=1, source_target_pairs={{0,16},{8,24},{16,0},{24,8},{1,17},{9,25},{17,1},{25,9},{2,18},{10... | collective-permute-start | bytes 196616 | tf_op jit(solution)/shard_map/ppermute | solution.py:39
  14.2 1.4 collective-permute-start.2
  15.5 0.1 concatenate.6.at_ref
  15.6 1.4 collective-permute-done.rest_1_
  17.0 2.0 %collective-permute-done.1.rest_2_ = bf16[16,2048]{1,0:T(8,128)(2,1)S(1)} collective-permute-done((bf16[16,2048]{1,0:T(8,128)(2,1)}, bf16[16,2048]{1,0:T(8,128)(2,1)S(1)}, u32[]{:S(2)}, u32[]{:S(2)}) %collective-permute-start.1) | collective-permute-done | bytes 65568 | tf_op jit(solution)/shard_map/ppermute | solution.py:39
  19.0 0.0 collective-permute-done.2.rest_3_
  19.0 0.8 copy-done.16
  19.9 0.9 own_rows.1
  20.9 2.3 %copy-done = bf16[1024,2048]{1,0:T(8,128)(2,1)S(1)} copy-done((bf16[1024,2048]{1,0:T(8,128)(2,1)S(1)}, bf16[1024,2048]{1,0:T(8,128)(2,1)}, u32[]{:S(2)}) %copy-start) | copy-done | bytes 4194328
  23.1 4.4 %base_product.3 = bf16[1,4,128,2048]{3,2,1,0:T(8,128)(2,1)} custom-call(s32[59]{0:T(128)S(1)} %concatenate.6.at_ref, bf16[4,2,128,1024]{3,2,1,0:T(8,128)(2,1)S(1)} %bitcast.66, bf16[1024,2048]{1,0:T(8,128)(2,1)S(1)} %copy-done), custom_call_target="tpu_custom_call" | custom-call | flops 1024 | bytes 1024 | tf_op jit(solution)/shard_map/base_product/pallas_call | solution.py:136
  27.5 4.4 %all-to-all-start = ((bf16[4,2048,128]{2,1,0:T(8,128)(2,1)}), bf16[4,2048,128]{2,1,0:T(8,128)(2,1)}, u32[]{:S(2)}, u32[]{:S(2)}) async-start(bf16[4,2048,128]{2,1,0:T(8,128)(2,1)} %get-tuple-element.38), calls=%async_computation | async-start | bytes 4194304 | tf_op jit(solution)/shard_map/all_to_all | solution.py:521
  32.0 0.6 collective-permute-start.9
  32.6 1.4 collective-permute-start.7
  34.0 1.5 %collective-permute-start.6 = (bf16[128,128]{1,0:T(8,128)(2,1)S(1)}, bf16[128,128]{1,0:T(8,128)(2,1)S(1)}, u32[]{:S(2)}, u32[]{:S(2)}) collective-permute-start(bf16[128,128]{1,0:T(8,128)(2,1)S(1)} %get-tuple-element.41), channel_id=1, source_target_pairs={{0,4},{2,6},{4,0},{6,2},{1,5},{3,7},{5,1},{7,3},{8,12},{10,14},{12... | collective-permute-start | bytes 98312 | tf_op jit(solution)/shard_map/ppermute | solution.py:60
  35.6 0.6 collective-permute-start.5
  36.1 1.0 slice.53
  37.1 4.7 %collective-permute-done.7 = bf16[128,128]{1,0:T(8,128)(2,1)S(1)} collective-permute-done((bf16[128,128]{1,0:T(8,128)(2,1)S(1)}, bf16[128,128]{1,0:T(8,128)(2,1)S(1)}, u32[]{:S(2)}, u32[]{:S(2)}) %collective-permute-start.7) | collective-permute-done | bytes 32800 | tf_op jit(solution)/shard_map/ppermute | solution.py:60
  41.8 1.5 %collective-permute-start.10 = (bf16[64,2048]{1,0:T(8,128)(2,1)S(1)}, bf16[64,2048]{1,0:T(8,128)(2,1)S(1)}, u32[]{:S(2)}, u32[]{:S(2)}) collective-permute-start(bf16[64,2048]{1,0:T(8,128)(2,1)S(1)} %slice.53), channel_id=1, source_target_pairs={{0,4},{2,6},{4,0},{6,2},{1,5},{3,7},{5,1},{7,3},{8,12},{10,14},{12... | collective-permute-start | bytes 786440 | tf_op jit(solution)/shard_map/ppermute | solution.py:60
  43.3 0.3 collective-permute-start.8
  43.6 2.2 %copy-done.1 = bf16[1024,2048]{1,0:T(8,128)(2,1)S(1)} copy-done((bf16[1024,2048]{1,0:T(8,128)(2,1)S(1)}, bf16[1024,2048]{1,0:T(8,128)(2,1)}, u32[]{:S(2)}) %copy-start.1) | copy-done | bytes 4194328
  45.8 3.6 %base_product.2 = bf16[1,4,128,2048]{3,2,1,0:T(8,128)(2,1)S(1)} custom-call(s32[59]{0:T(128)S(1)} %concatenate.6.at_ref, bf16[4,2,128,1024]{3,2,1,0:T(8,128)(2,1)S(1)} %bitcast.67, bf16[1024,2048]{1,0:T(8,128)(2,1)S(1)} %copy-done.1), custom_call_target="tpu_custom_call" | custom-call | flops 1024 | bytes 1024 | tf_op jit(solution)/shard_map/base_product/pallas_call | solution.py:136
  49.4 0.3 collective-permute-start.12
  49.8 0.7 constant_dynamic-update-slice_fusion.1
  50.5 0.0 collective-permute-done.10
  50.5 0.2 collective-permute-start.13
  50.7 0.7 constant_dynamic-update-slice_fusion.rest_3_.rest_5_
  51.4 0.3 collective-permute-start.14
  51.7 3.6 %convert_add_fusion = (f32[128,2048]{1,0:T(8,128)}, bf16[128,2048]{1,0:T(8,128)(2,1)}, bf16[128,2048]{1,0:T(8,128)(2,1)}, bf16[128,2048]{1,0:T(8,128)(2,1)}) fusion(bf16[4,128,2048]{2,1,0:T(8,128)(2,1)} %collective-permute-done.15, bf16[1,4,128,2048]{3,2,1,0:T(8,128)(2,1)S(1)} %base_product.2), kind=kLoop, calls=%fused_computation | loop fusion | flops 3932160 | bytes 6815744 | tf_op jit(solution)/shard_map/add | solution.py:532
  55.3 1.5 %collective-permute-start.17 = (bf16[128,2048]{1,0:T(8,128)(2,1)}, bf16[128,2048]{1,0:T(8,128)(2,1)}, u32[]{:S(2)}, u32[]{:S(2)}) collective-permute-start(bf16[128,2048]{1,0:T(8,128)(2,1)} %get-tuple-element.62), channel_id=1, source_target_pairs={{0,4},{2,6},{4,0},{6,2},{1,5},{3,7},{5,1},{7,3},{8,12},{10,14},{12... | collective-permute-start | bytes 1572872 | tf_op jit(solution)/shard_map/ppermute | solution.py:60
  56.9 0.8 copy-done.9
  57.7 0.6 collective-permute-start.16
  58.2 2.5 %copy.11 = bf16[1024,1024]{1,0:T(8,128)(2,1)} copy(bf16[1024,1024]{0,1:T(8,128)(2,1)S(1)} %bitcast.68) | data formatting | bytes 4194304 | tf_op jit(solution)/shard_map/transpose | solution.py:545
  60.8 1.6 %copy-done.6 = bf16[1024,1024]{1,0:T(8,128)(2,1)S(1)} copy-done((bf16[1024,1024]{1,0:T(8,128)(2,1)S(1)}, bf16[1024,1024]{1,0:T(8,128)(2,1)}, u32[]{:S(2)}) %copy-start.6) | copy-done | bytes 2097176
  62.4 3.1 %grad_down_pieces.1 = bf16[4,8,256,128]{3,2,1,0:T(8,128)(2,1)} custom-call(s32[59]{0:T(128)S(1)} %concatenate.6.at_ref, bf16[4,256,1024]{2,1,0:T(8,128)(2,1)S(1)} %bitcast.69, bf16[4,128,128]{2,1,0:T(8,128)(2,1)S(1)} %pad_maximum_fusion.rest_0_, bf16[4,128,128]{2,1,0:T(8,128)(2,1)S(1)} %collective-permute-done.8.rest_1_), custom_call_target="tpu_custom_call" | custom-call | flops 1024 | bytes 1024 | tf_op jit(solution)/shard_map/grad_down_pieces/pallas_call | solution.py:290
  65.4 1.0 copy-done.10
  66.5 8.0 %cotangent_product.1.base_ref = f32[1024,1024]{1,0:T(8,128)S(1)} custom-call(s32[59]{0:T(128)S(1)} %concatenate.6.at_ref, bf16[1024,2048]{1,0:T(8,128)(2,1)S(1)} %copy-done.2, bf16[128,2048]{1,0:T(8,128)(2,1)S(1)} %copy-done.7, bf16[128,2048]{1,0:T(8,128)(2,1)} %collective-permute-done.3.rest_1_.rest_3_, ...), custom_call_target="tpu_custom_call" | custom-call | flops 1024 | bytes 1024 | tf_op jit(solution)/shard_map/cotangent_product/pallas_call | solution.py:209
  74.5 2.0 %copy-done.4 = f32[1024,1024]{1,0:T(8,128)} copy-done((f32[1024,1024]{1,0:T(8,128)}, f32[1024,1024]{1,0:T(8,128)S(1)}, u32[]{:S(2)}) %copy-start.4) | copy-done | bytes 4194328
  76.4 4.8 %all-to-all-done.a_ref = bf16[4,2048,128]{2,1,0:T(8,128)(2,1)} async-done(((bf16[4,2048,128]{2,1,0:T(8,128)(2,1)}), bf16[4,2048,128]{2,1,0:T(8,128)(2,1)}, u32[]{:S(2)}, u32[]{:S(2)}) %all-to-all-start) | async-done | bytes 2097184 | tf_op jit(solution)/shard_map/all_to_all | solution.py:521
  81.2 4.5 %all-to-all-start.1 = ((bf16[4,8,256,128]{3,2,1,0:T(8,128)(2,1)}), bf16[4,8,256,128]{3,2,1,0:T(8,128)(2,1)}, u32[]{:S(2)}, u32[]{:S(2)}) async-start(bf16[4,8,256,128]{3,2,1,0:T(8,128)(2,1)} %grad_down_pieces.1), calls=%async_computation.1 | async-start | bytes 4194304 | tf_op jit(solution)/shard_map/all_to_all | solution.py:551
  85.7 0.5 collective-permute-start.18
  86.2 14.2 %collective-permute-done.18.rest_3_ = bf16[128,2048]{1,0:T(8,128)(2,1)S(1)} collective-permute-done((bf16[128,2048]{1,0:T(8,128)(2,1)}, bf16[128,2048]{1,0:T(8,128)(2,1)S(1)}, u32[]{:S(2)}, u32[]{:S(2)}) %collective-permute-start.18) | collective-permute-done | bytes 524320 | tf_op jit(solution)/shard_map/ppermute | solution.py:60
  100.4 2.3 %low_product.1 = bf16[2,4,128,128]{3,2,1,0:T(8,128)(2,1)S(1)} custom-call(s32[59]{0:T(128)S(1)} %concatenate.6.at_ref, bf16[1024,1024]{1,0:T(8,128)(2,1)S(1)} %copy-done.3, bf16[4,2048,128]{2,1,0:T(8,128)(2,1)} %all-to-all-done.a_ref), custom_call_target="tpu_custom_call" | custom-call | flops 1024 | bytes 1024 | tf_op jit(solution)/shard_map/low_product/pallas_call | solution.py:170
  102.7 0.1 collective-permute-start.19
  102.8 1.3 collective-permute-done.19
  104.2 0.5 collective-permute-start.22
  104.7 1.6 %collective-permute-start.21 = (bf16[4,128,128]{2,1,0:T(8,128)(2,1)S(1)}, bf16[4,128,128]{2,1,0:T(8,128)(2,1)S(1)}, u32[]{:S(2)}, u32[]{:S(2)}) collective-permute-start(bf16[4,128,128]{2,1,0:T(8,128)(2,1)S(1)} %fusion.3), channel_id=1, source_target_pairs={{0,4},{2,6},{4,0},{6,2},{1,5},{3,7},{5,1},{7,3},{8,12},{10,14},{12... | collective-permute-start | bytes 393224 | tf_op jit(solution)/shard_map/ppermute | solution.py:60
  106.3 1.5 %collective-permute-start.20 = (bf16[4,128,128]{2,1,0:T(8,128)(2,1)S(1)}, bf16[4,128,128]{2,1,0:T(8,128)(2,1)S(1)}, u32[]{:S(2)}, u32[]{:S(2)}) collective-permute-start(bf16[4,128,128]{2,1,0:T(8,128)(2,1)S(1)} %fusion.3), channel_id=1, source_target_pairs={{0,2},{2,0},{4,6},{6,4},{1,3},{3,1},{5,7},{7,5},{8,10},{10,8},{12,... | collective-permute-start | bytes 393224 | tf_op jit(solution)/shard_map/ppermute | solution.py:60
  107.7 3.8 %collective-permute-done.22 = bf16[4,128,128]{2,1,0:T(8,128)(2,1)S(1)} collective-permute-done((bf16[4,128,128]{2,1,0:T(8,128)(2,1)S(1)}, bf16[4,128,128]{2,1,0:T(8,128)(2,1)S(1)}, u32[]{:S(2)}, u32[]{:S(2)}) %collective-permute-start.22) | collective-permute-done | bytes 131104 | tf_op jit(solution)/shard_map/ppermute | solution.py:60
  111.5 1.2 collective-permute-done.21
  112.8 0.1 add_convert_fusion.low_ref.rest_0_
  112.9 0.1 collective-permute-start.23
  113.0 1.3 collective-permute-done.23.rest_1_
  114.3 1.9 %grad_up_pieces.1 = bf16[4,8,16,256]{3,2,1,0:T(8,128)(2,1)S(1)} custom-call(s32[59]{0:T(128)S(1)} %concatenate.6.at_ref, bf16[4,128,128]{2,1,0:T(8,128)(2,1)S(1)} %add_convert_fusion.low_ref.rest_0_, bf16[4,128,128]{2,1,0:T(8,128)(2,1)S(1)} %collective-permute-done.23.rest_1_, bf16[128,2048]{1,0:T(8,128)(2,1)S(1)} %copy-done.7, ...), custom_call_target="tpu_custom_call" | custom-call | flops 1024 | bytes 1024 | tf_op jit(solution)/shard_map/grad_up_pieces/pallas_call | solution.py:398
  116.3 3.5 %collective-permute-start.26 = (bf16[8,16,256]{2,1,0:T(8,128)(2,1)S(1)}, bf16[8,16,256]{2,1,0:T(8,128)(2,1)S(1)}, u32[]{:S(2)}, u32[]{:S(2)}) collective-permute-start(bf16[8,16,256]{2,1,0:T(8,128)(2,1)S(1)} %get-tuple-element.64), channel_id=1, source_target_pairs={{0,24},{8,0},{16,8},{24,16},{1,25},{9,1},{17,9},{25,17},{2,26},{10... | collective-permute-start | bytes 196616 | tf_op jit(solution)/shard_map/ppermute | solution.py:39
  119.8 1.1 collective-permute-start.24
  120.9 4.5 %input_gradient.1 = bf16[1024,1024]{1,0:T(8,128)(2,1)} custom-call(s32[59]{0:T(128)S(1)} %concatenate.6.at_ref, f32[1024,1024]{1,0:T(8,128)S(1)} %copy-done.5, bf16[4,2048,128]{2,1,0:T(8,128)(2,1)} %all-to-all-done.a_ref, bf16[4,128,128]{2,1,0:T(8,128)(2,1)S(1)} %pad_maximum_fusion.rest_0_, bf16[4,128,128]{2,1,0:T(8,128)(2,1)S(1)} %collective-permute-done.8.rest_1_), custom_call_target="tpu_custom_call" | custom-call | flops 1024 | bytes 1024 | tf_op jit(solution)/shard_map/input_gradient/pallas_call | solution.py:250
  125.4 2.5 %keys_and_values.1 = bf16[128,2048]{1,0:T(8,128)(2,1)} custom-call(s32[59]{0:T(128)S(1)} %concatenate.6.at_ref, bf16[4,128,128]{2,1,0:T(8,128)(2,1)S(1)} %add_convert_fusion.low_ref.rest_0_, bf16[64,2048]{1,0:T(8,128)(2,1)S(1)} %copy-done.13, f32[128,2048]{1,0:T(8,128)S(1)} %copy-done.8, bf16[128,2048]{1,0:T(8,128)(2,1)} %collective-permute-done.16.rest_1_, ...), custom_call_target="tpu_custom_call" | custom-call | flops 1024 | bytes 1024 | tf_op jit(solution)/shard_map/keys_and_values/pallas_call | solution.py:484
  127.9 10.0 %all-to-all-done.1.piece_ref = bf16[4,8,256,128]{3,2,1,0:T(8,128)(2,1)} async-done(((bf16[4,8,256,128]{3,2,1,0:T(8,128)(2,1)}), bf16[4,8,256,128]{3,2,1,0:T(8,128)(2,1)}, u32[]{:S(2)}, u32[]{:S(2)}) %all-to-all-start.1) | async-done | bytes 2097184 | tf_op jit(solution)/shard_map/all_to_all | solution.py:551
  137.9 4.2 %grad_down.1 = f32[24,256,128]{2,1,0:T(8,128)} custom-call(s32[59]{0:T(128)} %copy-done.14, bf16[4,8,256,128]{3,2,1,0:T(8,128)(2,1)} %all-to-all-done.1.piece_ref), custom_call_target="tpu_custom_call" | custom-call | flops 1024 | bytes 1024 | tf_op jit(solution)/shard_map/grad_down/pallas_call | solution.py:336
  142.1 1.5 %grad_up.1 = f32[24,16,256]{2,1,0:T(8,128)} custom-call(s32[59]{0:T(128)S(1)} %copy-done.15, bf16[8,16,256]{2,1,0:T(8,128)(2,1)S(1)} %get-tuple-element.56.rest_0_, bf16[8,16,256]{2,1,0:T(8,128)(2,1)S(1)} %collective-permute-done.24.rest_1_, bf16[8,16,256]{2,1,0:T(8,128)(2,1)S(1)} %collective-permute-done.25.rest_2_, ...), custom_call_target="tpu_custom_call" | custom-call | flops 1024 | bytes 1024 | tf_op jit(solution)/shard_map/grad_up/pallas_call | solution.py:425
  (56 shorter events, 0.2 us)
Async XLA Ops:
  0.6 18.4 %copy-start.7 = (bf16[128,2048]{1,0:T(8,128)(2,1)S(1)}, bf16[128,2048]{1,0:T(8,128)(2,1)}, u32[]{:S(2)}) copy-start(bf16[128,2048]{1,0:T(8,128)(2,1)} %rest_2_.1) | copy-start | bytes 1572868
  0.6 14.9 %copy-start.18 = (s32[24]{0:T(128)S(1)}, s32[24]{0:T(128)}, u32[]{:S(2)}) copy-start(s32[24]{0:T(128)} %slot_ref.1) | copy-start | bytes 292
  0.7 14.9 %copy-start.17 = (s32[32]{0:T(128)S(1)}, s32[32]{0:T(128)}, u32[]{:S(2)}) copy-start(s32[32]{0:T(128)} %tenant_ref.1) | copy-start | bytes 388
  0.7 20.2 %copy-start.3 = (bf16[1024,1024]{1,0:T(8,128)(2,1)S(1)}, bf16[1024,1024]{1,0:T(8,128)(2,1)}, u32[]{:S(2)}) copy-start(bf16[1024,1024]{1,0:T(8,128)(2,1)} %x_ref.1) | copy-start | bytes 6291460
  0.7 20.1 %collective-permute-start.4 = (bf16[128,2048]{1,0:T(8,128)(2,1)}, bf16[128,2048]{1,0:T(8,128)(2,1)S(1)}, u32[]{:S(2)}, u32[]{:S(2)}) collective-permute-start(bf16[128,2048]{1,0:T(8,128)(2,1)} %rest_2_.1), channel_id=1, source_target_pairs={{0,4},{2,6},{4,0},{6,2},{1,5},{3,7},{5,1},{7,3},{8,12},{10,14},{12... | collective-permute-start | bytes 1572872 | tf_op jit(solution)/shard_map/ppermute | solution.py:60
  3.7 17.1 %collective-permute-start.3 = (bf16[128,2048]{1,0:T(8,128)(2,1)}, bf16[128,2048]{1,0:T(8,128)(2,1)}, u32[]{:S(2)}, u32[]{:S(2)}) collective-permute-start(bf16[128,2048]{1,0:T(8,128)(2,1)} %rest_2_.1), channel_id=1, source_target_pairs={{0,2},{2,0},{4,6},{6,4},{1,3},{3,1},{5,7},{7,5},{8,10},{10,8},{12,... | collective-permute-start | bytes 1572872 | tf_op jit(solution)/shard_map/ppermute | solution.py:60
  10.0 7.1 %collective-permute-start = (bf16[16,2048]{1,0:T(8,128)(2,1)}, bf16[16,2048]{1,0:T(8,128)(2,1)S(1)}, u32[]{:S(2)}, u32[]{:S(2)}) collective-permute-start(bf16[16,2048]{1,0:T(8,128)(2,1)} %get-tuple-element.34), channel_id=1, source_target_pairs={{0,8},{8,16},{16,24},{24,0},{1,9},{9,17},{17,25},{25,1},{2,10},{10... | collective-permute-start | bytes 196616 | tf_op jit(solution)/shard_map/ppermute | solution.py:39
  11.6 7.4 %collective-permute-start.1 = (bf16[16,2048]{1,0:T(8,128)(2,1)}, bf16[16,2048]{1,0:T(8,128)(2,1)S(1)}, u32[]{:S(2)}, u32[]{:S(2)}) collective-permute-start(bf16[16,2048]{1,0:T(8,128)(2,1)} %get-tuple-element.35), channel_id=1, source_target_pairs={{0,16},{8,24},{16,0},{24,8},{1,17},{9,25},{17,1},{25,9},{2,18},{10... | collective-permute-start | bytes 196616 | tf_op jit(solution)/shard_map/ppermute | solution.py:39
  14.2 4.9 %collective-permute-start.2 = (bf16[16,2048]{1,0:T(8,128)(2,1)}, bf16[16,2048]{1,0:T(8,128)(2,1)S(1)}, u32[]{:S(2)}, u32[]{:S(2)}) collective-permute-start(bf16[16,2048]{1,0:T(8,128)(2,1)} %get-tuple-element.36), channel_id=1, source_target_pairs={{0,24},{8,0},{16,8},{24,16},{1,25},{9,1},{17,9},{25,17},{2,26},{10... | collective-permute-start | bytes 196616 | tf_op jit(solution)/shard_map/ppermute | solution.py:39
  15.6 109.8 %copy-start.14 = (s32[59]{0:T(128)}, s32[59]{0:T(128)S(1)}, u32[]{:S(2)}) copy-start(s32[59]{0:T(128)S(1)} %concatenate.6.at_ref) | copy-start | bytes 712
  19.0 0.8 copy-start.16
  20.8 6.7 %copy-start.12 = (bf16[64,2048]{1,0:T(8,128)(2,1)}, bf16[64,2048]{1,0:T(8,128)(2,1)S(1)}, u32[]{:S(2)}) copy-start(bf16[64,2048]{1,0:T(8,128)(2,1)S(1)} %get-tuple-element.49.b_ref) | copy-start | bytes 786436
  20.8 2.3 %copy-start = (bf16[1024,2048]{1,0:T(8,128)(2,1)S(1)}, bf16[1024,2048]{1,0:T(8,128)(2,1)}, u32[]{:S(2)}) copy-start(bf16[1024,2048]{1,0:T(8,128)(2,1)} %w_ref.5) | copy-start | bytes 12582916
  27.5 23.9 %collective-permute-start.15 = (bf16[4,128,2048]{2,1,0:T(8,128)(2,1)}, bf16[4,128,2048]{2,1,0:T(8,128)(2,1)}, u32[]{:S(2)}, u32[]{:S(2)}) collective-permute-start(bf16[4,128,2048]{2,1,0:T(8,128)(2,1)} %bitcast.11), channel_id=1, source_target_pairs={{0,1},{1,0},{2,3},{3,2},{4,5},{5,4},{6,7},{7,6},{8,9},{9,8},{10,11... | collective-permute-start | bytes 6291464 | tf_op jit(solution)/shard_map/ppermute | solution.py:60
  27.5 53.7 %all-to-all-start = ((bf16[4,2048,128]{2,1,0:T(8,128)(2,1)}), bf16[4,2048,128]{2,1,0:T(8,128)(2,1)}, u32[]{:S(2)}, u32[]{:S(2)}) async-start(bf16[4,2048,128]{2,1,0:T(8,128)(2,1)} %get-tuple-element.38), calls=%async_computation | async-start | bytes 4194304 | tf_op jit(solution)/shard_map/all_to_all | solution.py:521
  32.0 17.4 %collective-permute-start.9 = (bf16[64,2048]{1,0:T(8,128)(2,1)S(1)}, bf16[64,2048]{1,0:T(8,128)(2,1)S(1)}, u32[]{:S(2)}, u32[]{:S(2)}) collective-permute-start(bf16[64,2048]{1,0:T(8,128)(2,1)S(1)} %slice.52), channel_id=1, source_target_pairs={{0,2},{2,0},{4,6},{6,4},{1,3},{3,1},{5,7},{7,5},{8,10},{10,8},{12,... | collective-permute-start | bytes 786440 | tf_op jit(solution)/shard_map/ppermute | solution.py:60
  32.6 9.2 %collective-permute-start.7 = (bf16[128,128]{1,0:T(8,128)(2,1)S(1)}, bf16[128,128]{1,0:T(8,128)(2,1)S(1)}, u32[]{:S(2)}, u32[]{:S(2)}) collective-permute-start(bf16[128,128]{1,0:T(8,128)(2,1)S(1)} %get-tuple-element.41), channel_id=1, source_target_pairs={{0,6},{2,4},{4,2},{6,0},{1,7},{3,5},{5,3},{7,1},{8,14},{10,12},{12... | collective-permute-start | bytes 98312 | tf_op jit(solution)/shard_map/ppermute | solution.py:60
  34.0 7.8 %collective-permute-start.6 = (bf16[128,128]{1,0:T(8,128)(2,1)S(1)}, bf16[128,128]{1,0:T(8,128)(2,1)S(1)}, u32[]{:S(2)}, u32[]{:S(2)}) collective-permute-start(bf16[128,128]{1,0:T(8,128)(2,1)S(1)} %get-tuple-element.41), channel_id=1, source_target_pairs={{0,4},{2,6},{4,0},{6,2},{1,5},{3,7},{5,1},{7,3},{8,12},{10,14},{12... | collective-permute-start | bytes 98312 | tf_op jit(solution)/shard_map/ppermute | solution.py:60
  35.6 7.8 %collective-permute-start.5 = (bf16[128,128]{1,0:T(8,128)(2,1)S(1)}, bf16[128,128]{1,0:T(8,128)(2,1)S(1)}, u32[]{:S(2)}, u32[]{:S(2)}) collective-permute-start(bf16[128,128]{1,0:T(8,128)(2,1)S(1)} %get-tuple-element.41), channel_id=1, source_target_pairs={{0,2},{2,0},{4,6},{6,4},{1,3},{3,1},{5,7},{7,5},{8,10},{10,8},{12,... | collective-permute-start | bytes 98312 | tf_op jit(solution)/shard_map/ppermute | solution.py:60
  41.8 15.1 %collective-permute-start.11 = (bf16[128,2048]{1,0:T(8,128)(2,1)S(1)}, bf16[128,2048]{1,0:T(8,128)(2,1)S(1)}, u32[]{:S(2)}, u32[]{:S(2)}) collective-permute-start(bf16[128,2048]{1,0:T(8,128)(2,1)S(1)} %copy-done.7), channel_id=1, source_target_pairs={{0,1},{1,0},{2,3},{3,2},{4,5},{5,4},{6,7},{7,6},{8,9},{9,8},{10,11... | collective-permute-start | bytes 1572872 | tf_op jit(solution)/shard_map/ppermute | solution.py:60
  41.8 8.7 %collective-permute-start.10 = (bf16[64,2048]{1,0:T(8,128)(2,1)S(1)}, bf16[64,2048]{1,0:T(8,128)(2,1)S(1)}, u32[]{:S(2)}, u32[]{:S(2)}) collective-permute-start(bf16[64,2048]{1,0:T(8,128)(2,1)S(1)} %slice.53), channel_id=1, source_target_pairs={{0,4},{2,6},{4,0},{6,2},{1,5},{3,7},{5,1},{7,3},{8,12},{10,14},{12... | collective-permute-start | bytes 786440 | tf_op jit(solution)/shard_map/ppermute | solution.py:60
  43.3 12.0 %collective-permute-start.8 = (bf16[4,128,128]{2,1,0:T(8,128)(2,1)S(1)}, bf16[4,128,128]{2,1,0:T(8,128)(2,1)S(1)}, u32[]{:S(2)}, u32[]{:S(2)}) collective-permute-start(bf16[4,128,128]{2,1,0:T(8,128)(2,1)S(1)} %pad_maximum_fusion.rest_0_), channel_id=1, source_target_pairs={{0,1},{1,0},{2,3},{3,2},{4,5},{5,4},{6,7},{7,6},{8,9},{9,8},{10,11... | collective-permute-start | bytes 393224 | tf_op jit(solution)/shard_map/ppermute | solution.py:60
  43.6 2.2 %copy-start.1 = (bf16[1024,2048]{1,0:T(8,128)(2,1)S(1)}, bf16[1024,2048]{1,0:T(8,128)(2,1)}, u32[]{:S(2)}) copy-start(bf16[1024,2048]{1,0:T(8,128)(2,1)} %w_ref.5) | copy-start | bytes 12582916
  49.4 16.0 %collective-permute-start.12 = (bf16[128,2048]{1,0:T(8,128)(2,1)}, bf16[128,2048]{1,0:T(8,128)(2,1)}, u32[]{:S(2)}, u32[]{:S(2)}) collective-permute-start(bf16[128,2048]{1,0:T(8,128)(2,1)} %collective-permute-done.3.rest_1_.rest_3_), channel_id=1, source_target_pairs={{0,1},{1,0},{2,3},{3,2},{4,5},{5,4},{6,7},{7,6},{8,9},{9,8},{10,11... | collective-permute-start | bytes 1572872 | tf_op jit(solution)/shard_map/ppermute | solution.py:60
  50.5 14.9 %collective-permute-start.13 = (bf16[128,2048]{1,0:T(8,128)(2,1)S(1)}, bf16[128,2048]{1,0:T(8,128)(2,1)}, u32[]{:S(2)}, u32[]{:S(2)}) collective-permute-start(bf16[128,2048]{1,0:T(8,128)(2,1)S(1)} %collective-permute-done.4.rest_2_.rest_4_), channel_id=1, source_target_pairs={{0,1},{1,0},{2,3},{3,2},{4,5},{5,4},{6,7},{7,6},{8,9},{9,8},{10,11... | collective-permute-start | bytes 1572872 | tf_op jit(solution)/shard_map/ppermute | solution.py:60
  51.4 14.0 %collective-permute-start.14 = (bf16[128,2048]{1,0:T(8,128)(2,1)}, bf16[128,2048]{1,0:T(8,128)(2,1)}, u32[]{:S(2)}, u32[]{:S(2)}) collective-permute-start(bf16[128,2048]{1,0:T(8,128)(2,1)} %constant_dynamic-update-slice_fusion.rest_3_.rest_5_), channel_id=1, source_target_pairs={{0,1},{1,0},{2,3},{3,2},{4,5},{5,4},{6,7},{7,6},{8,9},{9,8},{10,11... | collective-permute-start | bytes 1572872 | tf_op jit(solution)/shard_map/ppermute | solution.py:60
  55.3 21.1 %collective-permute-start.17 = (bf16[128,2048]{1,0:T(8,128)(2,1)}, bf16[128,2048]{1,0:T(8,128)(2,1)}, u32[]{:S(2)}, u32[]{:S(2)}) collective-permute-start(bf16[128,2048]{1,0:T(8,128)(2,1)} %get-tuple-element.62), channel_id=1, source_target_pairs={{0,4},{2,6},{4,0},{6,2},{1,5},{3,7},{5,1},{7,3},{8,12},{10,14},{12... | collective-permute-start | bytes 1572872 | tf_op jit(solution)/shard_map/ppermute | solution.py:60
  56.9 0.8 copy-start.9
  57.7 18.8 %collective-permute-start.16 = (bf16[128,2048]{1,0:T(8,128)(2,1)}, bf16[128,2048]{1,0:T(8,128)(2,1)}, u32[]{:S(2)}, u32[]{:S(2)}) collective-permute-start(bf16[128,2048]{1,0:T(8,128)(2,1)} %get-tuple-element.63), channel_id=1, source_target_pairs={{0,2},{2,0},{4,6},{6,4},{1,3},{3,1},{5,7},{7,5},{8,10},{10,8},{12,... | collective-permute-start | bytes 1572872 | tf_op jit(solution)/shard_map/ppermute | solution.py:60
  60.8 1.6 %copy-start.6 = (bf16[1024,1024]{1,0:T(8,128)(2,1)S(1)}, bf16[1024,1024]{1,0:T(8,128)(2,1)}, u32[]{:S(2)}) copy-start(bf16[1024,1024]{1,0:T(8,128)(2,1)} %copy.11) | copy-start | bytes 6291460
  62.4 3.1 %copy-start.2 = (bf16[1024,2048]{1,0:T(8,128)(2,1)S(1)}, bf16[1024,2048]{1,0:T(8,128)(2,1)}, u32[]{:S(2)}) copy-start(bf16[1024,2048]{1,0:T(8,128)(2,1)} %w_ref.5) | copy-start | bytes 12582916
  65.4 1.0 copy-start.10
  74.4 2.0 %copy-start.4 = (f32[1024,1024]{1,0:T(8,128)}, f32[1024,1024]{1,0:T(8,128)S(1)}, u32[]{:S(2)}) copy-start(f32[1024,1024]{1,0:T(8,128)S(1)} %cotangent_product.1.base_ref) | copy-start | bytes 12582916
  81.2 56.7 %all-to-all-start.1 = ((bf16[4,8,256,128]{3,2,1,0:T(8,128)(2,1)}), bf16[4,8,256,128]{3,2,1,0:T(8,128)(2,1)}, u32[]{:S(2)}, u32[]{:S(2)}) async-start(bf16[4,8,256,128]{3,2,1,0:T(8,128)(2,1)} %grad_down_pieces.1), calls=%async_computation.1 | async-start | bytes 4194304 | tf_op jit(solution)/shard_map/all_to_all | solution.py:551
  85.6 28.7 %copy-start.11 = (bf16[128,2048]{1,0:T(8,128)(2,1)S(1)}, bf16[128,2048]{1,0:T(8,128)(2,1)}, u32[]{:S(2)}) copy-start(bf16[128,2048]{1,0:T(8,128)(2,1)} %copy-done.9) | copy-start | bytes 1572868
  85.7 14.7 %collective-permute-start.18 = (bf16[128,2048]{1,0:T(8,128)(2,1)}, bf16[128,2048]{1,0:T(8,128)(2,1)S(1)}, u32[]{:S(2)}, u32[]{:S(2)}) collective-permute-start(bf16[128,2048]{1,0:T(8,128)(2,1)} %get-tuple-element.61), channel_id=1, source_target_pairs={{0,6},{2,4},{4,2},{6,0},{1,7},{3,5},{5,3},{7,1},{8,14},{10,12},{12... | collective-permute-start | bytes 1572872 | tf_op jit(solution)/shard_map/ppermute | solution.py:60
  102.7 1.4 collective-permute-start.19
  104.2 7.3 %collective-permute-start.22 = (bf16[4,128,128]{2,1,0:T(8,128)(2,1)S(1)}, bf16[4,128,128]{2,1,0:T(8,128)(2,1)S(1)}, u32[]{:S(2)}, u32[]{:S(2)}) collective-permute-start(bf16[4,128,128]{2,1,0:T(8,128)(2,1)S(1)} %fusion.3), channel_id=1, source_target_pairs={{0,6},{2,4},{4,2},{6,0},{1,7},{3,5},{5,3},{7,1},{8,14},{10,12},{12... | collective-permute-start | bytes 393224 | tf_op jit(solution)/shard_map/ppermute | solution.py:60
  104.7 8.1 %collective-permute-start.21 = (bf16[4,128,128]{2,1,0:T(8,128)(2,1)S(1)}, bf16[4,128,128]{2,1,0:T(8,128)(2,1)S(1)}, u32[]{:S(2)}, u32[]{:S(2)}) collective-permute-start(bf16[4,128,128]{2,1,0:T(8,128)(2,1)S(1)} %fusion.3), channel_id=1, source_target_pairs={{0,4},{2,6},{4,0},{6,2},{1,5},{3,7},{5,1},{7,3},{8,12},{10,14},{12... | collective-permute-start | bytes 393224 | tf_op jit(solution)/shard_map/ppermute | solution.py:60
  106.3 6.5 %collective-permute-start.20 = (bf16[4,128,128]{2,1,0:T(8,128)(2,1)S(1)}, bf16[4,128,128]{2,1,0:T(8,128)(2,1)S(1)}, u32[]{:S(2)}, u32[]{:S(2)}) collective-permute-start(bf16[4,128,128]{2,1,0:T(8,128)(2,1)S(1)} %fusion.3), channel_id=1, source_target_pairs={{0,2},{2,0},{4,6},{6,4},{1,3},{3,1},{5,7},{7,5},{8,10},{10,8},{12,... | collective-permute-start | bytes 393224 | tf_op jit(solution)/shard_map/ppermute | solution.py:60
  112.9 8.0 %copy-start.5 = (f32[1024,1024]{1,0:T(8,128)S(1)}, f32[1024,1024]{1,0:T(8,128)}, u32[]{:S(2)}) copy-start(f32[1024,1024]{1,0:T(8,128)} %copy-done.4) | copy-start | bytes 12582916
  112.9 1.4 collective-permute-start.23
  116.3 25.8 %collective-permute-start.26 = (bf16[8,16,256]{2,1,0:T(8,128)(2,1)S(1)}, bf16[8,16,256]{2,1,0:T(8,128)(2,1)S(1)}, u32[]{:S(2)}, u32[]{:S(2)}) collective-permute-start(bf16[8,16,256]{2,1,0:T(8,128)(2,1)S(1)} %get-tuple-element.64), channel_id=1, source_target_pairs={{0,24},{8,0},{16,8},{24,16},{1,25},{9,1},{17,9},{25,17},{2,26},{10... | collective-permute-start | bytes 196616 | tf_op jit(solution)/shard_map/ppermute | solution.py:39
  119.7 22.4 %collective-permute-start.25 = (bf16[8,16,256]{2,1,0:T(8,128)(2,1)S(1)}, bf16[8,16,256]{2,1,0:T(8,128)(2,1)S(1)}, u32[]{:S(2)}, u32[]{:S(2)}) collective-permute-start(bf16[8,16,256]{2,1,0:T(8,128)(2,1)S(1)} %get-tuple-element.65), channel_id=1, source_target_pairs={{0,16},{8,24},{16,0},{24,8},{1,17},{9,25},{17,1},{25,9},{2,18},{10... | collective-permute-start | bytes 196616 | tf_op jit(solution)/shard_map/ppermute | solution.py:39
  119.7 5.7 %copy-start.8 = (f32[128,2048]{1,0:T(8,128)S(1)}, f32[128,2048]{1,0:T(8,128)}, u32[]{:S(2)}) copy-start(f32[128,2048]{1,0:T(8,128)} %get-tuple-element.60.rest_0_) | copy-start | bytes 3145732
  119.7 5.7 %copy-start.13 = (bf16[64,2048]{1,0:T(8,128)(2,1)S(1)}, bf16[64,2048]{1,0:T(8,128)(2,1)}, u32[]{:S(2)}) copy-start(bf16[64,2048]{1,0:T(8,128)(2,1)} %copy-done.12) | copy-start | bytes 786436
  119.8 22.4 %collective-permute-start.24 = (bf16[8,16,256]{2,1,0:T(8,128)(2,1)S(1)}, bf16[8,16,256]{2,1,0:T(8,128)(2,1)S(1)}, u32[]{:S(2)}, u32[]{:S(2)}) collective-permute-start(bf16[8,16,256]{2,1,0:T(8,128)(2,1)S(1)} %get-tuple-element.66), channel_id=1, source_target_pairs={{0,8},{8,16},{16,24},{24,0},{1,9},{9,17},{17,25},{25,1},{2,10},{10... | collective-permute-start | bytes 196616 | tf_op jit(solution)/shard_map/ppermute | solution.py:39
  127.9 14.3 %copy-start.15 = (s32[59]{0:T(128)S(1)}, s32[59]{0:T(128)}, u32[]{:S(2)}) copy-start(s32[59]{0:T(128)} %copy-done.14) | copy-start | bytes 712

commit v16 on v13

--- a/solution.py
+++ b/solution.py
@@ -123,17 +123,23 @@
     return out[:data_count], out[data_count]
 
 
-def base_product(at, tokens, weight, first, count):
+def base_product(at, tokens, weight, first, count, parts):
     pipe_count, tensor_count, rows, depth = tokens.shape
     tile = 1024
-
-    def kernel(at_ref, x_ref, w_ref, out_ref):
+    chips = pipe_count // parts
+
+    def kernel(at_ref, x_ref, w_ref, *out_refs):
         x = x_ref[...].reshape(pipe_count * rows, depth)
-        y = jnp.dot(x, w_ref[...], preferred_element_type=jnp.float32).astype(out_ref.dtype)
+        y = jnp.dot(x, w_ref[...], preferred_element_type=jnp.float32).astype(out_refs[0].dtype)
         for chip in range(pipe_count):
-            out_ref[0, which_partner(chip, at_ref[1], pipe_count)] = y[chip * rows : (chip + 1) * rows]
-
-    return call(
+            k = which_partner(chip, at_ref[1], pipe_count)
+            for part, out_ref in enumerate(out_refs):
+
+                @pl.when((k >= part * chips) & (k < (part + 1) * chips))
+                def _():
+                    out_ref[0, k - part * chips] = y[chip * rows : (chip + 1) * rows]
+
+    out = call(
         kernel,
         "base_product",
         grid_spec=pltpu.PrefetchScalarGridSpec(
@@ -146,10 +152,11 @@
                 ),
                 pl.BlockSpec((depth, tile), lambda n, s, at: (0, n)),
             ],
-            out_specs=pl.BlockSpec((1, pipe_count, rows, tile), lambda n, s, at: (s, 0, 0, n)),
+            out_specs=(pl.BlockSpec((1, chips, rows, tile), lambda n, s, at: (s, 0, 0, n)),) * parts,
         ),
-        out_shape=jax.ShapeDtypeStruct((count, pipe_count, rows, WIDTH), jnp.bfloat16),
+        out_shape=(jax.ShapeDtypeStruct((count, chips, rows, WIDTH), jnp.bfloat16),) * parts,
     )(at, tokens, weight)
+    return out
 
 
 def low_product(at, tokens, down, pipe_count, tensor_count):
@@ -525,11 +532,18 @@
     cot_chips = [cotangent] + cot_chips
 
     tokens_by_group = base_tokens.reshape(pipe_count, tensor_count, rows, feature_count)
-    base_send = base_product(at, tokens_by_group, key_value_weight, 1, tensor_count - 1)
-    base_came = [swap(base_send[s - 1], "tensor", s) for s in range(1, tensor_count)]
-    base_keep = base_product(at, tokens_by_group, key_value_weight, 0, 1)[0]
+    parts = 2 if pipe_count % 2 == 0 else 1
+    chips = pipe_count // parts
+    base_send = base_product(at, tokens_by_group, key_value_weight, 1, tensor_count - 1, parts)
+    base_came = [
+        [swap(part[s - 1], "tensor", s) for part in base_send] for s in range(1, tensor_count)
+    ]
+    (base_keep,) = base_product(at, tokens_by_group, key_value_weight, 0, 1, 1)
     base_chip = [
-        sum([base_keep[k].astype(jnp.float32)] + [b[k].astype(jnp.float32) for b in base_came])
+        sum(
+            [base_keep[0, k].astype(jnp.float32)]
+            + [came[k // chips][k % chips].astype(jnp.float32) for came in base_came]
+        )
         for k in range(pipe_count)
     ]
     base_chip[1:] = [piece.astype(jnp.bfloat16) for piece in base_chip[1:]]

time: 143 us -> 150 us (1.049)
  waiting for transfers between devices: 43.6 us -> 53.6 us
  local copies, waits for them, and re-layouts: 14.9 us -> 12.7 us
  starting transfers between devices: 36.8 us -> 38.7 us
  other arithmetic: 3.74 us -> 2.17 us
    ppermute x21 -> x22, waiting for transfers between devices: 25.4 us -> 40.5 us  [swap(): lax.ppermute(piece, axis, [(i, partner(i, k, count)) for i in range(count)])]
    all_to_all x1, waiting for transfers between devices: 4.78 us -> 0.01 us  [body(): a_recv = lax.all_to_all(a_send, 'dp', 0, 0, tiled=True)]
    unnamed x39 -> x37, local copies, waits for them, and re-layouts: 10.5 us -> 8.35 us
    ppermute x6, starting transfers between devices: 10.2 us -> 11.9 us  [shift(): lax.ppermute(piece, axis, [(i, (i + k) % count) for i in range(count)])]
    add x1, other arithmetic: 3.61 us -> 2.04 us  [body(): sum([base_keep[0, k].astype(jnp.float32)] + [came[k // chips][k % chips]....]
    ppermute x21 -> x22, starting transfers between devices: 17.6 us -> 17.4 us  [swap(): lax.ppermute(piece, axis, [(i, partner(i, k, count)) for i in range(count)])]
  transfers between devices with their start and end apart: 29 -> 30, of which waited for: 11 -> 14; matrix products, arithmetic and copies ran while one was open for 6% -> 5% of each run, Pallas kernels for 25% -> 23%
where the time goes in v16:
time: 150 us; the launch traced here: 149 us
  waiting for transfers between devices  53.6 us (36%)
  Pallas kernels  41.2 us (27%)
  starting transfers between devices  38.7 us (26%)
  local copies, waits for them, and re-layouts  12.7 us (8%)
  other arithmetic  2.17 us (1%)
    ppermute x22, waiting for transfers between devices, swap(): lax.ppermute(piece, axis, [(i, partner(i, k, count)) for i in range(count)])  40.5 us
    ppermute x22, starting transfers between devices, swap(): lax.ppermute(piece, axis, [(i, partner(i, k, count)) for i in range(count)])  17.4 us
    ppermute x6, starting transfers between devices, shift(): lax.ppermute(piece, axis, [(i, (i + k) % count) for i in range(count)])  11.9 us
    all_to_all x1, waiting for transfers between devices, body(): down_recv = lax.all_to_all(down_send, 'dp', 0, 0, tiled=True)  9.54 us
    unnamed x37, local copies, waits for them, and re-layouts  8.35 us
    pallas_call x1, Pallas kernels, cotangent_product(): call(kernel, 'cotangent_product', grid=(depth // tile,), in_specs=[SMEM,...  7.96 us
    pallas_call x2, Pallas kernels, base_product(): call(kernel, 'base_product', grid_spec=pltpu.PrefetchScalarGridSpec(num_s...  7.73 us
    all_to_all x1, starting transfers between devices, body(): a_recv = lax.all_to_all(a_send, 'dp', 0, 0, tiled=True)  4.72 us
  transfers between devices with their start and end apart: 30, of which 14 were waited for; matrix products, arithmetic and copies ran while one was open for 5% of the time, Pallas kernels for 23%

profile of v16, /device:TPU:0, one launch (start us, length us, event | category | flops | bytes accessed | tf_op | source)
XLA Modules:
  0.0 149.4 jit_solution(9144088547199662951)
XLA Ops:
  0.6 4.6 %pick_rows.1 = (bf16[16,2048]{1,0:T(8,128)(2,1)}, bf16[16,2048]{1,0:T(8,128)(2,1)}, bf16[16,2048]{1,0:T(8,128)(2,1)}, bf16[16,2048]{1,0:T(8,128)(2,1)}, bf16[4,2048,128]{2,1,0:T(8,128)(2,1)}) custom-call(s32[32]{0:T(128)} %tenant_ref.1, s32[24]{0:T(128)} %slot_ref.1, bf16[24,256,128]{2,1,0:T(8,128)(2,1)} %down_ref.1, bf16[24,16,2048]{2,1,0:T(8,128)(2,1)} %up_ref.1), custom_call_target="tpu_custom_call" | custom-call | flops 1024 | bytes 1024 | tf_op jit(solution)/shard_map/pick_rows/pallas_call | solution.py:108
  5.3 3.1 %collective-permute-start = (bf16[16,2048]{1,0:T(8,128)(2,1)}, bf16[16,2048]{1,0:T(8,128)(2,1)S(1)}, u32[]{:S(2)}, u32[]{:S(2)}) collective-permute-start(bf16[16,2048]{1,0:T(8,128)(2,1)} %get-tuple-element.35), channel_id=1, source_target_pairs={{0,8},{8,16},{16,24},{24,0},{1,9},{9,17},{17,25},{25,1},{2,10},{10... | collective-permute-start | bytes 196616 | tf_op jit(solution)/shard_map/ppermute | solution.py:39
  8.4 2.6 %collective-permute-start.1 = (bf16[16,2048]{1,0:T(8,128)(2,1)}, bf16[16,2048]{1,0:T(8,128)(2,1)S(1)}, u32[]{:S(2)}, u32[]{:S(2)}) collective-permute-start(bf16[16,2048]{1,0:T(8,128)(2,1)} %get-tuple-element.36), channel_id=1, source_target_pairs={{0,16},{8,24},{16,0},{24,8},{1,17},{9,25},{17,1},{25,9},{2,18},{10... | collective-permute-start | bytes 196616 | tf_op jit(solution)/shard_map/ppermute | solution.py:39
  11.0 1.3 collective-permute-start.2
  12.3 0.9 collective-permute-done.rest_1_
  13.1 2.5 %collective-permute-done.1.rest_2_ = bf16[16,2048]{1,0:T(8,128)(2,1)S(1)} collective-permute-done((bf16[16,2048]{1,0:T(8,128)(2,1)}, bf16[16,2048]{1,0:T(8,128)(2,1)S(1)}, u32[]{:S(2)}, u32[]{:S(2)}) %collective-permute-start.1) | collective-permute-done | bytes 65568 | tf_op jit(solution)/shard_map/ppermute | solution.py:39
  15.7 0.2 collective-permute-done.2.rest_3_
  15.9 4.7 %all-to-all-start = ((bf16[4,2048,128]{2,1,0:T(8,128)(2,1)}), bf16[4,2048,128]{2,1,0:T(8,128)(2,1)}, u32[]{:S(2)}, u32[]{:S(2)}) async-start(bf16[4,2048,128]{2,1,0:T(8,128)(2,1)} %get-tuple-element.38), calls=%async_computation | async-start | bytes 4194304 | tf_op jit(solution)/shard_map/all_to_all | solution.py:528
  20.6 1.6 %collective-permute-start.4 = (bf16[128,2048]{1,0:T(8,128)(2,1)S(1)}, bf16[128,2048]{1,0:T(8,128)(2,1)S(1)}, u32[]{:S(2)}, u32[]{:S(2)}) collective-permute-start(bf16[128,2048]{1,0:T(8,128)(2,1)S(1)} %copy-done.6), channel_id=1, source_target_pairs={{0,4},{2,6},{4,0},{6,2},{1,5},{3,7},{5,1},{7,3},{8,12},{10,14},{12... | collective-permute-start | bytes 1572872 | tf_op jit(solution)/shard_map/ppermute | solution.py:60
  22.3 1.5 %collective-permute-start.3 = (bf16[128,2048]{1,0:T(8,128)(2,1)S(1)}, bf16[128,2048]{1,0:T(8,128)(2,1)}, u32[]{:S(2)}, u32[]{:S(2)}) collective-permute-start(bf16[128,2048]{1,0:T(8,128)(2,1)S(1)} %copy-done.6), channel_id=1, source_target_pairs={{0,2},{2,0},{4,6},{6,4},{1,3},{3,1},{5,7},{7,5},{8,10},{10,8},{12,... | collective-permute-start | bytes 1572872 | tf_op jit(solution)/shard_map/ppermute | solution.py:60
  23.8 0.1 concatenate.6.at_ref
  23.9 10.2 %collective-permute-done.4.rest_2_.rest_4_ = bf16[128,2048]{1,0:T(8,128)(2,1)S(1)} collective-permute-done((bf16[128,2048]{1,0:T(8,128)(2,1)S(1)}, bf16[128,2048]{1,0:T(8,128)(2,1)S(1)}, u32[]{:S(2)}, u32[]{:S(2)}) %collective-permute-start.4) | collective-permute-done | bytes 524320 | tf_op jit(solution)/shard_map/ppermute | solution.py:60
  34.1 1.3 collective-permute-done.3.rest_1_.rest_3_
  35.4 2.2 %copy-done = bf16[1024,2048]{1,0:T(8,128)(2,1)S(1)} copy-done((bf16[1024,2048]{1,0:T(8,128)(2,1)S(1)}, bf16[1024,2048]{1,0:T(8,128)(2,1)}, u32[]{:S(2)}) %copy-start) | copy-done | bytes 4194328
  37.6 3.9 %base_product.3 = (bf16[1,2,128,2048]{3,2,1,0:T(8,128)(2,1)S(1)}, bf16[1,2,128,2048]{3,2,1,0:T(8,128)(2,1)S(1)}) custom-call(s32[59]{0:T(128)S(1)} %concatenate.6.at_ref, bf16[4,2,128,1024]{3,2,1,0:T(8,128)(2,1)S(1)} %bitcast.67, bf16[1024,2048]{1,0:T(8,128)(2,1)S(1)} %copy-done), custom_call_target="tpu_custom_call" | custom-call | flops 1024 | bytes 1024 | tf_op jit(solution)/shard_map/base_product/pallas_call | solution.py:142
  41.5 0.1 collective-permute-start.17
  41.5 0.5 collective-permute-start.15
  42.1 0.8 collective-permute-start.9
  42.9 0.9 own_rows.1
  43.8 1.3 collective-permute-start.7
  45.1 1.5 collective-permute-start.6
  46.6 4.5 %collective-permute-done.7 = bf16[128,128]{1,0:T(8,128)(2,1)S(1)} collective-permute-done((bf16[128,128]{1,0:T(8,128)(2,1)S(1)}, bf16[128,128]{1,0:T(8,128)(2,1)S(1)}, u32[]{:S(2)}, u32[]{:S(2)}) %collective-permute-start.7) | collective-permute-done | bytes 32800 | tf_op jit(solution)/shard_map/ppermute | solution.py:60
  51.1 0.7 collective-permute-start.5
  51.8 1.0 slice.49
  52.9 2.2 %collective-permute-done.5 = bf16[128,128]{1,0:T(8,128)(2,1)S(1)} collective-permute-done((bf16[128,128]{1,0:T(8,128)(2,1)S(1)}, bf16[128,128]{1,0:T(8,128)(2,1)S(1)}, u32[]{:S(2)}, u32[]{:S(2)}) %collective-permute-start.5) | collective-permute-done | bytes 32800 | tf_op jit(solution)/shard_map/ppermute | solution.py:60
  55.0 1.5 collective-permute-start.10
  56.5 3.8 %base_product.2 = bf16[1,4,128,2048]{3,2,1,0:T(8,128)(2,1)S(1)} custom-call(s32[59]{0:T(128)S(1)} %concatenate.6.at_ref, bf16[4,2,128,1024]{3,2,1,0:T(8,128)(2,1)S(1)} %bitcast.68, bf16[1024,2048]{1,0:T(8,128)(2,1)S(1)} %copy-done), custom_call_target="tpu_custom_call" | custom-call | flops 1024 | bytes 1024 | tf_op jit(solution)/shard_map/base_product/pallas_call | solution.py:142
  60.5 0.7 constant_dynamic-update-slice_fusion.1
  61.2 0.4 collective-permute-done.10
  61.6 0.1 collective-permute-start.12
  61.7 0.7 constant_dynamic-update-slice_fusion.rest_3_.rest_5_
  62.4 0.4 collective-permute-start.13
  62.8 0.1 collective-permute-start.14
  62.9 2.0 %convert_add_fusion = (f32[128,2048]{1,0:T(8,128)}, bf16[128,2048]{1,0:T(8,128)(2,1)}, bf16[128,2048]{1,0:T(8,128)(2,1)}, bf16[128,2048]{1,0:T(8,128)(2,1)}) fusion(bf16[2,128,2048]{2,1,0:T(8,128)(2,1)S(1)} %collective-permute-done.15, bf16[1,4,128,2048]{3,2,1,0:T(8,128)(2,1)S(1)} %base_product.2, bf16[2,128,2048]{2,1,0:T(8,128)(2,1)S(1)} %collective-permute-done.17), kind=kLoop, calls=%fused_computation | loop fusion | flops 3932160 | bytes 6815744 | tf_op jit(solution)/shard_map/add | solution.py:543
  65.0 1.3 collective-permute-start.16
  66.3 0.8 copy-done.8
  67.1 1.5 collective-permute-start.18
  68.6 2.5 %copy.11 = bf16[1024,1024]{1,0:T(8,128)(2,1)} copy(bf16[1024,1024]{0,1:T(8,128)(2,1)S(1)} %bitcast.69) | data formatting | bytes 4194304 | tf_op jit(solution)/shard_map/transpose | solution.py:559
  71.1 1.6 %copy-done.5 = bf16[1024,1024]{1,0:T(8,128)(2,1)S(1)} copy-done((bf16[1024,1024]{1,0:T(8,128)(2,1)S(1)}, bf16[1024,1024]{1,0:T(8,128)(2,1)}, u32[]{:S(2)}) %copy-start.5) | copy-done | bytes 2097176
  72.7 3.1 %grad_down_pieces.1 = bf16[4,8,256,128]{3,2,1,0:T(8,128)(2,1)} custom-call(s32[59]{0:T(128)S(1)} %concatenate.6.at_ref, bf16[4,256,1024]{2,1,0:T(8,128)(2,1)S(1)} %bitcast.70, bf16[4,128,128]{2,1,0:T(8,128)(2,1)S(1)} %pad_maximum_fusion.rest_0_, bf16[4,128,128]{2,1,0:T(8,128)(2,1)S(1)} %collective-permute-done.8.rest_1_), custom_call_target="tpu_custom_call" | custom-call | flops 1024 | bytes 1024 | tf_op jit(solution)/shard_map/grad_down_pieces/pallas_call | solution.py:297
  75.8 1.0 copy-done.9
  76.8 8.0 %cotangent_product.1.base_ref = f32[1024,1024]{1,0:T(8,128)S(1)} custom-call(s32[59]{0:T(128)S(1)} %concatenate.6.at_ref, bf16[1024,2048]{1,0:T(8,128)(2,1)S(1)} %copy-done.1, bf16[128,2048]{1,0:T(8,128)(2,1)S(1)} %copy-done.6, bf16[128,2048]{1,0:T(8,128)(2,1)} %collective-permute-done.3.rest_1_.rest_3_, ...), custom_call_target="tpu_custom_call" | custom-call | flops 1024 | bytes 1024 | tf_op jit(solution)/shard_map/cotangent_product/pallas_call | solution.py:216
  84.8 2.0 %copy-done.3 = f32[1024,1024]{1,0:T(8,128)} copy-done((f32[1024,1024]{1,0:T(8,128)}, f32[1024,1024]{1,0:T(8,128)S(1)}, u32[]{:S(2)}) %copy-start.3) | copy-done | bytes 4194328
  86.8 4.7 %all-to-all-start.1 = ((bf16[4,8,256,128]{3,2,1,0:T(8,128)(2,1)}), bf16[4,8,256,128]{3,2,1,0:T(8,128)(2,1)}, u32[]{:S(2)}, u32[]{:S(2)}) async-start(bf16[4,8,256,128]{3,2,1,0:T(8,128)(2,1)} %grad_down_pieces.1), calls=%async_computation.1 | async-start | bytes 4194304 | tf_op jit(solution)/shard_map/all_to_all | solution.py:565
  91.5 0.7 collective-permute-start.19
  92.2 13.9 %collective-permute-done.19.rest_3_ = bf16[128,2048]{1,0:T(8,128)(2,1)S(1)} collective-permute-done((bf16[128,2048]{1,0:T(8,128)(2,1)}, bf16[128,2048]{1,0:T(8,128)(2,1)S(1)}, u32[]{:S(2)}, u32[]{:S(2)}) %collective-permute-start.19) | collective-permute-done | bytes 524320 | tf_op jit(solution)/shard_map/ppermute | solution.py:60
  106.1 2.3 %low_product.1 = bf16[2,4,128,128]{3,2,1,0:T(8,128)(2,1)S(1)} custom-call(s32[59]{0:T(128)S(1)} %concatenate.6.at_ref, bf16[1024,1024]{1,0:T(8,128)(2,1)S(1)} %copy-done.2, bf16[4,2048,128]{2,1,0:T(8,128)(2,1)} %all-to-all-done.a_ref), custom_call_target="tpu_custom_call" | custom-call | flops 1024 | bytes 1024 | tf_op jit(solution)/shard_map/low_product/pallas_call | solution.py:177
  108.6 1.3 collective-permute-done.20
  109.9 0.8 collective-permute-start.23
  110.7 1.5 %collective-permute-start.22 = (bf16[4,128,128]{2,1,0:T(8,128)(2,1)S(1)}, bf16[4,128,128]{2,1,0:T(8,128)(2,1)S(1)}, u32[]{:S(2)}, u32[]{:S(2)}) collective-permute-start(bf16[4,128,128]{2,1,0:T(8,128)(2,1)S(1)} %fusion.3), channel_id=1, source_target_pairs={{0,4},{2,6},{4,0},{6,2},{1,5},{3,7},{5,1},{7,3},{8,12},{10,14},{12... | collective-permute-start | bytes 393224 | tf_op jit(solution)/shard_map/ppermute | solution.py:60
  112.2 1.3 collective-permute-start.21
  113.5 3.8 %collective-permute-done.23 = bf16[4,128,128]{2,1,0:T(8,128)(2,1)S(1)} collective-permute-done((bf16[4,128,128]{2,1,0:T(8,128)(2,1)S(1)}, bf16[4,128,128]{2,1,0:T(8,128)(2,1)S(1)}, u32[]{:S(2)}, u32[]{:S(2)}) %collective-permute-start.23) | collective-permute-done | bytes 131104 | tf_op jit(solution)/shard_map/ppermute | solution.py:60
  117.3 1.5 collective-permute-done.22
  118.8 0.1 add_convert_fusion.low_ref.rest_0_
  119.0 1.3 collective-permute-done.24.rest_1_
  120.3 1.9 %grad_up_pieces.1 = bf16[4,8,16,256]{3,2,1,0:T(8,128)(2,1)S(1)} custom-call(s32[59]{0:T(128)S(1)} %concatenate.6.at_ref, bf16[4,128,128]{2,1,0:T(8,128)(2,1)S(1)} %add_convert_fusion.low_ref.rest_0_, bf16[4,128,128]{2,1,0:T(8,128)(2,1)S(1)} %collective-permute-done.24.rest_1_, bf16[128,2048]{1,0:T(8,128)(2,1)S(1)} %copy-done.6, ...), custom_call_target="tpu_custom_call" | custom-call | flops 1024 | bytes 1024 | tf_op jit(solution)/shard_map/grad_up_pieces/pallas_call | solution.py:405
  122.3 3.5 %collective-permute-start.27 = (bf16[8,16,256]{2,1,0:T(8,128)(2,1)S(1)}, bf16[8,16,256]{2,1,0:T(8,128)(2,1)S(1)}, u32[]{:S(2)}, u32[]{:S(2)}) collective-permute-start(bf16[8,16,256]{2,1,0:T(8,128)(2,1)S(1)} %get-tuple-element.68), channel_id=1, source_target_pairs={{0,24},{8,0},{16,8},{24,16},{1,25},{9,1},{17,9},{25,17},{2,26},{10... | collective-permute-start | bytes 196616 | tf_op jit(solution)/shard_map/ppermute | solution.py:39
  125.8 0.4 collective-permute-start.26
  126.2 0.9 collective-permute-start.25
  127.2 4.5 %input_gradient.1 = bf16[1024,1024]{1,0:T(8,128)(2,1)} custom-call(s32[59]{0:T(128)S(1)} %concatenate.6.at_ref, f32[1024,1024]{1,0:T(8,128)S(1)} %copy-done.4, bf16[4,2048,128]{2,1,0:T(8,128)(2,1)} %all-to-all-done.a_ref, bf16[4,128,128]{2,1,0:T(8,128)(2,1)S(1)} %pad_maximum_fusion.rest_0_, bf16[4,128,128]{2,1,0:T(8,128)(2,1)S(1)} %collective-permute-done.8.rest_1_), custom_call_target="tpu_custom_call" | custom-call | flops 1024 | bytes 1024 | tf_op jit(solution)/shard_map/input_gradient/pallas_call | solution.py:257
  131.7 2.5 %keys_and_values.1 = bf16[128,2048]{1,0:T(8,128)(2,1)} custom-call(s32[59]{0:T(128)S(1)} %concatenate.6.at_ref, bf16[4,128,128]{2,1,0:T(8,128)(2,1)S(1)} %add_convert_fusion.low_ref.rest_0_, bf16[64,2048]{1,0:T(8,128)(2,1)S(1)} %copy-done.12, f32[128,2048]{1,0:T(8,128)S(1)} %copy-done.7, bf16[128,2048]{1,0:T(8,128)(2,1)} %collective-permute-done.16.rest_1_, ...), custom_call_target="tpu_custom_call" | custom-call | flops 1024 | bytes 1024 | tf_op jit(solution)/shard_map/keys_and_values/pallas_call | solution.py:491
  134.2 9.5 %all-to-all-done.1.piece_ref = bf16[4,8,256,128]{3,2,1,0:T(8,128)(2,1)} async-done(((bf16[4,8,256,128]{3,2,1,0:T(8,128)(2,1)}), bf16[4,8,256,128]{3,2,1,0:T(8,128)(2,1)}, u32[]{:S(2)}, u32[]{:S(2)}) %all-to-all-start.1) | async-done | bytes 2097184 | tf_op jit(solution)/shard_map/all_to_all | solution.py:565
  143.7 4.2 %grad_down.1 = f32[24,256,128]{2,1,0:T(8,128)} custom-call(s32[59]{0:T(128)} %copy-done.13, bf16[4,8,256,128]{3,2,1,0:T(8,128)(2,1)} %all-to-all-done.1.piece_ref), custom_call_target="tpu_custom_call" | custom-call | flops 1024 | bytes 1024 | tf_op jit(solution)/shard_map/grad_down/pallas_call | solution.py:343
  147.9 1.5 grad_up.1
  (56 shorter events, 0.5 us)
Async XLA Ops:
  5.3 7.9 %collective-permute-start = (bf16[16,2048]{1,0:T(8,128)(2,1)}, bf16[16,2048]{1,0:T(8,128)(2,1)S(1)}, u32[]{:S(2)}, u32[]{:S(2)}) collective-permute-start(bf16[16,2048]{1,0:T(8,128)(2,1)} %get-tuple-element.35), channel_id=1, source_target_pairs={{0,8},{8,16},{16,24},{24,0},{1,9},{9,17},{17,25},{25,1},{2,10},{10... | collective-permute-start | bytes 196616 | tf_op jit(solution)/shard_map/ppermute | solution.py:39
  8.4 7.3 %collective-permute-start.1 = (bf16[16,2048]{1,0:T(8,128)(2,1)}, bf16[16,2048]{1,0:T(8,128)(2,1)S(1)}, u32[]{:S(2)}, u32[]{:S(2)}) collective-permute-start(bf16[16,2048]{1,0:T(8,128)(2,1)} %get-tuple-element.36), channel_id=1, source_target_pairs={{0,16},{8,24},{16,0},{24,8},{1,17},{9,25},{17,1},{25,9},{2,18},{10... | collective-permute-start | bytes 196616 | tf_op jit(solution)/shard_map/ppermute | solution.py:39
  11.0 4.9 %collective-permute-start.2 = (bf16[16,2048]{1,0:T(8,128)(2,1)}, bf16[16,2048]{1,0:T(8,128)(2,1)S(1)}, u32[]{:S(2)}, u32[]{:S(2)}) collective-permute-start(bf16[16,2048]{1,0:T(8,128)(2,1)} %get-tuple-element.37), channel_id=1, source_target_pairs={{0,24},{8,0},{16,8},{24,16},{1,25},{9,1},{17,9},{25,17},{2,26},{10... | collective-permute-start | bytes 196616 | tf_op jit(solution)/shard_map/ppermute | solution.py:39
  15.9 4.7 %copy-start.6 = (bf16[128,2048]{1,0:T(8,128)(2,1)S(1)}, bf16[128,2048]{1,0:T(8,128)(2,1)}, u32[]{:S(2)}) copy-start(bf16[128,2048]{1,0:T(8,128)(2,1)} %rest_2_.1) | copy-start | bytes 1572868
  15.9 7.9 %copy-start.16 = (s32[32]{0:T(128)S(1)}, s32[32]{0:T(128)}, u32[]{:S(2)}) copy-start(s32[32]{0:T(128)} %tenant_ref.1) | copy-start | bytes 388
  15.9 7.9 %copy-start.17 = (s32[24]{0:T(128)S(1)}, s32[24]{0:T(128)}, u32[]{:S(2)}) copy-start(s32[24]{0:T(128)} %slot_ref.1) | copy-start | bytes 292
  15.9 19.5 %copy-start.2 = (bf16[1024,1024]{1,0:T(8,128)(2,1)S(1)}, bf16[1024,1024]{1,0:T(8,128)(2,1)}, u32[]{:S(2)}) copy-start(bf16[1024,1024]{1,0:T(8,128)(2,1)} %x_ref.1) | copy-start | bytes 6291460
  15.9 70.9 %all-to-all-start = ((bf16[4,2048,128]{2,1,0:T(8,128)(2,1)}), bf16[4,2048,128]{2,1,0:T(8,128)(2,1)}, u32[]{:S(2)}, u32[]{:S(2)}) async-start(bf16[4,2048,128]{2,1,0:T(8,128)(2,1)} %get-tuple-element.38), calls=%async_computation | async-start | bytes 4194304 | tf_op jit(solution)/shard_map/all_to_all | solution.py:528
  20.6 13.5 %collective-permute-start.4 = (bf16[128,2048]{1,0:T(8,128)(2,1)S(1)}, bf16[128,2048]{1,0:T(8,128)(2,1)S(1)}, u32[]{:S(2)}, u32[]{:S(2)}) collective-permute-start(bf16[128,2048]{1,0:T(8,128)(2,1)S(1)} %copy-done.6), channel_id=1, source_target_pairs={{0,4},{2,6},{4,0},{6,2},{1,5},{3,7},{5,1},{7,3},{8,12},{10,14},{12... | collective-permute-start | bytes 1572872 | tf_op jit(solution)/shard_map/ppermute | solution.py:60
  22.3 13.1 %collective-permute-start.3 = (bf16[128,2048]{1,0:T(8,128)(2,1)S(1)}, bf16[128,2048]{1,0:T(8,128)(2,1)}, u32[]{:S(2)}, u32[]{:S(2)}) collective-permute-start(bf16[128,2048]{1,0:T(8,128)(2,1)S(1)} %copy-done.6), channel_id=1, source_target_pairs={{0,2},{2,0},{4,6},{6,4},{1,3},{3,1},{5,7},{7,5},{8,10},{10,8},{12,... | collective-permute-start | bytes 1572872 | tf_op jit(solution)/shard_map/ppermute | solution.py:60
  23.9 107.8 %copy-start.13 = (s32[59]{0:T(128)}, s32[59]{0:T(128)S(1)}, u32[]{:S(2)}) copy-start(s32[59]{0:T(128)S(1)} %concatenate.6.at_ref) | copy-start | bytes 712
  35.4 2.2 %copy-start = (bf16[1024,2048]{1,0:T(8,128)(2,1)S(1)}, bf16[1024,2048]{1,0:T(8,128)(2,1)}, u32[]{:S(2)}) copy-start(bf16[1024,2048]{1,0:T(8,128)(2,1)} %w_ref.5) | copy-start | bytes 12582916
  37.6 5.3 %copy-start.15 = (bf16[16,2048]{1,0:T(8,128)(2,1)S(1)}, bf16[16,2048]{1,0:T(8,128)(2,1)}, u32[]{:S(2)}) copy-start(bf16[16,2048]{1,0:T(8,128)(2,1)} %get-tuple-element.34.rest_0_) | copy-start | bytes 196612
  41.5 20.9 %collective-permute-start.17 = (bf16[2,128,2048]{2,1,0:T(8,128)(2,1)S(1)}, bf16[2,128,2048]{2,1,0:T(8,128)(2,1)S(1)}, u32[]{:S(2)}, u32[]{:S(2)}) collective-permute-start(bf16[2,128,2048]{2,1,0:T(8,128)(2,1)S(1)} %bitcast.73), channel_id=1, source_target_pairs={{0,1},{1,0},{2,3},{3,2},{4,5},{5,4},{6,7},{7,6},{8,9},{9,8},{10,11... | collective-permute-start | bytes 3145736 | tf_op jit(solution)/shard_map/ppermute | solution.py:60
  41.5 21.3 %collective-permute-start.15 = (bf16[2,128,2048]{2,1,0:T(8,128)(2,1)S(1)}, bf16[2,128,2048]{2,1,0:T(8,128)(2,1)S(1)}, u32[]{:S(2)}, u32[]{:S(2)}) collective-permute-start(bf16[2,128,2048]{2,1,0:T(8,128)(2,1)S(1)} %bitcast.72), channel_id=1, source_target_pairs={{0,1},{1,0},{2,3},{3,2},{4,5},{5,4},{6,7},{7,6},{8,9},{9,8},{10,11... | collective-permute-start | bytes 3145736 | tf_op jit(solution)/shard_map/ppermute | solution.py:60
  42.1 18.3 %collective-permute-start.9 = (bf16[64,2048]{1,0:T(8,128)(2,1)S(1)}, bf16[64,2048]{1,0:T(8,128)(2,1)S(1)}, u32[]{:S(2)}, u32[]{:S(2)}) collective-permute-start(bf16[64,2048]{1,0:T(8,128)(2,1)S(1)} %slice.48), channel_id=1, source_target_pairs={{0,2},{2,0},{4,6},{6,4},{1,3},{3,1},{5,7},{7,5},{8,10},{10,8},{12,... | collective-permute-start | bytes 786440 | tf_op jit(solution)/shard_map/ppermute | solution.py:60
  43.8 12.7 %copy-start.11 = (bf16[64,2048]{1,0:T(8,128)(2,1)}, bf16[64,2048]{1,0:T(8,128)(2,1)S(1)}, u32[]{:S(2)}) copy-start(bf16[64,2048]{1,0:T(8,128)(2,1)S(1)} %get-tuple-element.51.b_ref) | copy-start | bytes 786436
  43.8 7.3 %collective-permute-start.7 = (bf16[128,128]{1,0:T(8,128)(2,1)S(1)}, bf16[128,128]{1,0:T(8,128)(2,1)S(1)}, u32[]{:S(2)}, u32[]{:S(2)}) collective-permute-start(bf16[128,128]{1,0:T(8,128)(2,1)S(1)} %get-tuple-element.41), channel_id=1, source_target_pairs={{0,6},{2,4},{4,2},{6,0},{1,7},{3,5},{5,3},{7,1},{8,14},{10,12},{12... | collective-permute-start | bytes 98312 | tf_op jit(solution)/shard_map/ppermute | solution.py:60
  45.1 7.6 %collective-permute-start.6 = (bf16[128,128]{1,0:T(8,128)(2,1)S(1)}, bf16[128,128]{1,0:T(8,128)(2,1)S(1)}, u32[]{:S(2)}, u32[]{:S(2)}) collective-permute-start(bf16[128,128]{1,0:T(8,128)(2,1)S(1)} %get-tuple-element.41), channel_id=1, source_target_pairs={{0,4},{2,6},{4,0},{6,2},{1,5},{3,7},{5,1},{7,3},{8,12},{10,14},{12... | collective-permute-start | bytes 98312 | tf_op jit(solution)/shard_map/ppermute | solution.py:60
  51.1 3.9 %collective-permute-start.5 = (bf16[128,128]{1,0:T(8,128)(2,1)S(1)}, bf16[128,128]{1,0:T(8,128)(2,1)S(1)}, u32[]{:S(2)}, u32[]{:S(2)}) collective-permute-start(bf16[128,128]{1,0:T(8,128)(2,1)S(1)} %get-tuple-element.41), channel_id=1, source_target_pairs={{0,2},{2,0},{4,6},{6,4},{1,3},{3,1},{5,7},{7,5},{8,10},{10,8},{12,... | collective-permute-start | bytes 98312 | tf_op jit(solution)/shard_map/ppermute | solution.py:60
  52.8 13.5 %collective-permute-start.11 = (bf16[128,2048]{1,0:T(8,128)(2,1)S(1)}, bf16[128,2048]{1,0:T(8,128)(2,1)S(1)}, u32[]{:S(2)}, u32[]{:S(2)}) collective-permute-start(bf16[128,2048]{1,0:T(8,128)(2,1)S(1)} %copy-done.6), channel_id=1, source_target_pairs={{0,1},{1,0},{2,3},{3,2},{4,5},{5,4},{6,7},{7,6},{8,9},{9,8},{10,11... | collective-permute-start | bytes 1572872 | tf_op jit(solution)/shard_map/ppermute | solution.py:60
  55.0 6.6 %collective-permute-start.10 = (bf16[64,2048]{1,0:T(8,128)(2,1)S(1)}, bf16[64,2048]{1,0:T(8,128)(2,1)S(1)}, u32[]{:S(2)}, u32[]{:S(2)}) collective-permute-start(bf16[64,2048]{1,0:T(8,128)(2,1)S(1)} %slice.49), channel_id=1, source_target_pairs={{0,4},{2,6},{4,0},{6,2},{1,5},{3,7},{5,1},{7,3},{8,12},{10,14},{12... | collective-permute-start | bytes 786440 | tf_op jit(solution)/shard_map/ppermute | solution.py:60
  60.4 4.6 %collective-permute-start.8 = (bf16[4,128,128]{2,1,0:T(8,128)(2,1)S(1)}, bf16[4,128,128]{2,1,0:T(8,128)(2,1)S(1)}, u32[]{:S(2)}, u32[]{:S(2)}) collective-permute-start(bf16[4,128,128]{2,1,0:T(8,128)(2,1)S(1)} %pad_maximum_fusion.rest_0_), channel_id=1, source_target_pairs={{0,1},{1,0},{2,3},{3,2},{4,5},{5,4},{6,7},{7,6},{8,9},{9,8},{10,11... | collective-permute-start | bytes 393224 | tf_op jit(solution)/shard_map/ppermute | solution.py:60
  61.6 14.2 %collective-permute-start.12 = (bf16[128,2048]{1,0:T(8,128)(2,1)}, bf16[128,2048]{1,0:T(8,128)(2,1)}, u32[]{:S(2)}, u32[]{:S(2)}) collective-permute-start(bf16[128,2048]{1,0:T(8,128)(2,1)} %collective-permute-done.3.rest_1_.rest_3_), channel_id=1, source_target_pairs={{0,1},{1,0},{2,3},{3,2},{4,5},{5,4},{6,7},{7,6},{8,9},{9,8},{10,11... | collective-permute-start | bytes 1572872 | tf_op jit(solution)/shard_map/ppermute | solution.py:60
  62.4 13.3 %collective-permute-start.13 = (bf16[128,2048]{1,0:T(8,128)(2,1)S(1)}, bf16[128,2048]{1,0:T(8,128)(2,1)}, u32[]{:S(2)}, u32[]{:S(2)}) collective-permute-start(bf16[128,2048]{1,0:T(8,128)(2,1)S(1)} %collective-permute-done.4.rest_2_.rest_4_), channel_id=1, source_target_pairs={{0,1},{1,0},{2,3},{3,2},{4,5},{5,4},{6,7},{7,6},{8,9},{9,8},{10,11... | collective-permute-start | bytes 1572872 | tf_op jit(solution)/shard_map/ppermute | solution.py:60
  62.8 12.9 %collective-permute-start.14 = (bf16[128,2048]{1,0:T(8,128)(2,1)}, bf16[128,2048]{1,0:T(8,128)(2,1)}, u32[]{:S(2)}, u32[]{:S(2)}) collective-permute-start(bf16[128,2048]{1,0:T(8,128)(2,1)} %constant_dynamic-update-slice_fusion.rest_3_.rest_5_), channel_id=1, source_target_pairs={{0,1},{1,0},{2,3},{3,2},{4,5},{5,4},{6,7},{7,6},{8,9},{9,8},{10,11... | collective-permute-start | bytes 1572872 | tf_op jit(solution)/shard_map/ppermute | solution.py:60
  65.0 21.8 %collective-permute-start.16 = (bf16[128,2048]{1,0:T(8,128)(2,1)}, bf16[128,2048]{1,0:T(8,128)(2,1)}, u32[]{:S(2)}, u32[]{:S(2)}) collective-permute-start(bf16[128,2048]{1,0:T(8,128)(2,1)} %get-tuple-element.63), channel_id=1, source_target_pairs={{0,2},{2,0},{4,6},{6,4},{1,3},{3,1},{5,7},{7,5},{8,10},{10,8},{12,... | collective-permute-start | bytes 1572872 | tf_op jit(solution)/shard_map/ppermute | solution.py:60
  66.3 0.8 copy-start.8
  67.1 19.7 %collective-permute-start.18 = (bf16[128,2048]{1,0:T(8,128)(2,1)}, bf16[128,2048]{1,0:T(8,128)(2,1)}, u32[]{:S(2)}, u32[]{:S(2)}) collective-permute-start(bf16[128,2048]{1,0:T(8,128)(2,1)} %get-tuple-element.66), channel_id=1, source_target_pairs={{0,4},{2,6},{4,0},{6,2},{1,5},{3,7},{5,1},{7,3},{8,12},{10,14},{12... | collective-permute-start | bytes 1572872 | tf_op jit(solution)/shard_map/ppermute | solution.py:60
  71.1 1.6 %copy-start.5 = (bf16[1024,1024]{1,0:T(8,128)(2,1)S(1)}, bf16[1024,1024]{1,0:T(8,128)(2,1)}, u32[]{:S(2)}) copy-start(bf16[1024,1024]{1,0:T(8,128)(2,1)} %copy.11) | copy-start | bytes 6291460
  72.7 3.1 %copy-start.1 = (bf16[1024,2048]{1,0:T(8,128)(2,1)S(1)}, bf16[1024,2048]{1,0:T(8,128)(2,1)}, u32[]{:S(2)}) copy-start(bf16[1024,2048]{1,0:T(8,128)(2,1)} %w_ref.5) | copy-start | bytes 12582916
  75.8 1.0 copy-start.9
  84.8 2.0 %copy-start.3 = (f32[1024,1024]{1,0:T(8,128)}, f32[1024,1024]{1,0:T(8,128)S(1)}, u32[]{:S(2)}) copy-start(f32[1024,1024]{1,0:T(8,128)S(1)} %cotangent_product.1.base_ref) | copy-start | bytes 12582916
  86.8 56.9 %all-to-all-start.1 = ((bf16[4,8,256,128]{3,2,1,0:T(8,128)(2,1)}), bf16[4,8,256,128]{3,2,1,0:T(8,128)(2,1)}, u32[]{:S(2)}, u32[]{:S(2)}) async-start(bf16[4,8,256,128]{3,2,1,0:T(8,128)(2,1)} %grad_down_pieces.1), calls=%async_computation.1 | async-start | bytes 4194304 | tf_op jit(solution)/shard_map/all_to_all | solution.py:565
  91.5 28.8 %copy-start.10 = (bf16[128,2048]{1,0:T(8,128)(2,1)S(1)}, bf16[128,2048]{1,0:T(8,128)(2,1)}, u32[]{:S(2)}) copy-start(bf16[128,2048]{1,0:T(8,128)(2,1)} %copy-done.8) | copy-start | bytes 1572868
  91.5 14.7 %collective-permute-start.19 = (bf16[128,2048]{1,0:T(8,128)(2,1)}, bf16[128,2048]{1,0:T(8,128)(2,1)S(1)}, u32[]{:S(2)}, u32[]{:S(2)}) collective-permute-start(bf16[128,2048]{1,0:T(8,128)(2,1)} %get-tuple-element.67), channel_id=1, source_target_pairs={{0,6},{2,4},{4,2},{6,0},{1,7},{3,5},{5,3},{7,1},{8,14},{10,12},{12... | collective-permute-start | bytes 1572872 | tf_op jit(solution)/shard_map/ppermute | solution.py:60
  108.5 1.4 collective-permute-start.20
  109.9 7.4 %collective-permute-start.23 = (bf16[4,128,128]{2,1,0:T(8,128)(2,1)S(1)}, bf16[4,128,128]{2,1,0:T(8,128)(2,1)S(1)}, u32[]{:S(2)}, u32[]{:S(2)}) collective-permute-start(bf16[4,128,128]{2,1,0:T(8,128)(2,1)S(1)} %fusion.3), channel_id=1, source_target_pairs={{0,6},{2,4},{4,2},{6,0},{1,7},{3,5},{5,3},{7,1},{8,14},{10,12},{12... | collective-permute-start | bytes 393224 | tf_op jit(solution)/shard_map/ppermute | solution.py:60
  110.7 8.1 %collective-permute-start.22 = (bf16[4,128,128]{2,1,0:T(8,128)(2,1)S(1)}, bf16[4,128,128]{2,1,0:T(8,128)(2,1)S(1)}, u32[]{:S(2)}, u32[]{:S(2)}) collective-permute-start(bf16[4,128,128]{2,1,0:T(8,128)(2,1)S(1)} %fusion.3), channel_id=1, source_target_pairs={{0,4},{2,6},{4,0},{6,2},{1,5},{3,7},{5,1},{7,3},{8,12},{10,14},{12... | collective-permute-start | bytes 393224 | tf_op jit(solution)/shard_map/ppermute | solution.py:60
  112.2 6.5 %collective-permute-start.21 = (bf16[4,128,128]{2,1,0:T(8,128)(2,1)S(1)}, bf16[4,128,128]{2,1,0:T(8,128)(2,1)S(1)}, u32[]{:S(2)}, u32[]{:S(2)}) collective-permute-start(bf16[4,128,128]{2,1,0:T(8,128)(2,1)S(1)} %fusion.3), channel_id=1, source_target_pairs={{0,2},{2,0},{4,6},{6,4},{1,3},{3,1},{5,7},{7,5},{8,10},{10,8},{12,... | collective-permute-start | bytes 393224 | tf_op jit(solution)/shard_map/ppermute | solution.py:60
  118.9 8.3 %copy-start.4 = (f32[1024,1024]{1,0:T(8,128)S(1)}, f32[1024,1024]{1,0:T(8,128)}, u32[]{:S(2)}) copy-start(f32[1024,1024]{1,0:T(8,128)} %copy-done.3) | copy-start | bytes 12582916
  118.9 1.4 collective-permute-start.24
  122.3 25.6 %collective-permute-start.27 = (bf16[8,16,256]{2,1,0:T(8,128)(2,1)S(1)}, bf16[8,16,256]{2,1,0:T(8,128)(2,1)S(1)}, u32[]{:S(2)}, u32[]{:S(2)}) collective-permute-start(bf16[8,16,256]{2,1,0:T(8,128)(2,1)S(1)} %get-tuple-element.68), channel_id=1, source_target_pairs={{0,24},{8,0},{16,8},{24,16},{1,25},{9,1},{17,9},{25,17},{2,26},{10... | collective-permute-start | bytes 196616 | tf_op jit(solution)/shard_map/ppermute | solution.py:39
  125.8 22.1 %collective-permute-start.26 = (bf16[8,16,256]{2,1,0:T(8,128)(2,1)S(1)}, bf16[8,16,256]{2,1,0:T(8,128)(2,1)S(1)}, u32[]{:S(2)}, u32[]{:S(2)}) collective-permute-start(bf16[8,16,256]{2,1,0:T(8,128)(2,1)S(1)} %get-tuple-element.69), channel_id=1, source_target_pairs={{0,16},{8,24},{16,0},{24,8},{1,17},{9,25},{17,1},{25,9},{2,18},{10... | collective-permute-start | bytes 196616 | tf_op jit(solution)/shard_map/ppermute | solution.py:39
  126.2 5.5 %copy-start.7 = (f32[128,2048]{1,0:T(8,128)S(1)}, f32[128,2048]{1,0:T(8,128)}, u32[]{:S(2)}) copy-start(f32[128,2048]{1,0:T(8,128)} %get-tuple-element.62.rest_0_) | copy-start | bytes 3145732
  126.2 5.5 %copy-start.12 = (bf16[64,2048]{1,0:T(8,128)(2,1)S(1)}, bf16[64,2048]{1,0:T(8,128)(2,1)}, u32[]{:S(2)}) copy-start(bf16[64,2048]{1,0:T(8,128)(2,1)} %copy-done.11) | copy-start | bytes 786436
  126.2 21.7 %collective-permute-start.25 = (bf16[8,16,256]{2,1,0:T(8,128)(2,1)S(1)}, bf16[8,16,256]{2,1,0:T(8,128)(2,1)S(1)}, u32[]{:S(2)}, u32[]{:S(2)}) collective-permute-start(bf16[8,16,256]{2,1,0:T(8,128)(2,1)S(1)} %get-tuple-element.70), channel_id=1, source_target_pairs={{0,8},{8,16},{16,24},{24,0},{1,9},{9,17},{17,25},{25,1},{2,10},{10... | collective-permute-start | bytes 196616 | tf_op jit(solution)/shard_map/ppermute | solution.py:39
  134.2 13.8 %copy-start.14 = (s32[59]{0:T(128)S(1)}, s32[59]{0:T(128)}, u32[]{:S(2)}) copy-start(s32[59]{0:T(128)} %copy-done.13) | copy-start | bytes 712

commit v17 on v16

--- a/solution.py
+++ b/solution.py
@@ -60,16 +60,14 @@
     return lax.ppermute(piece, axis, [(i, partner(i, k, count)) for i in range(count)])
 
 
-def gather_chips(piece, behind):
+def gather_chips(piece):
     count = lax.axis_size("pipe")
-    in_halves = count == 4 and piece.shape[0] % 32 == 0
-    came = [swap(piece, "pipe", k) for k in range(1, 3 if in_halves else count)]
-    came, one, two = lax.optimization_barrier((came, behind, behind))
-    if in_halves:
-        half = piece.shape[0] // 2
-        third = [swap(came[1][:half], "pipe", 1), swap(came[0][half:], "pipe", 2)]
-        came = came + [jnp.concatenate(third)]
-    return came, one, two
+    if count != 4 or piece.shape[0] % 32:
+        return [swap(piece, "pipe", k) for k in range(1, count)]
+    first, second = swap(piece, "pipe", 1), swap(piece, "pipe", 2)
+    half = piece.shape[0] // 2
+    third = [swap(second[:half], "pipe", 1), swap(first[half:], "pipe", 2)]
+    return [first, second, jnp.concatenate(third)]
 
 
 def pick(tenant_of_block, slot_of_tenant, adapter_down, adapter_up, group_rows):
@@ -527,10 +525,9 @@
     a_send, b_came = lax.optimization_barrier((a_send, b_came))
     a_recv = lax.all_to_all(a_send, "dp", 0, 0, tiled=True)
 
-    behind, a_send = lax.optimization_barrier((tokens, a_send))
-    cot_chips, base_tokens, x_tokens = gather_chips(cotangent, behind)
-    cot_chips = [cotangent] + cot_chips
-
+    cot_chips = [cotangent] + gather_chips(cotangent)
+
+    base_tokens, a_send = lax.optimization_barrier((tokens, a_send))
     tokens_by_group = base_tokens.reshape(pipe_count, tensor_count, rows, feature_count)
     parts = 2 if pipe_count % 2 == 0 else 1
     chips = pipe_count // parts
@@ -552,20 +549,22 @@
     cot_pieces = [cot_chips] + [
         [swap(piece, "tensor", s) for piece in cot_chips] for s in range(1, tensor_count)
     ]
-    input_base = cotangent_product(at, cot_pieces, key_value_weight)
 
     grad_chips = jnp.stack([grad_rows] + [swap(grad_rows, "pipe", k) for k in range(1, pipe_count)])
     grad_pieces = [grad_chips] + [swap(grad_chips, "tensor", s) for s in range(1, tensor_count)]
-    x_features = x_tokens.T.reshape(data_count, down_rows, tok_dev)
+    x_features = base_tokens.T.reshape(data_count, down_rows, tok_dev)
     down_send = grad_down_pieces(at, x_features, grad_pieces)
 
-    a_recv, down_send, input_base, base_chip_came[:2] = lax.optimization_barrier(
-        (a_recv, down_send, input_base, base_chip_came[:2])
+    a_recv, down_send, cot_pieces, base_chip_came[:2] = lax.optimization_barrier(
+        (a_recv, down_send, cot_pieces, base_chip_came[:2])
     )
     down_recv = lax.all_to_all(down_send, "dp", 0, 0, tiled=True)
+
+    input_base = cotangent_product(at, cot_pieces, key_value_weight)
+    low_down, base_chip_came, input_base = lax.optimization_barrier(
+        (a_recv, base_chip_came, input_base)
+    )
     input_grad = input_gradient(at, input_base, grad_pieces, a_recv)
-
-    low_down, base_chip_came = lax.optimization_barrier((a_recv, base_chip_came))
     low_part = low_product(at, tokens, low_down, pipe_count, tensor_count)
     low_core = sum(
         [low_part[0].astype(jnp.float32)]

time: 150 us -> 141 us (0.940)
  waiting for transfers between devices: 53.6 us -> 41.9 us
    ppermute x22, waiting for transfers between devices: 40.5 us -> 29.4 us  [swap(): lax.ppermute(piece, axis, [(i, partner(i, k, count)) for i in range(count)])]
    unnamed x37 -> x31, local copies, waits for them, and re-layouts: 8.35 us -> 9.26 us
  transfers between devices with their start and end apart: 30 -> 30, of which waited for: 14 -> 14; matrix products, arithmetic and copies ran while one was open for 5% -> 5% of each run, Pallas kernels for 23% -> 25%
where the time goes in v17:
time: 141 us; the launch traced here: 140 us
  waiting for transfers between devices  41.9 us (30%)
  Pallas kernels  41.4 us (29%)
  starting transfers between devices  40.1 us (28%)
  local copies, waits for them, and re-layouts  13.6 us (10%)
  other arithmetic  2.18 us (2%)
    ppermute x22, waiting for transfers between devices, swap(): lax.ppermute(piece, axis, [(i, partner(i, k, count)) for i in range(count)])  29.4 us
    ppermute x22, starting transfers between devices, swap(): lax.ppermute(piece, axis, [(i, partner(i, k, count)) for i in range(count)])  18.4 us
    ppermute x6, starting transfers between devices, shift(): lax.ppermute(piece, axis, [(i, (i + k) % count) for i in range(count)])  12.5 us
    unnamed x31, local copies, waits for them, and re-layouts  9.26 us
    all_to_all x1, waiting for transfers between devices, body(): down_recv = lax.all_to_all(down_send, 'dp', 0, 0, tiled=True)  8.77 us
    pallas_call x1, Pallas kernels, cotangent_product(): call(kernel, 'cotangent_product', grid=(depth // tile,), in_specs=[SMEM,...  7.96 us
    pallas_call x2, Pallas kernels, base_product(): call(kernel, 'base_product', grid_spec=pltpu.PrefetchScalarGridSpec(num_s...  7.73 us
    pallas_call x1, Pallas kernels, pick(): call(kernel, 'pick_rows', VMEM_MOST, out_shape=(up_shape,) * data_count +...  4.84 us
  transfers between devices with their start and end apart: 30, of which 14 were waited for; matrix products, arithmetic and copies ran while one was open for 5% of the time, Pallas kernels for 25%

profile of v17, /device:TPU:0, one launch (start us, length us, event | category | flops | bytes accessed | tf_op | source)
XLA Modules:
  0.0 140.0 jit_solution(15444190561508511781)
XLA Ops:
  0.6 4.8 %pick_rows.1 = (bf16[16,2048]{1,0:T(8,128)(2,1)}, bf16[16,2048]{1,0:T(8,128)(2,1)}, bf16[16,2048]{1,0:T(8,128)(2,1)}, bf16[16,2048]{1,0:T(8,128)(2,1)}, bf16[4,2048,128]{2,1,0:T(8,128)(2,1)}) custom-call(s32[32]{0:T(128)} %tenant_ref.1, s32[24]{0:T(128)} %slot_ref.1, bf16[24,256,128]{2,1,0:T(8,128)(2,1)} %down_ref.1, bf16[24,16,2048]{2,1,0:T(8,128)(2,1)} %up_ref.1), custom_call_target="tpu_custom_call" | custom-call | flops 1024 | bytes 1024 | tf_op jit(solution)/shard_map/pick_rows/pallas_call | solution.py:106
  5.5 3.1 %collective-permute-start = (bf16[16,2048]{1,0:T(8,128)(2,1)}, bf16[16,2048]{1,0:T(8,128)(2,1)S(1)}, u32[]{:S(2)}, u32[]{:S(2)}) collective-permute-start(bf16[16,2048]{1,0:T(8,128)(2,1)} %get-tuple-element.39), channel_id=1, source_target_pairs={{0,8},{8,16},{16,24},{24,0},{1,9},{9,17},{17,25},{25,1},{2,10},{10... | collective-permute-start | bytes 196616 | tf_op jit(solution)/shard_map/ppermute | solution.py:39
  8.6 2.6 %collective-permute-start.1 = (bf16[16,2048]{1,0:T(8,128)(2,1)}, bf16[16,2048]{1,0:T(8,128)(2,1)S(1)}, u32[]{:S(2)}, u32[]{:S(2)}) collective-permute-start(bf16[16,2048]{1,0:T(8,128)(2,1)} %get-tuple-element.40), channel_id=1, source_target_pairs={{0,16},{8,24},{16,0},{24,8},{1,17},{9,25},{17,1},{25,9},{2,18},{10... | collective-permute-start | bytes 196616 | tf_op jit(solution)/shard_map/ppermute | solution.py:39
  11.1 1.3 collective-permute-start.2
  12.5 0.8 collective-permute-done.rest_1_
  13.3 2.7 %collective-permute-done.1.rest_2_ = bf16[16,2048]{1,0:T(8,128)(2,1)S(1)} collective-permute-done((bf16[16,2048]{1,0:T(8,128)(2,1)}, bf16[16,2048]{1,0:T(8,128)(2,1)S(1)}, u32[]{:S(2)}, u32[]{:S(2)}) %collective-permute-start.1) | collective-permute-done | bytes 65568 | tf_op jit(solution)/shard_map/ppermute | solution.py:39
  15.9 0.3 collective-permute-done.2.rest_3_
  16.2 4.7 %all-to-all-start = ((bf16[4,2048,128]{2,1,0:T(8,128)(2,1)}), bf16[4,2048,128]{2,1,0:T(8,128)(2,1)}, u32[]{:S(2)}, u32[]{:S(2)}) async-start(bf16[4,2048,128]{2,1,0:T(8,128)(2,1)} %get-tuple-element.42), calls=%async_computation | async-start | bytes 4194304 | tf_op jit(solution)/shard_map/all_to_all | solution.py:526
  20.9 1.6 %collective-permute-start.8 = (bf16[128,2048]{1,0:T(8,128)(2,1)S(1)}, bf16[128,2048]{1,0:T(8,128)(2,1)S(1)}, u32[]{:S(2)}, u32[]{:S(2)}) collective-permute-start(bf16[128,2048]{1,0:T(8,128)(2,1)S(1)} %copy-done.4), channel_id=1, source_target_pairs={{0,4},{2,6},{4,0},{6,2},{1,5},{3,7},{5,1},{7,3},{8,12},{10,14},{12... | collective-permute-start | bytes 1572872 | tf_op jit(solution)/shard_map/ppermute | solution.py:60
  22.5 1.4 %collective-permute-start.7 = (bf16[128,2048]{1,0:T(8,128)(2,1)S(1)}, bf16[128,2048]{1,0:T(8,128)(2,1)}, u32[]{:S(2)}, u32[]{:S(2)}) collective-permute-start(bf16[128,2048]{1,0:T(8,128)(2,1)S(1)} %copy-done.4), channel_id=1, source_target_pairs={{0,2},{2,0},{4,6},{6,4},{1,3},{3,1},{5,7},{7,5},{8,10},{10,8},{12,... | collective-permute-start | bytes 1572872 | tf_op jit(solution)/shard_map/ppermute | solution.py:60
  23.9 0.1 concatenate.6.at_ref
  24.0 2.2 %copy-done = bf16[1024,2048]{1,0:T(8,128)(2,1)S(1)} copy-done((bf16[1024,2048]{1,0:T(8,128)(2,1)S(1)}, bf16[1024,2048]{1,0:T(8,128)(2,1)}, u32[]{:S(2)}) %copy-start) | copy-done | bytes 4194328
  26.2 3.9 %base_product.3 = (bf16[1,2,128,2048]{3,2,1,0:T(8,128)(2,1)S(1)}, bf16[1,2,128,2048]{3,2,1,0:T(8,128)(2,1)S(1)}) custom-call(s32[59]{0:T(128)S(1)} %concatenate.6.at_ref, bf16[4,2,128,1024]{3,2,1,0:T(8,128)(2,1)S(1)} %bitcast.67, bf16[1024,2048]{1,0:T(8,128)(2,1)S(1)} %copy-done), custom_call_target="tpu_custom_call" | custom-call | flops 1024 | bytes 1024 | tf_op jit(solution)/shard_map/base_product/pallas_call | solution.py:140
  30.2 0.5 collective-permute-start.17
  30.7 3.8 %collective-permute-done.8.rest_2_.rest_4_ = bf16[128,2048]{1,0:T(8,128)(2,1)S(1)} collective-permute-done((bf16[128,2048]{1,0:T(8,128)(2,1)S(1)}, bf16[128,2048]{1,0:T(8,128)(2,1)S(1)}, u32[]{:S(2)}, u32[]{:S(2)}) %collective-permute-start.8) | collective-permute-done | bytes 524320 | tf_op jit(solution)/shard_map/ppermute | solution.py:60
  34.5 1.0 collective-permute-start.9
  35.5 0.9 own_rows.1
  36.5 0.7 copy-done.8
  37.2 1.1 collective-permute-start.3
  38.2 4.1 %collective-permute-done.3 = bf16[128,128]{1,0:T(8,128)(2,1)S(1)} collective-permute-done((bf16[128,128]{1,0:T(8,128)(2,1)S(1)}, bf16[128,128]{1,0:T(8,128)(2,1)S(1)}, u32[]{:S(2)}, u32[]{:S(2)}) %collective-permute-start.3) | collective-permute-done | bytes 32800 | tf_op jit(solution)/shard_map/ppermute | solution.py:60
  42.4 1.0 collective-permute-start.4
  43.4 1.3 collective-permute-start.5
  44.7 3.8 %base_product.2 = bf16[1,4,128,2048]{3,2,1,0:T(8,128)(2,1)S(1)} custom-call(s32[59]{0:T(128)S(1)} %concatenate.6.at_ref, bf16[4,2,128,1024]{3,2,1,0:T(8,128)(2,1)S(1)} %bitcast.68, bf16[1024,2048]{1,0:T(8,128)(2,1)S(1)} %copy-done), custom_call_target="tpu_custom_call" | custom-call | flops 1024 | bytes 1024 | tf_op jit(solution)/shard_map/base_product/pallas_call | solution.py:140
  48.5 1.0 slice.65
  49.5 0.1 collective-permute-start.11
  49.6 1.7 %collective-permute-start.10 = (bf16[64,2048]{1,0:T(8,128)(2,1)S(1)}, bf16[64,2048]{1,0:T(8,128)(2,1)S(1)}, u32[]{:S(2)}, u32[]{:S(2)}) collective-permute-start(bf16[64,2048]{1,0:T(8,128)(2,1)S(1)} %slice.65), channel_id=1, source_target_pairs={{0,4},{2,6},{4,0},{6,2},{1,5},{3,7},{5,1},{7,3},{8,12},{10,14},{12... | collective-permute-start | bytes 786440 | tf_op jit(solution)/shard_map/ppermute | solution.py:60
  51.3 0.2 collective-permute-start.6
  51.5 0.7 constant_dynamic-update-slice_fusion.1
  52.3 6.1 %collective-permute-done.10 = bf16[64,2048]{1,0:T(8,128)(2,1)S(1)} collective-permute-done((bf16[64,2048]{1,0:T(8,128)(2,1)S(1)}, bf16[64,2048]{1,0:T(8,128)(2,1)S(1)}, u32[]{:S(2)}, u32[]{:S(2)}) %collective-permute-start.10) | collective-permute-done | bytes 262176 | tf_op jit(solution)/shard_map/ppermute | solution.py:60
  58.3 0.7 constant_dynamic-update-slice_fusion.rest_3_.rest_5_
  59.1 0.5 collective-permute-start.13
  59.6 2.1 %convert_add_fusion = (f32[128,2048]{1,0:T(8,128)}, bf16[128,2048]{1,0:T(8,128)(2,1)}, bf16[128,2048]{1,0:T(8,128)(2,1)}, bf16[128,2048]{1,0:T(8,128)(2,1)}) fusion(bf16[2,128,2048]{2,1,0:T(8,128)(2,1)S(1)} %collective-permute-done.15, bf16[1,4,128,2048]{3,2,1,0:T(8,128)(2,1)S(1)} %base_product.2, bf16[2,128,2048]{2,1,0:T(8,128)(2,1)S(1)} %collective-permute-done.17), kind=kLoop, calls=%fused_computation | loop fusion | flops 3932160 | bytes 6815744 | tf_op jit(solution)/shard_map/add | solution.py:540
  61.7 1.2 collective-permute-start.16
  62.9 0.8 copy-done.6
  63.7 1.0 collective-permute-start.18
  64.7 2.5 %copy.11 = bf16[1024,1024]{1,0:T(8,128)(2,1)} copy(bf16[1024,1024]{0,1:T(8,128)(2,1)S(1)} %bitcast.69) | data formatting | bytes 4194304 | tf_op jit(solution)/shard_map/transpose | solution.py:555
  67.2 1.6 %copy-done.3 = bf16[1024,1024]{1,0:T(8,128)(2,1)S(1)} copy-done((bf16[1024,1024]{1,0:T(8,128)(2,1)S(1)}, bf16[1024,1024]{1,0:T(8,128)(2,1)}, u32[]{:S(2)}) %copy-start.3) | copy-done | bytes 2097176
  68.8 3.1 %grad_down_pieces.1 = bf16[4,8,256,128]{3,2,1,0:T(8,128)(2,1)} custom-call(s32[59]{0:T(128)S(1)} %concatenate.6.at_ref, bf16[4,256,1024]{2,1,0:T(8,128)(2,1)S(1)} %bitcast.70, bf16[4,128,128]{2,1,0:T(8,128)(2,1)S(1)} %pad_maximum_fusion.rest_0_, bf16[4,128,128]{2,1,0:T(8,128)(2,1)S(1)} %collective-permute-done.6.rest_1_), custom_call_target="tpu_custom_call" | custom-call | flops 1024 | bytes 1024 | tf_op jit(solution)/shard_map/grad_down_pieces/pallas_call | solution.py:295
  71.9 4.4 %collective-permute-done.16.rest_1_ = bf16[128,2048]{1,0:T(8,128)(2,1)} collective-permute-done((bf16[128,2048]{1,0:T(8,128)(2,1)}, bf16[128,2048]{1,0:T(8,128)(2,1)}, u32[]{:S(2)}, u32[]{:S(2)}) %collective-permute-start.16) | collective-permute-done | bytes 524320 | tf_op jit(solution)/shard_map/ppermute | solution.py:60
  76.3 1.7 %collective-permute-done.18.rest_2_ = bf16[128,2048]{1,0:T(8,128)(2,1)} collective-permute-done((bf16[128,2048]{1,0:T(8,128)(2,1)}, bf16[128,2048]{1,0:T(8,128)(2,1)}, u32[]{:S(2)}, u32[]{:S(2)}) %collective-permute-start.18) | collective-permute-done | bytes 524320 | tf_op jit(solution)/shard_map/ppermute | solution.py:60
  78.0 4.4 %all-to-all-start.1 = ((bf16[4,8,256,128]{3,2,1,0:T(8,128)(2,1)}), bf16[4,8,256,128]{3,2,1,0:T(8,128)(2,1)}, u32[]{:S(2)}, u32[]{:S(2)}) async-start(bf16[4,8,256,128]{3,2,1,0:T(8,128)(2,1)} %grad_down_pieces.1), calls=%async_computation.1 | async-start | bytes 4194304 | tf_op jit(solution)/shard_map/all_to_all | solution.py:561
  82.4 2.0 %collective-permute-start.19 = (bf16[128,2048]{1,0:T(8,128)(2,1)}, bf16[128,2048]{1,0:T(8,128)(2,1)S(1)}, u32[]{:S(2)}, u32[]{:S(2)}) collective-permute-start(bf16[128,2048]{1,0:T(8,128)(2,1)} %get-tuple-element.75), channel_id=1, source_target_pairs={{0,6},{2,4},{4,2},{6,0},{1,7},{3,5},{5,3},{7,1},{8,14},{10,12},{12... | collective-permute-start | bytes 1572872 | tf_op jit(solution)/shard_map/ppermute | solution.py:60
  84.4 2.2 %copy-done.1 = bf16[1024,2048]{1,0:T(8,128)(2,1)S(1)} copy-done((bf16[1024,2048]{1,0:T(8,128)(2,1)S(1)}, bf16[1024,2048]{1,0:T(8,128)(2,1)}, u32[]{:S(2)}) %copy-start.1) | copy-done | bytes 4194328
  86.6 1.0 copy-done.7
  87.6 8.0 %cotangent_product.1.base_ref = f32[1024,1024]{1,0:T(8,128)S(1)} custom-call(s32[59]{0:T(128)S(1)} %concatenate.6.at_ref, bf16[1024,2048]{1,0:T(8,128)(2,1)S(1)} %copy-done.1, bf16[128,2048]{1,0:T(8,128)(2,1)S(1)} %copy-done.4, bf16[128,2048]{1,0:T(8,128)(2,1)} %collective-permute-done.7.rest_1_.rest_3_, ...), custom_call_target="tpu_custom_call" | custom-call | flops 1024 | bytes 1024 | tf_op jit(solution)/shard_map/cotangent_product/pallas_call | solution.py:214
  95.6 1.2 collective-permute-done.19.rest_3_
  96.8 2.3 %low_product.1 = bf16[2,4,128,128]{3,2,1,0:T(8,128)(2,1)S(1)} custom-call(s32[59]{0:T(128)S(1)} %concatenate.6.at_ref, bf16[1024,1024]{1,0:T(8,128)(2,1)S(1)} %copy-done.2, bf16[4,2048,128]{2,1,0:T(8,128)(2,1)} %all-to-all-done.a_ref), custom_call_target="tpu_custom_call" | custom-call | flops 1024 | bytes 1024 | tf_op jit(solution)/shard_map/low_product/pallas_call | solution.py:175
  99.2 1.3 collective-permute-done.20
  100.6 0.9 collective-permute-start.21
  101.5 1.6 %collective-permute-start.22 = (bf16[4,128,128]{2,1,0:T(8,128)(2,1)S(1)}, bf16[4,128,128]{2,1,0:T(8,128)(2,1)S(1)}, u32[]{:S(2)}, u32[]{:S(2)}) collective-permute-start(bf16[4,128,128]{2,1,0:T(8,128)(2,1)S(1)} %fusion.3), channel_id=1, source_target_pairs={{0,4},{2,6},{4,0},{6,2},{1,5},{3,7},{5,1},{7,3},{8,12},{10,14},{12... | collective-permute-start | bytes 393224 | tf_op jit(solution)/shard_map/ppermute | solution.py:60
  103.1 1.0 collective-permute-start.23
  104.1 2.9 %collective-permute-done.21 = bf16[4,128,128]{2,1,0:T(8,128)(2,1)S(1)} collective-permute-done((bf16[4,128,128]{2,1,0:T(8,128)(2,1)S(1)}, bf16[4,128,128]{2,1,0:T(8,128)(2,1)S(1)}, u32[]{:S(2)}, u32[]{:S(2)}) %collective-permute-start.21) | collective-permute-done | bytes 131104 | tf_op jit(solution)/shard_map/ppermute | solution.py:60
  107.0 2.6 %collective-permute-done.22 = bf16[4,128,128]{2,1,0:T(8,128)(2,1)S(1)} collective-permute-done((bf16[4,128,128]{2,1,0:T(8,128)(2,1)S(1)}, bf16[4,128,128]{2,1,0:T(8,128)(2,1)S(1)}, u32[]{:S(2)}, u32[]{:S(2)}) %collective-permute-start.22) | collective-permute-done | bytes 131104 | tf_op jit(solution)/shard_map/ppermute | solution.py:60
  109.6 0.1 add_convert_fusion.low_ref.rest_0_
  109.7 1.3 collective-permute-done.24.rest_1_
  111.1 1.9 %grad_up_pieces.1 = bf16[4,8,16,256]{3,2,1,0:T(8,128)(2,1)S(1)} custom-call(s32[59]{0:T(128)S(1)} %concatenate.6.at_ref, bf16[4,128,128]{2,1,0:T(8,128)(2,1)S(1)} %add_convert_fusion.low_ref.rest_0_, bf16[4,128,128]{2,1,0:T(8,128)(2,1)S(1)} %collective-permute-done.24.rest_1_, bf16[128,2048]{1,0:T(8,128)(2,1)S(1)} %copy-done.4, ...), custom_call_target="tpu_custom_call" | custom-call | flops 1024 | bytes 1024 | tf_op jit(solution)/shard_map/grad_up_pieces/pallas_call | solution.py:403
  113.1 2.0 %collective-permute-start.25 = (bf16[8,16,256]{2,1,0:T(8,128)(2,1)S(1)}, bf16[8,16,256]{2,1,0:T(8,128)(2,1)S(1)}, u32[]{:S(2)}, u32[]{:S(2)}) collective-permute-start(bf16[8,16,256]{2,1,0:T(8,128)(2,1)S(1)} %get-tuple-element.78), channel_id=1, source_target_pairs={{0,8},{8,16},{16,24},{24,0},{1,9},{9,17},{17,25},{25,1},{2,10},{10... | collective-permute-start | bytes 196616 | tf_op jit(solution)/shard_map/ppermute | solution.py:39
  115.0 2.1 %collective-permute-start.26 = (bf16[8,16,256]{2,1,0:T(8,128)(2,1)S(1)}, bf16[8,16,256]{2,1,0:T(8,128)(2,1)S(1)}, u32[]{:S(2)}, u32[]{:S(2)}) collective-permute-start(bf16[8,16,256]{2,1,0:T(8,128)(2,1)S(1)} %get-tuple-element.77), channel_id=1, source_target_pairs={{0,16},{8,24},{16,0},{24,8},{1,17},{9,25},{17,1},{25,9},{2,18},{10... | collective-permute-start | bytes 196616 | tf_op jit(solution)/shard_map/ppermute | solution.py:39
  117.1 1.5 %collective-permute-start.27 = (bf16[8,16,256]{2,1,0:T(8,128)(2,1)S(1)}, bf16[8,16,256]{2,1,0:T(8,128)(2,1)S(1)}, u32[]{:S(2)}, u32[]{:S(2)}) collective-permute-start(bf16[8,16,256]{2,1,0:T(8,128)(2,1)S(1)} %get-tuple-element.76), channel_id=1, source_target_pairs={{0,24},{8,0},{16,8},{24,16},{1,25},{9,1},{17,9},{25,17},{2,26},{10... | collective-permute-start | bytes 196616 | tf_op jit(solution)/shard_map/ppermute | solution.py:39
  118.6 4.5 %input_gradient.1 = bf16[1024,1024]{1,0:T(8,128)(2,1)} custom-call(s32[59]{0:T(128)S(1)} %concatenate.6.at_ref, f32[1024,1024]{1,0:T(8,128)S(1)} %cotangent_product.1.base_ref, bf16[4,2048,128]{2,1,0:T(8,128)(2,1)} %all-to-all-done.a_ref, bf16[4,128,128]{2,1,0:T(8,128)(2,1)S(1)} %pad_maximum_fusion.rest_0_, ...), custom_call_target="tpu_custom_call" | custom-call | flops 1024 | bytes 1024 | tf_op jit(solution)/shard_map/input_gradient/pallas_call | solution.py:255
  123.1 2.5 %keys_and_values.1 = bf16[128,2048]{1,0:T(8,128)(2,1)} custom-call(s32[59]{0:T(128)S(1)} %concatenate.6.at_ref, bf16[4,128,128]{2,1,0:T(8,128)(2,1)S(1)} %add_convert_fusion.low_ref.rest_0_, bf16[64,2048]{1,0:T(8,128)(2,1)S(1)} %copy-done.9, f32[128,2048]{1,0:T(8,128)S(1)} %copy-done.5, bf16[128,2048]{1,0:T(8,128)(2,1)} %collective-permute-done.16.rest_1_, ...), custom_call_target="tpu_custom_call" | custom-call | flops 1024 | bytes 1024 | tf_op jit(solution)/shard_map/keys_and_values/pallas_call | solution.py:489
  125.6 8.8 %all-to-all-done.1.piece_ref = bf16[4,8,256,128]{3,2,1,0:T(8,128)(2,1)} async-done(((bf16[4,8,256,128]{3,2,1,0:T(8,128)(2,1)}), bf16[4,8,256,128]{3,2,1,0:T(8,128)(2,1)}, u32[]{:S(2)}, u32[]{:S(2)}) %all-to-all-start.1) | async-done | bytes 2097184 | tf_op jit(solution)/shard_map/all_to_all | solution.py:561
  134.3 4.2 %grad_down.1 = f32[24,256,128]{2,1,0:T(8,128)} custom-call(s32[59]{0:T(128)} %copy-done.10, bf16[4,8,256,128]{3,2,1,0:T(8,128)(2,1)} %all-to-all-done.1.piece_ref), custom_call_target="tpu_custom_call" | custom-call | flops 1024 | bytes 1024 | tf_op jit(solution)/shard_map/grad_down/pallas_call | solution.py:341
  138.6 1.5 %grad_up.1 = f32[24,16,256]{2,1,0:T(8,128)} custom-call(s32[59]{0:T(128)S(1)} %copy-done.11, bf16[8,16,256]{2,1,0:T(8,128)(2,1)S(1)} %get-tuple-element.66.rest_0_, bf16[8,16,256]{2,1,0:T(8,128)(2,1)S(1)} %collective-permute-done.25.rest_1_, bf16[8,16,256]{2,1,0:T(8,128)(2,1)S(1)} %collective-permute-done.26.rest_2_, ...), custom_call_target="tpu_custom_call" | custom-call | flops 1024 | bytes 1024 | tf_op jit(solution)/shard_map/grad_up/pallas_call | solution.py:430
  (50 shorter events, 0.5 us)
Async XLA Ops:
  5.5 7.8 %collective-permute-start = (bf16[16,2048]{1,0:T(8,128)(2,1)}, bf16[16,2048]{1,0:T(8,128)(2,1)S(1)}, u32[]{:S(2)}, u32[]{:S(2)}) collective-permute-start(bf16[16,2048]{1,0:T(8,128)(2,1)} %get-tuple-element.39), channel_id=1, source_target_pairs={{0,8},{8,16},{16,24},{24,0},{1,9},{9,17},{17,25},{25,1},{2,10},{10... | collective-permute-start | bytes 196616 | tf_op jit(solution)/shard_map/ppermute | solution.py:39
  8.6 7.4 %collective-permute-start.1 = (bf16[16,2048]{1,0:T(8,128)(2,1)}, bf16[16,2048]{1,0:T(8,128)(2,1)S(1)}, u32[]{:S(2)}, u32[]{:S(2)}) collective-permute-start(bf16[16,2048]{1,0:T(8,128)(2,1)} %get-tuple-element.40), channel_id=1, source_target_pairs={{0,16},{8,24},{16,0},{24,8},{1,17},{9,25},{17,1},{25,9},{2,18},{10... | collective-permute-start | bytes 196616 | tf_op jit(solution)/shard_map/ppermute | solution.py:39
  11.1 5.0 %collective-permute-start.2 = (bf16[16,2048]{1,0:T(8,128)(2,1)}, bf16[16,2048]{1,0:T(8,128)(2,1)S(1)}, u32[]{:S(2)}, u32[]{:S(2)}) collective-permute-start(bf16[16,2048]{1,0:T(8,128)(2,1)} %get-tuple-element.41), channel_id=1, source_target_pairs={{0,24},{8,0},{16,8},{24,16},{1,25},{9,1},{17,9},{25,17},{2,26},{10... | collective-permute-start | bytes 196616 | tf_op jit(solution)/shard_map/ppermute | solution.py:39
  16.2 4.7 %copy-start.4 = (bf16[128,2048]{1,0:T(8,128)(2,1)S(1)}, bf16[128,2048]{1,0:T(8,128)(2,1)}, u32[]{:S(2)}) copy-start(bf16[128,2048]{1,0:T(8,128)(2,1)} %rest_2_) | copy-start | bytes 1572868
  16.2 7.7 %copy-start.13 = (s32[32]{0:T(128)S(1)}, s32[32]{0:T(128)}, u32[]{:S(2)}) copy-start(s32[32]{0:T(128)} %tenant_ref.1) | copy-start | bytes 388
  16.2 7.7 %copy-start.14 = (s32[24]{0:T(128)S(1)}, s32[24]{0:T(128)}, u32[]{:S(2)}) copy-start(s32[24]{0:T(128)} %slot_ref.1) | copy-start | bytes 292
  16.2 7.8 %copy-start.2 = (bf16[1024,1024]{1,0:T(8,128)(2,1)S(1)}, bf16[1024,1024]{1,0:T(8,128)(2,1)}, u32[]{:S(2)}) copy-start(bf16[1024,1024]{1,0:T(8,128)(2,1)} %x_ref.1) | copy-start | bytes 6291460
  16.2 61.8 %all-to-all-start = ((bf16[4,2048,128]{2,1,0:T(8,128)(2,1)}), bf16[4,2048,128]{2,1,0:T(8,128)(2,1)}, u32[]{:S(2)}, u32[]{:S(2)}) async-start(bf16[4,2048,128]{2,1,0:T(8,128)(2,1)} %get-tuple-element.42), calls=%async_computation | async-start | bytes 4194304 | tf_op jit(solution)/shard_map/all_to_all | solution.py:526
  20.9 13.6 %collective-permute-start.8 = (bf16[128,2048]{1,0:T(8,128)(2,1)S(1)}, bf16[128,2048]{1,0:T(8,128)(2,1)S(1)}, u32[]{:S(2)}, u32[]{:S(2)}) collective-permute-start(bf16[128,2048]{1,0:T(8,128)(2,1)S(1)} %copy-done.4), channel_id=1, source_target_pairs={{0,4},{2,6},{4,0},{6,2},{1,5},{3,7},{5,1},{7,3},{8,12},{10,14},{12... | collective-permute-start | bytes 1572872 | tf_op jit(solution)/shard_map/ppermute | solution.py:60
  22.5 20.9 %collective-permute-start.7 = (bf16[128,2048]{1,0:T(8,128)(2,1)S(1)}, bf16[128,2048]{1,0:T(8,128)(2,1)}, u32[]{:S(2)}, u32[]{:S(2)}) collective-permute-start(bf16[128,2048]{1,0:T(8,128)(2,1)S(1)} %copy-done.4), channel_id=1, source_target_pairs={{0,2},{2,0},{4,6},{6,4},{1,3},{3,1},{5,7},{7,5},{8,10},{10,8},{12,... | collective-permute-start | bytes 1572872 | tf_op jit(solution)/shard_map/ppermute | solution.py:60
  24.0 99.1 %copy-start.10 = (s32[59]{0:T(128)}, s32[59]{0:T(128)S(1)}, u32[]{:S(2)}) copy-start(s32[59]{0:T(128)S(1)} %concatenate.6.at_ref) | copy-start | bytes 712
  24.0 2.2 %copy-start = (bf16[1024,2048]{1,0:T(8,128)(2,1)S(1)}, bf16[1024,2048]{1,0:T(8,128)(2,1)}, u32[]{:S(2)}) copy-start(bf16[1024,2048]{1,0:T(8,128)(2,1)} %w_ref.5) | copy-start | bytes 12582916
  26.2 9.3 %copy-start.12 = (bf16[16,2048]{1,0:T(8,128)(2,1)S(1)}, bf16[16,2048]{1,0:T(8,128)(2,1)}, u32[]{:S(2)}) copy-start(bf16[16,2048]{1,0:T(8,128)(2,1)} %get-tuple-element.38.rest_0_) | copy-start | bytes 196612
  30.1 29.0 %collective-permute-start.15 = (bf16[2,128,2048]{2,1,0:T(8,128)(2,1)S(1)}, bf16[2,128,2048]{2,1,0:T(8,128)(2,1)S(1)}, u32[]{:S(2)}, u32[]{:S(2)}) collective-permute-start(bf16[2,128,2048]{2,1,0:T(8,128)(2,1)S(1)} %bitcast.73), channel_id=1, source_target_pairs={{0,1},{1,0},{2,3},{3,2},{4,5},{5,4},{6,7},{7,6},{8,9},{9,8},{10,11... | collective-permute-start | bytes 3145736 | tf_op jit(solution)/shard_map/ppermute | solution.py:60
  30.2 29.4 %collective-permute-start.17 = (bf16[2,128,2048]{2,1,0:T(8,128)(2,1)S(1)}, bf16[2,128,2048]{2,1,0:T(8,128)(2,1)S(1)}, u32[]{:S(2)}, u32[]{:S(2)}) collective-permute-start(bf16[2,128,2048]{2,1,0:T(8,128)(2,1)S(1)} %bitcast.72), channel_id=1, source_target_pairs={{0,1},{1,0},{2,3},{3,2},{4,5},{5,4},{6,7},{7,6},{8,9},{9,8},{10,11... | collective-permute-start | bytes 3145736 | tf_op jit(solution)/shard_map/ppermute | solution.py:60
  34.5 16.8 %collective-permute-start.9 = (bf16[64,2048]{1,0:T(8,128)(2,1)S(1)}, bf16[64,2048]{1,0:T(8,128)(2,1)S(1)}, u32[]{:S(2)}, u32[]{:S(2)}) collective-permute-start(bf16[64,2048]{1,0:T(8,128)(2,1)S(1)} %slice.64), channel_id=1, source_target_pairs={{0,2},{2,0},{4,6},{6,4},{1,3},{3,1},{5,7},{7,5},{8,10},{10,8},{12,... | collective-permute-start | bytes 786440 | tf_op jit(solution)/shard_map/ppermute | solution.py:60
  36.5 0.7 copy-start.8
  37.2 5.2 %collective-permute-start.3 = (bf16[128,128]{1,0:T(8,128)(2,1)S(1)}, bf16[128,128]{1,0:T(8,128)(2,1)S(1)}, u32[]{:S(2)}, u32[]{:S(2)}) collective-permute-start(bf16[128,128]{1,0:T(8,128)(2,1)S(1)} %get-tuple-element.44), channel_id=1, source_target_pairs={{0,2},{2,0},{4,6},{6,4},{1,3},{3,1},{5,7},{7,5},{8,10},{10,8},{12,... | collective-permute-start | bytes 98312 | tf_op jit(solution)/shard_map/ppermute | solution.py:60
  42.4 7.2 %collective-permute-start.4 = (bf16[128,128]{1,0:T(8,128)(2,1)S(1)}, bf16[128,128]{1,0:T(8,128)(2,1)S(1)}, u32[]{:S(2)}, u32[]{:S(2)}) collective-permute-start(bf16[128,128]{1,0:T(8,128)(2,1)S(1)} %get-tuple-element.44), channel_id=1, source_target_pairs={{0,4},{2,6},{4,0},{6,2},{1,5},{3,7},{5,1},{7,3},{8,12},{10,14},{12... | collective-permute-start | bytes 98312 | tf_op jit(solution)/shard_map/ppermute | solution.py:60
  43.4 6.2 %collective-permute-start.5 = (bf16[128,128]{1,0:T(8,128)(2,1)S(1)}, bf16[128,128]{1,0:T(8,128)(2,1)S(1)}, u32[]{:S(2)}, u32[]{:S(2)}) collective-permute-start(bf16[128,128]{1,0:T(8,128)(2,1)S(1)} %get-tuple-element.44), channel_id=1, source_target_pairs={{0,6},{2,4},{4,2},{6,0},{1,7},{3,5},{5,3},{7,1},{8,14},{10,12},{12... | collective-permute-start | bytes 98312 | tf_op jit(solution)/shard_map/ppermute | solution.py:60
  49.5 13.3 %collective-permute-start.11 = (bf16[128,2048]{1,0:T(8,128)(2,1)S(1)}, bf16[128,2048]{1,0:T(8,128)(2,1)S(1)}, u32[]{:S(2)}, u32[]{:S(2)}) collective-permute-start(bf16[128,2048]{1,0:T(8,128)(2,1)S(1)} %copy-done.4), channel_id=1, source_target_pairs={{0,1},{1,0},{2,3},{3,2},{4,5},{5,4},{6,7},{7,6},{8,9},{9,8},{10,11... | collective-permute-start | bytes 1572872 | tf_op jit(solution)/shard_map/ppermute | solution.py:60
  49.6 8.7 %collective-permute-start.10 = (bf16[64,2048]{1,0:T(8,128)(2,1)S(1)}, bf16[64,2048]{1,0:T(8,128)(2,1)S(1)}, u32[]{:S(2)}, u32[]{:S(2)}) collective-permute-start(bf16[64,2048]{1,0:T(8,128)(2,1)S(1)} %slice.65), channel_id=1, source_target_pairs={{0,4},{2,6},{4,0},{6,2},{1,5},{3,7},{5,1},{7,3},{8,12},{10,14},{12... | collective-permute-start | bytes 786440 | tf_op jit(solution)/shard_map/ppermute | solution.py:60
  51.3 10.4 %collective-permute-start.6 = (bf16[4,128,128]{2,1,0:T(8,128)(2,1)S(1)}, bf16[4,128,128]{2,1,0:T(8,128)(2,1)S(1)}, u32[]{:S(2)}, u32[]{:S(2)}) collective-permute-start(bf16[4,128,128]{2,1,0:T(8,128)(2,1)S(1)} %pad_maximum_fusion.rest_0_), channel_id=1, source_target_pairs={{0,1},{1,0},{2,3},{3,2},{4,5},{5,4},{6,7},{7,6},{8,9},{9,8},{10,11... | collective-permute-start | bytes 393224 | tf_op jit(solution)/shard_map/ppermute | solution.py:60
  58.3 13.6 %collective-permute-start.12 = (bf16[128,2048]{1,0:T(8,128)(2,1)}, bf16[128,2048]{1,0:T(8,128)(2,1)}, u32[]{:S(2)}, u32[]{:S(2)}) collective-permute-start(bf16[128,2048]{1,0:T(8,128)(2,1)} %collective-permute-done.7.rest_1_.rest_3_), channel_id=1, source_target_pairs={{0,1},{1,0},{2,3},{3,2},{4,5},{5,4},{6,7},{7,6},{8,9},{9,8},{10,11... | collective-permute-start | bytes 1572872 | tf_op jit(solution)/shard_map/ppermute | solution.py:60
  59.1 12.8 %collective-permute-start.13 = (bf16[128,2048]{1,0:T(8,128)(2,1)S(1)}, bf16[128,2048]{1,0:T(8,128)(2,1)}, u32[]{:S(2)}, u32[]{:S(2)}) collective-permute-start(bf16[128,2048]{1,0:T(8,128)(2,1)S(1)} %collective-permute-done.8.rest_2_.rest_4_), channel_id=1, source_target_pairs={{0,1},{1,0},{2,3},{3,2},{4,5},{5,4},{6,7},{7,6},{8,9},{9,8},{10,11... | collective-permute-start | bytes 1572872 | tf_op jit(solution)/shard_map/ppermute | solution.py:60
  59.6 12.3 %collective-permute-start.14 = (bf16[128,2048]{1,0:T(8,128)(2,1)}, bf16[128,2048]{1,0:T(8,128)(2,1)}, u32[]{:S(2)}, u32[]{:S(2)}) collective-permute-start(bf16[128,2048]{1,0:T(8,128)(2,1)} %constant_dynamic-update-slice_fusion.rest_3_.rest_5_), channel_id=1, source_target_pairs={{0,1},{1,0},{2,3},{3,2},{4,5},{5,4},{6,7},{7,6},{8,9},{9,8},{10,11... | collective-permute-start | bytes 1572872 | tf_op jit(solution)/shard_map/ppermute | solution.py:60
  61.7 14.6 %collective-permute-start.16 = (bf16[128,2048]{1,0:T(8,128)(2,1)}, bf16[128,2048]{1,0:T(8,128)(2,1)}, u32[]{:S(2)}, u32[]{:S(2)}) collective-permute-start(bf16[128,2048]{1,0:T(8,128)(2,1)} %get-tuple-element.71), channel_id=1, source_target_pairs={{0,2},{2,0},{4,6},{6,4},{1,3},{3,1},{5,7},{7,5},{8,10},{10,8},{12,... | collective-permute-start | bytes 1572872 | tf_op jit(solution)/shard_map/ppermute | solution.py:60
  62.9 0.8 copy-start.6
  63.7 14.3 %collective-permute-start.18 = (bf16[128,2048]{1,0:T(8,128)(2,1)}, bf16[128,2048]{1,0:T(8,128)(2,1)}, u32[]{:S(2)}, u32[]{:S(2)}) collective-permute-start(bf16[128,2048]{1,0:T(8,128)(2,1)} %get-tuple-element.74), channel_id=1, source_target_pairs={{0,4},{2,6},{4,0},{6,2},{1,5},{3,7},{5,1},{7,3},{8,12},{10,14},{12... | collective-permute-start | bytes 1572872 | tf_op jit(solution)/shard_map/ppermute | solution.py:60
  67.2 1.6 %copy-start.3 = (bf16[1024,1024]{1,0:T(8,128)(2,1)S(1)}, bf16[1024,1024]{1,0:T(8,128)(2,1)}, u32[]{:S(2)}) copy-start(bf16[1024,1024]{1,0:T(8,128)(2,1)} %copy.11) | copy-start | bytes 6291460
  78.0 56.4 %all-to-all-start.1 = ((bf16[4,8,256,128]{3,2,1,0:T(8,128)(2,1)}), bf16[4,8,256,128]{3,2,1,0:T(8,128)(2,1)}, u32[]{:S(2)}, u32[]{:S(2)}) async-start(bf16[4,8,256,128]{3,2,1,0:T(8,128)(2,1)} %grad_down_pieces.1), calls=%async_computation.1 | async-start | bytes 4194304 | tf_op jit(solution)/shard_map/all_to_all | solution.py:561
  82.4 14.3 %collective-permute-start.19 = (bf16[128,2048]{1,0:T(8,128)(2,1)}, bf16[128,2048]{1,0:T(8,128)(2,1)S(1)}, u32[]{:S(2)}, u32[]{:S(2)}) collective-permute-start(bf16[128,2048]{1,0:T(8,128)(2,1)} %get-tuple-element.75), channel_id=1, source_target_pairs={{0,6},{2,4},{4,2},{6,0},{1,7},{3,5},{5,3},{7,1},{8,14},{10,12},{12... | collective-permute-start | bytes 1572872 | tf_op jit(solution)/shard_map/ppermute | solution.py:60
  84.4 2.2 %copy-start.1 = (bf16[1024,2048]{1,0:T(8,128)(2,1)S(1)}, bf16[1024,2048]{1,0:T(8,128)(2,1)}, u32[]{:S(2)}) copy-start(bf16[1024,2048]{1,0:T(8,128)(2,1)} %w_ref.5) | copy-start | bytes 12582916
  86.6 1.0 copy-start.7
  99.1 1.4 %collective-permute-start.20 = (bf16[4,128,128]{2,1,0:T(8,128)(2,1)S(1)}, bf16[4,128,128]{2,1,0:T(8,128)(2,1)S(1)}, u32[]{:S(2)}, u32[]{:S(2)}) collective-permute-start(bf16[4,128,128]{2,1,0:T(8,128)(2,1)S(1)} %slice_bitcast_fusion.8), channel_id=1, source_target_pairs={{0,1},{1,0},{2,3},{3,2},{4,5},{5,4},{6,7},{7,6},{8,9},{9,8},{10,11... | collective-permute-start | bytes 393224 | tf_op jit(solution)/shard_map/ppermute | solution.py:60
  100.6 6.4 %collective-permute-start.21 = (bf16[4,128,128]{2,1,0:T(8,128)(2,1)S(1)}, bf16[4,128,128]{2,1,0:T(8,128)(2,1)S(1)}, u32[]{:S(2)}, u32[]{:S(2)}) collective-permute-start(bf16[4,128,128]{2,1,0:T(8,128)(2,1)S(1)} %fusion.3), channel_id=1, source_target_pairs={{0,2},{2,0},{4,6},{6,4},{1,3},{3,1},{5,7},{7,5},{8,10},{10,8},{12,... | collective-permute-start | bytes 393224 | tf_op jit(solution)/shard_map/ppermute | solution.py:60
  101.5 8.1 %collective-permute-start.22 = (bf16[4,128,128]{2,1,0:T(8,128)(2,1)S(1)}, bf16[4,128,128]{2,1,0:T(8,128)(2,1)S(1)}, u32[]{:S(2)}, u32[]{:S(2)}) collective-permute-start(bf16[4,128,128]{2,1,0:T(8,128)(2,1)S(1)} %fusion.3), channel_id=1, source_target_pairs={{0,4},{2,6},{4,0},{6,2},{1,5},{3,7},{5,1},{7,3},{8,12},{10,14},{12... | collective-permute-start | bytes 393224 | tf_op jit(solution)/shard_map/ppermute | solution.py:60
  103.1 6.5 %collective-permute-start.23 = (bf16[4,128,128]{2,1,0:T(8,128)(2,1)S(1)}, bf16[4,128,128]{2,1,0:T(8,128)(2,1)S(1)}, u32[]{:S(2)}, u32[]{:S(2)}) collective-permute-start(bf16[4,128,128]{2,1,0:T(8,128)(2,1)S(1)} %fusion.3), channel_id=1, source_target_pairs={{0,6},{2,4},{4,2},{6,0},{1,7},{3,5},{5,3},{7,1},{8,14},{10,12},{12... | collective-permute-start | bytes 393224 | tf_op jit(solution)/shard_map/ppermute | solution.py:60
  109.7 1.4 %collective-permute-start.24 = (bf16[4,128,128]{2,1,0:T(8,128)(2,1)S(1)}, bf16[4,128,128]{2,1,0:T(8,128)(2,1)S(1)}, u32[]{:S(2)}, u32[]{:S(2)}) collective-permute-start(bf16[4,128,128]{2,1,0:T(8,128)(2,1)S(1)} %add_convert_fusion.low_ref.rest_0_), channel_id=1, source_target_pairs={{0,1},{1,0},{2,3},{3,2},{4,5},{5,4},{6,7},{7,6},{8,9},{9,8},{10,11... | collective-permute-start | bytes 393224 | tf_op jit(solution)/shard_map/ppermute | solution.py:60
  113.1 25.5 %collective-permute-start.25 = (bf16[8,16,256]{2,1,0:T(8,128)(2,1)S(1)}, bf16[8,16,256]{2,1,0:T(8,128)(2,1)S(1)}, u32[]{:S(2)}, u32[]{:S(2)}) collective-permute-start(bf16[8,16,256]{2,1,0:T(8,128)(2,1)S(1)} %get-tuple-element.78), channel_id=1, source_target_pairs={{0,8},{8,16},{16,24},{24,0},{1,9},{9,17},{17,25},{25,1},{2,10},{10... | collective-permute-start | bytes 196616 | tf_op jit(solution)/shard_map/ppermute | solution.py:39
  115.0 23.5 %collective-permute-start.26 = (bf16[8,16,256]{2,1,0:T(8,128)(2,1)S(1)}, bf16[8,16,256]{2,1,0:T(8,128)(2,1)S(1)}, u32[]{:S(2)}, u32[]{:S(2)}) collective-permute-start(bf16[8,16,256]{2,1,0:T(8,128)(2,1)S(1)} %get-tuple-element.77), channel_id=1, source_target_pairs={{0,16},{8,24},{16,0},{24,8},{1,17},{9,25},{17,1},{25,9},{2,18},{10... | collective-permute-start | bytes 196616 | tf_op jit(solution)/shard_map/ppermute | solution.py:39
  117.1 6.0 %copy-start.5 = (f32[128,2048]{1,0:T(8,128)S(1)}, f32[128,2048]{1,0:T(8,128)}, u32[]{:S(2)}) copy-start(f32[128,2048]{1,0:T(8,128)} %get-tuple-element.70.rest_0_) | copy-start | bytes 3145732
  117.1 6.0 %copy-start.9 = (bf16[64,2048]{1,0:T(8,128)(2,1)S(1)}, bf16[64,2048]{1,0:T(8,128)(2,1)}, u32[]{:S(2)}) copy-start(bf16[64,2048]{1,0:T(8,128)(2,1)} %copy-done.8) | copy-start | bytes 786436
  117.1 21.4 %collective-permute-start.27 = (bf16[8,16,256]{2,1,0:T(8,128)(2,1)S(1)}, bf16[8,16,256]{2,1,0:T(8,128)(2,1)S(1)}, u32[]{:S(2)}, u32[]{:S(2)}) collective-permute-start(bf16[8,16,256]{2,1,0:T(8,128)(2,1)S(1)} %get-tuple-element.76), channel_id=1, source_target_pairs={{0,24},{8,0},{16,8},{24,16},{1,25},{9,1},{17,9},{25,17},{2,26},{10... | collective-permute-start | bytes 196616 | tf_op jit(solution)/shard_map/ppermute | solution.py:39
  125.6 13.0 %copy-start.11 = (s32[59]{0:T(128)S(1)}, s32[59]{0:T(128)}, u32[]{:S(2)}) copy-start(s32[59]{0:T(128)} %copy-done.10) | copy-start | bytes 712

commit v18 on v17

--- a/solution.py
+++ b/solution.py
@@ -555,8 +555,8 @@
     x_features = base_tokens.T.reshape(data_count, down_rows, tok_dev)
     down_send = grad_down_pieces(at, x_features, grad_pieces)
 
-    a_recv, down_send, cot_pieces, base_chip_came[:2] = lax.optimization_barrier(
-        (a_recv, down_send, cot_pieces, base_chip_came[:2])
+    a_recv, down_send, cot_pieces, base_chip = lax.optimization_barrier(
+        (a_recv, down_send, cot_pieces, base_chip)
     )
     down_recv = lax.all_to_all(down_send, "dp", 0, 0, tiled=True)
 

time: 141 us -> 141 us (level)
  waiting for transfers between devices: 41.9 us -> 31.1 us
  local copies, waits for them, and re-layouts: 13.6 us -> 23.1 us
  Pallas kernels: 41.4 us -> 39.6 us
  other arithmetic: 2.18 us -> 3.76 us
    all_to_all x1, waiting for transfers between devices: 8.77 us -> 0.01 us  [body(): down_recv = lax.all_to_all(down_send, 'dp', 0, 0, tiled=True)]
    unnamed x31 -> x57, local copies, waits for them, and re-layouts: 9.26 us -> 18 us
    convert_element_type x0 -> x1, other arithmetic: none -> 3.63 us  [body(): base_chip[1:] = [piece.astype(jnp.bfloat16) for piece in base_chip[1:]]]
    add x1 -> x0, other arithmetic: 2.05 us -> none  [body(): sum([base_keep[0, k].astype(jnp.float32)] + [came[k // chips][k % chips]....]
    ppermute x22, waiting for transfers between devices: 29.4 us -> 27.5 us  [swap(): lax.ppermute(piece, axis, [(i, partner(i, k, count)) for i in range(count)])]
    pallas_call x1, Pallas kernels: 7.96 us -> 6.53 us  [cotangent_product(): call(kernel, 'cotangent_product', grid=(depth // tile,), in_specs=[SMEM,...]
  transfers between devices with their start and end apart: 30 -> 30, of which waited for: 14 -> 10; matrix products, arithmetic and copies ran while one was open for 5% -> 7% of each run, Pallas kernels for 25% -> 24%
where the time goes in v18:
time: 141 us; the launch traced here: 140 us
  starting transfers between devices  41.1 us (29%)
  Pallas kernels  39.6 us (28%)
  waiting for transfers between devices  31.1 us (22%)
  local copies, waits for them, and re-layouts  23.1 us (16%)
  other arithmetic  3.76 us (3%)
    ppermute x22, waiting for transfers between devices, swap(): lax.ppermute(piece, axis, [(i, partner(i, k, count)) for i in range(count)])  27.5 us
    ppermute x22, starting transfers between devices, swap(): lax.ppermute(piece, axis, [(i, partner(i, k, count)) for i in range(count)])  18.8 us
    unnamed x57, local copies, waits for them, and re-layouts  18 us
    ppermute x6, starting transfers between devices, shift(): lax.ppermute(piece, axis, [(i, (i + k) % count) for i in range(count)])  12.6 us
    pallas_call x2, Pallas kernels, base_product(): call(kernel, 'base_product', grid_spec=pltpu.PrefetchScalarGridSpec(num_s...  8.64 us
    pallas_call x1, Pallas kernels, cotangent_product(): call(kernel, 'cotangent_product', grid=(depth // tile,), in_specs=[SMEM,...  6.53 us
    pallas_call x1, Pallas kernels, pick(): call(kernel, 'pick_rows', VMEM_MOST, out_shape=(up_shape,) * data_count +...  5.03 us
    all_to_all x1, starting transfers between devices, body(): down_recv = lax.all_to_all(down_send, 'dp', 0, 0, tiled=True)  4.98 us
  transfers between devices with their start and end apart: 30, of which 10 were waited for; matrix products, arithmetic and copies ran while one was open for 7% of the time, Pallas kernels for 24%

profile of v18, /device:TPU:0, one launch (start us, length us, event | category | flops | bytes accessed | tf_op | source)
XLA Modules:
  0.0 139.6 jit_solution(965912635596934109)
XLA Ops:
  0.6 5.0 %pick_rows.1 = (bf16[16,2048]{1,0:T(8,128)(2,1)}, bf16[16,2048]{1,0:T(8,128)(2,1)}, bf16[16,2048]{1,0:T(8,128)(2,1)}, bf16[16,2048]{1,0:T(8,128)(2,1)}, bf16[4,2048,128]{2,1,0:T(8,128)(2,1)}) custom-call(s32[32]{0:T(128)} %tenant_ref.1, s32[24]{0:T(128)} %slot_ref.1, bf16[24,256,128]{2,1,0:T(8,128)(2,1)} %down_ref.1, bf16[24,16,2048]{2,1,0:T(8,128)(2,1)} %up_ref.1), custom_call_target="tpu_custom_call" | custom-call | flops 1024 | bytes 1024 | tf_op jit(solution)/shard_map/pick_rows/pallas_call | solution.py:106
  5.7 3.1 %collective-permute-start = (bf16[16,2048]{1,0:T(8,128)(2,1)}, bf16[16,2048]{1,0:T(8,128)(2,1)S(1)}, u32[]{:S(2)}, u32[]{:S(2)}) collective-permute-start(bf16[16,2048]{1,0:T(8,128)(2,1)} %get-tuple-element.38), channel_id=1, source_target_pairs={{0,8},{8,16},{16,24},{24,0},{1,9},{9,17},{17,25},{25,1},{2,10},{10... | collective-permute-start | bytes 196616 | tf_op jit(solution)/shard_map/ppermute | solution.py:39
  8.7 2.6 %collective-permute-start.1 = (bf16[16,2048]{1,0:T(8,128)(2,1)}, bf16[16,2048]{1,0:T(8,128)(2,1)S(1)}, u32[]{:S(2)}, u32[]{:S(2)}) collective-permute-start(bf16[16,2048]{1,0:T(8,128)(2,1)} %get-tuple-element.39), channel_id=1, source_target_pairs={{0,16},{8,24},{16,0},{24,8},{1,17},{9,25},{17,1},{25,9},{2,18},{10... | collective-permute-start | bytes 196616 | tf_op jit(solution)/shard_map/ppermute | solution.py:39
  11.3 1.3 collective-permute-start.2
  12.7 0.8 collective-permute-done.rest_1_
  13.5 2.5 %collective-permute-done.1.rest_2_ = bf16[16,2048]{1,0:T(8,128)(2,1)S(1)} collective-permute-done((bf16[16,2048]{1,0:T(8,128)(2,1)}, bf16[16,2048]{1,0:T(8,128)(2,1)S(1)}, u32[]{:S(2)}, u32[]{:S(2)}) %collective-permute-start.1) | collective-permute-done | bytes 65568 | tf_op jit(solution)/shard_map/ppermute | solution.py:39
  16.3 4.7 %all-to-all-start = ((bf16[4,2048,128]{2,1,0:T(8,128)(2,1)}), bf16[4,2048,128]{2,1,0:T(8,128)(2,1)}, u32[]{:S(2)}, u32[]{:S(2)}) async-start(bf16[4,2048,128]{2,1,0:T(8,128)(2,1)} %get-tuple-element.41), calls=%async_computation | async-start | bytes 4194304 | tf_op jit(solution)/shard_map/all_to_all | solution.py:526
  21.0 1.7 %collective-permute-start.8 = (bf16[128,2048]{1,0:T(8,128)(2,1)S(1)}, bf16[128,2048]{1,0:T(8,128)(2,1)S(1)}, u32[]{:S(2)}, u32[]{:S(2)}) collective-permute-start(bf16[128,2048]{1,0:T(8,128)(2,1)S(1)} %copy-done.6), channel_id=1, source_target_pairs={{0,4},{2,6},{4,0},{6,2},{1,5},{3,7},{5,1},{7,3},{8,12},{10,14},{12... | collective-permute-start | bytes 1572872 | tf_op jit(solution)/shard_map/ppermute | solution.py:60
  22.8 2.2 %copy-done = bf16[1024,2048]{1,0:T(8,128)(2,1)S(1)} copy-done((bf16[1024,2048]{1,0:T(8,128)(2,1)S(1)}, bf16[1024,2048]{1,0:T(8,128)(2,1)}, u32[]{:S(2)}) %copy-start) | copy-done | bytes 4194328
  25.0 4.8 %base_product.3 = (bf16[1,2,128,2048]{3,2,1,0:T(8,128)(2,1)}, bf16[1,2,128,2048]{3,2,1,0:T(8,128)(2,1)}) custom-call(s32[59]{0:T(128)S(1)} %concatenate.6.at_ref, bf16[4,2,128,1024]{3,2,1,0:T(8,128)(2,1)S(1)} %bitcast.67, bf16[1024,2048]{1,0:T(8,128)(2,1)S(1)} %copy-done), custom_call_target="tpu_custom_call" | custom-call | flops 1024 | bytes 1024 | tf_op jit(solution)/shard_map/base_product/pallas_call | solution.py:140
  29.8 0.5 collective-permute-start.16
  30.3 1.5 %collective-permute-start.7 = (bf16[128,2048]{1,0:T(8,128)(2,1)S(1)}, bf16[128,2048]{1,0:T(8,128)(2,1)S(1)}, u32[]{:S(2)}, u32[]{:S(2)}) collective-permute-start(bf16[128,2048]{1,0:T(8,128)(2,1)S(1)} %copy-done.6), channel_id=1, source_target_pairs={{0,2},{2,0},{4,6},{6,4},{1,3},{3,1},{5,7},{7,5},{8,10},{10,8},{12,... | collective-permute-start | bytes 1572872 | tf_op jit(solution)/shard_map/ppermute | solution.py:60
  31.8 0.9 own_rows.1
  32.7 0.6 collective-permute-start.3
  33.3 11.5 %collective-permute-done.3 = bf16[128,128]{1,0:T(8,128)(2,1)S(1)} collective-permute-done((bf16[128,128]{1,0:T(8,128)(2,1)S(1)}, bf16[128,128]{1,0:T(8,128)(2,1)S(1)}, u32[]{:S(2)}, u32[]{:S(2)}) %collective-permute-start.3) | collective-permute-done | bytes 32800 | tf_op jit(solution)/shard_map/ppermute | solution.py:60
  44.8 0.4 collective-permute-start.4
  45.3 2.5 %collective-permute-start.5 = (bf16[128,128]{1,0:T(8,128)(2,1)S(1)}, bf16[128,128]{1,0:T(8,128)(2,1)S(1)}, u32[]{:S(2)}, u32[]{:S(2)}) collective-permute-start(bf16[128,128]{1,0:T(8,128)(2,1)S(1)} %get-tuple-element.43), channel_id=1, source_target_pairs={{0,6},{2,4},{4,2},{6,0},{1,7},{3,5},{5,3},{7,1},{8,14},{10,12},{12... | collective-permute-start | bytes 98312 | tf_op jit(solution)/shard_map/ppermute | solution.py:60
  47.8 0.7 slice.64
  48.8 1.5 %collective-permute-start.9 = (bf16[64,2048]{1,0:T(8,128)(2,1)}, bf16[64,2048]{1,0:T(8,128)(2,1)}, u32[]{:S(2)}, u32[]{:S(2)}) collective-permute-start(bf16[64,2048]{1,0:T(8,128)(2,1)} %slice.64), channel_id=1, source_target_pairs={{0,2},{2,0},{4,6},{6,4},{1,3},{3,1},{5,7},{7,5},{8,10},{10,8},{12,... | collective-permute-start | bytes 786440 | tf_op jit(solution)/shard_map/ppermute | solution.py:60
  50.3 0.8 slice.65
  51.2 1.7 %collective-permute-start.10 = (bf16[64,2048]{1,0:T(8,128)(2,1)}, bf16[64,2048]{1,0:T(8,128)(2,1)}, u32[]{:S(2)}, u32[]{:S(2)}) collective-permute-start(bf16[64,2048]{1,0:T(8,128)(2,1)} %slice.65), channel_id=1, source_target_pairs={{0,4},{2,6},{4,0},{6,2},{1,5},{3,7},{5,1},{7,3},{8,12},{10,14},{12... | collective-permute-start | bytes 786440 | tf_op jit(solution)/shard_map/ppermute | solution.py:60
  52.9 3.8 %base_product.2 = bf16[1,4,128,2048]{3,2,1,0:T(8,128)(2,1)S(1)} custom-call(s32[59]{0:T(128)S(1)} %concatenate.6.at_ref, bf16[4,2,128,1024]{3,2,1,0:T(8,128)(2,1)S(1)} %bitcast.68, bf16[1024,2048]{1,0:T(8,128)(2,1)S(1)} %copy-done), custom_call_target="tpu_custom_call" | custom-call | flops 1024 | bytes 1024 | tf_op jit(solution)/shard_map/base_product/pallas_call | solution.py:140
  56.8 1.3 copy-done.4
  58.1 2.6 %copy.11 = bf16[1024,1024]{1,0:T(8,128)(2,1)} copy(bf16[1024,1024]{0,1:T(8,128)(2,1)S(1)} %bitcast.69) | data formatting | bytes 4194304 | tf_op jit(solution)/shard_map/transpose | solution.py:555
  60.9 1.6 %copy-done.3 = bf16[1024,1024]{1,0:T(8,128)(2,1)S(1)} copy-done((bf16[1024,1024]{1,0:T(8,128)(2,1)S(1)}, bf16[1024,1024]{1,0:T(8,128)(2,1)}, u32[]{:S(2)}) %copy-start.3) | copy-done | bytes 2097176
  62.5 3.1 %grad_down_pieces.1 = bf16[4,8,256,128]{3,2,1,0:T(8,128)(2,1)} custom-call(s32[59]{0:T(128)S(1)} %concatenate.6.at_ref, bf16[4,256,1024]{2,1,0:T(8,128)(2,1)S(1)} %bitcast.70, bf16[4,128,128]{2,1,0:T(8,128)(2,1)S(1)} %pad_maximum_fusion.rest_0_, bf16[4,128,128]{2,1,0:T(8,128)(2,1)S(1)} %collective-permute-done.6.rest_1_), custom_call_target="tpu_custom_call" | custom-call | flops 1024 | bytes 1024 | tf_op jit(solution)/shard_map/grad_down_pieces/pallas_call | solution.py:295
  65.6 0.3 collective-permute-start.12
  65.9 1.0 constant_dynamic-update-slice_fusion.1
  67.1 1.0 constant_dynamic-update-slice_fusion.rest_3_.rest_5_
  68.1 0.4 collective-permute-start.14
  68.5 3.6 %fusion = (bf16[128,2048]{1,0:T(8,128)(2,1)}, bf16[128,2048]{1,0:T(8,128)(2,1)}, f32[128,2048]{1,0:T(8,128)}, bf16[128,2048]{1,0:T(8,128)(2,1)}) fusion(bf16[2,128,2048]{2,1,0:T(8,128)(2,1)} %collective-permute-done.16, bf16[1,4,128,2048]{3,2,1,0:T(8,128)(2,1)S(1)} %copy-done.5, bf16[2,128,2048]{2,1,0:T(8,128)(2,1)} %collective-permute-done.15), kind=kLoop, calls=%fused_computation.1 | loop fusion | flops 3932160 | bytes 6815744 | tf_op jit(solution)/shard_map/convert_element_type | solution.py:546
  72.1 0.8 copy-done.13
  73.0 0.9 copy-done.15
  73.8 0.8 copy-done.17
  74.7 0.8 copy-done.19
  75.5 5.0 %all-to-all-start.1 = ((bf16[4,8,256,128]{3,2,1,0:T(8,128)(2,1)}), bf16[4,8,256,128]{3,2,1,0:T(8,128)(2,1)}, u32[]{:S(2)}, u32[]{:S(2)}) async-start(bf16[4,8,256,128]{3,2,1,0:T(8,128)(2,1)} %grad_down_pieces.1), calls=%async_computation.1 | async-start | bytes 4194304 | tf_op jit(solution)/shard_map/all_to_all | solution.py:561
  80.5 1.6 %collective-permute-start.17 = (bf16[128,2048]{1,0:T(8,128)(2,1)}, bf16[128,2048]{1,0:T(8,128)(2,1)S(1)}, u32[]{:S(2)}, u32[]{:S(2)}) collective-permute-start(bf16[128,2048]{1,0:T(8,128)(2,1)} %get-tuple-element.73), channel_id=1, source_target_pairs={{0,2},{2,0},{4,6},{6,4},{1,3},{3,1},{5,7},{7,5},{8,10},{10,8},{12,... | collective-permute-start | bytes 1572872 | tf_op jit(solution)/shard_map/ppermute | solution.py:60
  82.0 0.5 collective-permute-start.18
  82.5 1.5 %collective-permute-start.19 = (bf16[128,2048]{1,0:T(8,128)(2,1)}, bf16[128,2048]{1,0:T(8,128)(2,1)S(1)}, u32[]{:S(2)}, u32[]{:S(2)}) collective-permute-start(bf16[128,2048]{1,0:T(8,128)(2,1)} %get-tuple-element.68), channel_id=1, source_target_pairs={{0,6},{2,4},{4,2},{6,0},{1,7},{3,5},{5,3},{7,1},{8,14},{10,12},{12... | collective-permute-start | bytes 1572872 | tf_op jit(solution)/shard_map/ppermute | solution.py:60
  84.0 2.2 %copy-done.1 = bf16[1024,2048]{1,0:T(8,128)(2,1)S(1)} copy-done((bf16[1024,2048]{1,0:T(8,128)(2,1)S(1)}, bf16[1024,2048]{1,0:T(8,128)(2,1)}, u32[]{:S(2)}) %copy-start.1) | copy-done | bytes 4194328
  86.1 1.0 copy-done.10
  87.2 1.0 copy-done.12
  88.2 1.0 copy-done.14
  89.3 1.0 copy-done.16
  90.3 1.0 copy-done.18
  91.4 1.0 copy-done.20
  92.4 6.5 %cotangent_product.1.base_ref = f32[1024,1024]{1,0:T(8,128)S(1)} custom-call(s32[59]{0:T(128)S(1)} %concatenate.6.at_ref, bf16[1024,2048]{1,0:T(8,128)(2,1)S(1)} %copy-done.1, bf16[128,2048]{1,0:T(8,128)(2,1)S(1)} %copy-done.6, bf16[128,2048]{1,0:T(8,128)(2,1)S(1)} %copy-done.10, bf16[128,2048]{1,0:T(8,128)(2,1)S(1)} %collective-permute-done.8.rest_2_.rest_4_, ...), custom_call_target="tpu_custom_call" | custom-call | flops 1024 | bytes 1024 | tf_op jit(solution)/shard_map/cotangent_product/pallas_call | solution.py:214
  98.9 8.0 %collective-permute-done.18.rest_2_ = bf16[128,2048]{1,0:T(8,128)(2,1)S(1)} collective-permute-done((bf16[128,2048]{1,0:T(8,128)(2,1)}, bf16[128,2048]{1,0:T(8,128)(2,1)S(1)}, u32[]{:S(2)}, u32[]{:S(2)}) %collective-permute-start.18) | collective-permute-done | bytes 524320 | tf_op jit(solution)/shard_map/ppermute | solution.py:60
  107.0 2.3 %low_product.1 = bf16[2,4,128,128]{3,2,1,0:T(8,128)(2,1)S(1)} custom-call(s32[59]{0:T(128)S(1)} %concatenate.6.at_ref, bf16[1024,1024]{1,0:T(8,128)(2,1)S(1)} %copy-done.2, bf16[4,2048,128]{2,1,0:T(8,128)(2,1)} %all-to-all-done.a_ref), custom_call_target="tpu_custom_call" | custom-call | flops 1024 | bytes 1024 | tf_op jit(solution)/shard_map/low_product/pallas_call | solution.py:175
  109.4 1.3 collective-permute-done.20
  110.8 0.5 collective-permute-start.21
  111.3 1.3 collective-permute-start.22
  112.6 1.7 %collective-permute-start.23 = (bf16[4,128,128]{2,1,0:T(8,128)(2,1)S(1)}, bf16[4,128,128]{2,1,0:T(8,128)(2,1)S(1)}, u32[]{:S(2)}, u32[]{:S(2)}) collective-permute-start(bf16[4,128,128]{2,1,0:T(8,128)(2,1)S(1)} %fusion.3), channel_id=1, source_target_pairs={{0,6},{2,4},{4,2},{6,0},{1,7},{3,5},{5,3},{7,1},{8,14},{10,12},{12... | collective-permute-start | bytes 393224 | tf_op jit(solution)/shard_map/ppermute | solution.py:60
  114.3 2.9 %collective-permute-done.21 = bf16[4,128,128]{2,1,0:T(8,128)(2,1)S(1)} collective-permute-done((bf16[4,128,128]{2,1,0:T(8,128)(2,1)S(1)}, bf16[4,128,128]{2,1,0:T(8,128)(2,1)S(1)}, u32[]{:S(2)}, u32[]{:S(2)}) %collective-permute-start.21) | collective-permute-done | bytes 131104 | tf_op jit(solution)/shard_map/ppermute | solution.py:60
  117.2 2.2 %collective-permute-done.22 = bf16[4,128,128]{2,1,0:T(8,128)(2,1)S(1)} collective-permute-done((bf16[4,128,128]{2,1,0:T(8,128)(2,1)S(1)}, bf16[4,128,128]{2,1,0:T(8,128)(2,1)S(1)}, u32[]{:S(2)}, u32[]{:S(2)}) %collective-permute-start.22) | collective-permute-done | bytes 131104 | tf_op jit(solution)/shard_map/ppermute | solution.py:60
  119.5 1.3 collective-permute-done.24.rest_1_
  120.9 1.1 grad_up_pieces.1
  122.0 1.8 %collective-permute-start.25 = (bf16[8,16,256]{2,1,0:T(8,128)(2,1)S(1)}, bf16[8,16,256]{2,1,0:T(8,128)(2,1)S(1)}, u32[]{:S(2)}, u32[]{:S(2)}) collective-permute-start(bf16[8,16,256]{2,1,0:T(8,128)(2,1)S(1)} %get-tuple-element.76), channel_id=1, source_target_pairs={{0,8},{8,16},{16,24},{24,0},{1,9},{9,17},{17,25},{25,1},{2,10},{10... | collective-permute-start | bytes 196616 | tf_op jit(solution)/shard_map/ppermute | solution.py:39
  123.8 2.4 %collective-permute-start.26 = (bf16[8,16,256]{2,1,0:T(8,128)(2,1)S(1)}, bf16[8,16,256]{2,1,0:T(8,128)(2,1)S(1)}, u32[]{:S(2)}, u32[]{:S(2)}) collective-permute-start(bf16[8,16,256]{2,1,0:T(8,128)(2,1)S(1)} %get-tuple-element.75), channel_id=1, source_target_pairs={{0,16},{8,24},{16,0},{24,8},{1,17},{9,25},{17,1},{25,9},{2,18},{10... | collective-permute-start | bytes 196616 | tf_op jit(solution)/shard_map/ppermute | solution.py:39
  126.1 1.5 %collective-permute-start.27 = (bf16[8,16,256]{2,1,0:T(8,128)(2,1)S(1)}, bf16[8,16,256]{2,1,0:T(8,128)(2,1)S(1)}, u32[]{:S(2)}, u32[]{:S(2)}) collective-permute-start(bf16[8,16,256]{2,1,0:T(8,128)(2,1)S(1)} %get-tuple-element.74), channel_id=1, source_target_pairs={{0,24},{8,0},{16,8},{24,16},{1,25},{9,1},{17,9},{25,17},{2,26},{10... | collective-permute-start | bytes 196616 | tf_op jit(solution)/shard_map/ppermute | solution.py:39
  127.6 4.5 %input_gradient.1 = bf16[1024,1024]{1,0:T(8,128)(2,1)} custom-call(s32[59]{0:T(128)S(1)} %concatenate.6.at_ref, f32[1024,1024]{1,0:T(8,128)S(1)} %cotangent_product.1.base_ref, bf16[4,2048,128]{2,1,0:T(8,128)(2,1)} %all-to-all-done.a_ref, bf16[4,128,128]{2,1,0:T(8,128)(2,1)S(1)} %pad_maximum_fusion.rest_0_, ...), custom_call_target="tpu_custom_call" | custom-call | flops 1024 | bytes 1024 | tf_op jit(solution)/shard_map/input_gradient/pallas_call | solution.py:255
  132.1 1.8 %keys_and_values.1 = bf16[128,2048]{1,0:T(8,128)(2,1)} custom-call(s32[59]{0:T(128)S(1)} %concatenate.6.at_ref, bf16[4,128,128]{2,1,0:T(8,128)(2,1)S(1)} %add_convert_fusion.low_ref.rest_0_, bf16[64,2048]{1,0:T(8,128)(2,1)S(1)} %copy-done.22, f32[128,2048]{1,0:T(8,128)S(1)} %copy-done.7, bf16[128,2048]{1,0:T(8,128)(2,1)S(1)} %collective-permute-done.17.rest_1_, ...), custom_call_target="tpu_custom_call" | custom-call | flops 1024 | bytes 1024 | tf_op jit(solution)/shard_map/keys_and_values/pallas_call | solution.py:489
  133.9 4.3 %grad_down.1 = f32[24,256,128]{2,1,0:T(8,128)} custom-call(s32[59]{0:T(128)} %copy-done.23, bf16[4,8,256,128]{3,2,1,0:T(8,128)(2,1)} %all-to-all-done.1.piece_ref), custom_call_target="tpu_custom_call" | custom-call | flops 1024 | bytes 1024 | tf_op jit(solution)/shard_map/grad_down/pallas_call | solution.py:341
  138.2 1.5 %grad_up.1 = f32[24,16,256]{2,1,0:T(8,128)} custom-call(s32[59]{0:T(128)S(1)} %copy-done.24, bf16[8,16,256]{2,1,0:T(8,128)(2,1)S(1)} %get-tuple-element.64.rest_0_, bf16[8,16,256]{2,1,0:T(8,128)(2,1)S(1)} %collective-permute-done.25.rest_1_, bf16[8,16,256]{2,1,0:T(8,128)(2,1)S(1)} %collective-permute-done.26.rest_2_, ...), custom_call_target="tpu_custom_call" | custom-call | flops 1024 | bytes 1024 | tf_op jit(solution)/shard_map/grad_up/pallas_call | solution.py:430
  (76 shorter events, 1.7 us)
Async XLA Ops:
  5.7 7.8 %collective-permute-start = (bf16[16,2048]{1,0:T(8,128)(2,1)}, bf16[16,2048]{1,0:T(8,128)(2,1)S(1)}, u32[]{:S(2)}, u32[]{:S(2)}) collective-permute-start(bf16[16,2048]{1,0:T(8,128)(2,1)} %get-tuple-element.38), channel_id=1, source_target_pairs={{0,8},{8,16},{16,24},{24,0},{1,9},{9,17},{17,25},{25,1},{2,10},{10... | collective-permute-start | bytes 196616 | tf_op jit(solution)/shard_map/ppermute | solution.py:39
  8.7 7.3 %collective-permute-start.1 = (bf16[16,2048]{1,0:T(8,128)(2,1)}, bf16[16,2048]{1,0:T(8,128)(2,1)S(1)}, u32[]{:S(2)}, u32[]{:S(2)}) collective-permute-start(bf16[16,2048]{1,0:T(8,128)(2,1)} %get-tuple-element.39), channel_id=1, source_target_pairs={{0,16},{8,24},{16,0},{24,8},{1,17},{9,25},{17,1},{25,9},{2,18},{10... | collective-permute-start | bytes 196616 | tf_op jit(solution)/shard_map/ppermute | solution.py:39
  11.3 4.9 %collective-permute-start.2 = (bf16[16,2048]{1,0:T(8,128)(2,1)}, bf16[16,2048]{1,0:T(8,128)(2,1)S(1)}, u32[]{:S(2)}, u32[]{:S(2)}) collective-permute-start(bf16[16,2048]{1,0:T(8,128)(2,1)} %get-tuple-element.40), channel_id=1, source_target_pairs={{0,24},{8,0},{16,8},{24,16},{1,25},{9,1},{17,9},{25,17},{2,26},{10... | collective-permute-start | bytes 196616 | tf_op jit(solution)/shard_map/ppermute | solution.py:39
  16.3 4.8 %copy-start.6 = (bf16[128,2048]{1,0:T(8,128)(2,1)S(1)}, bf16[128,2048]{1,0:T(8,128)(2,1)}, u32[]{:S(2)}) copy-start(bf16[128,2048]{1,0:T(8,128)(2,1)} %rest_2_) | copy-start | bytes 1572868
  16.3 6.5 %copy-start.26 = (s32[32]{0:T(128)S(1)}, s32[32]{0:T(128)}, u32[]{:S(2)}) copy-start(s32[32]{0:T(128)} %tenant_ref.1) | copy-start | bytes 388
  16.3 6.5 %copy-start.27 = (s32[24]{0:T(128)S(1)}, s32[24]{0:T(128)}, u32[]{:S(2)}) copy-start(s32[24]{0:T(128)} %slot_ref.1) | copy-start | bytes 292
  16.3 6.5 %copy-start.2 = (bf16[1024,1024]{1,0:T(8,128)(2,1)S(1)}, bf16[1024,1024]{1,0:T(8,128)(2,1)}, u32[]{:S(2)}) copy-start(bf16[1024,1024]{1,0:T(8,128)(2,1)} %x_ref.1) | copy-start | bytes 6291460
  16.3 59.2 %all-to-all-start = ((bf16[4,2048,128]{2,1,0:T(8,128)(2,1)}), bf16[4,2048,128]{2,1,0:T(8,128)(2,1)}, u32[]{:S(2)}, u32[]{:S(2)}) async-start(bf16[4,2048,128]{2,1,0:T(8,128)(2,1)} %get-tuple-element.41), calls=%async_computation | async-start | bytes 4194304 | tf_op jit(solution)/shard_map/all_to_all | solution.py:526
  21.0 24.2 %collective-permute-start.8 = (bf16[128,2048]{1,0:T(8,128)(2,1)S(1)}, bf16[128,2048]{1,0:T(8,128)(2,1)S(1)}, u32[]{:S(2)}, u32[]{:S(2)}) collective-permute-start(bf16[128,2048]{1,0:T(8,128)(2,1)S(1)} %copy-done.6), channel_id=1, source_target_pairs={{0,4},{2,6},{4,0},{6,2},{1,5},{3,7},{5,1},{7,3},{8,12},{10,14},{12... | collective-permute-start | bytes 1572872 | tf_op jit(solution)/shard_map/ppermute | solution.py:60
  22.8 109.3 %copy-start.23 = (s32[59]{0:T(128)}, s32[59]{0:T(128)S(1)}, u32[]{:S(2)}) copy-start(s32[59]{0:T(128)S(1)} %concatenate.6.at_ref) | copy-start | bytes 712
  22.8 2.2 %copy-start = (bf16[1024,2048]{1,0:T(8,128)(2,1)S(1)}, bf16[1024,2048]{1,0:T(8,128)(2,1)}, u32[]{:S(2)}) copy-start(bf16[1024,2048]{1,0:T(8,128)(2,1)} %w_ref.5) | copy-start | bytes 12582916
  25.0 6.8 %copy-start.25 = (bf16[16,2048]{1,0:T(8,128)(2,1)S(1)}, bf16[16,2048]{1,0:T(8,128)(2,1)}, u32[]{:S(2)}) copy-start(bf16[16,2048]{1,0:T(8,128)(2,1)} %get-tuple-element.37.rest_0_) | copy-start | bytes 196612
  29.8 38.3 %collective-permute-start.15 = (bf16[2,128,2048]{2,1,0:T(8,128)(2,1)}, bf16[2,128,2048]{2,1,0:T(8,128)(2,1)}, u32[]{:S(2)}, u32[]{:S(2)}) collective-permute-start(bf16[2,128,2048]{2,1,0:T(8,128)(2,1)} %bitcast.11), channel_id=1, source_target_pairs={{0,1},{1,0},{2,3},{3,2},{4,5},{5,4},{6,7},{7,6},{8,9},{9,8},{10,11... | collective-permute-start | bytes 3145736 | tf_op jit(solution)/shard_map/ppermute | solution.py:60
  29.8 38.7 %collective-permute-start.16 = (bf16[2,128,2048]{2,1,0:T(8,128)(2,1)}, bf16[2,128,2048]{2,1,0:T(8,128)(2,1)}, u32[]{:S(2)}, u32[]{:S(2)}) collective-permute-start(bf16[2,128,2048]{2,1,0:T(8,128)(2,1)} %bitcast.16), channel_id=1, source_target_pairs={{0,1},{1,0},{2,3},{3,2},{4,5},{5,4},{6,7},{7,6},{8,9},{9,8},{10,11... | collective-permute-start | bytes 3145736 | tf_op jit(solution)/shard_map/ppermute | solution.py:60
  30.3 20.0 %collective-permute-start.7 = (bf16[128,2048]{1,0:T(8,128)(2,1)S(1)}, bf16[128,2048]{1,0:T(8,128)(2,1)S(1)}, u32[]{:S(2)}, u32[]{:S(2)}) collective-permute-start(bf16[128,2048]{1,0:T(8,128)(2,1)S(1)} %copy-done.6), channel_id=1, source_target_pairs={{0,2},{2,0},{4,6},{6,4},{1,3},{3,1},{5,7},{7,5},{8,10},{10,8},{12,... | collective-permute-start | bytes 1572872 | tf_op jit(solution)/shard_map/ppermute | solution.py:60
  32.7 18.4 %copy-start.21 = (bf16[64,2048]{1,0:T(8,128)(2,1)}, bf16[64,2048]{1,0:T(8,128)(2,1)S(1)}, u32[]{:S(2)}) copy-start(bf16[64,2048]{1,0:T(8,128)(2,1)S(1)} %get-tuple-element.56.b_ref) | copy-start | bytes 786436
  32.7 12.1 %collective-permute-start.3 = (bf16[128,128]{1,0:T(8,128)(2,1)S(1)}, bf16[128,128]{1,0:T(8,128)(2,1)S(1)}, u32[]{:S(2)}, u32[]{:S(2)}) collective-permute-start(bf16[128,128]{1,0:T(8,128)(2,1)S(1)} %get-tuple-element.43), channel_id=1, source_target_pairs={{0,2},{2,0},{4,6},{6,4},{1,3},{3,1},{5,7},{7,5},{8,10},{10,8},{12,... | collective-permute-start | bytes 98312 | tf_op jit(solution)/shard_map/ppermute | solution.py:60
  44.8 3.9 %collective-permute-start.4 = (bf16[128,128]{1,0:T(8,128)(2,1)S(1)}, bf16[128,128]{1,0:T(8,128)(2,1)S(1)}, u32[]{:S(2)}, u32[]{:S(2)}) collective-permute-start(bf16[128,128]{1,0:T(8,128)(2,1)S(1)} %get-tuple-element.43), channel_id=1, source_target_pairs={{0,4},{2,6},{4,0},{6,2},{1,5},{3,7},{5,1},{7,3},{8,12},{10,14},{12... | collective-permute-start | bytes 98312 | tf_op jit(solution)/shard_map/ppermute | solution.py:60
  45.3 5.0 %collective-permute-start.5 = (bf16[128,128]{1,0:T(8,128)(2,1)S(1)}, bf16[128,128]{1,0:T(8,128)(2,1)S(1)}, u32[]{:S(2)}, u32[]{:S(2)}) collective-permute-start(bf16[128,128]{1,0:T(8,128)(2,1)S(1)} %get-tuple-element.43), channel_id=1, source_target_pairs={{0,6},{2,4},{4,2},{6,0},{1,7},{3,5},{5,3},{7,1},{8,14},{10,12},{12... | collective-permute-start | bytes 98312 | tf_op jit(solution)/shard_map/ppermute | solution.py:60
  48.8 16.8 %collective-permute-start.9 = (bf16[64,2048]{1,0:T(8,128)(2,1)}, bf16[64,2048]{1,0:T(8,128)(2,1)}, u32[]{:S(2)}, u32[]{:S(2)}) collective-permute-start(bf16[64,2048]{1,0:T(8,128)(2,1)} %slice.64), channel_id=1, source_target_pairs={{0,2},{2,0},{4,6},{6,4},{1,3},{3,1},{5,7},{7,5},{8,10},{10,8},{12,... | collective-permute-start | bytes 786440 | tf_op jit(solution)/shard_map/ppermute | solution.py:60
  50.2 10.4 %collective-permute-start.6 = (bf16[4,128,128]{2,1,0:T(8,128)(2,1)S(1)}, bf16[4,128,128]{2,1,0:T(8,128)(2,1)S(1)}, u32[]{:S(2)}, u32[]{:S(2)}) collective-permute-start(bf16[4,128,128]{2,1,0:T(8,128)(2,1)S(1)} %pad_maximum_fusion.rest_0_), channel_id=1, source_target_pairs={{0,1},{1,0},{2,3},{3,2},{4,5},{5,4},{6,7},{7,6},{8,9},{9,8},{10,11... | collective-permute-start | bytes 393224 | tf_op jit(solution)/shard_map/ppermute | solution.py:60
  50.3 0.9 copy-start.8
  51.2 15.6 %collective-permute-start.10 = (bf16[64,2048]{1,0:T(8,128)(2,1)}, bf16[64,2048]{1,0:T(8,128)(2,1)}, u32[]{:S(2)}, u32[]{:S(2)}) collective-permute-start(bf16[64,2048]{1,0:T(8,128)(2,1)} %slice.65), channel_id=1, source_target_pairs={{0,4},{2,6},{4,0},{6,2},{1,5},{3,7},{5,1},{7,3},{8,12},{10,14},{12... | collective-permute-start | bytes 786440 | tf_op jit(solution)/shard_map/ppermute | solution.py:60
  56.8 1.3 copy-start.4
  60.7 11.5 %collective-permute-start.11 = (bf16[128,2048]{1,0:T(8,128)(2,1)S(1)}, bf16[128,2048]{1,0:T(8,128)(2,1)S(1)}, u32[]{:S(2)}, u32[]{:S(2)}) collective-permute-start(bf16[128,2048]{1,0:T(8,128)(2,1)S(1)} %copy-done.6), channel_id=1, source_target_pairs={{0,1},{1,0},{2,3},{3,2},{4,5},{5,4},{6,7},{7,6},{8,9},{9,8},{10,11... | collective-permute-start | bytes 1572872 | tf_op jit(solution)/shard_map/ppermute | solution.py:60
  60.9 1.6 %copy-start.3 = (bf16[1024,1024]{1,0:T(8,128)(2,1)S(1)}, bf16[1024,1024]{1,0:T(8,128)(2,1)}, u32[]{:S(2)}) copy-start(bf16[1024,1024]{1,0:T(8,128)(2,1)} %copy.11) | copy-start | bytes 6291460
  62.5 3.1 %copy-start.9 = (bf16[128,2048]{1,0:T(8,128)(2,1)S(1)}, bf16[128,2048]{1,0:T(8,128)(2,1)}, u32[]{:S(2)}) copy-start(bf16[128,2048]{1,0:T(8,128)(2,1)} %copy-done.8) | copy-start | bytes 1572868
  62.5 6.0 %copy-start.5 = (bf16[1,4,128,2048]{3,2,1,0:T(8,128)(2,1)S(1)}, bf16[1,4,128,2048]{3,2,1,0:T(8,128)(2,1)}, u32[]{:S(2)}) copy-start(bf16[1,4,128,2048]{3,2,1,0:T(8,128)(2,1)} %copy-done.4) | copy-start | bytes 6291460
  65.6 7.4 %collective-permute-start.12 = (bf16[128,2048]{1,0:T(8,128)(2,1)S(1)}, bf16[128,2048]{1,0:T(8,128)(2,1)S(1)}, u32[]{:S(2)}, u32[]{:S(2)}) collective-permute-start(bf16[128,2048]{1,0:T(8,128)(2,1)S(1)} %copy-done.9), channel_id=1, source_target_pairs={{0,1},{1,0},{2,3},{3,2},{4,5},{5,4},{6,7},{7,6},{8,9},{9,8},{10,11... | collective-permute-start | bytes 1572872 | tf_op jit(solution)/shard_map/ppermute | solution.py:60
  66.9 7.0 %collective-permute-start.13 = (bf16[128,2048]{1,0:T(8,128)(2,1)S(1)}, bf16[128,2048]{1,0:T(8,128)(2,1)S(1)}, u32[]{:S(2)}, u32[]{:S(2)}) collective-permute-start(bf16[128,2048]{1,0:T(8,128)(2,1)S(1)} %collective-permute-done.8.rest_2_.rest_4_), channel_id=1, source_target_pairs={{0,1},{1,0},{2,3},{3,2},{4,5},{5,4},{6,7},{7,6},{8,9},{9,8},{10,11... | collective-permute-start | bytes 1572872 | tf_op jit(solution)/shard_map/ppermute | solution.py:60
  68.1 4.0 %copy-start.11 = (bf16[128,2048]{1,0:T(8,128)(2,1)}, bf16[128,2048]{1,0:T(8,128)(2,1)S(1)}, u32[]{:S(2)}) copy-start(bf16[128,2048]{1,0:T(8,128)(2,1)S(1)} %constant_dynamic-update-slice_fusion.rest_3_.rest_5_) | copy-start | bytes 1572868
  68.1 6.6 %collective-permute-start.14 = (bf16[128,2048]{1,0:T(8,128)(2,1)S(1)}, bf16[128,2048]{1,0:T(8,128)(2,1)S(1)}, u32[]{:S(2)}, u32[]{:S(2)}) collective-permute-start(bf16[128,2048]{1,0:T(8,128)(2,1)S(1)} %constant_dynamic-update-slice_fusion.rest_3_.rest_5_), channel_id=1, source_target_pairs={{0,1},{1,0},{2,3},{3,2},{4,5},{5,4},{6,7},{7,6},{8,9},{9,8},{10,11... | collective-permute-start | bytes 1572872 | tf_op jit(solution)/shard_map/ppermute | solution.py:60
  72.1 0.8 copy-start.13
  73.0 0.9 copy-start.15
  73.8 0.8 copy-start.17
  74.7 0.8 copy-start.19
  75.5 58.4 %all-to-all-start.1 = ((bf16[4,8,256,128]{3,2,1,0:T(8,128)(2,1)}), bf16[4,8,256,128]{3,2,1,0:T(8,128)(2,1)}, u32[]{:S(2)}, u32[]{:S(2)}) async-start(bf16[4,8,256,128]{3,2,1,0:T(8,128)(2,1)} %grad_down_pieces.1), calls=%async_computation.1 | async-start | bytes 4194304 | tf_op jit(solution)/shard_map/all_to_all | solution.py:561
  80.5 18.5 %collective-permute-start.17 = (bf16[128,2048]{1,0:T(8,128)(2,1)}, bf16[128,2048]{1,0:T(8,128)(2,1)S(1)}, u32[]{:S(2)}, u32[]{:S(2)}) collective-permute-start(bf16[128,2048]{1,0:T(8,128)(2,1)} %get-tuple-element.73), channel_id=1, source_target_pairs={{0,2},{2,0},{4,6},{6,4},{1,3},{3,1},{5,7},{7,5},{8,10},{10,8},{12,... | collective-permute-start | bytes 1572872 | tf_op jit(solution)/shard_map/ppermute | solution.py:60
  82.0 24.9 %collective-permute-start.18 = (bf16[128,2048]{1,0:T(8,128)(2,1)}, bf16[128,2048]{1,0:T(8,128)(2,1)S(1)}, u32[]{:S(2)}, u32[]{:S(2)}) collective-permute-start(bf16[128,2048]{1,0:T(8,128)(2,1)} %get-tuple-element.69), channel_id=1, source_target_pairs={{0,4},{2,6},{4,0},{6,2},{1,5},{3,7},{5,1},{7,3},{8,12},{10,14},{12... | collective-permute-start | bytes 1572872 | tf_op jit(solution)/shard_map/ppermute | solution.py:60
  82.5 24.5 %collective-permute-start.19 = (bf16[128,2048]{1,0:T(8,128)(2,1)}, bf16[128,2048]{1,0:T(8,128)(2,1)S(1)}, u32[]{:S(2)}, u32[]{:S(2)}) collective-permute-start(bf16[128,2048]{1,0:T(8,128)(2,1)} %get-tuple-element.68), channel_id=1, source_target_pairs={{0,6},{2,4},{4,2},{6,0},{1,7},{3,5},{5,3},{7,1},{8,14},{10,12},{12... | collective-permute-start | bytes 1572872 | tf_op jit(solution)/shard_map/ppermute | solution.py:60
  84.0 2.2 %copy-start.1 = (bf16[1024,2048]{1,0:T(8,128)(2,1)S(1)}, bf16[1024,2048]{1,0:T(8,128)(2,1)}, u32[]{:S(2)}) copy-start(bf16[1024,2048]{1,0:T(8,128)(2,1)} %w_ref.5) | copy-start | bytes 12582916
  86.1 1.0 copy-start.10
  87.2 1.0 copy-start.12
  88.2 1.0 copy-start.14
  89.3 1.0 copy-start.16
  90.3 1.0 copy-start.18
  91.4 1.0 copy-start.20
  109.3 1.4 %collective-permute-start.20 = (bf16[4,128,128]{2,1,0:T(8,128)(2,1)S(1)}, bf16[4,128,128]{2,1,0:T(8,128)(2,1)S(1)}, u32[]{:S(2)}, u32[]{:S(2)}) collective-permute-start(bf16[4,128,128]{2,1,0:T(8,128)(2,1)S(1)} %slice_bitcast_fusion.8), channel_id=1, source_target_pairs={{0,1},{1,0},{2,3},{3,2},{4,5},{5,4},{6,7},{7,6},{8,9},{9,8},{10,11... | collective-permute-start | bytes 393224 | tf_op jit(solution)/shard_map/ppermute | solution.py:60
  110.8 6.4 %collective-permute-start.21 = (bf16[4,128,128]{2,1,0:T(8,128)(2,1)S(1)}, bf16[4,128,128]{2,1,0:T(8,128)(2,1)S(1)}, u32[]{:S(2)}, u32[]{:S(2)}) collective-permute-start(bf16[4,128,128]{2,1,0:T(8,128)(2,1)S(1)} %fusion.3), channel_id=1, source_target_pairs={{0,2},{2,0},{4,6},{6,4},{1,3},{3,1},{5,7},{7,5},{8,10},{10,8},{12,... | collective-permute-start | bytes 393224 | tf_op jit(solution)/shard_map/ppermute | solution.py:60
  111.3 8.1 %collective-permute-start.22 = (bf16[4,128,128]{2,1,0:T(8,128)(2,1)S(1)}, bf16[4,128,128]{2,1,0:T(8,128)(2,1)S(1)}, u32[]{:S(2)}, u32[]{:S(2)}) collective-permute-start(bf16[4,128,128]{2,1,0:T(8,128)(2,1)S(1)} %fusion.3), channel_id=1, source_target_pairs={{0,4},{2,6},{4,0},{6,2},{1,5},{3,7},{5,1},{7,3},{8,12},{10,14},{12... | collective-permute-start | bytes 393224 | tf_op jit(solution)/shard_map/ppermute | solution.py:60
  112.6 6.8 %collective-permute-start.23 = (bf16[4,128,128]{2,1,0:T(8,128)(2,1)S(1)}, bf16[4,128,128]{2,1,0:T(8,128)(2,1)S(1)}, u32[]{:S(2)}, u32[]{:S(2)}) collective-permute-start(bf16[4,128,128]{2,1,0:T(8,128)(2,1)S(1)} %fusion.3), channel_id=1, source_target_pairs={{0,6},{2,4},{4,2},{6,0},{1,7},{3,5},{5,3},{7,1},{8,14},{10,12},{12... | collective-permute-start | bytes 393224 | tf_op jit(solution)/shard_map/ppermute | solution.py:60
  119.4 1.4 %collective-permute-start.24 = (bf16[4,128,128]{2,1,0:T(8,128)(2,1)S(1)}, bf16[4,128,128]{2,1,0:T(8,128)(2,1)S(1)}, u32[]{:S(2)}, u32[]{:S(2)}) collective-permute-start(bf16[4,128,128]{2,1,0:T(8,128)(2,1)S(1)} %add_convert_fusion.low_ref.rest_0_), channel_id=1, source_target_pairs={{0,1},{1,0},{2,3},{3,2},{4,5},{5,4},{6,7},{7,6},{8,9},{9,8},{10,11... | collective-permute-start | bytes 393224 | tf_op jit(solution)/shard_map/ppermute | solution.py:60
  122.0 16.2 %collective-permute-start.25 = (bf16[8,16,256]{2,1,0:T(8,128)(2,1)S(1)}, bf16[8,16,256]{2,1,0:T(8,128)(2,1)S(1)}, u32[]{:S(2)}, u32[]{:S(2)}) collective-permute-start(bf16[8,16,256]{2,1,0:T(8,128)(2,1)S(1)} %get-tuple-element.76), channel_id=1, source_target_pairs={{0,8},{8,16},{16,24},{24,0},{1,9},{9,17},{17,25},{25,1},{2,10},{10... | collective-permute-start | bytes 196616 | tf_op jit(solution)/shard_map/ppermute | solution.py:39
  123.8 14.4 %collective-permute-start.26 = (bf16[8,16,256]{2,1,0:T(8,128)(2,1)S(1)}, bf16[8,16,256]{2,1,0:T(8,128)(2,1)S(1)}, u32[]{:S(2)}, u32[]{:S(2)}) collective-permute-start(bf16[8,16,256]{2,1,0:T(8,128)(2,1)S(1)} %get-tuple-element.75), channel_id=1, source_target_pairs={{0,16},{8,24},{16,0},{24,8},{1,17},{9,25},{17,1},{25,9},{2,18},{10... | collective-permute-start | bytes 196616 | tf_op jit(solution)/shard_map/ppermute | solution.py:39
  126.1 6.0 %copy-start.7 = (f32[128,2048]{1,0:T(8,128)S(1)}, f32[128,2048]{1,0:T(8,128)}, u32[]{:S(2)}) copy-start(f32[128,2048]{1,0:T(8,128)} %get-tuple-element.57.rest_0_) | copy-start | bytes 3145732
  126.1 6.0 %copy-start.22 = (bf16[64,2048]{1,0:T(8,128)(2,1)S(1)}, bf16[64,2048]{1,0:T(8,128)(2,1)}, u32[]{:S(2)}) copy-start(bf16[64,2048]{1,0:T(8,128)(2,1)} %copy-done.21) | copy-start | bytes 786436
  126.1 12.0 %collective-permute-start.27 = (bf16[8,16,256]{2,1,0:T(8,128)(2,1)S(1)}, bf16[8,16,256]{2,1,0:T(8,128)(2,1)S(1)}, u32[]{:S(2)}, u32[]{:S(2)}) collective-permute-start(bf16[8,16,256]{2,1,0:T(8,128)(2,1)S(1)} %get-tuple-element.74), channel_id=1, source_target_pairs={{0,24},{8,0},{16,8},{24,16},{1,25},{9,1},{17,9},{25,17},{2,26},{10... | collective-permute-start | bytes 196616 | tf_op jit(solution)/shard_map/ppermute | solution.py:39
  133.9 4.3 %copy-start.24 = (s32[59]{0:T(128)S(1)}, s32[59]{0:T(128)}, u32[]{:S(2)}) copy-start(s32[59]{0:T(128)} %copy-done.23) | copy-start | bytes 712

commit v19 on v10

--- a/solution.py
+++ b/solution.py
@@ -60,41 +60,43 @@
     return lax.ppermute(piece, axis, [(i, partner(i, k, count)) for i in range(count)])
 
 
-def gather_chips(piece, behind):
+def gather_chips(piece):
     count = lax.axis_size("pipe")
-    in_halves = count == 4 and piece.shape[0] % 32 == 0
-    came = [swap(piece, "pipe", k) for k in range(1, 3 if in_halves else count)]
-    came, one, two = lax.optimization_barrier((came, behind, behind))
-    if in_halves:
-        half = piece.shape[0] // 2
-        third = [swap(came[1][:half], "pipe", 1), swap(came[0][half:], "pipe", 2)]
-        came = came + [jnp.concatenate(third)]
-    return came, one, two
+    if count != 4 or piece.shape[0] % 32:
+        return [swap(piece, "pipe", k) for k in range(1, count)]
+    first, second = swap(piece, "pipe", 1), swap(piece, "pipe", 2)
+    half = piece.shape[0] // 2
+    third = [swap(second[:half], "pipe", 1), swap(first[half:], "pipe", 2)]
+    return [first, second, jnp.concatenate(third)]
 
 
 def up_rides(adapter_up):
     return adapter_up.shape[1] % 16 == 0
 
 
-def pick(at, slot_of, adapter_down, adapter_up, data_count, blocks_dev):
+def pick(tenant_of_block, slot_of_tenant, adapter_down, adapter_up, blocks_dev, group_rows):
+    data_count = tenant_of_block.shape[0] // blocks_dev
     down_rows, ranks = adapter_down.shape[1:]
     up_rows, width = adapter_up.shape[1:]
     first_up = blocks_dev * down_rows
     rides = up_rides(adapter_up)
     total = first_up + (up_rows * width // ranks if rides else 0)
 
-    def kernel(at_ref, down_ref, up_ref, out_ref, rows, tiles, down_sem, up_sem, out_sem):
+    def kernel(
+        tenant_ref, slot_ref, down_ref, up_ref, out_ref, rows, tiles, down_sem, up_sem, out_sem
+    ):
+        own_block = lax.axis_index(("pipe", "tensor")) * group_rows // BLOCK
         downs, ups, outs = [], [], []
         for data in range(data_count):
             downs.append([])
             for block in range(blocks_dev):
                 here = rows.at[data, pl.ds(block * down_rows, down_rows)]
-                slot = slot_of(at_ref, data, block)
+                slot = slot_ref[tenant_ref[data * blocks_dev + block]]
                 downs[data].append(
                     pltpu.make_async_copy(down_ref.at[slot], here, down_sem.at[data, block])
                 )
             if rides:
-                slot = slot_of(at_ref, data, at_ref[3])
+                slot = slot_ref[tenant_ref[data * blocks_dev + own_block]]
                 ups.append(pltpu.make_async_copy(up_ref.at[slot], tiles.at[data], up_sem.at[data]))
             outs.append(pltpu.make_async_copy(rows.at[data], out_ref.at[data], out_sem.at[data]))
             for copy in downs[data] + ups[data:]:
@@ -114,7 +116,7 @@
         "pick_rows",
         VMEM_MOST,
         out_shape=pltpu.HBM((data_count, total, ranks), adapter_down.dtype),
-        in_specs=[SMEM, HBM, HBM],
+        in_specs=[SMEM, SMEM, HBM, HBM],
         out_specs=HBM,
         scratch_shapes=[
             pltpu.VMEM((data_count, total, ranks), adapter_down.dtype),
@@ -123,7 +125,7 @@
             pltpu.SemaphoreType.DMA((data_count,)),
             pltpu.SemaphoreType.DMA((data_count,)),
         ],
-    )(at, adapter_down, adapter_up)
+    )(tenant_of_block, slot_of_tenant, adapter_down, adapter_up)
 
 
 def pick_up(at, slot_of, adapter_up, data_count):
@@ -131,17 +133,23 @@
     return jnp.take(adapter_up, slots, axis=0)
 
 
-def base_product(at, tokens, weight, first, count):
+def base_product(at, tokens, weight, first, count, parts):
     pipe_count, tensor_count, rows, depth = tokens.shape
     tile = 1024
-
-    def kernel(at_ref, x_ref, w_ref, out_ref):
+    chips = pipe_count // parts
+
+    def kernel(at_ref, x_ref, w_ref, *out_refs):
         x = x_ref[...].reshape(pipe_count * rows, depth)
-        y = jnp.dot(x, w_ref[...], preferred_element_type=jnp.float32).astype(out_ref.dtype)
+        y = jnp.dot(x, w_ref[...], preferred_element_type=jnp.float32).astype(out_refs[0].dtype)
         for chip in range(pipe_count):
-            out_ref[0, which_partner(chip, at_ref[1], pipe_count)] = y[chip * rows : (chip + 1) * rows]
-
-    return call(
+            k = which_partner(chip, at_ref[1], pipe_count)
+            for part, out_ref in enumerate(out_refs):
+
+                @pl.when((k >= part * chips) & (k < (part + 1) * chips))
+                def _():
+                    out_ref[0, k - part * chips] = y[chip * rows : (chip + 1) * rows]
+
+    out = call(
         kernel,
         "base_product",
         grid_spec=pltpu.PrefetchScalarGridSpec(
@@ -154,10 +162,11 @@
                 ),
                 pl.BlockSpec((depth, tile), lambda n, s, at: (0, n)),
             ],
-            out_specs=pl.BlockSpec((1, pipe_count, rows, tile), lambda n, s, at: (s, 0, 0, n)),
+            out_specs=(pl.BlockSpec((1, chips, rows, tile), lambda n, s, at: (s, 0, 0, n)),) * parts,
         ),
-        out_shape=jax.ShapeDtypeStruct((count, pipe_count, rows, WIDTH), jnp.bfloat16),
+        out_shape=(jax.ShapeDtypeStruct((count, chips, rows, WIDTH), jnp.bfloat16),) * parts,
     )(at, tokens, weight)
+    return out
 
 
 def low_product(at, tokens, down, pipe_count, tensor_count):
@@ -491,23 +500,31 @@
     def slot_of(at_ref, data, block):
         return at_ref[4 + blocks + at_ref[4 + data * blocks_dev + block]]
 
-    a_send = pick(at, slot_of, adapter_down, adapter_up, data_count, blocks_dev)
+    a_send = pick(
+        tenant_of_block, slot_of_tenant, adapter_down, adapter_up, blocks_dev, rows
+    )
     a_recv = lax.all_to_all(a_send, "dp", 0, 0, tiled=True)
     up = None
     if not up_rides(adapter_up):
         up = lax.all_to_all(pick_up(at, slot_of, adapter_up, data_count), "dp", 0, 0, tiled=True)
         up = up.reshape(ADAPTER_RANK, WIDTH)
 
-    behind, a_send = lax.optimization_barrier((tokens, a_send))
-    cot_chips, base_tokens, x_tokens = gather_chips(cotangent, behind)
-    cot_chips = [cotangent] + cot_chips
-
+    cot_chips = [cotangent] + gather_chips(cotangent)
+
+    base_tokens, a_send = lax.optimization_barrier((tokens, a_send))
     tokens_by_group = base_tokens.reshape(pipe_count, tensor_count, rows, feature_count)
-    base_send = base_product(at, tokens_by_group, key_value_weight, 1, tensor_count - 1)
-    base_came = [swap(base_send[s - 1], "tensor", s) for s in range(1, tensor_count)]
-    base_keep = base_product(at, tokens_by_group, key_value_weight, 0, 1)[0]
+    parts = 2 if pipe_count % 2 == 0 else 1
+    chips = pipe_count // parts
+    base_send = base_product(at, tokens_by_group, key_value_weight, 1, tensor_count - 1, parts)
+    base_came = [
+        [swap(part[s - 1], "tensor", s) for part in base_send] for s in range(1, tensor_count)
+    ]
+    (base_keep,) = base_product(at, tokens_by_group, key_value_weight, 0, 1, 1)
     base_chip = [
-        sum([base_keep[k].astype(jnp.float32)] + [b[k].astype(jnp.float32) for b in base_came])
+        sum(
+            [base_keep[0, k].astype(jnp.float32)]
+            + [came[k // chips][k % chips].astype(jnp.float32) for came in base_came]
+        )
         for k in range(pipe_count)
     ]
     base_chip[1:] = [piece.astype(jnp.bfloat16) for piece in base_chip[1:]]
@@ -518,7 +535,7 @@
     ]
     input_base = cotangent_product(at, cot_pieces, key_value_weight)
 
-    x_send = x_tokens.T.reshape(data_count, down_rows, tok_dev)
+    x_send = base_tokens.T.reshape(data_count, down_rows, tok_dev)
 
     a_recv, x_send, input_base, base_chip_came[:2] = lax.optimization_barrier(
         (a_recv, x_send, input_base, base_chip_came[:2])

time: 138 us -> 140 us (1.014)
  starting transfers between devices: 31.9 us -> 37.9 us
  waiting for transfers between devices: 46.8 us -> 42.8 us
    all_to_all x1, waiting for transfers between devices: 11.4 us -> 0.01 us  [body(): a_recv = lax.all_to_all(a_send, 'dp', 0, 0, tiled=True)]
    ppermute x21 -> x22, waiting for transfers between devices: 25.3 us -> 34 us  [swap(): lax.ppermute(piece, axis, [(i, partner(i, k, count)) for i in range(count)])]
    ppermute x6, starting transfers between devices: 6.77 us -> 9.58 us  [shift(): lax.ppermute(piece, axis, [(i, (i + k) % count) for i in range(count)])]
    ppermute x21 -> x22, starting transfers between devices: 15.8 us -> 17.4 us  [swap(): lax.ppermute(piece, axis, [(i, partner(i, k, count)) for i in range(count)])]
    all_to_all x1, starting transfers between devices: 4.88 us -> 6.46 us  [body(): a_recv = lax.all_to_all(a_send, 'dp', 0, 0, tiled=True)]
    unnamed x39 -> x47, local copies, waits for them, and re-layouts: 12.9 us -> 13.7 us
  transfers between devices with their start and end apart: 29 -> 30, of which waited for: 16 -> 15; matrix products, arithmetic and copies ran while one was open for 7% -> 6% of each run, Pallas kernels for 25% -> 22%
where the time goes in v19:
time: 140 us
  waiting for transfers between devices  42.8 us (31%)
  starting transfers between devices  37.9 us (27%)
  Pallas kernels  36.2 us (26%)
  local copies, waits for them, and re-layouts  19.4 us (14%)
  other arithmetic  2.29 us (2%)
    ppermute x22, waiting for transfers between devices, swap(): lax.ppermute(piece, axis, [(i, partner(i, k, count)) for i in range(count)])  34 us
    ppermute x22, starting transfers between devices, swap(): lax.ppermute(piece, axis, [(i, partner(i, k, count)) for i in range(count)])  17.4 us
    unnamed x47, local copies, waits for them, and re-layouts  13.7 us
    ppermute x6, starting transfers between devices, shift(): lax.ppermute(piece, axis, [(i, (i + k) % count) for i in range(count)])  9.58 us
    pallas_call x1, Pallas kernels, cotangent_product(): call(kernel, 'cotangent_product', grid=(depth // tile,), in_specs=[SMEM,...  7.93 us
    pallas_call x2, Pallas kernels, base_product(): call(kernel, 'base_product', grid_spec=pltpu.PrefetchScalarGridSpec(num_s...  7.73 us
    all_to_all x1, starting transfers between devices, body(): a_recv = lax.all_to_all(a_send, 'dp', 0, 0, tiled=True)  6.46 us
    pallas_call x1, Pallas kernels, grad_down(): call(kernel, 'grad_down', VMEM_MOST, in_specs=[SMEM, HBM] + [VMEM] * tens...  5.15 us
  transfers between devices with their start and end apart: 30, of which 15 were waited for; matrix products, arithmetic and copies ran while one was open for 6% of the time, Pallas kernels for 22%

profile of v19, /device:TPU:0, one launch (start us, length us, event | category | flops | bytes accessed | tf_op | source)
XLA Modules:
  0.0 139.7 jit_solution(6536521719455793373)
XLA Ops:
  0.6 4.3 %pick_rows.1 = bf16[4,2304,128]{2,1,0:T(8,128)(2,1)} custom-call(s32[32]{0:T(128)} %tenant_ref.1, s32[24]{0:T(128)} %slot_ref.1, bf16[24,256,128]{2,1,0:T(8,128)(2,1)} %down_ref.1, bf16[24,16,2048]{2,1,0:T(8,128)(2,1)} %up_ref.1), custom_call_target="tpu_custom_call" | custom-call | flops 1024 | bytes 1024 | tf_op jit(solution)/shard_map/pick_rows/pallas_call | solution.py:114
  5.0 6.5 %all-to-all-start = ((bf16[4,2304,128]{2,1,0:T(8,128)(2,1)}), bf16[4,2304,128]{2,1,0:T(8,128)(2,1)S(1)}, u32[]{:S(2)}, u32[]{:S(2)}) async-start(bf16[4,2304,128]{2,1,0:T(8,128)(2,1)} %pick_rows.1), calls=%async_computation | async-start | bytes 4718592 | tf_op jit(solution)/shard_map/all_to_all | solution.py:506
  11.5 1.5 %collective-permute-start.1 = (bf16[128,2048]{1,0:T(8,128)(2,1)S(1)}, bf16[128,2048]{1,0:T(8,128)(2,1)S(1)}, u32[]{:S(2)}, u32[]{:S(2)}) collective-permute-start(bf16[128,2048]{1,0:T(8,128)(2,1)S(1)} %copy-done.8), channel_id=1, source_target_pairs={{0,4},{2,6},{4,0},{6,2},{1,5},{3,7},{5,1},{7,3},{8,12},{10,14},{12... | collective-permute-start | bytes 1572872 | tf_op jit(solution)/shard_map/ppermute | solution.py:60
  13.0 0.1 concatenate.6.at_ref
  13.1 2.2 %copy-done = bf16[1024,2048]{1,0:T(8,128)(2,1)S(1)} copy-done((bf16[1024,2048]{1,0:T(8,128)(2,1)S(1)}, bf16[1024,2048]{1,0:T(8,128)(2,1)}, u32[]{:S(2)}) %copy-start) | copy-done | bytes 4194328
  15.3 1.6 %copy-done.2 = bf16[1024,1024]{1,0:T(8,128)(2,1)S(1)} copy-done((bf16[1024,1024]{1,0:T(8,128)(2,1)S(1)}, bf16[1024,1024]{1,0:T(8,128)(2,1)}, u32[]{:S(2)}) %copy-start.2) | copy-done | bytes 2097176
  16.9 3.9 %base_product.3 = (bf16[1,2,128,2048]{3,2,1,0:T(8,128)(2,1)S(1)}, bf16[1,2,128,2048]{3,2,1,0:T(8,128)(2,1)S(1)}) custom-call(s32[60]{0:T(128)S(1)} %concatenate.6.at_ref, bf16[4,2,128,1024]{3,2,1,0:T(8,128)(2,1)S(1)} %bitcast.74, bf16[1024,2048]{1,0:T(8,128)(2,1)S(1)} %copy-done), custom_call_target="tpu_custom_call" | custom-call | flops 1024 | bytes 1024 | tf_op jit(solution)/shard_map/base_product/pallas_call | solution.py:152
  20.8 0.5 collective-permute-start.8
  21.3 1.5 %collective-permute-start = (bf16[128,2048]{1,0:T(8,128)(2,1)S(1)}, bf16[128,2048]{1,0:T(8,128)(2,1)}, u32[]{:S(2)}, u32[]{:S(2)}) collective-permute-start(bf16[128,2048]{1,0:T(8,128)(2,1)S(1)} %copy-done.8), channel_id=1, source_target_pairs={{0,2},{2,0},{4,6},{6,4},{1,3},{3,1},{5,7},{7,5},{8,10},{10,8},{12,... | collective-permute-start | bytes 1572872 | tf_op jit(solution)/shard_map/ppermute | solution.py:60
  22.8 2.0 %collective-permute-done.1.rest_2_.rest_4_ = bf16[128,2048]{1,0:T(8,128)(2,1)S(1)} collective-permute-done((bf16[128,2048]{1,0:T(8,128)(2,1)S(1)}, bf16[128,2048]{1,0:T(8,128)(2,1)S(1)}, u32[]{:S(2)}, u32[]{:S(2)}) %collective-permute-start.1) | collective-permute-done | bytes 524320 | tf_op jit(solution)/shard_map/ppermute | solution.py:60
  24.9 1.6 %collective-permute-start.2 = (bf16[64,2048]{1,0:T(8,128)(2,1)S(1)}, bf16[64,2048]{1,0:T(8,128)(2,1)S(1)}, u32[]{:S(2)}, u32[]{:S(2)}) collective-permute-start(bf16[64,2048]{1,0:T(8,128)(2,1)S(1)} %slice.64), channel_id=1, source_target_pairs={{0,2},{2,0},{4,6},{6,4},{1,3},{3,1},{5,7},{7,5},{8,10},{10,8},{12,... | collective-permute-start | bytes 786440 | tf_op jit(solution)/shard_map/ppermute | solution.py:60
  26.5 9.7 %collective-permute-done.rest_1_.rest_3_ = bf16[128,2048]{1,0:T(8,128)(2,1)} collective-permute-done((bf16[128,2048]{1,0:T(8,128)(2,1)S(1)}, bf16[128,2048]{1,0:T(8,128)(2,1)}, u32[]{:S(2)}, u32[]{:S(2)}) %collective-permute-start) | collective-permute-done | bytes 524320 | tf_op jit(solution)/shard_map/ppermute | solution.py:60
  36.2 1.0 slice.65
  37.2 0.6 collective-permute-start.3
  37.8 3.8 %base_product.2 = bf16[1,4,128,2048]{3,2,1,0:T(8,128)(2,1)S(1)} custom-call(s32[60]{0:T(128)S(1)} %concatenate.6.at_ref, bf16[4,2,128,1024]{3,2,1,0:T(8,128)(2,1)S(1)} %bitcast.75, bf16[1024,2048]{1,0:T(8,128)(2,1)S(1)} %copy-done), custom_call_target="tpu_custom_call" | custom-call | flops 1024 | bytes 1024 | tf_op jit(solution)/shard_map/base_product/pallas_call | solution.py:152
  41.6 0.6 collective-permute-start.6
  42.2 0.7 constant_dynamic-update-slice_fusion.1
  42.9 0.9 collective-permute-done.3
  43.8 0.7 constant_dynamic-update-slice_fusion.rest_3_.rest_5_
  44.6 0.5 collective-permute-start.7
  45.1 2.1 %convert_add_fusion = (f32[128,2048]{1,0:T(8,128)}, bf16[128,2048]{1,0:T(8,128)(2,1)}, bf16[128,2048]{1,0:T(8,128)(2,1)}, bf16[128,2048]{1,0:T(8,128)(2,1)}) fusion(bf16[2,128,2048]{2,1,0:T(8,128)(2,1)S(1)} %collective-permute-done.8, bf16[1,4,128,2048]{3,2,1,0:T(8,128)(2,1)S(1)} %base_product.2, bf16[2,128,2048]{2,1,0:T(8,128)(2,1)S(1)} %collective-permute-done.10), kind=kLoop, calls=%fused_computation | loop fusion | flops 3932160 | bytes 6815744 | tf_op jit(solution)/shard_map/add | solution.py:524
  47.2 1.5 %collective-permute-start.9 = (bf16[128,2048]{1,0:T(8,128)(2,1)}, bf16[128,2048]{1,0:T(8,128)(2,1)}, u32[]{:S(2)}, u32[]{:S(2)}) collective-permute-start(bf16[128,2048]{1,0:T(8,128)(2,1)} %get-tuple-element.53), channel_id=1, source_target_pairs={{0,2},{2,0},{4,6},{6,4},{1,3},{3,1},{5,7},{7,5},{8,10},{10,8},{12,... | collective-permute-start | bytes 1572872 | tf_op jit(solution)/shard_map/ppermute | solution.py:60
  48.6 0.8 copy-done.12
  49.4 0.6 collective-permute-start.11
  50.1 3.9 %copy.11 = bf16[1024,1024]{1,0:T(8,128)(2,1)} copy(bf16[1024,1024]{0,1:T(8,128)(2,1)} %bitcast.73) | data formatting | bytes 4194304 | tf_op jit(solution)/shard_map/transpose | solution.py:538
  54.1 2.2 %copy-done.1 = bf16[1024,2048]{1,0:T(8,128)(2,1)S(1)} copy-done((bf16[1024,2048]{1,0:T(8,128)(2,1)S(1)}, bf16[1024,2048]{1,0:T(8,128)(2,1)}, u32[]{:S(2)}) %copy-start.1) | copy-done | bytes 4194328
  56.2 1.0 copy-done.13
  57.3 7.9 %cotangent_product.1.base_ref = f32[1024,1024]{1,0:T(8,128)S(1)} custom-call(s32[60]{0:T(128)S(1)} %concatenate.6.at_ref, bf16[1024,2048]{1,0:T(8,128)(2,1)S(1)} %copy-done.1, bf16[128,2048]{1,0:T(8,128)(2,1)S(1)} %copy-done.8, bf16[128,2048]{1,0:T(8,128)(2,1)} %collective-permute-done.rest_1_.rest_3_, ...), custom_call_target="tpu_custom_call" | custom-call | flops 1024 | bytes 1024 | tf_op jit(solution)/shard_map/cotangent_product/pallas_call | solution.py:226
  65.2 2.0 %copy-done.5 = f32[1024,1024]{1,0:T(8,128)} copy-done((f32[1024,1024]{1,0:T(8,128)}, f32[1024,1024]{1,0:T(8,128)S(1)}, u32[]{:S(2)}) %copy-start.5) | copy-done | bytes 4194328
  67.2 0.4 own_rows.1
  67.6 0.7 copy-done.16
  68.3 3.8 %collective-permute-start.15 = (bf16[128,128]{1,0:T(8,128)(2,1)S(1)}, bf16[128,128]{1,0:T(8,128)(2,1)S(1)}, u32[]{:S(2)}, u32[]{:S(2)}) collective-permute-start(bf16[128,128]{1,0:T(8,128)(2,1)S(1)} %get-tuple-element.36), channel_id=1, source_target_pairs={{0,24},{8,0},{16,8},{24,16},{1,25},{9,1},{17,9},{25,17},{2,26},{10... | collective-permute-start | bytes 98312 | tf_op jit(solution)/shard_map/ppermute | solution.py:39
  72.2 1.2 collective-permute-start.13
  73.3 0.4 collective-permute-done.15
  73.8 3.2 %collective-permute-done.14 = bf16[128,128]{1,0:T(8,128)(2,1)S(1)} collective-permute-done((bf16[128,128]{1,0:T(8,128)(2,1)S(1)}, bf16[128,128]{1,0:T(8,128)(2,1)S(1)}, u32[]{:S(2)}, u32[]{:S(2)}) %collective-permute-start.14) | collective-permute-done | bytes 32800 | tf_op jit(solution)/shard_map/ppermute | solution.py:39
  77.0 0.9 collective-permute-done.13
  77.9 4.4 %all-to-all-start.1 = ((bf16[4,256,1024]{2,1,0:T(8,128)(2,1)}), bf16[4,256,1024]{2,1,0:T(8,128)(2,1)}, u32[]{:S(2)}, u32[]{:S(2)}) async-start(bf16[4,256,1024]{2,1,0:T(8,128)(2,1)} %bitcast.79), calls=%async_computation.1 | async-start | bytes 4194304 | tf_op jit(solution)/shard_map/all_to_all | solution.py:546
  82.3 1.5 %collective-permute-start.12 = (bf16[128,2048]{1,0:T(8,128)(2,1)S(1)}, bf16[128,2048]{1,0:T(8,128)(2,1)S(1)}, u32[]{:S(2)}, u32[]{:S(2)}) collective-permute-start(bf16[128,2048]{1,0:T(8,128)(2,1)S(1)} %copy-done.20), channel_id=1, source_target_pairs={{0,6},{2,4},{4,2},{6,0},{1,7},{3,5},{5,3},{7,1},{8,14},{10,12},{12... | collective-permute-start | bytes 1572872 | tf_op jit(solution)/shard_map/ppermute | solution.py:60
  83.8 11.4 %collective-permute-done.12.rest_3_ = bf16[128,2048]{1,0:T(8,128)(2,1)S(1)} collective-permute-done((bf16[128,2048]{1,0:T(8,128)(2,1)S(1)}, bf16[128,2048]{1,0:T(8,128)(2,1)S(1)}, u32[]{:S(2)}, u32[]{:S(2)}) %collective-permute-start.12) | collective-permute-done | bytes 524320 | tf_op jit(solution)/shard_map/ppermute | solution.py:60
  95.2 1.6 %copy-done.4 = bf16[1024,1024]{1,0:T(8,128)(2,1)S(1)} copy-done((bf16[1024,1024]{1,0:T(8,128)(2,1)S(1)}, bf16[1024,1024]{1,0:T(8,128)(2,1)}, u32[]{:S(2)}) %copy-start.4) | copy-done | bytes 2097176
  96.8 1.3 low_product.1
  98.2 1.5 %collective-permute-start.21 = (bf16[4,128,128]{2,1,0:T(8,128)(2,1)S(1)}, bf16[4,128,128]{2,1,0:T(8,128)(2,1)S(1)}, u32[]{:S(2)}, u32[]{:S(2)}) collective-permute-start(bf16[4,128,128]{2,1,0:T(8,128)(2,1)S(1)} %get-tuple-element.63), channel_id=1, source_target_pairs={{0,4},{2,6},{4,0},{6,2},{1,5},{3,7},{5,1},{7,3},{8,12},{10,14},{12... | collective-permute-start | bytes 393224 | tf_op jit(solution)/shard_map/ppermute | solution.py:60
  99.7 0.5 collective-permute-start.20
  100.2 1.6 %collective-permute-start.22 = (bf16[4,128,128]{2,1,0:T(8,128)(2,1)S(1)}, bf16[4,128,128]{2,1,0:T(8,128)(2,1)S(1)}, u32[]{:S(2)}, u32[]{:S(2)}) collective-permute-start(bf16[4,128,128]{2,1,0:T(8,128)(2,1)S(1)} %get-tuple-element.63), channel_id=1, source_target_pairs={{0,6},{2,4},{4,2},{6,0},{1,7},{3,5},{5,3},{7,1},{8,14},{10,12},{12... | collective-permute-start | bytes 393224 | tf_op jit(solution)/shard_map/ppermute | solution.py:60
  101.8 1.4 %collective-permute-start.19 = (bf16[4,128,128]{2,1,0:T(8,128)(2,1)S(1)}, bf16[4,128,128]{2,1,0:T(8,128)(2,1)S(1)}, u32[]{:S(2)}, u32[]{:S(2)}) collective-permute-start(bf16[4,128,128]{2,1,0:T(8,128)(2,1)S(1)} %fusion.3), channel_id=1, source_target_pairs={{0,6},{2,4},{4,2},{6,0},{1,7},{3,5},{5,3},{7,1},{8,14},{10,12},{12... | collective-permute-start | bytes 393224 | tf_op jit(solution)/shard_map/ppermute | solution.py:60
  103.2 0.6 collective-permute-start.18
  103.9 0.3 collective-permute-done.21
  104.2 1.2 collective-permute-start.17
  105.4 0.6 collective-permute-done.20
  106.0 3.0 %collective-permute-done.22 = bf16[4,128,128]{2,1,0:T(8,128)(2,1)S(1)} collective-permute-done((bf16[4,128,128]{2,1,0:T(8,128)(2,1)S(1)}, bf16[4,128,128]{2,1,0:T(8,128)(2,1)S(1)}, u32[]{:S(2)}, u32[]{:S(2)}) %collective-permute-start.22) | collective-permute-done | bytes 131104 | tf_op jit(solution)/shard_map/ppermute | solution.py:60
  109.1 2.6 %collective-permute-done.19 = bf16[4,128,128]{2,1,0:T(8,128)(2,1)S(1)} collective-permute-done((bf16[4,128,128]{2,1,0:T(8,128)(2,1)S(1)}, bf16[4,128,128]{2,1,0:T(8,128)(2,1)S(1)}, u32[]{:S(2)}, u32[]{:S(2)}) %collective-permute-start.19) | collective-permute-done | bytes 131104 | tf_op jit(solution)/shard_map/ppermute | solution.py:60
  111.7 1.6 %collective-permute-done.18 = bf16[4,128,128]{2,1,0:T(8,128)(2,1)S(1)} collective-permute-done((bf16[4,128,128]{2,1,0:T(8,128)(2,1)S(1)}, bf16[4,128,128]{2,1,0:T(8,128)(2,1)S(1)}, u32[]{:S(2)}, u32[]{:S(2)}) %collective-permute-start.18) | collective-permute-done | bytes 131104 | tf_op jit(solution)/shard_map/ppermute | solution.py:60
  113.3 0.4 collective-permute-done.17
  113.7 0.1 add_convert_fusion.low_ref.rest_0_
  113.9 1.3 collective-permute-done.24.rest_1_
  115.3 2.2 %grad_up_pieces.1 = bf16[4,8,16,256]{3,2,1,0:T(8,128)(2,1)S(1)} custom-call(s32[60]{0:T(128)S(1)} %concatenate.6.at_ref, bf16[4,128,128]{2,1,0:T(8,128)(2,1)S(1)} %add_convert_fusion.low_ref.rest_0_, bf16[4,128,128]{2,1,0:T(8,128)(2,1)S(1)} %collective-permute-done.24.rest_1_, bf16[128,2048]{1,0:T(8,128)(2,1)S(1)} %copy-done.8, ...), custom_call_target="tpu_custom_call" | custom-call | flops 1024 | bytes 1024 | tf_op jit(solution)/shard_map/grad_up_pieces/pallas_call | solution.py:377
  117.5 3.5 %collective-permute-start.27 = (bf16[8,16,256]{2,1,0:T(8,128)(2,1)S(1)}, bf16[8,16,256]{2,1,0:T(8,128)(2,1)S(1)}, u32[]{:S(2)}, u32[]{:S(2)}) collective-permute-start(bf16[8,16,256]{2,1,0:T(8,128)(2,1)S(1)} %get-tuple-element.58), channel_id=1, source_target_pairs={{0,24},{8,0},{16,8},{24,16},{1,25},{9,1},{17,9},{25,17},{2,26},{10... | collective-permute-start | bytes 196616 | tf_op jit(solution)/shard_map/ppermute | solution.py:39
  121.0 1.1 collective-permute-start.25
  122.1 2.5 %keys_and_values.1 = bf16[128,2048]{1,0:T(8,128)(2,1)} custom-call(s32[60]{0:T(128)S(1)} %concatenate.6.at_ref, bf16[4,128,128]{2,1,0:T(8,128)(2,1)S(1)} %add_convert_fusion.low_ref.rest_0_, bf16[64,2048]{1,0:T(8,128)(2,1)S(1)} %copy-done.17, f32[128,2048]{1,0:T(8,128)S(1)} %copy-done.9, bf16[128,2048]{1,0:T(8,128)(2,1)} %collective-permute-done.9.rest_1_, ...), custom_call_target="tpu_custom_call" | custom-call | flops 1024 | bytes 1024 | tf_op jit(solution)/shard_map/keys_and_values/pallas_call | solution.py:470
  124.6 3.3 %input_gradient.1 = bf16[1024,1024]{1,0:T(8,128)(2,1)} custom-call(s32[60]{0:T(128)S(1)} %concatenate.6.at_ref, f32[1024,1024]{1,0:T(8,128)S(1)} %copy-done.6, bf16[4,2304,128]{2,1,0:T(8,128)(2,1)S(1)} %all-to-all-done.came_ref.a_ref, bf16[4,4,128,128]{3,2,1,0:T(8,128)(2,1)S(1)} %pad_maximum_fusion.rest_0_, ...), custom_call_target="tpu_custom_call" | custom-call | flops 1024 | bytes 1024 | tf_op jit(solution)/shard_map/input_gradient/pallas_call | solution.py:268
  127.9 0.8 copy-done.15
  128.7 4.3 %all-to-all-done.1.x_ref = bf16[4,256,1024]{2,1,0:T(8,128)(2,1)} async-done(((bf16[4,256,1024]{2,1,0:T(8,128)(2,1)}), bf16[4,256,1024]{2,1,0:T(8,128)(2,1)}, u32[]{:S(2)}, u32[]{:S(2)}) %all-to-all-start.1) | async-done | bytes 2097184 | tf_op jit(solution)/shard_map/all_to_all | solution.py:546
  133.0 5.2 %grad_down.1 = f32[24,256,128]{2,1,0:T(8,128)} custom-call(s32[60]{0:T(128)} %copy-done.18, bf16[4,256,1024]{2,1,0:T(8,128)(2,1)} %all-to-all-done.1.x_ref, bf16[4,4,128,128]{3,2,1,0:T(8,128)(2,1)} %copy-done.7, bf16[4,4,128,128]{3,2,1,0:T(8,128)(2,1)} %copy-done.15), custom_call_target="tpu_custom_call" | custom-call | flops 1024 | bytes 1024 | tf_op jit(solution)/shard_map/grad_down/pallas_call | solution.py:316
  138.2 1.5 %grad_up.1 = f32[24,16,256]{2,1,0:T(8,128)} custom-call(s32[60]{0:T(128)S(1)} %copy-done.19, bf16[8,16,256]{2,1,0:T(8,128)(2,1)S(1)} %get-tuple-element.48.rest_0_, bf16[8,16,256]{2,1,0:T(8,128)(2,1)S(1)} %collective-permute-done.25.rest_1_, bf16[8,16,256]{2,1,0:T(8,128)(2,1)S(1)} %collective-permute-done.26.rest_2_, ...), custom_call_target="tpu_custom_call" | custom-call | flops 1024 | bytes 1024 | tf_op jit(solution)/shard_map/grad_up/pallas_call | solution.py:404
  (66 shorter events, 0.6 us)
Async XLA Ops:
  5.0 6.5 %copy-start.8 = (bf16[128,2048]{1,0:T(8,128)(2,1)S(1)}, bf16[128,2048]{1,0:T(8,128)(2,1)}, u32[]{:S(2)}) copy-start(bf16[128,2048]{1,0:T(8,128)(2,1)} %rest_2_.1) | copy-start | bytes 1572868
  5.0 8.0 %copy-start.21 = (s32[32]{0:T(128)S(1)}, s32[32]{0:T(128)}, u32[]{:S(2)}) copy-start(s32[32]{0:T(128)} %tenant_ref.1) | copy-start | bytes 388
  5.0 8.0 %copy-start.22 = (s32[24]{0:T(128)S(1)}, s32[24]{0:T(128)}, u32[]{:S(2)}) copy-start(s32[24]{0:T(128)} %slot_ref.1) | copy-start | bytes 292
  5.0 62.2 %all-to-all-start = ((bf16[4,2304,128]{2,1,0:T(8,128)(2,1)}), bf16[4,2304,128]{2,1,0:T(8,128)(2,1)S(1)}, u32[]{:S(2)}, u32[]{:S(2)}) async-start(bf16[4,2304,128]{2,1,0:T(8,128)(2,1)} %pick_rows.1), calls=%async_computation | async-start | bytes 4718592 | tf_op jit(solution)/shard_map/all_to_all | solution.py:506
  11.5 13.4 %collective-permute-start.1 = (bf16[128,2048]{1,0:T(8,128)(2,1)S(1)}, bf16[128,2048]{1,0:T(8,128)(2,1)S(1)}, u32[]{:S(2)}, u32[]{:S(2)}) collective-permute-start(bf16[128,2048]{1,0:T(8,128)(2,1)S(1)} %copy-done.8), channel_id=1, source_target_pairs={{0,4},{2,6},{4,0},{6,2},{1,5},{3,7},{5,1},{7,3},{8,12},{10,14},{12... | collective-permute-start | bytes 1572872 | tf_op jit(solution)/shard_map/ppermute | solution.py:60
  13.1 111.5 %copy-start.18 = (s32[60]{0:T(128)}, s32[60]{0:T(128)S(1)}, u32[]{:S(2)}) copy-start(s32[60]{0:T(128)S(1)} %concatenate.6.at_ref) | copy-start | bytes 724
  13.1 2.2 %copy-start = (bf16[1024,2048]{1,0:T(8,128)(2,1)S(1)}, bf16[1024,2048]{1,0:T(8,128)(2,1)}, u32[]{:S(2)}) copy-start(bf16[1024,2048]{1,0:T(8,128)(2,1)} %w_ref.5) | copy-start | bytes 12582916
  15.3 1.6 %copy-start.2 = (bf16[1024,1024]{1,0:T(8,128)(2,1)S(1)}, bf16[1024,1024]{1,0:T(8,128)(2,1)}, u32[]{:S(2)}) copy-start(bf16[1024,1024]{1,0:T(8,128)(2,1)} %x_ref.1) | copy-start | bytes 6291460
  16.9 20.9 %copy-start.3 = (bf16[1024,1024]{1,0:T(8,128)(2,1)S(1)}, bf16[1024,1024]{1,0:T(8,128)(2,1)}, u32[]{:S(2)}) copy-start(bf16[1024,1024]{1,0:T(8,128)(2,1)} %x_ref.1) | copy-start | bytes 6291460
  20.8 23.8 %collective-permute-start.10 = (bf16[2,128,2048]{2,1,0:T(8,128)(2,1)S(1)}, bf16[2,128,2048]{2,1,0:T(8,128)(2,1)S(1)}, u32[]{:S(2)}, u32[]{:S(2)}) collective-permute-start(bf16[2,128,2048]{2,1,0:T(8,128)(2,1)S(1)} %bitcast.78), channel_id=1, source_target_pairs={{0,1},{1,0},{2,3},{3,2},{4,5},{5,4},{6,7},{7,6},{8,9},{9,8},{10,11... | collective-permute-start | bytes 3145736 | tf_op jit(solution)/shard_map/ppermute | solution.py:60
  20.8 24.2 %collective-permute-start.8 = (bf16[2,128,2048]{2,1,0:T(8,128)(2,1)S(1)}, bf16[2,128,2048]{2,1,0:T(8,128)(2,1)S(1)}, u32[]{:S(2)}, u32[]{:S(2)}) collective-permute-start(bf16[2,128,2048]{2,1,0:T(8,128)(2,1)S(1)} %bitcast.77), channel_id=1, source_target_pairs={{0,1},{1,0},{2,3},{3,2},{4,5},{5,4},{6,7},{7,6},{8,9},{9,8},{10,11... | collective-permute-start | bytes 3145736 | tf_op jit(solution)/shard_map/ppermute | solution.py:60
  21.3 14.9 %collective-permute-start = (bf16[128,2048]{1,0:T(8,128)(2,1)S(1)}, bf16[128,2048]{1,0:T(8,128)(2,1)}, u32[]{:S(2)}, u32[]{:S(2)}) collective-permute-start(bf16[128,2048]{1,0:T(8,128)(2,1)S(1)} %copy-done.8), channel_id=1, source_target_pairs={{0,2},{2,0},{4,6},{6,4},{1,3},{3,1},{5,7},{7,5},{8,10},{10,8},{12,... | collective-permute-start | bytes 1572872 | tf_op jit(solution)/shard_map/ppermute | solution.py:60
  24.9 29.2 %copy-start.10 = (bf16[128,2048]{1,0:T(8,128)(2,1)}, bf16[128,2048]{1,0:T(8,128)(2,1)S(1)}, u32[]{:S(2)}) copy-start(bf16[128,2048]{1,0:T(8,128)(2,1)S(1)} %collective-permute-done.1.rest_2_.rest_4_) | copy-start | bytes 1572868
  24.9 16.7 %collective-permute-start.2 = (bf16[64,2048]{1,0:T(8,128)(2,1)S(1)}, bf16[64,2048]{1,0:T(8,128)(2,1)S(1)}, u32[]{:S(2)}, u32[]{:S(2)}) collective-permute-start(bf16[64,2048]{1,0:T(8,128)(2,1)S(1)} %slice.64), channel_id=1, source_target_pairs={{0,2},{2,0},{4,6},{6,4},{1,3},{3,1},{5,7},{7,5},{8,10},{10,8},{12,... | collective-permute-start | bytes 786440 | tf_op jit(solution)/shard_map/ppermute | solution.py:60
  37.2 6.6 %collective-permute-start.3 = (bf16[64,2048]{1,0:T(8,128)(2,1)S(1)}, bf16[64,2048]{1,0:T(8,128)(2,1)S(1)}, u32[]{:S(2)}, u32[]{:S(2)}) collective-permute-start(bf16[64,2048]{1,0:T(8,128)(2,1)S(1)} %slice.65), channel_id=1, source_target_pairs={{0,4},{2,6},{4,0},{6,2},{1,5},{3,7},{5,1},{7,3},{8,12},{10,14},{12... | collective-permute-start | bytes 786440 | tf_op jit(solution)/shard_map/ppermute | solution.py:60
  37.8 10.9 %collective-permute-start.4 = (bf16[128,2048]{1,0:T(8,128)(2,1)S(1)}, bf16[128,2048]{1,0:T(8,128)(2,1)S(1)}, u32[]{:S(2)}, u32[]{:S(2)}) collective-permute-start(bf16[128,2048]{1,0:T(8,128)(2,1)S(1)} %copy-done.8), channel_id=1, source_target_pairs={{0,1},{1,0},{2,3},{3,2},{4,5},{5,4},{6,7},{7,6},{8,9},{9,8},{10,11... | collective-permute-start | bytes 1572872 | tf_op jit(solution)/shard_map/ppermute | solution.py:60
  41.6 12.4 %collective-permute-start.6 = (bf16[128,2048]{1,0:T(8,128)(2,1)S(1)}, bf16[128,2048]{1,0:T(8,128)(2,1)}, u32[]{:S(2)}, u32[]{:S(2)}) collective-permute-start(bf16[128,2048]{1,0:T(8,128)(2,1)S(1)} %collective-permute-done.1.rest_2_.rest_4_), channel_id=1, source_target_pairs={{0,1},{1,0},{2,3},{3,2},{4,5},{5,4},{6,7},{7,6},{8,9},{9,8},{10,11... | collective-permute-start | bytes 1572872 | tf_op jit(solution)/shard_map/ppermute | solution.py:60
  43.8 10.2 %collective-permute-start.5 = (bf16[128,2048]{1,0:T(8,128)(2,1)}, bf16[128,2048]{1,0:T(8,128)(2,1)}, u32[]{:S(2)}, u32[]{:S(2)}) collective-permute-start(bf16[128,2048]{1,0:T(8,128)(2,1)} %collective-permute-done.rest_1_.rest_3_), channel_id=1, source_target_pairs={{0,1},{1,0},{2,3},{3,2},{4,5},{5,4},{6,7},{7,6},{8,9},{9,8},{10,11... | collective-permute-start | bytes 1572872 | tf_op jit(solution)/shard_map/ppermute | solution.py:60
  44.6 9.5 %collective-permute-start.7 = (bf16[128,2048]{1,0:T(8,128)(2,1)}, bf16[128,2048]{1,0:T(8,128)(2,1)}, u32[]{:S(2)}, u32[]{:S(2)}) collective-permute-start(bf16[128,2048]{1,0:T(8,128)(2,1)} %constant_dynamic-update-slice_fusion.rest_3_.rest_5_), channel_id=1, source_target_pairs={{0,1},{1,0},{2,3},{3,2},{4,5},{5,4},{6,7},{7,6},{8,9},{9,8},{10,11... | collective-permute-start | bytes 1572872 | tf_op jit(solution)/shard_map/ppermute | solution.py:60
  47.2 20.0 %collective-permute-start.9 = (bf16[128,2048]{1,0:T(8,128)(2,1)}, bf16[128,2048]{1,0:T(8,128)(2,1)}, u32[]{:S(2)}, u32[]{:S(2)}) collective-permute-start(bf16[128,2048]{1,0:T(8,128)(2,1)} %get-tuple-element.53), channel_id=1, source_target_pairs={{0,2},{2,0},{4,6},{6,4},{1,3},{3,1},{5,7},{7,5},{8,10},{10,8},{12,... | collective-permute-start | bytes 1572872 | tf_op jit(solution)/shard_map/ppermute | solution.py:60
  48.6 0.8 copy-start.12
  49.4 17.8 %collective-permute-start.11 = (bf16[128,2048]{1,0:T(8,128)(2,1)}, bf16[128,2048]{1,0:T(8,128)(2,1)}, u32[]{:S(2)}, u32[]{:S(2)}) collective-permute-start(bf16[128,2048]{1,0:T(8,128)(2,1)} %get-tuple-element.56), channel_id=1, source_target_pairs={{0,4},{2,6},{4,0},{6,2},{1,5},{3,7},{5,1},{7,3},{8,12},{10,14},{12... | collective-permute-start | bytes 1572872 | tf_op jit(solution)/shard_map/ppermute | solution.py:60
  54.0 2.2 %copy-start.1 = (bf16[1024,2048]{1,0:T(8,128)(2,1)S(1)}, bf16[1024,2048]{1,0:T(8,128)(2,1)}, u32[]{:S(2)}) copy-start(bf16[1024,2048]{1,0:T(8,128)(2,1)} %w_ref.5) | copy-start | bytes 12582916
  56.2 1.0 copy-start.13
  65.2 2.0 %copy-start.5 = (f32[1024,1024]{1,0:T(8,128)}, f32[1024,1024]{1,0:T(8,128)S(1)}, u32[]{:S(2)}) copy-start(f32[1024,1024]{1,0:T(8,128)S(1)} %cotangent_product.1.base_ref) | copy-start | bytes 12582916
  67.6 0.7 copy-start.16
  68.3 14.0 %copy-start.20 = (bf16[128,2048]{1,0:T(8,128)(2,1)S(1)}, bf16[128,2048]{1,0:T(8,128)(2,1)}, u32[]{:S(2)}) copy-start(bf16[128,2048]{1,0:T(8,128)(2,1)} %get-tuple-element.57) | copy-start | bytes 1572868
  68.3 5.4 %collective-permute-start.15 = (bf16[128,128]{1,0:T(8,128)(2,1)S(1)}, bf16[128,128]{1,0:T(8,128)(2,1)S(1)}, u32[]{:S(2)}, u32[]{:S(2)}) collective-permute-start(bf16[128,128]{1,0:T(8,128)(2,1)S(1)} %get-tuple-element.36), channel_id=1, source_target_pairs={{0,24},{8,0},{16,8},{24,16},{1,25},{9,1},{17,9},{25,17},{2,26},{10... | collective-permute-start | bytes 98312 | tf_op jit(solution)/shard_map/ppermute | solution.py:39
  72.2 4.8 %collective-permute-start.14 = (bf16[128,128]{1,0:T(8,128)(2,1)S(1)}, bf16[128,128]{1,0:T(8,128)(2,1)S(1)}, u32[]{:S(2)}, u32[]{:S(2)}) collective-permute-start(bf16[128,128]{1,0:T(8,128)(2,1)S(1)} %get-tuple-element.36), channel_id=1, source_target_pairs={{0,16},{8,24},{16,0},{24,8},{1,17},{9,25},{17,1},{25,9},{2,18},{10... | collective-permute-start | bytes 98312 | tf_op jit(solution)/shard_map/ppermute | solution.py:39
  72.2 5.7 %collective-permute-start.13 = (bf16[128,128]{1,0:T(8,128)(2,1)S(1)}, bf16[128,128]{1,0:T(8,128)(2,1)S(1)}, u32[]{:S(2)}, u32[]{:S(2)}) collective-permute-start(bf16[128,128]{1,0:T(8,128)(2,1)S(1)} %get-tuple-element.36), channel_id=1, source_target_pairs={{0,8},{8,16},{16,24},{24,0},{1,9},{9,17},{17,25},{25,1},{2,10},{10... | collective-permute-start | bytes 98312 | tf_op jit(solution)/shard_map/ppermute | solution.py:39
  77.9 55.1 %all-to-all-start.1 = ((bf16[4,256,1024]{2,1,0:T(8,128)(2,1)}), bf16[4,256,1024]{2,1,0:T(8,128)(2,1)}, u32[]{:S(2)}, u32[]{:S(2)}) async-start(bf16[4,256,1024]{2,1,0:T(8,128)(2,1)} %bitcast.79), calls=%async_computation.1 | async-start | bytes 4194304 | tf_op jit(solution)/shard_map/all_to_all | solution.py:546
  82.3 12.9 %collective-permute-start.12 = (bf16[128,2048]{1,0:T(8,128)(2,1)S(1)}, bf16[128,2048]{1,0:T(8,128)(2,1)S(1)}, u32[]{:S(2)}, u32[]{:S(2)}) collective-permute-start(bf16[128,2048]{1,0:T(8,128)(2,1)S(1)} %copy-done.20), channel_id=1, source_target_pairs={{0,6},{2,4},{4,2},{6,0},{1,7},{3,5},{5,3},{7,1},{8,14},{10,12},{12... | collective-permute-start | bytes 1572872 | tf_op jit(solution)/shard_map/ppermute | solution.py:60
  95.2 1.6 %copy-start.4 = (bf16[1024,1024]{1,0:T(8,128)(2,1)S(1)}, bf16[1024,1024]{1,0:T(8,128)(2,1)}, u32[]{:S(2)}) copy-start(bf16[1024,1024]{1,0:T(8,128)(2,1)} %x_ref.1) | copy-start | bytes 6291460
  98.0 17.2 %copy-start.11 = (bf16[128,2048]{1,0:T(8,128)(2,1)S(1)}, bf16[128,2048]{1,0:T(8,128)(2,1)}, u32[]{:S(2)}) copy-start(bf16[128,2048]{1,0:T(8,128)(2,1)} %copy-done.10) | copy-start | bytes 1572868
  98.1 17.2 %copy-start.14 = (bf16[128,2048]{1,0:T(8,128)(2,1)S(1)}, bf16[128,2048]{1,0:T(8,128)(2,1)}, u32[]{:S(2)}) copy-start(bf16[128,2048]{1,0:T(8,128)(2,1)} %copy-done.12) | copy-start | bytes 1572868
  98.1 3.7 %collective-permute-start.16 = (bf16[4,128,128]{2,1,0:T(8,128)(2,1)S(1)}, bf16[4,128,128]{2,1,0:T(8,128)(2,1)S(1)}, u32[]{:S(2)}, u32[]{:S(2)}) collective-permute-start(bf16[4,128,128]{2,1,0:T(8,128)(2,1)S(1)} %slice_bitcast_fusion.8), channel_id=1, source_target_pairs={{0,1},{1,0},{2,3},{3,2},{4,5},{5,4},{6,7},{7,6},{8,9},{9,8},{10,11... | collective-permute-start | bytes 393224 | tf_op jit(solution)/shard_map/ppermute | solution.py:60
  98.2 6.0 %collective-permute-start.21 = (bf16[4,128,128]{2,1,0:T(8,128)(2,1)S(1)}, bf16[4,128,128]{2,1,0:T(8,128)(2,1)S(1)}, u32[]{:S(2)}, u32[]{:S(2)}) collective-permute-start(bf16[4,128,128]{2,1,0:T(8,128)(2,1)S(1)} %get-tuple-element.63), channel_id=1, source_target_pairs={{0,4},{2,6},{4,0},{6,2},{1,5},{3,7},{5,1},{7,3},{8,12},{10,14},{12... | collective-permute-start | bytes 393224 | tf_op jit(solution)/shard_map/ppermute | solution.py:60
  99.7 6.3 %collective-permute-start.20 = (bf16[4,128,128]{2,1,0:T(8,128)(2,1)S(1)}, bf16[4,128,128]{2,1,0:T(8,128)(2,1)S(1)}, u32[]{:S(2)}, u32[]{:S(2)}) collective-permute-start(bf16[4,128,128]{2,1,0:T(8,128)(2,1)S(1)} %get-tuple-element.63), channel_id=1, source_target_pairs={{0,2},{2,0},{4,6},{6,4},{1,3},{3,1},{5,7},{7,5},{8,10},{10,8},{12,... | collective-permute-start | bytes 393224 | tf_op jit(solution)/shard_map/ppermute | solution.py:60
  100.2 8.8 %collective-permute-start.22 = (bf16[4,128,128]{2,1,0:T(8,128)(2,1)S(1)}, bf16[4,128,128]{2,1,0:T(8,128)(2,1)S(1)}, u32[]{:S(2)}, u32[]{:S(2)}) collective-permute-start(bf16[4,128,128]{2,1,0:T(8,128)(2,1)S(1)} %get-tuple-element.63), channel_id=1, source_target_pairs={{0,6},{2,4},{4,2},{6,0},{1,7},{3,5},{5,3},{7,1},{8,14},{10,12},{12... | collective-permute-start | bytes 393224 | tf_op jit(solution)/shard_map/ppermute | solution.py:60
  101.8 9.9 %collective-permute-start.19 = (bf16[4,128,128]{2,1,0:T(8,128)(2,1)S(1)}, bf16[4,128,128]{2,1,0:T(8,128)(2,1)S(1)}, u32[]{:S(2)}, u32[]{:S(2)}) collective-permute-start(bf16[4,128,128]{2,1,0:T(8,128)(2,1)S(1)} %fusion.3), channel_id=1, source_target_pairs={{0,6},{2,4},{4,2},{6,0},{1,7},{3,5},{5,3},{7,1},{8,14},{10,12},{12... | collective-permute-start | bytes 393224 | tf_op jit(solution)/shard_map/ppermute | solution.py:60
  103.2 10.1 %collective-permute-start.18 = (bf16[4,128,128]{2,1,0:T(8,128)(2,1)S(1)}, bf16[4,128,128]{2,1,0:T(8,128)(2,1)S(1)}, u32[]{:S(2)}, u32[]{:S(2)}) collective-permute-start(bf16[4,128,128]{2,1,0:T(8,128)(2,1)S(1)} %fusion.3), channel_id=1, source_target_pairs={{0,4},{2,6},{4,0},{6,2},{1,5},{3,7},{5,1},{7,3},{8,12},{10,14},{12... | collective-permute-start | bytes 393224 | tf_op jit(solution)/shard_map/ppermute | solution.py:60
  104.2 9.6 %collective-permute-start.17 = (bf16[4,128,128]{2,1,0:T(8,128)(2,1)S(1)}, bf16[4,128,128]{2,1,0:T(8,128)(2,1)S(1)}, u32[]{:S(2)}, u32[]{:S(2)}) collective-permute-start(bf16[4,128,128]{2,1,0:T(8,128)(2,1)S(1)} %fusion.3), channel_id=1, source_target_pairs={{0,2},{2,0},{4,6},{6,4},{1,3},{3,1},{5,7},{7,5},{8,10},{10,8},{12,... | collective-permute-start | bytes 393224 | tf_op jit(solution)/shard_map/ppermute | solution.py:60
  109.0 15.6 %copy-start.7 = (bf16[4,4,128,128]{3,2,1,0:T(8,128)(2,1)}, bf16[4,4,128,128]{3,2,1,0:T(8,128)(2,1)S(1)}, u32[]{:S(2)}) copy-start(bf16[4,4,128,128]{3,2,1,0:T(8,128)(2,1)S(1)} %pad_maximum_fusion.rest_0_) | copy-start | bytes 1572868
  109.0 15.5 %collective-permute-start.23 = (bf16[4,4,128,128]{3,2,1,0:T(8,128)(2,1)S(1)}, bf16[4,4,128,128]{3,2,1,0:T(8,128)(2,1)S(1)}, u32[]{:S(2)}, u32[]{:S(2)}) collective-permute-start(bf16[4,4,128,128]{3,2,1,0:T(8,128)(2,1)S(1)} %pad_maximum_fusion.rest_0_), channel_id=1, source_target_pairs={{0,1},{1,0},{2,3},{3,2},{4,5},{5,4},{6,7},{7,6},{8,9},{9,8},{10,11... | collective-permute-start | bytes 1572872 | tf_op jit(solution)/shard_map/ppermute | solution.py:60
  113.8 8.3 %copy-start.9 = (f32[128,2048]{1,0:T(8,128)S(1)}, f32[128,2048]{1,0:T(8,128)}, u32[]{:S(2)}) copy-start(f32[128,2048]{1,0:T(8,128)} %get-tuple-element.52.rest_0_) | copy-start | bytes 3145732
  113.8 8.3 %copy-start.17 = (bf16[64,2048]{1,0:T(8,128)(2,1)S(1)}, bf16[64,2048]{1,0:T(8,128)(2,1)}, u32[]{:S(2)}) copy-start(bf16[64,2048]{1,0:T(8,128)(2,1)} %copy-done.16) | copy-start | bytes 786436
  113.8 1.4 %collective-permute-start.24 = (bf16[4,128,128]{2,1,0:T(8,128)(2,1)S(1)}, bf16[4,128,128]{2,1,0:T(8,128)(2,1)S(1)}, u32[]{:S(2)}, u32[]{:S(2)}) collective-permute-start(bf16[4,128,128]{2,1,0:T(8,128)(2,1)S(1)} %add_convert_fusion.low_ref.rest_0_), channel_id=1, source_target_pairs={{0,1},{1,0},{2,3},{3,2},{4,5},{5,4},{6,7},{7,6},{8,9},{9,8},{10,11... | collective-permute-start | bytes 393224 | tf_op jit(solution)/shard_map/ppermute | solution.py:60
  115.3 9.3 %copy-start.6 = (f32[1024,1024]{1,0:T(8,128)S(1)}, f32[1024,1024]{1,0:T(8,128)}, u32[]{:S(2)}) copy-start(f32[1024,1024]{1,0:T(8,128)} %copy-done.5) | copy-start | bytes 12582916
  117.5 20.7 %collective-permute-start.27 = (bf16[8,16,256]{2,1,0:T(8,128)(2,1)S(1)}, bf16[8,16,256]{2,1,0:T(8,128)(2,1)S(1)}, u32[]{:S(2)}, u32[]{:S(2)}) collective-permute-start(bf16[8,16,256]{2,1,0:T(8,128)(2,1)S(1)} %get-tuple-element.58), channel_id=1, source_target_pairs={{0,24},{8,0},{16,8},{24,16},{1,25},{9,1},{17,9},{25,17},{2,26},{10... | collective-permute-start | bytes 196616 | tf_op jit(solution)/shard_map/ppermute | solution.py:39
  121.0 17.2 %collective-permute-start.26 = (bf16[8,16,256]{2,1,0:T(8,128)(2,1)S(1)}, bf16[8,16,256]{2,1,0:T(8,128)(2,1)S(1)}, u32[]{:S(2)}, u32[]{:S(2)}) collective-permute-start(bf16[8,16,256]{2,1,0:T(8,128)(2,1)S(1)} %get-tuple-element.59), channel_id=1, source_target_pairs={{0,16},{8,24},{16,0},{24,8},{1,17},{9,25},{17,1},{25,9},{2,18},{10... | collective-permute-start | bytes 196616 | tf_op jit(solution)/shard_map/ppermute | solution.py:39
  121.0 17.2 %collective-permute-start.25 = (bf16[8,16,256]{2,1,0:T(8,128)(2,1)S(1)}, bf16[8,16,256]{2,1,0:T(8,128)(2,1)S(1)}, u32[]{:S(2)}, u32[]{:S(2)}) collective-permute-start(bf16[8,16,256]{2,1,0:T(8,128)(2,1)S(1)} %get-tuple-element.60), channel_id=1, source_target_pairs={{0,8},{8,16},{16,24},{24,0},{1,9},{9,17},{17,25},{25,1},{2,10},{10... | collective-permute-start | bytes 196616 | tf_op jit(solution)/shard_map/ppermute | solution.py:39
  127.9 0.8 copy-start.15
  128.7 9.5 %copy-start.19 = (s32[60]{0:T(128)S(1)}, s32[60]{0:T(128)}, u32[]{:S(2)}) copy-start(s32[60]{0:T(128)} %copy-done.18) | copy-start | bytes 724

commit v20 on v19

--- a/solution.py
+++ b/solution.py
@@ -60,14 +60,16 @@
     return lax.ppermute(piece, axis, [(i, partner(i, k, count)) for i in range(count)])
 
 
-def gather_chips(piece):
+def gather_chips(piece, behind):
     count = lax.axis_size("pipe")
-    if count != 4 or piece.shape[0] % 32:
-        return [swap(piece, "pipe", k) for k in range(1, count)]
-    first, second = swap(piece, "pipe", 1), swap(piece, "pipe", 2)
-    half = piece.shape[0] // 2
-    third = [swap(second[:half], "pipe", 1), swap(first[half:], "pipe", 2)]
-    return [first, second, jnp.concatenate(third)]
+    in_halves = count == 4 and piece.shape[0] % 32 == 0
+    came = [swap(piece, "pipe", k) for k in range(1, 3 if in_halves else count)]
+    came, one, two = lax.optimization_barrier((came, behind, behind))
+    if in_halves:
+        half = piece.shape[0] // 2
+        third = [swap(came[1][:half], "pipe", 1), swap(came[0][half:], "pipe", 2)]
+        came = came + [jnp.concatenate(third)]
+    return came, one, two
 
 
 def up_rides(adapter_up):
@@ -509,9 +511,10 @@
         up = lax.all_to_all(pick_up(at, slot_of, adapter_up, data_count), "dp", 0, 0, tiled=True)
         up = up.reshape(ADAPTER_RANK, WIDTH)
 
-    cot_chips = [cotangent] + gather_chips(cotangent)
-
-    base_tokens, a_send = lax.optimization_barrier((tokens, a_send))
+    behind, a_send = lax.optimization_barrier((tokens, a_send))
+    cot_chips, base_tokens, x_tokens = gather_chips(cotangent, behind)
+    cot_chips = [cotangent] + cot_chips
+
     tokens_by_group = base_tokens.reshape(pipe_count, tensor_count, rows, feature_count)
     parts = 2 if pipe_count % 2 == 0 else 1
     chips = pipe_count // parts
@@ -535,7 +538,7 @@
     ]
     input_base = cotangent_product(at, cot_pieces, key_value_weight)
 
-    x_send = base_tokens.T.reshape(data_count, down_rows, tok_dev)
+    x_send = x_tokens.T.reshape(data_count, down_rows, tok_dev)
 
     a_recv, x_send, input_base, base_chip_came[:2] = lax.optimization_barrier(
         (a_recv, x_send, input_base, base_chip_came[:2])

time: 140 us -> 140 us (level)
  no operation moved by 1% of the time
where the time goes in v20:
time: 140 us; the launch traced here: 139 us
  waiting for transfers between devices  43 us (31%)
  starting transfers between devices  37.5 us (27%)
  Pallas kernels  36.1 us (26%)
  local copies, waits for them, and re-layouts  19.4 us (14%)
  other arithmetic  2.29 us (2%)
    ppermute x22, waiting for transfers between devices, swap(): lax.ppermute(piece, axis, [(i, partner(i, k, count)) for i in range(count)])  34.3 us
    ppermute x22, starting transfers between devices, swap(): lax.ppermute(piece, axis, [(i, partner(i, k, count)) for i in range(count)])  17.3 us
    unnamed x47, local copies, waits for them, and re-layouts  13.7 us
    ppermute x6, starting transfers between devices, shift(): lax.ppermute(piece, axis, [(i, (i + k) % count) for i in range(count)])  9.27 us
    pallas_call x1, Pallas kernels, cotangent_product(): call(kernel, 'cotangent_product', grid=(depth // tile,), in_specs=[SMEM,...  7.96 us
    pallas_call x2, Pallas kernels, base_product(): call(kernel, 'base_product', grid_spec=pltpu.PrefetchScalarGridSpec(num_s...  7.73 us
    all_to_all x1, starting transfers between devices, body(): a_recv = lax.all_to_all(a_send, 'dp', 0, 0, tiled=True)  6.46 us
    pallas_call x1, Pallas kernels, grad_down(): call(kernel, 'grad_down', VMEM_MOST, in_specs=[SMEM, HBM] + [VMEM] * tens...  5.15 us
  transfers between devices with their start and end apart: 30, of which 15 were waited for; matrix products, arithmetic and copies ran while one was open for 6% of the time, Pallas kernels for 22%

profile of v20, /device:TPU:0, one launch (start us, length us, event | category | flops | bytes accessed | tf_op | source)
XLA Modules:
  0.0 139.3 jit_solution(2325784633540029515)
XLA Ops:
  0.6 4.2 %pick_rows.1 = bf16[4,2304,128]{2,1,0:T(8,128)(2,1)} custom-call(s32[32]{0:T(128)} %tenant_ref.1, s32[24]{0:T(128)} %slot_ref.1, bf16[24,256,128]{2,1,0:T(8,128)(2,1)} %down_ref.1, bf16[24,16,2048]{2,1,0:T(8,128)(2,1)} %up_ref.1), custom_call_target="tpu_custom_call" | custom-call | flops 1024 | bytes 1024 | tf_op jit(solution)/shard_map/pick_rows/pallas_call | solution.py:116
  4.9 6.5 %all-to-all-start = ((bf16[4,2304,128]{2,1,0:T(8,128)(2,1)}), bf16[4,2304,128]{2,1,0:T(8,128)(2,1)S(1)}, u32[]{:S(2)}, u32[]{:S(2)}) async-start(bf16[4,2304,128]{2,1,0:T(8,128)(2,1)} %pick_rows.1), calls=%async_computation | async-start | bytes 4718592 | tf_op jit(solution)/shard_map/all_to_all | solution.py:508
  11.3 1.5 %collective-permute-start.1 = (bf16[128,2048]{1,0:T(8,128)(2,1)S(1)}, bf16[128,2048]{1,0:T(8,128)(2,1)S(1)}, u32[]{:S(2)}, u32[]{:S(2)}) collective-permute-start(bf16[128,2048]{1,0:T(8,128)(2,1)S(1)} %copy-done.8), channel_id=1, source_target_pairs={{0,4},{2,6},{4,0},{6,2},{1,5},{3,7},{5,1},{7,3},{8,12},{10,14},{12... | collective-permute-start | bytes 1572872 | tf_op jit(solution)/shard_map/ppermute | solution.py:60
  12.8 1.5 %collective-permute-start = (bf16[128,2048]{1,0:T(8,128)(2,1)S(1)}, bf16[128,2048]{1,0:T(8,128)(2,1)}, u32[]{:S(2)}, u32[]{:S(2)}) collective-permute-start(bf16[128,2048]{1,0:T(8,128)(2,1)S(1)} %copy-done.8), channel_id=1, source_target_pairs={{0,2},{2,0},{4,6},{6,4},{1,3},{3,1},{5,7},{7,5},{8,10},{10,8},{12,... | collective-permute-start | bytes 1572872 | tf_op jit(solution)/shard_map/ppermute | solution.py:60
  14.3 0.1 concatenate.6.at_ref
  14.4 10.3 %collective-permute-done.1.rest_2_.rest_4_ = bf16[128,2048]{1,0:T(8,128)(2,1)S(1)} collective-permute-done((bf16[128,2048]{1,0:T(8,128)(2,1)S(1)}, bf16[128,2048]{1,0:T(8,128)(2,1)S(1)}, u32[]{:S(2)}, u32[]{:S(2)}) %collective-permute-start.1) | collective-permute-done | bytes 524320 | tf_op jit(solution)/shard_map/ppermute | solution.py:60
  24.7 1.3 collective-permute-done.rest_1_.rest_3_
  26.0 2.2 %copy-done = bf16[1024,2048]{1,0:T(8,128)(2,1)S(1)} copy-done((bf16[1024,2048]{1,0:T(8,128)(2,1)S(1)}, bf16[1024,2048]{1,0:T(8,128)(2,1)}, u32[]{:S(2)}) %copy-start) | copy-done | bytes 4194328
  28.2 1.6 %copy-done.2 = bf16[1024,1024]{1,0:T(8,128)(2,1)S(1)} copy-done((bf16[1024,1024]{1,0:T(8,128)(2,1)S(1)}, bf16[1024,1024]{1,0:T(8,128)(2,1)}, u32[]{:S(2)}) %copy-start.2) | copy-done | bytes 2097176
  29.8 3.9 %base_product.3 = (bf16[1,2,128,2048]{3,2,1,0:T(8,128)(2,1)S(1)}, bf16[1,2,128,2048]{3,2,1,0:T(8,128)(2,1)S(1)}) custom-call(s32[60]{0:T(128)S(1)} %concatenate.6.at_ref, bf16[4,2,128,1024]{3,2,1,0:T(8,128)(2,1)S(1)} %bitcast.74, bf16[1024,2048]{1,0:T(8,128)(2,1)S(1)} %copy-done), custom_call_target="tpu_custom_call" | custom-call | flops 1024 | bytes 1024 | tf_op jit(solution)/shard_map/base_product/pallas_call | solution.py:154
  33.8 0.5 collective-permute-start.8
  34.3 1.6 %collective-permute-start.2 = (bf16[64,2048]{1,0:T(8,128)(2,1)S(1)}, bf16[64,2048]{1,0:T(8,128)(2,1)S(1)}, u32[]{:S(2)}, u32[]{:S(2)}) collective-permute-start(bf16[64,2048]{1,0:T(8,128)(2,1)S(1)} %slice.48), channel_id=1, source_target_pairs={{0,2},{2,0},{4,6},{6,4},{1,3},{3,1},{5,7},{7,5},{8,10},{10,8},{12,... | collective-permute-start | bytes 786440 | tf_op jit(solution)/shard_map/ppermute | solution.py:60
  35.8 1.0 slice.49
  36.8 0.6 collective-permute-start.3
  37.4 3.8 %base_product.2 = bf16[1,4,128,2048]{3,2,1,0:T(8,128)(2,1)S(1)} custom-call(s32[60]{0:T(128)S(1)} %concatenate.6.at_ref, bf16[4,2,128,1024]{3,2,1,0:T(8,128)(2,1)S(1)} %bitcast.75, bf16[1024,2048]{1,0:T(8,128)(2,1)S(1)} %copy-done), custom_call_target="tpu_custom_call" | custom-call | flops 1024 | bytes 1024 | tf_op jit(solution)/shard_map/base_product/pallas_call | solution.py:154
  41.2 1.4 %collective-permute-done.2 = bf16[64,2048]{1,0:T(8,128)(2,1)S(1)} collective-permute-done((bf16[64,2048]{1,0:T(8,128)(2,1)S(1)}, bf16[64,2048]{1,0:T(8,128)(2,1)S(1)}, u32[]{:S(2)}, u32[]{:S(2)}) %collective-permute-start.2) | collective-permute-done | bytes 262176 | tf_op jit(solution)/shard_map/ppermute | solution.py:60
  42.6 0.7 constant_dynamic-update-slice_fusion.1
  43.4 1.5 %collective-permute-done.3 = bf16[64,2048]{1,0:T(8,128)(2,1)S(1)} collective-permute-done((bf16[64,2048]{1,0:T(8,128)(2,1)S(1)}, bf16[64,2048]{1,0:T(8,128)(2,1)S(1)}, u32[]{:S(2)}, u32[]{:S(2)}) %collective-permute-start.3) | collective-permute-done | bytes 262176 | tf_op jit(solution)/shard_map/ppermute | solution.py:60
  44.9 0.7 constant_dynamic-update-slice_fusion.rest_3_.rest_5_
  45.6 0.5 collective-permute-start.7
  46.1 2.1 %convert_add_fusion = (f32[128,2048]{1,0:T(8,128)}, bf16[128,2048]{1,0:T(8,128)(2,1)}, bf16[128,2048]{1,0:T(8,128)(2,1)}, bf16[128,2048]{1,0:T(8,128)(2,1)}) fusion(bf16[2,128,2048]{2,1,0:T(8,128)(2,1)S(1)} %collective-permute-done.8, bf16[1,4,128,2048]{3,2,1,0:T(8,128)(2,1)S(1)} %base_product.2, bf16[2,128,2048]{2,1,0:T(8,128)(2,1)S(1)} %collective-permute-done.10), kind=kLoop, calls=%fused_computation | loop fusion | flops 3932160 | bytes 6815744 | tf_op jit(solution)/shard_map/add | solution.py:527
  48.2 0.5 collective-permute-start.9
  48.7 0.8 copy-done.12
  49.5 0.5 collective-permute-start.11
  50.0 3.9 %copy.11 = bf16[1024,1024]{1,0:T(8,128)(2,1)} copy(bf16[1024,1024]{0,1:T(8,128)(2,1)} %bitcast.73) | data formatting | bytes 4194304 | tf_op jit(solution)/shard_map/transpose | solution.py:541
  54.0 2.2 %copy-done.1 = bf16[1024,2048]{1,0:T(8,128)(2,1)S(1)} copy-done((bf16[1024,2048]{1,0:T(8,128)(2,1)S(1)}, bf16[1024,2048]{1,0:T(8,128)(2,1)}, u32[]{:S(2)}) %copy-start.1) | copy-done | bytes 4194328
  56.2 1.0 copy-done.13
  57.2 8.0 %cotangent_product.1.base_ref = f32[1024,1024]{1,0:T(8,128)S(1)} custom-call(s32[60]{0:T(128)S(1)} %concatenate.6.at_ref, bf16[1024,2048]{1,0:T(8,128)(2,1)S(1)} %copy-done.1, bf16[128,2048]{1,0:T(8,128)(2,1)S(1)} %copy-done.8, bf16[128,2048]{1,0:T(8,128)(2,1)} %collective-permute-done.rest_1_.rest_3_, ...), custom_call_target="tpu_custom_call" | custom-call | flops 1024 | bytes 1024 | tf_op jit(solution)/shard_map/cotangent_product/pallas_call | solution.py:228
  65.2 2.0 %copy-done.5 = f32[1024,1024]{1,0:T(8,128)} copy-done((f32[1024,1024]{1,0:T(8,128)}, f32[1024,1024]{1,0:T(8,128)S(1)}, u32[]{:S(2)}) %copy-start.5) | copy-done | bytes 4194328
  67.2 0.4 own_rows.1
  67.6 0.7 copy-done.16
  68.3 3.6 %collective-permute-start.15 = (bf16[128,128]{1,0:T(8,128)(2,1)S(1)}, bf16[128,128]{1,0:T(8,128)(2,1)S(1)}, u32[]{:S(2)}, u32[]{:S(2)}) collective-permute-start(bf16[128,128]{1,0:T(8,128)(2,1)S(1)} %get-tuple-element.44), channel_id=1, source_target_pairs={{0,24},{8,0},{16,8},{24,16},{1,25},{9,1},{17,9},{25,17},{2,26},{10... | collective-permute-start | bytes 98312 | tf_op jit(solution)/shard_map/ppermute | solution.py:39
  71.9 1.1 collective-permute-start.13
  73.0 0.5 collective-permute-done.15
  73.5 3.2 %collective-permute-done.14 = bf16[128,128]{1,0:T(8,128)(2,1)S(1)} collective-permute-done((bf16[128,128]{1,0:T(8,128)(2,1)S(1)}, bf16[128,128]{1,0:T(8,128)(2,1)S(1)}, u32[]{:S(2)}, u32[]{:S(2)}) %collective-permute-start.14) | collective-permute-done | bytes 32800 | tf_op jit(solution)/shard_map/ppermute | solution.py:39
  76.7 0.9 collective-permute-done.13
  77.6 4.4 %all-to-all-start.1 = ((bf16[4,256,1024]{2,1,0:T(8,128)(2,1)}), bf16[4,256,1024]{2,1,0:T(8,128)(2,1)}, u32[]{:S(2)}, u32[]{:S(2)}) async-start(bf16[4,256,1024]{2,1,0:T(8,128)(2,1)} %bitcast.79), calls=%async_computation.1 | async-start | bytes 4194304 | tf_op jit(solution)/shard_map/all_to_all | solution.py:549
  82.1 2.5 %collective-permute-start.12 = (bf16[128,2048]{1,0:T(8,128)(2,1)S(1)}, bf16[128,2048]{1,0:T(8,128)(2,1)S(1)}, u32[]{:S(2)}, u32[]{:S(2)}) collective-permute-start(bf16[128,2048]{1,0:T(8,128)(2,1)S(1)} %copy-done.20), channel_id=1, source_target_pairs={{0,6},{2,4},{4,2},{6,0},{1,7},{3,5},{5,3},{7,1},{8,14},{10,12},{12... | collective-permute-start | bytes 1572872 | tf_op jit(solution)/shard_map/ppermute | solution.py:60
  84.6 10.3 %collective-permute-done.12.rest_3_ = bf16[128,2048]{1,0:T(8,128)(2,1)S(1)} collective-permute-done((bf16[128,2048]{1,0:T(8,128)(2,1)S(1)}, bf16[128,2048]{1,0:T(8,128)(2,1)S(1)}, u32[]{:S(2)}, u32[]{:S(2)}) %collective-permute-start.12) | collective-permute-done | bytes 524320 | tf_op jit(solution)/shard_map/ppermute | solution.py:60
  94.9 1.6 %copy-done.4 = bf16[1024,1024]{1,0:T(8,128)(2,1)S(1)} copy-done((bf16[1024,1024]{1,0:T(8,128)(2,1)S(1)}, bf16[1024,1024]{1,0:T(8,128)(2,1)}, u32[]{:S(2)}) %copy-start.4) | copy-done | bytes 2097176
  96.4 1.3 low_product.1
  97.8 0.1 collective-permute-start.16
  97.9 1.6 %collective-permute-start.21 = (bf16[4,128,128]{2,1,0:T(8,128)(2,1)S(1)}, bf16[4,128,128]{2,1,0:T(8,128)(2,1)S(1)}, u32[]{:S(2)}, u32[]{:S(2)}) collective-permute-start(bf16[4,128,128]{2,1,0:T(8,128)(2,1)S(1)} %get-tuple-element.71), channel_id=1, source_target_pairs={{0,4},{2,6},{4,0},{6,2},{1,5},{3,7},{5,1},{7,3},{8,12},{10,14},{12... | collective-permute-start | bytes 393224 | tf_op jit(solution)/shard_map/ppermute | solution.py:60
  99.5 1.5 %collective-permute-start.20 = (bf16[4,128,128]{2,1,0:T(8,128)(2,1)S(1)}, bf16[4,128,128]{2,1,0:T(8,128)(2,1)S(1)}, u32[]{:S(2)}, u32[]{:S(2)}) collective-permute-start(bf16[4,128,128]{2,1,0:T(8,128)(2,1)S(1)} %get-tuple-element.71), channel_id=1, source_target_pairs={{0,2},{2,0},{4,6},{6,4},{1,3},{3,1},{5,7},{7,5},{8,10},{10,8},{12,... | collective-permute-start | bytes 393224 | tf_op jit(solution)/shard_map/ppermute | solution.py:60
  100.9 0.5 collective-permute-start.22
  101.5 2.5 %collective-permute-start.19 = (bf16[4,128,128]{2,1,0:T(8,128)(2,1)S(1)}, bf16[4,128,128]{2,1,0:T(8,128)(2,1)S(1)}, u32[]{:S(2)}, u32[]{:S(2)}) collective-permute-start(bf16[4,128,128]{2,1,0:T(8,128)(2,1)S(1)} %fusion.3), channel_id=1, source_target_pairs={{0,6},{2,4},{4,2},{6,0},{1,7},{3,5},{5,3},{7,1},{8,14},{10,12},{12... | collective-permute-start | bytes 393224 | tf_op jit(solution)/shard_map/ppermute | solution.py:60
  104.0 0.5 collective-permute-start.18
  104.5 0.8 collective-permute-start.17
  105.3 0.5 collective-permute-done.20
  105.8 2.8 %collective-permute-done.22 = bf16[4,128,128]{2,1,0:T(8,128)(2,1)S(1)} collective-permute-done((bf16[4,128,128]{2,1,0:T(8,128)(2,1)S(1)}, bf16[4,128,128]{2,1,0:T(8,128)(2,1)S(1)}, u32[]{:S(2)}, u32[]{:S(2)}) %collective-permute-start.22) | collective-permute-done | bytes 131104 | tf_op jit(solution)/shard_map/ppermute | solution.py:60
  108.7 2.6 %collective-permute-done.19 = bf16[4,128,128]{2,1,0:T(8,128)(2,1)S(1)} collective-permute-done((bf16[4,128,128]{2,1,0:T(8,128)(2,1)S(1)}, bf16[4,128,128]{2,1,0:T(8,128)(2,1)S(1)}, u32[]{:S(2)}, u32[]{:S(2)}) %collective-permute-start.19) | collective-permute-done | bytes 131104 | tf_op jit(solution)/shard_map/ppermute | solution.py:60
  111.3 2.1 %collective-permute-done.18 = bf16[4,128,128]{2,1,0:T(8,128)(2,1)S(1)} collective-permute-done((bf16[4,128,128]{2,1,0:T(8,128)(2,1)S(1)}, bf16[4,128,128]{2,1,0:T(8,128)(2,1)S(1)}, u32[]{:S(2)}, u32[]{:S(2)}) %collective-permute-start.18) | collective-permute-done | bytes 131104 | tf_op jit(solution)/shard_map/ppermute | solution.py:60
  113.4 0.1 collective-permute-done.17
  113.5 0.1 add_convert_fusion.low_ref.rest_0_
  113.7 1.3 collective-permute-done.24.rest_1_
  115.1 2.2 %grad_up_pieces.1 = bf16[4,8,16,256]{3,2,1,0:T(8,128)(2,1)S(1)} custom-call(s32[60]{0:T(128)S(1)} %concatenate.6.at_ref, bf16[4,128,128]{2,1,0:T(8,128)(2,1)S(1)} %add_convert_fusion.low_ref.rest_0_, bf16[4,128,128]{2,1,0:T(8,128)(2,1)S(1)} %collective-permute-done.24.rest_1_, bf16[128,2048]{1,0:T(8,128)(2,1)S(1)} %copy-done.8, ...), custom_call_target="tpu_custom_call" | custom-call | flops 1024 | bytes 1024 | tf_op jit(solution)/shard_map/grad_up_pieces/pallas_call | solution.py:379
  117.3 3.5 %collective-permute-start.27 = (bf16[8,16,256]{2,1,0:T(8,128)(2,1)S(1)}, bf16[8,16,256]{2,1,0:T(8,128)(2,1)S(1)}, u32[]{:S(2)}, u32[]{:S(2)}) collective-permute-start(bf16[8,16,256]{2,1,0:T(8,128)(2,1)S(1)} %get-tuple-element.66), channel_id=1, source_target_pairs={{0,24},{8,0},{16,8},{24,16},{1,25},{9,1},{17,9},{25,17},{2,26},{10... | collective-permute-start | bytes 196616 | tf_op jit(solution)/shard_map/ppermute | solution.py:39
  120.8 1.1 collective-permute-start.25
  121.9 2.5 %keys_and_values.1 = bf16[128,2048]{1,0:T(8,128)(2,1)} custom-call(s32[60]{0:T(128)S(1)} %concatenate.6.at_ref, bf16[4,128,128]{2,1,0:T(8,128)(2,1)S(1)} %add_convert_fusion.low_ref.rest_0_, bf16[64,2048]{1,0:T(8,128)(2,1)S(1)} %copy-done.17, f32[128,2048]{1,0:T(8,128)S(1)} %copy-done.9, bf16[128,2048]{1,0:T(8,128)(2,1)} %collective-permute-done.9.rest_1_, ...), custom_call_target="tpu_custom_call" | custom-call | flops 1024 | bytes 1024 | tf_op jit(solution)/shard_map/keys_and_values/pallas_call | solution.py:472
  124.4 3.3 %input_gradient.1 = bf16[1024,1024]{1,0:T(8,128)(2,1)} custom-call(s32[60]{0:T(128)S(1)} %concatenate.6.at_ref, f32[1024,1024]{1,0:T(8,128)S(1)} %copy-done.6, bf16[4,2304,128]{2,1,0:T(8,128)(2,1)S(1)} %all-to-all-done.came_ref.a_ref, bf16[4,4,128,128]{3,2,1,0:T(8,128)(2,1)S(1)} %pad_maximum_fusion.rest_0_, ...), custom_call_target="tpu_custom_call" | custom-call | flops 1024 | bytes 1024 | tf_op jit(solution)/shard_map/input_gradient/pallas_call | solution.py:270
  127.7 0.8 copy-done.15
  128.5 4.2 %all-to-all-done.1.x_ref = bf16[4,256,1024]{2,1,0:T(8,128)(2,1)} async-done(((bf16[4,256,1024]{2,1,0:T(8,128)(2,1)}), bf16[4,256,1024]{2,1,0:T(8,128)(2,1)}, u32[]{:S(2)}, u32[]{:S(2)}) %all-to-all-start.1) | async-done | bytes 2097184 | tf_op jit(solution)/shard_map/all_to_all | solution.py:549
  132.7 5.1 %grad_down.1 = f32[24,256,128]{2,1,0:T(8,128)} custom-call(s32[60]{0:T(128)} %copy-done.18, bf16[4,256,1024]{2,1,0:T(8,128)(2,1)} %all-to-all-done.1.x_ref, bf16[4,4,128,128]{3,2,1,0:T(8,128)(2,1)} %copy-done.7, bf16[4,4,128,128]{3,2,1,0:T(8,128)(2,1)} %copy-done.15), custom_call_target="tpu_custom_call" | custom-call | flops 1024 | bytes 1024 | tf_op jit(solution)/shard_map/grad_down/pallas_call | solution.py:318
  137.9 1.5 %grad_up.1 = f32[24,16,256]{2,1,0:T(8,128)} custom-call(s32[60]{0:T(128)S(1)} %copy-done.19, bf16[8,16,256]{2,1,0:T(8,128)(2,1)S(1)} %get-tuple-element.56.rest_0_, bf16[8,16,256]{2,1,0:T(8,128)(2,1)S(1)} %collective-permute-done.25.rest_1_, bf16[8,16,256]{2,1,0:T(8,128)(2,1)S(1)} %collective-permute-done.26.rest_2_, ...), custom_call_target="tpu_custom_call" | custom-call | flops 1024 | bytes 1024 | tf_op jit(solution)/shard_map/grad_up/pallas_call | solution.py:406
  (66 shorter events, 0.5 us)
Async XLA Ops:
  4.8 6.5 %copy-start.8 = (bf16[128,2048]{1,0:T(8,128)(2,1)S(1)}, bf16[128,2048]{1,0:T(8,128)(2,1)}, u32[]{:S(2)}) copy-start(bf16[128,2048]{1,0:T(8,128)(2,1)} %rest_2_.1) | copy-start | bytes 1572868
  4.8 9.4 %copy-start.21 = (s32[32]{0:T(128)S(1)}, s32[32]{0:T(128)}, u32[]{:S(2)}) copy-start(s32[32]{0:T(128)} %tenant_ref.1) | copy-start | bytes 388
  4.8 9.4 %copy-start.22 = (s32[24]{0:T(128)S(1)}, s32[24]{0:T(128)}, u32[]{:S(2)}) copy-start(s32[24]{0:T(128)} %slot_ref.1) | copy-start | bytes 292
  4.9 62.3 %all-to-all-start = ((bf16[4,2304,128]{2,1,0:T(8,128)(2,1)}), bf16[4,2304,128]{2,1,0:T(8,128)(2,1)S(1)}, u32[]{:S(2)}, u32[]{:S(2)}) async-start(bf16[4,2304,128]{2,1,0:T(8,128)(2,1)} %pick_rows.1), calls=%async_computation | async-start | bytes 4718592 | tf_op jit(solution)/shard_map/all_to_all | solution.py:508
  11.3 13.3 %collective-permute-start.1 = (bf16[128,2048]{1,0:T(8,128)(2,1)S(1)}, bf16[128,2048]{1,0:T(8,128)(2,1)S(1)}, u32[]{:S(2)}, u32[]{:S(2)}) collective-permute-start(bf16[128,2048]{1,0:T(8,128)(2,1)S(1)} %copy-done.8), channel_id=1, source_target_pairs={{0,4},{2,6},{4,0},{6,2},{1,5},{3,7},{5,1},{7,3},{8,12},{10,14},{12... | collective-permute-start | bytes 1572872 | tf_op jit(solution)/shard_map/ppermute | solution.py:60
  12.8 13.2 %collective-permute-start = (bf16[128,2048]{1,0:T(8,128)(2,1)S(1)}, bf16[128,2048]{1,0:T(8,128)(2,1)}, u32[]{:S(2)}, u32[]{:S(2)}) collective-permute-start(bf16[128,2048]{1,0:T(8,128)(2,1)S(1)} %copy-done.8), channel_id=1, source_target_pairs={{0,2},{2,0},{4,6},{6,4},{1,3},{3,1},{5,7},{7,5},{8,10},{10,8},{12,... | collective-permute-start | bytes 1572872 | tf_op jit(solution)/shard_map/ppermute | solution.py:60
  14.4 110.0 %copy-start.18 = (s32[60]{0:T(128)}, s32[60]{0:T(128)S(1)}, u32[]{:S(2)}) copy-start(s32[60]{0:T(128)S(1)} %concatenate.6.at_ref) | copy-start | bytes 724
  24.7 29.3 %copy-start.10 = (bf16[128,2048]{1,0:T(8,128)(2,1)}, bf16[128,2048]{1,0:T(8,128)(2,1)S(1)}, u32[]{:S(2)}) copy-start(bf16[128,2048]{1,0:T(8,128)(2,1)S(1)} %collective-permute-done.1.rest_2_.rest_4_) | copy-start | bytes 1572868
  26.0 2.2 %copy-start = (bf16[1024,2048]{1,0:T(8,128)(2,1)S(1)}, bf16[1024,2048]{1,0:T(8,128)(2,1)}, u32[]{:S(2)}) copy-start(bf16[1024,2048]{1,0:T(8,128)(2,1)} %w_ref.5) | copy-start | bytes 12582916
  28.2 1.6 %copy-start.2 = (bf16[1024,1024]{1,0:T(8,128)(2,1)S(1)}, bf16[1024,1024]{1,0:T(8,128)(2,1)}, u32[]{:S(2)}) copy-start(bf16[1024,1024]{1,0:T(8,128)(2,1)} %x_ref.1) | copy-start | bytes 6291460
  29.8 7.6 %copy-start.3 = (bf16[1024,1024]{1,0:T(8,128)(2,1)S(1)}, bf16[1024,1024]{1,0:T(8,128)(2,1)}, u32[]{:S(2)}) copy-start(bf16[1024,1024]{1,0:T(8,128)(2,1)} %x_ref.1) | copy-start | bytes 6291460
  33.7 11.9 %collective-permute-start.10 = (bf16[2,128,2048]{2,1,0:T(8,128)(2,1)S(1)}, bf16[2,128,2048]{2,1,0:T(8,128)(2,1)S(1)}, u32[]{:S(2)}, u32[]{:S(2)}) collective-permute-start(bf16[2,128,2048]{2,1,0:T(8,128)(2,1)S(1)} %bitcast.78), channel_id=1, source_target_pairs={{0,1},{1,0},{2,3},{3,2},{4,5},{5,4},{6,7},{7,6},{8,9},{9,8},{10,11... | collective-permute-start | bytes 3145736 | tf_op jit(solution)/shard_map/ppermute | solution.py:60
  33.8 12.4 %collective-permute-start.8 = (bf16[2,128,2048]{2,1,0:T(8,128)(2,1)S(1)}, bf16[2,128,2048]{2,1,0:T(8,128)(2,1)S(1)}, u32[]{:S(2)}, u32[]{:S(2)}) collective-permute-start(bf16[2,128,2048]{2,1,0:T(8,128)(2,1)S(1)} %bitcast.77), channel_id=1, source_target_pairs={{0,1},{1,0},{2,3},{3,2},{4,5},{5,4},{6,7},{7,6},{8,9},{9,8},{10,11... | collective-permute-start | bytes 3145736 | tf_op jit(solution)/shard_map/ppermute | solution.py:60
  34.3 8.4 %collective-permute-start.2 = (bf16[64,2048]{1,0:T(8,128)(2,1)S(1)}, bf16[64,2048]{1,0:T(8,128)(2,1)S(1)}, u32[]{:S(2)}, u32[]{:S(2)}) collective-permute-start(bf16[64,2048]{1,0:T(8,128)(2,1)S(1)} %slice.48), channel_id=1, source_target_pairs={{0,2},{2,0},{4,6},{6,4},{1,3},{3,1},{5,7},{7,5},{8,10},{10,8},{12,... | collective-permute-start | bytes 786440 | tf_op jit(solution)/shard_map/ppermute | solution.py:60
  36.8 8.1 %collective-permute-start.3 = (bf16[64,2048]{1,0:T(8,128)(2,1)S(1)}, bf16[64,2048]{1,0:T(8,128)(2,1)S(1)}, u32[]{:S(2)}, u32[]{:S(2)}) collective-permute-start(bf16[64,2048]{1,0:T(8,128)(2,1)S(1)} %slice.49), channel_id=1, source_target_pairs={{0,4},{2,6},{4,0},{6,2},{1,5},{3,7},{5,1},{7,3},{8,12},{10,14},{12... | collective-permute-start | bytes 786440 | tf_op jit(solution)/shard_map/ppermute | solution.py:60
  37.4 11.4 %collective-permute-start.4 = (bf16[128,2048]{1,0:T(8,128)(2,1)S(1)}, bf16[128,2048]{1,0:T(8,128)(2,1)S(1)}, u32[]{:S(2)}, u32[]{:S(2)}) collective-permute-start(bf16[128,2048]{1,0:T(8,128)(2,1)S(1)} %copy-done.8), channel_id=1, source_target_pairs={{0,1},{1,0},{2,3},{3,2},{4,5},{5,4},{6,7},{7,6},{8,9},{9,8},{10,11... | collective-permute-start | bytes 1572872 | tf_op jit(solution)/shard_map/ppermute | solution.py:60
  42.6 11.4 %collective-permute-start.5 = (bf16[128,2048]{1,0:T(8,128)(2,1)}, bf16[128,2048]{1,0:T(8,128)(2,1)}, u32[]{:S(2)}, u32[]{:S(2)}) collective-permute-start(bf16[128,2048]{1,0:T(8,128)(2,1)} %collective-permute-done.rest_1_.rest_3_), channel_id=1, source_target_pairs={{0,1},{1,0},{2,3},{3,2},{4,5},{5,4},{6,7},{7,6},{8,9},{9,8},{10,11... | collective-permute-start | bytes 1572872 | tf_op jit(solution)/shard_map/ppermute | solution.py:60
  44.9 9.1 %collective-permute-start.6 = (bf16[128,2048]{1,0:T(8,128)(2,1)S(1)}, bf16[128,2048]{1,0:T(8,128)(2,1)}, u32[]{:S(2)}, u32[]{:S(2)}) collective-permute-start(bf16[128,2048]{1,0:T(8,128)(2,1)S(1)} %collective-permute-done.1.rest_2_.rest_4_), channel_id=1, source_target_pairs={{0,1},{1,0},{2,3},{3,2},{4,5},{5,4},{6,7},{7,6},{8,9},{9,8},{10,11... | collective-permute-start | bytes 1572872 | tf_op jit(solution)/shard_map/ppermute | solution.py:60
  45.6 8.4 %collective-permute-start.7 = (bf16[128,2048]{1,0:T(8,128)(2,1)}, bf16[128,2048]{1,0:T(8,128)(2,1)}, u32[]{:S(2)}, u32[]{:S(2)}) collective-permute-start(bf16[128,2048]{1,0:T(8,128)(2,1)} %constant_dynamic-update-slice_fusion.rest_3_.rest_5_), channel_id=1, source_target_pairs={{0,1},{1,0},{2,3},{3,2},{4,5},{5,4},{6,7},{7,6},{8,9},{9,8},{10,11... | collective-permute-start | bytes 1572872 | tf_op jit(solution)/shard_map/ppermute | solution.py:60
  48.2 19.0 %collective-permute-start.9 = (bf16[128,2048]{1,0:T(8,128)(2,1)}, bf16[128,2048]{1,0:T(8,128)(2,1)}, u32[]{:S(2)}, u32[]{:S(2)}) collective-permute-start(bf16[128,2048]{1,0:T(8,128)(2,1)} %get-tuple-element.61), channel_id=1, source_target_pairs={{0,2},{2,0},{4,6},{6,4},{1,3},{3,1},{5,7},{7,5},{8,10},{10,8},{12,... | collective-permute-start | bytes 1572872 | tf_op jit(solution)/shard_map/ppermute | solution.py:60
  48.7 0.8 copy-start.12
  49.5 17.7 %collective-permute-start.11 = (bf16[128,2048]{1,0:T(8,128)(2,1)}, bf16[128,2048]{1,0:T(8,128)(2,1)}, u32[]{:S(2)}, u32[]{:S(2)}) collective-permute-start(bf16[128,2048]{1,0:T(8,128)(2,1)} %get-tuple-element.64), channel_id=1, source_target_pairs={{0,4},{2,6},{4,0},{6,2},{1,5},{3,7},{5,1},{7,3},{8,12},{10,14},{12... | collective-permute-start | bytes 1572872 | tf_op jit(solution)/shard_map/ppermute | solution.py:60
  54.0 2.2 %copy-start.1 = (bf16[1024,2048]{1,0:T(8,128)(2,1)S(1)}, bf16[1024,2048]{1,0:T(8,128)(2,1)}, u32[]{:S(2)}) copy-start(bf16[1024,2048]{1,0:T(8,128)(2,1)} %w_ref.5) | copy-start | bytes 12582916
  56.2 1.0 copy-start.13
  65.2 2.0 %copy-start.5 = (f32[1024,1024]{1,0:T(8,128)}, f32[1024,1024]{1,0:T(8,128)S(1)}, u32[]{:S(2)}) copy-start(f32[1024,1024]{1,0:T(8,128)S(1)} %cotangent_product.1.base_ref) | copy-start | bytes 12582916
  67.6 0.7 copy-start.16
  68.3 13.7 %copy-start.20 = (bf16[128,2048]{1,0:T(8,128)(2,1)S(1)}, bf16[128,2048]{1,0:T(8,128)(2,1)}, u32[]{:S(2)}) copy-start(bf16[128,2048]{1,0:T(8,128)(2,1)} %get-tuple-element.65) | copy-start | bytes 1572868
  68.3 5.2 %collective-permute-start.15 = (bf16[128,128]{1,0:T(8,128)(2,1)S(1)}, bf16[128,128]{1,0:T(8,128)(2,1)S(1)}, u32[]{:S(2)}, u32[]{:S(2)}) collective-permute-start(bf16[128,128]{1,0:T(8,128)(2,1)S(1)} %get-tuple-element.44), channel_id=1, source_target_pairs={{0,24},{8,0},{16,8},{24,16},{1,25},{9,1},{17,9},{25,17},{2,26},{10... | collective-permute-start | bytes 98312 | tf_op jit(solution)/shard_map/ppermute | solution.py:39
  71.9 4.8 %collective-permute-start.14 = (bf16[128,128]{1,0:T(8,128)(2,1)S(1)}, bf16[128,128]{1,0:T(8,128)(2,1)S(1)}, u32[]{:S(2)}, u32[]{:S(2)}) collective-permute-start(bf16[128,128]{1,0:T(8,128)(2,1)S(1)} %get-tuple-element.44), channel_id=1, source_target_pairs={{0,16},{8,24},{16,0},{24,8},{1,17},{9,25},{17,1},{25,9},{2,18},{10... | collective-permute-start | bytes 98312 | tf_op jit(solution)/shard_map/ppermute | solution.py:39
  71.9 5.7 %collective-permute-start.13 = (bf16[128,128]{1,0:T(8,128)(2,1)S(1)}, bf16[128,128]{1,0:T(8,128)(2,1)S(1)}, u32[]{:S(2)}, u32[]{:S(2)}) collective-permute-start(bf16[128,128]{1,0:T(8,128)(2,1)S(1)} %get-tuple-element.44), channel_id=1, source_target_pairs={{0,8},{8,16},{16,24},{24,0},{1,9},{9,17},{17,25},{25,1},{2,10},{10... | collective-permute-start | bytes 98312 | tf_op jit(solution)/shard_map/ppermute | solution.py:39
  77.6 55.1 %all-to-all-start.1 = ((bf16[4,256,1024]{2,1,0:T(8,128)(2,1)}), bf16[4,256,1024]{2,1,0:T(8,128)(2,1)}, u32[]{:S(2)}, u32[]{:S(2)}) async-start(bf16[4,256,1024]{2,1,0:T(8,128)(2,1)} %bitcast.79), calls=%async_computation.1 | async-start | bytes 4194304 | tf_op jit(solution)/shard_map/all_to_all | solution.py:549
  82.1 12.8 %collective-permute-start.12 = (bf16[128,2048]{1,0:T(8,128)(2,1)S(1)}, bf16[128,2048]{1,0:T(8,128)(2,1)S(1)}, u32[]{:S(2)}, u32[]{:S(2)}) collective-permute-start(bf16[128,2048]{1,0:T(8,128)(2,1)S(1)} %copy-done.20), channel_id=1, source_target_pairs={{0,6},{2,4},{4,2},{6,0},{1,7},{3,5},{5,3},{7,1},{8,14},{10,12},{12... | collective-permute-start | bytes 1572872 | tf_op jit(solution)/shard_map/ppermute | solution.py:60
  94.9 1.6 %copy-start.4 = (bf16[1024,1024]{1,0:T(8,128)(2,1)S(1)}, bf16[1024,1024]{1,0:T(8,128)(2,1)}, u32[]{:S(2)}) copy-start(bf16[1024,1024]{1,0:T(8,128)(2,1)} %x_ref.1) | copy-start | bytes 6291460
  97.7 17.3 %copy-start.11 = (bf16[128,2048]{1,0:T(8,128)(2,1)S(1)}, bf16[128,2048]{1,0:T(8,128)(2,1)}, u32[]{:S(2)}) copy-start(bf16[128,2048]{1,0:T(8,128)(2,1)} %copy-done.10) | copy-start | bytes 1572868
  97.7 17.3 %copy-start.14 = (bf16[128,2048]{1,0:T(8,128)(2,1)S(1)}, bf16[128,2048]{1,0:T(8,128)(2,1)}, u32[]{:S(2)}) copy-start(bf16[128,2048]{1,0:T(8,128)(2,1)} %copy-done.12) | copy-start | bytes 1572868
  97.8 3.7 %collective-permute-start.16 = (bf16[4,128,128]{2,1,0:T(8,128)(2,1)S(1)}, bf16[4,128,128]{2,1,0:T(8,128)(2,1)S(1)}, u32[]{:S(2)}, u32[]{:S(2)}) collective-permute-start(bf16[4,128,128]{2,1,0:T(8,128)(2,1)S(1)} %slice_bitcast_fusion.8), channel_id=1, source_target_pairs={{0,1},{1,0},{2,3},{3,2},{4,5},{5,4},{6,7},{7,6},{8,9},{9,8},{10,11... | collective-permute-start | bytes 393224 | tf_op jit(solution)/shard_map/ppermute | solution.py:60
  97.9 6.6 %collective-permute-start.21 = (bf16[4,128,128]{2,1,0:T(8,128)(2,1)S(1)}, bf16[4,128,128]{2,1,0:T(8,128)(2,1)S(1)}, u32[]{:S(2)}, u32[]{:S(2)}) collective-permute-start(bf16[4,128,128]{2,1,0:T(8,128)(2,1)S(1)} %get-tuple-element.71), channel_id=1, source_target_pairs={{0,4},{2,6},{4,0},{6,2},{1,5},{3,7},{5,1},{7,3},{8,12},{10,14},{12... | collective-permute-start | bytes 393224 | tf_op jit(solution)/shard_map/ppermute | solution.py:60
  99.5 6.3 %collective-permute-start.20 = (bf16[4,128,128]{2,1,0:T(8,128)(2,1)S(1)}, bf16[4,128,128]{2,1,0:T(8,128)(2,1)S(1)}, u32[]{:S(2)}, u32[]{:S(2)}) collective-permute-start(bf16[4,128,128]{2,1,0:T(8,128)(2,1)S(1)} %get-tuple-element.71), channel_id=1, source_target_pairs={{0,2},{2,0},{4,6},{6,4},{1,3},{3,1},{5,7},{7,5},{8,10},{10,8},{12,... | collective-permute-start | bytes 393224 | tf_op jit(solution)/shard_map/ppermute | solution.py:60
  100.9 7.6 %collective-permute-start.22 = (bf16[4,128,128]{2,1,0:T(8,128)(2,1)S(1)}, bf16[4,128,128]{2,1,0:T(8,128)(2,1)S(1)}, u32[]{:S(2)}, u32[]{:S(2)}) collective-permute-start(bf16[4,128,128]{2,1,0:T(8,128)(2,1)S(1)} %get-tuple-element.71), channel_id=1, source_target_pairs={{0,6},{2,4},{4,2},{6,0},{1,7},{3,5},{5,3},{7,1},{8,14},{10,12},{12... | collective-permute-start | bytes 393224 | tf_op jit(solution)/shard_map/ppermute | solution.py:60
  101.5 9.8 %collective-permute-start.19 = (bf16[4,128,128]{2,1,0:T(8,128)(2,1)S(1)}, bf16[4,128,128]{2,1,0:T(8,128)(2,1)S(1)}, u32[]{:S(2)}, u32[]{:S(2)}) collective-permute-start(bf16[4,128,128]{2,1,0:T(8,128)(2,1)S(1)} %fusion.3), channel_id=1, source_target_pairs={{0,6},{2,4},{4,2},{6,0},{1,7},{3,5},{5,3},{7,1},{8,14},{10,12},{12... | collective-permute-start | bytes 393224 | tf_op jit(solution)/shard_map/ppermute | solution.py:60
  104.0 9.5 %collective-permute-start.18 = (bf16[4,128,128]{2,1,0:T(8,128)(2,1)S(1)}, bf16[4,128,128]{2,1,0:T(8,128)(2,1)S(1)}, u32[]{:S(2)}, u32[]{:S(2)}) collective-permute-start(bf16[4,128,128]{2,1,0:T(8,128)(2,1)S(1)} %fusion.3), channel_id=1, source_target_pairs={{0,4},{2,6},{4,0},{6,2},{1,5},{3,7},{5,1},{7,3},{8,12},{10,14},{12... | collective-permute-start | bytes 393224 | tf_op jit(solution)/shard_map/ppermute | solution.py:60
  104.5 9.1 %collective-permute-start.17 = (bf16[4,128,128]{2,1,0:T(8,128)(2,1)S(1)}, bf16[4,128,128]{2,1,0:T(8,128)(2,1)S(1)}, u32[]{:S(2)}, u32[]{:S(2)}) collective-permute-start(bf16[4,128,128]{2,1,0:T(8,128)(2,1)S(1)} %fusion.3), channel_id=1, source_target_pairs={{0,2},{2,0},{4,6},{6,4},{1,3},{3,1},{5,7},{7,5},{8,10},{10,8},{12,... | collective-permute-start | bytes 393224 | tf_op jit(solution)/shard_map/ppermute | solution.py:60
  108.6 15.8 %copy-start.7 = (bf16[4,4,128,128]{3,2,1,0:T(8,128)(2,1)}, bf16[4,4,128,128]{3,2,1,0:T(8,128)(2,1)S(1)}, u32[]{:S(2)}) copy-start(bf16[4,4,128,128]{3,2,1,0:T(8,128)(2,1)S(1)} %pad_maximum_fusion.rest_0_) | copy-start | bytes 1572868
  108.6 15.8 %collective-permute-start.23 = (bf16[4,4,128,128]{3,2,1,0:T(8,128)(2,1)S(1)}, bf16[4,4,128,128]{3,2,1,0:T(8,128)(2,1)S(1)}, u32[]{:S(2)}, u32[]{:S(2)}) collective-permute-start(bf16[4,4,128,128]{3,2,1,0:T(8,128)(2,1)S(1)} %pad_maximum_fusion.rest_0_), channel_id=1, source_target_pairs={{0,1},{1,0},{2,3},{3,2},{4,5},{5,4},{6,7},{7,6},{8,9},{9,8},{10,11... | collective-permute-start | bytes 1572872 | tf_op jit(solution)/shard_map/ppermute | solution.py:60
  113.6 8.3 %copy-start.9 = (f32[128,2048]{1,0:T(8,128)S(1)}, f32[128,2048]{1,0:T(8,128)}, u32[]{:S(2)}) copy-start(f32[128,2048]{1,0:T(8,128)} %get-tuple-element.60.rest_0_) | copy-start | bytes 3145732
  113.6 8.3 %copy-start.17 = (bf16[64,2048]{1,0:T(8,128)(2,1)S(1)}, bf16[64,2048]{1,0:T(8,128)(2,1)}, u32[]{:S(2)}) copy-start(bf16[64,2048]{1,0:T(8,128)(2,1)} %copy-done.16) | copy-start | bytes 786436
  113.6 1.4 %collective-permute-start.24 = (bf16[4,128,128]{2,1,0:T(8,128)(2,1)S(1)}, bf16[4,128,128]{2,1,0:T(8,128)(2,1)S(1)}, u32[]{:S(2)}, u32[]{:S(2)}) collective-permute-start(bf16[4,128,128]{2,1,0:T(8,128)(2,1)S(1)} %add_convert_fusion.low_ref.rest_0_), channel_id=1, source_target_pairs={{0,1},{1,0},{2,3},{3,2},{4,5},{5,4},{6,7},{7,6},{8,9},{9,8},{10,11... | collective-permute-start | bytes 393224 | tf_op jit(solution)/shard_map/ppermute | solution.py:60
  115.1 9.3 %copy-start.6 = (f32[1024,1024]{1,0:T(8,128)S(1)}, f32[1024,1024]{1,0:T(8,128)}, u32[]{:S(2)}) copy-start(f32[1024,1024]{1,0:T(8,128)} %copy-done.5) | copy-start | bytes 12582916
  117.3 20.5 %collective-permute-start.27 = (bf16[8,16,256]{2,1,0:T(8,128)(2,1)S(1)}, bf16[8,16,256]{2,1,0:T(8,128)(2,1)S(1)}, u32[]{:S(2)}, u32[]{:S(2)}) collective-permute-start(bf16[8,16,256]{2,1,0:T(8,128)(2,1)S(1)} %get-tuple-element.66), channel_id=1, source_target_pairs={{0,24},{8,0},{16,8},{24,16},{1,25},{9,1},{17,9},{25,17},{2,26},{10... | collective-permute-start | bytes 196616 | tf_op jit(solution)/shard_map/ppermute | solution.py:39
  120.8 17.1 %collective-permute-start.26 = (bf16[8,16,256]{2,1,0:T(8,128)(2,1)S(1)}, bf16[8,16,256]{2,1,0:T(8,128)(2,1)S(1)}, u32[]{:S(2)}, u32[]{:S(2)}) collective-permute-start(bf16[8,16,256]{2,1,0:T(8,128)(2,1)S(1)} %get-tuple-element.67), channel_id=1, source_target_pairs={{0,16},{8,24},{16,0},{24,8},{1,17},{9,25},{17,1},{25,9},{2,18},{10... | collective-permute-start | bytes 196616 | tf_op jit(solution)/shard_map/ppermute | solution.py:39
  120.8 17.1 %collective-permute-start.25 = (bf16[8,16,256]{2,1,0:T(8,128)(2,1)S(1)}, bf16[8,16,256]{2,1,0:T(8,128)(2,1)S(1)}, u32[]{:S(2)}, u32[]{:S(2)}) collective-permute-start(bf16[8,16,256]{2,1,0:T(8,128)(2,1)S(1)} %get-tuple-element.68), channel_id=1, source_target_pairs={{0,8},{8,16},{16,24},{24,0},{1,9},{9,17},{17,25},{25,1},{2,10},{10... | collective-permute-start | bytes 196616 | tf_op jit(solution)/shard_map/ppermute | solution.py:39
  127.7 0.8 copy-start.15
  128.5 9.4 %copy-start.19 = (s32[60]{0:T(128)S(1)}, s32[60]{0:T(128)}, u32[]{:S(2)}) copy-start(s32[60]{0:T(128)} %copy-done.18) | copy-start | bytes 724
